TPU v7x, 32 devices: a whole 2x2x4 slice. The times are simulated.
32 devices in a mesh: groups: 2 (over y), seq: 4 (over z), head: 4 (over x, core).
Axes of the slice: x: 2, y: 2, z: 4, core: 2. Of those that a mesh axis runs over, the one named last changes fastest.
Arguments:
- x_in: bfloat16 [1024, 8192], P(('groups', 'seq'), 'head'), parts along dimension 0, may hold values from -6 to 6
- bc_in: bfloat16 [1024, 8, 256], P(('groups', 'seq'), 'head'), parts along dimension 0, may hold values from -6 to 6
- z_in: bfloat16 [1024, 8192], P(('groups', 'seq'), 'head'), parts along dimension 0, may hold values from -6 to 6
- dt_raw: float32 [1024, 128], P(('groups', 'seq'), 'head'), parts along dimension 0, may hold values from -12 to 0
- conv_x: float32 [4, 8192], P(None, 'head'), may hold values from -3 to 3
- conv_bc: float32 [4, 8, 256], P(None, 'head'), may hold values from -3 to 3
- a_log: float32 [128], P('head'), may hold values from -0.35 to 0.35
- d_skip: float32 [128], P('head'), may hold values from 0.5 to 1.5
- norm_gain: float32 [8192], P('head'), may hold values from 0.25 to 1.75
Outputs:
- out: bfloat16 [1024, 8192], P(('groups', 'seq'), 'head'), parts along dimension 0
There are 2 independent parts, one for each index of `groups`. A program takes and returns all parts, laid end to end along the dimension named above; an argument that names none is the same for every part. Nothing has to cross between parts.
All inputs are finite; a program needn't handle non-finite values.
Results may differ from a plain program's by a relative error of at most 0.0056.
Values may be sent and summed in bfloat16 or wider, within the bound.
No kernel may reach another device: no remote copies, remote signals or barrier semaphores. Data moves between devices by JAX's collectives and lax.ppermute only.
A program may use at most 192 MiB of HBM per device.

v0:
```python
import jax
import jax.numpy as jnp
from jax import lax
from jax.sharding import PartitionSpec as P

CONV = 4
BLOCK = 128


EPS = 1e-05


def passed_along(block, axis, distance):
    devices = range(lax.axis_size(axis))
    route = [(i - distance, i) for i in devices if i - distance in devices]
    return lax.ppermute(block, axis, route)


def conv_silu(tail_rows, series, taps):
    length = series.shape[0]
    padded = jnp.concatenate([tail_rows.astype(jnp.float32), series.astype(jnp.float32)], axis=0)
    running = jnp.zeros(series.shape, jnp.float32)
    for offset in range(taps.shape[0]):
        running = running + taps[offset] * padded[offset : offset + length]
    return jax.nn.silu(running).astype(jnp.bfloat16)


def block_terms(inputs, b_input, c_output, deltas, rates):
    cum_rate = jnp.cumsum(rates, axis=0)
    cum_moved = jnp.transpose(cum_rate, (1, 2, 0))
    delta_moved = jnp.transpose(deltas, (1, 2, 0))
    places = jnp.arange(cum_rate.shape[0])
    causal = places[:, None] >= places[None, :]
    gaps_all = cum_moved[..., :, None] - cum_moved[..., None, :]
    decays = jnp.where(causal, jnp.exp(jnp.where(causal, gaps_all, 0.0)), 0.0)
    intersection = jnp.einsum("tgn,sgn->gts", c_output, b_input, preferred_element_type=jnp.float32)
    weight = (decays * delta_moved[..., None, :] * intersection[:, None]).astype(jnp.bfloat16)
    y_intra = jnp.einsum("ghts,sghp->tghp", weight, inputs, preferred_element_type=jnp.float32)
    tail_decay = jnp.exp(cum_rate[-1] - cum_rate) * deltas
    scaled = (tail_decay[..., None] * inputs.astype(jnp.float32)).astype(jnp.bfloat16)
    states = jnp.einsum("sghp,sgn->ghpn", scaled, b_input, preferred_element_type=jnp.float32)
    return (y_intra, states, cum_rate, jnp.exp(cum_rate[-1]))


def block_output(y_intra, cum_rate, c_output, inputs, gates, incoming, skip, gain):
    state_half = incoming.astype(jnp.bfloat16)
    from_state = jnp.einsum(
        "tgn,ghpn->tghp", c_output, state_half, preferred_element_type=jnp.float32
    )
    mixed = (
        y_intra
        + jnp.exp(cum_rate)[..., None] * from_state
        + skip[..., None] * inputs.astype(jnp.float32)
    )
    gated = mixed * jax.nn.silu(gates.astype(jnp.float32))
    mean_sq = jnp.mean(gated * gated, axis=(2, 3), keepdims=True)
    return (gated * lax.rsqrt(mean_sq + EPS) * gain).astype(jnp.bfloat16)


def summarize(carry, piece):
    block_decay, states = piece
    return ((carry[0] * block_decay, block_decay[..., None, None] * carry[1] + states), None)


def advance_rows(carry, piece):
    return (piece[0] * carry + piece[1], carry)


def shards(x_in, bc_in, z_in, dt_raw, conv_x, conv_bc, a_log, d_skip, norm_gain):
    rim = CONV - 1
    tokens = x_in.shape[0]
    groups_dev = bc_in.shape[1]
    heads_dev = dt_raw.shape[1]
    per_group = heads_dev // groups_dev
    state_dim = bc_in.shape[2] // 2
    head_dim = x_in.shape[1] // heads_dev
    width_x = x_in.shape[1]
    last_rows = jnp.concatenate(
        [x_in[tokens - rim :], bc_in[tokens - rim :].reshape(rim, groups_dev * 2 * state_dim)],
        axis=1,
    )
    got_rows = passed_along(last_rows, "seq", 1)
    x_act = conv_silu(got_rows[:, :width_x], x_in, conv_x)
    bc_act = conv_silu(
        got_rows[:, width_x:].reshape(rim, groups_dev, 2 * state_dim), bc_in, conv_bc
    )
    deltas = jax.nn.softplus(dt_raw)
    rates = -jnp.exp(a_log)[None, :] * deltas
    block_count = tokens // BLOCK
    inputs = x_act.reshape(block_count, BLOCK, groups_dev, per_group, head_dim)
    b_input = bc_act[:, :, :state_dim].reshape(block_count, BLOCK, groups_dev, state_dim)
    c_output = bc_act[:, :, state_dim:].reshape(block_count, BLOCK, groups_dev, state_dim)
    delta_blocks = deltas.reshape(block_count, BLOCK, groups_dev, per_group)
    rate_blocks = rates.reshape(block_count, BLOCK, groups_dev, per_group)
    y_intra, states, cum_rate, block_decay = jax.vmap(block_terms)(
        inputs, b_input, c_output, delta_blocks, rate_blocks
    )
    start_decay = jnp.ones((groups_dev, per_group), jnp.float32)
    start_state = jnp.zeros((groups_dev, per_group, head_dim, state_dim), jnp.float32)
    summary, _ = lax.scan(summarize, (start_decay, start_state), (block_decay, states))
    decay_dev, states_dev = summary
    seq_count = lax.axis_size("seq")
    width_block = states_dev.size // seq_count
    flat_states = states_dev.reshape(seq_count, width_block)
    decay_rows = jnp.broadcast_to(decay_dev.reshape(1, heads_dev), (seq_count, heads_dev))
    got_states, got_decays = (
        lax.all_to_all(flat_states, "seq", split_axis=0, concat_axis=0, tiled=True),
        lax.all_to_all(decay_rows, "seq", split_axis=0, concat_axis=0, tiled=True),
    )
    owner = (lax.axis_index("seq") * width_block + jnp.arange(width_block, dtype=jnp.int32)) // (
        head_dim * state_dim
    )
    select = (owner[:, None] == jnp.arange(heads_dev, dtype=jnp.int32)[None, :]).astype(jnp.float32)
    entry_decay = jnp.dot(got_decays, select.T, precision=lax.Precision.HIGHEST)
    _, before = lax.scan(
        advance_rows, jnp.zeros((width_block,), jnp.float32), (entry_decay, got_states)
    )
    incoming = lax.all_to_all(before, "seq", split_axis=0, concat_axis=0, tiled=True).reshape(
        states_dev.shape
    )
    gates = z_in.reshape(block_count, BLOCK, groups_dev, per_group, head_dim)
    skip = d_skip.reshape(groups_dev, per_group)
    gain = norm_gain.reshape(groups_dev, per_group, head_dim)

    def emit(carry, piece):
        y_part, state_part, cum_part, decay_part, c_part, input_part, gate_part = piece
        result = block_output(y_part, cum_part, c_part, input_part, gate_part, carry, skip, gain)
        return (decay_part[..., None, None] * carry + state_part, result)

    _, outputs = lax.scan(
        emit, incoming, (y_intra, states, cum_rate, block_decay, c_output, inputs, gates)
    )
    return outputs.reshape(tokens, width_x)


def solution(mesh):
    return jax.shard_map(
        shards,
        mesh=mesh,
        in_specs=(
            P(("groups", "seq"), "head"),
            P(("groups", "seq"), "head", None),
            P(("groups", "seq"), "head"),
            P(("groups", "seq"), "head"),
            P(None, "head"),
            P(None, "head", None),
            P("head"),
            P("head"),
            P("head"),
        ),
        out_specs=P(("groups", "seq"), "head"),
        check_vma=False,
    )
```

profile of v0, /device:TPU:0, one launch (start us, length us, event | category | flops | bytes accessed | tf_op | source)
XLA Modules:
  0.0 104.3 jit_solution(37182162923625253)
XLA Ops:
  0.0 0.8 slice.65
  0.8 0.7 slice_bitcast_fusion
  1.6 4.9 %collective-permute-start = (bf16[3,2560]{1,0:T(4,128)(2,1)S(1)}, bf16[3,2560]{1,0:T(4,128)(2,1)S(1)}, u32[]{:S(2)}, u32[]{:S(2)}) collective-permute-start(bf16[3,2560]{1,0:T(4,128)(2,1)S(1)} %pad_maximum_fusion.2), channel_id=1, source_target_pairs={{0,4},{4,8},{8,12},{1,5},{5,9},{9,13},{2,6},{6,10},{10,14},{3,7},{... | collective-permute-start | bytes 46088 | tf_op jit(solution)/shard_map/ppermute | solution.py:16
  6.5 0.7 exponential_negate_fusion
  7.2 0.8 broadcast_multiply_fusion
  8.3 0.6 broadcast_in_dim.57
  8.9 3.9 %all-to-all-start = ((f32[4,1,32]{2,1,0:T(1,128)}), f32[4,1,32]{2,1,0:T(1,128)S(1)}, u32[]{:S(2)}, u32[]{:S(2)}) async-start(f32[4,1,32]{2,1,0:T(1,128)} %broadcast_in_dim.57), calls=%async_computation | async-start | bytes 4096 | tf_op jit(solution)/shard_map/all_to_all | solution.py:108
  12.8 0.9 copy_convert_fusion
  13.8 0.6 bitcast_exponential_fusion
  14.6 0.7 multiply_convert_fusion.3
  15.2 0.3 copy.63
  15.5 0.2 multiply_convert_fusion.4
  15.7 1.3 %convolution_add_fusion = f32[2,16,64,128]{3,2,1,0:T(8,128)} fusion(bf16[128,2,16,64]{0,3,2,1:T(8,128)(2,1)S(1)} %bitcast.91, f32[128,2,16]{0,2,1:T(8,128)S(1)} %get-tuple-element.123, f32[2,16]{1,0:T(2,128)S(1)} %exponential_multiply_fusion, bf16[128,2,256]{2,0,1:T(8,128)(2,1)S(1)} %multiply_convert_fusion.4), kind=kOutput, calls=%fused_computation.15 | convolution fusion | flops 68157440 | bytes 1655808 | tf_op jit(solution)/shard_map/vmap(sghp,sgn->ghpn)/dot_general | solution.py:41
  17.0 1.1 %all-to-all-done = f32[4,1,32]{2,1,0:T(1,128)S(1)} async-done(((f32[4,1,32]{2,1,0:T(1,128)}), f32[4,1,32]{2,1,0:T(1,128)S(1)}, u32[]{:S(2)}, u32[]{:S(2)}) %all-to-all-start) | async-done | bytes 544 | tf_op jit(solution)/shard_map/all_to_all | solution.py:108
  18.1 4.0 %all-to-all-start.1 = ((f32[4,1,65536]{2,1,0:T(1,128)}), f32[4,1,65536]{2,1,0:T(1,128)S(1)}, u32[]{:S(2)}, u32[]{:S(2)}) async-start(f32[4,1,65536]{2,1,0:T(1,128)} %bitcast.26), calls=%async_computation.1 | async-start | bytes 2097152 | tf_op jit(solution)/shard_map/all_to_all | solution.py:107
  22.1 0.2 add_select_fusion
  22.3 2.6 %fusion = f32[4,65536]{1,0:T(4,128)S(1)} fusion(f32[4,32]{1,0:T(4,128)S(1)} %bitcast.106, s32[65536]{0:T(1024)S(1)} %add_select_fusion), kind=kOutput, calls=%fused_computation.5 | convolution fusion | flops 102760448 | bytes 1311232 | tf_op jit(solution)/shard_map/dot_general | solution.py:114
  24.9 22.1 %all-to-all-done.1 = f32[4,1,65536]{2,1,0:T(1,128)S(1)} async-done(((f32[4,1,65536]{2,1,0:T(1,128)}), f32[4,1,65536]{2,1,0:T(1,128)S(1)}, u32[]{:S(2)}, u32[]{:S(2)}) %all-to-all-start.1) | async-done | bytes 1048608 | tf_op jit(solution)/shard_map/all_to_all | solution.py:107
  47.0 0.7 copy.78
  47.7 24.1 %while.3 = (s32[]{:T(128)}, f32[65536]{0:T(1024)S(1)}, bf16[4,65536]{1,0:T(4,128)(2,1)}, f32[4,65536]{1,0:T(4,128)S(1)}, f32[4,65536]{1,0:T(4,128)S(1)}, /*index=5*/s32[]{:T(128)}, s32[]{:T(128)}) while((s32[]{:T(128)}, f32[65536]{0:T(1024)S(1)}, bf16[4,65536]{1,0:T(4,128)(2,1)}, f32[4,65536]{1,0:T(4,128)S(1)}, ...), condition=%wide.region_2.3_spmd.clone, body=%wide.region_1.2_spmd.clone.sunk | while | flops 196611 | bytes 2883679 | solution.py:115
  47.7 0.5 constant_dynamic-slice_fusion.3
  48.3 0.2 multiply_add_fusion.2
  48.4 5.3 %dynamic_update_slice.9 = bf16[4,65536]{1,0:T(4,128)(2,1)} dynamic-update-slice(bf16[4,65536]{1,0:T(4,128)(2,1)} %get-tuple-element.180, f32[1,65536]{1,0:T(1,128)S(1)} %bitcast.87, s32[]{:T(128)} %get-tuple-element.178, s32[]{:T(128)} %constant.78.clone.1..sunk) | dynamic-update-slice | bytes 524292 | tf_op jit(solution)/shard_map/while/body/jit(dynamic_update_index_in_dim)/dynamic_update_slice | solution.py:115
  53.7 0.5 constant_dynamic-slice_fusion.3
  54.3 0.2 multiply_add_fusion.2
  54.5 5.3 %dynamic_update_slice.9 = bf16[4,65536]{1,0:T(4,128)(2,1)} dynamic-update-slice(bf16[4,65536]{1,0:T(4,128)(2,1)} %get-tuple-element.180, f32[1,65536]{1,0:T(1,128)S(1)} %bitcast.87, s32[]{:T(128)} %get-tuple-element.178, s32[]{:T(128)} %constant.78.clone.1..sunk) | dynamic-update-slice | bytes 524292 | tf_op jit(solution)/shard_map/while/body/jit(dynamic_update_index_in_dim)/dynamic_update_slice | solution.py:115
  59.8 0.5 constant_dynamic-slice_fusion.3
  60.3 0.2 multiply_add_fusion.2
  60.5 5.3 %dynamic_update_slice.9 = bf16[4,65536]{1,0:T(4,128)(2,1)} dynamic-update-slice(bf16[4,65536]{1,0:T(4,128)(2,1)} %get-tuple-element.180, f32[1,65536]{1,0:T(1,128)S(1)} %bitcast.87, s32[]{:T(128)} %get-tuple-element.178, s32[]{:T(128)} %constant.78.clone.1..sunk) | dynamic-update-slice | bytes 524292 | tf_op jit(solution)/shard_map/while/body/jit(dynamic_update_index_in_dim)/dynamic_update_slice | solution.py:115
  65.8 0.5 constant_dynamic-slice_fusion.3
  66.4 0.2 multiply_add_fusion.2
  66.5 5.3 %dynamic_update_slice.9 = bf16[4,65536]{1,0:T(4,128)(2,1)} dynamic-update-slice(bf16[4,65536]{1,0:T(4,128)(2,1)} %get-tuple-element.180, f32[1,65536]{1,0:T(1,128)S(1)} %bitcast.87, s32[]{:T(128)} %get-tuple-element.178, s32[]{:T(128)} %constant.78.clone.1..sunk) | dynamic-update-slice | bytes 524292 | tf_op jit(solution)/shard_map/while/body/jit(dynamic_update_index_in_dim)/dynamic_update_slice | solution.py:115
  71.8 1.6 %all_to_all.22 = bf16[4,1,65536]{2,1,0:T(2,128)(2,1)S(1)} reshape(bf16[4,65536]{1,0:T(4,128)(2,1)} %get-tuple-element.69) | data formatting | bytes 1048576 | tf_op jit(solution)/shard_map/all_to_all | solution.py:118
  73.4 0.6 broadcast.125
  74.0 4.0 %reduce.2 = bf16[4,65536]{1,0:T(4,128)(2,1)S(1)} reduce(bf16[4,1,65536]{2,1,0:T(2,128)(2,1)S(1)} %all_to_all.22, bf16[]{:T(256)} %broadcast.125), dimensions={1}, to_apply=%all_to_all.22.reduce_sub_computation | reduce | bytes 1048578 | tf_op jit(solution)/shard_map/all_to_all | solution.py:118
  78.0 1.4 %reshape.194 = bf16[4,2,32768]{2,1,0:T(2,128)(2,1)} reshape(bf16[4,65536]{1,0:T(4,128)(2,1)S(1)} %reduce.2) | data formatting | bytes 1048576
  79.4 3.6 %all-to-all-start.2 = ((bf16[4,2,32768]{2,1,0:T(2,128)(2,1)}), bf16[4,2,32768]{2,1,0:T(2,128)(2,1)S(1)}, u32[]{:S(2)}, u32[]{:S(2)}) async-start(bf16[4,2,32768]{2,1,0:T(2,128)(2,1)} %reshape.194), calls=%async_computation.2 | async-start | bytes 1048576 | tf_op jit(solution)/shard_map/all_to_all | solution.py:118
  83.2 0.2 copy.70
  83.4 0.3 copy-done.10
  84.0 0.2 fusion.37
  84.2 1.9 %convolution_bitcast_fusion.1 = f32[128,2,16,64]{0,3,2,1:T(8,128)} fusion(bf16[128,2,16,64]{0,3,2,1:T(8,128)(2,1)S(1)} %bitcast.92, f32[2,128,128]{2,1,0:T(8,128)S(1)} %fusion.37, f32[2,16,128]{2,1,0:T(8,128)S(1)} %bitcast.99, f32[2,16,128]{2,1,0:T(8,128)S(1)} %copy.65, pred[128,128]{1,0:T(8,128)(4,1)S(1)} %iota_compare_fusion.2), kind=kOutput, calls=%fused_computation.16 | convolution fusion | flops 70254592 | bytes 1753088 | tf_op jit(solution)/shard_map/vmap(ghts,sghp->tghp)/dot_general | solution.py:38
  86.1 10.7 %all-to-all-done.2 = bf16[4,2,32768]{2,1,0:T(2,128)(2,1)S(1)} async-done(((bf16[4,2,32768]{2,1,0:T(2,128)(2,1)}), bf16[4,2,32768]{2,1,0:T(2,128)(2,1)S(1)}, u32[]{:S(2)}, u32[]{:S(2)}) %all-to-all-start.2) | async-done | bytes 524320 | tf_op jit(solution)/shard_map/all_to_all | solution.py:118
  96.8 0.5 reshape.195
  97.4 3.2 %convert_reduce_fusion = bf16[4,65536]{1,0:T(4,128)(2,1)S(1)} fusion(bf16[4,1,65536]{2,1,0:T(2,128)(2,1)S(1)} %reshape.195), kind=kLoop, calls=%fused_computation.34 | loop fusion | bytes 1048576 | tf_op jit(solution)/shard_map/while/body/eval_jaxpr/convert_element_type | solution.py:46
  100.6 0.5 convert_element_type.71
  101.1 1.8 %multiply_reduce_fusion = (f32[128,2]{0,1:T(2,128)S(1)}, f32[128,2,16,64]{0,3,2,1:T(8,128)S(1)}) fusion(f32[128,2,16,64]{0,3,2,1:T(8,128)S(1)} %bitcast.96, bf16[128,2,16,64]{0,3,2,1:T(8,128)(2,1)S(1)} %bitcast.93, f32[2,16]{1,0:T(2,128)S(1)} %mul.275, f32[128,2,16,64]{0,3,2,1:T(8,128)} %convolution_bitcast_fusion.1, ...), kind=kOutput, calls=%fused_computation.33 | convolution fusion | flops 70254336 | bytes 4278272 | tf_op jit(solution)/shard_map/while/body/eval_jaxpr/tgn,ghpn->tghp/dot_general | solution.py:47
  102.9 0.3 multiply_convert_fusion.2
  103.3 1.0 copy.71
  (43 shorter events, 1.0 us)
Async XLA Ops:
  0.0 14.4 %copy-start.4 = (bf16[128,2048]{1,0:T(8,128)(2,1)S(1)}, bf16[128,2048]{1,0:T(8,128)(2,1)}, u32[]{:S(2)}) copy-start(bf16[128,2048]{1,0:T(8,128)(2,1)} %param.11) | copy-start | bytes 1572868
  0.0 13.7 %copy-start.6 = (f32[4,2048]{1,0:T(4,128)S(1)}, f32[4,2048]{1,0:T(4,128)}, u32[]{:S(2)}) copy-start(f32[4,2048]{1,0:T(4,128)} %param.15) | copy-start | bytes 98308
  0.0 13.8 %copy-start.9 = (f32[4,2,256]{2,1,0:T(2,128)S(1)}, f32[4,2,256]{2,1,0:T(2,128)}, u32[]{:S(2)}) copy-start(f32[4,2,256]{2,1,0:T(2,128)} %param.16) | copy-start | bytes 24580
  1.6 13.0 %collective-permute-start = (bf16[3,2560]{1,0:T(4,128)(2,1)S(1)}, bf16[3,2560]{1,0:T(4,128)(2,1)S(1)}, u32[]{:S(2)}, u32[]{:S(2)}) collective-permute-start(bf16[3,2560]{1,0:T(4,128)(2,1)S(1)} %pad_maximum_fusion.2), channel_id=1, source_target_pairs={{0,4},{4,8},{8,12},{1,5},{5,9},{9,13},{2,6},{6,10},{10,14},{3,7},{... | collective-permute-start | bytes 46088 | tf_op jit(solution)/shard_map/ppermute | solution.py:16
  8.9 9.3 %all-to-all-start = ((f32[4,1,32]{2,1,0:T(1,128)}), f32[4,1,32]{2,1,0:T(1,128)S(1)}, u32[]{:S(2)}, u32[]{:S(2)}) async-start(f32[4,1,32]{2,1,0:T(1,128)} %broadcast_in_dim.57), calls=%async_computation | async-start | bytes 4096 | tf_op jit(solution)/shard_map/all_to_all | solution.py:108
  15.5 1.5 %copy-start = (bf16[128,2048]{0,1:T(8,128)(2,1)}, bf16[128,2048]{0,1:T(8,128)(2,1)S(1)}, u32[]{:S(2)}) copy-start(bf16[128,2048]{0,1:T(8,128)(2,1)S(1)} %copy.63) | copy-start | bytes 1572868
  15.7 2.4 %copy-start.2 = (bf16[128,2,256]{2,0,1:T(8,128)(2,1)}, bf16[128,2,256]{2,0,1:T(8,128)(2,1)S(1)}, u32[]{:S(2)}) copy-start(bf16[128,2,256]{2,0,1:T(8,128)(2,1)S(1)} %multiply_convert_fusion.4) | copy-start | bytes 393220
  18.1 28.9 %all-to-all-start.1 = ((f32[4,1,65536]{2,1,0:T(1,128)}), f32[4,1,65536]{2,1,0:T(1,128)S(1)}, u32[]{:S(2)}, u32[]{:S(2)}) async-start(f32[4,1,65536]{2,1,0:T(1,128)} %bitcast.26), calls=%async_computation.1 | async-start | bytes 2097152 | tf_op jit(solution)/shard_map/all_to_all | solution.py:107
  78.0 5.2 %copy-start.5 = (bf16[128,2048]{1,0:T(8,128)(2,1)S(1)}, bf16[128,2048]{1,0:T(8,128)(2,1)}, u32[]{:S(2)}) copy-start(bf16[128,2048]{1,0:T(8,128)(2,1)} %param.13) | copy-start | bytes 1572868
  79.4 17.4 %all-to-all-start.2 = ((bf16[4,2,32768]{2,1,0:T(2,128)(2,1)}), bf16[4,2,32768]{2,1,0:T(2,128)(2,1)S(1)}, u32[]{:S(2)}, u32[]{:S(2)}) async-start(bf16[4,2,32768]{2,1,0:T(2,128)(2,1)} %reshape.194), calls=%async_computation.2 | async-start | bytes 1048576 | tf_op jit(solution)/shard_map/all_to_all | solution.py:118
  83.1 0.7 copy-start.10
  83.1 0.7 copy-start.8
  83.1 0.9 copy-start.3
  83.1 1.1 %copy-start.1 = (bf16[128,2048]{0,1:T(8,128)(2,1)S(1)}, bf16[128,2048]{0,1:T(8,128)(2,1)}, u32[]{:S(2)}) copy-start(bf16[128,2048]{0,1:T(8,128)(2,1)} %copy-done) | copy-start | bytes 1572868
  97.4 3.8 %copy-start.7 = (f32[128,2,16]{0,2,1:T(8,128)S(1)}, f32[128,2,16]{0,2,1:T(8,128)}, u32[]{:S(2)}) copy-start(f32[128,2,16]{0,2,1:T(8,128)} %get-tuple-element.122) | copy-start | bytes 49156
where the time goes:
time: 106 us; the launch traced here: 104 us
  local copies, waits for them, and re-layouts  36.6 us (35%)
  waiting for transfers between devices  33.9 us (32%)
  starting transfers between devices  16.4 us (15%)
  other arithmetic  9.25 us (9%)
  matrix products  7.77 us (7%)
    all_to_all x1, waiting for transfers between devices, shards(): lax.all_to_all(flat_states, 'seq', split_axis=0, concat_axis=0, tiled=True)  22.1 us
    dynamic_update_slice x4, local copies, waits for them, and re-layouts, shards(): lax.scan(advance_rows, jnp.zeros((width_block,), jnp.float32), (entry_dec...  21.3 us
    all_to_all x1, waiting for transfers between devices, shards(): lax.all_to_all(before, 'seq', split_axis=0, concat_axis=0, tiled=True)  10.7 us
    ppermute x1, starting transfers between devices, passed_along(): return lax.ppermute(block, axis, route)  4.93 us
    all_to_all x1, other arithmetic, shards(): lax.all_to_all(before, 'seq', split_axis=0, concat_axis=0, tiled=True)  4 us
    all_to_all x1, starting transfers between devices, shards(): lax.all_to_all(flat_states, 'seq', split_axis=0, concat_axis=0, tiled=True)  3.98 us
    all_to_all x1, starting transfers between devices, shards(): lax.all_to_all(decay_rows, 'seq', split_axis=0, concat_axis=0, tiled=True)  3.86 us
    unnamed x27, local copies, waits for them, and re-layouts  3.8 us
  transfers between devices with their start and end apart: 4, of which 3 were waited for; matrix products, arithmetic and copies ran while one was open for 11% of the time, Pallas kernels for 0%

commit v1 on v0

v1 whole, which is shorter than its diff:
```python
import functools

import jax
import jax.numpy as jnp
from jax import lax
from jax.experimental import pallas as pl
from jax.experimental.pallas import tpu as pltpu
from jax.sharding import PartitionSpec as P

EPS = 1e-05
F32 = jnp.float32
BF16 = jnp.bfloat16
CHAIN_MOST = 4


def silu(u):
    return 0.5 * u * (1.0 + jnp.tanh(0.5 * u))


def softplus(v):
    return jnp.maximum(v, 0.0) + jnp.log1p(jnp.exp(-jnp.abs(v)))


def halves(v, count, axis):
    parts = []
    for _ in range(count - 1):
        part = v.astype(BF16)
        parts.append(part)
        v = v - part.astype(F32)
    parts.append(v.astype(BF16))
    return jnp.concatenate(parts, axis=axis)


def spread(per_head, head_dim, count):
    heads = per_head.shape[0]
    rows = lax.broadcasted_iota(jnp.int32, (heads * count, heads * head_dim), 0)
    cols = lax.broadcasted_iota(jnp.int32, (heads * count, heads * head_dim), 1)
    pick = (rows % heads == cols // head_dim).astype(F32).astype(BF16)
    return lax.dot_general(
        halves(per_head, count, 0), pick, (((0,), (0,)), ((), ())), preferred_element_type=F32
    )


def spread_row(column, head_dim):
    heads = column.shape[0]
    rows = lax.broadcasted_iota(jnp.int32, (heads, heads * head_dim), 0)
    cols = lax.broadcasted_iota(jnp.int32, (heads, heads * head_dim), 1)
    return jnp.sum(jnp.where(rows == cols // head_dim, column, 0.0), axis=0, keepdims=True)


def as_column(row, start, heads):
    every = row.shape[1]
    rows = lax.broadcasted_iota(jnp.int32, (heads, every), 0)
    cols = lax.broadcasted_iota(jnp.int32, (heads, every), 1)
    return jnp.sum(jnp.where(cols == rows + start, row, 0.0), axis=1, keepdims=True)


def conv_act(series, tail, taps):
    count = taps.shape[0]
    above = tail.shape[0]
    padded = jnp.concatenate([tail, series], axis=0)
    total = taps[count - 1 : count] * series
    for back in range(1, count):
        total = total + taps[count - 1 - back : count - back] * pltpu.roll(padded, back, 0)[above:]
    return silu(total).astype(BF16)


def rates(dt_raw, a_log_row, start):
    heads, tokens = dt_raw.shape
    dt = softplus(dt_raw)
    rate = -jnp.exp(as_column(a_log_row, start, heads)) * dt
    earlier = lax.broadcasted_iota(jnp.int32, (tokens, tokens), 0)
    later = lax.broadcasted_iota(jnp.int32, (tokens, tokens), 1)
    upto = (earlier <= later).astype(F32)
    cum = jnp.dot(rate, upto, precision=lax.Precision.HIGHEST, preferred_element_type=F32)
    return dt, cum


def state_kernel(
    group, start, head_dim, x, tail_x, bc, tail_bc, taps_x, taps_bc, dt_raw, a_log,
    x_act, bc_act, state, state_half, decay,
):
    dt, cum = rates(dt_raw[...], a_log[...], start)
    end = cum[:, -1:]
    act = conv_act(x[...].astype(F32), tail_x[...].astype(F32), taps_x[...])
    x_act[...] = act
    bc_here = conv_act(
        bc[...].astype(F32)[:, group], tail_bc[...].astype(F32), taps_bc[...][:, group]
    )
    bc_act[...] = bc_here
    tail_decay = spread(jnp.exp(end - cum) * dt, head_dim, 2)
    scaled = (tail_decay * act.astype(F32)).astype(BF16)
    b = bc_here[:, : bc_here.shape[1] // 2]
    total = lax.dot_general(b, scaled, (((0,), (0,)), ((), ())), preferred_element_type=F32)
    state[...] = total
    state_half[...] = total.astype(BF16)
    decay[...] = spread_row(jnp.exp(end), head_dim)


def intra_kernel(start, head_dim, x_act, bc_act, z, dt_raw, a_log, d_skip, y_part, lead):
    dt, cum = rates(dt_raw[...], a_log[...], start)
    heads, tokens = dt.shape
    state_dim = bc_act.shape[1] // 2
    b, c = bc_act[:, :state_dim], bc_act[:, state_dim:]
    inner = lax.dot_general(c, b, (((1,), (1,)), ((), ())), preferred_element_type=F32)
    t_at = lax.broadcasted_iota(jnp.int32, (tokens, tokens), 0)
    s_at = lax.broadcasted_iota(jnp.int32, (tokens, tokens), 1)
    inner = jnp.where(t_at >= s_at, inner, 0.0)
    cum_t = cum.T
    gate = silu(z[...].astype(F32))
    lead[...] = gate * spread(jnp.exp(cum), head_dim, 2)
    skip = spread_row(as_column(d_skip[...], start, heads), head_dim)
    pair = 2 * head_dim
    for first in range(0, heads, 2):
        cut = slice(first * head_dim, first * head_dim + pair)
        act = x_act[:, cut]
        lane = lax.broadcasted_iota(jnp.int32, act.shape, 1)
        wide = act.astype(F32)
        blocks = jnp.concatenate(
            [jnp.where(lane < head_dim, wide, 0.0), jnp.where(lane < head_dim, 0.0, wide)], axis=0
        ).astype(BF16)
        weights = []
        for h in (first, first + 1):
            gap = jnp.minimum(cum_t[:, h : h + 1] - cum[h : h + 1, :], 0.0)
            weights.append((jnp.exp(gap) * dt[h : h + 1, :] * inner).astype(BF16))
        y = jnp.dot(jnp.concatenate(weights, axis=1), blocks, preferred_element_type=F32)
        y_part[:, cut] = (y + skip[:, cut] * wide) * gate[:, cut]


def output_kernel(seen, c, y_part, lead, gain, *refs):
    arrived, out = refs[:seen], refs[-1]
    state = arrived[0][...]
    for more in arrived[1:]:
        state = state + more[...]
    from_state = jnp.dot(c[...], state, preferred_element_type=F32)
    gated = y_part[...] + lead[...] * from_state
    mean_sq = jnp.mean(gated * gated, axis=1, keepdims=True)
    out[...] = (gated * lax.rsqrt(mean_sq + EPS) * gain[...]).astype(BF16)


def params():
    return pltpu.CompilerParams(vmem_limit_bytes=32 * 1024 * 1024)


def chain(state, to_send, decay, devices):
    arrived = []
    for hop in range(devices - 1):
        came = lax.ppermute(to_send, "seq", [(hop, hop + 1)])
        arrived.append(came)
        to_send = (decay * came.astype(F32) + state).astype(BF16)
    return arrived


def doubling(state, to_send, decay, devices):
    def moved(value, distance):
        return lax.ppermute(value, "seq", [(i, i + distance) for i in range(devices - distance)])

    total, decay = moved(to_send, 1), moved(decay, 1)
    distance = 1
    while distance < devices - 1:
        came = moved(total, distance)
        total = (decay * came.astype(F32) + total.astype(F32)).astype(BF16)
        decay = decay * moved(decay, distance)
        distance *= 2
    return [total]


def shards(x_in, bc_in, z_in, dt_raw, conv_x, conv_bc, a_log, d_skip, norm_gain):
    tokens, width = x_in.shape
    groups = bc_in.shape[1]
    state_dim = bc_in.shape[2] // 2
    heads = dt_raw.shape[1]
    head_dim = width // heads
    taps = conv_x.shape[0]
    cols = width // groups
    per_group = heads // groups
    devices = lax.axis_size("seq")
    rim = 8

    route = [(i, i + 1) for i in range(devices - 1)]
    rows = jnp.concatenate(
        [x_in[tokens - rim :], bc_in[tokens - rim :].reshape(rim, groups * 2 * state_dim)], axis=1
    )
    got = lax.ppermute(rows, "seq", route)
    dt_t = dt_raw.T
    a_row = a_log.reshape(1, heads)
    d_row = d_skip.reshape(1, heads)
    gain = norm_gain.reshape(1, width)

    def whole(array):
        return pl.BlockSpec(array.shape, lambda i: (0,) * array.ndim)

    def column(height, wide, at):
        return pl.BlockSpec((height, wide), lambda i: (0, at))

    states = []
    for g in range(groups):
        states.append(
            pl.pallas_call(
                functools.partial(state_kernel, g, g * per_group, head_dim),
                out_shape=(
                    jax.ShapeDtypeStruct((tokens, cols), BF16),
                    jax.ShapeDtypeStruct((tokens, 2 * state_dim), BF16),
                    jax.ShapeDtypeStruct((state_dim, cols), F32),
                    jax.ShapeDtypeStruct((state_dim, cols), BF16),
                    jax.ShapeDtypeStruct((1, cols), F32),
                ),
                in_specs=[
                    column(tokens, cols, g),
                    column(rim, cols, g),
                    whole(bc_in),
                    column(rim, 2 * state_dim, width // (2 * state_dim) + g),
                    column(taps, cols, g),
                    whole(conv_bc),
                    pl.BlockSpec((per_group, tokens), lambda i, g=g: (g, 0)),
                    whole(a_row),
                ],
                out_specs=(
                    column(tokens, cols, 0),
                    column(tokens, 2 * state_dim, 0),
                    column(state_dim, cols, 0),
                    column(state_dim, cols, 0),
                    column(1, cols, 0),
                ),
                grid=(1,),
                compiler_params=params(),
                name="states",
            )(x_in, got, bc_in, got, conv_x, conv_bc, dt_t, a_row)
        )

    scan = chain if devices <= CHAIN_MOST else doubling
    arrived = [scan(*states[g][2:], devices) for g in range(groups)]

    parts = []
    for g in range(groups):
        act, bc_act, _, _, _ = states[g]
        parts.append(
            pl.pallas_call(
                functools.partial(intra_kernel, g * per_group, head_dim),
                out_shape=(
                    jax.ShapeDtypeStruct((tokens, cols), F32),
                    jax.ShapeDtypeStruct((tokens, cols), F32),
                ),
                in_specs=[
                    whole(act),
                    whole(bc_act),
                    column(tokens, cols, g),
                    pl.BlockSpec((per_group, tokens), lambda i, g=g: (g, 0)),
                    whole(a_row),
                    whole(d_row),
                ],
                out_specs=(column(tokens, cols, 0), column(tokens, cols, 0)),
                grid=(1,),
                compiler_params=params(),
                cost_estimate=pl.CostEstimate(
                    flops=4 * tokens * tokens * cols,
                    bytes_accessed=12 * tokens * cols,
                    transcendentals=tokens * tokens * per_group,
                ),
                name="intra",
            )(act, bc_act, z_in, dt_t, a_row, d_row)
        )

    out = None
    for g in range(groups):
        y_part, lead = parts[g]
        bc_act = states[g][1]
        operands = [bc_act, y_part, lead, gain] + arrived[g]
        specs = [
            column(tokens, state_dim, 1), whole(y_part), whole(lead), column(1, cols, g)
        ] + [whole(v) for v in arrived[g]]
        aliases = {}
        if out is not None:
            aliases = {len(operands): 0}
            operands.append(out)
            specs.append(pl.BlockSpec(memory_space=pl.ANY))
        out = pl.pallas_call(
            functools.partial(output_kernel, len(arrived[g])),
            out_shape=jax.ShapeDtypeStruct((tokens, width), BF16),
            in_specs=specs,
            out_specs=column(tokens, cols, g),
            grid=(1,),
            input_output_aliases=aliases,
            compiler_params=params(),
            name="outputs",
        )(*operands)
    return out


def solution(mesh):
    return jax.shard_map(
        shards,
        mesh=mesh,
        in_specs=(
            P(("groups", "seq"), "head"),
            P(("groups", "seq"), "head", None),
            P(("groups", "seq"), "head"),
            P(("groups", "seq"), "head"),
            P(None, "head"),
            P(None, "head", None),
            P("head"),
            P("head"),
            P("head"),
        ),
        out_specs=P(("groups", "seq"), "head"),
        check_vma=False,
    )
```

time: 106 us -> 44.2 us (0.42)
  the two profiles are of different devices: /device:TPU:0 before, /device:TPU:30 now
where the time goes in v1:
time: 44.2 us; the launch traced here: 43.8 us
  waiting for transfers between devices  25.5 us (58%)
  starting transfers between devices  6.85 us (15%)
  Pallas kernels  6.24 us (14%)
  local copies, waits for them, and re-layouts  4.72 us (11%)
    ppermute x6, waiting for transfers between devices, chain(): came = lax.ppermute(to_send, 'seq', [(hop, hop + 1)])  20.9 us
    ppermute x6, starting transfers between devices, chain(): came = lax.ppermute(to_send, 'seq', [(hop, hop + 1)])  5.43 us
    ppermute x1, waiting for transfers between devices, shards(): got = lax.ppermute(rows, 'seq', route)  4.6 us
    unnamed x20, local copies, waits for them, and re-layouts  3.96 us
    pallas_call x2, Pallas kernels, shards(): pl.pallas_call(functools.partial(output_kernel, len(arrived[g])), out_sha...  2.11 us
    pallas_call x2, Pallas kernels, shards(): pl.pallas_call(functools.partial(intra_kernel, g * per_group, head_dim),...  2.07 us
    pallas_call x2, Pallas kernels, shards(): pl.pallas_call(functools.partial(state_kernel, g, g * per_group, head_dim...  2.06 us
    ppermute x1, starting transfers between devices, shards(): got = lax.ppermute(rows, 'seq', route)  1.42 us
  transfers between devices with their start and end apart: 7, of which 3 were waited for; matrix products, arithmetic and copies ran while one was open for 1% of the time, Pallas kernels for 9%

profile of v1, /device:TPU:30, one launch (start us, length us, event | category | flops | bytes accessed | tf_op | source)
XLA Modules:
  0.0 43.8 jit_solution(8396783066042558517)
XLA Ops:
  0.0 0.7 %slice_bitcast_fusion = bf16[1,8,2,256]{3,2,1,0:T(2,128)(2,1)S(1)} fusion(bf16[128,2,256]{2,1,0:T(2,128)(2,1)} %bc.3), kind=kLoop, calls=%fused_computation.5 | loop fusion | bytes 16384
  0.7 0.0 slice-start
  0.7 0.7 %slice-done = bf16[8,2048]{1,0:T(8,128)(2,1)S(1)} async-done(((bf16[128,2048]{1,0:T(8,128)(2,1)}), bf16[8,2048]{1,0:T(8,128)(2,1)S(1)}, s32[]{:S(2)}) %slice-start) | async-done | bytes 32792 | tf_op jit(solution)/shard_map/slice | solution.py:182
  1.5 0.0 copy-start.3
  1.5 0.0 copy-start.4
  1.5 0.0 copy-start.5
  1.5 1.4 %collective-permute-start = (bf16[8,2560]{1,0:T(8,128)(2,1)S(1)}, bf16[8,2560]{1,0:T(8,128)(2,1)S(1)}, u32[]{:S(2)}, u32[]{:S(2)}) collective-permute-start(bf16[8,2560]{1,0:T(8,128)(2,1)S(1)} %pad_maximum_fusion), channel_id=1, source_target_pairs={{0,4},{4,8},{8,12},{1,5},{5,9},{9,13},{2,6},{6,10},{10,14},{3,7},{... | collective-permute-start | bytes 122888 | tf_op jit(solution)/shard_map/ppermute | solution.py:184
  2.9 4.6 %collective-permute-done.tail_x.tail_bc = bf16[8,2560]{1,0:T(8,128)(2,1)S(1)} collective-permute-done((bf16[8,2560]{1,0:T(8,128)(2,1)S(1)}, bf16[8,2560]{1,0:T(8,128)(2,1)S(1)}, u32[]{:S(2)}, u32[]{:S(2)}) %collective-permute-start) | collective-permute-done | bytes 40992 | tf_op jit(solution)/shard_map/ppermute | solution.py:184
  7.5 0.0 copy-start.7
  7.5 0.0 copy-done.3
  7.5 0.0 copy-done.4
  7.5 0.0 copy-done.5
  7.5 0.6 %copy-done.7 = f32[32]{0:T(128)S(1)} copy-done((f32[32]{0:T(128)S(1)}, f32[32]{0:T(128)}, u32[]{:S(2)}) %copy-start.7) | copy-done | bytes 152
  8.2 0.0 copy-start
  8.2 1.0 %copy-done = bf16[128,2048]{1,0:T(8,128)(2,1)S(1)} copy-done((bf16[128,2048]{1,0:T(8,128)(2,1)S(1)}, bf16[128,2048]{1,0:T(8,128)(2,1)}, u32[]{:S(2)}) %copy-start) | copy-done | bytes 524312
  9.2 0.0 copy-start.2
  9.2 0.9 %copy-done.2 = bf16[128,2,256]{2,1,0:T(2,128)(2,1)S(1)} copy-done((bf16[128,2,256]{2,1,0:T(2,128)(2,1)S(1)}, bf16[128,2,256]{2,1,0:T(2,128)(2,1)}, u32[]{:S(2)}) %copy-start.2) | copy-done | bytes 131096
  10.1 1.0 %states.3 = (bf16[128,1024]{1,0:T(8,128)(2,1)S(1)}, bf16[128,256]{1,0:T(8,128)(2,1)S(1)}, f32[128,1024]{1,0:T(8,128)S(1)}, bf16[128,1024]{1,0:T(8,128)(2,1)S(1)}, f32[1,1024]{1,0:T(1,128)S(1)}) custom-call(bf16[128,2048]{1,0:T(8,128)(2,1)S(1)} %copy-done, bf16[8,2560]{1,0:T(8,128)(2,1)S(1)} %collective-permute-done.tail_x.tail_bc, ...), custom_call_target="tpu_custom_call" | custom-call | tf_op jit(solution)/shard_map/states/pallas_call | solution.py:199
  11.1 0.7 %collective-permute-start.4 = (bf16[128,1024]{1,0:T(8,128)(2,1)S(1)}, bf16[128,1024]{1,0:T(8,128)(2,1)S(1)}, u32[]{:S(2)}, u32[]{:S(2)}) collective-permute-start(bf16[128,1024]{1,0:T(8,128)(2,1)S(1)} %get-tuple-element.30), channel_id=1, source_target_pairs={{0,4},{1,5},{2,6},{3,7},{16,20},{17,21},{18,22},{19,23}} | collective-permute-start | bytes 786440 | tf_op jit(solution)/shard_map/ppermute | solution.py:148
  11.8 1.0 %states.2 = (bf16[128,1024]{1,0:T(8,128)(2,1)S(1)}, bf16[128,256]{1,0:T(8,128)(2,1)S(1)}, f32[128,1024]{1,0:T(8,128)S(1)}, bf16[128,1024]{1,0:T(8,128)(2,1)S(1)}, f32[1,1024]{1,0:T(1,128)S(1)}) custom-call(bf16[128,2048]{1,0:T(8,128)(2,1)S(1)} %copy-done, bf16[8,2560]{1,0:T(8,128)(2,1)S(1)} %collective-permute-done.tail_x.tail_bc, ...), custom_call_target="tpu_custom_call" | custom-call | tf_op jit(solution)/shard_map/states/pallas_call | solution.py:199
  12.9 0.7 %collective-permute-start.1 = (bf16[128,1024]{1,0:T(8,128)(2,1)S(1)}, bf16[128,1024]{1,0:T(8,128)(2,1)S(1)}, u32[]{:S(2)}, u32[]{:S(2)}) collective-permute-start(bf16[128,1024]{1,0:T(8,128)(2,1)S(1)} %get-tuple-element.23), channel_id=1, source_target_pairs={{0,4},{1,5},{2,6},{3,7},{16,20},{17,21},{18,22},{19,23}} | collective-permute-start | bytes 786440 | tf_op jit(solution)/shard_map/ppermute | solution.py:148
  13.6 0.0 collective-permute-done.4.refs_0_
  13.6 0.1 add_convert_fusion.1
  13.6 0.7 %collective-permute-start.5 = (bf16[128,1024]{1,0:T(8,128)(2,1)S(1)}, bf16[128,1024]{1,0:T(8,128)(2,1)S(1)}, u32[]{:S(2)}, u32[]{:S(2)}) collective-permute-start(bf16[128,1024]{1,0:T(8,128)(2,1)S(1)} %add_convert_fusion.1), channel_id=1, source_target_pairs={{4,8},{5,9},{6,10},{7,11},{20,24},{21,25},{22,26},{23,27}} | collective-permute-start | bytes 786440 | tf_op jit(solution)/shard_map/ppermute | solution.py:148
  14.3 0.0 collective-permute-done.1.refs_0_
  14.3 0.1 add_convert_fusion.3
  14.4 0.7 %collective-permute-start.2 = (bf16[128,1024]{1,0:T(8,128)(2,1)S(1)}, bf16[128,1024]{1,0:T(8,128)(2,1)S(1)}, u32[]{:S(2)}, u32[]{:S(2)}) collective-permute-start(bf16[128,1024]{1,0:T(8,128)(2,1)S(1)} %add_convert_fusion.3), channel_id=1, source_target_pairs={{4,8},{5,9},{6,10},{7,11},{20,24},{21,25},{22,26},{23,27}} | collective-permute-start | bytes 786440 | tf_op jit(solution)/shard_map/ppermute | solution.py:148
  15.1 0.0 collective-permute-done.5.refs_1_
  15.1 0.1 add_convert_fusion
  15.2 0.0 copy-start.1
  15.2 1.4 %collective-permute-start.6 = (bf16[128,1024]{1,0:T(8,128)(2,1)S(1)}, bf16[128,1024]{1,0:T(8,128)(2,1)S(1)}, u32[]{:S(2)}, u32[]{:S(2)}) collective-permute-start(bf16[128,1024]{1,0:T(8,128)(2,1)S(1)} %add_convert_fusion), channel_id=1, source_target_pairs={{8,12},{9,13},{10,14},{11,15},{24,28},{25,29},{26,30},{27,31}} | collective-permute-start | bytes 786440 | tf_op jit(solution)/shard_map/ppermute | solution.py:148
  16.7 0.0 collective-permute-done.2.refs_1_
  16.7 0.1 add_convert_fusion.2
  16.8 1.3 %collective-permute-start.3 = (bf16[128,1024]{1,0:T(8,128)(2,1)S(1)}, bf16[128,1024]{1,0:T(8,128)(2,1)S(1)}, u32[]{:S(2)}, u32[]{:S(2)}) collective-permute-start(bf16[128,1024]{1,0:T(8,128)(2,1)S(1)} %add_convert_fusion.2), channel_id=1, source_target_pairs={{8,12},{9,13},{10,14},{11,15},{24,28},{25,29},{26,30},{27,31}} | collective-permute-start | bytes 786440 | tf_op jit(solution)/shard_map/ppermute | solution.py:148
  18.1 0.0 copy-start.8
  18.1 0.0 copy-done.1
  18.1 0.6 %copy-done.8 = f32[32]{0:T(128)S(1)} copy-done((f32[32]{0:T(128)S(1)}, f32[32]{0:T(128)}, u32[]{:S(2)}) %copy-start.8) | copy-done | bytes 152
  18.7 1.0 %intra.3 = (f32[128,1024]{1,0:T(8,128)S(1)}, f32[128,1024]{1,0:T(8,128)S(1)}) custom-call(bf16[128,1024]{1,0:T(8,128)(2,1)S(1)} %get-tuple-element.27.x_act, bf16[128,256]{1,0:T(8,128)(2,1)S(1)} %get-tuple-element.26.bc_act.c, bf16[128,2048]{1,0:T(8,128)(2,1)S(1)} %copy-done.1, f32[32,128]{1,0:T(8,128)S(1)} %bitcast.11, f32[1,32]{1,0:T(1,128)S(1)} %bitcast.21, ...), custom_call_target="tpu_custom_call" | custom-call | flops 67108864 | bytes 1572864 | tf_op jit(solution)/shard_map/intra/pallas_call | solution.py:238
  19.8 0.0 copy-start.6
  19.8 1.0 %intra.2 = (f32[128,1024]{1,0:T(8,128)S(1)}, f32[128,1024]{1,0:T(8,128)S(1)}) custom-call(bf16[128,1024]{1,0:T(8,128)(2,1)S(1)} %get-tuple-element.20.x_act, bf16[128,256]{1,0:T(8,128)(2,1)S(1)} %get-tuple-element.19.bc_act.c, bf16[128,2048]{1,0:T(8,128)(2,1)S(1)} %copy-done.1, f32[32,128]{1,0:T(8,128)S(1)} %bitcast.12, f32[1,32]{1,0:T(1,128)S(1)} %bitcast.22, ...), custom_call_target="tpu_custom_call" | custom-call | flops 67108864 | bytes 1572864 | tf_op jit(solution)/shard_map/intra/pallas_call | solution.py:238
  20.8 19.1 %collective-permute-done.6.refs_2_ = bf16[128,1024]{1,0:T(8,128)(2,1)S(1)} collective-permute-done((bf16[128,1024]{1,0:T(8,128)(2,1)S(1)}, bf16[128,1024]{1,0:T(8,128)(2,1)S(1)}, u32[]{:S(2)}, u32[]{:S(2)}) %collective-permute-start.6) | collective-permute-done | bytes 262176 | tf_op jit(solution)/shard_map/ppermute | solution.py:148
  39.9 0.0 copy-done.6
  39.9 1.0 %outputs.2.refs_3_ = bf16[128,2048]{1,0:T(8,128)(2,1)} custom-call(bf16[128,256]{1,0:T(8,128)(2,1)S(1)} %get-tuple-element.26.bc_act.c, f32[128,1024]{1,0:T(8,128)S(1)} %get-tuple-element.28.y_part, f32[128,1024]{1,0:T(8,128)S(1)} %get-tuple-element.29.lead, f32[1,2048]{1,0:T(1,128)S(1)} %bitcast.13, bf16[128,1024]{1,0:T(8,128)(2,1)S(1)} %collective-permute-done.4.refs_0_, ...), custom_call_target="tpu_custom_call" | custom-call | tf_op jit(solution)/shard_map/outputs/pallas_call | solution.py:277
  41.0 1.8 %collective-permute-done.3.refs_2_ = bf16[128,1024]{1,0:T(8,128)(2,1)S(1)} collective-permute-done((bf16[128,1024]{1,0:T(8,128)(2,1)S(1)}, bf16[128,1024]{1,0:T(8,128)(2,1)S(1)}, u32[]{:S(2)}, u32[]{:S(2)}) %collective-permute-start.3) | collective-permute-done | bytes 262176 | tf_op jit(solution)/shard_map/ppermute | solution.py:148
  42.7 1.1 %outputs.3 = bf16[128,2048]{1,0:T(8,128)(2,1)} custom-call(bf16[128,256]{1,0:T(8,128)(2,1)S(1)} %get-tuple-element.19.bc_act.c, f32[128,1024]{1,0:T(8,128)S(1)} %get-tuple-element.21.y_part, f32[128,1024]{1,0:T(8,128)S(1)} %get-tuple-element.22.lead, f32[1,2048]{1,0:T(1,128)S(1)} %bitcast.14, ...), custom_call_target="tpu_custom_call", output_to_operand_aliasing={{}: (7, {})} | custom-call | tf_op jit(solution)/shard_map/outputs/pallas_call | solution.py:277
  (2 shorter events, 0.0 us)
Async XLA Ops:
  0.7 0.8 %slice-start = ((bf16[128,2048]{1,0:T(8,128)(2,1)}), bf16[8,2048]{1,0:T(8,128)(2,1)S(1)}, s32[]{:S(2)}) async-start(bf16[128,2048]{1,0:T(8,128)(2,1)} %x.3), calls=%async_computation | async-start | bytes 65536 | tf_op jit(solution)/shard_map/slice | solution.py:182
  1.5 6.0 %copy-start.3 = (f32[128,32]{0,1:T(8,128)S(1)}, f32[128,32]{0,1:T(8,128)}, u32[]{:S(2)}) copy-start(f32[128,32]{0,1:T(8,128)} %param.12) | copy-start | bytes 49156
  1.5 6.0 %copy-start.4 = (f32[4,2048]{1,0:T(4,128)S(1)}, f32[4,2048]{1,0:T(4,128)}, u32[]{:S(2)}) copy-start(f32[4,2048]{1,0:T(4,128)} %taps_x.3) | copy-start | bytes 98308
  1.5 6.0 %copy-start.5 = (f32[4,2,256]{2,1,0:T(2,128)S(1)}, f32[4,2,256]{2,1,0:T(2,128)}, u32[]{:S(2)}) copy-start(f32[4,2,256]{2,1,0:T(2,128)} %taps_bc.3) | copy-start | bytes 24580
  1.5 6.0 %collective-permute-start = (bf16[8,2560]{1,0:T(8,128)(2,1)S(1)}, bf16[8,2560]{1,0:T(8,128)(2,1)S(1)}, u32[]{:S(2)}, u32[]{:S(2)}) collective-permute-start(bf16[8,2560]{1,0:T(8,128)(2,1)S(1)} %pad_maximum_fusion), channel_id=1, source_target_pairs={{0,4},{4,8},{8,12},{1,5},{5,9},{9,13},{2,6},{6,10},{10,14},{3,7},{... | collective-permute-start | bytes 122888 | tf_op jit(solution)/shard_map/ppermute | solution.py:184
  7.5 0.7 %copy-start.7 = (f32[32]{0:T(128)S(1)}, f32[32]{0:T(128)}, u32[]{:S(2)}) copy-start(f32[32]{0:T(128)} %param.15) | copy-start | bytes 388
  8.2 1.0 %copy-start = (bf16[128,2048]{1,0:T(8,128)(2,1)S(1)}, bf16[128,2048]{1,0:T(8,128)(2,1)}, u32[]{:S(2)}) copy-start(bf16[128,2048]{1,0:T(8,128)(2,1)} %x.3) | copy-start | bytes 1572868
  9.2 0.9 %copy-start.2 = (bf16[128,2,256]{2,1,0:T(2,128)(2,1)S(1)}, bf16[128,2,256]{2,1,0:T(2,128)(2,1)}, u32[]{:S(2)}) copy-start(bf16[128,2,256]{2,1,0:T(2,128)(2,1)} %bc.3) | copy-start | bytes 393220
  11.1 2.4 %collective-permute-start.4 = (bf16[128,1024]{1,0:T(8,128)(2,1)S(1)}, bf16[128,1024]{1,0:T(8,128)(2,1)S(1)}, u32[]{:S(2)}, u32[]{:S(2)}) collective-permute-start(bf16[128,1024]{1,0:T(8,128)(2,1)S(1)} %get-tuple-element.30), channel_id=1, source_target_pairs={{0,4},{1,5},{2,6},{3,7},{16,20},{17,21},{18,22},{19,23}} | collective-permute-start | bytes 786440 | tf_op jit(solution)/shard_map/ppermute | solution.py:148
  12.9 1.5 %collective-permute-start.1 = (bf16[128,1024]{1,0:T(8,128)(2,1)S(1)}, bf16[128,1024]{1,0:T(8,128)(2,1)S(1)}, u32[]{:S(2)}, u32[]{:S(2)}) collective-permute-start(bf16[128,1024]{1,0:T(8,128)(2,1)S(1)} %get-tuple-element.23), channel_id=1, source_target_pairs={{0,4},{1,5},{2,6},{3,7},{16,20},{17,21},{18,22},{19,23}} | collective-permute-start | bytes 786440 | tf_op jit(solution)/shard_map/ppermute | solution.py:148
  13.6 1.5 %collective-permute-start.5 = (bf16[128,1024]{1,0:T(8,128)(2,1)S(1)}, bf16[128,1024]{1,0:T(8,128)(2,1)S(1)}, u32[]{:S(2)}, u32[]{:S(2)}) collective-permute-start(bf16[128,1024]{1,0:T(8,128)(2,1)S(1)} %add_convert_fusion.1), channel_id=1, source_target_pairs={{4,8},{5,9},{6,10},{7,11},{20,24},{21,25},{22,26},{23,27}} | collective-permute-start | bytes 786440 | tf_op jit(solution)/shard_map/ppermute | solution.py:148
  14.4 2.2 %collective-permute-start.2 = (bf16[128,1024]{1,0:T(8,128)(2,1)S(1)}, bf16[128,1024]{1,0:T(8,128)(2,1)S(1)}, u32[]{:S(2)}, u32[]{:S(2)}) collective-permute-start(bf16[128,1024]{1,0:T(8,128)(2,1)S(1)} %add_convert_fusion.3), channel_id=1, source_target_pairs={{4,8},{5,9},{6,10},{7,11},{20,24},{21,25},{22,26},{23,27}} | collective-permute-start | bytes 786440 | tf_op jit(solution)/shard_map/ppermute | solution.py:148
  15.2 2.9 %copy-start.1 = (bf16[128,2048]{1,0:T(8,128)(2,1)S(1)}, bf16[128,2048]{1,0:T(8,128)(2,1)}, u32[]{:S(2)}) copy-start(bf16[128,2048]{1,0:T(8,128)(2,1)} %z.3) | copy-start | bytes 1572868
  15.2 24.7 %collective-permute-start.6 = (bf16[128,1024]{1,0:T(8,128)(2,1)S(1)}, bf16[128,1024]{1,0:T(8,128)(2,1)S(1)}, u32[]{:S(2)}, u32[]{:S(2)}) collective-permute-start(bf16[128,1024]{1,0:T(8,128)(2,1)S(1)} %add_convert_fusion), channel_id=1, source_target_pairs={{8,12},{9,13},{10,14},{11,15},{24,28},{25,29},{26,30},{27,31}} | collective-permute-start | bytes 786440 | tf_op jit(solution)/shard_map/ppermute | solution.py:148
  16.8 26.0 %collective-permute-start.3 = (bf16[128,1024]{1,0:T(8,128)(2,1)S(1)}, bf16[128,1024]{1,0:T(8,128)(2,1)S(1)}, u32[]{:S(2)}, u32[]{:S(2)}) collective-permute-start(bf16[128,1024]{1,0:T(8,128)(2,1)S(1)} %add_convert_fusion.2), channel_id=1, source_target_pairs={{8,12},{9,13},{10,14},{11,15},{24,28},{25,29},{26,30},{27,31}} | collective-permute-start | bytes 786440 | tf_op jit(solution)/shard_map/ppermute | solution.py:148
  18.1 0.7 %copy-start.8 = (f32[32]{0:T(128)S(1)}, f32[32]{0:T(128)}, u32[]{:S(2)}) copy-start(f32[32]{0:T(128)} %param.16) | copy-start | bytes 388
  19.8 20.2 %copy-start.6 = (f32[2048]{0:T(1024)S(1)}, f32[2048]{0:T(1024)}, u32[]{:S(2)}) copy-start(f32[2048]{0:T(1024)} %param.17) | copy-start | bytes 24580

commit v2 on v1

v2 whole, which is shorter than its diff:
```python
import functools

import jax
import jax.numpy as jnp
from jax import lax
from jax.experimental import pallas as pl
from jax.experimental.pallas import tpu as pltpu
from jax.sharding import PartitionSpec as P

EPS = 1e-05
F32 = jnp.float32
BF16 = jnp.bfloat16
CHAIN_MOST = 4
SLICES = 3
CHUNK = 256
LANES = 128


def silu(u):
    return 0.5 * u * (1.0 + jnp.tanh(0.5 * u))


def softplus(v):
    return jnp.maximum(v, 0.0) + jnp.log1p(jnp.exp(-jnp.abs(v)))


def halves(v, count, axis):
    parts = []
    for _ in range(count - 1):
        part = v.astype(BF16)
        parts.append(part)
        v = v - part.astype(F32)
    parts.append(v.astype(BF16))
    return jnp.concatenate(parts, axis=axis)


def spread(per_head, head_dim, count):
    heads = per_head.shape[0]
    rows = lax.broadcasted_iota(jnp.int32, (heads * count, heads * head_dim), 0)
    cols = lax.broadcasted_iota(jnp.int32, (heads * count, heads * head_dim), 1)
    pick = (rows % heads == cols // head_dim).astype(F32).astype(BF16)
    return lax.dot_general(
        halves(per_head, count, 0), pick, (((0,), (0,)), ((), ())), preferred_element_type=F32
    )


def spread_row(column, head_dim):
    heads = column.shape[0]
    rows = lax.broadcasted_iota(jnp.int32, (heads, heads * head_dim), 0)
    cols = lax.broadcasted_iota(jnp.int32, (heads, heads * head_dim), 1)
    return jnp.sum(jnp.where(rows == cols // head_dim, column, 0.0), axis=0, keepdims=True)


def as_column(row, start, heads):
    every = row.shape[1]
    rows = lax.broadcasted_iota(jnp.int32, (heads, every), 0)
    cols = lax.broadcasted_iota(jnp.int32, (heads, every), 1)
    return jnp.sum(jnp.where(cols == rows + start, row, 0.0), axis=1, keepdims=True)


def conv_act(series, tail, taps):
    count = taps.shape[0]
    above = tail.shape[0]
    padded = jnp.concatenate([tail, series], axis=0)
    total = taps[count - 1 : count] * series
    for back in range(1, count):
        total = total + taps[count - 1 - back : count - back] * pltpu.roll(padded, back, 0)[above:]
    return silu(total).astype(BF16)


def rates(dt_raw, a_log_row, start):
    heads, tokens = dt_raw.shape
    dt = softplus(dt_raw)
    rate = -jnp.exp(as_column(a_log_row, start, heads)) * dt
    earlier = lax.broadcasted_iota(jnp.int32, (tokens, tokens), 0)
    later = lax.broadcasted_iota(jnp.int32, (tokens, tokens), 1)
    upto = (earlier <= later).astype(F32)
    cum = jnp.dot(rate, upto, precision=lax.Precision.HIGHEST, preferred_element_type=F32)
    return dt, cum


def started(pairs, sems):
    copies = [pltpu.make_async_copy(src, dst, sems.at[i]) for i, (src, dst) in enumerate(pairs)]
    for copy in copies:
        copy.start()
    return copies


def emit_states(head_dim, x, tail_x, bc, tail_bc, taps_x, taps_bc, dt_raw, a_log, wide, emit):
    dt, cum = rates(dt_raw[...], a_log[...], 0)
    end = cum[:, -1:]
    tail_decay = jnp.exp(end - cum) * dt
    groups = bc.shape[1]
    state_dim = bc.shape[2] // 2
    cols = x.shape[1] // groups
    heads = dt.shape[0] // groups
    for g in range(groups):
        b = conv_act(
            bc[:, :, :state_dim].astype(F32)[:, g],
            tail_bc(g),
            taps_bc[:, :, :state_dim][:, g],
        )
        b_t = b.astype(F32).T.astype(BF16)
        wide[...] = spread(tail_decay[g * heads : (g + 1) * heads], head_dim, 2)
        for at in range(0, cols, CHUNK):
            cut = slice(g * cols + at, g * cols + at + CHUNK)
            act = conv_act(x[:, cut].astype(F32), tail_x(cut), taps_x[:, cut])
            scaled = (wide[:, at : at + CHUNK] * act.astype(F32)).astype(BF16)
            emit(cut, jnp.dot(b_t, scaled, preferred_element_type=F32))
    return end


def first_kernel(head_dim, cuts, *refs):
    active, x_hbm, bc_hbm, taps_x_hbm, taps_bc_hbm, dt_hbm, a_hbm = refs[:7]
    pack, halves_out = refs[7], refs[8 : 8 + len(cuts)]
    x, bc, taps_x, taps_bc, dt_raw, a_log, last_x, last_bc, wide, sems = refs[8 + len(cuts) :]
    tokens, width = x.shape
    rows, groups, both = last_bc.shape
    first = active[0] == 1
    ends = started(
        [
            (x_hbm.at[pl.ds(tokens - rows, rows)], last_x),
            (bc_hbm.at[pl.ds(tokens - rows, rows)], last_bc),
        ],
        sems,
    )
    inner = [(x_hbm, x), (bc_hbm, bc), (taps_x_hbm, taps_x), (taps_bc_hbm, taps_bc),
             (dt_hbm, dt_raw), (a_hbm, a_log)]
    rest = sems.at[pl.ds(2, len(inner))]

    @pl.when(first)
    def _():
        started(inner, rest)

    for copy in ends:
        copy.wait()
    pack[:, :width] = last_x[...]
    wide_bc = last_bc[...].astype(F32)
    for g in range(groups):
        pack[:, width + g * both : width + (g + 1) * both] = wide_bc[:, g].astype(BF16)

    @pl.when(first)
    def _():
        for i, (src, dst) in enumerate(inner):
            pltpu.make_async_copy(src, dst, rest.at[i]).wait()

        def emit(cut, total):
            for (low, high), out in zip(cuts, halves_out):
                begin, stop = max(low, cut.start), min(high, cut.stop)
                if begin < stop:
                    out[:, begin - low : stop - low] = total[
                        :, begin - cut.start : stop - cut.start
                    ].astype(BF16)

        emit_states(
            head_dim, x,
            lambda cut: jnp.zeros((8, cut.stop - cut.start), F32),
            bc, lambda g: jnp.zeros((8, both // 2), F32),
            taps_x, taps_bc, dt_raw, a_log, wide, emit,
        )


def later_kernel(head_dim, *refs):
    active, got, x_hbm, bc_hbm, taps_x_hbm, taps_bc_hbm, dt_hbm, a_hbm = refs[:8]
    state, decay = refs[8:10]
    x, bc, taps_x, taps_bc, dt_raw, a_log, wide, sems = refs[10:]
    width = x.shape[1]
    both = bc.shape[2]
    pairs = [(x_hbm, x), (bc_hbm, bc), (taps_x_hbm, taps_x), (taps_bc_hbm, taps_bc),
             (dt_hbm, dt_raw), (a_hbm, a_log)]

    @pl.when(active[0] == 1)
    def _():
        for copy in started(pairs, sems):
            copy.wait()

        def emit(cut, total):
            state[:, cut] = total

        def tail_bc(g):
            at = width + g * both
            return got[:, at : at + both // 2].astype(F32)[-8:]

        end = emit_states(
            head_dim, x, lambda cut: got[:, cut].astype(F32)[-8:], bc, tail_bc,
            taps_x, taps_bc, dt_raw, a_log, wide, emit,
        )
        decay[...] = spread_row(jnp.exp(end), head_dim)


def intra_kernel(
    head_dim, x, got, bc, z, taps_x, taps_bc, dt_raw, a_log, d_skip, y_part, lead, c_act, wide
):
    dt, cum = rates(dt_raw[...], a_log[...], 0)
    tokens, width = x.shape
    groups, both = bc.shape[1:]
    state_dim = both // 2
    cols = width // groups
    heads = dt.shape[0] // groups
    cum_t = cum.T
    leading = jnp.exp(cum)
    skip = spread_row(as_column(d_skip[...], 0, dt.shape[0]), head_dim)
    t_at = lax.broadcasted_iota(jnp.int32, (tokens, tokens), 0)
    s_at = lax.broadcasted_iota(jnp.int32, (tokens, tokens), 1)
    pair = 2 * head_dim
    for g in range(groups):
        at = width + g * both
        bc_act = conv_act(
            bc[...].astype(F32)[:, g], got[:, at : at + both].astype(F32)[-8:], taps_bc[...][:, g]
        )
        b, c = bc_act[:, :state_dim], bc_act[:, state_dim:]
        c_act[:, g * state_dim : (g + 1) * state_dim] = c
        inner = lax.dot_general(c, b, (((1,), (1,)), ((), ())), preferred_element_type=F32)
        inner = jnp.where(t_at >= s_at, inner, 0.0)
        wide[...] = spread(leading[g * heads : (g + 1) * heads], head_dim, 2)
        for first in range(0, heads, 2):
            here = first * head_dim
            cut = slice(g * cols + here, g * cols + here + pair)
            act = conv_act(x[:, cut].astype(F32), got[:, cut].astype(F32)[-8:], taps_x[:, cut])
            lane = lax.broadcasted_iota(jnp.int32, act.shape, 1)
            full = act.astype(F32)
            blocks = jnp.concatenate(
                [jnp.where(lane < head_dim, full, 0.0), jnp.where(lane < head_dim, 0.0, full)],
                axis=0,
            ).astype(BF16)
            weights = []
            for h in (g * heads + first, g * heads + first + 1):
                gap = jnp.minimum(cum_t[:, h : h + 1] - cum[h : h + 1, :], 0.0)
                weights.append((jnp.exp(gap) * dt[h : h + 1, :] * inner).astype(BF16))
            y = jnp.dot(jnp.concatenate(weights, axis=1), blocks, preferred_element_type=F32)
            gate = silu(z[:, cut].astype(F32))
            y_part[:, cut] = (y + skip[:, cut] * full) * gate
            lead[:, cut] = wide[:, here : here + pair] * gate


def output_kernel(spans, seen, c, y_part, lead, gain, *refs):
    arrived, out = refs[: len(spans) * seen], refs[-1]
    gated = []
    for i, (low, high, at) in enumerate(spans):
        state = arrived[i * seen][:, low:high]
        for more in arrived[i * seen + 1 : (i + 1) * seen]:
            state = state + more[:, low:high]
        from_state = jnp.dot(c[...], state, preferred_element_type=F32)
        cut = slice(at, at + high - low)
        gated.append(y_part[:, cut] + lead[:, cut] * from_state)
    gated = jnp.concatenate(gated, axis=1)
    mean_sq = jnp.mean(gated * gated, axis=1, keepdims=True)
    out[...] = (gated * lax.rsqrt(mean_sq + EPS) * gain[...]).astype(BF16)


def params(mib):
    return pltpu.CompilerParams(vmem_limit_bytes=mib * 1024 * 1024)


def chain(firsts, state, decay, cuts, devices):
    arrived = [[] for _ in cuts]
    to_send = firsts
    for hop in range(devices - 1):
        came = [lax.ppermute(v, "seq", [(hop, hop + 1)]) for v in to_send]
        for seen, v in zip(arrived, came):
            seen.append(v)
        to_send = [
            (decay[:, low:high] * v.astype(F32) + state[:, low:high]).astype(BF16)
            for (low, high), v in zip(cuts, came)
        ]
    return arrived


def doubling(state, decay, devices):
    def moved(value, distance):
        return lax.ppermute(value, "seq", [(i, i + distance) for i in range(devices - distance)])

    total, decay = moved(state.astype(BF16), 1), moved(decay, 1)
    distance = 1
    while distance < devices - 1:
        came = moved(total, distance)
        total = (decay * came.astype(F32) + total.astype(F32)).astype(BF16)
        decay = decay * moved(decay, distance)
        distance *= 2
    return total


def shards(x_in, bc_in, z_in, dt_raw, conv_x, conv_bc, a_log, d_skip, norm_gain):
    tokens, width = x_in.shape
    groups, both = bc_in.shape[1:]
    state_dim = both // 2
    heads = dt_raw.shape[1]
    head_dim = width // heads
    cols = width // groups
    devices = lax.axis_size("seq")
    place = lax.axis_index("seq")
    rows = 16

    tiles = width // LANES
    edges = [LANES * (tiles * i // SLICES) for i in range(SLICES + 1)]
    cuts = list(zip(edges[:-1], edges[1:]))
    chained = devices <= CHAIN_MOST

    dt_t = dt_raw.T
    a_row = a_log.reshape(1, heads)
    d_row = d_skip.reshape(1, heads)
    gain = norm_gain.reshape(1, width)
    is_first = (place == 0).astype(jnp.int32).reshape(1)
    operands = [x_in, bc_in, conv_x, conv_bc, dt_t, a_row]
    landed = [pltpu.VMEM(v.shape, v.dtype) for v in operands]
    scalar = pl.BlockSpec(memory_space=pltpu.SMEM)
    any_space = [pl.BlockSpec(memory_space=pl.ANY)] * len(operands)

    def column(height, wide, at):
        return pl.BlockSpec((height, wide), lambda i: (0, at))

    def whole(array):
        return pl.BlockSpec(array.shape, lambda i: (0,) * len(array.shape))

    last, *firsts = pl.pallas_call(
        functools.partial(first_kernel, head_dim, cuts),
        out_shape=[jax.ShapeDtypeStruct((rows, width + groups * both), BF16)]
        + [jax.ShapeDtypeStruct((state_dim, high - low), BF16) for low, high in cuts],
        in_specs=[scalar] + any_space,
        scratch_shapes=landed
        + [
            pltpu.VMEM((rows, width), BF16),
            pltpu.VMEM((rows, groups, both), BF16),
            pltpu.VMEM((tokens, cols), F32),
            pltpu.SemaphoreType.DMA((2 + len(operands),)),
        ],
        compiler_params=params(56),
        name="first_states",
    )(is_first, *operands)

    got = lax.ppermute(last, "seq", [(i, i + 1) for i in range(devices - 1)])
    runs = 1 - is_first if chained else jnp.ones((1,), jnp.int32)
    state, decay = pl.pallas_call(
        functools.partial(later_kernel, head_dim),
        out_shape=(
            jax.ShapeDtypeStruct((state_dim, width), F32),
            jax.ShapeDtypeStruct((1, width), F32),
        ),
        in_specs=[scalar, pl.BlockSpec(memory_space=pltpu.VMEM)] + any_space,
        scratch_shapes=landed
        + [pltpu.VMEM((tokens, cols), F32), pltpu.SemaphoreType.DMA((len(operands),))],
        compiler_params=params(56),
        name="later_states",
    )(runs, got, *operands)

    if chained:
        arrived = chain(firsts, state, decay, cuts, devices)
    else:
        total = doubling(state, decay, devices)
        arrived = [[total[:, low:high]] for low, high in cuts]

    y_part, lead, c_act = pl.pallas_call(
        functools.partial(intra_kernel, head_dim),
        out_shape=(
            jax.ShapeDtypeStruct((tokens, width), F32),
            jax.ShapeDtypeStruct((tokens, width), F32),
            jax.ShapeDtypeStruct((tokens, groups * state_dim), BF16),
        ),
        scratch_shapes=[pltpu.VMEM((tokens, cols), F32)],
        compiler_params=params(32),
        cost_estimate=pl.CostEstimate(
            flops=4 * tokens * tokens * width,
            bytes_accessed=12 * tokens * width,
            transcendentals=tokens * tokens * heads,
        ),
        name="intra",
    )(x_in, got, bc_in, z_in, conv_x, conv_bc, dt_t, a_row, d_row)

    out = None
    for g in range(groups):
        spans, taken = [], []
        for (low, high), seen in zip(cuts, arrived):
            begin, stop = max(low, g * cols), min(high, (g + 1) * cols)
            if begin < stop:
                spans.append((begin - low, stop - low, begin - g * cols))
                taken += seen
        inputs = [c_act, y_part, lead, gain] + taken
        specs = [
            column(tokens, state_dim, g),
            column(tokens, cols, g),
            column(tokens, cols, g),
            column(1, cols, g),
        ] + [whole(v) for v in taken]
        aliases = {}
        if out is not None:
            aliases = {len(inputs): 0}
            inputs.append(out)
            specs.append(pl.BlockSpec(memory_space=pl.ANY))
        out = pl.pallas_call(
            functools.partial(output_kernel, spans, len(arrived[0])),
            out_shape=jax.ShapeDtypeStruct((tokens, width), BF16),
            in_specs=specs,
            out_specs=column(tokens, cols, g),
            grid=(1,),
            input_output_aliases=aliases,
            compiler_params=params(32),
            name="outputs",
        )(*inputs)
    return out


def solution(mesh):
    return jax.shard_map(
        shards,
        mesh=mesh,
        in_specs=(
            P(("groups", "seq"), "head"),
            P(("groups", "seq"), "head", None),
            P(("groups", "seq"), "head"),
            P(("groups", "seq"), "head"),
            P(None, "head"),
            P(None, "head", None),
            P("head"),
            P("head"),
            P("head"),
        ),
        out_specs=P(("groups", "seq"), "head"),
        check_vma=False,
    )
```

time: 44.2 us -> 45 us (1.018)
  waiting for transfers between devices: 25.5 us -> 20.1 us
  Pallas kernels: 6.24 us -> 10.8 us
  local copies, waits for them, and re-layouts: 4.72 us -> 1.48 us
  starting transfers between devices: 6.85 us -> 9.33 us
  other arithmetic: 0.32 us -> 2.45 us
    ppermute x7 -> x10, waiting for transfers between devices: 25.5 us -> 20.1 us  [the longest x9 16.9 us: chain(): came = [lax.ppermute(v, 'seq', [(hop, hop + 1)]) for v in to_send]]
    pallas_call x6 -> x5, Pallas kernels: 6.24 us -> 10.8 us  [the longest x1 4.62 us: shards(): pl.pallas_call(functools.partial(later_kernel, head_dim), out_shape=(jax....]
    unnamed x20 -> x26, local copies, waits for them, and re-layouts: 3.96 us -> 0.7 us
    ppermute x7 -> x10, starting transfers between devices: 6.85 us -> 9.33 us  [the longest x9 8.04 us: chain(): came = [lax.ppermute(v, 'seq', [(hop, hop + 1)]) for v in to_send]]
    convert_element_type x4, other arithmetic: 0.31 us -> 2.45 us  [chain(): (decay[:, low:high] * v.astype(F32) + state[:, low:high]).astype(BF16)]
  transfers between devices with their start and end apart: 7 -> 10, of which waited for: 3 -> 3; matrix products, arithmetic and copies ran while one was open for 1% -> 7% of each run, Pallas kernels for 9% -> 18%
where the time goes in v2:
time: 45 us; the launch traced here: 44.5 us
  waiting for transfers between devices  20.1 us (45%)
  Pallas kernels  10.8 us (24%)
  starting transfers between devices  9.33 us (21%)
  other arithmetic  2.45 us (5%)
  local copies, waits for them, and re-layouts  1.48 us (3%)
    ppermute x9, waiting for transfers between devices, chain(): came = [lax.ppermute(v, 'seq', [(hop, hop + 1)]) for v in to_send]  16.9 us
    ppermute x9, starting transfers between devices, chain(): came = [lax.ppermute(v, 'seq', [(hop, hop + 1)]) for v in to_send]  8.04 us
    pallas_call x1, Pallas kernels, shards(): pl.pallas_call(functools.partial(later_kernel, head_dim), out_shape=(jax....  4.62 us
    ppermute x1, waiting for transfers between devices, shards(): got = lax.ppermute(last, 'seq', [(i, i + 1) for i in range(devices - 1)])  3.2 us
    convert_element_type x4, other arithmetic, chain(): (decay[:, low:high] * v.astype(F32) + state[:, low:high]).astype(BF16)  2.45 us
    pallas_call x1, Pallas kernels, shards(): pl.pallas_call(functools.partial(intra_kernel, head_dim), out_shape=(jax....  2.26 us
    pallas_call x2, Pallas kernels, shards(): pl.pallas_call(functools.partial(output_kernel, spans, len(arrived[0])),...  2.12 us
    pallas_call x1, Pallas kernels, shards(): pl.pallas_call(functools.partial(first_kernel, head_dim, cuts), out_shape...  1.77 us
  transfers between devices with their start and end apart: 10, of which 3 were waited for; matrix products, arithmetic and copies ran while one was open for 7% of the time, Pallas kernels for 18%

profile of v2, /device:TPU:30, one launch (start us, length us, event | category | flops | bytes accessed | tf_op | source)
XLA Modules:
  0.0 44.5 jit_solution(13262814915881397606)
XLA Ops:
  0.0 1.8 %first_states.1 = (bf16[16,2560]{1,0:T(8,128)(2,1)}, bf16[128,640]{1,0:T(8,128)(2,1)}, bf16[128,640]{1,0:T(8,128)(2,1)}, bf16[128,768]{1,0:T(8,128)(2,1)}) custom-call(s32[1]{0:T(128)} %bitcast.refs_0_, bf16[128,2048]{1,0:T(8,128)(2,1)} %refs_2_.3, bf16[128,2,256]{2,1,0:T(2,128)(2,1)} %refs_3_.3, f32[4,2048]{1,0:T(4,128)} %refs_4_.3, f32[4,2,256]{2,1,0:T(2,128)} %refs_5_.1, ...), custom_call_target="tpu_custom_call" | custom-call | tf_op jit(solution)/shard_map/first_states/pallas_call | solution.py:315
  1.8 1.3 %collective-permute-start = (bf16[16,2560]{1,0:T(8,128)(2,1)}, bf16[16,2560]{1,0:T(8,128)(2,1)S(1)}, u32[]{:S(2)}, u32[]{:S(2)}) collective-permute-start(bf16[16,2560]{1,0:T(8,128)(2,1)} %get-tuple-element.14), channel_id=1, source_target_pairs={{0,4},{4,8},{8,12},{1,5},{5,9},{9,13},{2,6},{6,10},{10,14},{3,7},{... | collective-permute-start | bytes 245768 | tf_op jit(solution)/shard_map/ppermute | solution.py:331
  3.1 0.7 %collective-permute-start.1 = (bf16[128,640]{1,0:T(8,128)(2,1)}, bf16[128,640]{1,0:T(8,128)(2,1)S(1)}, u32[]{:S(2)}, u32[]{:S(2)}) collective-permute-start(bf16[128,640]{1,0:T(8,128)(2,1)} %get-tuple-element.18), channel_id=1, source_target_pairs={{0,4},{1,5},{2,6},{3,7},{16,20},{17,21},{18,22},{19,23}} | collective-permute-start | bytes 491528 | tf_op jit(solution)/shard_map/ppermute | solution.py:259
  3.8 0.7 %collective-permute-start.7 = (bf16[128,640]{1,0:T(8,128)(2,1)}, bf16[128,640]{1,0:T(8,128)(2,1)S(1)}, u32[]{:S(2)}, u32[]{:S(2)}) collective-permute-start(bf16[128,640]{1,0:T(8,128)(2,1)} %get-tuple-element.22), channel_id=1, source_target_pairs={{0,4},{1,5},{2,6},{3,7},{16,20},{17,21},{18,22},{19,23}} | collective-permute-start | bytes 491528 | tf_op jit(solution)/shard_map/ppermute | solution.py:259
  4.4 0.7 %collective-permute-start.4 = (bf16[128,768]{1,0:T(8,128)(2,1)}, bf16[128,768]{1,0:T(8,128)(2,1)S(1)}, u32[]{:S(2)}, u32[]{:S(2)}) collective-permute-start(bf16[128,768]{1,0:T(8,128)(2,1)} %get-tuple-element.21), channel_id=1, source_target_pairs={{0,4},{1,5},{2,6},{3,7},{16,20},{17,21},{18,22},{19,23}} | collective-permute-start | bytes 589832 | tf_op jit(solution)/shard_map/ppermute | solution.py:259
  5.1 3.2 %collective-permute-done.got.refs_1_ = bf16[16,2560]{1,0:T(8,128)(2,1)S(1)} collective-permute-done((bf16[16,2560]{1,0:T(8,128)(2,1)}, bf16[16,2560]{1,0:T(8,128)(2,1)S(1)}, u32[]{:S(2)}, u32[]{:S(2)}) %collective-permute-start) | collective-permute-done | bytes 81952 | tf_op jit(solution)/shard_map/ppermute | solution.py:331
  8.3 0.6 %copy-done.3 = bf16[16,2560]{1,0:T(8,128)(2,1)} copy-done((bf16[16,2560]{1,0:T(8,128)(2,1)}, bf16[16,2560]{1,0:T(8,128)(2,1)S(1)}, u32[]{:S(2)}) %copy-start.3) | copy-done | bytes 81944
  9.0 4.6 %later_states.1 = (f32[128,2048]{1,0:T(8,128)}, f32[1,2048]{1,0:T(1,128)}) custom-call(s32[1]{0:T(128)S(6)} %sub.3.refs_0_, bf16[16,2560]{1,0:T(8,128)(2,1)} %copy-done.3, bf16[128,2048]{1,0:T(8,128)(2,1)} %refs_2_.3, bf16[128,2,256]{2,1,0:T(2,128)(2,1)} %refs_3_.3, f32[4,2048]{1,0:T(4,128)} %refs_4_.3, f32[4,2,256]{2,1,0:T(2,128)} %refs_5_.1, ...), custom_call_target="tpu_custom_call" | custom-call | tf_op jit(solution)/shard_map/later_states/pallas_call | solution.py:333
  13.6 0.0 copy-start.12
  13.6 0.8 %slice_reduce_fusion = f32[768]{0:T(1024)S(1)} fusion(f32[1,2048]{1,0:T(1,128)} %get-tuple-element.19), kind=kLoop, calls=%fused_computation.6 | loop fusion | bytes 6144 | tf_op jit(solution)/shard_map/slice | solution.py:263
  14.4 0.0 copy-done.12
  14.4 0.0 collective-permute-done.4.refs_3_
  14.4 0.0 copy-start.11
  14.4 1.1 %add_convert_fusion.1 = bf16[128,768]{1,0:T(8,128)(2,1)S(1)} fusion(bf16[128,768]{1,0:T(8,128)(2,1)S(1)} %collective-permute-done.4.refs_3_, f32[128,2048]{1,0:T(8,128)} %get-tuple-element.20, f32[768]{0:T(1024)S(1)} %slice_reduce_fusion), kind=kLoop, calls=%fused_computation.1 | loop fusion | flops 393216 | bytes 789504 | tf_op jit(solution)/shard_map/convert_element_type | solution.py:263
  15.6 0.7 %collective-permute-start.5 = (bf16[128,768]{1,0:T(8,128)(2,1)S(1)}, bf16[128,768]{1,0:T(8,128)(2,1)S(1)}, u32[]{:S(2)}, u32[]{:S(2)}) collective-permute-start(bf16[128,768]{1,0:T(8,128)(2,1)S(1)} %add_convert_fusion.1), channel_id=1, source_target_pairs={{4,8},{5,9},{6,10},{7,11},{20,24},{21,25},{22,26},{23,27}} | collective-permute-start | bytes 589832 | tf_op jit(solution)/shard_map/ppermute | solution.py:259
  16.2 0.0 collective-permute-done.1.refs_3_.refs_0_
  16.2 0.0 collective-permute-done.7.refs_0_
  16.3 1.2 %add_convert_fusion.3 = (bf16[128,640]{1,0:T(8,128)(2,1)S(1)}, bf16[128,640]{1,0:T(8,128)(2,1)S(1)}) fusion(bf16[128,640]{1,0:T(8,128)(2,1)S(1)} %collective-permute-done.7.refs_0_, f32[128,2048]{1,0:T(8,128)} %get-tuple-element.20, f32[640]{0:T(1024)S(1)} %get-tuple-element.23, bf16[128,640]{1,0:T(8,128)(2,1)S(1)} %collective-permute-done.1.refs_3_.refs_0_, ...), kind=kLoop, calls=%fused_computation.3 | loop fusion | flops 655360 | bytes 1315840 | tf_op jit(solution)/shard_map/convert_element_type | solution.py:263
  17.4 0.7 %collective-permute-start.8 = (bf16[128,640]{1,0:T(8,128)(2,1)S(1)}, bf16[128,640]{1,0:T(8,128)(2,1)S(1)}, u32[]{:S(2)}, u32[]{:S(2)}) collective-permute-start(bf16[128,640]{1,0:T(8,128)(2,1)S(1)} %get-tuple-element.27), channel_id=1, source_target_pairs={{4,8},{5,9},{6,10},{7,11},{20,24},{21,25},{22,26},{23,27}} | collective-permute-start | bytes 491528 | tf_op jit(solution)/shard_map/ppermute | solution.py:259
  18.1 0.7 %collective-permute-start.2 = (bf16[128,640]{1,0:T(8,128)(2,1)S(1)}, bf16[128,640]{1,0:T(8,128)(2,1)S(1)}, u32[]{:S(2)}, u32[]{:S(2)}) collective-permute-start(bf16[128,640]{1,0:T(8,128)(2,1)S(1)} %get-tuple-element.28), channel_id=1, source_target_pairs={{4,8},{5,9},{6,10},{7,11},{20,24},{21,25},{22,26},{23,27}} | collective-permute-start | bytes 491528 | tf_op jit(solution)/shard_map/ppermute | solution.py:259
  18.8 0.0 collective-permute-done.5.refs_4_
  18.8 0.0 copy-done.11
  18.8 0.1 add_convert_fusion
  18.9 0.0 copy-start
  18.9 0.0 copy-start.1
  18.9 0.0 copy-start.2
  18.9 0.0 copy-start.4
  18.9 0.0 copy-start.5
  18.9 1.4 %collective-permute-start.6 = (bf16[128,768]{1,0:T(8,128)(2,1)S(1)}, bf16[128,768]{1,0:T(8,128)(2,1)S(1)}, u32[]{:S(2)}, u32[]{:S(2)}) collective-permute-start(bf16[128,768]{1,0:T(8,128)(2,1)S(1)} %add_convert_fusion), channel_id=1, source_target_pairs={{8,12},{9,13},{10,14},{11,15},{24,28},{25,29},{26,30},{27,31}} | collective-permute-start | bytes 589832 | tf_op jit(solution)/shard_map/ppermute | solution.py:259
  20.3 0.0 collective-permute-done.8.refs_1_
  20.4 0.0 collective-permute-done.2.refs_4_.refs_1_
  20.4 0.0 copy-start.6
  20.4 0.0 copy-start.7
  20.4 0.1 add_convert_fusion.2
  20.5 1.3 %collective-permute-start.9 = (bf16[128,640]{1,0:T(8,128)(2,1)S(1)}, bf16[128,640]{1,0:T(8,128)(2,1)S(1)}, u32[]{:S(2)}, u32[]{:S(2)}) collective-permute-start(bf16[128,640]{1,0:T(8,128)(2,1)S(1)} %get-tuple-element.25), channel_id=1, source_target_pairs={{8,12},{9,13},{10,14},{11,15},{24,28},{25,29},{26,30},{27,31}} | collective-permute-start | bytes 491528 | tf_op jit(solution)/shard_map/ppermute | solution.py:259
  21.8 0.0 copy-start.9
  21.8 0.0 copy-start.10
  21.8 1.3 %collective-permute-start.3 = (bf16[128,640]{1,0:T(8,128)(2,1)S(1)}, bf16[128,640]{1,0:T(8,128)(2,1)S(1)}, u32[]{:S(2)}, u32[]{:S(2)}) collective-permute-start(bf16[128,640]{1,0:T(8,128)(2,1)S(1)} %get-tuple-element.26), channel_id=1, source_target_pairs={{8,12},{9,13},{10,14},{11,15},{24,28},{25,29},{26,30},{27,31}} | collective-permute-start | bytes 491528 | tf_op jit(solution)/shard_map/ppermute | solution.py:259
  23.1 0.0 copy-done
  23.1 0.0 copy-done.1
  23.1 0.0 copy-done.2
  23.2 0.0 copy-start.8
  23.2 2.3 %intra.1 = (f32[128,2048]{1,0:T(8,128)S(1)}, f32[128,2048]{1,0:T(8,128)S(1)}, bf16[128,256]{1,0:T(8,128)(2,1)S(1)}) custom-call(bf16[128,2048]{1,0:T(8,128)(2,1)S(1)} %copy-done, bf16[16,2560]{1,0:T(8,128)(2,1)S(1)} %copy-done.4, bf16[128,2,256]{2,1,0:T(2,128)(2,1)S(1)} %copy-done.1, bf16[128,2048]{1,0:T(8,128)(2,1)S(1)} %copy-done.2, ...), custom_call_target="tpu_custom_call" | custom-call | flops 134217728 | bytes 3145728 | tf_op jit(solution)/shard_map/intra/pallas_call | solution.py:352
  25.5 15.1 %collective-permute-done.9.refs_2_ = bf16[128,640]{1,0:T(8,128)(2,1)S(1)} collective-permute-done((bf16[128,640]{1,0:T(8,128)(2,1)S(1)}, bf16[128,640]{1,0:T(8,128)(2,1)S(1)}, u32[]{:S(2)}, u32[]{:S(2)}) %collective-permute-start.9) | collective-permute-done | bytes 163872 | tf_op jit(solution)/shard_map/ppermute | solution.py:259
  40.6 1.8 %collective-permute-done.3.refs_5_.refs_2_ = bf16[128,640]{1,0:T(8,128)(2,1)S(1)} collective-permute-done((bf16[128,640]{1,0:T(8,128)(2,1)S(1)}, bf16[128,640]{1,0:T(8,128)(2,1)S(1)}, u32[]{:S(2)}, u32[]{:S(2)}) %collective-permute-start.3) | collective-permute-done | bytes 163872 | tf_op jit(solution)/shard_map/ppermute | solution.py:259
  42.4 1.1 %outputs.2.refs_6_ = bf16[128,2048]{1,0:T(8,128)(2,1)} custom-call(bf16[128,256]{1,0:T(8,128)(2,1)S(1)} %get-tuple-element.15.c, f32[128,2048]{1,0:T(8,128)S(1)} %get-tuple-element.16.y_part, f32[128,2048]{1,0:T(8,128)S(1)} %get-tuple-element.17.lead, f32[1,2048]{1,0:T(1,128)S(1)} %bitcast.8, bf16[128,640]{1,0:T(8,128)(2,1)S(1)} %collective-permute-done.7.refs_0_, ...), custom_call_target="tpu_custom_call" | custom-call | tf_op jit(solution)/shard_map/outputs/pallas_call | solution.py:389
  43.4 0.0 collective-permute-done.6.refs_5_
  43.4 1.1 %outputs.3 = bf16[128,2048]{1,0:T(8,128)(2,1)} custom-call(bf16[128,256]{1,0:T(8,128)(2,1)S(1)} %get-tuple-element.15.c, f32[128,2048]{1,0:T(8,128)S(1)} %get-tuple-element.16.y_part, f32[128,2048]{1,0:T(8,128)S(1)} %get-tuple-element.17.lead, f32[1,2048]{1,0:T(1,128)S(1)} %bitcast.9, ...), custom_call_target="tpu_custom_call", output_to_operand_aliasing={{}: (10, {})} | custom-call | tf_op jit(solution)/shard_map/outputs/pallas_call | solution.py:389
  (9 shorter events, 0.0 us)
Async XLA Ops:
  1.8 6.5 %collective-permute-start = (bf16[16,2560]{1,0:T(8,128)(2,1)}, bf16[16,2560]{1,0:T(8,128)(2,1)S(1)}, u32[]{:S(2)}, u32[]{:S(2)}) collective-permute-start(bf16[16,2560]{1,0:T(8,128)(2,1)} %get-tuple-element.14), channel_id=1, source_target_pairs={{0,4},{4,8},{8,12},{1,5},{5,9},{9,13},{2,6},{6,10},{10,14},{3,7},{... | collective-permute-start | bytes 245768 | tf_op jit(solution)/shard_map/ppermute | solution.py:331
  3.1 13.2 %collective-permute-start.1 = (bf16[128,640]{1,0:T(8,128)(2,1)}, bf16[128,640]{1,0:T(8,128)(2,1)S(1)}, u32[]{:S(2)}, u32[]{:S(2)}) collective-permute-start(bf16[128,640]{1,0:T(8,128)(2,1)} %get-tuple-element.18), channel_id=1, source_target_pairs={{0,4},{1,5},{2,6},{3,7},{16,20},{17,21},{18,22},{19,23}} | collective-permute-start | bytes 491528 | tf_op jit(solution)/shard_map/ppermute | solution.py:259
  3.8 12.5 %collective-permute-start.7 = (bf16[128,640]{1,0:T(8,128)(2,1)}, bf16[128,640]{1,0:T(8,128)(2,1)S(1)}, u32[]{:S(2)}, u32[]{:S(2)}) collective-permute-start(bf16[128,640]{1,0:T(8,128)(2,1)} %get-tuple-element.22), channel_id=1, source_target_pairs={{0,4},{1,5},{2,6},{3,7},{16,20},{17,21},{18,22},{19,23}} | collective-permute-start | bytes 491528 | tf_op jit(solution)/shard_map/ppermute | solution.py:259
  4.4 10.0 %collective-permute-start.4 = (bf16[128,768]{1,0:T(8,128)(2,1)}, bf16[128,768]{1,0:T(8,128)(2,1)S(1)}, u32[]{:S(2)}, u32[]{:S(2)}) collective-permute-start(bf16[128,768]{1,0:T(8,128)(2,1)} %get-tuple-element.21), channel_id=1, source_target_pairs={{0,4},{1,5},{2,6},{3,7},{16,20},{17,21},{18,22},{19,23}} | collective-permute-start | bytes 589832 | tf_op jit(solution)/shard_map/ppermute | solution.py:259
  8.3 0.6 %copy-start.3 = (bf16[16,2560]{1,0:T(8,128)(2,1)}, bf16[16,2560]{1,0:T(8,128)(2,1)S(1)}, u32[]{:S(2)}) copy-start(bf16[16,2560]{1,0:T(8,128)(2,1)S(1)} %collective-permute-done.got.refs_1_) | copy-start | bytes 245764
  13.6 0.8 %copy-start.12 = (f32[1,2048]{1,0:T(1,128)S(1)}, f32[1,2048]{1,0:T(1,128)}, u32[]{:S(2)}) copy-start(f32[1,2048]{1,0:T(1,128)} %get-tuple-element.19) | copy-start | bytes 24580
  14.4 4.4 %copy-start.11 = (f32[128,2048]{1,0:T(8,128)S(1)}, f32[128,2048]{1,0:T(8,128)}, u32[]{:S(2)}) copy-start(f32[128,2048]{1,0:T(8,128)} %get-tuple-element.20) | copy-start | bytes 3145732
  15.6 3.2 %collective-permute-start.5 = (bf16[128,768]{1,0:T(8,128)(2,1)S(1)}, bf16[128,768]{1,0:T(8,128)(2,1)S(1)}, u32[]{:S(2)}, u32[]{:S(2)}) collective-permute-start(bf16[128,768]{1,0:T(8,128)(2,1)S(1)} %add_convert_fusion.1), channel_id=1, source_target_pairs={{4,8},{5,9},{6,10},{7,11},{20,24},{21,25},{22,26},{23,27}} | collective-permute-start | bytes 589832 | tf_op jit(solution)/shard_map/ppermute | solution.py:259
  17.4 2.9 %collective-permute-start.8 = (bf16[128,640]{1,0:T(8,128)(2,1)S(1)}, bf16[128,640]{1,0:T(8,128)(2,1)S(1)}, u32[]{:S(2)}, u32[]{:S(2)}) collective-permute-start(bf16[128,640]{1,0:T(8,128)(2,1)S(1)} %get-tuple-element.27), channel_id=1, source_target_pairs={{4,8},{5,9},{6,10},{7,11},{20,24},{21,25},{22,26},{23,27}} | collective-permute-start | bytes 491528 | tf_op jit(solution)/shard_map/ppermute | solution.py:259
  18.1 2.3 %collective-permute-start.2 = (bf16[128,640]{1,0:T(8,128)(2,1)S(1)}, bf16[128,640]{1,0:T(8,128)(2,1)S(1)}, u32[]{:S(2)}, u32[]{:S(2)}) collective-permute-start(bf16[128,640]{1,0:T(8,128)(2,1)S(1)} %get-tuple-element.28), channel_id=1, source_target_pairs={{4,8},{5,9},{6,10},{7,11},{20,24},{21,25},{22,26},{23,27}} | collective-permute-start | bytes 491528 | tf_op jit(solution)/shard_map/ppermute | solution.py:259
  18.9 4.3 %copy-start = (bf16[128,2048]{1,0:T(8,128)(2,1)S(1)}, bf16[128,2048]{1,0:T(8,128)(2,1)}, u32[]{:S(2)}) copy-start(bf16[128,2048]{1,0:T(8,128)(2,1)} %refs_2_.3) | copy-start | bytes 1572868
  18.9 4.3 %copy-start.1 = (bf16[128,2,256]{2,1,0:T(2,128)(2,1)S(1)}, bf16[128,2,256]{2,1,0:T(2,128)(2,1)}, u32[]{:S(2)}) copy-start(bf16[128,2,256]{2,1,0:T(2,128)(2,1)} %refs_3_.3) | copy-start | bytes 393220
  18.9 4.3 %copy-start.2 = (bf16[128,2048]{1,0:T(8,128)(2,1)S(1)}, bf16[128,2048]{1,0:T(8,128)(2,1)}, u32[]{:S(2)}) copy-start(bf16[128,2048]{1,0:T(8,128)(2,1)} %z.1) | copy-start | bytes 1572868
  18.9 4.3 %copy-start.4 = (bf16[16,2560]{1,0:T(8,128)(2,1)S(1)}, bf16[16,2560]{1,0:T(8,128)(2,1)}, u32[]{:S(2)}) copy-start(bf16[16,2560]{1,0:T(8,128)(2,1)} %copy-done.3) | copy-start | bytes 245764
  18.9 4.3 %copy-start.5 = (f32[4,2048]{1,0:T(4,128)S(1)}, f32[4,2048]{1,0:T(4,128)}, u32[]{:S(2)}) copy-start(f32[4,2048]{1,0:T(4,128)} %refs_4_.3) | copy-start | bytes 98308
  18.9 24.5 %collective-permute-start.6 = (bf16[128,768]{1,0:T(8,128)(2,1)S(1)}, bf16[128,768]{1,0:T(8,128)(2,1)S(1)}, u32[]{:S(2)}, u32[]{:S(2)}) collective-permute-start(bf16[128,768]{1,0:T(8,128)(2,1)S(1)} %add_convert_fusion), channel_id=1, source_target_pairs={{8,12},{9,13},{10,14},{11,15},{24,28},{25,29},{26,30},{27,31}} | collective-permute-start | bytes 589832 | tf_op jit(solution)/shard_map/ppermute | solution.py:259
  20.4 2.8 %copy-start.6 = (f32[128,32]{0,1:T(8,128)S(1)}, f32[128,32]{0,1:T(8,128)}, u32[]{:S(2)}) copy-start(f32[128,32]{0,1:T(8,128)} %param.12) | copy-start | bytes 49156
  20.4 2.8 %copy-start.7 = (f32[4,2,256]{2,1,0:T(2,128)S(1)}, f32[4,2,256]{2,1,0:T(2,128)}, u32[]{:S(2)}) copy-start(f32[4,2,256]{2,1,0:T(2,128)} %refs_5_.1) | copy-start | bytes 24580
  20.5 20.1 %collective-permute-start.9 = (bf16[128,640]{1,0:T(8,128)(2,1)S(1)}, bf16[128,640]{1,0:T(8,128)(2,1)S(1)}, u32[]{:S(2)}, u32[]{:S(2)}) collective-permute-start(bf16[128,640]{1,0:T(8,128)(2,1)S(1)} %get-tuple-element.25), channel_id=1, source_target_pairs={{8,12},{9,13},{10,14},{11,15},{24,28},{25,29},{26,30},{27,31}} | collective-permute-start | bytes 491528 | tf_op jit(solution)/shard_map/ppermute | solution.py:259
  21.8 1.4 %copy-start.9 = (f32[32]{0:T(128)S(1)}, f32[32]{0:T(128)}, u32[]{:S(2)}) copy-start(f32[32]{0:T(128)} %param.15) | copy-start | bytes 388
  21.8 1.4 %copy-start.10 = (f32[32]{0:T(128)S(1)}, f32[32]{0:T(128)}, u32[]{:S(2)}) copy-start(f32[32]{0:T(128)} %param.16) | copy-start | bytes 388
  21.8 20.5 %collective-permute-start.3 = (bf16[128,640]{1,0:T(8,128)(2,1)S(1)}, bf16[128,640]{1,0:T(8,128)(2,1)S(1)}, u32[]{:S(2)}, u32[]{:S(2)}) collective-permute-start(bf16[128,640]{1,0:T(8,128)(2,1)S(1)} %get-tuple-element.26), channel_id=1, source_target_pairs={{8,12},{9,13},{10,14},{11,15},{24,28},{25,29},{26,30},{27,31}} | collective-permute-start | bytes 491528 | tf_op jit(solution)/shard_map/ppermute | solution.py:259
  23.2 19.2 %copy-start.8 = (f32[2048]{0:T(1024)S(1)}, f32[2048]{0:T(1024)}, u32[]{:S(2)}) copy-start(f32[2048]{0:T(1024)} %param.17) | copy-start | bytes 24580

commit v3 on v2

--- a/solution.py
+++ b/solution.py
@@ -11,9 +11,8 @@
 F32 = jnp.float32
 BF16 = jnp.bfloat16
 CHAIN_MOST = 4
-SLICES = 3
+SLICES = 2
 CHUNK = 256
-LANES = 128
 
 
 def silu(u):
@@ -86,15 +85,20 @@
     return copies
 
 
-def emit_states(head_dim, x, tail_x, bc, tail_bc, taps_x, taps_bc, dt_raw, a_log, wide, emit):
+def emit_states(
+    head_dim, chunks, x, tail_x, bc, tail_bc, taps_x, taps_bc, dt_raw, a_log, wide, emit
+):
     dt, cum = rates(dt_raw[...], a_log[...], 0)
     end = cum[:, -1:]
     tail_decay = jnp.exp(end - cum) * dt
     groups = bc.shape[1]
     state_dim = bc.shape[2] // 2
-    cols = x.shape[1] // groups
     heads = dt.shape[0] // groups
+    cols = heads * head_dim
     for g in range(groups):
+        mine = [c for c in chunks if c.start // cols == g]
+        if not mine:
+            continue
         b = conv_act(
             bc[:, :, :state_dim].astype(F32)[:, g],
             tail_bc(g),
@@ -102,21 +106,65 @@
         )
         b_t = b.astype(F32).T.astype(BF16)
         wide[...] = spread(tail_decay[g * heads : (g + 1) * heads], head_dim, 2)
-        for at in range(0, cols, CHUNK):
-            cut = slice(g * cols + at, g * cols + at + CHUNK)
+        for cut in mine:
             act = conv_act(x[:, cut].astype(F32), tail_x(cut), taps_x[:, cut])
-            scaled = (wide[:, at : at + CHUNK] * act.astype(F32)).astype(BF16)
+            at = cut.start - g * cols
+            scaled = (wide[:, at : at + cut.stop - cut.start] * act.astype(F32)).astype(BF16)
             emit(cut, jnp.dot(b_t, scaled, preferred_element_type=F32))
     return end
 
 
+def chunks_of(cuts):
+    return [slice(at, at + CHUNK) for low, high in cuts for at in range(low, high, CHUNK)]
+
+
+def owner_of(cut, cuts):
+    at = [i for i, (low, high) in enumerate(cuts) if low <= cut.start < high][0]
+    return at, slice(cut.start - cuts[at][0], cut.stop - cuts[at][0])
+
+
 def first_kernel(head_dim, cuts, *refs):
     active, x_hbm, bc_hbm, taps_x_hbm, taps_bc_hbm, dt_hbm, a_hbm = refs[:7]
-    pack, halves_out = refs[7], refs[8 : 8 + len(cuts)]
-    x, bc, taps_x, taps_bc, dt_raw, a_log, last_x, last_bc, wide, sems = refs[8 + len(cuts) :]
+    outs = refs[7 : 7 + len(cuts)]
+    x, bc, taps_x, taps_bc, dt_raw, a_log, wide, sems = refs[7 + len(cuts) :]
+    span = pl.ds(cuts[0][0], cuts[-1][1] - cuts[0][0])
+
+    @pl.when(active[0] == 1)
+    def _():
+        make_first(
+            head_dim, cuts, outs,
+            started(
+                [(x_hbm.at[:, span], x.at[:, span]), (bc_hbm, bc), (taps_x_hbm, taps_x),
+                 (taps_bc_hbm, taps_bc), (dt_hbm, dt_raw), (a_hbm, a_log)],
+                sems,
+            ),
+            x, bc, taps_x, taps_bc, dt_raw, a_log, wide,
+        )
+
+
+def make_first(head_dim, cuts, outs, copies, x, bc, *more):
+    for copy in copies:
+        copy.wait()
+
+    def emit(cut, total):
+        at, here = owner_of(cut, cuts)
+        outs[at][:, here] = total.astype(BF16)
+
+    emit_states(
+        head_dim, chunks_of(cuts), x,
+        lambda cut: jnp.zeros((8, cut.stop - cut.start), F32),
+        bc, lambda g: jnp.zeros((8, bc.shape[2] // 2), F32),
+        *more, emit,
+    )
+
+
+def second_kernel(head_dim, cuts, *refs):
+    active, _, x_hbm, bc_hbm, taps_x_hbm, taps_bc_hbm, dt_hbm, a_hbm = refs[:8]
+    pack, outs = refs[8], refs[9 : 9 + len(cuts)]
+    x, bc, taps_x, taps_bc, dt_raw, a_log, wide, last_x, last_bc, sems = refs[9 + len(cuts) :]
     tokens, width = x.shape
     rows, groups, both = last_bc.shape
-    first = active[0] == 1
+    span = pl.ds(cuts[0][0], cuts[-1][1] - cuts[0][0])
     ends = started(
         [
             (x_hbm.at[pl.ds(tokens - rows, rows)], last_x),
@@ -124,46 +172,34 @@
         ],
         sems,
     )
-    inner = [(x_hbm, x), (bc_hbm, bc), (taps_x_hbm, taps_x), (taps_bc_hbm, taps_bc),
-             (dt_hbm, dt_raw), (a_hbm, a_log)]
+    inner = [(x_hbm.at[:, span], x.at[:, span]), (bc_hbm, bc), (taps_x_hbm, taps_x),
+             (taps_bc_hbm, taps_bc), (dt_hbm, dt_raw), (a_hbm, a_log)]
     rest = sems.at[pl.ds(2, len(inner))]
 
-    @pl.when(first)
+    @pl.when(active[0] == 1)
     def _():
         started(inner, rest)
 
     for copy in ends:
         copy.wait()
-    pack[:, :width] = last_x[...]
+    pack[:, :width] = last_x[...].astype(F32)[-8:].astype(BF16)
     wide_bc = last_bc[...].astype(F32)
     for g in range(groups):
-        pack[:, width + g * both : width + (g + 1) * both] = wide_bc[:, g].astype(BF16)
-
-    @pl.when(first)
+        pack[:, width + g * both : width + (g + 1) * both] = wide_bc[-8:, g].astype(BF16)
+
+    @pl.when(active[0] == 1)
     def _():
-        for i, (src, dst) in enumerate(inner):
-            pltpu.make_async_copy(src, dst, rest.at[i]).wait()
-
-        def emit(cut, total):
-            for (low, high), out in zip(cuts, halves_out):
-                begin, stop = max(low, cut.start), min(high, cut.stop)
-                if begin < stop:
-                    out[:, begin - low : stop - low] = total[
-                        :, begin - cut.start : stop - cut.start
-                    ].astype(BF16)
-
-        emit_states(
-            head_dim, x,
-            lambda cut: jnp.zeros((8, cut.stop - cut.start), F32),
-            bc, lambda g: jnp.zeros((8, both // 2), F32),
-            taps_x, taps_bc, dt_raw, a_log, wide, emit,
+        make_first(
+            head_dim, cuts, outs,
+            [pltpu.make_async_copy(src, dst, rest.at[i]) for i, (src, dst) in enumerate(inner)],
+            x, bc, taps_x, taps_bc, dt_raw, a_log, wide,
         )
 
 
-def later_kernel(head_dim, *refs):
+def later_kernel(head_dim, cuts, *refs):
     active, got, x_hbm, bc_hbm, taps_x_hbm, taps_bc_hbm, dt_hbm, a_hbm = refs[:8]
-    state, decay = refs[8:10]
-    x, bc, taps_x, taps_bc, dt_raw, a_log, wide, sems = refs[10:]
+    states, decays = refs[8 : 8 + len(cuts)], refs[8 + len(cuts) : 8 + 2 * len(cuts)]
+    x, bc, taps_x, taps_bc, dt_raw, a_log, wide, sems = refs[8 + 2 * len(cuts) :]
     width = x.shape[1]
     both = bc.shape[2]
     pairs = [(x_hbm, x), (bc_hbm, bc), (taps_x_hbm, taps_x), (taps_bc_hbm, taps_bc),
@@ -175,17 +211,20 @@
             copy.wait()
 
         def emit(cut, total):
-            state[:, cut] = total
+            at, here = owner_of(cut, cuts)
+            states[at][:, here] = total
 
         def tail_bc(g):
             at = width + g * both
-            return got[:, at : at + both // 2].astype(F32)[-8:]
+            return got[:, at : at + both // 2].astype(F32)
 
         end = emit_states(
-            head_dim, x, lambda cut: got[:, cut].astype(F32)[-8:], bc, tail_bc,
+            head_dim, chunks_of(cuts), x, lambda cut: got[:, cut].astype(F32), bc, tail_bc,
             taps_x, taps_bc, dt_raw, a_log, wide, emit,
         )
-        decay[...] = spread_row(jnp.exp(end), head_dim)
+        row = spread_row(jnp.exp(end), head_dim)
+        for decay, (low, high) in zip(decays, cuts):
+            decay[...] = row[:, low:high]
 
 
 def intra_kernel(
@@ -206,7 +245,7 @@
     for g in range(groups):
         at = width + g * both
         bc_act = conv_act(
-            bc[...].astype(F32)[:, g], got[:, at : at + both].astype(F32)[-8:], taps_bc[...][:, g]
+            bc[...].astype(F32)[:, g], got[:, at : at + both].astype(F32), taps_bc[...][:, g]
         )
         b, c = bc_act[:, :state_dim], bc_act[:, state_dim:]
         c_act[:, g * state_dim : (g + 1) * state_dim] = c
@@ -216,7 +255,7 @@
         for first in range(0, heads, 2):
             here = first * head_dim
             cut = slice(g * cols + here, g * cols + here + pair)
-            act = conv_act(x[:, cut].astype(F32), got[:, cut].astype(F32)[-8:], taps_x[:, cut])
+            act = conv_act(x[:, cut].astype(F32), got[:, cut].astype(F32), taps_x[:, cut])
             lane = lax.broadcasted_iota(jnp.int32, act.shape, 1)
             full = act.astype(F32)
             blocks = jnp.concatenate(
@@ -252,17 +291,18 @@
     return pltpu.CompilerParams(vmem_limit_bytes=mib * 1024 * 1024)
 
 
-def chain(firsts, state, decay, cuts, devices):
-    arrived = [[] for _ in cuts]
+def chain(firsts, states, decays, devices):
+    arrived = [[] for _ in firsts]
     to_send = firsts
     for hop in range(devices - 1):
         came = [lax.ppermute(v, "seq", [(hop, hop + 1)]) for v in to_send]
         for seen, v in zip(arrived, came):
             seen.append(v)
-        to_send = [
-            (decay[:, low:high] * v.astype(F32) + state[:, low:high]).astype(BF16)
-            for (low, high), v in zip(cuts, came)
-        ]
+        to_send = []
+        for decay, state, v in zip(decays, states, came):
+            if to_send:
+                v, _ = lax.optimization_barrier((v, to_send[-1]))
+            to_send.append((decay * v.astype(F32) + state).astype(BF16))
     return arrived
 
 
@@ -289,10 +329,9 @@
     cols = width // groups
     devices = lax.axis_size("seq")
     place = lax.axis_index("seq")
-    rows = 16
-
-    tiles = width // LANES
-    edges = [LANES * (tiles * i // SLICES) for i in range(SLICES + 1)]
+    rim = 8
+    tiles = width // CHUNK
+    edges = [CHUNK * -(-tiles * i // SLICES) for i in range(SLICES + 1)]
     cuts = list(zip(edges[:-1], edges[1:]))
     chained = devices <= CHAIN_MOST
 
@@ -302,9 +341,12 @@
     gain = norm_gain.reshape(1, width)
     is_first = (place == 0).astype(jnp.int32).reshape(1)
     operands = [x_in, bc_in, conv_x, conv_bc, dt_t, a_row]
-    landed = [pltpu.VMEM(v.shape, v.dtype) for v in operands]
+    operands = [pltpu.with_memory_space_constraint(v, pltpu.HBM) for v in operands]
+    scratch = [pltpu.VMEM(v.shape, v.dtype) for v in operands] + [pltpu.VMEM((tokens, cols), F32)]
     scalar = pl.BlockSpec(memory_space=pltpu.SMEM)
-    any_space = [pl.BlockSpec(memory_space=pl.ANY)] * len(operands)
+    in_vmem = pl.BlockSpec(memory_space=pltpu.VMEM)
+    anywhere = pl.BlockSpec(memory_space=pl.ANY)
+    in_hbm = [pl.BlockSpec(memory_space=pltpu.HBM)] * len(operands)
 
     def column(height, wide, at):
         return pl.BlockSpec((height, wide), lambda i: (0, at))
@@ -312,42 +354,48 @@
     def whole(array):
         return pl.BlockSpec(array.shape, lambda i: (0,) * len(array.shape))
 
-    last, *firsts = pl.pallas_call(
-        functools.partial(first_kernel, head_dim, cuts),
-        out_shape=[jax.ShapeDtypeStruct((rows, width + groups * both), BF16)]
-        + [jax.ShapeDtypeStruct((state_dim, high - low), BF16) for low, high in cuts],
-        in_specs=[scalar] + any_space,
-        scratch_shapes=landed
+    def sent(some):
+        return [jax.ShapeDtypeStruct((state_dim, high - low), BF16) for low, high in some]
+
+    (first,) = pl.pallas_call(
+        functools.partial(first_kernel, head_dim, cuts[:1]),
+        out_shape=sent(cuts[:1]),
+        in_specs=[scalar] + in_hbm,
+        scratch_shapes=scratch + [pltpu.SemaphoreType.DMA((len(operands),))],
+        compiler_params=params(16),
+        name="first_states",
+    )(is_first, *operands)
+    last, *others = pl.pallas_call(
+        functools.partial(second_kernel, head_dim, cuts[1:]),
+        out_shape=[jax.ShapeDtypeStruct((rim, width + groups * both), BF16)] + sent(cuts[1:]),
+        in_specs=[scalar, anywhere] + in_hbm,
+        scratch_shapes=scratch
         + [
-            pltpu.VMEM((rows, width), BF16),
-            pltpu.VMEM((rows, groups, both), BF16),
-            pltpu.VMEM((tokens, cols), F32),
+            pltpu.VMEM((2 * rim, width), BF16),
+            pltpu.VMEM((2 * rim, groups, both), BF16),
             pltpu.SemaphoreType.DMA((2 + len(operands),)),
         ],
-        compiler_params=params(56),
-        name="first_states",
-    )(is_first, *operands)
+        compiler_params=params(16),
+        name="second_states",
+    )(is_first, first, *operands)
 
     got = lax.ppermute(last, "seq", [(i, i + 1) for i in range(devices - 1)])
     runs = 1 - is_first if chained else jnp.ones((1,), jnp.int32)
-    state, decay = pl.pallas_call(
-        functools.partial(later_kernel, head_dim),
-        out_shape=(
-            jax.ShapeDtypeStruct((state_dim, width), F32),
-            jax.ShapeDtypeStruct((1, width), F32),
-        ),
-        in_specs=[scalar, pl.BlockSpec(memory_space=pltpu.VMEM)] + any_space,
-        scratch_shapes=landed
-        + [pltpu.VMEM((tokens, cols), F32), pltpu.SemaphoreType.DMA((len(operands),))],
-        compiler_params=params(56),
+    made = pl.pallas_call(
+        functools.partial(later_kernel, head_dim, cuts),
+        out_shape=[jax.ShapeDtypeStruct((state_dim, high - low), F32) for low, high in cuts]
+        + [jax.ShapeDtypeStruct((1, high - low), F32) for low, high in cuts],
+        in_specs=[scalar, in_vmem] + in_hbm,
+        scratch_shapes=scratch + [pltpu.SemaphoreType.DMA((len(operands),))],
+        compiler_params=params(16),
         name="later_states",
     )(runs, got, *operands)
+    states, decays = made[: len(cuts)], made[len(cuts) :]
 
     if chained:
-        arrived = chain(firsts, state, decay, cuts, devices)
+        arrived = chain([first] + others, states, decays, devices)
     else:
-        total = doubling(state, decay, devices)
-        arrived = [[total[:, low:high]] for low, high in cuts]
+        arrived = [[doubling(state, decay, devices)] for state, decay in zip(states, decays)]
 
     y_part, lead, c_act = pl.pallas_call(
         functools.partial(intra_kernel, head_dim),

time: 45 us -> 37 us (0.82)
  Pallas kernels: 10.8 us -> 8.1 us
  starting transfers between devices: 9.33 us -> 6.72 us
  other arithmetic: 2.45 us -> 0.32 us
  local copies, waits for them, and re-layouts: 1.48 us -> 0.06 us
  waiting for transfers between devices: 20.1 us -> 21.2 us
    pallas_call x2 -> x3, Pallas kernels: 6.39 us -> 3.74 us  [the longest x1 2.74 us: shards(): pl.pallas_call(functools.partial(later_kernel, head_dim, cuts), out_shape...]
    ppermute x9 -> x6, starting transfers between devices: 8.04 us -> 5.43 us  [chain(): came = [lax.ppermute(v, 'seq', [(hop, hop + 1)]) for v in to_send]]
    convert_element_type x4, other arithmetic: 2.45 us -> 0.32 us  [chain(): to_send.append((decay * v.astype(F32) + state).astype(BF16))]
    slice x2 -> x0, local copies, waits for them, and re-layouts: 0.78 us -> none  [chain(): decay[:, low:high] * v.astype(F32) + state[:, low:high]]
    ppermute x1, waiting for transfers between devices: 3.2 us -> 3.91 us  [shards(): got = lax.ppermute(last, 'seq', [(i, i + 1) for i in range(devices - 1)])]
    unnamed x26 -> x18, local copies, waits for them, and re-layouts: 0.7 us -> 0.06 us
    ppermute x9 -> x6, waiting for transfers between devices: 16.9 us -> 17.3 us  [chain(): came = [lax.ppermute(v, 'seq', [(hop, hop + 1)]) for v in to_send]]
  transfers between devices with their start and end apart: 10 -> 7, of which waited for: 3 -> 3; matrix products, arithmetic and copies ran while one was open for 7% -> 1% of each run, Pallas kernels for 18% -> 19%
where the time goes in v3:
time: 37 us; the launch traced here: 36.7 us
  waiting for transfers between devices  21.2 us (57%)
  Pallas kernels  8.1 us (22%)
  starting transfers between devices  6.72 us (18%)
    ppermute x6, waiting for transfers between devices, chain(): came = [lax.ppermute(v, 'seq', [(hop, hop + 1)]) for v in to_send]  17.3 us
    ppermute x6, starting transfers between devices, chain(): came = [lax.ppermute(v, 'seq', [(hop, hop + 1)]) for v in to_send]  5.43 us
    ppermute x1, waiting for transfers between devices, shards(): got = lax.ppermute(last, 'seq', [(i, i + 1) for i in range(devices - 1)])  3.91 us
    pallas_call x1, Pallas kernels, shards(): pl.pallas_call(functools.partial(later_kernel, head_dim, cuts), out_shape...  2.74 us
    pallas_call x1, Pallas kernels, shards(): pl.pallas_call(functools.partial(intra_kernel, head_dim), out_shape=(jax....  2.26 us
    pallas_call x2, Pallas kernels, shards(): pl.pallas_call(functools.partial(output_kernel, spans, len(arrived[0])),...  2.1 us
    ppermute x1, starting transfers between devices, shards(): got = lax.ppermute(last, 'seq', [(i, i + 1) for i in range(devices - 1)])  1.29 us
    pallas_call x1, Pallas kernels, shards(): pl.pallas_call(functools.partial(second_kernel, head_dim, cuts[1:]), out_...  0.95 us
  transfers between devices with their start and end apart: 7, of which 3 were waited for; matrix products, arithmetic and copies ran while one was open for 1% of the time, Pallas kernels for 19%

profile of v3, /device:TPU:30, one launch (start us, length us, event | category | flops | bytes accessed | tf_op | source)
XLA Modules:
  0.0 36.7 jit_solution(16592680842807000400)
XLA Ops:
  0.0 0.1 first_states.1.refs_1_
  0.1 0.7 %collective-permute-start.2 = (bf16[128,1024]{1,0:T(8,128)(2,1)S(1)}, bf16[128,1024]{1,0:T(8,128)(2,1)S(1)}, u32[]{:S(2)}, u32[]{:S(2)}) collective-permute-start(bf16[128,1024]{1,0:T(8,128)(2,1)S(1)} %first_states.1.refs_1_), channel_id=1, source_target_pairs={{0,4},{1,5},{2,6},{3,7},{16,20},{17,21},{18,22},{19,23}} | collective-permute-start | bytes 786440 | tf_op jit(solution)/shard_map/ppermute | solution.py:298
  0.7 0.9 %second_states.1 = (bf16[8,2560]{1,0:T(8,128)(2,1)S(1)}, bf16[128,1024]{1,0:T(8,128)(2,1)S(1)}) custom-call(s32[1]{0:T(128)} %bitcast.refs_0_, bf16[128,1024]{1,0:T(8,128)(2,1)S(1)} %first_states.1.refs_1_, bf16[128,2048]{1,0:T(8,128)(2,1)} %refs_2_.5, bf16[128,2,256]{2,1,0:T(2,128)(2,1)} %refs_3_.5, f32[4,2048]{1,0:T(4,128)} %refs_4_.5, ...), custom_call_target="tpu_custom_call" | custom-call | tf_op jit(solution)/shard_map/second_states/pallas_call | solution.py:368
  1.7 1.3 %collective-permute-start = (bf16[8,2560]{1,0:T(8,128)(2,1)S(1)}, bf16[8,2560]{1,0:T(8,128)(2,1)S(1)}, u32[]{:S(2)}, u32[]{:S(2)}) collective-permute-start(bf16[8,2560]{1,0:T(8,128)(2,1)S(1)} %get-tuple-element.16), channel_id=1, source_target_pairs={{0,4},{4,8},{8,12},{1,5},{5,9},{9,13},{2,6},{6,10},{10,14},{3,7},{... | collective-permute-start | bytes 122888 | tf_op jit(solution)/shard_map/ppermute | solution.py:382
  3.0 0.7 %collective-permute-start.1 = (bf16[128,1024]{1,0:T(8,128)(2,1)S(1)}, bf16[128,1024]{1,0:T(8,128)(2,1)S(1)}, u32[]{:S(2)}, u32[]{:S(2)}) collective-permute-start(bf16[128,1024]{1,0:T(8,128)(2,1)S(1)} %get-tuple-element.20), channel_id=1, source_target_pairs={{0,4},{1,5},{2,6},{3,7},{16,20},{17,21},{18,22},{19,23}} | collective-permute-start | bytes 786440 | tf_op jit(solution)/shard_map/ppermute | solution.py:298
  3.7 3.9 %collective-permute-done.got.refs_1_ = bf16[8,2560]{1,0:T(8,128)(2,1)S(1)} collective-permute-done((bf16[8,2560]{1,0:T(8,128)(2,1)S(1)}, bf16[8,2560]{1,0:T(8,128)(2,1)S(1)}, u32[]{:S(2)}, u32[]{:S(2)}) %collective-permute-start) | collective-permute-done | bytes 40992 | tf_op jit(solution)/shard_map/ppermute | solution.py:382
  7.6 2.7 %later_states.1 = (f32[128,1024]{1,0:T(8,128)S(1)}, f32[128,1024]{1,0:T(8,128)S(1)}, f32[1,1024]{1,0:T(1,128)S(1)}, f32[1,1024]{1,0:T(1,128)S(1)}) custom-call(s32[1]{0:T(128)S(6)} %sub.3.refs_0_, bf16[8,2560]{1,0:T(8,128)(2,1)S(1)} %collective-permute-done.got.refs_1_, bf16[128,2048]{1,0:T(8,128)(2,1)} %refs_2_.5, bf16[128,2,256]{2,1,0:T(2,128)(2,1)} %refs_3_.5, ...), custom_call_target="tpu_custom_call" | custom-call | tf_op jit(solution)/shard_map/later_states/pallas_call | solution.py:384
  10.3 0.0 collective-permute-done.2.refs_0_
  10.4 0.1 add_convert_fusion.3
  10.4 0.7 %collective-permute-start.4 = (bf16[128,1024]{1,0:T(8,128)(2,1)S(1)}, bf16[128,1024]{1,0:T(8,128)(2,1)S(1)}, u32[]{:S(2)}, u32[]{:S(2)}) collective-permute-start(bf16[128,1024]{1,0:T(8,128)(2,1)S(1)} %add_convert_fusion.3), channel_id=1, source_target_pairs={{4,8},{5,9},{6,10},{7,11},{20,24},{21,25},{22,26},{23,27}} | collective-permute-start | bytes 786440 | tf_op jit(solution)/shard_map/ppermute | solution.py:298
  11.1 0.0 collective-permute-done.1.refs_0_
  11.1 0.1 add_convert_fusion.2
  11.2 0.7 %collective-permute-start.3 = (bf16[128,1024]{1,0:T(8,128)(2,1)S(1)}, bf16[128,1024]{1,0:T(8,128)(2,1)S(1)}, u32[]{:S(2)}, u32[]{:S(2)}) collective-permute-start(bf16[128,1024]{1,0:T(8,128)(2,1)S(1)} %add_convert_fusion.2), channel_id=1, source_target_pairs={{4,8},{5,9},{6,10},{7,11},{20,24},{21,25},{22,26},{23,27}} | collective-permute-start | bytes 786440 | tf_op jit(solution)/shard_map/ppermute | solution.py:298
  11.9 0.0 collective-permute-done.4.refs_1_
  11.9 0.0 copy-start.3
  11.9 0.1 add_convert_fusion.1
  12.0 0.0 copy-start
  12.0 0.0 copy-start.1
  12.0 0.0 copy-start.2
  12.1 0.0 copy-start.4
  12.1 0.0 copy-start.5
  12.1 1.4 %collective-permute-start.6 = (bf16[128,1024]{1,0:T(8,128)(2,1)S(1)}, bf16[128,1024]{1,0:T(8,128)(2,1)S(1)}, u32[]{:S(2)}, u32[]{:S(2)}) collective-permute-start(bf16[128,1024]{1,0:T(8,128)(2,1)S(1)} %add_convert_fusion.1), channel_id=1, source_target_pairs={{8,12},{9,13},{10,14},{11,15},{24,28},{25,29},{26,30},{27,31}} | collective-permute-start | bytes 786440 | tf_op jit(solution)/shard_map/ppermute | solution.py:298
  13.5 0.0 collective-permute-done.3.refs_1_
  13.5 0.1 add_convert_fusion
  13.6 0.0 copy-start.7
  13.6 0.0 copy-start.8
  13.6 1.3 %collective-permute-start.5 = (bf16[128,1024]{1,0:T(8,128)(2,1)S(1)}, bf16[128,1024]{1,0:T(8,128)(2,1)S(1)}, u32[]{:S(2)}, u32[]{:S(2)}) collective-permute-start(bf16[128,1024]{1,0:T(8,128)(2,1)S(1)} %add_convert_fusion), channel_id=1, source_target_pairs={{8,12},{9,13},{10,14},{11,15},{24,28},{25,29},{26,30},{27,31}} | collective-permute-start | bytes 786440 | tf_op jit(solution)/shard_map/ppermute | solution.py:298
  14.9 0.0 copy-done.3
  14.9 0.0 copy-done
  15.0 0.0 copy-done.1
  15.0 0.0 copy-done.2
  15.0 0.0 copy-done.4
  15.0 0.0 copy-done.5
  15.0 0.0 copy-done.7
  15.0 0.0 copy-done.8
  15.0 0.0 copy-start.6
  15.0 2.3 %intra.1 = (f32[128,2048]{1,0:T(8,128)S(1)}, f32[128,2048]{1,0:T(8,128)S(1)}, bf16[128,256]{1,0:T(8,128)(2,1)S(1)}) custom-call(bf16[128,2048]{1,0:T(8,128)(2,1)S(1)} %copy-done, bf16[8,2560]{1,0:T(8,128)(2,1)S(1)} %collective-permute-done.got.refs_1_, bf16[128,2,256]{2,1,0:T(2,128)(2,1)S(1)} %copy-done.1, bf16[128,2048]{1,0:T(8,128)(2,1)S(1)} %copy-done.3, ...), custom_call_target="tpu_custom_call" | custom-call | flops 134217728 | bytes 3145728 | tf_op jit(solution)/shard_map/intra/pallas_call | solution.py:400
  17.3 15.6 %collective-permute-done.6.refs_2_ = bf16[128,1024]{1,0:T(8,128)(2,1)S(1)} collective-permute-done((bf16[128,1024]{1,0:T(8,128)(2,1)S(1)}, bf16[128,1024]{1,0:T(8,128)(2,1)S(1)}, u32[]{:S(2)}, u32[]{:S(2)}) %collective-permute-start.6) | collective-permute-done | bytes 262176 | tf_op jit(solution)/shard_map/ppermute | solution.py:298
  32.9 0.0 copy-done.6
  32.9 1.1 %outputs.2.refs_3_ = bf16[128,2048]{1,0:T(8,128)(2,1)} custom-call(bf16[128,256]{1,0:T(8,128)(2,1)S(1)} %get-tuple-element.17.c, f32[128,2048]{1,0:T(8,128)S(1)} %get-tuple-element.18.y_part, f32[128,2048]{1,0:T(8,128)S(1)} %get-tuple-element.19.lead, f32[1,2048]{1,0:T(1,128)S(1)} %bitcast.11, bf16[128,1024]{1,0:T(8,128)(2,1)S(1)} %collective-permute-done.2.refs_0_, ...), custom_call_target="tpu_custom_call" | custom-call | tf_op jit(solution)/shard_map/outputs/pallas_call | solution.py:437
  33.9 1.8 %collective-permute-done.5.refs_2_ = bf16[128,1024]{1,0:T(8,128)(2,1)S(1)} collective-permute-done((bf16[128,1024]{1,0:T(8,128)(2,1)S(1)}, bf16[128,1024]{1,0:T(8,128)(2,1)S(1)}, u32[]{:S(2)}, u32[]{:S(2)}) %collective-permute-start.5) | collective-permute-done | bytes 262176 | tf_op jit(solution)/shard_map/ppermute | solution.py:298
  35.7 1.0 %outputs.3 = bf16[128,2048]{1,0:T(8,128)(2,1)} custom-call(bf16[128,256]{1,0:T(8,128)(2,1)S(1)} %get-tuple-element.17.c, f32[128,2048]{1,0:T(8,128)S(1)} %get-tuple-element.18.y_part, f32[128,2048]{1,0:T(8,128)S(1)} %get-tuple-element.19.lead, f32[1,2048]{1,0:T(1,128)S(1)} %bitcast.12, ...), custom_call_target="tpu_custom_call", output_to_operand_aliasing={{}: (7, {})} | custom-call | tf_op jit(solution)/shard_map/outputs/pallas_call | solution.py:437
Async XLA Ops:
  0.1 10.3 %collective-permute-start.2 = (bf16[128,1024]{1,0:T(8,128)(2,1)S(1)}, bf16[128,1024]{1,0:T(8,128)(2,1)S(1)}, u32[]{:S(2)}, u32[]{:S(2)}) collective-permute-start(bf16[128,1024]{1,0:T(8,128)(2,1)S(1)} %first_states.1.refs_1_), channel_id=1, source_target_pairs={{0,4},{1,5},{2,6},{3,7},{16,20},{17,21},{18,22},{19,23}} | collective-permute-start | bytes 786440 | tf_op jit(solution)/shard_map/ppermute | solution.py:298
  1.7 5.9 %collective-permute-start = (bf16[8,2560]{1,0:T(8,128)(2,1)S(1)}, bf16[8,2560]{1,0:T(8,128)(2,1)S(1)}, u32[]{:S(2)}, u32[]{:S(2)}) collective-permute-start(bf16[8,2560]{1,0:T(8,128)(2,1)S(1)} %get-tuple-element.16), channel_id=1, source_target_pairs={{0,4},{4,8},{8,12},{1,5},{5,9},{9,13},{2,6},{6,10},{10,14},{3,7},{... | collective-permute-start | bytes 122888 | tf_op jit(solution)/shard_map/ppermute | solution.py:382
  3.0 8.1 %collective-permute-start.1 = (bf16[128,1024]{1,0:T(8,128)(2,1)S(1)}, bf16[128,1024]{1,0:T(8,128)(2,1)S(1)}, u32[]{:S(2)}, u32[]{:S(2)}) collective-permute-start(bf16[128,1024]{1,0:T(8,128)(2,1)S(1)} %get-tuple-element.20), channel_id=1, source_target_pairs={{0,4},{1,5},{2,6},{3,7},{16,20},{17,21},{18,22},{19,23}} | collective-permute-start | bytes 786440 | tf_op jit(solution)/shard_map/ppermute | solution.py:298
  10.4 1.5 %collective-permute-start.4 = (bf16[128,1024]{1,0:T(8,128)(2,1)S(1)}, bf16[128,1024]{1,0:T(8,128)(2,1)S(1)}, u32[]{:S(2)}, u32[]{:S(2)}) collective-permute-start(bf16[128,1024]{1,0:T(8,128)(2,1)S(1)} %add_convert_fusion.3), channel_id=1, source_target_pairs={{4,8},{5,9},{6,10},{7,11},{20,24},{21,25},{22,26},{23,27}} | collective-permute-start | bytes 786440 | tf_op jit(solution)/shard_map/ppermute | solution.py:298
  11.2 2.3 %collective-permute-start.3 = (bf16[128,1024]{1,0:T(8,128)(2,1)S(1)}, bf16[128,1024]{1,0:T(8,128)(2,1)S(1)}, u32[]{:S(2)}, u32[]{:S(2)}) collective-permute-start(bf16[128,1024]{1,0:T(8,128)(2,1)S(1)} %add_convert_fusion.2), channel_id=1, source_target_pairs={{4,8},{5,9},{6,10},{7,11},{20,24},{21,25},{22,26},{23,27}} | collective-permute-start | bytes 786440 | tf_op jit(solution)/shard_map/ppermute | solution.py:298
  11.9 3.0 %copy-start.3 = (bf16[128,2048]{1,0:T(8,128)(2,1)S(1)}, bf16[128,2048]{1,0:T(8,128)(2,1)}, u32[]{:S(2)}) copy-start(bf16[128,2048]{1,0:T(8,128)(2,1)} %z.1) | copy-start | bytes 1572868
  12.0 2.9 %copy-start = (bf16[128,2048]{1,0:T(8,128)(2,1)S(1)}, bf16[128,2048]{1,0:T(8,128)(2,1)}, u32[]{:S(2)}) copy-start(bf16[128,2048]{1,0:T(8,128)(2,1)} %refs_2_.5) | copy-start | bytes 1572868
  12.0 2.9 %copy-start.1 = (bf16[128,2,256]{2,1,0:T(2,128)(2,1)S(1)}, bf16[128,2,256]{2,1,0:T(2,128)(2,1)}, u32[]{:S(2)}) copy-start(bf16[128,2,256]{2,1,0:T(2,128)(2,1)} %refs_3_.5) | copy-start | bytes 393220
  12.0 2.9 %copy-start.2 = (f32[4,2048]{1,0:T(4,128)S(1)}, f32[4,2048]{1,0:T(4,128)}, u32[]{:S(2)}) copy-start(f32[4,2048]{1,0:T(4,128)} %refs_4_.5) | copy-start | bytes 98308
  12.1 2.9 %copy-start.4 = (f32[128,32]{0,1:T(8,128)S(1)}, f32[128,32]{0,1:T(8,128)}, u32[]{:S(2)}) copy-start(f32[128,32]{0,1:T(8,128)} %param.12) | copy-start | bytes 49156
  12.1 2.9 %copy-start.5 = (f32[4,2,256]{2,1,0:T(2,128)S(1)}, f32[4,2,256]{2,1,0:T(2,128)}, u32[]{:S(2)}) copy-start(f32[4,2,256]{2,1,0:T(2,128)} %refs_5_.3) | copy-start | bytes 24580
  12.1 20.8 %collective-permute-start.6 = (bf16[128,1024]{1,0:T(8,128)(2,1)S(1)}, bf16[128,1024]{1,0:T(8,128)(2,1)S(1)}, u32[]{:S(2)}, u32[]{:S(2)}) collective-permute-start(bf16[128,1024]{1,0:T(8,128)(2,1)S(1)} %add_convert_fusion.1), channel_id=1, source_target_pairs={{8,12},{9,13},{10,14},{11,15},{24,28},{25,29},{26,30},{27,31}} | collective-permute-start | bytes 786440 | tf_op jit(solution)/shard_map/ppermute | solution.py:298
  13.6 1.4 %copy-start.7 = (f32[32]{0:T(128)S(1)}, f32[32]{0:T(128)}, u32[]{:S(2)}) copy-start(f32[32]{0:T(128)} %param.15) | copy-start | bytes 388
  13.6 1.4 %copy-start.8 = (f32[32]{0:T(128)S(1)}, f32[32]{0:T(128)}, u32[]{:S(2)}) copy-start(f32[32]{0:T(128)} %param.16) | copy-start | bytes 388
  13.6 22.0 %collective-permute-start.5 = (bf16[128,1024]{1,0:T(8,128)(2,1)S(1)}, bf16[128,1024]{1,0:T(8,128)(2,1)S(1)}, u32[]{:S(2)}, u32[]{:S(2)}) collective-permute-start(bf16[128,1024]{1,0:T(8,128)(2,1)S(1)} %add_convert_fusion), channel_id=1, source_target_pairs={{8,12},{9,13},{10,14},{11,15},{24,28},{25,29},{26,30},{27,31}} | collective-permute-start | bytes 786440 | tf_op jit(solution)/shard_map/ppermute | solution.py:298
  15.0 17.8 %copy-start.6 = (f32[2048]{0:T(1024)S(1)}, f32[2048]{0:T(1024)}, u32[]{:S(2)}) copy-start(f32[2048]{0:T(1024)} %param.17) | copy-start | bytes 24580

commit v4 on v2

v4 whole, which is shorter than its diff:
```python
import functools

import jax
import jax.numpy as jnp
from jax import lax
from jax.experimental import pallas as pl
from jax.experimental.pallas import tpu as pltpu
from jax.sharding import PartitionSpec as P

EPS = 1e-05
F32 = jnp.float32
BF16 = jnp.bfloat16
CHAIN_MOST = 4
PER_GROUP = 2
CHUNK = 256
RIM = 8


def silu(u):
    return 0.5 * u * (1.0 + jnp.tanh(0.5 * u))


def softplus(v):
    return jnp.maximum(v, 0.0) + jnp.log1p(jnp.exp(-jnp.abs(v)))


def halves(v, count, axis):
    parts = []
    for _ in range(count - 1):
        part = v.astype(BF16)
        parts.append(part)
        v = v - part.astype(F32)
    parts.append(v.astype(BF16))
    return jnp.concatenate(parts, axis=axis)


def spread(per_head, head_dim, count):
    heads = per_head.shape[0]
    rows = lax.broadcasted_iota(jnp.int32, (heads * count, heads * head_dim), 0)
    cols = lax.broadcasted_iota(jnp.int32, (heads * count, heads * head_dim), 1)
    pick = (rows % heads == cols // head_dim).astype(F32).astype(BF16)
    return lax.dot_general(
        halves(per_head, count, 0), pick, (((0,), (0,)), ((), ())), preferred_element_type=F32
    )


def spread_row(column, head_dim):
    heads = column.shape[0]
    rows = lax.broadcasted_iota(jnp.int32, (heads, heads * head_dim), 0)
    cols = lax.broadcasted_iota(jnp.int32, (heads, heads * head_dim), 1)
    return jnp.sum(jnp.where(rows == cols // head_dim, column, 0.0), axis=0, keepdims=True)


def as_column(row, start, heads):
    every = row.shape[1]
    rows = lax.broadcasted_iota(jnp.int32, (heads, every), 0)
    cols = lax.broadcasted_iota(jnp.int32, (heads, every), 1)
    return jnp.sum(jnp.where(cols == rows + start, row, 0.0), axis=1, keepdims=True)


def conv_act(series, tail, taps):
    count = taps.shape[0]
    above = tail.shape[0]
    padded = jnp.concatenate([tail, series], axis=0)
    total = taps[count - 1 : count] * series
    for back in range(1, count):
        total = total + taps[count - 1 - back : count - back] * pltpu.roll(padded, back, 0)[above:]
    return silu(total).astype(BF16)


def rates(dt_raw, a_log_row, start):
    heads, tokens = dt_raw.shape
    dt = softplus(dt_raw)
    rate = -jnp.exp(as_column(a_log_row, start, heads)) * dt
    earlier = lax.broadcasted_iota(jnp.int32, (tokens, tokens), 0)
    later = lax.broadcasted_iota(jnp.int32, (tokens, tokens), 1)
    upto = (earlier <= later).astype(F32)
    cum = jnp.dot(rate, upto, precision=lax.Precision.HIGHEST, preferred_element_type=F32)
    return dt, cum


def emit_states(
    head_dim, group, chunks, x, tail_x, bc, tail_bc, taps_x, taps_bc, dt_raw, a_log, wide, emit
):
    dt, cum = rates(dt_raw[...], a_log[...], 0)
    end = cum[:, -1:]
    tail_decay = jnp.exp(end - cum) * dt
    state_dim = bc.shape[2] // 2
    heads = dt.shape[0] // bc.shape[1]
    mine = slice(group * heads, (group + 1) * heads)
    b = conv_act(
        bc[:, :, :state_dim].astype(F32)[:, group], tail_bc, taps_bc[:, :, :state_dim][:, group]
    )
    b_t = b.astype(F32).T.astype(BF16)
    wide[...] = spread(tail_decay[mine], head_dim, 2)
    decay = spread_row(jnp.exp(end[mine]), head_dim)
    for cut in chunks:
        act = conv_act(x[:, cut].astype(F32), tail_x(cut), taps_x[:, cut])
        at = cut.start - group * heads * head_dim
        here = slice(at, at + cut.stop - cut.start)
        scaled = (wide[:, here] * act.astype(F32)).astype(BF16)
        emit(cut, jnp.dot(b_t, scaled, preferred_element_type=F32), decay[:, here])


def chunks_of(low, high):
    return [slice(at, at + CHUNK) for at in range(low, high, CHUNK)]


def first_kernel(
    head_dim, group, low, high, active, _, x_hbm, bc_hbm, taps_x_hbm, taps_bc_hbm, dt_hbm, a_hbm,
    out, x, bc, taps_x, taps_bc, dt_raw, a_log, wide, sems,
):
    span = pl.ds(low, high - low)

    @pl.when(active[0] == 1)
    def _():
        pairs = [
            (x_hbm.at[:, span], x.at[:, span]), (bc_hbm, bc), (taps_x_hbm, taps_x),
            (taps_bc_hbm, taps_bc), (dt_hbm, dt_raw), (a_hbm, a_log),
        ]
        copies = [pltpu.make_async_copy(*pair, sems.at[i]) for i, pair in enumerate(pairs)]
        for copy in copies:
            copy.start()
        for copy in copies:
            copy.wait()
        both = bc.shape[2]
        state_dim = out.shape[0] - RIM
        tail_bc = bc[...].astype(F32)[-RIM:, group]
        if high - low > both:
            tail_bc = jnp.concatenate(
                [tail_bc, jnp.zeros((RIM, high - low - both), F32)], axis=1
            )
        rows = lax.broadcasted_iota(jnp.int32, (RIM, high - low), 0)
        tail_x = x[:, low:high].astype(F32)[-RIM:]
        keep = taps_x.shape[0] - 1
        tail = jnp.where(rows >= RIM - keep, tail_x, pltpu.roll(tail_bc, RIM - keep, 0))
        out[state_dim:, :] = tail.astype(BF16)

        def emit(cut, total, _):
            out[:state_dim, cut.start - low : cut.stop - low] = total.astype(BF16)

        emit_states(
            head_dim, group, chunks_of(low, high), x,
            lambda cut: jnp.zeros((RIM, cut.stop - cut.start), F32),
            bc, jnp.zeros((RIM, both // 2), F32), taps_x, taps_bc, dt_raw, a_log, wide, emit,
        )


def join_kernel(
    head_dim, group, low, high, active, came, x, bc, taps_x, taps_bc, dt_raw, a_log, out, wide
):
    @pl.when(active[0] == 1)
    def _():
        state_dim = out.shape[0]
        keep = taps_x.shape[0] - 1
        tail = came[...].astype(F32)[state_dim:]
        tail_bc = pltpu.roll(tail[:, : bc.shape[2]], keep, 0)[:, : bc.shape[2] // 2]

        def emit(cut, total, decay):
            here = slice(cut.start - low, cut.stop - low)
            before = came[:state_dim, here].astype(F32)
            out[:, here] = (decay * before + total).astype(BF16)

        emit_states(
            head_dim, group, chunks_of(low, high), x,
            lambda cut: tail[:, cut.start - low : cut.stop - low],
            bc, tail_bc, taps_x, taps_bc, dt_raw, a_log, wide, emit,
        )


def pack_kernel(_, x_hbm, bc_hbm, pack, last_x, last_bc, sems):
    tokens, width = x_hbm.shape
    rows, groups, both = last_bc.shape
    copies = [
        pltpu.make_async_copy(x_hbm.at[pl.ds(tokens - rows, rows)], last_x, sems.at[0]),
        pltpu.make_async_copy(bc_hbm.at[pl.ds(tokens - rows, rows)], last_bc, sems.at[1]),
    ]
    for copy in copies:
        copy.start()
    for copy in copies:
        copy.wait()
    pack[:, :width] = last_x[...].astype(F32)[-RIM:].astype(BF16)
    wide_bc = last_bc[...].astype(F32)
    for g in range(groups):
        pack[:, width + g * both : width + (g + 1) * both] = wide_bc[-RIM:, g].astype(BF16)


def later_kernel(head_dim, cuts, active, got, _, x, bc, taps_x, taps_bc, dt_raw, a_log, *refs):
    states, decays, wide = refs[: len(cuts)], refs[len(cuts) : 2 * len(cuts)], refs[-1]
    width = x.shape[1]
    both = bc.shape[2]

    @pl.when(active[0] == 1)
    def _():
        for state, row, (group, low, high) in zip(states, decays, cuts):

            def emit(cut, total, decay):
                here = slice(cut.start - low, cut.stop - low)
                state[:, here] = total
                row[:, here] = decay

            at = width + group * both
            emit_states(
                head_dim, group, chunks_of(low, high), x, lambda cut: got[:, cut].astype(F32),
                bc, got[:, at : at + both // 2].astype(F32),
                taps_x, taps_bc, dt_raw, a_log, wide, emit,
            )


def intra_kernel(
    head_dim, x, got, bc, z, taps_x, taps_bc, dt_raw, a_log, d_skip, y_part, lead, c_act, wide
):
    dt, cum = rates(dt_raw[...], a_log[...], 0)
    tokens, width = x.shape
    groups, both = bc.shape[1:]
    state_dim = both // 2
    cols = width // groups
    heads = dt.shape[0] // groups
    cum_t = cum.T
    leading = jnp.exp(cum)
    skip = spread_row(as_column(d_skip[...], 0, dt.shape[0]), head_dim)
    t_at = lax.broadcasted_iota(jnp.int32, (tokens, tokens), 0)
    s_at = lax.broadcasted_iota(jnp.int32, (tokens, tokens), 1)
    pair = 2 * head_dim
    for g in range(groups):
        at = width + g * both
        bc_act = conv_act(
            bc[...].astype(F32)[:, g], got[:, at : at + both].astype(F32), taps_bc[...][:, g]
        )
        b, c = bc_act[:, :state_dim], bc_act[:, state_dim:]
        c_act[:, g * state_dim : (g + 1) * state_dim] = c
        inner = lax.dot_general(c, b, (((1,), (1,)), ((), ())), preferred_element_type=F32)
        inner = jnp.where(t_at >= s_at, inner, 0.0)
        wide[...] = spread(leading[g * heads : (g + 1) * heads], head_dim, 2)
        for first in range(0, heads, 2):
            here = first * head_dim
            cut = slice(g * cols + here, g * cols + here + pair)
            act = conv_act(x[:, cut].astype(F32), got[:, cut].astype(F32), taps_x[:, cut])
            lane = lax.broadcasted_iota(jnp.int32, act.shape, 1)
            full = act.astype(F32)
            blocks = jnp.concatenate(
                [jnp.where(lane < head_dim, full, 0.0), jnp.where(lane < head_dim, 0.0, full)],
                axis=0,
            ).astype(BF16)
            weights = []
            for h in (g * heads + first, g * heads + first + 1):
                gap = jnp.minimum(cum_t[:, h : h + 1] - cum[h : h + 1, :], 0.0)
                weights.append((jnp.exp(gap) * dt[h : h + 1, :] * inner).astype(BF16))
            y = jnp.dot(jnp.concatenate(weights, axis=1), blocks, preferred_element_type=F32)
            gate = silu(z[:, cut].astype(F32))
            y_part[:, cut] = (y + skip[:, cut] * full) * gate
            lead[:, cut] = wide[:, here : here + pair] * gate


def gated_slice(c, y_part, lead, arrived):
    state = arrived[0][: c.shape[1]]
    for more in arrived[1:]:
        state = state + more[...]
    return y_part[...] + lead[...] * jnp.dot(c[...], state, preferred_element_type=F32)


def gated_kernel(c, y_part, lead, *refs):
    refs[-1][...] = gated_slice(c, y_part, lead, refs[:-1])


def output_kernel(ready, seen, c, y_part, lead, gain, *refs):
    gated = [v[...] for v in refs[:ready]]
    gated.append(gated_slice(c, y_part, lead, refs[ready : ready + seen]))
    gated = jnp.concatenate(gated, axis=1)
    mean_sq = jnp.mean(gated * gated, axis=1, keepdims=True)
    refs[-1][...] = (gated * lax.rsqrt(mean_sq + EPS) * gain[...]).astype(BF16)


def params(mib):
    return pltpu.CompilerParams(vmem_limit_bytes=mib * 1024 * 1024)


def doubling(state, decay, devices):
    def moved(value, distance):
        return lax.ppermute(value, "seq", [(i, i + distance) for i in range(devices - distance)])

    total, decay = moved(state.astype(BF16), 1), moved(decay, 1)
    distance = 1
    while distance < devices - 1:
        came = moved(total, distance)
        total = (decay * came.astype(F32) + total.astype(F32)).astype(BF16)
        decay = decay * moved(decay, distance)
        distance *= 2
    return total


def seen_last(arrived, cuts, group):
    return [seen for (g, _, _), seen in zip(cuts, arrived) if g == group][-1]


def shards(x_in, bc_in, z_in, dt_raw, conv_x, conv_bc, a_log, d_skip, norm_gain):
    tokens, width = x_in.shape
    groups, both = bc_in.shape[1:]
    state_dim = both // 2
    heads = dt_raw.shape[1]
    head_dim = width // heads
    cols = width // groups
    devices = lax.axis_size("seq")
    place = lax.axis_index("seq")
    step = cols // PER_GROUP
    cuts = [(at // cols, at, at + step) for at in range(0, width, step)]

    dt_t = dt_raw.T
    a_row = a_log.reshape(1, heads)
    d_row = d_skip.reshape(1, heads)
    gain = norm_gain.reshape(1, width)
    operands = [x_in, bc_in, conv_x, conv_bc, dt_t, a_row]
    pinned = [pltpu.with_memory_space_constraint(v, pltpu.HBM) for v in operands]
    wide = pltpu.VMEM((tokens, cols), F32)
    landed = [pltpu.VMEM(v.shape, v.dtype) for v in operands] + [wide]
    scalar = pl.BlockSpec(memory_space=pltpu.SMEM)
    in_vmem = pl.BlockSpec(memory_space=pltpu.VMEM)
    anywhere = pl.BlockSpec(memory_space=pl.ANY)
    in_hbm = [pl.BlockSpec(memory_space=pltpu.HBM)] * len(operands)

    def column(height, wide, at):
        return pl.BlockSpec((height, wide), lambda i: (0, at))

    def whole(array):
        return pl.BlockSpec(array.shape, lambda i: (0,) * len(array.shape))

    def here(condition):
        return condition.astype(jnp.int32).reshape(1)

    def shifted(value, route):
        return lax.ppermute(value, "seq", route)

    def first_states(token, group, low, high):
        return pl.pallas_call(
            functools.partial(first_kernel, head_dim, group, low, high),
            out_shape=jax.ShapeDtypeStruct((state_dim + RIM, high - low), BF16),
            in_specs=[scalar, anywhere] + in_hbm,
            scratch_shapes=landed + [pltpu.SemaphoreType.DMA((len(operands),))],
            compiler_params=params(16),
            name="first_states",
        )(here(place == 0), token, *pinned)

    def joined(came, group, low, high):
        return pl.pallas_call(
            functools.partial(join_kernel, head_dim, group, low, high),
            out_shape=jax.ShapeDtypeStruct((state_dim, high - low), BF16),
            in_specs=[scalar] + [in_vmem] * (1 + len(operands)),
            scratch_shapes=[wide],
            compiler_params=params(16),
            name="joined_states",
        )(here(place == 1), came, *operands)

    def packed(token):
        return pl.pallas_call(
            pack_kernel,
            out_shape=jax.ShapeDtypeStruct((RIM, width + groups * both), BF16),
            in_specs=[anywhere] + in_hbm[:2],
            scratch_shapes=[
                pltpu.VMEM((2 * RIM, width), BF16),
                pltpu.VMEM((2 * RIM, groups, both), BF16),
                pltpu.SemaphoreType.DMA((2,)),
            ],
            compiler_params=params(16),
            name="last_rows",
        )(token, *pinned[:2])

    def later_states(condition, got, token):
        made = pl.pallas_call(
            functools.partial(later_kernel, head_dim, cuts),
            out_shape=[
                jax.ShapeDtypeStruct((state_dim, high - low), F32) for _, low, high in cuts
            ]
            + [jax.ShapeDtypeStruct((1, high - low), F32) for _, low, high in cuts],
            in_specs=[scalar, in_vmem, anywhere] + [in_vmem] * len(operands),
            scratch_shapes=[wide],
            compiler_params=params(16),
            name="later_states",
        )(here(condition), got, token, *operands)
        return made[: len(cuts)], made[len(cuts) :]

    along = [(i, i + 1) for i in range(devices - 1)]
    if devices <= CHAIN_MOST:
        arrived = []
        token = a_row
        for cut in cuts:
            token = first_states(token, *cut)
            arrived.append([shifted(token, along[:1])])
        got = shifted(packed(token), along)
        if devices > 2:
            token = None
            for seen, cut in zip(arrived, cuts):
                if token is not None:
                    seen[0], _ = lax.optimization_barrier((seen[0], token))
                token = joined(seen[0], *cut)
                seen.append(shifted(token, along[1:2]))
        if devices > 3:
            states, decays = later_states(place >= 2, got, token)
        for hop in range(2, devices - 1):
            token = None
            for seen, decay, state in zip(arrived, decays, states):
                if token is not None:
                    seen[-1], _ = lax.optimization_barrier((seen[-1], token))
                token = (decay * seen[-1].astype(F32) + state).astype(BF16)
                seen.append(shifted(token, along[hop : hop + 1]))
    else:
        got = shifted(packed(a_row), along)
        states, decays = later_states(place >= 0, got, a_row)
        arrived = [[doubling(state, decay, devices)] for state, decay in zip(states, decays)]

    y_part, lead, c_act = pl.pallas_call(
        functools.partial(intra_kernel, head_dim),
        out_shape=(
            jax.ShapeDtypeStruct((tokens, width), F32),
            jax.ShapeDtypeStruct((tokens, width), F32),
            jax.ShapeDtypeStruct((tokens, groups * state_dim), BF16),
        ),
        scratch_shapes=[pltpu.VMEM((tokens, cols), F32)],
        compiler_params=params(32),
        cost_estimate=pl.CostEstimate(
            flops=4 * tokens * tokens * width,
            bytes_accessed=12 * tokens * width,
            transcendentals=tokens * tokens * heads,
        ),
        name="intra",
    )(x_in, got, bc_in, z_in, conv_x, conv_bc, dt_t, a_row, d_row)

    out = None
    for g in range(groups):
        ready = []
        for (group, low, high), seen in zip(cuts, arrived):
            if group != g:
                continue
            inputs = [c_act, y_part, lead]
            specs = [column(tokens, state_dim, g)] + [column(tokens, step, low // step)] * 2
            if high < (g + 1) * cols:
                ready.append(
                    pl.pallas_call(
                        gated_kernel,
                        out_shape=jax.ShapeDtypeStruct((tokens, step), F32),
                        in_specs=specs + [whole(v) for v in seen],
                        out_specs=column(tokens, step, 0),
                        grid=(1,),
                        compiler_params=params(16),
                        name="gated",
                    )(*inputs, *seen)
                )
        inputs += [gain] + ready + seen_last(arrived, cuts, g)
        specs += [column(1, cols, g)] + [whole(v) for v in ready + seen_last(arrived, cuts, g)]
        aliases = {}
        if out is not None:
            aliases = {len(inputs): 0}
            inputs.append(out)
            specs.append(pl.BlockSpec(memory_space=pl.ANY))
        out = pl.pallas_call(
            functools.partial(output_kernel, len(ready), len(arrived[0])),
            out_shape=jax.ShapeDtypeStruct((tokens, width), BF16),
            in_specs=specs,
            out_specs=column(tokens, cols, g),
            grid=(1,),
            input_output_aliases=aliases,
            compiler_params=params(32),
            name="outputs",
        )(*inputs)
    return out


def solution(mesh):
    return jax.shard_map(
        shards,
        mesh=mesh,
        in_specs=(
            P(("groups", "seq"), "head"),
            P(("groups", "seq"), "head", None),
            P(("groups", "seq"), "head"),
            P(("groups", "seq"), "head"),
            P(None, "head"),
            P(None, "head", None),
            P("head"),
            P("head"),
            P("head"),
        ),
        out_specs=P(("groups", "seq"), "head"),
        check_vma=False,
    )
```

time: 45 us -> 31.7 us (0.70)
  waiting for transfers between devices: 20.1 us -> 9.13 us
  starting transfers between devices: 9.33 us -> 12.2 us
  other arithmetic: 2.45 us -> 0.17 us
  Pallas kernels: 10.8 us -> 8.6 us
  local copies, waits for them, and re-layouts: 1.48 us -> 0.65 us
    ppermute x10 -> x13, waiting for transfers between devices: 20.1 us -> 9.13 us  [shifted(): return lax.ppermute(value, 'seq', route)]
    ppermute x10 -> x13, starting transfers between devices: 9.33 us -> 12.2 us  [shifted(): return lax.ppermute(value, 'seq', route)]
    convert_element_type x4, other arithmetic: 2.45 us -> 0.17 us  [shards(): token = (decay * seen[-1].astype(F32) + state).astype(BF16)]
    pallas_call x4 -> x14, Pallas kernels: 8.51 us -> 6.33 us  [the longest x1 2.78 us: later_states(): pl.pallas_call(functools.partial(later_kernel, head_dim, cuts), out_shape...]
    slice x2 -> x0, local copies, waits for them, and re-layouts: 0.78 us -> none  [chain(): decay[:, low:high] * v.astype(F32) + state[:, low:high]]
  transfers between devices with their start and end apart: 10 -> 13, of which waited for: 3 -> 4; matrix products, arithmetic and copies ran while one was open for 7% -> 1% of each run, Pallas kernels for 18% -> 24%
where the time goes in v4:
time: 31.7 us; the launch traced here: 31.2 us
  starting transfers between devices  12.2 us (38%)
  waiting for transfers between devices  9.13 us (29%)
  Pallas kernels  8.6 us (27%)
  local copies, waits for them, and re-layouts  0.65 us (2%)
  between operations  0.45 us (1%)
    ppermute x13, starting transfers between devices, shifted(): return lax.ppermute(value, 'seq', route)  12.2 us
    ppermute x13, waiting for transfers between devices, shifted(): return lax.ppermute(value, 'seq', route)  9.13 us
    pallas_call x1, Pallas kernels, later_states(): pl.pallas_call(functools.partial(later_kernel, head_dim, cuts), out_shape...  2.78 us
    pallas_call x1, Pallas kernels, shards(): pl.pallas_call(functools.partial(intra_kernel, head_dim), out_shape=(jax....  2.26 us
    pallas_call x2, Pallas kernels, shards(): pl.pallas_call(functools.partial(output_kernel, len(ready), len(arrived[0...  2.01 us
    pallas_call x1, Pallas kernels, packed(): pl.pallas_call(pack_kernel, out_shape=jax.ShapeDtypeStruct((RIM, width +...  0.89 us
    unnamed x22, local copies, waits for them, and re-layouts  0.65 us
  transfers between devices with their start and end apart: 13, of which 4 were waited for; matrix products, arithmetic and copies ran while one was open for 1% of the time, Pallas kernels for 24%

profile of v4, /device:TPU:30, one launch (start us, length us, event | category | flops | bytes accessed | tf_op | source)
XLA Modules:
  0.0 31.2 jit_solution(7883188744263255949)
XLA Ops:
  0.0 0.1 first_states.4._
  0.1 0.7 %collective-permute-start.3 = (bf16[136,512]{1,0:T(8,128)(2,1)S(1)}, bf16[136,512]{1,0:T(8,128)(2,1)S(1)}, u32[]{:S(2)}, u32[]{:S(2)}) collective-permute-start(bf16[136,512]{1,0:T(8,128)(2,1)S(1)} %first_states.4._), channel_id=1, source_target_pairs={{0,4},{1,5},{2,6},{3,7},{16,20},{17,21},{18,22},{19,23}} | collective-permute-start | bytes 417800 | tf_op jit(solution)/shard_map/ppermute | solution.py:331
  0.7 0.1 first_states.5._
  0.8 0.7 %collective-permute-start.2 = (bf16[136,512]{1,0:T(8,128)(2,1)S(1)}, bf16[136,512]{1,0:T(8,128)(2,1)S(1)}, u32[]{:S(2)}, u32[]{:S(2)}) collective-permute-start(bf16[136,512]{1,0:T(8,128)(2,1)S(1)} %first_states.5._), channel_id=1, source_target_pairs={{0,4},{1,5},{2,6},{3,7},{16,20},{17,21},{18,22},{19,23}} | collective-permute-start | bytes 417800 | tf_op jit(solution)/shard_map/ppermute | solution.py:331
  1.5 0.1 first_states.6._
  1.6 0.0 copy-start
  1.6 0.0 copy-start.2
  1.6 0.0 copy-start.4
  1.6 0.8 %collective-permute-start.1 = (bf16[136,512]{1,0:T(8,128)(2,1)S(1)}, bf16[136,512]{1,0:T(8,128)(2,1)S(1)}, u32[]{:S(2)}, u32[]{:S(2)}) collective-permute-start(bf16[136,512]{1,0:T(8,128)(2,1)S(1)} %first_states.6._), channel_id=1, source_target_pairs={{0,4},{1,5},{2,6},{3,7},{16,20},{17,21},{18,22},{19,23}} | collective-permute-start | bytes 417800 | tf_op jit(solution)/shard_map/ppermute | solution.py:331
  2.4 0.0 copy-start.5
  2.4 0.0 copy-start.6
  2.4 0.1 first_states.7._
  2.5 0.7 %collective-permute-start.5 = (bf16[136,512]{1,0:T(8,128)(2,1)S(1)}, bf16[136,512]{1,0:T(8,128)(2,1)S(1)}, u32[]{:S(2)}, u32[]{:S(2)}) collective-permute-start(bf16[136,512]{1,0:T(8,128)(2,1)S(1)} %first_states.7._), channel_id=1, source_target_pairs={{0,4},{1,5},{2,6},{3,7},{16,20},{17,21},{18,22},{19,23}} | collective-permute-start | bytes 417800 | tf_op jit(solution)/shard_map/ppermute | solution.py:331
  3.2 0.0 copy-start.8
  3.2 0.0 collective-permute-done.3.came.refs_0_
  3.2 0.0 copy-done
  3.3 0.6 %copy-done.8 = f32[32]{0:T(128)S(1)} copy-done((f32[32]{0:T(128)S(1)}, f32[32]{0:T(128)}, u32[]{:S(2)}) %copy-start.8) | copy-done | bytes 152
  3.9 0.8 %collective-permute-start.7 = (bf16[128,512]{1,0:T(8,128)(2,1)S(1)}, bf16[128,512]{1,0:T(8,128)(2,1)S(1)}, u32[]{:S(2)}, u32[]{:S(2)}) collective-permute-start(bf16[128,512]{1,0:T(8,128)(2,1)S(1)} %joined_states.4), channel_id=1, source_target_pairs={{4,8},{5,9},{6,10},{7,11},{20,24},{21,25},{22,26},{23,27}} | collective-permute-start | bytes 393224 | tf_op jit(solution)/shard_map/ppermute | solution.py:331
  4.7 0.9 %last_rows.1 = bf16[8,2560]{1,0:T(8,128)(2,1)S(1)} custom-call(bf16[136,512]{1,0:T(8,128)(2,1)S(1)} %first_states.7._, bf16[128,2048]{1,0:T(8,128)(2,1)} %x.11, bf16[128,2,256]{2,1,0:T(2,128)(2,1)} %bc.11), custom_call_target="tpu_custom_call" | custom-call | tf_op jit(solution)/shard_map/last_rows/pallas_call | solution.py:354
  5.5 1.3 %collective-permute-start = (bf16[8,2560]{1,0:T(8,128)(2,1)S(1)}, bf16[8,2560]{1,0:T(8,128)(2,1)S(1)}, u32[]{:S(2)}, u32[]{:S(2)}) collective-permute-start(bf16[8,2560]{1,0:T(8,128)(2,1)S(1)} %last_rows.1), channel_id=1, source_target_pairs={{0,4},{4,8},{8,12},{1,5},{5,9},{9,13},{2,6},{6,10},{10,14},{3,7},{... | collective-permute-start | bytes 122888 | tf_op jit(solution)/shard_map/ppermute | solution.py:331
  6.9 0.0 collective-permute-done.2.came.refs_1_
  6.9 0.7 %collective-permute-start.6 = (bf16[128,512]{1,0:T(8,128)(2,1)S(1)}, bf16[128,512]{1,0:T(8,128)(2,1)S(1)}, u32[]{:S(2)}, u32[]{:S(2)}) collective-permute-start(bf16[128,512]{1,0:T(8,128)(2,1)S(1)} %joined_states.5), channel_id=1, source_target_pairs={{4,8},{5,9},{6,10},{7,11},{20,24},{21,25},{22,26},{23,27}} | collective-permute-start | bytes 393224 | tf_op jit(solution)/shard_map/ppermute | solution.py:331
  7.6 0.0 collective-permute-done.1.came.refs_0_
  7.6 0.7 %collective-permute-start.4 = (bf16[128,512]{1,0:T(8,128)(2,1)S(1)}, bf16[128,512]{1,0:T(8,128)(2,1)S(1)}, u32[]{:S(2)}, u32[]{:S(2)}) collective-permute-start(bf16[128,512]{1,0:T(8,128)(2,1)S(1)} %joined_states.6), channel_id=1, source_target_pairs={{4,8},{5,9},{6,10},{7,11},{20,24},{21,25},{22,26},{23,27}} | collective-permute-start | bytes 393224 | tf_op jit(solution)/shard_map/ppermute | solution.py:331
  8.3 0.0 collective-permute-done.5.came.refs_1_
  8.3 0.7 %collective-permute-start.9 = (bf16[128,512]{1,0:T(8,128)(2,1)S(1)}, bf16[128,512]{1,0:T(8,128)(2,1)S(1)}, u32[]{:S(2)}, u32[]{:S(2)}) collective-permute-start(bf16[128,512]{1,0:T(8,128)(2,1)S(1)} %joined_states.7._), channel_id=1, source_target_pairs={{4,8},{5,9},{6,10},{7,11},{20,24},{21,25},{22,26},{23,27}} | collective-permute-start | bytes 393224 | tf_op jit(solution)/shard_map/ppermute | solution.py:331
  9.0 2.5 %collective-permute-done.got = bf16[8,2560]{1,0:T(8,128)(2,1)S(1)} collective-permute-done((bf16[8,2560]{1,0:T(8,128)(2,1)S(1)}, bf16[8,2560]{1,0:T(8,128)(2,1)S(1)}, u32[]{:S(2)}, u32[]{:S(2)}) %collective-permute-start) | collective-permute-done | bytes 40992 | tf_op jit(solution)/shard_map/ppermute | solution.py:331
  11.4 2.8 %later_states.1 = (f32[128,512]{1,0:T(8,128)S(1)}, f32[128,512]{1,0:T(8,128)S(1)}, f32[128,512]{1,0:T(8,128)S(1)}, f32[128,512]{1,0:T(8,128)S(1)}, f32[1,512]{1,...) custom-call(s32[1]{0:T(128)} %bitcast.6.active, ...), custom_call_target="tpu_custom_call" | custom-call | tf_op jit(solution)/shard_map/later_states/pallas_call | solution.py:368
  14.2 0.0 collective-permute-done.7.refs_1_
  14.3 1.3 %collective-permute-start.11 = (bf16[128,512]{1,0:T(8,128)(2,1)S(1)}, bf16[128,512]{1,0:T(8,128)(2,1)S(1)}, u32[]{:S(2)}, u32[]{:S(2)}) collective-permute-start(bf16[128,512]{1,0:T(8,128)(2,1)S(1)} %add_convert_fusion.3), channel_id=1, source_target_pairs={{8,12},{9,13},{10,14},{11,15},{24,28},{25,29},{26,30},{27,31}} | collective-permute-start | bytes 393224 | tf_op jit(solution)/shard_map/ppermute | solution.py:331
  15.6 0.0 collective-permute-done.6.refs_2_
  15.6 1.3 %collective-permute-start.12 = (bf16[128,512]{1,0:T(8,128)(2,1)S(1)}, bf16[128,512]{1,0:T(8,128)(2,1)S(1)}, u32[]{:S(2)}, u32[]{:S(2)}) collective-permute-start(bf16[128,512]{1,0:T(8,128)(2,1)S(1)} %add_convert_fusion.2), channel_id=1, source_target_pairs={{8,12},{9,13},{10,14},{11,15},{24,28},{25,29},{26,30},{27,31}} | collective-permute-start | bytes 393224 | tf_op jit(solution)/shard_map/ppermute | solution.py:331
  16.9 0.0 collective-permute-done.4.refs_1_
  16.9 0.0 copy-start.7
  17.0 1.4 %collective-permute-start.8 = (bf16[128,512]{1,0:T(8,128)(2,1)S(1)}, bf16[128,512]{1,0:T(8,128)(2,1)S(1)}, u32[]{:S(2)}, u32[]{:S(2)}) collective-permute-start(bf16[128,512]{1,0:T(8,128)(2,1)S(1)} %add_convert_fusion.1), channel_id=1, source_target_pairs={{8,12},{9,13},{10,14},{11,15},{24,28},{25,29},{26,30},{27,31}} | collective-permute-start | bytes 393224 | tf_op jit(solution)/shard_map/ppermute | solution.py:331
  18.4 0.0 collective-permute-done.9.refs_2_
  18.5 0.0 copy-start.10
  18.5 1.3 %collective-permute-start.10 = (bf16[128,512]{1,0:T(8,128)(2,1)S(1)}, bf16[128,512]{1,0:T(8,128)(2,1)S(1)}, u32[]{:S(2)}, u32[]{:S(2)}) collective-permute-start(bf16[128,512]{1,0:T(8,128)(2,1)S(1)} %add_convert_fusion), channel_id=1, source_target_pairs={{8,12},{9,13},{10,14},{11,15},{24,28},{25,29},{26,30},{27,31}} | collective-permute-start | bytes 393224 | tf_op jit(solution)/shard_map/ppermute | solution.py:331
  19.8 2.3 %intra.1 = (f32[128,2048]{1,0:T(8,128)S(1)}, f32[128,2048]{1,0:T(8,128)S(1)}, bf16[128,256]{1,0:T(8,128)(2,1)S(1)}) custom-call(bf16[128,2048]{1,0:T(8,128)(2,1)S(1)} %copy-done.1, bf16[8,2560]{1,0:T(8,128)(2,1)S(1)} %collective-permute-done.got, bf16[128,2,256]{2,1,0:T(2,128)(2,1)S(1)} %copy-done.3, bf16[128,2048]{1,0:T(8,128)(2,1)S(1)} %copy-done.7, ...), custom_call_target="tpu_custom_call" | custom-call | flops 134217728 | bytes 3145728 | tf_op jit(solution)/shard_map/intra/pallas_call | solution.py:410
  22.1 1.3 %collective-permute-done.11.refs_2_ = bf16[128,512]{1,0:T(8,128)(2,1)S(1)} collective-permute-done((bf16[128,512]{1,0:T(8,128)(2,1)S(1)}, bf16[128,512]{1,0:T(8,128)(2,1)S(1)}, u32[]{:S(2)}, u32[]{:S(2)}) %collective-permute-start.11) | collective-permute-done | bytes 131104 | tf_op jit(solution)/shard_map/ppermute | solution.py:331
  23.4 0.2 gated.3.refs_0_
  23.6 0.0 copy-start.9
  23.6 5.2 %collective-permute-done.8.refs_2_ = bf16[128,512]{1,0:T(8,128)(2,1)S(1)} collective-permute-done((bf16[128,512]{1,0:T(8,128)(2,1)S(1)}, bf16[128,512]{1,0:T(8,128)(2,1)S(1)}, u32[]{:S(2)}, u32[]{:S(2)}) %collective-permute-start.8) | collective-permute-done | bytes 131104 | tf_op jit(solution)/shard_map/ppermute | solution.py:331
  28.8 0.2 gated.2.refs_0_
  29.0 0.0 collective-permute-done.12.refs_3_
  29.0 1.0 %outputs.2.refs_4_ = bf16[128,2048]{1,0:T(8,128)(2,1)} custom-call(bf16[128,256]{1,0:T(8,128)(2,1)S(1)} %get-tuple-element.22.c, f32[128,2048]{1,0:T(8,128)S(1)} %get-tuple-element.23.y_part, f32[128,2048]{1,0:T(8,128)S(1)} %get-tuple-element.24.lead, f32[1,2048]{1,0:T(1,128)S(1)} %bitcast.32, f32[128,512]{1,0:T(8,128)S(1)} %gated.3.refs_0_, ...), custom_call_target="tpu_custom_call" | custom-call | tf_op jit(solution)/shard_map/outputs/pallas_call | solution.py:454
  30.0 0.2 collective-permute-done.10.refs_3_
  30.2 1.0 %outputs.3 = bf16[128,2048]{1,0:T(8,128)(2,1)} custom-call(bf16[128,256]{1,0:T(8,128)(2,1)S(1)} %get-tuple-element.22.c, f32[128,2048]{1,0:T(8,128)S(1)} %get-tuple-element.23.y_part, f32[128,2048]{1,0:T(8,128)S(1)} %get-tuple-element.24.lead, f32[1,2048]{1,0:T(1,128)S(1)} %bitcast.33, f32[128,512]{1,0:T(8,128)S(1)} %gated.2.refs_0_, ...), custom_call_target="tpu_custom_call", output_to_operand_aliasing={{}: (8, {})} | custom-call | tf_op jit(solution)/shard_map/outputs/pallas_call | solution.py:454
  (19 shorter events, 0.2 us)
Async XLA Ops:
  0.1 3.1 %collective-permute-start.3 = (bf16[136,512]{1,0:T(8,128)(2,1)S(1)}, bf16[136,512]{1,0:T(8,128)(2,1)S(1)}, u32[]{:S(2)}, u32[]{:S(2)}) collective-permute-start(bf16[136,512]{1,0:T(8,128)(2,1)S(1)} %first_states.4._), channel_id=1, source_target_pairs={{0,4},{1,5},{2,6},{3,7},{16,20},{17,21},{18,22},{19,23}} | collective-permute-start | bytes 417800 | tf_op jit(solution)/shard_map/ppermute | solution.py:331
  0.8 6.0 %collective-permute-start.2 = (bf16[136,512]{1,0:T(8,128)(2,1)S(1)}, bf16[136,512]{1,0:T(8,128)(2,1)S(1)}, u32[]{:S(2)}, u32[]{:S(2)}) collective-permute-start(bf16[136,512]{1,0:T(8,128)(2,1)S(1)} %first_states.5._), channel_id=1, source_target_pairs={{0,4},{1,5},{2,6},{3,7},{16,20},{17,21},{18,22},{19,23}} | collective-permute-start | bytes 417800 | tf_op jit(solution)/shard_map/ppermute | solution.py:331
  1.6 1.7 %copy-start = (bf16[128,2048]{1,0:T(8,128)(2,1)S(1)}, bf16[128,2048]{1,0:T(8,128)(2,1)}, u32[]{:S(2)}) copy-start(bf16[128,2048]{1,0:T(8,128)(2,1)} %x.11) | copy-start | bytes 1572868
  1.6 1.6 %copy-start.2 = (bf16[128,2,256]{2,1,0:T(2,128)(2,1)S(1)}, bf16[128,2,256]{2,1,0:T(2,128)(2,1)}, u32[]{:S(2)}) copy-start(bf16[128,2,256]{2,1,0:T(2,128)(2,1)} %bc.11) | copy-start | bytes 393220
  1.6 1.6 %copy-start.4 = (f32[4,2048]{1,0:T(4,128)S(1)}, f32[4,2048]{1,0:T(4,128)}, u32[]{:S(2)}) copy-start(f32[4,2048]{1,0:T(4,128)} %taps_x.11) | copy-start | bytes 98308
  1.6 6.0 %collective-permute-start.1 = (bf16[136,512]{1,0:T(8,128)(2,1)S(1)}, bf16[136,512]{1,0:T(8,128)(2,1)S(1)}, u32[]{:S(2)}, u32[]{:S(2)}) collective-permute-start(bf16[136,512]{1,0:T(8,128)(2,1)S(1)} %first_states.6._), channel_id=1, source_target_pairs={{0,4},{1,5},{2,6},{3,7},{16,20},{17,21},{18,22},{19,23}} | collective-permute-start | bytes 417800 | tf_op jit(solution)/shard_map/ppermute | solution.py:331
  2.4 0.8 %copy-start.5 = (f32[128,32]{0,1:T(8,128)S(1)}, f32[128,32]{0,1:T(8,128)}, u32[]{:S(2)}) copy-start(f32[128,32]{0,1:T(8,128)} %param.12) | copy-start | bytes 49156
  2.4 0.8 %copy-start.6 = (f32[4,2,256]{2,1,0:T(2,128)S(1)}, f32[4,2,256]{2,1,0:T(2,128)}, u32[]{:S(2)}) copy-start(f32[4,2,256]{2,1,0:T(2,128)} %taps_bc.11) | copy-start | bytes 24580
  2.5 5.8 %collective-permute-start.5 = (bf16[136,512]{1,0:T(8,128)(2,1)S(1)}, bf16[136,512]{1,0:T(8,128)(2,1)S(1)}, u32[]{:S(2)}, u32[]{:S(2)}) collective-permute-start(bf16[136,512]{1,0:T(8,128)(2,1)S(1)} %first_states.7._), channel_id=1, source_target_pairs={{0,4},{1,5},{2,6},{3,7},{16,20},{17,21},{18,22},{19,23}} | collective-permute-start | bytes 417800 | tf_op jit(solution)/shard_map/ppermute | solution.py:331
  3.2 0.7 %copy-start.8 = (f32[32]{0:T(128)S(1)}, f32[32]{0:T(128)}, u32[]{:S(2)}) copy-start(f32[32]{0:T(128)} %param.15) | copy-start | bytes 388
  3.9 3.0 %copy-start.1 = (bf16[128,2048]{1,0:T(8,128)(2,1)S(1)}, bf16[128,2048]{1,0:T(8,128)(2,1)}, u32[]{:S(2)}) copy-start(bf16[128,2048]{1,0:T(8,128)(2,1)} %x.11) | copy-start | bytes 1572868
  3.9 3.0 %copy-start.3 = (bf16[128,2,256]{2,1,0:T(2,128)(2,1)S(1)}, bf16[128,2,256]{2,1,0:T(2,128)(2,1)}, u32[]{:S(2)}) copy-start(bf16[128,2,256]{2,1,0:T(2,128)(2,1)} %bc.11) | copy-start | bytes 393220
  3.9 10.4 %collective-permute-start.7 = (bf16[128,512]{1,0:T(8,128)(2,1)S(1)}, bf16[128,512]{1,0:T(8,128)(2,1)S(1)}, u32[]{:S(2)}, u32[]{:S(2)}) collective-permute-start(bf16[128,512]{1,0:T(8,128)(2,1)S(1)} %joined_states.4), channel_id=1, source_target_pairs={{4,8},{5,9},{6,10},{7,11},{20,24},{21,25},{22,26},{23,27}} | collective-permute-start | bytes 393224 | tf_op jit(solution)/shard_map/ppermute | solution.py:331
  5.5 5.9 %collective-permute-start = (bf16[8,2560]{1,0:T(8,128)(2,1)S(1)}, bf16[8,2560]{1,0:T(8,128)(2,1)S(1)}, u32[]{:S(2)}, u32[]{:S(2)}) collective-permute-start(bf16[8,2560]{1,0:T(8,128)(2,1)S(1)} %last_rows.1), channel_id=1, source_target_pairs={{0,4},{4,8},{8,12},{1,5},{5,9},{9,13},{2,6},{6,10},{10,14},{3,7},{... | collective-permute-start | bytes 122888 | tf_op jit(solution)/shard_map/ppermute | solution.py:331
  6.9 8.7 %collective-permute-start.6 = (bf16[128,512]{1,0:T(8,128)(2,1)S(1)}, bf16[128,512]{1,0:T(8,128)(2,1)S(1)}, u32[]{:S(2)}, u32[]{:S(2)}) collective-permute-start(bf16[128,512]{1,0:T(8,128)(2,1)S(1)} %joined_states.5), channel_id=1, source_target_pairs={{4,8},{5,9},{6,10},{7,11},{20,24},{21,25},{22,26},{23,27}} | collective-permute-start | bytes 393224 | tf_op jit(solution)/shard_map/ppermute | solution.py:331
  7.6 9.3 %collective-permute-start.4 = (bf16[128,512]{1,0:T(8,128)(2,1)S(1)}, bf16[128,512]{1,0:T(8,128)(2,1)S(1)}, u32[]{:S(2)}, u32[]{:S(2)}) collective-permute-start(bf16[128,512]{1,0:T(8,128)(2,1)S(1)} %joined_states.6), channel_id=1, source_target_pairs={{4,8},{5,9},{6,10},{7,11},{20,24},{21,25},{22,26},{23,27}} | collective-permute-start | bytes 393224 | tf_op jit(solution)/shard_map/ppermute | solution.py:331
  8.3 10.1 %collective-permute-start.9 = (bf16[128,512]{1,0:T(8,128)(2,1)S(1)}, bf16[128,512]{1,0:T(8,128)(2,1)S(1)}, u32[]{:S(2)}, u32[]{:S(2)}) collective-permute-start(bf16[128,512]{1,0:T(8,128)(2,1)S(1)} %joined_states.7._), channel_id=1, source_target_pairs={{4,8},{5,9},{6,10},{7,11},{20,24},{21,25},{22,26},{23,27}} | collective-permute-start | bytes 393224 | tf_op jit(solution)/shard_map/ppermute | solution.py:331
  14.3 9.1 %collective-permute-start.11 = (bf16[128,512]{1,0:T(8,128)(2,1)S(1)}, bf16[128,512]{1,0:T(8,128)(2,1)S(1)}, u32[]{:S(2)}, u32[]{:S(2)}) collective-permute-start(bf16[128,512]{1,0:T(8,128)(2,1)S(1)} %add_convert_fusion.3), channel_id=1, source_target_pairs={{8,12},{9,13},{10,14},{11,15},{24,28},{25,29},{26,30},{27,31}} | collective-permute-start | bytes 393224 | tf_op jit(solution)/shard_map/ppermute | solution.py:331
  15.6 13.3 %collective-permute-start.12 = (bf16[128,512]{1,0:T(8,128)(2,1)S(1)}, bf16[128,512]{1,0:T(8,128)(2,1)S(1)}, u32[]{:S(2)}, u32[]{:S(2)}) collective-permute-start(bf16[128,512]{1,0:T(8,128)(2,1)S(1)} %add_convert_fusion.2), channel_id=1, source_target_pairs={{8,12},{9,13},{10,14},{11,15},{24,28},{25,29},{26,30},{27,31}} | collective-permute-start | bytes 393224 | tf_op jit(solution)/shard_map/ppermute | solution.py:331
  16.9 2.9 %copy-start.7 = (bf16[128,2048]{1,0:T(8,128)(2,1)S(1)}, bf16[128,2048]{1,0:T(8,128)(2,1)}, u32[]{:S(2)}) copy-start(bf16[128,2048]{1,0:T(8,128)(2,1)} %z.1) | copy-start | bytes 1572868
  17.0 11.8 %collective-permute-start.8 = (bf16[128,512]{1,0:T(8,128)(2,1)S(1)}, bf16[128,512]{1,0:T(8,128)(2,1)S(1)}, u32[]{:S(2)}, u32[]{:S(2)}) collective-permute-start(bf16[128,512]{1,0:T(8,128)(2,1)S(1)} %add_convert_fusion.1), channel_id=1, source_target_pairs={{8,12},{9,13},{10,14},{11,15},{24,28},{25,29},{26,30},{27,31}} | collective-permute-start | bytes 393224 | tf_op jit(solution)/shard_map/ppermute | solution.py:331
  18.5 1.3 %copy-start.10 = (f32[32]{0:T(128)S(1)}, f32[32]{0:T(128)}, u32[]{:S(2)}) copy-start(f32[32]{0:T(128)} %param.16) | copy-start | bytes 388
  18.5 11.7 %collective-permute-start.10 = (bf16[128,512]{1,0:T(8,128)(2,1)S(1)}, bf16[128,512]{1,0:T(8,128)(2,1)S(1)}, u32[]{:S(2)}, u32[]{:S(2)}) collective-permute-start(bf16[128,512]{1,0:T(8,128)(2,1)S(1)} %add_convert_fusion), channel_id=1, source_target_pairs={{8,12},{9,13},{10,14},{11,15},{24,28},{25,29},{26,30},{27,31}} | collective-permute-start | bytes 393224 | tf_op jit(solution)/shard_map/ppermute | solution.py:331
  23.6 5.4 %copy-start.9 = (f32[2048]{0:T(1024)S(1)}, f32[2048]{0:T(1024)}, u32[]{:S(2)}) copy-start(f32[2048]{0:T(1024)} %param.17) | copy-start | bytes 24580

commit v5 on v4

--- a/solution.py
+++ b/solution.py
@@ -106,16 +106,31 @@
     return [slice(at, at + CHUNK) for at in range(low, high, CHUNK)]
 
 
+def head_rows(x, bc, group, low, high, out, taps_x, taps_bc, dt_raw, a_log, wide):
+    head_dim = x.shape[1] // dt_raw.shape[0]
+    state_dim = bc.shape[2] // 2
+
+    def emit(cut, total, _):
+        out[:state_dim, cut.start - low : cut.stop - low] = total.astype(BF16)
+
+    emit_states(
+        head_dim, group, chunks_of(low, high), x,
+        lambda cut: jnp.zeros((RIM, cut.stop - cut.start), F32),
+        bc, jnp.zeros((RIM, state_dim), F32), taps_x, taps_bc, dt_raw, a_log, wide, emit,
+    )
+
+
 def first_kernel(
-    head_dim, group, low, high, active, _, x_hbm, bc_hbm, taps_x_hbm, taps_bc_hbm, dt_hbm, a_hbm,
+    group, low, high, active, x_hbm, bc_hbm, taps_x_hbm, taps_bc_hbm, dt_hbm, a_hbm,
     out, x, bc, taps_x, taps_bc, dt_raw, a_log, wide, sems,
 ):
-    span = pl.ds(low, high - low)
+    tokens, width = x.shape
+    groups, both = bc.shape[1:]
 
     @pl.when(active[0] == 1)
     def _():
         pairs = [
-            (x_hbm.at[:, span], x.at[:, span]), (bc_hbm, bc), (taps_x_hbm, taps_x),
+            (x_hbm, x), (bc_hbm, bc), (taps_x_hbm, taps_x),
             (taps_bc_hbm, taps_bc), (dt_hbm, dt_raw), (a_hbm, a_log),
         ]
         copies = [pltpu.make_async_copy(*pair, sems.at[i]) for i, pair in enumerate(pairs)]
@@ -123,88 +138,69 @@
             copy.start()
         for copy in copies:
             copy.wait()
-        both = bc.shape[2]
-        state_dim = out.shape[0] - RIM
-        tail_bc = bc[...].astype(F32)[-RIM:, group]
-        if high - low > both:
-            tail_bc = jnp.concatenate(
-                [tail_bc, jnp.zeros((RIM, high - low - both), F32)], axis=1
-            )
-        rows = lax.broadcasted_iota(jnp.int32, (RIM, high - low), 0)
-        tail_x = x[:, low:high].astype(F32)[-RIM:]
+        state_dim, step = both // 2, high - low
         keep = taps_x.shape[0] - 1
-        tail = jnp.where(rows >= RIM - keep, tail_x, pltpu.roll(tail_bc, RIM - keep, 0))
-        out[state_dim:, :] = tail.astype(BF16)
-
-        def emit(cut, total, _):
-            out[:state_dim, cut.start - low : cut.stop - low] = total.astype(BF16)
-
-        emit_states(
-            head_dim, group, chunks_of(low, high), x,
-            lambda cut: jnp.zeros((RIM, cut.stop - cut.start), F32),
-            bc, jnp.zeros((RIM, both // 2), F32), taps_x, taps_bc, dt_raw, a_log, wide, emit,
-        )
-
-
-def join_kernel(
-    head_dim, group, low, high, active, came, x, bc, taps_x, taps_bc, dt_raw, a_log, out, wide
+        extra = out.shape[0] - state_dim
+        last_bc = bc[tokens - 2 * RIM :].astype(F32)[-RIM:]
+        last = [x[tokens - 2 * RIM :, :].astype(F32)[-RIM:]] + [last_bc[:, g] for g in range(groups)]
+        last = jnp.concatenate(last, axis=1)
+        at = lax.broadcasted_iota(jnp.int32, (extra, step), 0)
+        below = jnp.zeros((extra, step), F32)
+        fill = jnp.zeros((extra - RIM, step), F32)
+        for k in range(last.shape[1] // step):
+            block = jnp.concatenate([last[:, k * step : (k + 1) * step], fill], axis=0)
+            block = pltpu.roll(block, (keep * (k + 1) - RIM) % extra, 0)
+            below = jnp.where((at >= keep * k) & (at < keep * (k + 1)), block, below)
+        out[state_dim:, :] = below.astype(BF16)
+        head_rows(x, bc, group, low, high, out, taps_x, taps_bc, dt_raw, a_log, wide)
+
+
+def next_kernel(
+    group, low, high, active, _, x, bc, taps_x, taps_bc, dt_raw, a_log, out, wide
 ):
     @pl.when(active[0] == 1)
     def _():
-        state_dim = out.shape[0]
-        keep = taps_x.shape[0] - 1
-        tail = came[...].astype(F32)[state_dim:]
-        tail_bc = pltpu.roll(tail[:, : bc.shape[2]], keep, 0)[:, : bc.shape[2] // 2]
-
-        def emit(cut, total, decay):
-            here = slice(cut.start - low, cut.stop - low)
-            before = came[:state_dim, here].astype(F32)
-            out[:, here] = (decay * before + total).astype(BF16)
-
-        emit_states(
-            head_dim, group, chunks_of(low, high), x,
-            lambda cut: tail[:, cut.start - low : cut.stop - low],
-            bc, tail_bc, taps_x, taps_bc, dt_raw, a_log, wide, emit,
-        )
-
-
-def pack_kernel(_, x_hbm, bc_hbm, pack, last_x, last_bc, sems):
-    tokens, width = x_hbm.shape
-    rows, groups, both = last_bc.shape
-    copies = [
-        pltpu.make_async_copy(x_hbm.at[pl.ds(tokens - rows, rows)], last_x, sems.at[0]),
-        pltpu.make_async_copy(bc_hbm.at[pl.ds(tokens - rows, rows)], last_bc, sems.at[1]),
-    ]
-    for copy in copies:
-        copy.start()
-    for copy in copies:
-        copy.wait()
-    pack[:, :width] = last_x[...].astype(F32)[-RIM:].astype(BF16)
-    wide_bc = last_bc[...].astype(F32)
+        head_rows(x, bc, group, low, high, out, taps_x, taps_bc, dt_raw, a_log, wide)
+
+
+def pack_kernel(_, x, bc, pack):
+    tokens, width = x.shape
+    groups, both = bc.shape[1:]
+    pack[:, :width] = x[tokens - 2 * RIM :, :].astype(F32)[-RIM:].astype(BF16)
+    last_bc = bc[tokens - 2 * RIM :].astype(F32)[-RIM:]
     for g in range(groups):
-        pack[:, width + g * both : width + (g + 1) * both] = wide_bc[-RIM:, g].astype(BF16)
-
-
-def later_kernel(head_dim, cuts, active, got, _, x, bc, taps_x, taps_bc, dt_raw, a_log, *refs):
-    states, decays, wide = refs[: len(cuts)], refs[len(cuts) : 2 * len(cuts)], refs[-1]
+        pack[:, width + g * both : width + (g + 1) * both] = last_bc[:, g].astype(BF16)
+
+
+def later_kernel(
+    group, low, high, active, rows, _, x, bc, taps_x, taps_bc, dt_raw, a_log, state, decay, wide
+):
     width = x.shape[1]
     both = bc.shape[2]
+    state_dim = both // 2
+    keep = taps_x.shape[0] - 1
+    head_dim = width // dt_raw.shape[0]
+
+    def tail(begin, stop):
+        if rows.shape[0] == RIM:
+            return rows[:, begin:stop].astype(F32)
+        step = rows.shape[1]
+        below = rows[state_dim:, begin % step : begin % step + stop - begin].astype(F32)
+        extra = below.shape[0]
+        return pltpu.roll(below, (RIM - keep * (begin // step + 1)) % extra, 0)[:RIM]
 
     @pl.when(active[0] == 1)
     def _():
-        for state, row, (group, low, high) in zip(states, decays, cuts):
-
-            def emit(cut, total, decay):
-                here = slice(cut.start - low, cut.stop - low)
-                state[:, here] = total
-                row[:, here] = decay
-
-            at = width + group * both
-            emit_states(
-                head_dim, group, chunks_of(low, high), x, lambda cut: got[:, cut].astype(F32),
-                bc, got[:, at : at + both // 2].astype(F32),
-                taps_x, taps_bc, dt_raw, a_log, wide, emit,
-            )
+        def emit(cut, total, along):
+            here = slice(cut.start - low, cut.stop - low)
+            state[:, here] = total
+            decay[:, here] = along
+
+        at = width + group * both
+        emit_states(
+            head_dim, group, chunks_of(low, high), x, lambda cut: tail(cut.start, cut.stop),
+            bc, tail(at, at + state_dim), taps_x, taps_bc, dt_raw, a_log, wide, emit,
+        )
 
 
 def intra_kernel(
@@ -305,6 +301,7 @@
     step = cols // PER_GROUP
     cuts = [(at // cols, at, at + step) for at in range(0, width, step)]
 
+    taps = conv_x.shape[0]
     dt_t = dt_raw.T
     a_row = a_log.reshape(1, heads)
     d_row = d_skip.reshape(1, heads)
@@ -330,82 +327,75 @@
     def shifted(value, route):
         return lax.ppermute(value, "seq", route)
 
-    def first_states(token, group, low, high):
+    def first_states(group, low, high):
+        blocks = (width + groups * both) // step
+        extra = -(-(taps - 1) * blocks // (2 * RIM)) * 2 * RIM
         return pl.pallas_call(
-            functools.partial(first_kernel, head_dim, group, low, high),
-            out_shape=jax.ShapeDtypeStruct((state_dim + RIM, high - low), BF16),
-            in_specs=[scalar, anywhere] + in_hbm,
+            functools.partial(first_kernel, group, low, high),
+            out_shape=jax.ShapeDtypeStruct((state_dim + extra, high - low), BF16),
+            in_specs=[scalar] + in_hbm,
             scratch_shapes=landed + [pltpu.SemaphoreType.DMA((len(operands),))],
             compiler_params=params(16),
             name="first_states",
-        )(here(place == 0), token, *pinned)
-
-    def joined(came, group, low, high):
+        )(here(place == 0), *pinned)
+
+    def next_states(token, group, low, high):
         return pl.pallas_call(
-            functools.partial(join_kernel, head_dim, group, low, high),
+            functools.partial(next_kernel, group, low, high),
             out_shape=jax.ShapeDtypeStruct((state_dim, high - low), BF16),
-            in_specs=[scalar] + [in_vmem] * (1 + len(operands)),
+            in_specs=[scalar, anywhere] + [in_vmem] * len(operands),
             scratch_shapes=[wide],
             compiler_params=params(16),
-            name="joined_states",
-        )(here(place == 1), came, *operands)
+            name="next_states",
+        )(here(place == 0), token, *operands)
 
     def packed(token):
         return pl.pallas_call(
             pack_kernel,
             out_shape=jax.ShapeDtypeStruct((RIM, width + groups * both), BF16),
-            in_specs=[anywhere] + in_hbm[:2],
-            scratch_shapes=[
-                pltpu.VMEM((2 * RIM, width), BF16),
-                pltpu.VMEM((2 * RIM, groups, both), BF16),
-                pltpu.SemaphoreType.DMA((2,)),
-            ],
+            in_specs=[anywhere] + [in_vmem] * 2,
             compiler_params=params(16),
             name="last_rows",
-        )(token, *pinned[:2])
-
-    def later_states(condition, got, token):
-        made = pl.pallas_call(
-            functools.partial(later_kernel, head_dim, cuts),
+        )(token, x_in, bc_in)
+
+    def later_states(condition, rows, token, group, low, high):
+        return pl.pallas_call(
+            functools.partial(later_kernel, group, low, high),
             out_shape=[
-                jax.ShapeDtypeStruct((state_dim, high - low), F32) for _, low, high in cuts
-            ]
-            + [jax.ShapeDtypeStruct((1, high - low), F32) for _, low, high in cuts],
+                jax.ShapeDtypeStruct((state_dim, high - low), F32),
+                jax.ShapeDtypeStruct((1, high - low), F32),
+            ],
             in_specs=[scalar, in_vmem, anywhere] + [in_vmem] * len(operands),
             scratch_shapes=[wide],
             compiler_params=params(16),
             name="later_states",
-        )(here(condition), got, token, *operands)
-        return made[: len(cuts)], made[len(cuts) :]
+        )(here(condition), rows, token, *operands)
 
     along = [(i, i + 1) for i in range(devices - 1)]
     if devices <= CHAIN_MOST:
-        arrived = []
-        token = a_row
-        for cut in cuts:
-            token = first_states(token, *cut)
-            arrived.append([shifted(token, along[:1])])
-        got = shifted(packed(token), along)
-        if devices > 2:
-            token = None
+        sent = [first_states(*cuts[0])]
+        for cut in cuts[1:]:
+            sent.append(next_states(sent[-1], *cut))
+        arrived = [[shifted(v, along[:1])] for v in sent]
+        last = packed(sent[-1])
+        got = shifted(last, along)
+        rows, token = arrived[0][0], last
+        for hop in range(1, devices - 1):
+            condition = place == 1 if hop == 1 else place >= 2
             for seen, cut in zip(arrived, cuts):
-                if token is not None:
-                    seen[0], _ = lax.optimization_barrier((seen[0], token))
-                token = joined(seen[0], *cut)
-                seen.append(shifted(token, along[1:2]))
-        if devices > 3:
-            states, decays = later_states(place >= 2, got, token)
-        for hop in range(2, devices - 1):
-            token = None
-            for seen, decay, state in zip(arrived, decays, states):
-                if token is not None:
-                    seen[-1], _ = lax.optimization_barrier((seen[-1], token))
-                token = (decay * seen[-1].astype(F32) + state).astype(BF16)
+                if hop <= 2:
+                    made = later_states(condition, rows, token, *cut)
+                    states = [made] if seen is arrived[0] else states + [made]
+                before, _ = lax.optimization_barrier((seen[-1], token))
+                state, decay = states[len(states) - 1 if hop <= 2 else cuts.index(cut)]
+                token = (decay * before[:state_dim].astype(F32) + state).astype(BF16)
                 seen.append(shifted(token, along[hop : hop + 1]))
+            rows = got
     else:
         got = shifted(packed(a_row), along)
-        states, decays = later_states(place >= 0, got, a_row)
-        arrived = [[doubling(state, decay, devices)] for state, decay in zip(states, decays)]
+        arrived = [
+            [doubling(*later_states(place >= 0, got, a_row, *cut), devices)] for cut in cuts
+        ]
 
     y_part, lead, c_act = pl.pallas_call(
         functools.partial(intra_kernel, head_dim),

time: 31.7 us -> 31.1 us (0.981)
  the two profiles are of different devices: /device:TPU:30 before, /device:TPU:20 now
where the time goes in v5:
time: 31.1 us; the launch traced here: 30.7 us
  starting transfers between devices  16.8 us (54%)
  Pallas kernels  8.53 us (27%)
  waiting for transfers between devices  4.01 us (13%)
  local copies, waits for them, and re-layouts  0.64 us (2%)
  between operations  0.41 us (1%)
  other arithmetic  0.33 us (1%)
    ppermute x13, starting transfers between devices, shifted(): return lax.ppermute(value, 'seq', route)  16.8 us
    ppermute x13, waiting for transfers between devices, shifted(): return lax.ppermute(value, 'seq', route)  4.01 us
    pallas_call x8, Pallas kernels, later_states(): pl.pallas_call(functools.partial(later_kernel, group, low, high), out_sha...  3.72 us
    pallas_call x1, Pallas kernels, shards(): pl.pallas_call(functools.partial(intra_kernel, head_dim), out_shape=(jax....  2.27 us
    pallas_call x2, Pallas kernels, shards(): pl.pallas_call(functools.partial(output_kernel, len(ready), len(arrived[0...  2.02 us
    unnamed x18, local copies, waits for them, and re-layouts  0.64 us
  transfers between devices with their start and end apart: 13, of which 3 were waited for; matrix products, arithmetic and copies ran while one was open for 1% of the time, Pallas kernels for 24%

profile of v5, /device:TPU:20, one launch (start us, length us, event | category | flops | bytes accessed | tf_op | source)
XLA Modules:
  0.0 30.7 jit_solution(18170756602859621724)
XLA Ops:
  0.0 0.0 copy-start.3
  0.0 0.0 copy-start.4
  0.0 0.0 copy-start.6
  0.0 0.1 first_states.1._
  0.1 0.8 %collective-permute-start.2 = (bf16[144,512]{1,0:T(8,128)(2,1)S(1)}, bf16[144,512]{1,0:T(8,128)(2,1)S(1)}, u32[]{:S(2)}, u32[]{:S(2)}) collective-permute-start(bf16[144,512]{1,0:T(8,128)(2,1)S(1)} %first_states.1._), channel_id=1, source_target_pairs={{0,4},{1,5},{2,6},{3,7},{16,20},{17,21},{18,22},{19,23}} | collective-permute-start | bytes 442376 | tf_op jit(solution)/shard_map/ppermute | solution.py:328
  0.9 0.1 copy-done
  1.0 0.0 copy-done.1
  1.1 0.0 copy-done.2
  1.1 0.0 copy-done.4
  1.1 0.7 %collective-permute-start.3 = (bf16[128,512]{1,0:T(8,128)(2,1)S(1)}, bf16[128,512]{1,0:T(8,128)(2,1)S(1)}, u32[]{:S(2)}, u32[]{:S(2)}) collective-permute-start(bf16[128,512]{1,0:T(8,128)(2,1)S(1)} %next_states.3._), channel_id=1, source_target_pairs={{0,4},{1,5},{2,6},{3,7},{16,20},{17,21},{18,22},{19,23}} | collective-permute-start | bytes 393224 | tf_op jit(solution)/shard_map/ppermute | solution.py:328
  1.8 0.7 %collective-permute-start.1 = (bf16[128,512]{1,0:T(8,128)(2,1)S(1)}, bf16[128,512]{1,0:T(8,128)(2,1)S(1)}, u32[]{:S(2)}, u32[]{:S(2)}) collective-permute-start(bf16[128,512]{1,0:T(8,128)(2,1)S(1)} %next_states.4._), channel_id=1, source_target_pairs={{0,4},{1,5},{2,6},{3,7},{16,20},{17,21},{18,22},{19,23}} | collective-permute-start | bytes 393224 | tf_op jit(solution)/shard_map/ppermute | solution.py:328
  2.5 0.7 %collective-permute-start.5 = (bf16[128,512]{1,0:T(8,128)(2,1)S(1)}, bf16[128,512]{1,0:T(8,128)(2,1)S(1)}, u32[]{:S(2)}, u32[]{:S(2)}) collective-permute-start(bf16[128,512]{1,0:T(8,128)(2,1)S(1)} %next_states.5._), channel_id=1, source_target_pairs={{0,4},{1,5},{2,6},{3,7},{16,20},{17,21},{18,22},{19,23}} | collective-permute-start | bytes 393224 | tf_op jit(solution)/shard_map/ppermute | solution.py:328
  3.2 3.5 %collective-permute-start = (bf16[8,2560]{1,0:T(8,128)(2,1)S(1)}, bf16[8,2560]{1,0:T(8,128)(2,1)S(1)}, u32[]{:S(2)}, u32[]{:S(2)}) collective-permute-start(bf16[8,2560]{1,0:T(8,128)(2,1)S(1)} %last_rows.1._), channel_id=1, source_target_pairs={{0,4},{4,8},{8,12},{1,5},{5,9},{9,13},{2,6},{6,10},{10,14},{3,7},{... | collective-permute-start | bytes 122888 | tf_op jit(solution)/shard_map/ppermute | solution.py:328
  6.7 0.0 collective-permute-done.2.rows.refs_0_
  6.8 1.3 %collective-permute-start.6 = (bf16[128,512]{1,0:T(8,128)(2,1)S(1)}, bf16[128,512]{1,0:T(8,128)(2,1)S(1)}, u32[]{:S(2)}, u32[]{:S(2)}) collective-permute-start(bf16[128,512]{1,0:T(8,128)(2,1)S(1)} %add_convert_fusion.7._), channel_id=1, source_target_pairs={{4,8},{5,9},{6,10},{7,11},{20,24},{21,25},{22,26},{23,27}} | collective-permute-start | bytes 393224 | tf_op jit(solution)/shard_map/ppermute | solution.py:328
  8.1 0.0 collective-permute-done.3.refs_1_
  8.2 1.3 %collective-permute-start.7 = (bf16[128,512]{1,0:T(8,128)(2,1)S(1)}, bf16[128,512]{1,0:T(8,128)(2,1)S(1)}, u32[]{:S(2)}, u32[]{:S(2)}) collective-permute-start(bf16[128,512]{1,0:T(8,128)(2,1)S(1)} %add_convert_fusion.6._), channel_id=1, source_target_pairs={{4,8},{5,9},{6,10},{7,11},{20,24},{21,25},{22,26},{23,27}} | collective-permute-start | bytes 393224 | tf_op jit(solution)/shard_map/ppermute | solution.py:328
  9.5 0.0 collective-permute-done.1.refs_0_
  9.5 1.3 %collective-permute-start.4 = (bf16[128,512]{1,0:T(8,128)(2,1)S(1)}, bf16[128,512]{1,0:T(8,128)(2,1)S(1)}, u32[]{:S(2)}, u32[]{:S(2)}) collective-permute-start(bf16[128,512]{1,0:T(8,128)(2,1)S(1)} %add_convert_fusion.5._), channel_id=1, source_target_pairs={{4,8},{5,9},{6,10},{7,11},{20,24},{21,25},{22,26},{23,27}} | collective-permute-start | bytes 393224 | tf_op jit(solution)/shard_map/ppermute | solution.py:328
  10.8 0.0 collective-permute-done.5.refs_1_
  10.9 1.3 %collective-permute-start.9 = (bf16[128,512]{1,0:T(8,128)(2,1)S(1)}, bf16[128,512]{1,0:T(8,128)(2,1)S(1)}, u32[]{:S(2)}, u32[]{:S(2)}) collective-permute-start(bf16[128,512]{1,0:T(8,128)(2,1)S(1)} %add_convert_fusion.4._), channel_id=1, source_target_pairs={{4,8},{5,9},{6,10},{7,11},{20,24},{21,25},{22,26},{23,27}} | collective-permute-start | bytes 393224 | tf_op jit(solution)/shard_map/ppermute | solution.py:328
  12.2 0.0 collective-permute-done.got.rows
  12.2 0.9 %later_states.12 = (f32[128,512]{1,0:T(8,128)S(1)}, f32[1,512]{1,0:T(1,128)S(1)}) custom-call(s32[1]{0:T(128)} %bitcast.9.active, bf16[8,2560]{1,0:T(8,128)(2,1)S(1)} %collective-permute-done.got.rows, bf16[128,512]{1,0:T(8,128)(2,1)S(1)} %add_convert_fusion.4._, bf16[128,2048]{1,0:T(8,128)(2,1)S(1)} %copy-done, bf16[128,2,256]{2,1,0:T(2,128)(2,1)S(1)} %copy-done.1, ...), custom_call_target="tpu_custom_call" | custom-call | tf_op jit(solution)/shard_map/later_states/pallas_call | solution.py:362
  13.1 2.0 %collective-permute-done.6.refs_1_ = bf16[128,512]{1,0:T(8,128)(2,1)S(1)} collective-permute-done((bf16[128,512]{1,0:T(8,128)(2,1)S(1)}, bf16[128,512]{1,0:T(8,128)(2,1)S(1)}, u32[]{:S(2)}, u32[]{:S(2)}) %collective-permute-start.6) | collective-permute-done | bytes 131104 | tf_op jit(solution)/shard_map/ppermute | solution.py:328
  15.2 1.3 %collective-permute-start.11 = (bf16[128,512]{1,0:T(8,128)(2,1)S(1)}, bf16[128,512]{1,0:T(8,128)(2,1)S(1)}, u32[]{:S(2)}, u32[]{:S(2)}) collective-permute-start(bf16[128,512]{1,0:T(8,128)(2,1)S(1)} %add_convert_fusion.3._), channel_id=1, source_target_pairs={{8,12},{9,13},{10,14},{11,15},{24,28},{25,29},{26,30},{27,31}} | collective-permute-start | bytes 393224 | tf_op jit(solution)/shard_map/ppermute | solution.py:328
  16.5 1.5 %collective-permute-done.7.refs_2_ = bf16[128,512]{1,0:T(8,128)(2,1)S(1)} collective-permute-done((bf16[128,512]{1,0:T(8,128)(2,1)S(1)}, bf16[128,512]{1,0:T(8,128)(2,1)S(1)}, u32[]{:S(2)}, u32[]{:S(2)}) %collective-permute-start.7) | collective-permute-done | bytes 131104 | tf_op jit(solution)/shard_map/ppermute | solution.py:328
  18.0 0.9 %later_states.13 = (f32[128,512]{1,0:T(8,128)S(1)}, f32[1,512]{1,0:T(1,128)S(1)}) custom-call(s32[1]{0:T(128)} %bitcast.9.active, bf16[8,2560]{1,0:T(8,128)(2,1)S(1)} %collective-permute-done.got.rows, bf16[128,512]{1,0:T(8,128)(2,1)S(1)} %add_convert_fusion.3._, bf16[128,2048]{1,0:T(8,128)(2,1)S(1)} %copy-done, bf16[128,2,256]{2,1,0:T(2,128)(2,1)S(1)} %copy-done.1, ...), custom_call_target="tpu_custom_call" | custom-call | tf_op jit(solution)/shard_map/later_states/pallas_call | solution.py:362
  18.9 1.3 %collective-permute-start.12 = (bf16[128,512]{1,0:T(8,128)(2,1)S(1)}, bf16[128,512]{1,0:T(8,128)(2,1)S(1)}, u32[]{:S(2)}, u32[]{:S(2)}) collective-permute-start(bf16[128,512]{1,0:T(8,128)(2,1)S(1)} %add_convert_fusion.2._), channel_id=1, source_target_pairs={{8,12},{9,13},{10,14},{11,15},{24,28},{25,29},{26,30},{27,31}} | collective-permute-start | bytes 393224 | tf_op jit(solution)/shard_map/ppermute | solution.py:328
  20.2 0.5 %collective-permute-done.4.refs_1_ = bf16[128,512]{1,0:T(8,128)(2,1)S(1)} collective-permute-done((bf16[128,512]{1,0:T(8,128)(2,1)S(1)}, bf16[128,512]{1,0:T(8,128)(2,1)S(1)}, u32[]{:S(2)}, u32[]{:S(2)}) %collective-permute-start.4) | collective-permute-done | bytes 131104 | tf_op jit(solution)/shard_map/ppermute | solution.py:328
  20.8 0.9 %later_states.14 = (f32[128,512]{1,0:T(8,128)S(1)}, f32[1,512]{1,0:T(1,128)S(1)}) custom-call(s32[1]{0:T(128)} %bitcast.9.active, bf16[8,2560]{1,0:T(8,128)(2,1)S(1)} %collective-permute-done.got.rows, bf16[128,512]{1,0:T(8,128)(2,1)S(1)} %add_convert_fusion.2._, bf16[128,2048]{1,0:T(8,128)(2,1)S(1)} %copy-done, bf16[128,2,256]{2,1,0:T(2,128)(2,1)S(1)} %copy-done.1, ...), custom_call_target="tpu_custom_call" | custom-call | tf_op jit(solution)/shard_map/later_states/pallas_call | solution.py:362
  21.7 0.0 copy-start.5
  21.7 1.4 %collective-permute-start.8 = (bf16[128,512]{1,0:T(8,128)(2,1)S(1)}, bf16[128,512]{1,0:T(8,128)(2,1)S(1)}, u32[]{:S(2)}, u32[]{:S(2)}) collective-permute-start(bf16[128,512]{1,0:T(8,128)(2,1)S(1)} %add_convert_fusion.1._), channel_id=1, source_target_pairs={{8,12},{9,13},{10,14},{11,15},{24,28},{25,29},{26,30},{27,31}} | collective-permute-start | bytes 393224 | tf_op jit(solution)/shard_map/ppermute | solution.py:328
  23.2 0.0 collective-permute-done.9.refs_2_
  23.2 0.9 %later_states.15 = (f32[128,512]{1,0:T(8,128)S(1)}, f32[1,512]{1,0:T(1,128)S(1)}) custom-call(s32[1]{0:T(128)} %bitcast.9.active, bf16[8,2560]{1,0:T(8,128)(2,1)S(1)} %collective-permute-done.got.rows, bf16[128,512]{1,0:T(8,128)(2,1)S(1)} %add_convert_fusion.1._, bf16[128,2048]{1,0:T(8,128)(2,1)S(1)} %copy-done, bf16[128,2,256]{2,1,0:T(2,128)(2,1)S(1)} %copy-done.1, ...), custom_call_target="tpu_custom_call" | custom-call | tf_op jit(solution)/shard_map/later_states/pallas_call | solution.py:362
  24.1 0.0 copy-start.8
  24.2 1.3 %collective-permute-start.10 = (bf16[128,512]{1,0:T(8,128)(2,1)S(1)}, bf16[128,512]{1,0:T(8,128)(2,1)S(1)}, u32[]{:S(2)}, u32[]{:S(2)}) collective-permute-start(bf16[128,512]{1,0:T(8,128)(2,1)S(1)} %add_convert_fusion), channel_id=1, source_target_pairs={{8,12},{9,13},{10,14},{11,15},{24,28},{25,29},{26,30},{27,31}} | collective-permute-start | bytes 393224 | tf_op jit(solution)/shard_map/ppermute | solution.py:328
  25.5 0.0 copy-done.5
  25.5 2.3 %intra.1 = (f32[128,2048]{1,0:T(8,128)S(1)}, f32[128,2048]{1,0:T(8,128)S(1)}, bf16[128,256]{1,0:T(8,128)(2,1)S(1)}) custom-call(bf16[128,2048]{1,0:T(8,128)(2,1)S(1)} %copy-done, bf16[8,2560]{1,0:T(8,128)(2,1)S(1)} %collective-permute-done.got.rows, bf16[128,2,256]{2,1,0:T(2,128)(2,1)S(1)} %copy-done.1, bf16[128,2048]{1,0:T(8,128)(2,1)S(1)} %copy-done.5, ...), custom_call_target="tpu_custom_call" | custom-call | flops 134217728 | bytes 3145728 | tf_op jit(solution)/shard_map/intra/pallas_call | solution.py:400
  27.8 0.0 collective-permute-done.11.refs_2_
  27.8 0.2 gated.3.refs_0_
  28.0 0.0 copy-start.7
  28.0 0.0 collective-permute-done.8.refs_2_
  28.0 0.2 gated.2.refs_0_
  28.2 0.0 collective-permute-done.12.refs_3_
  28.2 0.5 %copy-done.7 = f32[2048]{0:T(1024)S(1)} copy-done((f32[2048]{0:T(1024)S(1)}, f32[2048]{0:T(1024)}, u32[]{:S(2)}) %copy-start.7) | copy-done | bytes 8216
  28.7 1.0 %outputs.2.refs_4_ = bf16[128,2048]{1,0:T(8,128)(2,1)} custom-call(bf16[128,256]{1,0:T(8,128)(2,1)S(1)} %get-tuple-element.32.c, f32[128,2048]{1,0:T(8,128)S(1)} %get-tuple-element.33.y_part, f32[128,2048]{1,0:T(8,128)S(1)} %get-tuple-element.34.lead, f32[1,2048]{1,0:T(1,128)S(1)} %bitcast.41, f32[128,512]{1,0:T(8,128)S(1)} %gated.3.refs_0_, ...), custom_call_target="tpu_custom_call" | custom-call | tf_op jit(solution)/shard_map/outputs/pallas_call | solution.py:444
  29.7 0.0 collective-permute-done.10.refs_3_
  29.7 1.0 %outputs.3 = bf16[128,2048]{1,0:T(8,128)(2,1)} custom-call(bf16[128,256]{1,0:T(8,128)(2,1)S(1)} %get-tuple-element.32.c, f32[128,2048]{1,0:T(8,128)S(1)} %get-tuple-element.33.y_part, f32[128,2048]{1,0:T(8,128)S(1)} %get-tuple-element.34.lead, f32[1,2048]{1,0:T(1,128)S(1)} %bitcast.42, f32[128,512]{1,0:T(8,128)S(1)} %gated.2.refs_0_, ...), custom_call_target="tpu_custom_call", output_to_operand_aliasing={{}: (8, {})} | custom-call | tf_op jit(solution)/shard_map/outputs/pallas_call | solution.py:444
  (22 shorter events, 0.4 us)
Async XLA Ops:
  0.0 1.0 %copy-start = (bf16[128,2048]{1,0:T(8,128)(2,1)S(1)}, bf16[128,2048]{1,0:T(8,128)(2,1)}, u32[]{:S(2)}) copy-start(bf16[128,2048]{1,0:T(8,128)(2,1)} %x.25) | copy-start | bytes 1572868
  0.0 1.1 %copy-start.1 = (bf16[128,2,256]{2,1,0:T(2,128)(2,1)S(1)}, bf16[128,2,256]{2,1,0:T(2,128)(2,1)}, u32[]{:S(2)}) copy-start(bf16[128,2,256]{2,1,0:T(2,128)(2,1)} %bc.25) | copy-start | bytes 393220
  0.0 1.1 %copy-start.2 = (f32[4,2048]{1,0:T(4,128)S(1)}, f32[4,2048]{1,0:T(4,128)}, u32[]{:S(2)}) copy-start(f32[4,2048]{1,0:T(4,128)} %taps_x.23) | copy-start | bytes 98308
  0.0 1.1 %copy-start.3 = (f32[128,32]{0,1:T(8,128)S(1)}, f32[128,32]{0,1:T(8,128)}, u32[]{:S(2)}) copy-start(f32[128,32]{0,1:T(8,128)} %param.12) | copy-start | bytes 49156
  0.0 1.1 %copy-start.4 = (f32[4,2,256]{2,1,0:T(2,128)S(1)}, f32[4,2,256]{2,1,0:T(2,128)}, u32[]{:S(2)}) copy-start(f32[4,2,256]{2,1,0:T(2,128)} %taps_bc.23) | copy-start | bytes 24580
  0.0 1.0 %copy-start.6 = (f32[32]{0:T(128)S(1)}, f32[32]{0:T(128)}, u32[]{:S(2)}) copy-start(f32[32]{0:T(128)} %param.15) | copy-start | bytes 388
  0.1 6.6 %collective-permute-start.2 = (bf16[144,512]{1,0:T(8,128)(2,1)S(1)}, bf16[144,512]{1,0:T(8,128)(2,1)S(1)}, u32[]{:S(2)}, u32[]{:S(2)}) collective-permute-start(bf16[144,512]{1,0:T(8,128)(2,1)S(1)} %first_states.1._), channel_id=1, source_target_pairs={{0,4},{1,5},{2,6},{3,7},{16,20},{17,21},{18,22},{19,23}} | collective-permute-start | bytes 442376 | tf_op jit(solution)/shard_map/ppermute | solution.py:328
  1.1 7.0 %collective-permute-start.3 = (bf16[128,512]{1,0:T(8,128)(2,1)S(1)}, bf16[128,512]{1,0:T(8,128)(2,1)S(1)}, u32[]{:S(2)}, u32[]{:S(2)}) collective-permute-start(bf16[128,512]{1,0:T(8,128)(2,1)S(1)} %next_states.3._), channel_id=1, source_target_pairs={{0,4},{1,5},{2,6},{3,7},{16,20},{17,21},{18,22},{19,23}} | collective-permute-start | bytes 393224 | tf_op jit(solution)/shard_map/ppermute | solution.py:328
  1.8 7.7 %collective-permute-start.1 = (bf16[128,512]{1,0:T(8,128)(2,1)S(1)}, bf16[128,512]{1,0:T(8,128)(2,1)S(1)}, u32[]{:S(2)}, u32[]{:S(2)}) collective-permute-start(bf16[128,512]{1,0:T(8,128)(2,1)S(1)} %next_states.4._), channel_id=1, source_target_pairs={{0,4},{1,5},{2,6},{3,7},{16,20},{17,21},{18,22},{19,23}} | collective-permute-start | bytes 393224 | tf_op jit(solution)/shard_map/ppermute | solution.py:328
  2.5 8.3 %collective-permute-start.5 = (bf16[128,512]{1,0:T(8,128)(2,1)S(1)}, bf16[128,512]{1,0:T(8,128)(2,1)S(1)}, u32[]{:S(2)}, u32[]{:S(2)}) collective-permute-start(bf16[128,512]{1,0:T(8,128)(2,1)S(1)} %next_states.5._), channel_id=1, source_target_pairs={{0,4},{1,5},{2,6},{3,7},{16,20},{17,21},{18,22},{19,23}} | collective-permute-start | bytes 393224 | tf_op jit(solution)/shard_map/ppermute | solution.py:328
  3.2 9.0 %collective-permute-start = (bf16[8,2560]{1,0:T(8,128)(2,1)S(1)}, bf16[8,2560]{1,0:T(8,128)(2,1)S(1)}, u32[]{:S(2)}, u32[]{:S(2)}) collective-permute-start(bf16[8,2560]{1,0:T(8,128)(2,1)S(1)} %last_rows.1._), channel_id=1, source_target_pairs={{0,4},{4,8},{8,12},{1,5},{5,9},{9,13},{2,6},{6,10},{10,14},{3,7},{... | collective-permute-start | bytes 122888 | tf_op jit(solution)/shard_map/ppermute | solution.py:328
  6.8 8.3 %collective-permute-start.6 = (bf16[128,512]{1,0:T(8,128)(2,1)S(1)}, bf16[128,512]{1,0:T(8,128)(2,1)S(1)}, u32[]{:S(2)}, u32[]{:S(2)}) collective-permute-start(bf16[128,512]{1,0:T(8,128)(2,1)S(1)} %add_convert_fusion.7._), channel_id=1, source_target_pairs={{4,8},{5,9},{6,10},{7,11},{20,24},{21,25},{22,26},{23,27}} | collective-permute-start | bytes 393224 | tf_op jit(solution)/shard_map/ppermute | solution.py:328
  8.2 9.8 %collective-permute-start.7 = (bf16[128,512]{1,0:T(8,128)(2,1)S(1)}, bf16[128,512]{1,0:T(8,128)(2,1)S(1)}, u32[]{:S(2)}, u32[]{:S(2)}) collective-permute-start(bf16[128,512]{1,0:T(8,128)(2,1)S(1)} %add_convert_fusion.6._), channel_id=1, source_target_pairs={{4,8},{5,9},{6,10},{7,11},{20,24},{21,25},{22,26},{23,27}} | collective-permute-start | bytes 393224 | tf_op jit(solution)/shard_map/ppermute | solution.py:328
  9.5 11.2 %collective-permute-start.4 = (bf16[128,512]{1,0:T(8,128)(2,1)S(1)}, bf16[128,512]{1,0:T(8,128)(2,1)S(1)}, u32[]{:S(2)}, u32[]{:S(2)}) collective-permute-start(bf16[128,512]{1,0:T(8,128)(2,1)S(1)} %add_convert_fusion.5._), channel_id=1, source_target_pairs={{4,8},{5,9},{6,10},{7,11},{20,24},{21,25},{22,26},{23,27}} | collective-permute-start | bytes 393224 | tf_op jit(solution)/shard_map/ppermute | solution.py:328
  10.9 12.3 %collective-permute-start.9 = (bf16[128,512]{1,0:T(8,128)(2,1)S(1)}, bf16[128,512]{1,0:T(8,128)(2,1)S(1)}, u32[]{:S(2)}, u32[]{:S(2)}) collective-permute-start(bf16[128,512]{1,0:T(8,128)(2,1)S(1)} %add_convert_fusion.4._), channel_id=1, source_target_pairs={{4,8},{5,9},{6,10},{7,11},{20,24},{21,25},{22,26},{23,27}} | collective-permute-start | bytes 393224 | tf_op jit(solution)/shard_map/ppermute | solution.py:328
  15.2 12.6 %collective-permute-start.11 = (bf16[128,512]{1,0:T(8,128)(2,1)S(1)}, bf16[128,512]{1,0:T(8,128)(2,1)S(1)}, u32[]{:S(2)}, u32[]{:S(2)}) collective-permute-start(bf16[128,512]{1,0:T(8,128)(2,1)S(1)} %add_convert_fusion.3._), channel_id=1, source_target_pairs={{8,12},{9,13},{10,14},{11,15},{24,28},{25,29},{26,30},{27,31}} | collective-permute-start | bytes 393224 | tf_op jit(solution)/shard_map/ppermute | solution.py:328
  18.9 9.3 %collective-permute-start.12 = (bf16[128,512]{1,0:T(8,128)(2,1)S(1)}, bf16[128,512]{1,0:T(8,128)(2,1)S(1)}, u32[]{:S(2)}, u32[]{:S(2)}) collective-permute-start(bf16[128,512]{1,0:T(8,128)(2,1)S(1)} %add_convert_fusion.2._), channel_id=1, source_target_pairs={{8,12},{9,13},{10,14},{11,15},{24,28},{25,29},{26,30},{27,31}} | collective-permute-start | bytes 393224 | tf_op jit(solution)/shard_map/ppermute | solution.py:328
  21.7 3.7 %copy-start.5 = (bf16[128,2048]{1,0:T(8,128)(2,1)S(1)}, bf16[128,2048]{1,0:T(8,128)(2,1)}, u32[]{:S(2)}) copy-start(bf16[128,2048]{1,0:T(8,128)(2,1)} %z.1) | copy-start | bytes 1572868
  21.7 6.3 %collective-permute-start.8 = (bf16[128,512]{1,0:T(8,128)(2,1)S(1)}, bf16[128,512]{1,0:T(8,128)(2,1)S(1)}, u32[]{:S(2)}, u32[]{:S(2)}) collective-permute-start(bf16[128,512]{1,0:T(8,128)(2,1)S(1)} %add_convert_fusion.1._), channel_id=1, source_target_pairs={{8,12},{9,13},{10,14},{11,15},{24,28},{25,29},{26,30},{27,31}} | collective-permute-start | bytes 393224 | tf_op jit(solution)/shard_map/ppermute | solution.py:328
  24.1 1.3 %copy-start.8 = (f32[32]{0:T(128)S(1)}, f32[32]{0:T(128)}, u32[]{:S(2)}) copy-start(f32[32]{0:T(128)} %param.16) | copy-start | bytes 388
  24.2 5.5 %collective-permute-start.10 = (bf16[128,512]{1,0:T(8,128)(2,1)S(1)}, bf16[128,512]{1,0:T(8,128)(2,1)S(1)}, u32[]{:S(2)}, u32[]{:S(2)}) collective-permute-start(bf16[128,512]{1,0:T(8,128)(2,1)S(1)} %add_convert_fusion), channel_id=1, source_target_pairs={{8,12},{9,13},{10,14},{11,15},{24,28},{25,29},{26,30},{27,31}} | collective-permute-start | bytes 393224 | tf_op jit(solution)/shard_map/ppermute | solution.py:328
  28.0 0.7 %copy-start.7 = (f32[2048]{0:T(1024)S(1)}, f32[2048]{0:T(1024)}, u32[]{:S(2)}) copy-start(f32[2048]{0:T(1024)} %param.17) | copy-start | bytes 24580

commit v6 on v5

--- a/solution.py
+++ b/solution.py
@@ -11,8 +11,9 @@
 F32 = jnp.float32
 BF16 = jnp.bfloat16
 CHAIN_MOST = 4
-PER_GROUP = 2
-CHUNK = 256
+FIRST_PARTS = (3, 5)
+OTHER_PARTS = (1, 1)
+CHUNK = 128
 RIM = 8
 
 
@@ -79,50 +80,41 @@
     return dt, cum
 
 
-def emit_states(
-    head_dim, group, chunks, x, tail_x, bc, tail_bc, taps_x, taps_bc, dt_raw, a_log, wide, emit
-):
+def scales(head_dim, dt_raw, a_log, scale):
     dt, cum = rates(dt_raw[...], a_log[...], 0)
     end = cum[:, -1:]
-    tail_decay = jnp.exp(end - cum) * dt
+    scale[...] = spread(jnp.exp(end - cum) * dt, head_dim, 2)
+    return spread_row(jnp.exp(end), head_dim)
+
+
+def emit_states(group, low, high, x, tail_x, bc, tail_bc, taps_x, taps_bc, scale, emit):
     state_dim = bc.shape[2] // 2
-    heads = dt.shape[0] // bc.shape[1]
-    mine = slice(group * heads, (group + 1) * heads)
     b = conv_act(
         bc[:, :, :state_dim].astype(F32)[:, group], tail_bc, taps_bc[:, :, :state_dim][:, group]
     )
     b_t = b.astype(F32).T.astype(BF16)
-    wide[...] = spread(tail_decay[mine], head_dim, 2)
-    decay = spread_row(jnp.exp(end[mine]), head_dim)
-    for cut in chunks:
+    for at in range(low, high, CHUNK):
+        cut = slice(at, at + CHUNK)
         act = conv_act(x[:, cut].astype(F32), tail_x(cut), taps_x[:, cut])
-        at = cut.start - group * heads * head_dim
-        here = slice(at, at + cut.stop - cut.start)
-        scaled = (wide[:, here] * act.astype(F32)).astype(BF16)
-        emit(cut, jnp.dot(b_t, scaled, preferred_element_type=F32), decay[:, here])
-
-
-def chunks_of(low, high):
-    return [slice(at, at + CHUNK) for at in range(low, high, CHUNK)]
-
-
-def head_rows(x, bc, group, low, high, out, taps_x, taps_bc, dt_raw, a_log, wide):
-    head_dim = x.shape[1] // dt_raw.shape[0]
+        scaled = (scale[:, cut] * act.astype(F32)).astype(BF16)
+        emit(slice(at - low, at - low + CHUNK), jnp.dot(b_t, scaled, preferred_element_type=F32))
+
+
+def head_rows(group, low, high, x, bc, taps_x, taps_bc, scale, out):
     state_dim = bc.shape[2] // 2
 
-    def emit(cut, total, _):
-        out[:state_dim, cut.start - low : cut.stop - low] = total.astype(BF16)
+    def emit(here, total):
+        out[:state_dim, here] = total.astype(BF16)
 
     emit_states(
-        head_dim, group, chunks_of(low, high), x,
-        lambda cut: jnp.zeros((RIM, cut.stop - cut.start), F32),
-        bc, jnp.zeros((RIM, state_dim), F32), taps_x, taps_bc, dt_raw, a_log, wide, emit,
+        group, low, high, x, lambda cut: jnp.zeros((RIM, CHUNK), F32),
+        bc, jnp.zeros((RIM, state_dim), F32), taps_x, taps_bc, scale, emit,
     )
 
 
 def first_kernel(
     group, low, high, active, x_hbm, bc_hbm, taps_x_hbm, taps_bc_hbm, dt_hbm, a_hbm,
-    out, x, bc, taps_x, taps_bc, dt_raw, a_log, wide, sems,
+    out, scale, x, bc, taps_x, taps_bc, dt_raw, a_log, sems,
 ):
     tokens, width = x.shape
     groups, both = bc.shape[1:]
@@ -130,56 +122,59 @@
     @pl.when(active[0] == 1)
     def _():
         pairs = [
-            (x_hbm, x), (bc_hbm, bc), (taps_x_hbm, taps_x),
-            (taps_bc_hbm, taps_bc), (dt_hbm, dt_raw), (a_hbm, a_log),
+            (dt_hbm, dt_raw), (a_hbm, a_log), (x_hbm, x), (bc_hbm, bc),
+            (taps_x_hbm, taps_x), (taps_bc_hbm, taps_bc),
         ]
         copies = [pltpu.make_async_copy(*pair, sems.at[i]) for i, pair in enumerate(pairs)]
         for copy in copies:
             copy.start()
-        for copy in copies:
+        for copy in copies[:2]:
+            copy.wait()
+        scales(width // dt_raw.shape[0], dt_raw, a_log, scale)
+        for copy in copies[2:]:
             copy.wait()
         state_dim, step = both // 2, high - low
         keep = taps_x.shape[0] - 1
         extra = out.shape[0] - state_dim
         last_bc = bc[tokens - 2 * RIM :].astype(F32)[-RIM:]
         last = [x[tokens - 2 * RIM :, :].astype(F32)[-RIM:]] + [last_bc[:, g] for g in range(groups)]
+        length = width + groups * both
+        last.append(jnp.zeros((RIM, -length % step + step), F32))
         last = jnp.concatenate(last, axis=1)
         at = lax.broadcasted_iota(jnp.int32, (extra, step), 0)
         below = jnp.zeros((extra, step), F32)
         fill = jnp.zeros((extra - RIM, step), F32)
-        for k in range(last.shape[1] // step):
+        for k in range(-(-length // step)):
             block = jnp.concatenate([last[:, k * step : (k + 1) * step], fill], axis=0)
             block = pltpu.roll(block, (keep * (k + 1) - RIM) % extra, 0)
             below = jnp.where((at >= keep * k) & (at < keep * (k + 1)), block, below)
         out[state_dim:, :] = below.astype(BF16)
-        head_rows(x, bc, group, low, high, out, taps_x, taps_bc, dt_raw, a_log, wide)
-
-
-def next_kernel(
-    group, low, high, active, _, x, bc, taps_x, taps_bc, dt_raw, a_log, out, wide
-):
+        head_rows(group, low, high, x, bc, taps_x, taps_bc, scale, out)
+
+
+def next_kernel(group, low, high, active, _, x, bc, taps_x, taps_bc, scale, out):
     @pl.when(active[0] == 1)
     def _():
-        head_rows(x, bc, group, low, high, out, taps_x, taps_bc, dt_raw, a_log, wide)
-
-
-def pack_kernel(_, x, bc, pack):
+        head_rows(group, low, high, x, bc, taps_x, taps_bc, scale, out)
+
+
+def prepare_kernel(cuts, _, x, bc, dt_raw, a_log, pack, scale, *decays):
     tokens, width = x.shape
     groups, both = bc.shape[1:]
     pack[:, :width] = x[tokens - 2 * RIM :, :].astype(F32)[-RIM:].astype(BF16)
     last_bc = bc[tokens - 2 * RIM :].astype(F32)[-RIM:]
     for g in range(groups):
         pack[:, width + g * both : width + (g + 1) * both] = last_bc[:, g].astype(BF16)
-
-
-def later_kernel(
-    group, low, high, active, rows, _, x, bc, taps_x, taps_bc, dt_raw, a_log, state, decay, wide
-):
+    row = scales(width // dt_raw.shape[0], dt_raw, a_log, scale)
+    for decay, (_, low, high) in zip(decays, cuts):
+        decay[...] = row[:, low:high]
+
+
+def later_kernel(group, low, high, active, rows, _, x, bc, taps_x, taps_bc, scale, state):
     width = x.shape[1]
     both = bc.shape[2]
     state_dim = both // 2
     keep = taps_x.shape[0] - 1
-    head_dim = width // dt_raw.shape[0]
 
     def tail(begin, stop):
         if rows.shape[0] == RIM:
@@ -191,15 +186,13 @@
 
     @pl.when(active[0] == 1)
     def _():
-        def emit(cut, total, along):
-            here = slice(cut.start - low, cut.stop - low)
+        def emit(here, total):
             state[:, here] = total
-            decay[:, here] = along
 
         at = width + group * both
         emit_states(
-            head_dim, group, chunks_of(low, high), x, lambda cut: tail(cut.start, cut.stop),
-            bc, tail(at, at + state_dim), taps_x, taps_bc, dt_raw, a_log, wide, emit,
+            group, low, high, x, lambda cut: tail(cut.start, cut.stop),
+            bc, tail(at, at + state_dim), taps_x, taps_bc, scale, emit,
         )
 
 
@@ -298,18 +291,22 @@
     cols = width // groups
     devices = lax.axis_size("seq")
     place = lax.axis_index("seq")
-    step = cols // PER_GROUP
-    cuts = [(at // cols, at, at + step) for at in range(0, width, step)]
+    cuts = []
+    for g in range(groups):
+        parts = FIRST_PARTS if g == 0 else OTHER_PARTS
+        edges = [g * cols + cols * sum(parts[:i]) // sum(parts) for i in range(len(parts) + 1)]
+        cuts += [(g, low, high) for low, high in zip(edges[:-1], edges[1:])]
 
     taps = conv_x.shape[0]
     dt_t = dt_raw.T
     a_row = a_log.reshape(1, heads)
     d_row = d_skip.reshape(1, heads)
     gain = norm_gain.reshape(1, width)
-    operands = [x_in, bc_in, conv_x, conv_bc, dt_t, a_row]
+    sources = [x_in, bc_in, conv_x, conv_bc]
+    operands = sources + [dt_t, a_row]
     pinned = [pltpu.with_memory_space_constraint(v, pltpu.HBM) for v in operands]
-    wide = pltpu.VMEM((tokens, cols), F32)
-    landed = [pltpu.VMEM(v.shape, v.dtype) for v in operands] + [wide]
+    landed = [pltpu.VMEM(v.shape, v.dtype) for v in operands]
+    scale_shape = jax.ShapeDtypeStruct((tokens, width), F32)
     scalar = pl.BlockSpec(memory_space=pltpu.SMEM)
     in_vmem = pl.BlockSpec(memory_space=pltpu.VMEM)
     anywhere = pl.BlockSpec(memory_space=pl.ANY)
@@ -318,6 +315,9 @@
     def column(height, wide, at):
         return pl.BlockSpec((height, wide), lambda i: (0, at))
 
+    def slab(low, high):
+        return pl.BlockSpec((pl.Element(tokens), pl.Element(high - low)), lambda i: (0, low))
+
     def whole(array):
         return pl.BlockSpec(array.shape, lambda i: (0,) * len(array.shape))
 
@@ -328,74 +328,76 @@
         return lax.ppermute(value, "seq", route)
 
     def first_states(group, low, high):
-        blocks = (width + groups * both) // step
+        blocks = -(-(width + groups * both) // (high - low))
         extra = -(-(taps - 1) * blocks // (2 * RIM)) * 2 * RIM
         return pl.pallas_call(
             functools.partial(first_kernel, group, low, high),
-            out_shape=jax.ShapeDtypeStruct((state_dim + extra, high - low), BF16),
+            out_shape=[jax.ShapeDtypeStruct((state_dim + extra, high - low), BF16), scale_shape],
             in_specs=[scalar] + in_hbm,
             scratch_shapes=landed + [pltpu.SemaphoreType.DMA((len(operands),))],
             compiler_params=params(16),
             name="first_states",
         )(here(place == 0), *pinned)
 
-    def next_states(token, group, low, high):
+    def next_states(token, scale, group, low, high):
         return pl.pallas_call(
             functools.partial(next_kernel, group, low, high),
             out_shape=jax.ShapeDtypeStruct((state_dim, high - low), BF16),
-            in_specs=[scalar, anywhere] + [in_vmem] * len(operands),
-            scratch_shapes=[wide],
+            in_specs=[scalar, anywhere] + [in_vmem] * (len(sources) + 1),
             compiler_params=params(16),
             name="next_states",
-        )(here(place == 0), token, *operands)
-
-    def packed(token):
+        )(here(place == 0), token, *sources, scale)
+
+    def prepared(token):
         return pl.pallas_call(
-            pack_kernel,
-            out_shape=jax.ShapeDtypeStruct((RIM, width + groups * both), BF16),
-            in_specs=[anywhere] + [in_vmem] * 2,
+            functools.partial(prepare_kernel, cuts),
+            out_shape=[jax.ShapeDtypeStruct((RIM, width + groups * both), BF16), scale_shape]
+            + [jax.ShapeDtypeStruct((1, high - low), F32) for _, low, high in cuts],
+            in_specs=[anywhere] + [in_vmem] * 4,
             compiler_params=params(16),
-            name="last_rows",
-        )(token, x_in, bc_in)
-
-    def later_states(condition, rows, token, group, low, high):
+            name="prepared",
+        )(token, x_in, bc_in, dt_t, a_row)
+
+    def later_states(condition, rows, token, scale, group, low, high):
         return pl.pallas_call(
             functools.partial(later_kernel, group, low, high),
-            out_shape=[
-                jax.ShapeDtypeStruct((state_dim, high - low), F32),
-                jax.ShapeDtypeStruct((1, high - low), F32),
-            ],
-            in_specs=[scalar, in_vmem, anywhere] + [in_vmem] * len(operands),
-            scratch_shapes=[wide],
+            out_shape=jax.ShapeDtypeStruct((state_dim, high - low), F32),
+            in_specs=[scalar, in_vmem, anywhere] + [in_vmem] * (len(sources) + 1),
             compiler_params=params(16),
             name="later_states",
-        )(here(condition), rows, token, *operands)
+        )(here(condition), rows, token, *sources, scale)
 
     along = [(i, i + 1) for i in range(devices - 1)]
     if devices <= CHAIN_MOST:
-        sent = [first_states(*cuts[0])]
+        first, scale = first_states(*cuts[0])
+        sent = [first]
         for cut in cuts[1:]:
-            sent.append(next_states(sent[-1], *cut))
+            sent.append(next_states(sent[-1], scale, *cut))
+        last, scale, *decays = prepared(sent[-1])
+        got = shifted(last, along)
         arrived = [[shifted(v, along[:1])] for v in sent]
-        last = packed(sent[-1])
-        got = shifted(last, along)
         rows, token = arrived[0][0], last
         for hop in range(1, devices - 1):
             condition = place == 1 if hop == 1 else place >= 2
-            for seen, cut in zip(arrived, cuts):
+            after = token
+            for i, (seen, cut) in enumerate(zip(arrived, cuts)):
                 if hop <= 2:
-                    made = later_states(condition, rows, token, *cut)
-                    states = [made] if seen is arrived[0] else states + [made]
-                before, _ = lax.optimization_barrier((seen[-1], token))
-                state, decay = states[len(states) - 1 if hop <= 2 else cuts.index(cut)]
-                token = (decay * before[:state_dim].astype(F32) + state).astype(BF16)
+                    made = later_states(condition, rows, after, scale, *cut)
+                    states = [made] if i == 0 else states + [made]
+                early = arrived[0][-1] if hop > 1 and i == len(cuts) - 1 else token
+                before, _, _ = lax.optimization_barrier((seen[-1], token, early))
+                joined = decays[i] * before[:state_dim].astype(F32) + states[i]
+                token = joined.astype(BF16)
+                after = token if hop == 1 and i == 0 else after
                 seen.append(shifted(token, along[hop : hop + 1]))
             rows = got
     else:
-        got = shifted(packed(a_row), along)
-        arrived = [
-            [doubling(*later_states(place >= 0, got, a_row, *cut), devices)] for cut in cuts
-        ]
+        last, scale, *decays = prepared(a_row)
+        got = shifted(last, along)
+        arrived = []
+        for decay, cut in zip(decays, cuts):
+            state = later_states(place >= 0, got, a_row, scale, *cut)
+            arrived.append([doubling(state, decay, devices)])
 
     y_part, lead, c_act = pl.pallas_call(
         functools.partial(intra_kernel, head_dim),
@@ -421,14 +423,14 @@
             if group != g:
                 continue
             inputs = [c_act, y_part, lead]
-            specs = [column(tokens, state_dim, g)] + [column(tokens, step, low // step)] * 2
+            specs = [column(tokens, state_dim, g)] + [slab(low, high)] * 2
             if high < (g + 1) * cols:
                 ready.append(
                     pl.pallas_call(
                         gated_kernel,
-                        out_shape=jax.ShapeDtypeStruct((tokens, step), F32),
+                        out_shape=jax.ShapeDtypeStruct((tokens, high - low), F32),
                         in_specs=specs + [whole(v) for v in seen],
-                        out_specs=column(tokens, step, 0),
+                        out_specs=column(tokens, high - low, 0),
                         grid=(1,),
                         compiler_params=params(16),
                         name="gated",

time: 31.1 us -> 30.7 us (0.987)
  the two profiles are of different devices: /device:TPU:20 before, /device:TPU:30 now
where the time goes in v6:
time: 30.7 us; the launch traced here: 30.3 us
  starting transfers between devices  12.1 us (39%)
  waiting for transfers between devices  9.94 us (32%)
  Pallas kernels  7.3 us (24%)
  between operations  0.4 us (1%)
  other arithmetic  0.37 us (1%)
    ppermute x13, starting transfers between devices, shifted(): return lax.ppermute(value, 'seq', route)  12.1 us
    ppermute x13, waiting for transfers between devices, shifted(): return lax.ppermute(value, 'seq', route)  9.94 us
    pallas_call x1, Pallas kernels, shards(): pl.pallas_call(functools.partial(intra_kernel, head_dim), out_shape=(jax....  2.26 us
    pallas_call x2, Pallas kernels, shards(): pl.pallas_call(functools.partial(output_kernel, len(ready), len(arrived[0...  2.05 us
    pallas_call x8, Pallas kernels, later_states(): pl.pallas_call(functools.partial(later_kernel, group, low, high), out_sha...  1.82 us
    pallas_call x1, Pallas kernels, prepared(): pl.pallas_call(functools.partial(prepare_kernel, cuts), out_shape=[jax.Sh...  0.71 us
  transfers between devices with their start and end apart: 13, of which 4 were waited for; matrix products, arithmetic and copies ran while one was open for 1% of the time, Pallas kernels for 21%

profile of v6, /device:TPU:30, one launch (start us, length us, event | category | flops | bytes accessed | tf_op | source)
XLA Modules:
  0.0 30.3 jit_solution(17166027839510559742)
XLA Ops:
  0.0 0.1 first_states.1
  0.1 0.8 %collective-permute-start.3 = (bf16[160,384]{1,0:T(8,128)(2,1)S(1)}, bf16[160,384]{1,0:T(8,128)(2,1)S(1)}, u32[]{:S(2)}, u32[]{:S(2)}) collective-permute-start(bf16[160,384]{1,0:T(8,128)(2,1)S(1)} %get-tuple-element.24._), channel_id=1, source_target_pairs={{0,4},{1,5},{2,6},{3,7},{16,20},{17,21},{18,22},{19,23}} | collective-permute-start | bytes 368648 | tf_op jit(solution)/shard_map/ppermute | solution.py:328
  0.9 0.1 copy-done
  1.0 0.0 copy-done.1
  1.1 0.0 copy-done.2
  1.1 0.7 %collective-permute-start.2 = (bf16[128,640]{1,0:T(8,128)(2,1)S(1)}, bf16[128,640]{1,0:T(8,128)(2,1)S(1)}, u32[]{:S(2)}, u32[]{:S(2)}) collective-permute-start(bf16[128,640]{1,0:T(8,128)(2,1)S(1)} %next_states.3._), channel_id=1, source_target_pairs={{0,4},{1,5},{2,6},{3,7},{16,20},{17,21},{18,22},{19,23}} | collective-permute-start | bytes 491528 | tf_op jit(solution)/shard_map/ppermute | solution.py:328
  1.8 0.0 copy-start.5
  1.8 0.0 copy-start.7
  1.8 0.7 %collective-permute-start.1 = (bf16[128,512]{1,0:T(8,128)(2,1)S(1)}, bf16[128,512]{1,0:T(8,128)(2,1)S(1)}, u32[]{:S(2)}, u32[]{:S(2)}) collective-permute-start(bf16[128,512]{1,0:T(8,128)(2,1)S(1)} %next_states.4._), channel_id=1, source_target_pairs={{0,4},{1,5},{2,6},{3,7},{16,20},{17,21},{18,22},{19,23}} | collective-permute-start | bytes 393224 | tf_op jit(solution)/shard_map/ppermute | solution.py:328
  2.5 0.7 %collective-permute-start.7 = (bf16[128,512]{1,0:T(8,128)(2,1)S(1)}, bf16[128,512]{1,0:T(8,128)(2,1)S(1)}, u32[]{:S(2)}, u32[]{:S(2)}) collective-permute-start(bf16[128,512]{1,0:T(8,128)(2,1)S(1)} %next_states.5._), channel_id=1, source_target_pairs={{0,4},{1,5},{2,6},{3,7},{16,20},{17,21},{18,22},{19,23}} | collective-permute-start | bytes 393224 | tf_op jit(solution)/shard_map/ppermute | solution.py:328
  3.2 0.7 %prepared.1 = (bf16[8,2560]{1,0:T(8,128)(2,1)S(1)}, f32[128,2048]{1,0:T(8,128)S(1)}, f32[1,384]{1,0:T(1,128)S(1)}, f32[1,640]{1,0:T(1,128)S(1)}, f32[1,512]{1,0:T(1,128)S(1)}, /*index=5*/f32[1,512]{1,0:T(1,128)S(1)}) custom-call(bf16[128,512]{1,0:T(8,128)(2,1)S(1)} %next_states.5._, bf16[128,2048]{1,0:T(8,128)(2,1)S(1)} %copy-done, ...), custom_call_target="tpu_custom_call" | custom-call | tf_op jit(solution)/shard_map/prepared/pallas_call | solution.py:352
  3.9 1.3 %collective-permute-start = (bf16[8,2560]{1,0:T(8,128)(2,1)S(1)}, bf16[8,2560]{1,0:T(8,128)(2,1)S(1)}, u32[]{:S(2)}, u32[]{:S(2)}) collective-permute-start(bf16[8,2560]{1,0:T(8,128)(2,1)S(1)} %get-tuple-element.26._), channel_id=1, source_target_pairs={{0,4},{4,8},{8,12},{1,5},{5,9},{9,13},{2,6},{6,10},{10,14},{3,7},{... | collective-permute-start | bytes 122888 | tf_op jit(solution)/shard_map/ppermute | solution.py:328
  5.2 0.0 collective-permute-done.3.rows.refs_0_
  5.3 0.7 %collective-permute-start.6 = (bf16[128,384]{1,0:T(8,128)(2,1)S(1)}, bf16[128,384]{1,0:T(8,128)(2,1)S(1)}, u32[]{:S(2)}, u32[]{:S(2)}) collective-permute-start(bf16[128,384]{1,0:T(8,128)(2,1)S(1)} %add_convert_fusion.7._), channel_id=1, source_target_pairs={{4,8},{5,9},{6,10},{7,11},{20,24},{21,25},{22,26},{23,27}} | collective-permute-start | bytes 294920 | tf_op jit(solution)/shard_map/ppermute | solution.py:328
  6.0 0.0 collective-permute-done.2.refs_1_
  6.1 0.1 add_convert_fusion.1
  6.1 0.7 %collective-permute-start.5 = (bf16[128,640]{1,0:T(8,128)(2,1)S(1)}, bf16[128,640]{1,0:T(8,128)(2,1)S(1)}, u32[]{:S(2)}, u32[]{:S(2)}) collective-permute-start(bf16[128,640]{1,0:T(8,128)(2,1)S(1)} %add_convert_fusion.1), channel_id=1, source_target_pairs={{4,8},{5,9},{6,10},{7,11},{20,24},{21,25},{22,26},{23,27}} | collective-permute-start | bytes 491528 | tf_op jit(solution)/shard_map/ppermute | solution.py:328
  6.8 0.0 collective-permute-done.1.refs_0_
  6.8 0.7 %collective-permute-start.4 = (bf16[128,512]{1,0:T(8,128)(2,1)S(1)}, bf16[128,512]{1,0:T(8,128)(2,1)S(1)}, u32[]{:S(2)}, u32[]{:S(2)}) collective-permute-start(bf16[128,512]{1,0:T(8,128)(2,1)S(1)} %add_convert_fusion.5), channel_id=1, source_target_pairs={{4,8},{5,9},{6,10},{7,11},{20,24},{21,25},{22,26},{23,27}} | collective-permute-start | bytes 393224 | tf_op jit(solution)/shard_map/ppermute | solution.py:328
  7.5 0.0 collective-permute-done.7.refs_1_
  7.6 0.7 %collective-permute-start.9 = (bf16[128,512]{1,0:T(8,128)(2,1)S(1)}, bf16[128,512]{1,0:T(8,128)(2,1)S(1)}, u32[]{:S(2)}, u32[]{:S(2)}) collective-permute-start(bf16[128,512]{1,0:T(8,128)(2,1)S(1)} %add_convert_fusion.4._), channel_id=1, source_target_pairs={{4,8},{5,9},{6,10},{7,11},{20,24},{21,25},{22,26},{23,27}} | collective-permute-start | bytes 393224 | tf_op jit(solution)/shard_map/ppermute | solution.py:328
  8.3 1.5 %collective-permute-done.got.rows = bf16[8,2560]{1,0:T(8,128)(2,1)S(1)} collective-permute-done((bf16[8,2560]{1,0:T(8,128)(2,1)S(1)}, bf16[8,2560]{1,0:T(8,128)(2,1)S(1)}, u32[]{:S(2)}, u32[]{:S(2)}) %collective-permute-start) | collective-permute-done | bytes 40992 | tf_op jit(solution)/shard_map/ppermute | solution.py:328
  9.8 0.4 %later_states.12 = f32[128,384]{1,0:T(8,128)S(1)} custom-call(s32[1]{0:T(128)} %bitcast.8.active, bf16[8,2560]{1,0:T(8,128)(2,1)S(1)} %collective-permute-done.got.rows, bf16[128,512]{1,0:T(8,128)(2,1)S(1)} %add_convert_fusion.4._, bf16[128,2048]{1,0:T(8,128)(2,1)S(1)} %copy-done, bf16[128,2,256]{2,1,0:T(2,128)(2,1)S(1)} %copy-done.1, ...), custom_call_target="tpu_custom_call" | custom-call | tf_op jit(solution)/shard_map/later_states/pallas_call | solution.py:362
  10.2 0.5 %later_states.15 = f32[128,512]{1,0:T(8,128)S(1)} custom-call(s32[1]{0:T(128)} %bitcast.8.active, bf16[8,2560]{1,0:T(8,128)(2,1)S(1)} %collective-permute-done.got.rows, bf16[128,512]{1,0:T(8,128)(2,1)S(1)} %add_convert_fusion.4._, bf16[128,2048]{1,0:T(8,128)(2,1)S(1)} %copy-done, bf16[128,2,256]{2,1,0:T(2,128)(2,1)S(1)} %copy-done.1, ...), custom_call_target="tpu_custom_call" | custom-call | tf_op jit(solution)/shard_map/later_states/pallas_call | solution.py:362
  10.6 0.4 %later_states.14 = f32[128,512]{1,0:T(8,128)S(1)} custom-call(s32[1]{0:T(128)} %bitcast.8.active, bf16[8,2560]{1,0:T(8,128)(2,1)S(1)} %collective-permute-done.got.rows, bf16[128,512]{1,0:T(8,128)(2,1)S(1)} %add_convert_fusion.4._, bf16[128,2048]{1,0:T(8,128)(2,1)S(1)} %copy-done, bf16[128,2,256]{2,1,0:T(2,128)(2,1)S(1)} %copy-done.1, ...), custom_call_target="tpu_custom_call" | custom-call | tf_op jit(solution)/shard_map/later_states/pallas_call | solution.py:362
  11.1 0.5 %later_states.13 = f32[128,640]{1,0:T(8,128)S(1)} custom-call(s32[1]{0:T(128)} %bitcast.8.active, bf16[8,2560]{1,0:T(8,128)(2,1)S(1)} %collective-permute-done.got.rows, bf16[128,512]{1,0:T(8,128)(2,1)S(1)} %add_convert_fusion.4._, bf16[128,2048]{1,0:T(8,128)(2,1)S(1)} %copy-done, bf16[128,2,256]{2,1,0:T(2,128)(2,1)S(1)} %copy-done.1, ...), custom_call_target="tpu_custom_call" | custom-call | tf_op jit(solution)/shard_map/later_states/pallas_call | solution.py:362
  11.6 0.0 collective-permute-done.6.refs_1_
  11.6 1.3 %collective-permute-start.10 = (bf16[128,384]{1,0:T(8,128)(2,1)S(1)}, bf16[128,384]{1,0:T(8,128)(2,1)S(1)}, u32[]{:S(2)}, u32[]{:S(2)}) collective-permute-start(bf16[128,384]{1,0:T(8,128)(2,1)S(1)} %add_convert_fusion.6), channel_id=1, source_target_pairs={{8,12},{9,13},{10,14},{11,15},{24,28},{25,29},{26,30},{27,31}} | collective-permute-start | bytes 294920 | tf_op jit(solution)/shard_map/ppermute | solution.py:328
  12.9 0.0 collective-permute-done.5.refs_2_
  12.9 0.1 add_convert_fusion
  13.0 0.0 copy-start.4
  13.0 1.4 %collective-permute-start.12 = (bf16[128,640]{1,0:T(8,128)(2,1)S(1)}, bf16[128,640]{1,0:T(8,128)(2,1)S(1)}, u32[]{:S(2)}, u32[]{:S(2)}) collective-permute-start(bf16[128,640]{1,0:T(8,128)(2,1)S(1)} %add_convert_fusion), channel_id=1, source_target_pairs={{8,12},{9,13},{10,14},{11,15},{24,28},{25,29},{26,30},{27,31}} | collective-permute-start | bytes 491528 | tf_op jit(solution)/shard_map/ppermute | solution.py:328
  14.4 0.0 collective-permute-done.4.refs_1_
  14.5 1.3 %collective-permute-start.8 = (bf16[128,512]{1,0:T(8,128)(2,1)S(1)}, bf16[128,512]{1,0:T(8,128)(2,1)S(1)}, u32[]{:S(2)}, u32[]{:S(2)}) collective-permute-start(bf16[128,512]{1,0:T(8,128)(2,1)S(1)} %add_convert_fusion.3), channel_id=1, source_target_pairs={{8,12},{9,13},{10,14},{11,15},{24,28},{25,29},{26,30},{27,31}} | collective-permute-start | bytes 393224 | tf_op jit(solution)/shard_map/ppermute | solution.py:328
  15.8 0.0 collective-permute-done.9.refs_2_
  15.8 3.3 %collective-permute-done.10.refs_2_ = bf16[128,384]{1,0:T(8,128)(2,1)S(1)} collective-permute-done((bf16[128,384]{1,0:T(8,128)(2,1)S(1)}, bf16[128,384]{1,0:T(8,128)(2,1)S(1)}, u32[]{:S(2)}, u32[]{:S(2)}) %collective-permute-start.10) | collective-permute-done | bytes 98336 | tf_op jit(solution)/shard_map/ppermute | solution.py:328
  19.2 0.0 copy-start.8
  19.2 1.3 %collective-permute-start.11 = (bf16[128,512]{1,0:T(8,128)(2,1)S(1)}, bf16[128,512]{1,0:T(8,128)(2,1)S(1)}, u32[]{:S(2)}, u32[]{:S(2)}) collective-permute-start(bf16[128,512]{1,0:T(8,128)(2,1)S(1)} %add_convert_fusion.2), channel_id=1, source_target_pairs={{8,12},{9,13},{10,14},{11,15},{24,28},{25,29},{26,30},{27,31}} | collective-permute-start | bytes 393224 | tf_op jit(solution)/shard_map/ppermute | solution.py:328
  20.5 2.3 %intra.1 = (f32[128,2048]{1,0:T(8,128)S(1)}, f32[128,2048]{1,0:T(8,128)S(1)}, bf16[128,256]{1,0:T(8,128)(2,1)S(1)}) custom-call(bf16[128,2048]{1,0:T(8,128)(2,1)S(1)} %copy-done, bf16[8,2560]{1,0:T(8,128)(2,1)S(1)} %collective-permute-done.got.rows, bf16[128,2,256]{2,1,0:T(2,128)(2,1)S(1)} %copy-done.1, bf16[128,2048]{1,0:T(8,128)(2,1)S(1)} %copy-done.4, ...), custom_call_target="tpu_custom_call" | custom-call | flops 134217728 | bytes 3145728 | tf_op jit(solution)/shard_map/intra/pallas_call | solution.py:402
  22.8 0.2 gated.3.refs_0_
  23.0 0.0 copy-start.6
  23.0 4.9 %collective-permute-done.8.refs_2_ = bf16[128,512]{1,0:T(8,128)(2,1)S(1)} collective-permute-done((bf16[128,512]{1,0:T(8,128)(2,1)S(1)}, bf16[128,512]{1,0:T(8,128)(2,1)S(1)}, u32[]{:S(2)}, u32[]{:S(2)}) %collective-permute-start.8) | collective-permute-done | bytes 131104 | tf_op jit(solution)/shard_map/ppermute | solution.py:328
  27.9 0.2 gated.2.refs_0_
  28.1 0.0 collective-permute-done.12.refs_3_
  28.1 0.0 copy-done.6
  28.1 1.0 %outputs.2.refs_4_ = bf16[128,2048]{1,0:T(8,128)(2,1)} custom-call(bf16[128,256]{1,0:T(8,128)(2,1)S(1)} %get-tuple-element.27.c, f32[128,2048]{1,0:T(8,128)S(1)} %get-tuple-element.28.y_part, f32[128,2048]{1,0:T(8,128)S(1)} %get-tuple-element.29.lead, f32[1,2048]{1,0:T(1,128)S(1)} %bitcast.12, f32[128,384]{1,0:T(8,128)S(1)} %gated.3.refs_0_, ...), custom_call_target="tpu_custom_call" | custom-call | tf_op jit(solution)/shard_map/outputs/pallas_call | solution.py:446
  29.1 0.2 collective-permute-done.11.refs_3_
  29.3 1.0 %outputs.3 = bf16[128,2048]{1,0:T(8,128)(2,1)} custom-call(bf16[128,256]{1,0:T(8,128)(2,1)S(1)} %get-tuple-element.27.c, f32[128,2048]{1,0:T(8,128)S(1)} %get-tuple-element.28.y_part, f32[128,2048]{1,0:T(8,128)S(1)} %get-tuple-element.29.lead, f32[1,2048]{1,0:T(1,128)S(1)} %bitcast.13, f32[128,512]{1,0:T(8,128)S(1)} %gated.2.refs_0_, ...), custom_call_target="tpu_custom_call", output_to_operand_aliasing={{}: (8, {})} | custom-call | tf_op jit(solution)/shard_map/outputs/pallas_call | solution.py:446
  (24 shorter events, 0.4 us)
Async XLA Ops:
  0.0 1.0 %copy-start = (bf16[128,2048]{1,0:T(8,128)(2,1)S(1)}, bf16[128,2048]{1,0:T(8,128)(2,1)}, u32[]{:S(2)}) copy-start(bf16[128,2048]{1,0:T(8,128)(2,1)} %x.25) | copy-start | bytes 1572868
  0.0 1.1 %copy-start.1 = (bf16[128,2,256]{2,1,0:T(2,128)(2,1)S(1)}, bf16[128,2,256]{2,1,0:T(2,128)(2,1)}, u32[]{:S(2)}) copy-start(bf16[128,2,256]{2,1,0:T(2,128)(2,1)} %bc.25) | copy-start | bytes 393220
  0.0 1.1 %copy-start.2 = (f32[4,2048]{1,0:T(4,128)S(1)}, f32[4,2048]{1,0:T(4,128)}, u32[]{:S(2)}) copy-start(f32[4,2048]{1,0:T(4,128)} %taps_x.23) | copy-start | bytes 98308
  0.0 1.1 %copy-start.3 = (f32[4,2,256]{2,1,0:T(2,128)S(1)}, f32[4,2,256]{2,1,0:T(2,128)}, u32[]{:S(2)}) copy-start(f32[4,2,256]{2,1,0:T(2,128)} %taps_bc.23) | copy-start | bytes 24580
  0.1 5.2 %collective-permute-start.3 = (bf16[160,384]{1,0:T(8,128)(2,1)S(1)}, bf16[160,384]{1,0:T(8,128)(2,1)S(1)}, u32[]{:S(2)}, u32[]{:S(2)}) collective-permute-start(bf16[160,384]{1,0:T(8,128)(2,1)S(1)} %get-tuple-element.24._), channel_id=1, source_target_pairs={{0,4},{1,5},{2,6},{3,7},{16,20},{17,21},{18,22},{19,23}} | collective-permute-start | bytes 368648 | tf_op jit(solution)/shard_map/ppermute | solution.py:328
  1.1 5.0 %collective-permute-start.2 = (bf16[128,640]{1,0:T(8,128)(2,1)S(1)}, bf16[128,640]{1,0:T(8,128)(2,1)S(1)}, u32[]{:S(2)}, u32[]{:S(2)}) collective-permute-start(bf16[128,640]{1,0:T(8,128)(2,1)S(1)} %next_states.3._), channel_id=1, source_target_pairs={{0,4},{1,5},{2,6},{3,7},{16,20},{17,21},{18,22},{19,23}} | collective-permute-start | bytes 491528 | tf_op jit(solution)/shard_map/ppermute | solution.py:328
  1.8 1.4 %copy-start.5 = (f32[128,32]{0,1:T(8,128)S(1)}, f32[128,32]{0,1:T(8,128)}, u32[]{:S(2)}) copy-start(f32[128,32]{0,1:T(8,128)} %param.12) | copy-start | bytes 49156
  1.8 1.4 %copy-start.7 = (f32[32]{0:T(128)S(1)}, f32[32]{0:T(128)}, u32[]{:S(2)}) copy-start(f32[32]{0:T(128)} %param.15) | copy-start | bytes 388
  1.8 5.0 %collective-permute-start.1 = (bf16[128,512]{1,0:T(8,128)(2,1)S(1)}, bf16[128,512]{1,0:T(8,128)(2,1)S(1)}, u32[]{:S(2)}, u32[]{:S(2)}) collective-permute-start(bf16[128,512]{1,0:T(8,128)(2,1)S(1)} %next_states.4._), channel_id=1, source_target_pairs={{0,4},{1,5},{2,6},{3,7},{16,20},{17,21},{18,22},{19,23}} | collective-permute-start | bytes 393224 | tf_op jit(solution)/shard_map/ppermute | solution.py:328
  2.5 5.0 %collective-permute-start.7 = (bf16[128,512]{1,0:T(8,128)(2,1)S(1)}, bf16[128,512]{1,0:T(8,128)(2,1)S(1)}, u32[]{:S(2)}, u32[]{:S(2)}) collective-permute-start(bf16[128,512]{1,0:T(8,128)(2,1)S(1)} %next_states.5._), channel_id=1, source_target_pairs={{0,4},{1,5},{2,6},{3,7},{16,20},{17,21},{18,22},{19,23}} | collective-permute-start | bytes 393224 | tf_op jit(solution)/shard_map/ppermute | solution.py:328
  3.9 5.9 %collective-permute-start = (bf16[8,2560]{1,0:T(8,128)(2,1)S(1)}, bf16[8,2560]{1,0:T(8,128)(2,1)S(1)}, u32[]{:S(2)}, u32[]{:S(2)}) collective-permute-start(bf16[8,2560]{1,0:T(8,128)(2,1)S(1)} %get-tuple-element.26._), channel_id=1, source_target_pairs={{0,4},{4,8},{8,12},{1,5},{5,9},{9,13},{2,6},{6,10},{10,14},{3,7},{... | collective-permute-start | bytes 122888 | tf_op jit(solution)/shard_map/ppermute | solution.py:328
  5.3 6.3 %collective-permute-start.6 = (bf16[128,384]{1,0:T(8,128)(2,1)S(1)}, bf16[128,384]{1,0:T(8,128)(2,1)S(1)}, u32[]{:S(2)}, u32[]{:S(2)}) collective-permute-start(bf16[128,384]{1,0:T(8,128)(2,1)S(1)} %add_convert_fusion.7._), channel_id=1, source_target_pairs={{4,8},{5,9},{6,10},{7,11},{20,24},{21,25},{22,26},{23,27}} | collective-permute-start | bytes 294920 | tf_op jit(solution)/shard_map/ppermute | solution.py:328
  6.1 6.8 %collective-permute-start.5 = (bf16[128,640]{1,0:T(8,128)(2,1)S(1)}, bf16[128,640]{1,0:T(8,128)(2,1)S(1)}, u32[]{:S(2)}, u32[]{:S(2)}) collective-permute-start(bf16[128,640]{1,0:T(8,128)(2,1)S(1)} %add_convert_fusion.1), channel_id=1, source_target_pairs={{4,8},{5,9},{6,10},{7,11},{20,24},{21,25},{22,26},{23,27}} | collective-permute-start | bytes 491528 | tf_op jit(solution)/shard_map/ppermute | solution.py:328
  6.8 7.6 %collective-permute-start.4 = (bf16[128,512]{1,0:T(8,128)(2,1)S(1)}, bf16[128,512]{1,0:T(8,128)(2,1)S(1)}, u32[]{:S(2)}, u32[]{:S(2)}) collective-permute-start(bf16[128,512]{1,0:T(8,128)(2,1)S(1)} %add_convert_fusion.5), channel_id=1, source_target_pairs={{4,8},{5,9},{6,10},{7,11},{20,24},{21,25},{22,26},{23,27}} | collective-permute-start | bytes 393224 | tf_op jit(solution)/shard_map/ppermute | solution.py:328
  7.6 8.2 %collective-permute-start.9 = (bf16[128,512]{1,0:T(8,128)(2,1)S(1)}, bf16[128,512]{1,0:T(8,128)(2,1)S(1)}, u32[]{:S(2)}, u32[]{:S(2)}) collective-permute-start(bf16[128,512]{1,0:T(8,128)(2,1)S(1)} %add_convert_fusion.4._), channel_id=1, source_target_pairs={{4,8},{5,9},{6,10},{7,11},{20,24},{21,25},{22,26},{23,27}} | collective-permute-start | bytes 393224 | tf_op jit(solution)/shard_map/ppermute | solution.py:328
  11.6 7.5 %collective-permute-start.10 = (bf16[128,384]{1,0:T(8,128)(2,1)S(1)}, bf16[128,384]{1,0:T(8,128)(2,1)S(1)}, u32[]{:S(2)}, u32[]{:S(2)}) collective-permute-start(bf16[128,384]{1,0:T(8,128)(2,1)S(1)} %add_convert_fusion.6), channel_id=1, source_target_pairs={{8,12},{9,13},{10,14},{11,15},{24,28},{25,29},{26,30},{27,31}} | collective-permute-start | bytes 294920 | tf_op jit(solution)/shard_map/ppermute | solution.py:328
  13.0 7.5 %copy-start.4 = (bf16[128,2048]{1,0:T(8,128)(2,1)S(1)}, bf16[128,2048]{1,0:T(8,128)(2,1)}, u32[]{:S(2)}) copy-start(bf16[128,2048]{1,0:T(8,128)(2,1)} %z.1) | copy-start | bytes 1572868
  13.0 15.1 %collective-permute-start.12 = (bf16[128,640]{1,0:T(8,128)(2,1)S(1)}, bf16[128,640]{1,0:T(8,128)(2,1)S(1)}, u32[]{:S(2)}, u32[]{:S(2)}) collective-permute-start(bf16[128,640]{1,0:T(8,128)(2,1)S(1)} %add_convert_fusion), channel_id=1, source_target_pairs={{8,12},{9,13},{10,14},{11,15},{24,28},{25,29},{26,30},{27,31}} | collective-permute-start | bytes 491528 | tf_op jit(solution)/shard_map/ppermute | solution.py:328
  14.5 13.4 %collective-permute-start.8 = (bf16[128,512]{1,0:T(8,128)(2,1)S(1)}, bf16[128,512]{1,0:T(8,128)(2,1)S(1)}, u32[]{:S(2)}, u32[]{:S(2)}) collective-permute-start(bf16[128,512]{1,0:T(8,128)(2,1)S(1)} %add_convert_fusion.3), channel_id=1, source_target_pairs={{8,12},{9,13},{10,14},{11,15},{24,28},{25,29},{26,30},{27,31}} | collective-permute-start | bytes 393224 | tf_op jit(solution)/shard_map/ppermute | solution.py:328
  19.2 1.3 %copy-start.8 = (f32[32]{0:T(128)S(1)}, f32[32]{0:T(128)}, u32[]{:S(2)}) copy-start(f32[32]{0:T(128)} %param.16) | copy-start | bytes 388
  19.2 10.1 %collective-permute-start.11 = (bf16[128,512]{1,0:T(8,128)(2,1)S(1)}, bf16[128,512]{1,0:T(8,128)(2,1)S(1)}, u32[]{:S(2)}, u32[]{:S(2)}) collective-permute-start(bf16[128,512]{1,0:T(8,128)(2,1)S(1)} %add_convert_fusion.2), channel_id=1, source_target_pairs={{8,12},{9,13},{10,14},{11,15},{24,28},{25,29},{26,30},{27,31}} | collective-permute-start | bytes 393224 | tf_op jit(solution)/shard_map/ppermute | solution.py:328
  23.0 5.1 %copy-start.6 = (f32[2048]{0:T(1024)S(1)}, f32[2048]{0:T(1024)}, u32[]{:S(2)}) copy-start(f32[2048]{0:T(1024)} %param.17) | copy-start | bytes 24580

commit v7 on v6

--- a/solution.py
+++ b/solution.py
@@ -197,9 +197,11 @@
 
 
 def intra_kernel(
-    head_dim, x, got, bc, z, taps_x, taps_bc, dt_raw, a_log, d_skip, y_part, lead, c_act, wide
+    head_dim, x, got_soon, got_late, bc, z, taps_x, taps_bc, dt_raw, a_log, d_skip,
+    y_part, lead, c_act, wide
 ):
     dt, cum = rates(dt_raw[...], a_log[...], 0)
+    got = got_soon[...].astype(F32) + got_late[...].astype(F32)
     tokens, width = x.shape
     groups, both = bc.shape[1:]
     state_dim = both // 2
@@ -214,7 +216,7 @@
     for g in range(groups):
         at = width + g * both
         bc_act = conv_act(
-            bc[...].astype(F32)[:, g], got[:, at : at + both].astype(F32), taps_bc[...][:, g]
+            bc[...].astype(F32)[:, g], got[:, at : at + both], taps_bc[...][:, g]
         )
         b, c = bc_act[:, :state_dim], bc_act[:, state_dim:]
         c_act[:, g * state_dim : (g + 1) * state_dim] = c
@@ -224,7 +226,7 @@
         for first in range(0, heads, 2):
             here = first * head_dim
             cut = slice(g * cols + here, g * cols + here + pair)
-            act = conv_act(x[:, cut].astype(F32), got[:, cut].astype(F32), taps_x[:, cut])
+            act = conv_act(x[:, cut].astype(F32), got[:, cut], taps_x[:, cut])
             lane = lax.broadcasted_iota(jnp.int32, act.shape, 1)
             full = act.astype(F32)
             blocks = jnp.concatenate(
@@ -374,9 +376,10 @@
         for cut in cuts[1:]:
             sent.append(next_states(sent[-1], scale, *cut))
         last, scale, *decays = prepared(sent[-1])
-        got = shifted(last, along)
+        soon = along[1 : max(devices - 2, 1)]
+        got = shifted(last, soon) if soon else jnp.zeros_like(last)
         arrived = [[shifted(v, along[:1])] for v in sent]
-        rows, token = arrived[0][0], last
+        rows, token, late = arrived[0][0], last, None
         for hop in range(1, devices - 1):
             condition = place == 1 if hop == 1 else place >= 2
             after = token
@@ -384,13 +387,19 @@
                 if hop <= 2:
                     made = later_states(condition, rows, after, scale, *cut)
                     states = [made] if i == 0 else states + [made]
-                early = arrived[0][-1] if hop > 1 and i == len(cuts) - 1 else token
-                before, _, _ = lax.optimization_barrier((seen[-1], token, early))
+                early = (arrived[0][-1], late) if hop > 1 and i == len(cuts) - 1 else ()
+                before, *_ = lax.optimization_barrier((seen[-1], token) + early)
                 joined = decays[i] * before[:state_dim].astype(F32) + states[i]
                 token = joined.astype(BF16)
+                if hop == devices - 2 and i == 0:
+                    last, _ = lax.optimization_barrier((last, token))
+                    late = shifted(last, [pair for pair in along if pair not in soon])
                 after = token if hop == 1 and i == 0 else after
                 seen.append(shifted(token, along[hop : hop + 1]))
             rows = got
+        if late is None:
+            late = shifted(last, along)
+        got = [got, late]
     else:
         last, scale, *decays = prepared(a_row)
         got = shifted(last, along)
@@ -398,6 +407,7 @@
         for decay, cut in zip(decays, cuts):
             state = later_states(place >= 0, got, a_row, scale, *cut)
             arrived.append([doubling(state, decay, devices)])
+        got = [got, jnp.zeros_like(got)]
 
     y_part, lead, c_act = pl.pallas_call(
         functools.partial(intra_kernel, head_dim),
@@ -414,7 +424,7 @@
             transcendentals=tokens * tokens * heads,
         ),
         name="intra",
-    )(x_in, got, bc_in, z_in, conv_x, conv_bc, dt_t, a_row, d_row)
+    )(x_in, *got, bc_in, z_in, conv_x, conv_bc, dt_t, a_row, d_row)
 
     out = None
     for g in range(groups):

time: 30.7 us -> 31.4 us (1.023)
  the two profiles are of different devices: /device:TPU:30 before, /device:TPU:0 now
where the time goes in v7:
time: 31.4 us; the launch traced here: 31 us
  starting transfers between devices  18.2 us (58%)
  Pallas kernels  8.85 us (28%)
  waiting for transfers between devices  2.65 us (8%)
  local copies, waits for them, and re-layouts  0.52 us (2%)
  between operations  0.43 us (1%)
  other arithmetic  0.37 us (1%)
    ppermute x14, starting transfers between devices, shifted(): return lax.ppermute(value, 'seq', route)  18.2 us
    ppermute x14, waiting for transfers between devices, shifted(): return lax.ppermute(value, 'seq', route)  2.65 us
    pallas_call x1, Pallas kernels, shards(): pl.pallas_call(functools.partial(intra_kernel, head_dim), out_shape=(jax....  2.27 us
    pallas_call x2, Pallas kernels, shards(): pl.pallas_call(functools.partial(output_kernel, len(ready), len(arrived[0...  2.03 us
    pallas_call x1, Pallas kernels, first_states(): pl.pallas_call(functools.partial(first_kernel, group, low, high), out_sha...  1.99 us
    pallas_call x3, Pallas kernels, next_states(): pl.pallas_call(functools.partial(next_kernel, group, low, high), out_shap...  1.39 us
    pallas_call x1, Pallas kernels, prepared(): pl.pallas_call(functools.partial(prepare_kernel, cuts), out_shape=[jax.Sh...  0.72 us
  transfers between devices with their start and end apart: 14, of which 2 were waited for; matrix products, arithmetic and copies ran while one was open for 1% of the time, Pallas kernels for 19%

profile of v7, /device:TPU:0, one launch (start us, length us, event | category | flops | bytes accessed | tf_op | source)
XLA Modules:
  0.0 31.0 jit_solution(1516822257757850833)
XLA Ops:
  0.0 2.0 %first_states.1 = (bf16[160,384]{1,0:T(8,128)(2,1)S(1)}, f32[128,2048]{1,0:T(8,128)S(1)}) custom-call(s32[1]{0:T(128)} %bitcast.active, bf16[128,2048]{1,0:T(8,128)(2,1)} %x.25, bf16[128,2,256]{2,1,0:T(2,128)(2,1)} %bc.25, f32[4,2048]{1,0:T(4,128)} %taps_x.23, f32[4,2,256]{2,1,0:T(2,128)} %taps_bc.23, f32[32,128]{1,0:T(8,128)} %bitcast.9, f32[1,32]{1,0:T(1,128)} %bitcast.18), custom_call_target="tpu_custom_call" | custom-call | tf_op jit(solution)/shard_map/first_states/pallas_call | solution.py:335
  2.0 3.1 %collective-permute-start.1 = (bf16[160,384]{1,0:T(8,128)(2,1)S(1)}, bf16[160,384]{1,0:T(8,128)(2,1)S(1)}, u32[]{:S(2)}, u32[]{:S(2)}) collective-permute-start(bf16[160,384]{1,0:T(8,128)(2,1)S(1)} %get-tuple-element.25._), channel_id=1, source_target_pairs={{0,4},{1,5},{2,6},{3,7},{16,20},{17,21},{18,22},{19,23}} | collective-permute-start | bytes 368648 | tf_op jit(solution)/shard_map/ppermute | solution.py:330
  5.2 0.0 copy-done
  5.2 0.0 copy-done.1
  5.2 0.5 %next_states.3._ = bf16[128,640]{1,0:T(8,128)(2,1)S(1)} custom-call(s32[1]{0:T(128)} %bitcast.active, bf16[160,384]{1,0:T(8,128)(2,1)S(1)} %get-tuple-element.25._, bf16[128,2048]{1,0:T(8,128)(2,1)S(1)} %copy-done, bf16[128,2,256]{2,1,0:T(2,128)(2,1)S(1)} %copy-done.1, f32[4,2048]{1,0:T(4,128)S(1)} %copy-done.2, f32[4,2,256]{2,1,0:T(2,128)S(1)} %copy-done.3, ...), custom_call_target="tpu_custom_call" | custom-call | tf_op jit(solution)/shard_map/next_states/pallas_call | solution.py:345
  5.7 1.3 %collective-permute-start.5 = (bf16[128,640]{1,0:T(8,128)(2,1)S(1)}, bf16[128,640]{1,0:T(8,128)(2,1)S(1)}, u32[]{:S(2)}, u32[]{:S(2)}) collective-permute-start(bf16[128,640]{1,0:T(8,128)(2,1)S(1)} %next_states.3._), channel_id=1, source_target_pairs={{0,4},{1,5},{2,6},{3,7},{16,20},{17,21},{18,22},{19,23}} | collective-permute-start | bytes 491528 | tf_op jit(solution)/shard_map/ppermute | solution.py:330
  7.0 0.4 %next_states.4._ = bf16[128,512]{1,0:T(8,128)(2,1)S(1)} custom-call(s32[1]{0:T(128)} %bitcast.active, bf16[128,640]{1,0:T(8,128)(2,1)S(1)} %next_states.3._, bf16[128,2048]{1,0:T(8,128)(2,1)S(1)} %copy-done, bf16[128,2,256]{2,1,0:T(2,128)(2,1)S(1)} %copy-done.1, f32[4,2048]{1,0:T(4,128)S(1)} %copy-done.2, f32[4,2,256]{2,1,0:T(2,128)S(1)} %copy-done.3, ...), custom_call_target="tpu_custom_call" | custom-call | tf_op jit(solution)/shard_map/next_states/pallas_call | solution.py:345
  7.4 0.0 copy-start.5
  7.5 0.0 copy-start.7
  7.5 1.3 %collective-permute-start.4 = (bf16[128,512]{1,0:T(8,128)(2,1)S(1)}, bf16[128,512]{1,0:T(8,128)(2,1)S(1)}, u32[]{:S(2)}, u32[]{:S(2)}) collective-permute-start(bf16[128,512]{1,0:T(8,128)(2,1)S(1)} %next_states.4._), channel_id=1, source_target_pairs={{0,4},{1,5},{2,6},{3,7},{16,20},{17,21},{18,22},{19,23}} | collective-permute-start | bytes 393224 | tf_op jit(solution)/shard_map/ppermute | solution.py:330
  8.8 0.5 %next_states.5._ = bf16[128,512]{1,0:T(8,128)(2,1)S(1)} custom-call(s32[1]{0:T(128)} %bitcast.active, bf16[128,512]{1,0:T(8,128)(2,1)S(1)} %next_states.4._, bf16[128,2048]{1,0:T(8,128)(2,1)S(1)} %copy-done, bf16[128,2,256]{2,1,0:T(2,128)(2,1)S(1)} %copy-done.1, f32[4,2048]{1,0:T(4,128)S(1)} %copy-done.2, f32[4,2,256]{2,1,0:T(2,128)S(1)} %copy-done.3, ...), custom_call_target="tpu_custom_call" | custom-call | tf_op jit(solution)/shard_map/next_states/pallas_call | solution.py:345
  9.2 1.3 %collective-permute-start.3 = (bf16[128,512]{1,0:T(8,128)(2,1)S(1)}, bf16[128,512]{1,0:T(8,128)(2,1)S(1)}, u32[]{:S(2)}, u32[]{:S(2)}) collective-permute-start(bf16[128,512]{1,0:T(8,128)(2,1)S(1)} %next_states.5._), channel_id=1, source_target_pairs={{0,4},{1,5},{2,6},{3,7},{16,20},{17,21},{18,22},{19,23}} | collective-permute-start | bytes 393224 | tf_op jit(solution)/shard_map/ppermute | solution.py:330
  10.6 0.7 %prepared.1 = (bf16[8,2560]{1,0:T(8,128)(2,1)S(1)}, f32[128,2048]{1,0:T(8,128)S(1)}, f32[1,384]{1,0:T(1,128)S(1)}, f32[1,640]{1,0:T(1,128)S(1)}, f32[1,512]{1,0:T(1,128)S(1)}, /*index=5*/f32[1,512]{1,0:T(1,128)S(1)}) custom-call(bf16[128,512]{1,0:T(8,128)(2,1)S(1)} %next_states.5._, bf16[128,2048]{1,0:T(8,128)(2,1)S(1)} %copy-done, ...), custom_call_target="tpu_custom_call" | custom-call | tf_op jit(solution)/shard_map/prepared/pallas_call | solution.py:354
  11.3 0.7 %collective-permute-start = (bf16[8,2560]{1,0:T(8,128)(2,1)S(1)}, bf16[8,2560]{1,0:T(8,128)(2,1)S(1)}, u32[]{:S(2)}, u32[]{:S(2)}) collective-permute-start(bf16[8,2560]{1,0:T(8,128)(2,1)S(1)} %get-tuple-element.38._), channel_id=1, source_target_pairs={{4,8},{5,9},{6,10},{7,11},{20,24},{21,25},{22,26},{23,27}} | collective-permute-start | bytes 122888 | tf_op jit(solution)/shard_map/ppermute | solution.py:330
  12.0 0.0 collective-permute-done.1.rows.refs_0_
  12.1 0.7 %collective-permute-start.2 = (bf16[128,384]{1,0:T(8,128)(2,1)S(1)}, bf16[128,384]{1,0:T(8,128)(2,1)S(1)}, u32[]{:S(2)}, u32[]{:S(2)}) collective-permute-start(bf16[128,384]{1,0:T(8,128)(2,1)S(1)} %add_convert_fusion.7._), channel_id=1, source_target_pairs={{4,8},{5,9},{6,10},{7,11},{20,24},{21,25},{22,26},{23,27}} | collective-permute-start | bytes 294920 | tf_op jit(solution)/shard_map/ppermute | solution.py:330
  12.8 0.0 collective-permute-done.5.refs_1_
  12.8 0.1 add_convert_fusion.1
  12.9 0.7 %collective-permute-start.8 = (bf16[128,640]{1,0:T(8,128)(2,1)S(1)}, bf16[128,640]{1,0:T(8,128)(2,1)S(1)}, u32[]{:S(2)}, u32[]{:S(2)}) collective-permute-start(bf16[128,640]{1,0:T(8,128)(2,1)S(1)} %add_convert_fusion.1), channel_id=1, source_target_pairs={{4,8},{5,9},{6,10},{7,11},{20,24},{21,25},{22,26},{23,27}} | collective-permute-start | bytes 491528 | tf_op jit(solution)/shard_map/ppermute | solution.py:330
  13.5 1.3 %collective-permute-done.4.refs_0_ = bf16[128,512]{1,0:T(8,128)(2,1)S(1)} collective-permute-done((bf16[128,512]{1,0:T(8,128)(2,1)S(1)}, bf16[128,512]{1,0:T(8,128)(2,1)S(1)}, u32[]{:S(2)}, u32[]{:S(2)}) %collective-permute-start.4) | collective-permute-done | bytes 131104 | tf_op jit(solution)/shard_map/ppermute | solution.py:330
  14.9 0.7 %collective-permute-start.7 = (bf16[128,512]{1,0:T(8,128)(2,1)S(1)}, bf16[128,512]{1,0:T(8,128)(2,1)S(1)}, u32[]{:S(2)}, u32[]{:S(2)}) collective-permute-start(bf16[128,512]{1,0:T(8,128)(2,1)S(1)} %add_convert_fusion.5), channel_id=1, source_target_pairs={{4,8},{5,9},{6,10},{7,11},{20,24},{21,25},{22,26},{23,27}} | collective-permute-start | bytes 393224 | tf_op jit(solution)/shard_map/ppermute | solution.py:330
  15.6 1.2 %collective-permute-done.3.refs_1_ = bf16[128,512]{1,0:T(8,128)(2,1)S(1)} collective-permute-done((bf16[128,512]{1,0:T(8,128)(2,1)S(1)}, bf16[128,512]{1,0:T(8,128)(2,1)S(1)}, u32[]{:S(2)}, u32[]{:S(2)}) %collective-permute-start.3) | collective-permute-done | bytes 131104 | tf_op jit(solution)/shard_map/ppermute | solution.py:330
  16.9 0.7 %collective-permute-start.10 = (bf16[128,512]{1,0:T(8,128)(2,1)S(1)}, bf16[128,512]{1,0:T(8,128)(2,1)S(1)}, u32[]{:S(2)}, u32[]{:S(2)}) collective-permute-start(bf16[128,512]{1,0:T(8,128)(2,1)S(1)} %add_convert_fusion.4._), channel_id=1, source_target_pairs={{4,8},{5,9},{6,10},{7,11},{20,24},{21,25},{22,26},{23,27}} | collective-permute-start | bytes 393224 | tf_op jit(solution)/shard_map/ppermute | solution.py:330
  17.6 0.0 collective-permute-done.rows.got_soon
  17.7 0.0 collective-permute-done.2.refs_1_
  17.7 0.7 %collective-permute-start.11 = (bf16[128,384]{1,0:T(8,128)(2,1)S(1)}, bf16[128,384]{1,0:T(8,128)(2,1)S(1)}, u32[]{:S(2)}, u32[]{:S(2)}) collective-permute-start(bf16[128,384]{1,0:T(8,128)(2,1)S(1)} %add_convert_fusion.6), channel_id=1, source_target_pairs={{8,12},{9,13},{10,14},{11,15},{24,28},{25,29},{26,30},{27,31}} | collective-permute-start | bytes 294920 | tf_op jit(solution)/shard_map/ppermute | solution.py:330
  18.4 5.0 %collective-permute-start.6 = (bf16[8,2560]{1,0:T(8,128)(2,1)S(1)}, bf16[8,2560]{1,0:T(8,128)(2,1)S(1)}, u32[]{:S(2)}, u32[]{:S(2)}) collective-permute-start(bf16[8,2560]{1,0:T(8,128)(2,1)S(1)} %get-tuple-element.38._), channel_id=1, source_target_pairs={{0,4},{8,12},{1,5},{9,13},{2,6},{10,14},{3,7},{11,15},{16,20},{24,... | collective-permute-start | bytes 122888 | tf_op jit(solution)/shard_map/ppermute | solution.py:330
  23.4 0.0 collective-permute-done.8.refs_2_
  23.4 0.1 add_convert_fusion
  23.5 0.0 copy-start.4
  23.5 0.8 %collective-permute-start.13 = (bf16[128,640]{1,0:T(8,128)(2,1)S(1)}, bf16[128,640]{1,0:T(8,128)(2,1)S(1)}, u32[]{:S(2)}, u32[]{:S(2)}) collective-permute-start(bf16[128,640]{1,0:T(8,128)(2,1)S(1)} %add_convert_fusion), channel_id=1, source_target_pairs={{8,12},{9,13},{10,14},{11,15},{24,28},{25,29},{26,30},{27,31}} | collective-permute-start | bytes 491528 | tf_op jit(solution)/shard_map/ppermute | solution.py:330
  24.3 0.0 collective-permute-done.7.refs_1_
  24.3 0.7 %collective-permute-start.9 = (bf16[128,512]{1,0:T(8,128)(2,1)S(1)}, bf16[128,512]{1,0:T(8,128)(2,1)S(1)}, u32[]{:S(2)}, u32[]{:S(2)}) collective-permute-start(bf16[128,512]{1,0:T(8,128)(2,1)S(1)} %add_convert_fusion.3), channel_id=1, source_target_pairs={{8,12},{9,13},{10,14},{11,15},{24,28},{25,29},{26,30},{27,31}} | collective-permute-start | bytes 393224 | tf_op jit(solution)/shard_map/ppermute | solution.py:330
  25.0 0.0 collective-permute-done.6.got_late
  25.1 0.0 collective-permute-done.10.refs_2_
  25.1 0.0 collective-permute-done.11.refs_2_
  25.1 0.0 copy-start.8
  25.1 0.7 %collective-permute-start.12 = (bf16[128,512]{1,0:T(8,128)(2,1)S(1)}, bf16[128,512]{1,0:T(8,128)(2,1)S(1)}, u32[]{:S(2)}, u32[]{:S(2)}) collective-permute-start(bf16[128,512]{1,0:T(8,128)(2,1)S(1)} %add_convert_fusion.2), channel_id=1, source_target_pairs={{8,12},{9,13},{10,14},{11,15},{24,28},{25,29},{26,30},{27,31}} | collective-permute-start | bytes 393224 | tf_op jit(solution)/shard_map/ppermute | solution.py:330
  25.8 2.3 %intra.1 = (f32[128,2048]{1,0:T(8,128)S(1)}, f32[128,2048]{1,0:T(8,128)S(1)}, bf16[128,256]{1,0:T(8,128)(2,1)S(1)}) custom-call(bf16[128,2048]{1,0:T(8,128)(2,1)S(1)} %copy-done, bf16[8,2560]{1,0:T(8,128)(2,1)S(1)} %collective-permute-done.rows.got_soon, bf16[8,2560]{1,0:T(8,128)(2,1)S(1)} %collective-permute-done.6.got_late, ...), custom_call_target="tpu_custom_call" | custom-call | flops 134217728 | bytes 3145728 | tf_op jit(solution)/shard_map/intra/pallas_call | solution.py:412
  28.1 0.2 gated.3.refs_0_
  28.3 0.0 copy-start.6
  28.3 0.0 collective-permute-done.9.refs_2_
  28.3 0.2 gated.2.refs_0_
  28.5 0.0 collective-permute-done.13.refs_3_
  28.5 0.5 %copy-done.6 = f32[2048]{0:T(1024)S(1)} copy-done((f32[2048]{0:T(1024)S(1)}, f32[2048]{0:T(1024)}, u32[]{:S(2)}) %copy-start.6) | copy-done | bytes 8216
  29.0 1.0 %outputs.2.refs_4_ = bf16[128,2048]{1,0:T(8,128)(2,1)} custom-call(bf16[128,256]{1,0:T(8,128)(2,1)S(1)} %get-tuple-element.39.c, f32[128,2048]{1,0:T(8,128)S(1)} %get-tuple-element.40.y_part, f32[128,2048]{1,0:T(8,128)S(1)} %get-tuple-element.41.lead, f32[1,2048]{1,0:T(1,128)S(1)} %bitcast.12, f32[128,384]{1,0:T(8,128)S(1)} %gated.3.refs_0_, ...), custom_call_target="tpu_custom_call" | custom-call | tf_op jit(solution)/shard_map/outputs/pallas_call | solution.py:456
  30.0 0.0 collective-permute-done.12.refs_3_
  30.0 1.0 %outputs.3 = bf16[128,2048]{1,0:T(8,128)(2,1)} custom-call(bf16[128,256]{1,0:T(8,128)(2,1)S(1)} %get-tuple-element.39.c, f32[128,2048]{1,0:T(8,128)S(1)} %get-tuple-element.40.y_part, f32[128,2048]{1,0:T(8,128)S(1)} %get-tuple-element.41.lead, f32[1,2048]{1,0:T(1,128)S(1)} %bitcast.13, f32[128,512]{1,0:T(8,128)S(1)} %gated.2.refs_0_, ...), custom_call_target="tpu_custom_call", output_to_operand_aliasing={{}: (8, {})} | custom-call | tf_op jit(solution)/shard_map/outputs/pallas_call | solution.py:456
  (26 shorter events, 0.4 us)
Async XLA Ops:
  0.0 5.2 %copy-start = (bf16[128,2048]{1,0:T(8,128)(2,1)S(1)}, bf16[128,2048]{1,0:T(8,128)(2,1)}, u32[]{:S(2)}) copy-start(bf16[128,2048]{1,0:T(8,128)(2,1)} %x.25) | copy-start | bytes 1572868
  0.0 5.2 %copy-start.1 = (bf16[128,2,256]{2,1,0:T(2,128)(2,1)S(1)}, bf16[128,2,256]{2,1,0:T(2,128)(2,1)}, u32[]{:S(2)}) copy-start(bf16[128,2,256]{2,1,0:T(2,128)(2,1)} %bc.25) | copy-start | bytes 393220
  0.0 5.2 %copy-start.2 = (f32[4,2048]{1,0:T(4,128)S(1)}, f32[4,2048]{1,0:T(4,128)}, u32[]{:S(2)}) copy-start(f32[4,2048]{1,0:T(4,128)} %taps_x.23) | copy-start | bytes 98308
  0.0 5.2 %copy-start.3 = (f32[4,2,256]{2,1,0:T(2,128)S(1)}, f32[4,2,256]{2,1,0:T(2,128)}, u32[]{:S(2)}) copy-start(f32[4,2,256]{2,1,0:T(2,128)} %taps_bc.23) | copy-start | bytes 24580
  2.0 10.0 %collective-permute-start.1 = (bf16[160,384]{1,0:T(8,128)(2,1)S(1)}, bf16[160,384]{1,0:T(8,128)(2,1)S(1)}, u32[]{:S(2)}, u32[]{:S(2)}) collective-permute-start(bf16[160,384]{1,0:T(8,128)(2,1)S(1)} %get-tuple-element.25._), channel_id=1, source_target_pairs={{0,4},{1,5},{2,6},{3,7},{16,20},{17,21},{18,22},{19,23}} | collective-permute-start | bytes 368648 | tf_op jit(solution)/shard_map/ppermute | solution.py:330
  5.7 7.1 %collective-permute-start.5 = (bf16[128,640]{1,0:T(8,128)(2,1)S(1)}, bf16[128,640]{1,0:T(8,128)(2,1)S(1)}, u32[]{:S(2)}, u32[]{:S(2)}) collective-permute-start(bf16[128,640]{1,0:T(8,128)(2,1)S(1)} %next_states.3._), channel_id=1, source_target_pairs={{0,4},{1,5},{2,6},{3,7},{16,20},{17,21},{18,22},{19,23}} | collective-permute-start | bytes 491528 | tf_op jit(solution)/shard_map/ppermute | solution.py:330
  7.4 3.1 %copy-start.5 = (f32[128,32]{0,1:T(8,128)S(1)}, f32[128,32]{0,1:T(8,128)}, u32[]{:S(2)}) copy-start(f32[128,32]{0,1:T(8,128)} %param.12) | copy-start | bytes 49156
  7.5 3.1 %copy-start.7 = (f32[32]{0:T(128)S(1)}, f32[32]{0:T(128)}, u32[]{:S(2)}) copy-start(f32[32]{0:T(128)} %param.15) | copy-start | bytes 388
  7.5 7.4 %collective-permute-start.4 = (bf16[128,512]{1,0:T(8,128)(2,1)S(1)}, bf16[128,512]{1,0:T(8,128)(2,1)S(1)}, u32[]{:S(2)}, u32[]{:S(2)}) collective-permute-start(bf16[128,512]{1,0:T(8,128)(2,1)S(1)} %next_states.4._), channel_id=1, source_target_pairs={{0,4},{1,5},{2,6},{3,7},{16,20},{17,21},{18,22},{19,23}} | collective-permute-start | bytes 393224 | tf_op jit(solution)/shard_map/ppermute | solution.py:330
  9.2 7.6 %collective-permute-start.3 = (bf16[128,512]{1,0:T(8,128)(2,1)S(1)}, bf16[128,512]{1,0:T(8,128)(2,1)S(1)}, u32[]{:S(2)}, u32[]{:S(2)}) collective-permute-start(bf16[128,512]{1,0:T(8,128)(2,1)S(1)} %next_states.5._), channel_id=1, source_target_pairs={{0,4},{1,5},{2,6},{3,7},{16,20},{17,21},{18,22},{19,23}} | collective-permute-start | bytes 393224 | tf_op jit(solution)/shard_map/ppermute | solution.py:330
  11.3 6.3 %collective-permute-start = (bf16[8,2560]{1,0:T(8,128)(2,1)S(1)}, bf16[8,2560]{1,0:T(8,128)(2,1)S(1)}, u32[]{:S(2)}, u32[]{:S(2)}) collective-permute-start(bf16[8,2560]{1,0:T(8,128)(2,1)S(1)} %get-tuple-element.38._), channel_id=1, source_target_pairs={{4,8},{5,9},{6,10},{7,11},{20,24},{21,25},{22,26},{23,27}} | collective-permute-start | bytes 122888 | tf_op jit(solution)/shard_map/ppermute | solution.py:330
  12.1 5.6 %collective-permute-start.2 = (bf16[128,384]{1,0:T(8,128)(2,1)S(1)}, bf16[128,384]{1,0:T(8,128)(2,1)S(1)}, u32[]{:S(2)}, u32[]{:S(2)}) collective-permute-start(bf16[128,384]{1,0:T(8,128)(2,1)S(1)} %add_convert_fusion.7._), channel_id=1, source_target_pairs={{4,8},{5,9},{6,10},{7,11},{20,24},{21,25},{22,26},{23,27}} | collective-permute-start | bytes 294920 | tf_op jit(solution)/shard_map/ppermute | solution.py:330
  12.9 10.6 %collective-permute-start.8 = (bf16[128,640]{1,0:T(8,128)(2,1)S(1)}, bf16[128,640]{1,0:T(8,128)(2,1)S(1)}, u32[]{:S(2)}, u32[]{:S(2)}) collective-permute-start(bf16[128,640]{1,0:T(8,128)(2,1)S(1)} %add_convert_fusion.1), channel_id=1, source_target_pairs={{4,8},{5,9},{6,10},{7,11},{20,24},{21,25},{22,26},{23,27}} | collective-permute-start | bytes 491528 | tf_op jit(solution)/shard_map/ppermute | solution.py:330
  14.9 9.4 %collective-permute-start.7 = (bf16[128,512]{1,0:T(8,128)(2,1)S(1)}, bf16[128,512]{1,0:T(8,128)(2,1)S(1)}, u32[]{:S(2)}, u32[]{:S(2)}) collective-permute-start(bf16[128,512]{1,0:T(8,128)(2,1)S(1)} %add_convert_fusion.5), channel_id=1, source_target_pairs={{4,8},{5,9},{6,10},{7,11},{20,24},{21,25},{22,26},{23,27}} | collective-permute-start | bytes 393224 | tf_op jit(solution)/shard_map/ppermute | solution.py:330
  16.9 8.2 %collective-permute-start.10 = (bf16[128,512]{1,0:T(8,128)(2,1)S(1)}, bf16[128,512]{1,0:T(8,128)(2,1)S(1)}, u32[]{:S(2)}, u32[]{:S(2)}) collective-permute-start(bf16[128,512]{1,0:T(8,128)(2,1)S(1)} %add_convert_fusion.4._), channel_id=1, source_target_pairs={{4,8},{5,9},{6,10},{7,11},{20,24},{21,25},{22,26},{23,27}} | collective-permute-start | bytes 393224 | tf_op jit(solution)/shard_map/ppermute | solution.py:330
  17.7 7.4 %collective-permute-start.11 = (bf16[128,384]{1,0:T(8,128)(2,1)S(1)}, bf16[128,384]{1,0:T(8,128)(2,1)S(1)}, u32[]{:S(2)}, u32[]{:S(2)}) collective-permute-start(bf16[128,384]{1,0:T(8,128)(2,1)S(1)} %add_convert_fusion.6), channel_id=1, source_target_pairs={{8,12},{9,13},{10,14},{11,15},{24,28},{25,29},{26,30},{27,31}} | collective-permute-start | bytes 294920 | tf_op jit(solution)/shard_map/ppermute | solution.py:330
  18.4 6.7 %collective-permute-start.6 = (bf16[8,2560]{1,0:T(8,128)(2,1)S(1)}, bf16[8,2560]{1,0:T(8,128)(2,1)S(1)}, u32[]{:S(2)}, u32[]{:S(2)}) collective-permute-start(bf16[8,2560]{1,0:T(8,128)(2,1)S(1)} %get-tuple-element.38._), channel_id=1, source_target_pairs={{0,4},{8,12},{1,5},{9,13},{2,6},{10,14},{3,7},{11,15},{16,20},{24,... | collective-permute-start | bytes 122888 | tf_op jit(solution)/shard_map/ppermute | solution.py:330
  23.5 2.3 %copy-start.4 = (bf16[128,2048]{1,0:T(8,128)(2,1)S(1)}, bf16[128,2048]{1,0:T(8,128)(2,1)}, u32[]{:S(2)}) copy-start(bf16[128,2048]{1,0:T(8,128)(2,1)} %z.1) | copy-start | bytes 1572868
  23.5 5.0 %collective-permute-start.13 = (bf16[128,640]{1,0:T(8,128)(2,1)S(1)}, bf16[128,640]{1,0:T(8,128)(2,1)S(1)}, u32[]{:S(2)}, u32[]{:S(2)}) collective-permute-start(bf16[128,640]{1,0:T(8,128)(2,1)S(1)} %add_convert_fusion), channel_id=1, source_target_pairs={{8,12},{9,13},{10,14},{11,15},{24,28},{25,29},{26,30},{27,31}} | collective-permute-start | bytes 491528 | tf_op jit(solution)/shard_map/ppermute | solution.py:330
  24.3 4.0 %collective-permute-start.9 = (bf16[128,512]{1,0:T(8,128)(2,1)S(1)}, bf16[128,512]{1,0:T(8,128)(2,1)S(1)}, u32[]{:S(2)}, u32[]{:S(2)}) collective-permute-start(bf16[128,512]{1,0:T(8,128)(2,1)S(1)} %add_convert_fusion.3), channel_id=1, source_target_pairs={{8,12},{9,13},{10,14},{11,15},{24,28},{25,29},{26,30},{27,31}} | collective-permute-start | bytes 393224 | tf_op jit(solution)/shard_map/ppermute | solution.py:330
  25.1 0.7 %copy-start.8 = (f32[32]{0:T(128)S(1)}, f32[32]{0:T(128)}, u32[]{:S(2)}) copy-start(f32[32]{0:T(128)} %param.16) | copy-start | bytes 388
  25.1 4.9 %collective-permute-start.12 = (bf16[128,512]{1,0:T(8,128)(2,1)S(1)}, bf16[128,512]{1,0:T(8,128)(2,1)S(1)}, u32[]{:S(2)}, u32[]{:S(2)}) collective-permute-start(bf16[128,512]{1,0:T(8,128)(2,1)S(1)} %add_convert_fusion.2), channel_id=1, source_target_pairs={{8,12},{9,13},{10,14},{11,15},{24,28},{25,29},{26,30},{27,31}} | collective-permute-start | bytes 393224 | tf_op jit(solution)/shard_map/ppermute | solution.py:330
  28.3 0.7 %copy-start.6 = (f32[2048]{0:T(1024)S(1)}, f32[2048]{0:T(1024)}, u32[]{:S(2)}) copy-start(f32[2048]{0:T(1024)} %param.17) | copy-start | bytes 24580

commit v8 on v6

--- a/solution.py
+++ b/solution.py
@@ -11,7 +11,7 @@
 F32 = jnp.float32
 BF16 = jnp.bfloat16
 CHAIN_MOST = 4
-FIRST_PARTS = (3, 5)
+FIRST_PARTS = (1, 1)
 OTHER_PARTS = (1, 1)
 CHUNK = 128
 RIM = 8
@@ -158,103 +158,110 @@
         head_rows(group, low, high, x, bc, taps_x, taps_bc, scale, out)
 
 
-def prepare_kernel(cuts, _, x, bc, dt_raw, a_log, pack, scale, *decays):
+def prepare_kernel(cuts, _, x, bc, dt_raw, a_log, gain, pack, gain_out, scale, *decays):
     tokens, width = x.shape
     groups, both = bc.shape[1:]
     pack[:, :width] = x[tokens - 2 * RIM :, :].astype(F32)[-RIM:].astype(BF16)
     last_bc = bc[tokens - 2 * RIM :].astype(F32)[-RIM:]
     for g in range(groups):
         pack[:, width + g * both : width + (g + 1) * both] = last_bc[:, g].astype(BF16)
+    gain_out[...] = gain[...]
     row = scales(width // dt_raw.shape[0], dt_raw, a_log, scale)
     for decay, (_, low, high) in zip(decays, cuts):
         decay[...] = row[:, low:high]
 
 
+def rows_before(rows, begin, stop, keep, state_dim):
+    if rows.shape[0] == RIM:
+        return rows[:, begin:stop].astype(F32)
+    step = rows.shape[1]
+    below = rows[state_dim:, begin % step : begin % step + stop - begin].astype(F32)
+    return pltpu.roll(below, (RIM - keep * (begin // step + 1)) % below.shape[0], 0)[:RIM]
+
+
 def later_kernel(group, low, high, active, rows, _, x, bc, taps_x, taps_bc, scale, state):
-    width = x.shape[1]
     both = bc.shape[2]
     state_dim = both // 2
     keep = taps_x.shape[0] - 1
-
-    def tail(begin, stop):
-        if rows.shape[0] == RIM:
-            return rows[:, begin:stop].astype(F32)
-        step = rows.shape[1]
-        below = rows[state_dim:, begin % step : begin % step + stop - begin].astype(F32)
-        extra = below.shape[0]
-        return pltpu.roll(below, (RIM - keep * (begin // step + 1)) % extra, 0)[:RIM]
 
     @pl.when(active[0] == 1)
     def _():
         def emit(here, total):
             state[:, here] = total
 
-        at = width + group * both
+        at = x.shape[1] + group * both
         emit_states(
-            group, low, high, x, lambda cut: tail(cut.start, cut.stop),
-            bc, tail(at, at + state_dim), taps_x, taps_bc, scale, emit,
+            group, low, high, x,
+            lambda cut: rows_before(rows, cut.start, cut.stop, keep, state_dim),
+            bc, rows_before(rows, at, at + state_dim, keep, state_dim),
+            taps_x, taps_bc, scale, emit,
         )
 
 
-def intra_kernel(
-    head_dim, x, got, bc, z, taps_x, taps_bc, dt_raw, a_log, d_skip, y_part, lead, c_act, wide
-):
-    dt, cum = rates(dt_raw[...], a_log[...], 0)
-    tokens, width = x.shape
-    groups, both = bc.shape[1:]
+def intra_kernel(group, count, _, *refs):
+    sources, refs = refs[:count], refs[count:]
+    x, bc, z, taps_x, taps_bc, dt_raw, a_log, d_skip, y_part, lead, c_act, wide = refs
+    tokens, cols = z.shape
+    both = bc.shape[2]
     state_dim = both // 2
-    cols = width // groups
-    heads = dt.shape[0] // groups
+    keep = taps_x.shape[0] - 1
+    heads = dt_raw.shape[0]
+    head_dim = cols // heads
+    dt, cum = rates(dt_raw[...], a_log[...], group * heads)
     cum_t = cum.T
-    leading = jnp.exp(cum)
-    skip = spread_row(as_column(d_skip[...], 0, dt.shape[0]), head_dim)
+    wide[...] = spread(jnp.exp(cum), head_dim, 2)
+    skip = spread_row(as_column(d_skip[...], group * heads, heads), head_dim)
+
+    def before(begin, stop):
+        found = [rows_before(rows, begin, stop, keep, state_dim) for rows in sources]
+        return sum(found[1:], found[0])
+
+    at = x.shape[1] + group * both
+    tail_bc = jnp.concatenate(
+        [before(at, at + state_dim), before(at + state_dim, at + both)], axis=1
+    )
+    bc_act = conv_act(bc[...].astype(F32)[:, group], tail_bc, taps_bc[...][:, group])
+    b, c = bc_act[:, :state_dim], bc_act[:, state_dim:]
+    c_act[...] = c
+    inner = lax.dot_general(c, b, (((1,), (1,)), ((), ())), preferred_element_type=F32)
     t_at = lax.broadcasted_iota(jnp.int32, (tokens, tokens), 0)
     s_at = lax.broadcasted_iota(jnp.int32, (tokens, tokens), 1)
+    inner = jnp.where(t_at >= s_at, inner, 0.0)
     pair = 2 * head_dim
-    for g in range(groups):
-        at = width + g * both
-        bc_act = conv_act(
-            bc[...].astype(F32)[:, g], got[:, at : at + both].astype(F32), taps_bc[...][:, g]
-        )
-        b, c = bc_act[:, :state_dim], bc_act[:, state_dim:]
-        c_act[:, g * state_dim : (g + 1) * state_dim] = c
-        inner = lax.dot_general(c, b, (((1,), (1,)), ((), ())), preferred_element_type=F32)
-        inner = jnp.where(t_at >= s_at, inner, 0.0)
-        wide[...] = spread(leading[g * heads : (g + 1) * heads], head_dim, 2)
-        for first in range(0, heads, 2):
-            here = first * head_dim
-            cut = slice(g * cols + here, g * cols + here + pair)
-            act = conv_act(x[:, cut].astype(F32), got[:, cut].astype(F32), taps_x[:, cut])
-            lane = lax.broadcasted_iota(jnp.int32, act.shape, 1)
-            full = act.astype(F32)
-            blocks = jnp.concatenate(
-                [jnp.where(lane < head_dim, full, 0.0), jnp.where(lane < head_dim, 0.0, full)],
-                axis=0,
-            ).astype(BF16)
-            weights = []
-            for h in (g * heads + first, g * heads + first + 1):
-                gap = jnp.minimum(cum_t[:, h : h + 1] - cum[h : h + 1, :], 0.0)
-                weights.append((jnp.exp(gap) * dt[h : h + 1, :] * inner).astype(BF16))
-            y = jnp.dot(jnp.concatenate(weights, axis=1), blocks, preferred_element_type=F32)
-            gate = silu(z[:, cut].astype(F32))
-            y_part[:, cut] = (y + skip[:, cut] * full) * gate
-            lead[:, cut] = wide[:, here : here + pair] * gate
-
-
-def gated_slice(c, y_part, lead, arrived):
-    state = arrived[0][: c.shape[1]]
-    for more in arrived[1:]:
-        state = state + more[...]
+    for first in range(0, heads, 2):
+        here = slice(first * head_dim, first * head_dim + pair)
+        cut = slice(group * cols + here.start, group * cols + here.stop)
+        act = conv_act(x[:, cut].astype(F32), before(cut.start, cut.stop), taps_x[:, cut])
+        lane = lax.broadcasted_iota(jnp.int32, act.shape, 1)
+        full = act.astype(F32)
+        blocks = jnp.concatenate(
+            [jnp.where(lane < head_dim, full, 0.0), jnp.where(lane < head_dim, 0.0, full)],
+            axis=0,
+        ).astype(BF16)
+        weights = []
+        for h in (first, first + 1):
+            gap = jnp.minimum(cum_t[:, h : h + 1] - cum[h : h + 1, :], 0.0)
+            weights.append((jnp.exp(gap) * dt[h : h + 1, :] * inner).astype(BF16))
+        y = jnp.dot(jnp.concatenate(weights, axis=1), blocks, preferred_element_type=F32)
+        gate = silu(z[:, here].astype(F32))
+        y_part[:, here] = (y + skip[:, here] * full) * gate
+        lead[:, here] = wide[:, here] * gate
+
+
+def gated_slice(which, c, y_part, lead, arrived):
+    state = jnp.zeros((c.shape[1], y_part.shape[1]), BF16)
+    for i, came in enumerate(arrived):
+        state = jnp.where(which[0] == i, came[...][: c.shape[1]], state)
     return y_part[...] + lead[...] * jnp.dot(c[...], state, preferred_element_type=F32)
 
 
-def gated_kernel(c, y_part, lead, *refs):
-    refs[-1][...] = gated_slice(c, y_part, lead, refs[:-1])
-
-
-def output_kernel(ready, seen, c, y_part, lead, gain, *refs):
+def gated_kernel(which, c, y_part, lead, *refs):
+    refs[-1][...] = gated_slice(which, c, y_part, lead, refs[:-1])
+
+
+def output_kernel(ready, seen, which, c, y_part, lead, gain, *refs):
     gated = [v[...] for v in refs[:ready]]
-    gated.append(gated_slice(c, y_part, lead, refs[ready : ready + seen]))
+    gated.append(gated_slice(which, c, y_part, lead, refs[ready : ready + seen]))
     gated = jnp.concatenate(gated, axis=1)
     mean_sq = jnp.mean(gated * gated, axis=1, keepdims=True)
     refs[-1][...] = (gated * lax.rsqrt(mean_sq + EPS) * gain[...]).astype(BF16)
@@ -339,10 +346,10 @@
             name="first_states",
         )(here(place == 0), *pinned)
 
-    def next_states(token, scale, group, low, high):
+    def next_states(token, scale, spare, group, low, high):
         return pl.pallas_call(
             functools.partial(next_kernel, group, low, high),
-            out_shape=jax.ShapeDtypeStruct((state_dim, high - low), BF16),
+            out_shape=jax.ShapeDtypeStruct((state_dim + spare, high - low), BF16),
             in_specs=[scalar, anywhere] + [in_vmem] * (len(sources) + 1),
             compiler_params=params(16),
             name="next_states",
@@ -351,12 +358,16 @@
     def prepared(token):
         return pl.pallas_call(
             functools.partial(prepare_kernel, cuts),
-            out_shape=[jax.ShapeDtypeStruct((RIM, width + groups * both), BF16), scale_shape]
+            out_shape=[
+                jax.ShapeDtypeStruct((RIM, width + groups * both), BF16),
+                jax.ShapeDtypeStruct((1, width), F32),
+                scale_shape,
+            ]
             + [jax.ShapeDtypeStruct((1, high - low), F32) for _, low, high in cuts],
-            in_specs=[anywhere] + [in_vmem] * 4,
+            in_specs=[anywhere] + [in_vmem] * 5,
             compiler_params=params(16),
             name="prepared",
-        )(token, x_in, bc_in, dt_t, a_row)
+        )(token, x_in, bc_in, dt_t, a_row, gain)
 
     def later_states(condition, rows, token, scale, group, low, high):
         return pl.pallas_call(
@@ -368,53 +379,92 @@
         )(here(condition), rows, token, *sources, scale)
 
     along = [(i, i + 1) for i in range(devices - 1)]
+    def intra(token, befores, group):
+        return pl.pallas_call(
+            functools.partial(intra_kernel, group, len(befores)),
+            out_shape=[
+                jax.ShapeDtypeStruct((tokens, cols), F32),
+                jax.ShapeDtypeStruct((tokens, cols), F32),
+                jax.ShapeDtypeStruct((tokens, state_dim), BF16),
+            ],
+            in_specs=[anywhere]
+            + [whole(v) for v in befores]
+            + [
+                whole(x_in), whole(bc_in), column(tokens, cols, group),
+                whole(conv_x), whole(conv_bc),
+                pl.BlockSpec((heads // groups, tokens), lambda i: (group, 0)),
+                whole(a_row), whole(d_row),
+            ],
+            out_specs=[column(tokens, cols, 0)] * 2 + [column(tokens, state_dim, 0)],
+            grid=(1,),
+            scratch_shapes=[pltpu.VMEM((tokens, cols), F32)],
+            compiler_params=params(24),
+            cost_estimate=pl.CostEstimate(
+                flops=4 * tokens * tokens * cols,
+                bytes_accessed=12 * tokens * cols,
+                transcendentals=tokens * tokens * heads // groups,
+            ),
+            name="intra",
+        )(token, *befores, x_in, bc_in, z_in, conv_x, conv_bc, dt_t, a_row, d_row)
+
     if devices <= CHAIN_MOST:
         first, scale = first_states(*cuts[0])
+        spare = first.shape[0] - state_dim + RIM
         sent = [first]
-        for cut in cuts[1:]:
-            sent.append(next_states(sent[-1], scale, *cut))
-        last, scale, *decays = prepared(sent[-1])
-        got = shifted(last, along)
-        arrived = [[shifted(v, along[:1])] for v in sent]
+        for i, cut in enumerate(cuts[1:], 1):
+            if i == len(cuts) - 2:
+                last, gain, scale_own, *decays = prepared(sent[-1])
+                sent.append(next_states(last, scale, 0, *cut))
+            else:
+                sent.append(next_states(sent[-1], scale, spare if i == 1 else 0, *cut))
+        soon = along[1 : max(devices - 2, 1)]
+        late = along[max(devices - 2, 1) :]
+        befores = [shifted(last, soon)] if soon else []
+        arrived = [[shifted(v, along[:1])] for v in sent[:-1]] + [[]]
+        waiting = sent[-1]
+        befores.append(arrived[0][0])
         rows, token = arrived[0][0], last
         for hop in range(1, devices - 1):
-            condition = place == 1 if hop == 1 else place >= 2
-            after = token
-            for i, (seen, cut) in enumerate(zip(arrived, cuts)):
+            runs = place == 1 if hop == 1 else (place >= 2) & (place < devices - 1)
+            after = token if hop == 1 else settled
+            for i, cut in enumerate(cuts):
                 if hop <= 2:
-                    made = later_states(condition, rows, after, scale, *cut)
+                    made = later_states(runs, rows, after, scale_own, *cut)
                     states = [made] if i == 0 else states + [made]
-                early = arrived[0][-1] if hop > 1 and i == len(cuts) - 1 else token
-                before, _, _ = lax.optimization_barrier((seen[-1], token, early))
+                early = ()
+                if hop == devices - 2 and hop > 1 and i == len(cuts) - 1:
+                    early = (befores[-1],)
+                before, *_ = lax.optimization_barrier((arrived[i][-1], token) + early)
                 joined = decays[i] * before[:state_dim].astype(F32) + states[i]
                 token = joined.astype(BF16)
-                after = token if hop == 1 and i == 0 else after
-                seen.append(shifted(token, along[hop : hop + 1]))
-            rows = got
+                if hop == 1 and i == 0:
+                    after = token
+                if hop == 1 and i == 1:
+                    settled = token
+                if i == 0:
+                    both_ways = jnp.where(place == hop - 1, waiting, token)
+                    came = shifted(both_ways, along[hop - 1 : hop + 1])
+                    arrived[-1].append(came)
+                    arrived[0].append(came)
+                elif i < len(cuts) - 1:
+                    arrived[i].append(shifted(token, along[hop : hop + 1]))
+            waiting = token
+            if hop == 1 and late:
+                moved, _ = lax.optimization_barrier((last, token))
+                befores.append(shifted(moved, late))
+            rows = befores[0]
+        arrived[-1].append(shifted(waiting, along[devices - 2 :]))
+        which = place - 1
     else:
-        last, scale, *decays = prepared(a_row)
-        got = shifted(last, along)
+        last, gain, scale, *decays = prepared(a_row)
+        befores = [shifted(last, along)]
         arrived = []
         for decay, cut in zip(decays, cuts):
-            state = later_states(place >= 0, got, a_row, scale, *cut)
+            state = later_states(place >= 0, befores[0], a_row, scale, *cut)
             arrived.append([doubling(state, decay, devices)])
-
-    y_part, lead, c_act = pl.pallas_call(
-        functools.partial(intra_kernel, head_dim),
-        out_shape=(
-            jax.ShapeDtypeStruct((tokens, width), F32),
-            jax.ShapeDtypeStruct((tokens, width), F32),
-            jax.ShapeDtypeStruct((tokens, groups * state_dim), BF16),
-        ),
-        scratch_shapes=[pltpu.VMEM((tokens, cols), F32)],
-        compiler_params=params(32),
-        cost_estimate=pl.CostEstimate(
-            flops=4 * tokens * tokens * width,
-            bytes_accessed=12 * tokens * width,
-            transcendentals=tokens * tokens * heads,
-        ),
-        name="intra",
-    )(x_in, got, bc_in, z_in, conv_x, conv_bc, dt_t, a_row, d_row)
+        which = jnp.zeros_like(place)
+    which = which.astype(jnp.int32).reshape(1)
+    parts = [intra(a_row, befores, g) for g in range(groups)]
 
     out = None
     for g in range(groups):
@@ -422,8 +472,9 @@
         for (group, low, high), seen in zip(cuts, arrived):
             if group != g:
                 continue
-            inputs = [c_act, y_part, lead]
-            specs = [column(tokens, state_dim, g)] + [slab(low, high)] * 2
+            y_part, lead, c_act = parts[g]
+            inputs = [which, c_act, y_part, lead]
+            specs = [scalar, whole(c_act)] + [slab(low - g * cols, high - g * cols)] * 2
             if high < (g + 1) * cols:
                 ready.append(
                     pl.pallas_call(

time: 30.7 us -> 34.1 us (1.11)
  the two profiles are of different devices: /device:TPU:30 before, /device:TPU:20 now
where the time goes in v8:
time: 34.1 us; the launch traced here: 33.7 us
  starting transfers between devices  16.3 us (48%)
  Pallas kernels  7.77 us (23%)
  waiting for transfers between devices  7.48 us (22%)
  other arithmetic  0.99 us (3%)
  local copies, waits for them, and re-layouts  0.84 us (2%)
  between operations  0.4 us (1%)
    ppermute x12, starting transfers between devices, shifted(): return lax.ppermute(value, 'seq', route)  16.3 us
    ppermute x12, waiting for transfers between devices, shifted(): return lax.ppermute(value, 'seq', route)  7.48 us
    pallas_call x2, Pallas kernels, intra(): pl.pallas_call(functools.partial(intra_kernel, group, len(befores)), out_...  2.75 us
    pallas_call x2, Pallas kernels, shards(): pl.pallas_call(functools.partial(output_kernel, len(ready), len(arrived[0...  2.01 us
    pallas_call x8, Pallas kernels, later_states(): pl.pallas_call(functools.partial(later_kernel, group, low, high), out_sha...  1.84 us
    convert_element_type x6, other arithmetic, shards(): token = joined.astype(BF16)  0.87 us
    unnamed x18, local copies, waits for them, and re-layouts  0.84 us
    pallas_call x1, Pallas kernels, prepared(): pl.pallas_call(functools.partial(prepare_kernel, cuts), out_shape=[jax.Sh...  0.71 us
  transfers between devices with their start and end apart: 12, of which 3 were waited for; matrix products, arithmetic and copies ran while one was open for 3% of the time, Pallas kernels for 20%

profile of v8, /device:TPU:20, one launch (start us, length us, event | category | flops | bytes accessed | tf_op | source)
XLA Modules:
  0.0 33.7 jit_solution(15914953798322313310)
XLA Ops:
  0.0 0.0 copy-start.4
  0.0 0.1 first_states.1
  0.1 0.8 %collective-permute-start.1 = (bf16[144,512]{1,0:T(8,128)(2,1)S(1)}, bf16[144,512]{1,0:T(8,128)(2,1)S(1)}, u32[]{:S(2)}, u32[]{:S(2)}) collective-permute-start(bf16[144,512]{1,0:T(8,128)(2,1)S(1)} %get-tuple-element.29._), channel_id=1, source_target_pairs={{0,4},{1,5},{2,6},{3,7},{16,20},{17,21},{18,22},{19,23}} | collective-permute-start | bytes 442376 | tf_op jit(solution)/shard_map/ppermute | solution.py:335
  0.9 0.1 copy-done
  1.0 0.0 copy-done.1
  1.1 0.0 copy-done.2
  1.1 0.0 copy-done.4
  1.1 0.0 copy-start.6
  1.1 0.7 %collective-permute-start.4 = (bf16[152,512]{1,0:T(8,128)(2,1)S(1)}, bf16[152,512]{1,0:T(8,128)(2,1)S(1)}, u32[]{:S(2)}, u32[]{:S(2)}) collective-permute-start(bf16[152,512]{1,0:T(8,128)(2,1)S(1)} %next_states.3._), channel_id=1, source_target_pairs={{0,4},{1,5},{2,6},{3,7},{16,20},{17,21},{18,22},{19,23}} | collective-permute-start | bytes 466952 | tf_op jit(solution)/shard_map/ppermute | solution.py:335
  1.8 0.7 %prepared.1 = (bf16[8,2560]{1,0:T(8,128)(2,1)S(1)}, f32[1,2048]{1,0:T(1,128)S(1)}, f32[128,2048]{1,0:T(8,128)S(1)}, f32[1,512]{1,0:T(1,128)S(1)}, f32[1,512]{1,0...) custom-call(bf16[152,512]{1,0:T(8,128)(2,1)S(1)} %next_states.3._, bf16[128,2048]{1,0:T(8,128)(2,1)S(1)} %copy-done, ...), custom_call_target="tpu_custom_call" | custom-call | tf_op jit(solution)/shard_map/prepared/pallas_call | solution.py:359
  2.5 1.3 %collective-permute-start = (bf16[8,2560]{1,0:T(8,128)(2,1)S(1)}, bf16[8,2560]{1,0:T(8,128)(2,1)S(1)}, u32[]{:S(2)}, u32[]{:S(2)}) collective-permute-start(bf16[8,2560]{1,0:T(8,128)(2,1)S(1)} %get-tuple-element.41._), channel_id=1, source_target_pairs={{4,8},{5,9},{6,10},{7,11},{20,24},{21,25},{22,26},{23,27}} | collective-permute-start | bytes 122888 | tf_op jit(solution)/shard_map/ppermute | solution.py:335
  3.9 0.7 %collective-permute-start.3 = (bf16[128,512]{1,0:T(8,128)(2,1)S(1)}, bf16[128,512]{1,0:T(8,128)(2,1)S(1)}, u32[]{:S(2)}, u32[]{:S(2)}) collective-permute-start(bf16[128,512]{1,0:T(8,128)(2,1)S(1)} %next_states.4._), channel_id=1, source_target_pairs={{0,4},{1,5},{2,6},{3,7},{16,20},{17,21},{18,22},{19,23}} | collective-permute-start | bytes 393224 | tf_op jit(solution)/shard_map/ppermute | solution.py:335
  4.6 0.0 collective-permute-done.1.rows.refs_1_.refs_0_
  4.6 0.1 broadcast_select_fusion.1
  4.7 1.3 %collective-permute-start.2 = (bf16[128,512]{1,0:T(8,128)(2,1)S(1)}, bf16[128,512]{1,0:T(8,128)(2,1)S(1)}, u32[]{:S(2)}, u32[]{:S(2)}) collective-permute-start(bf16[128,512]{1,0:T(8,128)(2,1)S(1)} %get-tuple-element.55), channel_id=1, source_target_pairs={{0,4},{4,8},{1,5},{5,9},{2,6},{6,10},{3,7},{7,11},{16,20},{20,24},... | collective-permute-start | bytes 393224 | tf_op jit(solution)/shard_map/ppermute | solution.py:335
  6.0 0.0 collective-permute-done.4.refs_1_
  6.1 1.3 %collective-permute-start.7 = (bf16[128,512]{1,0:T(8,128)(2,1)S(1)}, bf16[128,512]{1,0:T(8,128)(2,1)S(1)}, u32[]{:S(2)}, u32[]{:S(2)}) collective-permute-start(bf16[128,512]{1,0:T(8,128)(2,1)S(1)} %add_convert_fusion.6._), channel_id=1, source_target_pairs={{4,8},{5,9},{6,10},{7,11},{20,24},{21,25},{22,26},{23,27}} | collective-permute-start | bytes 393224 | tf_op jit(solution)/shard_map/ppermute | solution.py:335
  7.4 0.0 collective-permute-done.3.refs_0_
  7.4 1.3 %collective-permute-start.6 = (bf16[128,512]{1,0:T(8,128)(2,1)S(1)}, bf16[128,512]{1,0:T(8,128)(2,1)S(1)}, u32[]{:S(2)}, u32[]{:S(2)}) collective-permute-start(bf16[128,512]{1,0:T(8,128)(2,1)S(1)} %add_convert_fusion.5), channel_id=1, source_target_pairs={{4,8},{5,9},{6,10},{7,11},{20,24},{21,25},{22,26},{23,27}} | collective-permute-start | bytes 393224 | tf_op jit(solution)/shard_map/ppermute | solution.py:335
  8.7 0.0 collective-permute-done.refs_0_.rows
  8.7 0.5 %later_states.15 = f32[128,512]{1,0:T(8,128)S(1)} custom-call(s32[1]{0:T(128)} %bitcast.11.active, bf16[8,2560]{1,0:T(8,128)(2,1)S(1)} %collective-permute-done.refs_0_.rows, bf16[128,512]{1,0:T(8,128)(2,1)S(1)} %add_convert_fusion.6._, bf16[128,2048]{1,0:T(8,128)(2,1)S(1)} %copy-done, bf16[128,2,256]{2,1,0:T(2,128)(2,1)S(1)} %copy-done.1, ...), custom_call_target="tpu_custom_call" | custom-call | tf_op jit(solution)/shard_map/later_states/pallas_call | solution.py:373
  9.2 0.4 %later_states.14 = f32[128,512]{1,0:T(8,128)S(1)} custom-call(s32[1]{0:T(128)} %bitcast.11.active, bf16[8,2560]{1,0:T(8,128)(2,1)S(1)} %collective-permute-done.refs_0_.rows, bf16[128,512]{1,0:T(8,128)(2,1)S(1)} %add_convert_fusion.6._, bf16[128,2048]{1,0:T(8,128)(2,1)S(1)} %copy-done, bf16[128,2,256]{2,1,0:T(2,128)(2,1)S(1)} %copy-done.1, ...), custom_call_target="tpu_custom_call" | custom-call | tf_op jit(solution)/shard_map/later_states/pallas_call | solution.py:373
  9.6 0.4 %later_states.13 = f32[128,512]{1,0:T(8,128)S(1)} custom-call(s32[1]{0:T(128)} %bitcast.11.active, bf16[8,2560]{1,0:T(8,128)(2,1)S(1)} %collective-permute-done.refs_0_.rows, bf16[128,512]{1,0:T(8,128)(2,1)S(1)} %add_convert_fusion.6._, bf16[128,2048]{1,0:T(8,128)(2,1)S(1)} %copy-done, bf16[128,2,256]{2,1,0:T(2,128)(2,1)S(1)} %copy-done.1, ...), custom_call_target="tpu_custom_call" | custom-call | tf_op jit(solution)/shard_map/later_states/pallas_call | solution.py:373
  10.1 0.4 %later_states.12 = f32[128,512]{1,0:T(8,128)S(1)} custom-call(s32[1]{0:T(128)} %bitcast.11.active, bf16[8,2560]{1,0:T(8,128)(2,1)S(1)} %collective-permute-done.refs_0_.rows, bf16[128,512]{1,0:T(8,128)(2,1)S(1)} %add_convert_fusion.6._, bf16[128,2048]{1,0:T(8,128)(2,1)S(1)} %copy-done, bf16[128,2,256]{2,1,0:T(2,128)(2,1)S(1)} %copy-done.1, ...), custom_call_target="tpu_custom_call" | custom-call | tf_op jit(solution)/shard_map/later_states/pallas_call | solution.py:373
  10.6 5.4 %collective-permute-done.2.refs_1_ = bf16[128,512]{1,0:T(8,128)(2,1)S(1)} collective-permute-done((bf16[128,512]{1,0:T(8,128)(2,1)S(1)}, bf16[128,512]{1,0:T(8,128)(2,1)S(1)}, u32[]{:S(2)}, u32[]{:S(2)}) %collective-permute-start.2) | collective-permute-done | bytes 131104 | tf_op jit(solution)/shard_map/ppermute | solution.py:335
  16.0 1.3 %collective-permute-start.5 = (bf16[8,2560]{1,0:T(8,128)(2,1)S(1)}, bf16[8,2560]{1,0:T(8,128)(2,1)S(1)}, u32[]{:S(2)}, u32[]{:S(2)}) collective-permute-start(bf16[8,2560]{1,0:T(8,128)(2,1)S(1)} %get-tuple-element.41._), channel_id=1, source_target_pairs={{8,12},{9,13},{10,14},{11,15},{24,28},{25,29},{26,30},{27,31}} | collective-permute-start | bytes 122888 | tf_op jit(solution)/shard_map/ppermute | solution.py:335
  17.3 0.1 broadcast_select_fusion
  17.3 1.9 %collective-permute-start.9 = (bf16[128,512]{1,0:T(8,128)(2,1)S(1)}, bf16[128,512]{1,0:T(8,128)(2,1)S(1)}, u32[]{:S(2)}, u32[]{:S(2)}) collective-permute-start(bf16[128,512]{1,0:T(8,128)(2,1)S(1)} %broadcast_select_fusion), channel_id=1, source_target_pairs={{4,8},{8,12},{5,9},{9,13},{6,10},{10,14},{7,11},{11,15},{20,24},{2... | collective-permute-start | bytes 393224 | tf_op jit(solution)/shard_map/ppermute | solution.py:335
  19.3 0.0 collective-permute-done.7.refs_2_
  19.3 0.0 copy-start.3
  19.3 1.4 %collective-permute-start.11 = (bf16[128,512]{1,0:T(8,128)(2,1)S(1)}, bf16[128,512]{1,0:T(8,128)(2,1)S(1)}, u32[]{:S(2)}, u32[]{:S(2)}) collective-permute-start(bf16[128,512]{1,0:T(8,128)(2,1)S(1)} %add_convert_fusion.2), channel_id=1, source_target_pairs={{8,12},{9,13},{10,14},{11,15},{24,28},{25,29},{26,30},{27,31}} | collective-permute-start | bytes 393224 | tf_op jit(solution)/shard_map/ppermute | solution.py:335
  20.8 0.6 %collective-permute-done.6.refs_1_ = bf16[128,512]{1,0:T(8,128)(2,1)S(1)} collective-permute-done((bf16[128,512]{1,0:T(8,128)(2,1)S(1)}, bf16[128,512]{1,0:T(8,128)(2,1)S(1)}, u32[]{:S(2)}, u32[]{:S(2)}) %collective-permute-start.6) | collective-permute-done | bytes 131104 | tf_op jit(solution)/shard_map/ppermute | solution.py:335
  21.5 1.3 %collective-permute-start.8 = (bf16[128,512]{1,0:T(8,128)(2,1)S(1)}, bf16[128,512]{1,0:T(8,128)(2,1)S(1)}, u32[]{:S(2)}, u32[]{:S(2)}) collective-permute-start(bf16[128,512]{1,0:T(8,128)(2,1)S(1)} %add_convert_fusion.1), channel_id=1, source_target_pairs={{8,12},{9,13},{10,14},{11,15},{24,28},{25,29},{26,30},{27,31}} | collective-permute-start | bytes 393224 | tf_op jit(solution)/shard_map/ppermute | solution.py:335
  22.8 0.0 collective-permute-done.5.refs_2_
  22.8 1.4 %collective-permute-done.9.refs_2_ = bf16[128,512]{1,0:T(8,128)(2,1)S(1)} collective-permute-done((bf16[128,512]{1,0:T(8,128)(2,1)S(1)}, bf16[128,512]{1,0:T(8,128)(2,1)S(1)}, u32[]{:S(2)}, u32[]{:S(2)}) %collective-permute-start.9) | collective-permute-done | bytes 131104 | tf_op jit(solution)/shard_map/ppermute | solution.py:335
  24.2 0.7 %add_convert_fusion = bf16[128,512]{1,0:T(8,128)(2,1)} fusion(f32[128,512]{1,0:T(8,128)S(1)} %later_states.15, bf16[128,512]{1,0:T(8,128)(2,1)S(1)} %collective-permute-done.9.refs_2_, f32[512]{0:T(512)S(1)} %bitcast.24), kind=kLoop, calls=%fused_computation | loop fusion | flops 262144 | bytes 526336 | tf_op jit(solution)/shard_map/convert_element_type | solution.py:439
  24.9 3.0 %collective-permute-start.10 = (bf16[128,512]{1,0:T(8,128)(2,1)}, bf16[128,512]{1,0:T(8,128)(2,1)S(1)}, u32[]{:S(2)}, u32[]{:S(2)}) collective-permute-start(bf16[128,512]{1,0:T(8,128)(2,1)} %add_convert_fusion), channel_id=1, source_target_pairs={{8,12},{9,13},{10,14},{11,15},{24,28},{25,29},{26,30},{27,31}} | collective-permute-start | bytes 393224 | tf_op jit(solution)/shard_map/ppermute | solution.py:335
  27.9 0.0 copy-start.8
  27.9 0.6 %copy-done.8 = f32[32]{0:T(128)S(1)} copy-done((f32[32]{0:T(128)S(1)}, f32[32]{0:T(128)}, u32[]{:S(2)}) %copy-start.8) | copy-done | bytes 152
  28.6 1.4 %intra.3 = (f32[128,1024]{1,0:T(8,128)S(1)}, f32[128,1024]{1,0:T(8,128)S(1)}, bf16[128,128]{1,0:T(8,128)(2,1)S(1)}) custom-call(f32[1,32]{1,0:T(1,128)S(1)} %bitcast.18, bf16[8,2560]{1,0:T(8,128)(2,1)S(1)} %collective-permute-done.refs_0_.rows, bf16[144,512]{1,0:T(8,128)(2,1)S(1)} %collective-permute-done.1.rows.refs_1_.refs_0_, ...), custom_call_target="tpu_custom_call" | custom-call | flops 67108864 | bytes 1572864 | tf_op jit(solution)/shard_map/intra/pallas_call | solution.py:383
  29.9 1.4 %intra.2 = (f32[128,1024]{1,0:T(8,128)S(1)}, f32[128,1024]{1,0:T(8,128)S(1)}, bf16[128,128]{1,0:T(8,128)(2,1)S(1)}) custom-call(f32[1,32]{1,0:T(1,128)S(1)} %bitcast.20, bf16[8,2560]{1,0:T(8,128)(2,1)S(1)} %collective-permute-done.refs_0_.rows, bf16[144,512]{1,0:T(8,128)(2,1)S(1)} %collective-permute-done.1.rows.refs_1_.refs_0_, ...), custom_call_target="tpu_custom_call" | custom-call | flops 67108864 | bytes 1572864 | tf_op jit(solution)/shard_map/intra/pallas_call | solution.py:383
  31.3 0.2 gated.3.refs_0_
  31.5 0.0 collective-permute-done.11.refs_3_
  31.5 1.0 %outputs.2.refs_4_ = bf16[128,2048]{1,0:T(8,128)(2,1)} custom-call(s32[1]{0:T(128)} %bitcast.which, bf16[128,128]{1,0:T(8,128)(2,1)S(1)} %get-tuple-element.50.c, f32[128,1024]{1,0:T(8,128)S(1)} %get-tuple-element.51.y_part, f32[128,1024]{1,0:T(8,128)S(1)} %get-tuple-element.52.lead, f32[1,2048]{1,0:T(1,128)S(1)} %get-tuple-element.45.gain, ...), custom_call_target="tpu_custom_call" | custom-call | tf_op jit(solution)/shard_map/outputs/pallas_call | solution.py:497
  32.5 0.0 collective-permute-done.8.refs_2_
  32.5 0.2 gated.2.refs_0_
  32.7 0.0 collective-permute-done.10.refs_3_
  32.7 1.0 %outputs.3 = bf16[128,2048]{1,0:T(8,128)(2,1)} custom-call(s32[1]{0:T(128)} %bitcast.which, bf16[128,128]{1,0:T(8,128)(2,1)S(1)} %get-tuple-element.42.c, f32[128,1024]{1,0:T(8,128)S(1)} %get-tuple-element.43.y_part, f32[128,1024]{1,0:T(8,128)S(1)} %get-tuple-element.44.lead, f32[1,2048]{1,0:T(1,128)S(1)} %get-tuple-element.45.gain, ...), custom_call_target="tpu_custom_call", output_to_operand_aliasing={{}: (9, {})} | custom-call | tf_op jit(solution)/shard_map/outputs/pallas_call | solution.py:497
  (21 shorter events, 0.3 us)
Async XLA Ops:
  0.0 1.0 %copy-start = (bf16[128,2048]{1,0:T(8,128)(2,1)S(1)}, bf16[128,2048]{1,0:T(8,128)(2,1)}, u32[]{:S(2)}) copy-start(bf16[128,2048]{1,0:T(8,128)(2,1)} %refs_3_.3) | copy-start | bytes 1572868
  0.0 1.1 %copy-start.1 = (bf16[128,2,256]{2,1,0:T(2,128)(2,1)S(1)}, bf16[128,2,256]{2,1,0:T(2,128)(2,1)}, u32[]{:S(2)}) copy-start(bf16[128,2,256]{2,1,0:T(2,128)(2,1)} %refs_4_.3) | copy-start | bytes 393220
  0.0 1.1 %copy-start.2 = (f32[4,2048]{1,0:T(4,128)S(1)}, f32[4,2048]{1,0:T(4,128)}, u32[]{:S(2)}) copy-start(f32[4,2048]{1,0:T(4,128)} %refs_6_.3) | copy-start | bytes 98308
  0.0 1.1 %copy-start.4 = (f32[4,2,256]{2,1,0:T(2,128)S(1)}, f32[4,2,256]{2,1,0:T(2,128)}, u32[]{:S(2)}) copy-start(f32[4,2,256]{2,1,0:T(2,128)} %refs_7_.3) | copy-start | bytes 24580
  0.1 4.5 %collective-permute-start.1 = (bf16[144,512]{1,0:T(8,128)(2,1)S(1)}, bf16[144,512]{1,0:T(8,128)(2,1)S(1)}, u32[]{:S(2)}, u32[]{:S(2)}) collective-permute-start(bf16[144,512]{1,0:T(8,128)(2,1)S(1)} %get-tuple-element.29._), channel_id=1, source_target_pairs={{0,4},{1,5},{2,6},{3,7},{16,20},{17,21},{18,22},{19,23}} | collective-permute-start | bytes 442376 | tf_op jit(solution)/shard_map/ppermute | solution.py:335
  1.1 0.7 %copy-start.5 = (f32[128,32]{0,1:T(8,128)S(1)}, f32[128,32]{0,1:T(8,128)}, u32[]{:S(2)}) copy-start(f32[128,32]{0,1:T(8,128)} %param.12) | copy-start | bytes 49156
  1.1 0.7 %copy-start.7 = (f32[2048]{0:T(1024)S(1)}, f32[2048]{0:T(1024)}, u32[]{:S(2)}) copy-start(f32[2048]{0:T(1024)} %param.17) | copy-start | bytes 24580
  1.1 0.7 %copy-start.6 = (f32[32]{0:T(128)S(1)}, f32[32]{0:T(128)}, u32[]{:S(2)}) copy-start(f32[32]{0:T(128)} %param.15) | copy-start | bytes 388
  1.1 4.9 %collective-permute-start.4 = (bf16[152,512]{1,0:T(8,128)(2,1)S(1)}, bf16[152,512]{1,0:T(8,128)(2,1)S(1)}, u32[]{:S(2)}, u32[]{:S(2)}) collective-permute-start(bf16[152,512]{1,0:T(8,128)(2,1)S(1)} %next_states.3._), channel_id=1, source_target_pairs={{0,4},{1,5},{2,6},{3,7},{16,20},{17,21},{18,22},{19,23}} | collective-permute-start | bytes 466952 | tf_op jit(solution)/shard_map/ppermute | solution.py:335
  2.5 6.2 %collective-permute-start = (bf16[8,2560]{1,0:T(8,128)(2,1)S(1)}, bf16[8,2560]{1,0:T(8,128)(2,1)S(1)}, u32[]{:S(2)}, u32[]{:S(2)}) collective-permute-start(bf16[8,2560]{1,0:T(8,128)(2,1)S(1)} %get-tuple-element.41._), channel_id=1, source_target_pairs={{4,8},{5,9},{6,10},{7,11},{20,24},{21,25},{22,26},{23,27}} | collective-permute-start | bytes 122888 | tf_op jit(solution)/shard_map/ppermute | solution.py:335
  3.9 3.5 %collective-permute-start.3 = (bf16[128,512]{1,0:T(8,128)(2,1)S(1)}, bf16[128,512]{1,0:T(8,128)(2,1)S(1)}, u32[]{:S(2)}, u32[]{:S(2)}) collective-permute-start(bf16[128,512]{1,0:T(8,128)(2,1)S(1)} %next_states.4._), channel_id=1, source_target_pairs={{0,4},{1,5},{2,6},{3,7},{16,20},{17,21},{18,22},{19,23}} | collective-permute-start | bytes 393224 | tf_op jit(solution)/shard_map/ppermute | solution.py:335
  4.7 11.3 %collective-permute-start.2 = (bf16[128,512]{1,0:T(8,128)(2,1)S(1)}, bf16[128,512]{1,0:T(8,128)(2,1)S(1)}, u32[]{:S(2)}, u32[]{:S(2)}) collective-permute-start(bf16[128,512]{1,0:T(8,128)(2,1)S(1)} %get-tuple-element.55), channel_id=1, source_target_pairs={{0,4},{4,8},{1,5},{5,9},{2,6},{6,10},{3,7},{7,11},{16,20},{20,24},... | collective-permute-start | bytes 393224 | tf_op jit(solution)/shard_map/ppermute | solution.py:335
  6.1 13.2 %collective-permute-start.7 = (bf16[128,512]{1,0:T(8,128)(2,1)S(1)}, bf16[128,512]{1,0:T(8,128)(2,1)S(1)}, u32[]{:S(2)}, u32[]{:S(2)}) collective-permute-start(bf16[128,512]{1,0:T(8,128)(2,1)S(1)} %add_convert_fusion.6._), channel_id=1, source_target_pairs={{4,8},{5,9},{6,10},{7,11},{20,24},{21,25},{22,26},{23,27}} | collective-permute-start | bytes 393224 | tf_op jit(solution)/shard_map/ppermute | solution.py:335
  7.4 14.0 %collective-permute-start.6 = (bf16[128,512]{1,0:T(8,128)(2,1)S(1)}, bf16[128,512]{1,0:T(8,128)(2,1)S(1)}, u32[]{:S(2)}, u32[]{:S(2)}) collective-permute-start(bf16[128,512]{1,0:T(8,128)(2,1)S(1)} %add_convert_fusion.5), channel_id=1, source_target_pairs={{4,8},{5,9},{6,10},{7,11},{20,24},{21,25},{22,26},{23,27}} | collective-permute-start | bytes 393224 | tf_op jit(solution)/shard_map/ppermute | solution.py:335
  16.0 6.8 %collective-permute-start.5 = (bf16[8,2560]{1,0:T(8,128)(2,1)S(1)}, bf16[8,2560]{1,0:T(8,128)(2,1)S(1)}, u32[]{:S(2)}, u32[]{:S(2)}) collective-permute-start(bf16[8,2560]{1,0:T(8,128)(2,1)S(1)} %get-tuple-element.41._), channel_id=1, source_target_pairs={{8,12},{9,13},{10,14},{11,15},{24,28},{25,29},{26,30},{27,31}} | collective-permute-start | bytes 122888 | tf_op jit(solution)/shard_map/ppermute | solution.py:335
  17.3 6.9 %collective-permute-start.9 = (bf16[128,512]{1,0:T(8,128)(2,1)S(1)}, bf16[128,512]{1,0:T(8,128)(2,1)S(1)}, u32[]{:S(2)}, u32[]{:S(2)}) collective-permute-start(bf16[128,512]{1,0:T(8,128)(2,1)S(1)} %broadcast_select_fusion), channel_id=1, source_target_pairs={{4,8},{8,12},{5,9},{9,13},{6,10},{10,14},{7,11},{11,15},{20,24},{2... | collective-permute-start | bytes 393224 | tf_op jit(solution)/shard_map/ppermute | solution.py:335
  19.3 8.6 %copy-start.3 = (bf16[128,2048]{1,0:T(8,128)(2,1)S(1)}, bf16[128,2048]{1,0:T(8,128)(2,1)}, u32[]{:S(2)}) copy-start(bf16[128,2048]{1,0:T(8,128)(2,1)} %refs_5_.3) | copy-start | bytes 1572868
  19.3 12.2 %collective-permute-start.11 = (bf16[128,512]{1,0:T(8,128)(2,1)S(1)}, bf16[128,512]{1,0:T(8,128)(2,1)S(1)}, u32[]{:S(2)}, u32[]{:S(2)}) collective-permute-start(bf16[128,512]{1,0:T(8,128)(2,1)S(1)} %add_convert_fusion.2), channel_id=1, source_target_pairs={{8,12},{9,13},{10,14},{11,15},{24,28},{25,29},{26,30},{27,31}} | collective-permute-start | bytes 393224 | tf_op jit(solution)/shard_map/ppermute | solution.py:335
  21.5 11.1 %collective-permute-start.8 = (bf16[128,512]{1,0:T(8,128)(2,1)S(1)}, bf16[128,512]{1,0:T(8,128)(2,1)S(1)}, u32[]{:S(2)}, u32[]{:S(2)}) collective-permute-start(bf16[128,512]{1,0:T(8,128)(2,1)S(1)} %add_convert_fusion.1), channel_id=1, source_target_pairs={{8,12},{9,13},{10,14},{11,15},{24,28},{25,29},{26,30},{27,31}} | collective-permute-start | bytes 393224 | tf_op jit(solution)/shard_map/ppermute | solution.py:335
  24.9 7.8 %collective-permute-start.10 = (bf16[128,512]{1,0:T(8,128)(2,1)}, bf16[128,512]{1,0:T(8,128)(2,1)S(1)}, u32[]{:S(2)}, u32[]{:S(2)}) collective-permute-start(bf16[128,512]{1,0:T(8,128)(2,1)} %add_convert_fusion), channel_id=1, source_target_pairs={{8,12},{9,13},{10,14},{11,15},{24,28},{25,29},{26,30},{27,31}} | collective-permute-start | bytes 393224 | tf_op jit(solution)/shard_map/ppermute | solution.py:335
  27.9 0.7 %copy-start.8 = (f32[32]{0:T(128)S(1)}, f32[32]{0:T(128)}, u32[]{:S(2)}) copy-start(f32[32]{0:T(128)} %param.16) | copy-start | bytes 388

commit v9 on v6

--- a/solution.py
+++ b/solution.py
@@ -158,73 +158,83 @@
         head_rows(group, low, high, x, bc, taps_x, taps_bc, scale, out)
 
 
-def prepare_kernel(cuts, _, x, bc, dt_raw, a_log, pack, scale, *decays):
+def prepare_kernel(cuts, _, x, bc, dt_raw, a_log, gain, pack, gain_out, scale, *decays):
     tokens, width = x.shape
     groups, both = bc.shape[1:]
     pack[:, :width] = x[tokens - 2 * RIM :, :].astype(F32)[-RIM:].astype(BF16)
     last_bc = bc[tokens - 2 * RIM :].astype(F32)[-RIM:]
     for g in range(groups):
         pack[:, width + g * both : width + (g + 1) * both] = last_bc[:, g].astype(BF16)
+    gain_out[...] = gain[...]
     row = scales(width // dt_raw.shape[0], dt_raw, a_log, scale)
     for decay, (_, low, high) in zip(decays, cuts):
         decay[...] = row[:, low:high]
 
 
+def rows_before(rows, begin, stop, keep, state_dim):
+    if rows.shape[0] == RIM:
+        return rows[:, begin:stop].astype(F32)
+    step = rows.shape[1]
+    below = rows[state_dim:, begin % step : begin % step + stop - begin].astype(F32)
+    return pltpu.roll(below, (RIM - keep * (begin // step + 1)) % below.shape[0], 0)[:RIM]
+
+
 def later_kernel(group, low, high, active, rows, _, x, bc, taps_x, taps_bc, scale, state):
-    width = x.shape[1]
     both = bc.shape[2]
     state_dim = both // 2
     keep = taps_x.shape[0] - 1
-
-    def tail(begin, stop):
-        if rows.shape[0] == RIM:
-            return rows[:, begin:stop].astype(F32)
-        step = rows.shape[1]
-        below = rows[state_dim:, begin % step : begin % step + stop - begin].astype(F32)
-        extra = below.shape[0]
-        return pltpu.roll(below, (RIM - keep * (begin // step + 1)) % extra, 0)[:RIM]
 
     @pl.when(active[0] == 1)
     def _():
         def emit(here, total):
             state[:, here] = total
 
-        at = width + group * both
+        at = x.shape[1] + group * both
         emit_states(
-            group, low, high, x, lambda cut: tail(cut.start, cut.stop),
-            bc, tail(at, at + state_dim), taps_x, taps_bc, scale, emit,
+            group, low, high, x,
+            lambda cut: rows_before(rows, cut.start, cut.stop, keep, state_dim),
+            bc, rows_before(rows, at, at + state_dim, keep, state_dim),
+            taps_x, taps_bc, scale, emit,
         )
 
 
-def intra_kernel(
-    head_dim, x, got, bc, z, taps_x, taps_bc, dt_raw, a_log, d_skip, y_part, lead, c_act, wide
-):
-    dt, cum = rates(dt_raw[...], a_log[...], 0)
+def intra_kernel(count, _, *refs):
+    sources, refs = refs[:count], refs[count:]
+    x, bc, z, taps_x, taps_bc, dt_raw, a_log, d_skip, y_part, lead, c_act, wide = refs
     tokens, width = x.shape
     groups, both = bc.shape[1:]
     state_dim = both // 2
+    keep = taps_x.shape[0] - 1
     cols = width // groups
-    heads = dt.shape[0] // groups
+    heads = dt_raw.shape[0] // groups
+    head_dim = cols // heads
+    dt, cum = rates(dt_raw[...], a_log[...], 0)
     cum_t = cum.T
     leading = jnp.exp(cum)
-    skip = spread_row(as_column(d_skip[...], 0, dt.shape[0]), head_dim)
+    skip = spread_row(as_column(d_skip[...], 0, groups * heads), head_dim)
     t_at = lax.broadcasted_iota(jnp.int32, (tokens, tokens), 0)
     s_at = lax.broadcasted_iota(jnp.int32, (tokens, tokens), 1)
     pair = 2 * head_dim
+
+    def before(begin, stop):
+        found = [rows_before(rows, begin, stop, keep, state_dim) for rows in sources]
+        return sum(found[1:], found[0])
+
     for g in range(groups):
         at = width + g * both
-        bc_act = conv_act(
-            bc[...].astype(F32)[:, g], got[:, at : at + both].astype(F32), taps_bc[...][:, g]
+        tail_bc = jnp.concatenate(
+            [before(at, at + state_dim), before(at + state_dim, at + both)], axis=1
         )
+        bc_act = conv_act(bc[...].astype(F32)[:, g], tail_bc, taps_bc[...][:, g])
         b, c = bc_act[:, :state_dim], bc_act[:, state_dim:]
         c_act[:, g * state_dim : (g + 1) * state_dim] = c
         inner = lax.dot_general(c, b, (((1,), (1,)), ((), ())), preferred_element_type=F32)
         inner = jnp.where(t_at >= s_at, inner, 0.0)
         wide[...] = spread(leading[g * heads : (g + 1) * heads], head_dim, 2)
         for first in range(0, heads, 2):
-            here = first * head_dim
-            cut = slice(g * cols + here, g * cols + here + pair)
-            act = conv_act(x[:, cut].astype(F32), got[:, cut].astype(F32), taps_x[:, cut])
+            here = slice(first * head_dim, first * head_dim + pair)
+            cut = slice(g * cols + here.start, g * cols + here.stop)
+            act = conv_act(x[:, cut].astype(F32), before(cut.start, cut.stop), taps_x[:, cut])
             lane = lax.broadcasted_iota(jnp.int32, act.shape, 1)
             full = act.astype(F32)
             blocks = jnp.concatenate(
@@ -238,7 +248,7 @@
             y = jnp.dot(jnp.concatenate(weights, axis=1), blocks, preferred_element_type=F32)
             gate = silu(z[:, cut].astype(F32))
             y_part[:, cut] = (y + skip[:, cut] * full) * gate
-            lead[:, cut] = wide[:, here : here + pair] * gate
+            lead[:, cut] = wide[:, here] * gate
 
 
 def gated_slice(c, y_part, lead, arrived):
@@ -351,12 +361,16 @@
     def prepared(token):
         return pl.pallas_call(
             functools.partial(prepare_kernel, cuts),
-            out_shape=[jax.ShapeDtypeStruct((RIM, width + groups * both), BF16), scale_shape]
+            out_shape=[
+                jax.ShapeDtypeStruct((RIM, width + groups * both), BF16),
+                jax.ShapeDtypeStruct((1, width), F32),
+                scale_shape,
+            ]
             + [jax.ShapeDtypeStruct((1, high - low), F32) for _, low, high in cuts],
-            in_specs=[anywhere] + [in_vmem] * 4,
+            in_specs=[anywhere] + [in_vmem] * 5,
             compiler_params=params(16),
             name="prepared",
-        )(token, x_in, bc_in, dt_t, a_row)
+        )(token, x_in, bc_in, dt_t, a_row, gain)
 
     def later_states(condition, rows, token, scale, group, low, high):
         return pl.pallas_call(
@@ -368,53 +382,68 @@
         )(here(condition), rows, token, *sources, scale)
 
     along = [(i, i + 1) for i in range(devices - 1)]
+    def intra(token, befores):
+        return pl.pallas_call(
+            functools.partial(intra_kernel, len(befores)),
+            out_shape=[
+                scale_shape, scale_shape, jax.ShapeDtypeStruct((tokens, groups * state_dim), BF16)
+            ],
+            in_specs=[anywhere] + [in_vmem] * (len(befores) + 8),
+            scratch_shapes=[pltpu.VMEM((tokens, cols), F32)],
+            compiler_params=params(24),
+            cost_estimate=pl.CostEstimate(
+                flops=4 * tokens * tokens * width,
+                bytes_accessed=12 * tokens * width,
+                transcendentals=tokens * tokens * heads,
+            ),
+            name="intra",
+        )(token, *befores, x_in, bc_in, z_in, conv_x, conv_bc, dt_t, a_row, d_row)
+
+    part = None
     if devices <= CHAIN_MOST:
         first, scale = first_states(*cuts[0])
-        sent = [first]
-        for cut in cuts[1:]:
-            sent.append(next_states(sent[-1], scale, *cut))
-        last, scale, *decays = prepared(sent[-1])
-        got = shifted(last, along)
+        sent = [first, next_states(first, scale, *cuts[1])]
+        last, gain, scale_own, *decays = prepared(sent[-1])
+        token = last
+        for cut in cuts[2:]:
+            sent.append(next_states(token, scale, *cut))
+            token = sent[-1]
+        soon = along[1 : max(devices - 2, 1)]
+        late = along[max(devices - 2, 1) :]
+        befores = [shifted(last, soon)] if soon else []
         arrived = [[shifted(v, along[:1])] for v in sent]
+        befores.append(arrived[0][0])
         rows, token = arrived[0][0], last
         for hop in range(1, devices - 1):
-            condition = place == 1 if hop == 1 else place >= 2
+            runs = place == 1 if hop == 1 else (place >= 2) & (place < devices - 1)
             after = token
-            for i, (seen, cut) in enumerate(zip(arrived, cuts)):
+            for i, cut in enumerate(cuts):
                 if hop <= 2:
-                    made = later_states(condition, rows, after, scale, *cut)
+                    made = later_states(runs, rows, after, scale_own, *cut)
                     states = [made] if i == 0 else states + [made]
-                early = arrived[0][-1] if hop > 1 and i == len(cuts) - 1 else token
-                before, _, _ = lax.optimization_barrier((seen[-1], token, early))
+                early = ()
+                if hop == devices - 2 and hop > 1 and i == 1:
+                    part = intra(token, befores)
+                    early = (part[0],)
+                if hop == devices - 2 and hop > 1 and i == len(cuts) - 1:
+                    early = (arrived[0][-1],)
+                before, *_ = lax.optimization_barrier((arrived[i][-1], token) + early)
                 joined = decays[i] * before[:state_dim].astype(F32) + states[i]
                 token = joined.astype(BF16)
-                after = token if hop == 1 and i == 0 else after
-                seen.append(shifted(token, along[hop : hop + 1]))
-            rows = got
+                after = token if hop == 1 else after
+                arrived[i].append(shifted(token, along[hop : hop + 1]))
+            if hop == 1 and late:
+                moved, _ = lax.optimization_barrier((last, token))
+                befores.append(shifted(moved, late))
+            rows = befores[0]
     else:
-        last, scale, *decays = prepared(a_row)
-        got = shifted(last, along)
+        last, gain, scale, *decays = prepared(a_row)
+        befores = [shifted(last, along)]
         arrived = []
         for decay, cut in zip(decays, cuts):
-            state = later_states(place >= 0, got, a_row, scale, *cut)
+            state = later_states(place >= 0, befores[0], a_row, scale, *cut)
             arrived.append([doubling(state, decay, devices)])
-
-    y_part, lead, c_act = pl.pallas_call(
-        functools.partial(intra_kernel, head_dim),
-        out_shape=(
-            jax.ShapeDtypeStruct((tokens, width), F32),
-            jax.ShapeDtypeStruct((tokens, width), F32),
-            jax.ShapeDtypeStruct((tokens, groups * state_dim), BF16),
-        ),
-        scratch_shapes=[pltpu.VMEM((tokens, cols), F32)],
-        compiler_params=params(32),
-        cost_estimate=pl.CostEstimate(
-            flops=4 * tokens * tokens * width,
-            bytes_accessed=12 * tokens * width,
-            transcendentals=tokens * tokens * heads,
-        ),
-        name="intra",
-    )(x_in, got, bc_in, z_in, conv_x, conv_bc, dt_t, a_row, d_row)
+    y_part, lead, c_act = part or intra(a_row, befores)
 
     out = None
     for g in range(groups):

time: 30.7 us -> 30.8 us (level)
  Pallas kernels: 7.3 us -> 5.58 us
  waiting for transfers between devices: 9.94 us -> 11.1 us
  starting transfers between devices: 12.1 us -> 12.7 us
    pallas_call x8, Pallas kernels: 1.82 us -> 0.09 us  [later_states(): pl.pallas_call(functools.partial(later_kernel, group, low, high), out_sha...]
    ppermute x13 -> x14, waiting for transfers between devices: 9.94 us -> 11.1 us  [shifted(): return lax.ppermute(value, 'seq', route)]
    ppermute x13 -> x14, starting transfers between devices: 12.1 us -> 12.7 us  [shifted(): return lax.ppermute(value, 'seq', route)]
  transfers between devices with their start and end apart: 13 -> 14, of which waited for: 4 -> 3; matrix products, arithmetic and copies ran while one was open for 1% -> 1% of each run, Pallas kernels for 21% -> 15%
where the time goes in v9:
time: 30.8 us; the launch traced here: 30.4 us
  starting transfers between devices  12.7 us (41%)
  waiting for transfers between devices  11.1 us (36%)
  Pallas kernels  5.58 us (18%)
  between operations  0.45 us (1%)
  other arithmetic  0.37 us (1%)
    ppermute x14, starting transfers between devices, shifted(): return lax.ppermute(value, 'seq', route)  12.7 us
    ppermute x14, waiting for transfers between devices, shifted(): return lax.ppermute(value, 'seq', route)  11.1 us
    pallas_call x1, Pallas kernels, intra(): pl.pallas_call(functools.partial(intra_kernel, len(befores)), out_shape=[...  2.27 us
    pallas_call x2, Pallas kernels, shards(): pl.pallas_call(functools.partial(output_kernel, len(ready), len(arrived[0...  2.04 us
    pallas_call x1, Pallas kernels, prepared(): pl.pallas_call(functools.partial(prepare_kernel, cuts), out_shape=[jax.Sh...  0.71 us
  transfers between devices with their start and end apart: 14, of which 3 were waited for; matrix products, arithmetic and copies ran while one was open for 1% of the time, Pallas kernels for 15%

profile of v9, /device:TPU:30, one launch (start us, length us, event | category | flops | bytes accessed | tf_op | source)
XLA Modules:
  0.0 30.4 jit_solution(6951830615713491982)
XLA Ops:
  0.0 0.0 copy-start.3
  0.0 0.1 first_states.1
  0.1 0.8 %collective-permute-start = (bf16[160,384]{1,0:T(8,128)(2,1)S(1)}, bf16[160,384]{1,0:T(8,128)(2,1)S(1)}, u32[]{:S(2)}, u32[]{:S(2)}) collective-permute-start(bf16[160,384]{1,0:T(8,128)(2,1)S(1)} %get-tuple-element.26._), channel_id=1, source_target_pairs={{0,4},{1,5},{2,6},{3,7},{16,20},{17,21},{18,22},{19,23}} | collective-permute-start | bytes 368648 | tf_op jit(solution)/shard_map/ppermute | solution.py:338
  0.9 0.1 copy-done
  1.0 0.0 copy-done.1
  1.1 0.0 copy-done.2
  1.1 0.0 copy-done.3
  1.1 0.0 copy-start.7
  1.1 0.7 %collective-permute-start.4 = (bf16[128,640]{1,0:T(8,128)(2,1)S(1)}, bf16[128,640]{1,0:T(8,128)(2,1)S(1)}, u32[]{:S(2)}, u32[]{:S(2)}) collective-permute-start(bf16[128,640]{1,0:T(8,128)(2,1)S(1)} %next_states.3._), channel_id=1, source_target_pairs={{0,4},{1,5},{2,6},{3,7},{16,20},{17,21},{18,22},{19,23}} | collective-permute-start | bytes 491528 | tf_op jit(solution)/shard_map/ppermute | solution.py:338
  1.8 0.0 copy-done.5
  1.8 0.0 copy-done.6
  1.8 0.0 copy-done.7
  1.8 0.7 %prepared.1 = (bf16[8,2560]{1,0:T(8,128)(2,1)S(1)}, f32[1,2048]{1,0:T(1,128)S(1)}, f32[128,2048]{1,0:T(8,128)S(1)}, f32[1,384]{1,0:T(1,128)S(1)}, f32[1,640]{1,0...) custom-call(bf16[128,640]{1,0:T(8,128)(2,1)S(1)} %next_states.3._, bf16[128,2048]{1,0:T(8,128)(2,1)S(1)} %copy-done, ...), custom_call_target="tpu_custom_call" | custom-call | tf_op jit(solution)/shard_map/prepared/pallas_call | solution.py:362
  2.5 0.7 %collective-permute-start.5 = (bf16[8,2560]{1,0:T(8,128)(2,1)S(1)}, bf16[8,2560]{1,0:T(8,128)(2,1)S(1)}, u32[]{:S(2)}, u32[]{:S(2)}) collective-permute-start(bf16[8,2560]{1,0:T(8,128)(2,1)S(1)} %get-tuple-element.39._), channel_id=1, source_target_pairs={{4,8},{5,9},{6,10},{7,11},{20,24},{21,25},{22,26},{23,27}} | collective-permute-start | bytes 122888 | tf_op jit(solution)/shard_map/ppermute | solution.py:338
  3.2 0.7 %collective-permute-start.3 = (bf16[128,512]{1,0:T(8,128)(2,1)S(1)}, bf16[128,512]{1,0:T(8,128)(2,1)S(1)}, u32[]{:S(2)}, u32[]{:S(2)}) collective-permute-start(bf16[128,512]{1,0:T(8,128)(2,1)S(1)} %next_states.4._), channel_id=1, source_target_pairs={{0,4},{1,5},{2,6},{3,7},{16,20},{17,21},{18,22},{19,23}} | collective-permute-start | bytes 393224 | tf_op jit(solution)/shard_map/ppermute | solution.py:338
  3.9 0.7 %collective-permute-start.2 = (bf16[128,512]{1,0:T(8,128)(2,1)S(1)}, bf16[128,512]{1,0:T(8,128)(2,1)S(1)}, u32[]{:S(2)}, u32[]{:S(2)}) collective-permute-start(bf16[128,512]{1,0:T(8,128)(2,1)S(1)} %next_states.5), channel_id=1, source_target_pairs={{0,4},{1,5},{2,6},{3,7},{16,20},{17,21},{18,22},{19,23}} | collective-permute-start | bytes 393224 | tf_op jit(solution)/shard_map/ppermute | solution.py:338
  4.6 0.0 collective-permute-done.rows.refs_1_.refs_0_
  4.7 0.7 %collective-permute-start.1 = (bf16[128,384]{1,0:T(8,128)(2,1)S(1)}, bf16[128,384]{1,0:T(8,128)(2,1)S(1)}, u32[]{:S(2)}, u32[]{:S(2)}) collective-permute-start(bf16[128,384]{1,0:T(8,128)(2,1)S(1)} %add_convert_fusion.7._), channel_id=1, source_target_pairs={{4,8},{5,9},{6,10},{7,11},{20,24},{21,25},{22,26},{23,27}} | collective-permute-start | bytes 294920 | tf_op jit(solution)/shard_map/ppermute | solution.py:338
  5.4 0.0 collective-permute-done.4.refs_1_
  5.4 0.1 add_convert_fusion.1._
  5.5 0.7 %collective-permute-start.8 = (bf16[128,640]{1,0:T(8,128)(2,1)S(1)}, bf16[128,640]{1,0:T(8,128)(2,1)S(1)}, u32[]{:S(2)}, u32[]{:S(2)}) collective-permute-start(bf16[128,640]{1,0:T(8,128)(2,1)S(1)} %add_convert_fusion.1._), channel_id=1, source_target_pairs={{4,8},{5,9},{6,10},{7,11},{20,24},{21,25},{22,26},{23,27}} | collective-permute-start | bytes 491528 | tf_op jit(solution)/shard_map/ppermute | solution.py:338
  6.2 0.0 collective-permute-done.3.refs_0_
  6.2 0.7 %collective-permute-start.7 = (bf16[128,512]{1,0:T(8,128)(2,1)S(1)}, bf16[128,512]{1,0:T(8,128)(2,1)S(1)}, u32[]{:S(2)}, u32[]{:S(2)}) collective-permute-start(bf16[128,512]{1,0:T(8,128)(2,1)S(1)} %add_convert_fusion.5._), channel_id=1, source_target_pairs={{4,8},{5,9},{6,10},{7,11},{20,24},{21,25},{22,26},{23,27}} | collective-permute-start | bytes 393224 | tf_op jit(solution)/shard_map/ppermute | solution.py:338
  6.9 0.0 collective-permute-done.2.refs_1_
  7.0 0.7 %collective-permute-start.10 = (bf16[128,512]{1,0:T(8,128)(2,1)S(1)}, bf16[128,512]{1,0:T(8,128)(2,1)S(1)}, u32[]{:S(2)}, u32[]{:S(2)}) collective-permute-start(bf16[128,512]{1,0:T(8,128)(2,1)S(1)} %add_convert_fusion.4._), channel_id=1, source_target_pairs={{4,8},{5,9},{6,10},{7,11},{20,24},{21,25},{22,26},{23,27}} | collective-permute-start | bytes 393224 | tf_op jit(solution)/shard_map/ppermute | solution.py:338
  7.7 0.0 collective-permute-done.5.rows.refs_0_
  7.7 1.3 %collective-permute-start.6 = (bf16[8,2560]{1,0:T(8,128)(2,1)S(1)}, bf16[8,2560]{1,0:T(8,128)(2,1)S(1)}, u32[]{:S(2)}, u32[]{:S(2)}) collective-permute-start(bf16[8,2560]{1,0:T(8,128)(2,1)S(1)} %get-tuple-element.39._), channel_id=1, source_target_pairs={{8,12},{9,13},{10,14},{11,15},{24,28},{25,29},{26,30},{27,31}} | collective-permute-start | bytes 122888 | tf_op jit(solution)/shard_map/ppermute | solution.py:338
  9.0 0.0 copy-start.4
  9.1 0.0 collective-permute-done.1.refs_1_
  9.1 0.0 copy-start.8
  9.1 1.4 %collective-permute-start.11 = (bf16[128,384]{1,0:T(8,128)(2,1)S(1)}, bf16[128,384]{1,0:T(8,128)(2,1)S(1)}, u32[]{:S(2)}, u32[]{:S(2)}) collective-permute-start(bf16[128,384]{1,0:T(8,128)(2,1)S(1)} %add_convert_fusion.6._), channel_id=1, source_target_pairs={{8,12},{9,13},{10,14},{11,15},{24,28},{25,29},{26,30},{27,31}} | collective-permute-start | bytes 294920 | tf_op jit(solution)/shard_map/ppermute | solution.py:338
  10.6 4.0 %collective-permute-done.6.refs_2_ = bf16[8,2560]{1,0:T(8,128)(2,1)S(1)} collective-permute-done((bf16[8,2560]{1,0:T(8,128)(2,1)S(1)}, bf16[8,2560]{1,0:T(8,128)(2,1)S(1)}, u32[]{:S(2)}, u32[]{:S(2)}) %collective-permute-start.6) | collective-permute-done | bytes 40992 | tf_op jit(solution)/shard_map/ppermute | solution.py:338
  14.5 2.3 %intra.1 = (f32[128,2048]{1,0:T(8,128)S(1)}, f32[128,2048]{1,0:T(8,128)S(1)}, bf16[128,256]{1,0:T(8,128)(2,1)S(1)}) custom-call(bf16[128,384]{1,0:T(8,128)(2,1)S(1)} %add_convert_fusion.6._, bf16[8,2560]{1,0:T(8,128)(2,1)S(1)} %collective-permute-done.5.rows.refs_0_, bf16[160,384]{1,0:T(8,128)(2,1)S(1)} %collective-permute-done.rows.refs_1_.refs_0_, ...), custom_call_target="tpu_custom_call" | custom-call | flops 134217728 | bytes 3145728 | tf_op jit(solution)/shard_map/intra/pallas_call | solution.py:386
  16.8 0.0 collective-permute-done.8.refs_2_
  16.8 0.1 add_convert_fusion
  16.9 1.3 %collective-permute-start.13 = (bf16[128,640]{1,0:T(8,128)(2,1)S(1)}, bf16[128,640]{1,0:T(8,128)(2,1)S(1)}, u32[]{:S(2)}, u32[]{:S(2)}) collective-permute-start(bf16[128,640]{1,0:T(8,128)(2,1)S(1)} %add_convert_fusion), channel_id=1, source_target_pairs={{8,12},{9,13},{10,14},{11,15},{24,28},{25,29},{26,30},{27,31}} | collective-permute-start | bytes 491528 | tf_op jit(solution)/shard_map/ppermute | solution.py:338
  18.2 0.0 collective-permute-done.7.refs_1_
  18.2 1.3 %collective-permute-start.9 = (bf16[128,512]{1,0:T(8,128)(2,1)S(1)}, bf16[128,512]{1,0:T(8,128)(2,1)S(1)}, u32[]{:S(2)}, u32[]{:S(2)}) collective-permute-start(bf16[128,512]{1,0:T(8,128)(2,1)S(1)} %add_convert_fusion.3), channel_id=1, source_target_pairs={{8,12},{9,13},{10,14},{11,15},{24,28},{25,29},{26,30},{27,31}} | collective-permute-start | bytes 393224 | tf_op jit(solution)/shard_map/ppermute | solution.py:338
  19.5 0.0 collective-permute-done.10.refs_2_
  19.5 0.0 collective-permute-done.11.refs_2_
  19.6 1.3 %collective-permute-start.12 = (bf16[128,512]{1,0:T(8,128)(2,1)S(1)}, bf16[128,512]{1,0:T(8,128)(2,1)S(1)}, u32[]{:S(2)}, u32[]{:S(2)}) collective-permute-start(bf16[128,512]{1,0:T(8,128)(2,1)S(1)} %add_convert_fusion.2), channel_id=1, source_target_pairs={{8,12},{9,13},{10,14},{11,15},{24,28},{25,29},{26,30},{27,31}} | collective-permute-start | bytes 393224 | tf_op jit(solution)/shard_map/ppermute | solution.py:338
  20.9 0.2 gated.3.refs_0_
  21.1 6.9 %collective-permute-done.9.refs_2_ = bf16[128,512]{1,0:T(8,128)(2,1)S(1)} collective-permute-done((bf16[128,512]{1,0:T(8,128)(2,1)S(1)}, bf16[128,512]{1,0:T(8,128)(2,1)S(1)}, u32[]{:S(2)}, u32[]{:S(2)}) %collective-permute-start.9) | collective-permute-done | bytes 131104 | tf_op jit(solution)/shard_map/ppermute | solution.py:338
  28.0 0.2 gated.2.refs_0_
  28.2 0.0 collective-permute-done.13.refs_3_
  28.2 1.0 %outputs.2.refs_4_ = bf16[128,2048]{1,0:T(8,128)(2,1)} custom-call(bf16[128,256]{1,0:T(8,128)(2,1)S(1)} %get-tuple-element.40.c, f32[128,2048]{1,0:T(8,128)S(1)} %get-tuple-element.41.y_part, f32[128,2048]{1,0:T(8,128)S(1)} %get-tuple-element.42.lead, f32[1,2048]{1,0:T(1,128)S(1)} %get-tuple-element.43.gain, f32[128,384]{1,0:T(8,128)S(1)} %gated.3.refs_0_, ...), custom_call_target="tpu_custom_call" | custom-call | tf_op jit(solution)/shard_map/outputs/pallas_call | solution.py:475
  29.3 0.2 collective-permute-done.12.refs_3_
  29.4 1.0 %outputs.3 = bf16[128,2048]{1,0:T(8,128)(2,1)} custom-call(bf16[128,256]{1,0:T(8,128)(2,1)S(1)} %get-tuple-element.40.c, f32[128,2048]{1,0:T(8,128)S(1)} %get-tuple-element.41.y_part, f32[128,2048]{1,0:T(8,128)S(1)} %get-tuple-element.42.lead, f32[1,2048]{1,0:T(1,128)S(1)} %get-tuple-element.43.gain, ...), custom_call_target="tpu_custom_call", output_to_operand_aliasing={{}: (8, {})} | custom-call | tf_op jit(solution)/shard_map/outputs/pallas_call | solution.py:475
  (26 shorter events, 0.4 us)
Async XLA Ops:
  0.0 1.0 %copy-start = (bf16[128,2048]{1,0:T(8,128)(2,1)S(1)}, bf16[128,2048]{1,0:T(8,128)(2,1)}, u32[]{:S(2)}) copy-start(bf16[128,2048]{1,0:T(8,128)(2,1)} %x.23) | copy-start | bytes 1572868
  0.0 1.1 %copy-start.1 = (bf16[128,2,256]{2,1,0:T(2,128)(2,1)S(1)}, bf16[128,2,256]{2,1,0:T(2,128)(2,1)}, u32[]{:S(2)}) copy-start(bf16[128,2,256]{2,1,0:T(2,128)(2,1)} %bc.23) | copy-start | bytes 393220
  0.0 1.1 %copy-start.2 = (f32[4,2048]{1,0:T(4,128)S(1)}, f32[4,2048]{1,0:T(4,128)}, u32[]{:S(2)}) copy-start(f32[4,2048]{1,0:T(4,128)} %taps_x.21) | copy-start | bytes 98308
  0.0 1.1 %copy-start.3 = (f32[4,2,256]{2,1,0:T(2,128)S(1)}, f32[4,2,256]{2,1,0:T(2,128)}, u32[]{:S(2)}) copy-start(f32[4,2,256]{2,1,0:T(2,128)} %taps_bc.21) | copy-start | bytes 24580
  0.1 4.6 %collective-permute-start = (bf16[160,384]{1,0:T(8,128)(2,1)S(1)}, bf16[160,384]{1,0:T(8,128)(2,1)S(1)}, u32[]{:S(2)}, u32[]{:S(2)}) collective-permute-start(bf16[160,384]{1,0:T(8,128)(2,1)S(1)} %get-tuple-element.26._), channel_id=1, source_target_pairs={{0,4},{1,5},{2,6},{3,7},{16,20},{17,21},{18,22},{19,23}} | collective-permute-start | bytes 368648 | tf_op jit(solution)/shard_map/ppermute | solution.py:338
  1.1 0.7 %copy-start.5 = (f32[128,32]{0,1:T(8,128)S(1)}, f32[128,32]{0,1:T(8,128)}, u32[]{:S(2)}) copy-start(f32[128,32]{0,1:T(8,128)} %param.12) | copy-start | bytes 49156
  1.1 0.7 %copy-start.6 = (f32[2048]{0:T(1024)S(1)}, f32[2048]{0:T(1024)}, u32[]{:S(2)}) copy-start(f32[2048]{0:T(1024)} %param.17) | copy-start | bytes 24580
  1.1 0.7 %copy-start.7 = (f32[32]{0:T(128)S(1)}, f32[32]{0:T(128)}, u32[]{:S(2)}) copy-start(f32[32]{0:T(128)} %param.15) | copy-start | bytes 388
  1.1 4.3 %collective-permute-start.4 = (bf16[128,640]{1,0:T(8,128)(2,1)S(1)}, bf16[128,640]{1,0:T(8,128)(2,1)S(1)}, u32[]{:S(2)}, u32[]{:S(2)}) collective-permute-start(bf16[128,640]{1,0:T(8,128)(2,1)S(1)} %next_states.3._), channel_id=1, source_target_pairs={{0,4},{1,5},{2,6},{3,7},{16,20},{17,21},{18,22},{19,23}} | collective-permute-start | bytes 491528 | tf_op jit(solution)/shard_map/ppermute | solution.py:338
  2.5 5.1 %collective-permute-start.5 = (bf16[8,2560]{1,0:T(8,128)(2,1)S(1)}, bf16[8,2560]{1,0:T(8,128)(2,1)S(1)}, u32[]{:S(2)}, u32[]{:S(2)}) collective-permute-start(bf16[8,2560]{1,0:T(8,128)(2,1)S(1)} %get-tuple-element.39._), channel_id=1, source_target_pairs={{4,8},{5,9},{6,10},{7,11},{20,24},{21,25},{22,26},{23,27}} | collective-permute-start | bytes 122888 | tf_op jit(solution)/shard_map/ppermute | solution.py:338
  3.2 2.9 %collective-permute-start.3 = (bf16[128,512]{1,0:T(8,128)(2,1)S(1)}, bf16[128,512]{1,0:T(8,128)(2,1)S(1)}, u32[]{:S(2)}, u32[]{:S(2)}) collective-permute-start(bf16[128,512]{1,0:T(8,128)(2,1)S(1)} %next_states.4._), channel_id=1, source_target_pairs={{0,4},{1,5},{2,6},{3,7},{16,20},{17,21},{18,22},{19,23}} | collective-permute-start | bytes 393224 | tf_op jit(solution)/shard_map/ppermute | solution.py:338
  3.9 3.0 %collective-permute-start.2 = (bf16[128,512]{1,0:T(8,128)(2,1)S(1)}, bf16[128,512]{1,0:T(8,128)(2,1)S(1)}, u32[]{:S(2)}, u32[]{:S(2)}) collective-permute-start(bf16[128,512]{1,0:T(8,128)(2,1)S(1)} %next_states.5), channel_id=1, source_target_pairs={{0,4},{1,5},{2,6},{3,7},{16,20},{17,21},{18,22},{19,23}} | collective-permute-start | bytes 393224 | tf_op jit(solution)/shard_map/ppermute | solution.py:338
  4.7 4.3 %collective-permute-start.1 = (bf16[128,384]{1,0:T(8,128)(2,1)S(1)}, bf16[128,384]{1,0:T(8,128)(2,1)S(1)}, u32[]{:S(2)}, u32[]{:S(2)}) collective-permute-start(bf16[128,384]{1,0:T(8,128)(2,1)S(1)} %add_convert_fusion.7._), channel_id=1, source_target_pairs={{4,8},{5,9},{6,10},{7,11},{20,24},{21,25},{22,26},{23,27}} | collective-permute-start | bytes 294920 | tf_op jit(solution)/shard_map/ppermute | solution.py:338
  5.5 11.3 %collective-permute-start.8 = (bf16[128,640]{1,0:T(8,128)(2,1)S(1)}, bf16[128,640]{1,0:T(8,128)(2,1)S(1)}, u32[]{:S(2)}, u32[]{:S(2)}) collective-permute-start(bf16[128,640]{1,0:T(8,128)(2,1)S(1)} %add_convert_fusion.1._), channel_id=1, source_target_pairs={{4,8},{5,9},{6,10},{7,11},{20,24},{21,25},{22,26},{23,27}} | collective-permute-start | bytes 491528 | tf_op jit(solution)/shard_map/ppermute | solution.py:338
  6.2 11.9 %collective-permute-start.7 = (bf16[128,512]{1,0:T(8,128)(2,1)S(1)}, bf16[128,512]{1,0:T(8,128)(2,1)S(1)}, u32[]{:S(2)}, u32[]{:S(2)}) collective-permute-start(bf16[128,512]{1,0:T(8,128)(2,1)S(1)} %add_convert_fusion.5._), channel_id=1, source_target_pairs={{4,8},{5,9},{6,10},{7,11},{20,24},{21,25},{22,26},{23,27}} | collective-permute-start | bytes 393224 | tf_op jit(solution)/shard_map/ppermute | solution.py:338
  7.0 12.5 %collective-permute-start.10 = (bf16[128,512]{1,0:T(8,128)(2,1)S(1)}, bf16[128,512]{1,0:T(8,128)(2,1)S(1)}, u32[]{:S(2)}, u32[]{:S(2)}) collective-permute-start(bf16[128,512]{1,0:T(8,128)(2,1)S(1)} %add_convert_fusion.4._), channel_id=1, source_target_pairs={{4,8},{5,9},{6,10},{7,11},{20,24},{21,25},{22,26},{23,27}} | collective-permute-start | bytes 393224 | tf_op jit(solution)/shard_map/ppermute | solution.py:338
  7.7 6.8 %collective-permute-start.6 = (bf16[8,2560]{1,0:T(8,128)(2,1)S(1)}, bf16[8,2560]{1,0:T(8,128)(2,1)S(1)}, u32[]{:S(2)}, u32[]{:S(2)}) collective-permute-start(bf16[8,2560]{1,0:T(8,128)(2,1)S(1)} %get-tuple-element.39._), channel_id=1, source_target_pairs={{8,12},{9,13},{10,14},{11,15},{24,28},{25,29},{26,30},{27,31}} | collective-permute-start | bytes 122888 | tf_op jit(solution)/shard_map/ppermute | solution.py:338
  9.0 5.5 %copy-start.4 = (bf16[128,2048]{1,0:T(8,128)(2,1)S(1)}, bf16[128,2048]{1,0:T(8,128)(2,1)}, u32[]{:S(2)}) copy-start(bf16[128,2048]{1,0:T(8,128)(2,1)} %refs_5_.1) | copy-start | bytes 1572868
  9.1 5.4 %copy-start.8 = (f32[32]{0:T(128)S(1)}, f32[32]{0:T(128)}, u32[]{:S(2)}) copy-start(f32[32]{0:T(128)} %param.16) | copy-start | bytes 388
  9.1 10.4 %collective-permute-start.11 = (bf16[128,384]{1,0:T(8,128)(2,1)S(1)}, bf16[128,384]{1,0:T(8,128)(2,1)S(1)}, u32[]{:S(2)}, u32[]{:S(2)}) collective-permute-start(bf16[128,384]{1,0:T(8,128)(2,1)S(1)} %add_convert_fusion.6._), channel_id=1, source_target_pairs={{8,12},{9,13},{10,14},{11,15},{24,28},{25,29},{26,30},{27,31}} | collective-permute-start | bytes 294920 | tf_op jit(solution)/shard_map/ppermute | solution.py:338
  16.9 11.4 %collective-permute-start.13 = (bf16[128,640]{1,0:T(8,128)(2,1)S(1)}, bf16[128,640]{1,0:T(8,128)(2,1)S(1)}, u32[]{:S(2)}, u32[]{:S(2)}) collective-permute-start(bf16[128,640]{1,0:T(8,128)(2,1)S(1)} %add_convert_fusion), channel_id=1, source_target_pairs={{8,12},{9,13},{10,14},{11,15},{24,28},{25,29},{26,30},{27,31}} | collective-permute-start | bytes 491528 | tf_op jit(solution)/shard_map/ppermute | solution.py:338
  18.2 9.8 %collective-permute-start.9 = (bf16[128,512]{1,0:T(8,128)(2,1)S(1)}, bf16[128,512]{1,0:T(8,128)(2,1)S(1)}, u32[]{:S(2)}, u32[]{:S(2)}) collective-permute-start(bf16[128,512]{1,0:T(8,128)(2,1)S(1)} %add_convert_fusion.3), channel_id=1, source_target_pairs={{8,12},{9,13},{10,14},{11,15},{24,28},{25,29},{26,30},{27,31}} | collective-permute-start | bytes 393224 | tf_op jit(solution)/shard_map/ppermute | solution.py:338
  19.6 9.8 %collective-permute-start.12 = (bf16[128,512]{1,0:T(8,128)(2,1)S(1)}, bf16[128,512]{1,0:T(8,128)(2,1)S(1)}, u32[]{:S(2)}, u32[]{:S(2)}) collective-permute-start(bf16[128,512]{1,0:T(8,128)(2,1)S(1)} %add_convert_fusion.2), channel_id=1, source_target_pairs={{8,12},{9,13},{10,14},{11,15},{24,28},{25,29},{26,30},{27,31}} | collective-permute-start | bytes 393224 | tf_op jit(solution)/shard_map/ppermute | solution.py:338

commit v10 on v9

--- a/solution.py
+++ b/solution.py
@@ -399,7 +399,6 @@
             name="intra",
         )(token, *befores, x_in, bc_in, z_in, conv_x, conv_bc, dt_t, a_row, d_row)
 
-    part = None
     if devices <= CHAIN_MOST:
         first, scale = first_states(*cuts[0])
         sent = [first, next_states(first, scale, *cuts[1])]
@@ -422,11 +421,8 @@
                     made = later_states(runs, rows, after, scale_own, *cut)
                     states = [made] if i == 0 else states + [made]
                 early = ()
-                if hop == devices - 2 and hop > 1 and i == 1:
-                    part = intra(token, befores)
-                    early = (part[0],)
                 if hop == devices - 2 and hop > 1 and i == len(cuts) - 1:
-                    early = (arrived[0][-1],)
+                    early = (arrived[0][-1], befores[-1])
                 before, *_ = lax.optimization_barrier((arrived[i][-1], token) + early)
                 joined = decays[i] * before[:state_dim].astype(F32) + states[i]
                 token = joined.astype(BF16)
@@ -443,7 +439,7 @@
         for decay, cut in zip(decays, cuts):
             state = later_states(place >= 0, befores[0], a_row, scale, *cut)
             arrived.append([doubling(state, decay, devices)])
-    y_part, lead, c_act = part or intra(a_row, befores)
+    y_part, lead, c_act = intra(a_row, befores)
 
     out = None
     for g in range(groups):

time: 30.8 us -> 30.1 us (0.977)
  waiting for transfers between devices: 11.1 us -> 10.4 us
    ppermute x14, waiting for transfers between devices: 11.1 us -> 10.4 us  [shifted(): return lax.ppermute(value, 'seq', route)]
  transfers between devices with their start and end apart: 14 -> 14, of which waited for: 3 -> 4; matrix products, arithmetic and copies ran while one was open for 1% -> 1% of each run, Pallas kernels for 15% -> 15%
where the time goes in v10:
time: 30.1 us; the launch traced here: 29.7 us
  starting transfers between devices  12.7 us (42%)
  waiting for transfers between devices  10.4 us (35%)
  Pallas kernels  5.58 us (19%)
  between operations  0.44 us (1%)
  other arithmetic  0.37 us (1%)
    ppermute x14, starting transfers between devices, shifted(): return lax.ppermute(value, 'seq', route)  12.7 us
    ppermute x14, waiting for transfers between devices, shifted(): return lax.ppermute(value, 'seq', route)  10.4 us
    pallas_call x1, Pallas kernels, intra(): pl.pallas_call(functools.partial(intra_kernel, len(befores)), out_shape=[...  2.28 us
    pallas_call x2, Pallas kernels, shards(): pl.pallas_call(functools.partial(output_kernel, len(ready), len(arrived[0...  2.04 us
    pallas_call x1, Pallas kernels, prepared(): pl.pallas_call(functools.partial(prepare_kernel, cuts), out_shape=[jax.Sh...  0.71 us
  transfers between devices with their start and end apart: 14, of which 4 were waited for; matrix products, arithmetic and copies ran while one was open for 1% of the time, Pallas kernels for 15%

profile of v10, /device:TPU:30, one launch (start us, length us, event | category | flops | bytes accessed | tf_op | source)
XLA Modules:
  0.0 29.7 jit_solution(13722854844085417885)
XLA Ops:
  0.0 0.0 copy-start.3
  0.0 0.1 first_states.1
  0.1 0.8 %collective-permute-start.1 = (bf16[160,384]{1,0:T(8,128)(2,1)S(1)}, bf16[160,384]{1,0:T(8,128)(2,1)S(1)}, u32[]{:S(2)}, u32[]{:S(2)}) collective-permute-start(bf16[160,384]{1,0:T(8,128)(2,1)S(1)} %get-tuple-element.26._), channel_id=1, source_target_pairs={{0,4},{1,5},{2,6},{3,7},{16,20},{17,21},{18,22},{19,23}} | collective-permute-start | bytes 368648 | tf_op jit(solution)/shard_map/ppermute | solution.py:338
  0.9 0.1 copy-done
  1.0 0.0 copy-done.1
  1.1 0.0 copy-done.2
  1.1 0.0 copy-done.3
  1.1 0.0 copy-start.7
  1.1 0.7 %collective-permute-start.4 = (bf16[128,640]{1,0:T(8,128)(2,1)S(1)}, bf16[128,640]{1,0:T(8,128)(2,1)S(1)}, u32[]{:S(2)}, u32[]{:S(2)}) collective-permute-start(bf16[128,640]{1,0:T(8,128)(2,1)S(1)} %next_states.3._), channel_id=1, source_target_pairs={{0,4},{1,5},{2,6},{3,7},{16,20},{17,21},{18,22},{19,23}} | collective-permute-start | bytes 491528 | tf_op jit(solution)/shard_map/ppermute | solution.py:338
  1.8 0.0 copy-done.5
  1.8 0.0 copy-done.6
  1.8 0.0 copy-done.7
  1.8 0.7 %prepared.1 = (bf16[8,2560]{1,0:T(8,128)(2,1)S(1)}, f32[1,2048]{1,0:T(1,128)S(1)}, f32[128,2048]{1,0:T(8,128)S(1)}, f32[1,384]{1,0:T(1,128)S(1)}, f32[1,640]{1,0...) custom-call(bf16[128,640]{1,0:T(8,128)(2,1)S(1)} %next_states.3._, bf16[128,2048]{1,0:T(8,128)(2,1)S(1)} %copy-done, ...), custom_call_target="tpu_custom_call" | custom-call | tf_op jit(solution)/shard_map/prepared/pallas_call | solution.py:362
  2.5 0.7 %collective-permute-start = (bf16[8,2560]{1,0:T(8,128)(2,1)S(1)}, bf16[8,2560]{1,0:T(8,128)(2,1)S(1)}, u32[]{:S(2)}, u32[]{:S(2)}) collective-permute-start(bf16[8,2560]{1,0:T(8,128)(2,1)S(1)} %get-tuple-element.38._), channel_id=1, source_target_pairs={{4,8},{5,9},{6,10},{7,11},{20,24},{21,25},{22,26},{23,27}} | collective-permute-start | bytes 122888 | tf_op jit(solution)/shard_map/ppermute | solution.py:338
  3.2 0.7 %collective-permute-start.3 = (bf16[128,512]{1,0:T(8,128)(2,1)S(1)}, bf16[128,512]{1,0:T(8,128)(2,1)S(1)}, u32[]{:S(2)}, u32[]{:S(2)}) collective-permute-start(bf16[128,512]{1,0:T(8,128)(2,1)S(1)} %next_states.4._), channel_id=1, source_target_pairs={{0,4},{1,5},{2,6},{3,7},{16,20},{17,21},{18,22},{19,23}} | collective-permute-start | bytes 393224 | tf_op jit(solution)/shard_map/ppermute | solution.py:338
  3.9 0.7 %collective-permute-start.2 = (bf16[128,512]{1,0:T(8,128)(2,1)S(1)}, bf16[128,512]{1,0:T(8,128)(2,1)S(1)}, u32[]{:S(2)}, u32[]{:S(2)}) collective-permute-start(bf16[128,512]{1,0:T(8,128)(2,1)S(1)} %next_states.5), channel_id=1, source_target_pairs={{0,4},{1,5},{2,6},{3,7},{16,20},{17,21},{18,22},{19,23}} | collective-permute-start | bytes 393224 | tf_op jit(solution)/shard_map/ppermute | solution.py:338
  4.6 0.0 collective-permute-done.1.rows.refs_1_.refs_0_
  4.7 0.7 %collective-permute-start.8 = (bf16[128,384]{1,0:T(8,128)(2,1)S(1)}, bf16[128,384]{1,0:T(8,128)(2,1)S(1)}, u32[]{:S(2)}, u32[]{:S(2)}) collective-permute-start(bf16[128,384]{1,0:T(8,128)(2,1)S(1)} %add_convert_fusion.7._), channel_id=1, source_target_pairs={{4,8},{5,9},{6,10},{7,11},{20,24},{21,25},{22,26},{23,27}} | collective-permute-start | bytes 294920 | tf_op jit(solution)/shard_map/ppermute | solution.py:338
  5.4 0.0 collective-permute-done.4.refs_1_
  5.4 0.1 add_convert_fusion.1._
  5.5 0.7 %collective-permute-start.7 = (bf16[128,640]{1,0:T(8,128)(2,1)S(1)}, bf16[128,640]{1,0:T(8,128)(2,1)S(1)}, u32[]{:S(2)}, u32[]{:S(2)}) collective-permute-start(bf16[128,640]{1,0:T(8,128)(2,1)S(1)} %add_convert_fusion.1._), channel_id=1, source_target_pairs={{4,8},{5,9},{6,10},{7,11},{20,24},{21,25},{22,26},{23,27}} | collective-permute-start | bytes 491528 | tf_op jit(solution)/shard_map/ppermute | solution.py:338
  6.2 0.0 collective-permute-done.3.refs_0_
  6.2 0.7 %collective-permute-start.6 = (bf16[128,512]{1,0:T(8,128)(2,1)S(1)}, bf16[128,512]{1,0:T(8,128)(2,1)S(1)}, u32[]{:S(2)}, u32[]{:S(2)}) collective-permute-start(bf16[128,512]{1,0:T(8,128)(2,1)S(1)} %add_convert_fusion.5._), channel_id=1, source_target_pairs={{4,8},{5,9},{6,10},{7,11},{20,24},{21,25},{22,26},{23,27}} | collective-permute-start | bytes 393224 | tf_op jit(solution)/shard_map/ppermute | solution.py:338
  6.9 0.0 collective-permute-done.2.refs_1_
  7.0 0.7 %collective-permute-start.10 = (bf16[128,512]{1,0:T(8,128)(2,1)S(1)}, bf16[128,512]{1,0:T(8,128)(2,1)S(1)}, u32[]{:S(2)}, u32[]{:S(2)}) collective-permute-start(bf16[128,512]{1,0:T(8,128)(2,1)S(1)} %add_convert_fusion.4._), channel_id=1, source_target_pairs={{4,8},{5,9},{6,10},{7,11},{20,24},{21,25},{22,26},{23,27}} | collective-permute-start | bytes 393224 | tf_op jit(solution)/shard_map/ppermute | solution.py:338
  7.7 0.0 collective-permute-done.refs_0_.rows
  7.7 1.3 %collective-permute-start.5 = (bf16[8,2560]{1,0:T(8,128)(2,1)S(1)}, bf16[8,2560]{1,0:T(8,128)(2,1)S(1)}, u32[]{:S(2)}, u32[]{:S(2)}) collective-permute-start(bf16[8,2560]{1,0:T(8,128)(2,1)S(1)} %get-tuple-element.38._), channel_id=1, source_target_pairs={{8,12},{9,13},{10,14},{11,15},{24,28},{25,29},{26,30},{27,31}} | collective-permute-start | bytes 122888 | tf_op jit(solution)/shard_map/ppermute | solution.py:338
  9.0 0.0 collective-permute-done.8.refs_1_
  9.1 1.3 %collective-permute-start.11 = (bf16[128,384]{1,0:T(8,128)(2,1)S(1)}, bf16[128,384]{1,0:T(8,128)(2,1)S(1)}, u32[]{:S(2)}, u32[]{:S(2)}) collective-permute-start(bf16[128,384]{1,0:T(8,128)(2,1)S(1)} %add_convert_fusion.6), channel_id=1, source_target_pairs={{8,12},{9,13},{10,14},{11,15},{24,28},{25,29},{26,30},{27,31}} | collective-permute-start | bytes 294920 | tf_op jit(solution)/shard_map/ppermute | solution.py:338
  10.4 0.0 collective-permute-done.7.refs_2_
  10.4 0.1 add_convert_fusion
  10.5 0.0 copy-start.4
  10.5 1.4 %collective-permute-start.13 = (bf16[128,640]{1,0:T(8,128)(2,1)S(1)}, bf16[128,640]{1,0:T(8,128)(2,1)S(1)}, u32[]{:S(2)}, u32[]{:S(2)}) collective-permute-start(bf16[128,640]{1,0:T(8,128)(2,1)S(1)} %add_convert_fusion), channel_id=1, source_target_pairs={{8,12},{9,13},{10,14},{11,15},{24,28},{25,29},{26,30},{27,31}} | collective-permute-start | bytes 491528 | tf_op jit(solution)/shard_map/ppermute | solution.py:338
  11.9 0.0 collective-permute-done.6.refs_1_
  12.0 1.3 %collective-permute-start.9 = (bf16[128,512]{1,0:T(8,128)(2,1)S(1)}, bf16[128,512]{1,0:T(8,128)(2,1)S(1)}, u32[]{:S(2)}, u32[]{:S(2)}) collective-permute-start(bf16[128,512]{1,0:T(8,128)(2,1)S(1)} %add_convert_fusion.3), channel_id=1, source_target_pairs={{8,12},{9,13},{10,14},{11,15},{24,28},{25,29},{26,30},{27,31}} | collective-permute-start | bytes 393224 | tf_op jit(solution)/shard_map/ppermute | solution.py:338
  13.3 1.2 %collective-permute-done.5.refs_2_ = bf16[8,2560]{1,0:T(8,128)(2,1)S(1)} collective-permute-done((bf16[8,2560]{1,0:T(8,128)(2,1)S(1)}, bf16[8,2560]{1,0:T(8,128)(2,1)S(1)}, u32[]{:S(2)}, u32[]{:S(2)}) %collective-permute-start.5) | collective-permute-done | bytes 40992 | tf_op jit(solution)/shard_map/ppermute | solution.py:338
  14.5 0.0 collective-permute-done.10.refs_2_
  14.5 3.9 %collective-permute-done.11.refs_2_ = bf16[128,384]{1,0:T(8,128)(2,1)S(1)} collective-permute-done((bf16[128,384]{1,0:T(8,128)(2,1)S(1)}, bf16[128,384]{1,0:T(8,128)(2,1)S(1)}, u32[]{:S(2)}, u32[]{:S(2)}) %collective-permute-start.11) | collective-permute-done | bytes 98336 | tf_op jit(solution)/shard_map/ppermute | solution.py:338
  18.5 0.0 copy-start.8
  18.5 1.3 %collective-permute-start.12 = (bf16[128,512]{1,0:T(8,128)(2,1)S(1)}, bf16[128,512]{1,0:T(8,128)(2,1)S(1)}, u32[]{:S(2)}, u32[]{:S(2)}) collective-permute-start(bf16[128,512]{1,0:T(8,128)(2,1)S(1)} %add_convert_fusion.2), channel_id=1, source_target_pairs={{8,12},{9,13},{10,14},{11,15},{24,28},{25,29},{26,30},{27,31}} | collective-permute-start | bytes 393224 | tf_op jit(solution)/shard_map/ppermute | solution.py:338
  19.8 2.3 %intra.1 = (f32[128,2048]{1,0:T(8,128)S(1)}, f32[128,2048]{1,0:T(8,128)S(1)}, bf16[128,256]{1,0:T(8,128)(2,1)S(1)}) custom-call(f32[1,32]{1,0:T(1,128)S(1)} %bitcast.19, bf16[8,2560]{1,0:T(8,128)(2,1)S(1)} %collective-permute-done.refs_0_.rows, bf16[160,384]{1,0:T(8,128)(2,1)S(1)} %collective-permute-done.1.rows.refs_1_.refs_0_, ...), custom_call_target="tpu_custom_call" | custom-call | flops 134217728 | bytes 3145728 | tf_op jit(solution)/shard_map/intra/pallas_call | solution.py:386
  22.1 0.2 gated.3.refs_0_
  22.3 5.0 %collective-permute-done.9.refs_2_ = bf16[128,512]{1,0:T(8,128)(2,1)S(1)} collective-permute-done((bf16[128,512]{1,0:T(8,128)(2,1)S(1)}, bf16[128,512]{1,0:T(8,128)(2,1)S(1)}, u32[]{:S(2)}, u32[]{:S(2)}) %collective-permute-start.9) | collective-permute-done | bytes 131104 | tf_op jit(solution)/shard_map/ppermute | solution.py:338
  27.3 0.2 gated.2.refs_0_
  27.5 0.0 collective-permute-done.13.refs_3_
  27.5 1.0 %outputs.2.refs_4_ = bf16[128,2048]{1,0:T(8,128)(2,1)} custom-call(bf16[128,256]{1,0:T(8,128)(2,1)S(1)} %get-tuple-element.39.c, f32[128,2048]{1,0:T(8,128)S(1)} %get-tuple-element.40.y_part, f32[128,2048]{1,0:T(8,128)S(1)} %get-tuple-element.41.lead, f32[1,2048]{1,0:T(1,128)S(1)} %get-tuple-element.42.gain, f32[128,384]{1,0:T(8,128)S(1)} %gated.3.refs_0_, ...), custom_call_target="tpu_custom_call" | custom-call | tf_op jit(solution)/shard_map/outputs/pallas_call | solution.py:471
  28.5 0.2 collective-permute-done.12.refs_3_
  28.7 1.0 %outputs.3 = bf16[128,2048]{1,0:T(8,128)(2,1)} custom-call(bf16[128,256]{1,0:T(8,128)(2,1)S(1)} %get-tuple-element.39.c, f32[128,2048]{1,0:T(8,128)S(1)} %get-tuple-element.40.y_part, f32[128,2048]{1,0:T(8,128)S(1)} %get-tuple-element.41.lead, f32[1,2048]{1,0:T(1,128)S(1)} %get-tuple-element.42.gain, ...), custom_call_target="tpu_custom_call", output_to_operand_aliasing={{}: (8, {})} | custom-call | tf_op jit(solution)/shard_map/outputs/pallas_call | solution.py:471
  (26 shorter events, 0.4 us)
Async XLA Ops:
  0.0 1.0 %copy-start = (bf16[128,2048]{1,0:T(8,128)(2,1)S(1)}, bf16[128,2048]{1,0:T(8,128)(2,1)}, u32[]{:S(2)}) copy-start(bf16[128,2048]{1,0:T(8,128)(2,1)} %x.23) | copy-start | bytes 1572868
  0.0 1.1 %copy-start.1 = (bf16[128,2,256]{2,1,0:T(2,128)(2,1)S(1)}, bf16[128,2,256]{2,1,0:T(2,128)(2,1)}, u32[]{:S(2)}) copy-start(bf16[128,2,256]{2,1,0:T(2,128)(2,1)} %bc.23) | copy-start | bytes 393220
  0.0 1.1 %copy-start.2 = (f32[4,2048]{1,0:T(4,128)S(1)}, f32[4,2048]{1,0:T(4,128)}, u32[]{:S(2)}) copy-start(f32[4,2048]{1,0:T(4,128)} %taps_x.21) | copy-start | bytes 98308
  0.0 1.1 %copy-start.3 = (f32[4,2,256]{2,1,0:T(2,128)S(1)}, f32[4,2,256]{2,1,0:T(2,128)}, u32[]{:S(2)}) copy-start(f32[4,2,256]{2,1,0:T(2,128)} %taps_bc.21) | copy-start | bytes 24580
  0.1 4.6 %collective-permute-start.1 = (bf16[160,384]{1,0:T(8,128)(2,1)S(1)}, bf16[160,384]{1,0:T(8,128)(2,1)S(1)}, u32[]{:S(2)}, u32[]{:S(2)}) collective-permute-start(bf16[160,384]{1,0:T(8,128)(2,1)S(1)} %get-tuple-element.26._), channel_id=1, source_target_pairs={{0,4},{1,5},{2,6},{3,7},{16,20},{17,21},{18,22},{19,23}} | collective-permute-start | bytes 368648 | tf_op jit(solution)/shard_map/ppermute | solution.py:338
  1.1 0.7 %copy-start.5 = (f32[128,32]{0,1:T(8,128)S(1)}, f32[128,32]{0,1:T(8,128)}, u32[]{:S(2)}) copy-start(f32[128,32]{0,1:T(8,128)} %param.12) | copy-start | bytes 49156
  1.1 0.7 %copy-start.6 = (f32[2048]{0:T(1024)S(1)}, f32[2048]{0:T(1024)}, u32[]{:S(2)}) copy-start(f32[2048]{0:T(1024)} %param.17) | copy-start | bytes 24580
  1.1 0.7 %copy-start.7 = (f32[32]{0:T(128)S(1)}, f32[32]{0:T(128)}, u32[]{:S(2)}) copy-start(f32[32]{0:T(128)} %param.15) | copy-start | bytes 388
  1.1 4.3 %collective-permute-start.4 = (bf16[128,640]{1,0:T(8,128)(2,1)S(1)}, bf16[128,640]{1,0:T(8,128)(2,1)S(1)}, u32[]{:S(2)}, u32[]{:S(2)}) collective-permute-start(bf16[128,640]{1,0:T(8,128)(2,1)S(1)} %next_states.3._), channel_id=1, source_target_pairs={{0,4},{1,5},{2,6},{3,7},{16,20},{17,21},{18,22},{19,23}} | collective-permute-start | bytes 491528 | tf_op jit(solution)/shard_map/ppermute | solution.py:338
  2.5 5.1 %collective-permute-start = (bf16[8,2560]{1,0:T(8,128)(2,1)S(1)}, bf16[8,2560]{1,0:T(8,128)(2,1)S(1)}, u32[]{:S(2)}, u32[]{:S(2)}) collective-permute-start(bf16[8,2560]{1,0:T(8,128)(2,1)S(1)} %get-tuple-element.38._), channel_id=1, source_target_pairs={{4,8},{5,9},{6,10},{7,11},{20,24},{21,25},{22,26},{23,27}} | collective-permute-start | bytes 122888 | tf_op jit(solution)/shard_map/ppermute | solution.py:338
  3.2 2.9 %collective-permute-start.3 = (bf16[128,512]{1,0:T(8,128)(2,1)S(1)}, bf16[128,512]{1,0:T(8,128)(2,1)S(1)}, u32[]{:S(2)}, u32[]{:S(2)}) collective-permute-start(bf16[128,512]{1,0:T(8,128)(2,1)S(1)} %next_states.4._), channel_id=1, source_target_pairs={{0,4},{1,5},{2,6},{3,7},{16,20},{17,21},{18,22},{19,23}} | collective-permute-start | bytes 393224 | tf_op jit(solution)/shard_map/ppermute | solution.py:338
  3.9 3.0 %collective-permute-start.2 = (bf16[128,512]{1,0:T(8,128)(2,1)S(1)}, bf16[128,512]{1,0:T(8,128)(2,1)S(1)}, u32[]{:S(2)}, u32[]{:S(2)}) collective-permute-start(bf16[128,512]{1,0:T(8,128)(2,1)S(1)} %next_states.5), channel_id=1, source_target_pairs={{0,4},{1,5},{2,6},{3,7},{16,20},{17,21},{18,22},{19,23}} | collective-permute-start | bytes 393224 | tf_op jit(solution)/shard_map/ppermute | solution.py:338
  4.7 4.3 %collective-permute-start.8 = (bf16[128,384]{1,0:T(8,128)(2,1)S(1)}, bf16[128,384]{1,0:T(8,128)(2,1)S(1)}, u32[]{:S(2)}, u32[]{:S(2)}) collective-permute-start(bf16[128,384]{1,0:T(8,128)(2,1)S(1)} %add_convert_fusion.7._), channel_id=1, source_target_pairs={{4,8},{5,9},{6,10},{7,11},{20,24},{21,25},{22,26},{23,27}} | collective-permute-start | bytes 294920 | tf_op jit(solution)/shard_map/ppermute | solution.py:338
  5.5 4.9 %collective-permute-start.7 = (bf16[128,640]{1,0:T(8,128)(2,1)S(1)}, bf16[128,640]{1,0:T(8,128)(2,1)S(1)}, u32[]{:S(2)}, u32[]{:S(2)}) collective-permute-start(bf16[128,640]{1,0:T(8,128)(2,1)S(1)} %add_convert_fusion.1._), channel_id=1, source_target_pairs={{4,8},{5,9},{6,10},{7,11},{20,24},{21,25},{22,26},{23,27}} | collective-permute-start | bytes 491528 | tf_op jit(solution)/shard_map/ppermute | solution.py:338
  6.2 5.7 %collective-permute-start.6 = (bf16[128,512]{1,0:T(8,128)(2,1)S(1)}, bf16[128,512]{1,0:T(8,128)(2,1)S(1)}, u32[]{:S(2)}, u32[]{:S(2)}) collective-permute-start(bf16[128,512]{1,0:T(8,128)(2,1)S(1)} %add_convert_fusion.5._), channel_id=1, source_target_pairs={{4,8},{5,9},{6,10},{7,11},{20,24},{21,25},{22,26},{23,27}} | collective-permute-start | bytes 393224 | tf_op jit(solution)/shard_map/ppermute | solution.py:338
  7.0 7.5 %collective-permute-start.10 = (bf16[128,512]{1,0:T(8,128)(2,1)S(1)}, bf16[128,512]{1,0:T(8,128)(2,1)S(1)}, u32[]{:S(2)}, u32[]{:S(2)}) collective-permute-start(bf16[128,512]{1,0:T(8,128)(2,1)S(1)} %add_convert_fusion.4._), channel_id=1, source_target_pairs={{4,8},{5,9},{6,10},{7,11},{20,24},{21,25},{22,26},{23,27}} | collective-permute-start | bytes 393224 | tf_op jit(solution)/shard_map/ppermute | solution.py:338
  7.7 6.8 %collective-permute-start.5 = (bf16[8,2560]{1,0:T(8,128)(2,1)S(1)}, bf16[8,2560]{1,0:T(8,128)(2,1)S(1)}, u32[]{:S(2)}, u32[]{:S(2)}) collective-permute-start(bf16[8,2560]{1,0:T(8,128)(2,1)S(1)} %get-tuple-element.38._), channel_id=1, source_target_pairs={{8,12},{9,13},{10,14},{11,15},{24,28},{25,29},{26,30},{27,31}} | collective-permute-start | bytes 122888 | tf_op jit(solution)/shard_map/ppermute | solution.py:338
  9.1 9.4 %collective-permute-start.11 = (bf16[128,384]{1,0:T(8,128)(2,1)S(1)}, bf16[128,384]{1,0:T(8,128)(2,1)S(1)}, u32[]{:S(2)}, u32[]{:S(2)}) collective-permute-start(bf16[128,384]{1,0:T(8,128)(2,1)S(1)} %add_convert_fusion.6), channel_id=1, source_target_pairs={{8,12},{9,13},{10,14},{11,15},{24,28},{25,29},{26,30},{27,31}} | collective-permute-start | bytes 294920 | tf_op jit(solution)/shard_map/ppermute | solution.py:338
  10.5 9.3 %copy-start.4 = (bf16[128,2048]{1,0:T(8,128)(2,1)S(1)}, bf16[128,2048]{1,0:T(8,128)(2,1)}, u32[]{:S(2)}) copy-start(bf16[128,2048]{1,0:T(8,128)(2,1)} %refs_5_.1) | copy-start | bytes 1572868
  10.5 17.0 %collective-permute-start.13 = (bf16[128,640]{1,0:T(8,128)(2,1)S(1)}, bf16[128,640]{1,0:T(8,128)(2,1)S(1)}, u32[]{:S(2)}, u32[]{:S(2)}) collective-permute-start(bf16[128,640]{1,0:T(8,128)(2,1)S(1)} %add_convert_fusion), channel_id=1, source_target_pairs={{8,12},{9,13},{10,14},{11,15},{24,28},{25,29},{26,30},{27,31}} | collective-permute-start | bytes 491528 | tf_op jit(solution)/shard_map/ppermute | solution.py:338
  12.0 15.3 %collective-permute-start.9 = (bf16[128,512]{1,0:T(8,128)(2,1)S(1)}, bf16[128,512]{1,0:T(8,128)(2,1)S(1)}, u32[]{:S(2)}, u32[]{:S(2)}) collective-permute-start(bf16[128,512]{1,0:T(8,128)(2,1)S(1)} %add_convert_fusion.3), channel_id=1, source_target_pairs={{8,12},{9,13},{10,14},{11,15},{24,28},{25,29},{26,30},{27,31}} | collective-permute-start | bytes 393224 | tf_op jit(solution)/shard_map/ppermute | solution.py:338
  18.5 1.3 %copy-start.8 = (f32[32]{0:T(128)S(1)}, f32[32]{0:T(128)}, u32[]{:S(2)}) copy-start(f32[32]{0:T(128)} %param.16) | copy-start | bytes 388
  18.5 10.2 %collective-permute-start.12 = (bf16[128,512]{1,0:T(8,128)(2,1)S(1)}, bf16[128,512]{1,0:T(8,128)(2,1)S(1)}, u32[]{:S(2)}, u32[]{:S(2)}) collective-permute-start(bf16[128,512]{1,0:T(8,128)(2,1)S(1)} %add_convert_fusion.2), channel_id=1, source_target_pairs={{8,12},{9,13},{10,14},{11,15},{24,28},{25,29},{26,30},{27,31}} | collective-permute-start | bytes 393224 | tf_op jit(solution)/shard_map/ppermute | solution.py:338

commit v11 on v10

--- a/solution.py
+++ b/solution.py
@@ -11,8 +11,7 @@
 F32 = jnp.float32
 BF16 = jnp.bfloat16
 CHAIN_MOST = 4
-FIRST_PARTS = (3, 5)
-OTHER_PARTS = (1, 1)
+PARTS = (3, 5, 4, 4)
 CHUNK = 128
 RIM = 8
 
@@ -75,45 +74,66 @@
     rate = -jnp.exp(as_column(a_log_row, start, heads)) * dt
     earlier = lax.broadcasted_iota(jnp.int32, (tokens, tokens), 0)
     later = lax.broadcasted_iota(jnp.int32, (tokens, tokens), 1)
-    upto = (earlier <= later).astype(F32)
-    cum = jnp.dot(rate, upto, precision=lax.Precision.HIGHEST, preferred_element_type=F32)
+    upto = (earlier <= later).astype(F32).astype(BF16)
+    cum = jnp.dot(
+        halves(rate, 3, 1), jnp.concatenate([upto] * 3, axis=0), preferred_element_type=F32
+    )
     return dt, cum
 
 
-def scales(head_dim, dt_raw, a_log, scale):
+def scales(groups, head_dim, dt_raw, a_log, scale):
     dt, cum = rates(dt_raw[...], a_log[...], 0)
     end = cum[:, -1:]
-    scale[...] = spread(jnp.exp(end - cum) * dt, head_dim, 2)
+    tail_decay = jnp.exp(end - cum) * dt
+    heads = dt.shape[0] // groups
+    for g in range(groups):
+        scale[:, g * heads * head_dim : (g + 1) * heads * head_dim] = spread(
+            tail_decay[g * heads : (g + 1) * heads], head_dim, 2
+        )
     return spread_row(jnp.exp(end), head_dim)
 
 
-def emit_states(group, low, high, x, tail_x, bc, tail_bc, taps_x, taps_bc, scale, emit):
-    state_dim = bc.shape[2] // 2
-    b = conv_act(
-        bc[:, :, :state_dim].astype(F32)[:, group], tail_bc, taps_bc[:, :, :state_dim][:, group]
-    )
-    b_t = b.astype(F32).T.astype(BF16)
-    for at in range(low, high, CHUNK):
-        cut = slice(at, at + CHUNK)
-        act = conv_act(x[:, cut].astype(F32), tail_x(cut), taps_x[:, cut])
-        scaled = (scale[:, cut] * act.astype(F32)).astype(BF16)
-        emit(slice(at - low, at - low + CHUNK), jnp.dot(b_t, scaled, preferred_element_type=F32))
-
-
-def head_rows(group, low, high, x, bc, taps_x, taps_bc, scale, out):
+def by_group(low, high, cols):
+    found = []
+    while low < high:
+        stop = min(high, (low // cols + 1) * cols)
+        found.append((low // cols, low, stop))
+        low = stop
+    return found
+
+
+def emit_states(low, high, x, tail_x, bc, tail_bc, taps_x, taps_bc, scale, emit):
+    groups, both = bc.shape[1:]
+    state_dim = both // 2
+    for group, begin, stop in by_group(low, high, x.shape[1] // groups):
+        b = conv_act(
+            bc[:, :, :state_dim].astype(F32)[:, group],
+            tail_bc(group),
+            taps_bc[:, :, :state_dim][:, group],
+        )
+        b_t = b.astype(F32).T.astype(BF16)
+        for at in range(begin, stop, CHUNK):
+            cut = slice(at, at + CHUNK)
+            act = conv_act(x[:, cut].astype(F32), tail_x(cut), taps_x[:, cut])
+            scaled = (scale[:, cut] * act.astype(F32)).astype(BF16)
+            here = slice(at - low, at - low + CHUNK)
+            emit(here, jnp.dot(b_t, scaled, preferred_element_type=F32))
+
+
+def head_rows(low, high, x, bc, taps_x, taps_bc, scale, out):
     state_dim = bc.shape[2] // 2
 
     def emit(here, total):
         out[:state_dim, here] = total.astype(BF16)
 
     emit_states(
-        group, low, high, x, lambda cut: jnp.zeros((RIM, CHUNK), F32),
-        bc, jnp.zeros((RIM, state_dim), F32), taps_x, taps_bc, scale, emit,
+        low, high, x, lambda cut: jnp.zeros((RIM, CHUNK), F32),
+        bc, lambda group: jnp.zeros((RIM, state_dim), F32), taps_x, taps_bc, scale, emit,
     )
 
 
 def first_kernel(
-    group, low, high, active, x_hbm, bc_hbm, taps_x_hbm, taps_bc_hbm, dt_hbm, a_hbm,
+    low, high, active, x_hbm, bc_hbm, taps_x_hbm, taps_bc_hbm, dt_hbm, a_hbm,
     out, scale, x, bc, taps_x, taps_bc, dt_raw, a_log, sems,
 ):
     tokens, width = x.shape
@@ -130,7 +150,7 @@
             copy.start()
         for copy in copies[:2]:
             copy.wait()
-        scales(width // dt_raw.shape[0], dt_raw, a_log, scale)
+        scales(groups, width // dt_raw.shape[0], dt_raw, a_log, scale)
         for copy in copies[2:]:
             copy.wait()
         state_dim, step = both // 2, high - low
@@ -149,13 +169,13 @@
             block = pltpu.roll(block, (keep * (k + 1) - RIM) % extra, 0)
             below = jnp.where((at >= keep * k) & (at < keep * (k + 1)), block, below)
         out[state_dim:, :] = below.astype(BF16)
-        head_rows(group, low, high, x, bc, taps_x, taps_bc, scale, out)
-
-
-def next_kernel(group, low, high, active, _, x, bc, taps_x, taps_bc, scale, out):
+        head_rows(low, high, x, bc, taps_x, taps_bc, scale, out)
+
+
+def next_kernel(low, high, active, _, x, bc, taps_x, taps_bc, scale, out):
     @pl.when(active[0] == 1)
     def _():
-        head_rows(group, low, high, x, bc, taps_x, taps_bc, scale, out)
+        head_rows(low, high, x, bc, taps_x, taps_bc, scale, out)
 
 
 def prepare_kernel(cuts, _, x, bc, dt_raw, a_log, gain, pack, gain_out, scale, *decays):
@@ -166,8 +186,8 @@
     for g in range(groups):
         pack[:, width + g * both : width + (g + 1) * both] = last_bc[:, g].astype(BF16)
     gain_out[...] = gain[...]
-    row = scales(width // dt_raw.shape[0], dt_raw, a_log, scale)
-    for decay, (_, low, high) in zip(decays, cuts):
+    row = scales(groups, width // dt_raw.shape[0], dt_raw, a_log, scale)
+    for decay, (low, high) in zip(decays, cuts):
         decay[...] = row[:, low:high]
 
 
@@ -179,21 +199,25 @@
     return pltpu.roll(below, (RIM - keep * (begin // step + 1)) % below.shape[0], 0)[:RIM]
 
 
-def later_kernel(group, low, high, active, rows, _, x, bc, taps_x, taps_bc, scale, state):
+def later_kernel(low, high, active, rows, _, x, bc, taps_x, taps_bc, scale, state):
     both = bc.shape[2]
     state_dim = both // 2
     keep = taps_x.shape[0] - 1
+
+    def before(begin, stop):
+        return rows_before(rows, begin, stop, keep, state_dim)
+
+    def tail_bc(group):
+        at = x.shape[1] + group * both
+        return before(at, at + state_dim)
 
     @pl.when(active[0] == 1)
     def _():
         def emit(here, total):
             state[:, here] = total
 
-        at = x.shape[1] + group * both
         emit_states(
-            group, low, high, x,
-            lambda cut: rows_before(rows, cut.start, cut.stop, keep, state_dim),
-            bc, rows_before(rows, at, at + state_dim, keep, state_dim),
+            low, high, x, lambda cut: before(cut.start, cut.stop), bc, tail_bc,
             taps_x, taps_bc, scale, emit,
         )
 
@@ -251,23 +275,58 @@
             lead[:, cut] = wide[:, here] * gate
 
 
-def gated_slice(c, y_part, lead, arrived):
-    state = arrived[0][: c.shape[1]]
-    for more in arrived[1:]:
-        state = state + more[...]
-    return y_part[...] + lead[...] * jnp.dot(c[...], state, preferred_element_type=F32)
-
-
-def gated_kernel(c, y_part, lead, *refs):
-    refs[-1][...] = gated_slice(c, y_part, lead, refs[:-1])
-
-
-def output_kernel(ready, seen, c, y_part, lead, gain, *refs):
-    gated = [v[...] for v in refs[:ready]]
-    gated.append(gated_slice(c, y_part, lead, refs[ready : ready + seen]))
-    gated = jnp.concatenate(gated, axis=1)
-    mean_sq = jnp.mean(gated * gated, axis=1, keepdims=True)
-    refs[-1][...] = (gated * lax.rsqrt(mean_sq + EPS) * gain[...]).astype(BF16)
+def gated_slice(low, which, c, y_part, lead, arrived):
+    tokens, width = y_part.shape
+    state_dim = arrived[-1].shape[0]
+    size = arrived[-1].shape[1]
+    state = jnp.zeros((state_dim, size), BF16)
+    for i, came in enumerate(arrived):
+        state = jnp.where(which[0] == i, came[...][:state_dim], state)
+    pieces = []
+    for group, begin, stop in by_group(low, low + size, width * state_dim // c.shape[1]):
+        from_state = jnp.dot(
+            c[:, group * state_dim : (group + 1) * state_dim],
+            state[:, begin - low : stop - low],
+            preferred_element_type=F32,
+        )
+        pieces.append(y_part[:, begin:stop] + lead[:, begin:stop] * from_state)
+    return pieces
+
+
+def gated_kernel(low, which, c, y_part, lead, *refs):
+    at = 0
+    for piece in gated_slice(low, which, c, y_part, lead, refs[:-1]):
+        refs[-1][:, at : at + piece.shape[1]] = piece
+        at += piece.shape[1]
+
+
+def output_kernel(begin, ready, low, which, c, y_part, lead, gain, *refs):
+    out, made, sems = refs[-3:]
+    tokens, cols = made.shape
+    pieces = [refs[i][:, a:b] for i, (a, b) in enumerate(ready)]
+    if low is not None:
+        arrived = refs[len(ready) : len(refs) - 3]
+        if begin > 0:
+            arrived = arrived[:-1]
+        pieces += gated_slice(low, which, c, y_part, lead, arrived)
+    total = jnp.zeros((tokens, 1), F32)
+    for piece in pieces:
+        total = total + jnp.sum(piece * piece, axis=1, keepdims=True)
+    factor = lax.rsqrt(total / cols + EPS)
+    copies = []
+    at = 0
+    for i, piece in enumerate(pieces):
+        span = slice(at, at + piece.shape[1])
+        made[:, span] = (piece * factor * gain[:, begin + at : begin + span.stop]).astype(BF16)
+        copies.append(
+            pltpu.make_async_copy(
+                made.at[:, span], out.at[:, pl.ds(begin + at, piece.shape[1])], sems.at[i]
+            )
+        )
+        copies[-1].start()
+        at = span.stop
+    for copy in copies:
+        copy.wait()
 
 
 def params(mib):
@@ -286,10 +345,6 @@
         decay = decay * moved(decay, distance)
         distance *= 2
     return total
-
-
-def seen_last(arrived, cuts, group):
-    return [seen for (g, _, _), seen in zip(cuts, arrived) if g == group][-1]
 
 
 def shards(x_in, bc_in, z_in, dt_raw, conv_x, conv_bc, a_log, d_skip, norm_gain):
@@ -301,11 +356,8 @@
     cols = width // groups
     devices = lax.axis_size("seq")
     place = lax.axis_index("seq")
-    cuts = []
-    for g in range(groups):
-        parts = FIRST_PARTS if g == 0 else OTHER_PARTS
-        edges = [g * cols + cols * sum(parts[:i]) // sum(parts) for i in range(len(parts) + 1)]
-        cuts += [(g, low, high) for low, high in zip(edges[:-1], edges[1:])]
+    edges = [width * sum(PARTS[:i]) // sum(PARTS) for i in range(len(PARTS) + 1)]
+    cuts = list(zip(edges[:-1], edges[1:]))
 
     taps = conv_x.shape[0]
     dt_t = dt_raw.T
@@ -322,26 +374,17 @@
     anywhere = pl.BlockSpec(memory_space=pl.ANY)
     in_hbm = [pl.BlockSpec(memory_space=pltpu.HBM)] * len(operands)
 
-    def column(height, wide, at):
-        return pl.BlockSpec((height, wide), lambda i: (0, at))
-
-    def slab(low, high):
-        return pl.BlockSpec((pl.Element(tokens), pl.Element(high - low)), lambda i: (0, low))
-
-    def whole(array):
-        return pl.BlockSpec(array.shape, lambda i: (0,) * len(array.shape))
-
     def here(condition):
         return condition.astype(jnp.int32).reshape(1)
 
     def shifted(value, route):
         return lax.ppermute(value, "seq", route)
 
-    def first_states(group, low, high):
+    def first_states(low, high):
         blocks = -(-(width + groups * both) // (high - low))
         extra = -(-(taps - 1) * blocks // (2 * RIM)) * 2 * RIM
         return pl.pallas_call(
-            functools.partial(first_kernel, group, low, high),
+            functools.partial(first_kernel, low, high),
             out_shape=[jax.ShapeDtypeStruct((state_dim + extra, high - low), BF16), scale_shape],
             in_specs=[scalar] + in_hbm,
             scratch_shapes=landed + [pltpu.SemaphoreType.DMA((len(operands),))],
@@ -349,9 +392,9 @@
             name="first_states",
         )(here(place == 0), *pinned)
 
-    def next_states(token, scale, group, low, high):
+    def next_states(token, scale, low, high):
         return pl.pallas_call(
-            functools.partial(next_kernel, group, low, high),
+            functools.partial(next_kernel, low, high),
             out_shape=jax.ShapeDtypeStruct((state_dim, high - low), BF16),
             in_specs=[scalar, anywhere] + [in_vmem] * (len(sources) + 1),
             compiler_params=params(16),
@@ -366,15 +409,15 @@
                 jax.ShapeDtypeStruct((1, width), F32),
                 scale_shape,
             ]
-            + [jax.ShapeDtypeStruct((1, high - low), F32) for _, low, high in cuts],
+            + [jax.ShapeDtypeStruct((1, high - low), F32) for low, high in cuts],
             in_specs=[anywhere] + [in_vmem] * 5,
             compiler_params=params(16),
             name="prepared",
         )(token, x_in, bc_in, dt_t, a_row, gain)
 
-    def later_states(condition, rows, token, scale, group, low, high):
+    def later_states(condition, rows, token, scale, low, high):
         return pl.pallas_call(
-            functools.partial(later_kernel, group, low, high),
+            functools.partial(later_kernel, low, high),
             out_shape=jax.ShapeDtypeStruct((state_dim, high - low), F32),
             in_specs=[scalar, in_vmem, anywhere] + [in_vmem] * (len(sources) + 1),
             compiler_params=params(16),
@@ -432,6 +475,7 @@
                 moved, _ = lax.optimization_barrier((last, token))
                 befores.append(shifted(moved, late))
             rows = befores[0]
+        which = place - 1
     else:
         last, gain, scale, *decays = prepared(a_row)
         befores = [shifted(last, along)]
@@ -439,45 +483,56 @@
         for decay, cut in zip(decays, cuts):
             state = later_states(place >= 0, befores[0], a_row, scale, *cut)
             arrived.append([doubling(state, decay, devices)])
+        which = jnp.zeros_like(place)
+    which = which.astype(jnp.int32).reshape(1)
     y_part, lead, c_act = intra(a_row, befores)
 
+    common = [which, c_act, y_part, lead]
+    common_specs = [scalar] + [in_vmem] * 3
+    last_low, last_high = cuts[-1]
+    ready = []
+    for (low, high), seen in zip(cuts[:-1], arrived):
+        ready.append(
+            pl.pallas_call(
+                functools.partial(gated_kernel, low),
+                out_shape=jax.ShapeDtypeStruct((tokens, high - low), F32),
+                in_specs=common_specs + [in_vmem] * len(seen),
+                compiler_params=params(16),
+                name="gated",
+            )(*common, *seen)
+        )
     out = None
     for g in range(groups):
-        ready = []
-        for (group, low, high), seen in zip(cuts, arrived):
-            if group != g:
-                continue
-            inputs = [c_act, y_part, lead]
-            specs = [column(tokens, state_dim, g)] + [slab(low, high)] * 2
-            if high < (g + 1) * cols:
-                ready.append(
-                    pl.pallas_call(
-                        gated_kernel,
-                        out_shape=jax.ShapeDtypeStruct((tokens, high - low), F32),
-                        in_specs=specs + [whole(v) for v in seen],
-                        out_specs=column(tokens, high - low, 0),
-                        grid=(1,),
-                        compiler_params=params(16),
-                        name="gated",
-                    )(*inputs, *seen)
-                )
-        inputs += [gain] + ready + seen_last(arrived, cuts, g)
-        specs += [column(1, cols, g)] + [whole(v) for v in ready + seen_last(arrived, cuts, g)]
+        begin, stop = g * cols, (g + 1) * cols
+        taken, spans = [], []
+        for (low, high), v in zip(cuts[:-1], ready):
+            if low < stop and high > begin:
+                taken.append(v)
+                spans.append((max(low, begin) - low, min(high, stop) - low))
+        inputs = taken
+        unready = None
+        if last_low < stop:
+            unready = last_low
+            inputs = taken + arrived[-1]
         aliases = {}
+        specs = common_specs + [in_vmem] * (1 + len(inputs))
         if out is not None:
-            aliases = {len(inputs): 0}
-            inputs.append(out)
-            specs.append(pl.BlockSpec(memory_space=pl.ANY))
+            aliases = {len(common) + 1 + len(inputs): 0}
+            inputs = inputs + [out]
+            specs = specs + [anywhere]
         out = pl.pallas_call(
-            functools.partial(output_kernel, len(ready), len(arrived[0])),
+            functools.partial(output_kernel, begin, spans, unready),
             out_shape=jax.ShapeDtypeStruct((tokens, width), BF16),
             in_specs=specs,
-            out_specs=column(tokens, cols, g),
-            grid=(1,),
+            out_specs=anywhere,
+            scratch_shapes=[
+                pltpu.VMEM((tokens, cols), BF16),
+                pltpu.SemaphoreType.DMA((len(cuts) + groups,)),
+            ],
             input_output_aliases=aliases,
-            compiler_params=params(32),
+            compiler_params=params(16),
             name="outputs",
-        )(*inputs)
+        )(*common, gain, *inputs)
     return out
 
 

time: 30.1 us -> 30 us (level)
  waiting for transfers between devices: 10.4 us -> 9.75 us
  local copies, waits for them, and re-layouts: 0.2 us -> 0.84 us
    unnamed x18, local copies, waits for them, and re-layouts: 0.2 us -> 0.84 us
    ppermute x14, waiting for transfers between devices: 10.4 us -> 9.75 us  [shifted(): return lax.ppermute(value, 'seq', route)]
    pallas_call x16 -> x17, Pallas kernels: 2.59 us -> 2.72 us  [the longest x2 1.96 us: shards(): pl.pallas_call(functools.partial(output_kernel, begin, spans, unready), o...]
where the time goes in v11:
time: 30 us; the launch traced here: 29.6 us
  starting transfers between devices  12.7 us (42%)
  waiting for transfers between devices  9.75 us (32%)
  Pallas kernels  5.5 us (18%)
  local copies, waits for them, and re-layouts  0.84 us (3%)
  between operations  0.45 us (2%)
  other arithmetic  0.37 us (1%)
    ppermute x14, starting transfers between devices, shifted(): return lax.ppermute(value, 'seq', route)  12.7 us
    ppermute x14, waiting for transfers between devices, shifted(): return lax.ppermute(value, 'seq', route)  9.75 us
    pallas_call x1, Pallas kernels, intra(): pl.pallas_call(functools.partial(intra_kernel, len(befores)), out_shape=[...  2.15 us
    pallas_call x2, Pallas kernels, shards(): pl.pallas_call(functools.partial(output_kernel, begin, spans, unready), o...  1.96 us
    unnamed x18, local copies, waits for them, and re-layouts  0.84 us
    pallas_call x1, Pallas kernels, prepared(): pl.pallas_call(functools.partial(prepare_kernel, cuts), out_shape=[jax.Sh...  0.62 us
  transfers between devices with their start and end apart: 14, of which 4 were waited for; matrix products, arithmetic and copies ran while one was open for 1% of the time, Pallas kernels for 15%

profile of v11, /device:TPU:30, one launch (start us, length us, event | category | flops | bytes accessed | tf_op | source)
XLA Modules:
  0.0 29.6 jit_solution(2628512943501197159)
XLA Ops:
  0.0 0.0 copy-start.3
  0.0 0.1 first_states.1
  0.1 0.8 %collective-permute-start.1 = (bf16[160,384]{1,0:T(8,128)(2,1)S(1)}, bf16[160,384]{1,0:T(8,128)(2,1)S(1)}, u32[]{:S(2)}, u32[]{:S(2)}) collective-permute-start(bf16[160,384]{1,0:T(8,128)(2,1)S(1)} %get-tuple-element.26._), channel_id=1, source_target_pairs={{0,4},{1,5},{2,6},{3,7},{16,20},{17,21},{18,22},{19,23}} | collective-permute-start | bytes 368648 | tf_op jit(solution)/shard_map/ppermute | solution.py:381
  0.9 0.1 copy-done
  1.0 0.0 copy-done.1
  1.1 0.0 copy-done.2
  1.1 0.0 copy-done.3
  1.1 0.0 copy-start.7
  1.1 0.7 %collective-permute-start.4 = (bf16[128,640]{1,0:T(8,128)(2,1)S(1)}, bf16[128,640]{1,0:T(8,128)(2,1)S(1)}, u32[]{:S(2)}, u32[]{:S(2)}) collective-permute-start(bf16[128,640]{1,0:T(8,128)(2,1)S(1)} %next_states.3._), channel_id=1, source_target_pairs={{0,4},{1,5},{2,6},{3,7},{16,20},{17,21},{18,22},{19,23}} | collective-permute-start | bytes 491528 | tf_op jit(solution)/shard_map/ppermute | solution.py:381
  1.8 0.0 copy-done.5
  1.8 0.6 %prepared.1 = (bf16[8,2560]{1,0:T(8,128)(2,1)S(1)}, f32[1,2048]{1,0:T(1,128)S(1)}, f32[128,2048]{1,0:T(8,128)S(1)}, f32[1,384]{1,0:T(1,128)S(1)}, f32[1,640]{1,0...) custom-call(bf16[128,640]{1,0:T(8,128)(2,1)S(1)} %next_states.3._, bf16[128,2048]{1,0:T(8,128)(2,1)S(1)} %copy-done, ...), custom_call_target="tpu_custom_call" | custom-call | tf_op jit(solution)/shard_map/prepared/pallas_call | solution.py:405
  2.4 0.7 %collective-permute-start = (bf16[8,2560]{1,0:T(8,128)(2,1)S(1)}, bf16[8,2560]{1,0:T(8,128)(2,1)S(1)}, u32[]{:S(2)}, u32[]{:S(2)}) collective-permute-start(bf16[8,2560]{1,0:T(8,128)(2,1)S(1)} %get-tuple-element.38._), channel_id=1, source_target_pairs={{4,8},{5,9},{6,10},{7,11},{20,24},{21,25},{22,26},{23,27}} | collective-permute-start | bytes 122888 | tf_op jit(solution)/shard_map/ppermute | solution.py:381
  3.1 0.7 %collective-permute-start.3 = (bf16[128,512]{1,0:T(8,128)(2,1)S(1)}, bf16[128,512]{1,0:T(8,128)(2,1)S(1)}, u32[]{:S(2)}, u32[]{:S(2)}) collective-permute-start(bf16[128,512]{1,0:T(8,128)(2,1)S(1)} %next_states.4._), channel_id=1, source_target_pairs={{0,4},{1,5},{2,6},{3,7},{16,20},{17,21},{18,22},{19,23}} | collective-permute-start | bytes 393224 | tf_op jit(solution)/shard_map/ppermute | solution.py:381
  3.8 0.7 %collective-permute-start.2 = (bf16[128,512]{1,0:T(8,128)(2,1)S(1)}, bf16[128,512]{1,0:T(8,128)(2,1)S(1)}, u32[]{:S(2)}, u32[]{:S(2)}) collective-permute-start(bf16[128,512]{1,0:T(8,128)(2,1)S(1)} %next_states.5), channel_id=1, source_target_pairs={{0,4},{1,5},{2,6},{3,7},{16,20},{17,21},{18,22},{19,23}} | collective-permute-start | bytes 393224 | tf_op jit(solution)/shard_map/ppermute | solution.py:381
  4.6 0.0 collective-permute-done.1.rows.refs_1_.refs_0_
  4.6 0.7 %collective-permute-start.8 = (bf16[128,384]{1,0:T(8,128)(2,1)S(1)}, bf16[128,384]{1,0:T(8,128)(2,1)S(1)}, u32[]{:S(2)}, u32[]{:S(2)}) collective-permute-start(bf16[128,384]{1,0:T(8,128)(2,1)S(1)} %add_convert_fusion.7._), channel_id=1, source_target_pairs={{4,8},{5,9},{6,10},{7,11},{20,24},{21,25},{22,26},{23,27}} | collective-permute-start | bytes 294920 | tf_op jit(solution)/shard_map/ppermute | solution.py:381
  5.3 0.0 collective-permute-done.4.refs_0_
  5.3 0.1 add_convert_fusion.1._
  5.4 0.7 %collective-permute-start.7 = (bf16[128,640]{1,0:T(8,128)(2,1)S(1)}, bf16[128,640]{1,0:T(8,128)(2,1)S(1)}, u32[]{:S(2)}, u32[]{:S(2)}) collective-permute-start(bf16[128,640]{1,0:T(8,128)(2,1)S(1)} %add_convert_fusion.1._), channel_id=1, source_target_pairs={{4,8},{5,9},{6,10},{7,11},{20,24},{21,25},{22,26},{23,27}} | collective-permute-start | bytes 491528 | tf_op jit(solution)/shard_map/ppermute | solution.py:381
  6.1 0.0 collective-permute-done.3.refs_0_
  6.1 0.7 %collective-permute-start.6 = (bf16[128,512]{1,0:T(8,128)(2,1)S(1)}, bf16[128,512]{1,0:T(8,128)(2,1)S(1)}, u32[]{:S(2)}, u32[]{:S(2)}) collective-permute-start(bf16[128,512]{1,0:T(8,128)(2,1)S(1)} %add_convert_fusion.5._), channel_id=1, source_target_pairs={{4,8},{5,9},{6,10},{7,11},{20,24},{21,25},{22,26},{23,27}} | collective-permute-start | bytes 393224 | tf_op jit(solution)/shard_map/ppermute | solution.py:381
  6.8 0.0 collective-permute-done.2.refs_1_
  6.9 0.7 %collective-permute-start.10 = (bf16[128,512]{1,0:T(8,128)(2,1)S(1)}, bf16[128,512]{1,0:T(8,128)(2,1)S(1)}, u32[]{:S(2)}, u32[]{:S(2)}) collective-permute-start(bf16[128,512]{1,0:T(8,128)(2,1)S(1)} %add_convert_fusion.4._), channel_id=1, source_target_pairs={{4,8},{5,9},{6,10},{7,11},{20,24},{21,25},{22,26},{23,27}} | collective-permute-start | bytes 393224 | tf_op jit(solution)/shard_map/ppermute | solution.py:381
  7.6 0.0 collective-permute-done.refs_0_.rows
  7.6 1.3 %collective-permute-start.5 = (bf16[8,2560]{1,0:T(8,128)(2,1)S(1)}, bf16[8,2560]{1,0:T(8,128)(2,1)S(1)}, u32[]{:S(2)}, u32[]{:S(2)}) collective-permute-start(bf16[8,2560]{1,0:T(8,128)(2,1)S(1)} %get-tuple-element.38._), channel_id=1, source_target_pairs={{8,12},{9,13},{10,14},{11,15},{24,28},{25,29},{26,30},{27,31}} | collective-permute-start | bytes 122888 | tf_op jit(solution)/shard_map/ppermute | solution.py:381
  9.0 0.0 collective-permute-done.8.refs_1_
  9.0 1.3 %collective-permute-start.11 = (bf16[128,384]{1,0:T(8,128)(2,1)S(1)}, bf16[128,384]{1,0:T(8,128)(2,1)S(1)}, u32[]{:S(2)}, u32[]{:S(2)}) collective-permute-start(bf16[128,384]{1,0:T(8,128)(2,1)S(1)} %add_convert_fusion.6), channel_id=1, source_target_pairs={{8,12},{9,13},{10,14},{11,15},{24,28},{25,29},{26,30},{27,31}} | collective-permute-start | bytes 294920 | tf_op jit(solution)/shard_map/ppermute | solution.py:381
  10.3 0.0 collective-permute-done.7.refs_1_
  10.3 0.1 add_convert_fusion
  10.4 0.0 copy-start.4
  10.4 1.4 %collective-permute-start.13 = (bf16[128,640]{1,0:T(8,128)(2,1)S(1)}, bf16[128,640]{1,0:T(8,128)(2,1)S(1)}, u32[]{:S(2)}, u32[]{:S(2)}) collective-permute-start(bf16[128,640]{1,0:T(8,128)(2,1)S(1)} %add_convert_fusion), channel_id=1, source_target_pairs={{8,12},{9,13},{10,14},{11,15},{24,28},{25,29},{26,30},{27,31}} | collective-permute-start | bytes 491528 | tf_op jit(solution)/shard_map/ppermute | solution.py:381
  11.8 0.0 collective-permute-done.6.refs_1_
  11.9 1.3 %collective-permute-start.9 = (bf16[128,512]{1,0:T(8,128)(2,1)S(1)}, bf16[128,512]{1,0:T(8,128)(2,1)S(1)}, u32[]{:S(2)}, u32[]{:S(2)}) collective-permute-start(bf16[128,512]{1,0:T(8,128)(2,1)S(1)} %add_convert_fusion.3), channel_id=1, source_target_pairs={{8,12},{9,13},{10,14},{11,15},{24,28},{25,29},{26,30},{27,31}} | collective-permute-start | bytes 393224 | tf_op jit(solution)/shard_map/ppermute | solution.py:381
  13.2 1.2 %collective-permute-done.5.refs_2_ = bf16[8,2560]{1,0:T(8,128)(2,1)S(1)} collective-permute-done((bf16[8,2560]{1,0:T(8,128)(2,1)S(1)}, bf16[8,2560]{1,0:T(8,128)(2,1)S(1)}, u32[]{:S(2)}, u32[]{:S(2)}) %collective-permute-start.5) | collective-permute-done | bytes 40992 | tf_op jit(solution)/shard_map/ppermute | solution.py:381
  14.4 0.0 collective-permute-done.10.refs_2_
  14.4 3.9 %collective-permute-done.11.refs_2_ = bf16[128,384]{1,0:T(8,128)(2,1)S(1)} collective-permute-done((bf16[128,384]{1,0:T(8,128)(2,1)S(1)}, bf16[128,384]{1,0:T(8,128)(2,1)S(1)}, u32[]{:S(2)}, u32[]{:S(2)}) %collective-permute-start.11) | collective-permute-done | bytes 98336 | tf_op jit(solution)/shard_map/ppermute | solution.py:381
  18.4 1.3 %collective-permute-start.12 = (bf16[128,512]{1,0:T(8,128)(2,1)S(1)}, bf16[128,512]{1,0:T(8,128)(2,1)S(1)}, u32[]{:S(2)}, u32[]{:S(2)}) collective-permute-start(bf16[128,512]{1,0:T(8,128)(2,1)S(1)} %add_convert_fusion.2), channel_id=1, source_target_pairs={{8,12},{9,13},{10,14},{11,15},{24,28},{25,29},{26,30},{27,31}} | collective-permute-start | bytes 393224 | tf_op jit(solution)/shard_map/ppermute | solution.py:381
  19.7 0.0 copy-start.8
  19.7 0.6 %copy-done.8 = f32[32]{0:T(128)S(1)} copy-done((f32[32]{0:T(128)S(1)}, f32[32]{0:T(128)}, u32[]{:S(2)}) %copy-start.8) | copy-done | bytes 152
  20.4 2.2 %intra.1 = (f32[128,2048]{1,0:T(8,128)S(1)}, f32[128,2048]{1,0:T(8,128)S(1)}, bf16[128,256]{1,0:T(8,128)(2,1)S(1)}) custom-call(f32[1,32]{1,0:T(1,128)S(1)} %bitcast.20, bf16[8,2560]{1,0:T(8,128)(2,1)S(1)} %collective-permute-done.refs_0_.rows, bf16[160,384]{1,0:T(8,128)(2,1)S(1)} %collective-permute-done.1.rows.refs_1_.refs_0_, ...), custom_call_target="tpu_custom_call" | custom-call | flops 134217728 | bytes 3145728 | tf_op jit(solution)/shard_map/intra/pallas_call | solution.py:429
  22.5 0.2 gated.4.refs_0_
  22.7 4.5 %collective-permute-done.9.refs_2_ = bf16[128,512]{1,0:T(8,128)(2,1)S(1)} collective-permute-done((bf16[128,512]{1,0:T(8,128)(2,1)S(1)}, bf16[128,512]{1,0:T(8,128)(2,1)S(1)}, u32[]{:S(2)}, u32[]{:S(2)}) %collective-permute-start.9) | collective-permute-done | bytes 131104 | tf_op jit(solution)/shard_map/ppermute | solution.py:381
  27.2 0.2 gated.3.refs_0_
  27.4 0.0 collective-permute-done.13.refs_2_
  27.4 0.2 gated.5.refs_1_
  27.6 0.9 %outputs.2.refs_4_ = bf16[128,2048]{1,0:T(8,128)(2,1)} custom-call(s32[1]{0:T(128)} %bitcast.which, bf16[128,256]{1,0:T(8,128)(2,1)S(1)} %get-tuple-element.39.c, f32[128,2048]{1,0:T(8,128)S(1)} %get-tuple-element.40.y_part, f32[128,2048]{1,0:T(8,128)S(1)} %get-tuple-element.41.lead, f32[1,2048]{1,0:T(1,128)S(1)} %get-tuple-element.42.gain, ...), custom_call_target="tpu_custom_call" | custom-call | tf_op jit(solution)/shard_map/outputs/pallas_call | solution.py:523
  28.5 0.1 collective-permute-done.12.refs_3_
  28.6 1.1 %outputs.3 = bf16[128,2048]{1,0:T(8,128)(2,1)} custom-call(s32[1]{0:T(128)} %bitcast.which, bf16[128,256]{1,0:T(8,128)(2,1)S(1)} %get-tuple-element.39.c, f32[128,2048]{1,0:T(8,128)S(1)} %get-tuple-element.40.y_part, f32[128,2048]{1,0:T(8,128)S(1)} %get-tuple-element.41.lead, f32[1,2048]{1,0:T(1,128)S(1)} %get-tuple-element.42.gain, ...), custom_call_target="tpu_custom_call", output_to_operand_aliasing={{}: (9, {})} | custom-call | tf_op jit(solution)/shard_map/outputs/pallas_call | solution.py:523
  (27 shorter events, 0.4 us)
Async XLA Ops:
  0.0 1.0 %copy-start = (bf16[128,2048]{1,0:T(8,128)(2,1)S(1)}, bf16[128,2048]{1,0:T(8,128)(2,1)}, u32[]{:S(2)}) copy-start(bf16[128,2048]{1,0:T(8,128)(2,1)} %x.23) | copy-start | bytes 1572868
  0.0 1.1 %copy-start.1 = (bf16[128,2,256]{2,1,0:T(2,128)(2,1)S(1)}, bf16[128,2,256]{2,1,0:T(2,128)(2,1)}, u32[]{:S(2)}) copy-start(bf16[128,2,256]{2,1,0:T(2,128)(2,1)} %bc.23) | copy-start | bytes 393220
  0.0 1.1 %copy-start.2 = (f32[4,2048]{1,0:T(4,128)S(1)}, f32[4,2048]{1,0:T(4,128)}, u32[]{:S(2)}) copy-start(f32[4,2048]{1,0:T(4,128)} %taps_x.21) | copy-start | bytes 98308
  0.0 1.1 %copy-start.3 = (f32[4,2,256]{2,1,0:T(2,128)S(1)}, f32[4,2,256]{2,1,0:T(2,128)}, u32[]{:S(2)}) copy-start(f32[4,2,256]{2,1,0:T(2,128)} %taps_bc.21) | copy-start | bytes 24580
  0.1 4.5 %collective-permute-start.1 = (bf16[160,384]{1,0:T(8,128)(2,1)S(1)}, bf16[160,384]{1,0:T(8,128)(2,1)S(1)}, u32[]{:S(2)}, u32[]{:S(2)}) collective-permute-start(bf16[160,384]{1,0:T(8,128)(2,1)S(1)} %get-tuple-element.26._), channel_id=1, source_target_pairs={{0,4},{1,5},{2,6},{3,7},{16,20},{17,21},{18,22},{19,23}} | collective-permute-start | bytes 368648 | tf_op jit(solution)/shard_map/ppermute | solution.py:381
  1.1 0.7 %copy-start.5 = (f32[128,32]{0,1:T(8,128)S(1)}, f32[128,32]{0,1:T(8,128)}, u32[]{:S(2)}) copy-start(f32[128,32]{0,1:T(8,128)} %param.12) | copy-start | bytes 49156
  1.1 0.7 %copy-start.6 = (f32[2048]{0:T(1024)S(1)}, f32[2048]{0:T(1024)}, u32[]{:S(2)}) copy-start(f32[2048]{0:T(1024)} %param.17) | copy-start | bytes 24580
  1.1 0.7 %copy-start.7 = (f32[32]{0:T(128)S(1)}, f32[32]{0:T(128)}, u32[]{:S(2)}) copy-start(f32[32]{0:T(128)} %param.15) | copy-start | bytes 388
  1.1 4.2 %collective-permute-start.4 = (bf16[128,640]{1,0:T(8,128)(2,1)S(1)}, bf16[128,640]{1,0:T(8,128)(2,1)S(1)}, u32[]{:S(2)}, u32[]{:S(2)}) collective-permute-start(bf16[128,640]{1,0:T(8,128)(2,1)S(1)} %next_states.3._), channel_id=1, source_target_pairs={{0,4},{1,5},{2,6},{3,7},{16,20},{17,21},{18,22},{19,23}} | collective-permute-start | bytes 491528 | tf_op jit(solution)/shard_map/ppermute | solution.py:381
  2.4 5.1 %collective-permute-start = (bf16[8,2560]{1,0:T(8,128)(2,1)S(1)}, bf16[8,2560]{1,0:T(8,128)(2,1)S(1)}, u32[]{:S(2)}, u32[]{:S(2)}) collective-permute-start(bf16[8,2560]{1,0:T(8,128)(2,1)S(1)} %get-tuple-element.38._), channel_id=1, source_target_pairs={{4,8},{5,9},{6,10},{7,11},{20,24},{21,25},{22,26},{23,27}} | collective-permute-start | bytes 122888 | tf_op jit(solution)/shard_map/ppermute | solution.py:381
  3.1 2.9 %collective-permute-start.3 = (bf16[128,512]{1,0:T(8,128)(2,1)S(1)}, bf16[128,512]{1,0:T(8,128)(2,1)S(1)}, u32[]{:S(2)}, u32[]{:S(2)}) collective-permute-start(bf16[128,512]{1,0:T(8,128)(2,1)S(1)} %next_states.4._), channel_id=1, source_target_pairs={{0,4},{1,5},{2,6},{3,7},{16,20},{17,21},{18,22},{19,23}} | collective-permute-start | bytes 393224 | tf_op jit(solution)/shard_map/ppermute | solution.py:381
  3.8 3.0 %collective-permute-start.2 = (bf16[128,512]{1,0:T(8,128)(2,1)S(1)}, bf16[128,512]{1,0:T(8,128)(2,1)S(1)}, u32[]{:S(2)}, u32[]{:S(2)}) collective-permute-start(bf16[128,512]{1,0:T(8,128)(2,1)S(1)} %next_states.5), channel_id=1, source_target_pairs={{0,4},{1,5},{2,6},{3,7},{16,20},{17,21},{18,22},{19,23}} | collective-permute-start | bytes 393224 | tf_op jit(solution)/shard_map/ppermute | solution.py:381
  4.6 4.3 %collective-permute-start.8 = (bf16[128,384]{1,0:T(8,128)(2,1)S(1)}, bf16[128,384]{1,0:T(8,128)(2,1)S(1)}, u32[]{:S(2)}, u32[]{:S(2)}) collective-permute-start(bf16[128,384]{1,0:T(8,128)(2,1)S(1)} %add_convert_fusion.7._), channel_id=1, source_target_pairs={{4,8},{5,9},{6,10},{7,11},{20,24},{21,25},{22,26},{23,27}} | collective-permute-start | bytes 294920 | tf_op jit(solution)/shard_map/ppermute | solution.py:381
  5.4 4.9 %collective-permute-start.7 = (bf16[128,640]{1,0:T(8,128)(2,1)S(1)}, bf16[128,640]{1,0:T(8,128)(2,1)S(1)}, u32[]{:S(2)}, u32[]{:S(2)}) collective-permute-start(bf16[128,640]{1,0:T(8,128)(2,1)S(1)} %add_convert_fusion.1._), channel_id=1, source_target_pairs={{4,8},{5,9},{6,10},{7,11},{20,24},{21,25},{22,26},{23,27}} | collective-permute-start | bytes 491528 | tf_op jit(solution)/shard_map/ppermute | solution.py:381
  6.1 5.7 %collective-permute-start.6 = (bf16[128,512]{1,0:T(8,128)(2,1)S(1)}, bf16[128,512]{1,0:T(8,128)(2,1)S(1)}, u32[]{:S(2)}, u32[]{:S(2)}) collective-permute-start(bf16[128,512]{1,0:T(8,128)(2,1)S(1)} %add_convert_fusion.5._), channel_id=1, source_target_pairs={{4,8},{5,9},{6,10},{7,11},{20,24},{21,25},{22,26},{23,27}} | collective-permute-start | bytes 393224 | tf_op jit(solution)/shard_map/ppermute | solution.py:381
  6.9 7.5 %collective-permute-start.10 = (bf16[128,512]{1,0:T(8,128)(2,1)S(1)}, bf16[128,512]{1,0:T(8,128)(2,1)S(1)}, u32[]{:S(2)}, u32[]{:S(2)}) collective-permute-start(bf16[128,512]{1,0:T(8,128)(2,1)S(1)} %add_convert_fusion.4._), channel_id=1, source_target_pairs={{4,8},{5,9},{6,10},{7,11},{20,24},{21,25},{22,26},{23,27}} | collective-permute-start | bytes 393224 | tf_op jit(solution)/shard_map/ppermute | solution.py:381
  7.6 6.8 %collective-permute-start.5 = (bf16[8,2560]{1,0:T(8,128)(2,1)S(1)}, bf16[8,2560]{1,0:T(8,128)(2,1)S(1)}, u32[]{:S(2)}, u32[]{:S(2)}) collective-permute-start(bf16[8,2560]{1,0:T(8,128)(2,1)S(1)} %get-tuple-element.38._), channel_id=1, source_target_pairs={{8,12},{9,13},{10,14},{11,15},{24,28},{25,29},{26,30},{27,31}} | collective-permute-start | bytes 122888 | tf_op jit(solution)/shard_map/ppermute | solution.py:381
  9.0 9.4 %collective-permute-start.11 = (bf16[128,384]{1,0:T(8,128)(2,1)S(1)}, bf16[128,384]{1,0:T(8,128)(2,1)S(1)}, u32[]{:S(2)}, u32[]{:S(2)}) collective-permute-start(bf16[128,384]{1,0:T(8,128)(2,1)S(1)} %add_convert_fusion.6), channel_id=1, source_target_pairs={{8,12},{9,13},{10,14},{11,15},{24,28},{25,29},{26,30},{27,31}} | collective-permute-start | bytes 294920 | tf_op jit(solution)/shard_map/ppermute | solution.py:381
  10.4 9.3 %copy-start.4 = (bf16[128,2048]{1,0:T(8,128)(2,1)S(1)}, bf16[128,2048]{1,0:T(8,128)(2,1)}, u32[]{:S(2)}) copy-start(bf16[128,2048]{1,0:T(8,128)(2,1)} %refs_5_.1) | copy-start | bytes 1572868
  10.4 17.0 %collective-permute-start.13 = (bf16[128,640]{1,0:T(8,128)(2,1)S(1)}, bf16[128,640]{1,0:T(8,128)(2,1)S(1)}, u32[]{:S(2)}, u32[]{:S(2)}) collective-permute-start(bf16[128,640]{1,0:T(8,128)(2,1)S(1)} %add_convert_fusion), channel_id=1, source_target_pairs={{8,12},{9,13},{10,14},{11,15},{24,28},{25,29},{26,30},{27,31}} | collective-permute-start | bytes 491528 | tf_op jit(solution)/shard_map/ppermute | solution.py:381
  11.9 15.3 %collective-permute-start.9 = (bf16[128,512]{1,0:T(8,128)(2,1)S(1)}, bf16[128,512]{1,0:T(8,128)(2,1)S(1)}, u32[]{:S(2)}, u32[]{:S(2)}) collective-permute-start(bf16[128,512]{1,0:T(8,128)(2,1)S(1)} %add_convert_fusion.3), channel_id=1, source_target_pairs={{8,12},{9,13},{10,14},{11,15},{24,28},{25,29},{26,30},{27,31}} | collective-permute-start | bytes 393224 | tf_op jit(solution)/shard_map/ppermute | solution.py:381
  18.4 10.2 %collective-permute-start.12 = (bf16[128,512]{1,0:T(8,128)(2,1)S(1)}, bf16[128,512]{1,0:T(8,128)(2,1)S(1)}, u32[]{:S(2)}, u32[]{:S(2)}) collective-permute-start(bf16[128,512]{1,0:T(8,128)(2,1)S(1)} %add_convert_fusion.2), channel_id=1, source_target_pairs={{8,12},{9,13},{10,14},{11,15},{24,28},{25,29},{26,30},{27,31}} | collective-permute-start | bytes 393224 | tf_op jit(solution)/shard_map/ppermute | solution.py:381
  19.7 0.7 %copy-start.8 = (f32[32]{0:T(128)S(1)}, f32[32]{0:T(128)}, u32[]{:S(2)}) copy-start(f32[32]{0:T(128)} %param.16) | copy-start | bytes 388

commit v12 on v11

--- a/solution.py
+++ b/solution.py
@@ -222,19 +222,38 @@
         )
 
 
-def intra_kernel(count, _, *refs):
+def gate_kernel(groups, _, z_hbm, dt_raw, a_log, gate, lead, dt_out, cum_out, z, sem):
+    copy = pltpu.make_async_copy(z_hbm, z, sem)
+    copy.start()
+    dt, cum = rates(dt_raw[...], a_log[...], 0)
+    dt_out[...] = dt
+    cum_out[...] = cum
+    leading = jnp.exp(cum)
+    heads = dt.shape[0] // groups
+    cols = z.shape[1] // groups
+    for g in range(groups):
+        lead[:, g * cols : (g + 1) * cols] = spread(
+            leading[g * heads : (g + 1) * heads], cols // heads, 2
+        )
+    copy.wait()
+    for at in range(0, z.shape[1], CHUNK):
+        cut = slice(at, at + CHUNK)
+        here = silu(z[:, cut].astype(F32))
+        gate[:, cut] = here
+        lead[:, cut] = lead[:, cut] * here
+
+
+def intra_kernel(count, *refs):
     sources, refs = refs[:count], refs[count:]
-    x, bc, z, taps_x, taps_bc, dt_raw, a_log, d_skip, y_part, lead, c_act, wide = refs
+    x, bc, gate, taps_x, taps_bc, dt, cum, d_skip, y_part, c_act = refs
     tokens, width = x.shape
     groups, both = bc.shape[1:]
     state_dim = both // 2
     keep = taps_x.shape[0] - 1
     cols = width // groups
-    heads = dt_raw.shape[0] // groups
+    heads = dt.shape[0] // groups
     head_dim = cols // heads
-    dt, cum = rates(dt_raw[...], a_log[...], 0)
-    cum_t = cum.T
-    leading = jnp.exp(cum)
+    cum_t = cum[...].T
     skip = spread_row(as_column(d_skip[...], 0, groups * heads), head_dim)
     t_at = lax.broadcasted_iota(jnp.int32, (tokens, tokens), 0)
     s_at = lax.broadcasted_iota(jnp.int32, (tokens, tokens), 1)
@@ -254,10 +273,9 @@
         c_act[:, g * state_dim : (g + 1) * state_dim] = c
         inner = lax.dot_general(c, b, (((1,), (1,)), ((), ())), preferred_element_type=F32)
         inner = jnp.where(t_at >= s_at, inner, 0.0)
-        wide[...] = spread(leading[g * heads : (g + 1) * heads], head_dim, 2)
         for first in range(0, heads, 2):
-            here = slice(first * head_dim, first * head_dim + pair)
-            cut = slice(g * cols + here.start, g * cols + here.stop)
+            here = first * head_dim
+            cut = slice(g * cols + here, g * cols + here + pair)
             act = conv_act(x[:, cut].astype(F32), before(cut.start, cut.stop), taps_x[:, cut])
             lane = lax.broadcasted_iota(jnp.int32, act.shape, 1)
             full = act.astype(F32)
@@ -270,9 +288,7 @@
                 gap = jnp.minimum(cum_t[:, h : h + 1] - cum[h : h + 1, :], 0.0)
                 weights.append((jnp.exp(gap) * dt[h : h + 1, :] * inner).astype(BF16))
             y = jnp.dot(jnp.concatenate(weights, axis=1), blocks, preferred_element_type=F32)
-            gate = silu(z[:, cut].astype(F32))
-            y_part[:, cut] = (y + skip[:, cut] * full) * gate
-            lead[:, cut] = wide[:, here] * gate
+            y_part[:, cut] = (y + skip[:, cut] * full) * gate[:, cut]
 
 
 def gated_slice(low, which, c, y_part, lead, arrived):
@@ -425,14 +441,24 @@
         )(here(condition), rows, token, *sources, scale)
 
     along = [(i, i + 1) for i in range(devices - 1)]
-    def intra(token, befores):
+    def gates(token):
+        per_head = jax.ShapeDtypeStruct((heads, tokens), F32)
+        return pl.pallas_call(
+            functools.partial(gate_kernel, groups),
+            out_shape=[scale_shape, scale_shape, per_head, per_head],
+            in_specs=[anywhere, pl.BlockSpec(memory_space=pltpu.HBM)] + [in_vmem] * 2,
+            scratch_shapes=[pltpu.VMEM(z_in.shape, z_in.dtype), pltpu.SemaphoreType.DMA],
+            compiler_params=params(16),
+            name="gates",
+        )(token, pltpu.with_memory_space_constraint(z_in, pltpu.HBM), dt_t, a_row)
+
+    def intra(befores, gate, dt, cum):
         return pl.pallas_call(
             functools.partial(intra_kernel, len(befores)),
             out_shape=[
-                scale_shape, scale_shape, jax.ShapeDtypeStruct((tokens, groups * state_dim), BF16)
+                scale_shape, jax.ShapeDtypeStruct((tokens, groups * state_dim), BF16)
             ],
-            in_specs=[anywhere] + [in_vmem] * (len(befores) + 8),
-            scratch_shapes=[pltpu.VMEM((tokens, cols), F32)],
+            in_specs=[in_vmem] * (len(befores) + 8),
             compiler_params=params(24),
             cost_estimate=pl.CostEstimate(
                 flops=4 * tokens * tokens * width,
@@ -440,8 +466,9 @@
                 transcendentals=tokens * tokens * heads,
             ),
             name="intra",
-        )(token, *befores, x_in, bc_in, z_in, conv_x, conv_bc, dt_t, a_row, d_row)
-
+        )(*befores, x_in, bc_in, gate, conv_x, conv_bc, dt, cum, d_row)
+
+    gate_parts = None
     if devices <= CHAIN_MOST:
         first, scale = first_states(*cuts[0])
         sent = [first, next_states(first, scale, *cuts[1])]
@@ -458,23 +485,27 @@
         rows, token = arrived[0][0], last
         for hop in range(1, devices - 1):
             runs = place == 1 if hop == 1 else (place >= 2) & (place < devices - 1)
-            after = token
             for i, cut in enumerate(cuts):
+                if hop == 1:
+                    after = last if i == 0 else made_at[1 if i == len(cuts) - 1 else 0]
                 if hop <= 2:
                     made = later_states(runs, rows, after, scale_own, *cut)
                     states = [made] if i == 0 else states + [made]
                 early = ()
+                if hop == devices - 2 and hop > 1 and i == 1:
+                    gate_parts = gates(token)
+                    early = (gate_parts[0],)
                 if hop == devices - 2 and hop > 1 and i == len(cuts) - 1:
                     early = (arrived[0][-1], befores[-1])
                 before, *_ = lax.optimization_barrier((arrived[i][-1], token) + early)
                 joined = decays[i] * before[:state_dim].astype(F32) + states[i]
                 token = joined.astype(BF16)
-                after = token if hop == 1 else after
+                made_at = [token] if i == 0 else made_at + [token]
+                if hop == 1 and i == 1 and late:
+                    moved, _ = lax.optimization_barrier((last, token))
+                    befores.append(shifted(moved, late))
                 arrived[i].append(shifted(token, along[hop : hop + 1]))
-            if hop == 1 and late:
-                moved, _ = lax.optimization_barrier((last, token))
-                befores.append(shifted(moved, late))
-            rows = befores[0]
+            rows, after = befores[0], token
         which = place - 1
     else:
         last, gain, scale, *decays = prepared(a_row)
@@ -485,7 +516,8 @@
             arrived.append([doubling(state, decay, devices)])
         which = jnp.zeros_like(place)
     which = which.astype(jnp.int32).reshape(1)
-    y_part, lead, c_act = intra(a_row, befores)
+    gate, lead, dt, cum = gate_parts or gates(a_row)
+    y_part, c_act = intra(befores, gate, dt, cum)
 
     common = [which, c_act, y_part, lead]
     common_specs = [scalar] + [in_vmem] * 3

time: 30 us -> 39.5 us (1.32)
  the two profiles are of different devices: /device:TPU:30 before, /device:TPU:8 now
where the time goes in v12:
time: 39.5 us; the launch traced here: 38.8 us
  starting transfers between devices  18.2 us (46%)
  Pallas kernels  11.7 us (30%)
  local copies, waits for them, and re-layouts  4.26 us (11%)
  other arithmetic  2.39 us (6%)
  waiting for transfers between devices  1.72 us (4%)
  between operations  0.58 us (1%)
    ppermute x14, starting transfers between devices, shifted(): return lax.ppermute(value, 'seq', route)  18.2 us
    unnamed x60, local copies, waits for them, and re-layouts  4.26 us
    pallas_call x2, Pallas kernels, shards(): pl.pallas_call(functools.partial(output_kernel, begin, spans, unready), o...  2.87 us
    pallas_call x3, Pallas kernels, shards(): pl.pallas_call(functools.partial(gated_kernel, low), out_shape=jax.ShapeD...  2.4 us
    convert_element_type x8, other arithmetic, shards(): token = joined.astype(BF16)  2.35 us
    pallas_call x1, Pallas kernels, intra(): pl.pallas_call(functools.partial(intra_kernel, len(befores)), out_shape=[...  1.91 us
    pallas_call x8, Pallas kernels, later_states(): pl.pallas_call(functools.partial(later_kernel, low, high), out_shape=jax....  1.84 us
    ppermute x14, waiting for transfers between devices, shifted(): return lax.ppermute(value, 'seq', route)  1.72 us
  transfers between devices with their start and end apart: 14, of which 2 were waited for; matrix products, arithmetic and copies ran while one was open for 6% of the time, Pallas kernels for 25%

profile of v12, /device:TPU:8, one launch (start us, length us, event | category | flops | bytes accessed | tf_op | source)
XLA Modules:
  0.0 38.8 jit_solution(575014086962409587)
XLA Ops:
  0.0 0.1 first_states.1
  0.1 1.4 %collective-permute-start.1 = (bf16[160,384]{1,0:T(8,128)(2,1)S(1)}, bf16[160,384]{1,0:T(8,128)(2,1)S(1)}, u32[]{:S(2)}, u32[]{:S(2)}) collective-permute-start(bf16[160,384]{1,0:T(8,128)(2,1)S(1)} %get-tuple-element.29._), channel_id=1, source_target_pairs={{0,4},{1,5},{2,6},{3,7},{16,20},{17,21},{18,22},{19,23}} | collective-permute-start | bytes 368648 | tf_op jit(solution)/shard_map/ppermute | solution.py:397
  1.6 0.0 copy-start.10
  1.6 0.0 copy-start.20
  1.6 0.0 copy-start.25
  1.6 1.3 %collective-permute-start.2 = (bf16[128,640]{1,0:T(8,128)(2,1)S(1)}, bf16[128,640]{1,0:T(8,128)(2,1)S(1)}, u32[]{:S(2)}, u32[]{:S(2)}) collective-permute-start(bf16[128,640]{1,0:T(8,128)(2,1)S(1)} %next_states.3._), channel_id=1, source_target_pairs={{0,4},{1,5},{2,6},{3,7},{16,20},{17,21},{18,22},{19,23}} | collective-permute-start | bytes 491528 | tf_op jit(solution)/shard_map/ppermute | solution.py:397
  2.9 1.2 %prepared.1 = (bf16[8,2560]{1,0:T(8,128)(2,1)}, f32[1,2048]{1,0:T(1,128)S(1)}, f32[128,2048]{1,0:T(8,128)S(1)}, f32[1,384]{1,0:T(1,128)S(1)}, f32[1,640]{1,0:T(1...) custom-call(bf16[128,640]{1,0:T(8,128)(2,1)S(1)} %next_states.3._, bf16[128,2048]{1,0:T(8,128)(2,1)S(1)} %copy-done, ...), custom_call_target="tpu_custom_call" | custom-call | tf_op jit(solution)/shard_map/prepared/pallas_call | solution.py:421
  4.1 2.3 %collective-permute-start = (bf16[8,2560]{1,0:T(8,128)(2,1)}, bf16[8,2560]{1,0:T(8,128)(2,1)S(1)}, u32[]{:S(2)}, u32[]{:S(2)}) collective-permute-start(bf16[8,2560]{1,0:T(8,128)(2,1)} %get-tuple-element.37._), channel_id=1, source_target_pairs={{4,8},{5,9},{6,10},{7,11},{20,24},{21,25},{22,26},{23,27}} | collective-permute-start | bytes 122888 | tf_op jit(solution)/shard_map/ppermute | solution.py:397
  6.5 1.3 %collective-permute-start.6 = (bf16[128,512]{1,0:T(8,128)(2,1)S(1)}, bf16[128,512]{1,0:T(8,128)(2,1)S(1)}, u32[]{:S(2)}, u32[]{:S(2)}) collective-permute-start(bf16[128,512]{1,0:T(8,128)(2,1)S(1)} %next_states.4._), channel_id=1, source_target_pairs={{0,4},{1,5},{2,6},{3,7},{16,20},{17,21},{18,22},{19,23}} | collective-permute-start | bytes 393224 | tf_op jit(solution)/shard_map/ppermute | solution.py:397
  7.8 1.3 %collective-permute-start.5 = (bf16[128,512]{1,0:T(8,128)(2,1)S(1)}, bf16[128,512]{1,0:T(8,128)(2,1)S(1)}, u32[]{:S(2)}, u32[]{:S(2)}) collective-permute-start(bf16[128,512]{1,0:T(8,128)(2,1)S(1)} %next_states.5), channel_id=1, source_target_pairs={{0,4},{1,5},{2,6},{3,7},{16,20},{17,21},{18,22},{19,23}} | collective-permute-start | bytes 393224 | tf_op jit(solution)/shard_map/ppermute | solution.py:397
  9.2 0.0 copy-start.28
  9.2 0.0 collective-permute-done.1.rows.refs_1_.refs_0_
  9.2 0.4 %later_states.8 = f32[128,384]{1,0:T(8,128)S(1)} custom-call(s32[1]{0:T(128)} %bitcast.5.active, bf16[160,384]{1,0:T(8,128)(2,1)S(1)} %collective-permute-done.1.rows.refs_1_.refs_0_, bf16[8,2560]{1,0:T(8,128)(2,1)} %get-tuple-element.37._, bf16[128,2048]{1,0:T(8,128)(2,1)S(1)} %copy-done, bf16[128,2,256]{2,1,0:T(2,128)(2,1)S(1)} %copy-done.1, ...), custom_call_target="tpu_custom_call" | custom-call | tf_op jit(solution)/shard_map/later_states/pallas_call | solution.py:435
  9.6 1.3 %collective-permute-start.4 = (bf16[128,384]{1,0:T(8,128)(2,1)S(1)}, bf16[128,384]{1,0:T(8,128)(2,1)S(1)}, u32[]{:S(2)}, u32[]{:S(2)}) collective-permute-start(bf16[128,384]{1,0:T(8,128)(2,1)S(1)} %add_convert_fusion.7._), channel_id=1, source_target_pairs={{4,8},{5,9},{6,10},{7,11},{20,24},{21,25},{22,26},{23,27}} | collective-permute-start | bytes 294920 | tf_op jit(solution)/shard_map/ppermute | solution.py:397
  10.9 0.5 %later_states.10 = f32[128,512]{1,0:T(8,128)S(1)} custom-call(s32[1]{0:T(128)} %bitcast.5.active, bf16[160,384]{1,0:T(8,128)(2,1)S(1)} %collective-permute-done.1.rows.refs_1_.refs_0_, bf16[128,384]{1,0:T(8,128)(2,1)S(1)} %add_convert_fusion.7._, bf16[128,2048]{1,0:T(8,128)(2,1)S(1)} %copy-done, bf16[128,2,256]{2,1,0:T(2,128)(2,1)S(1)} %copy-done.1, ...), custom_call_target="tpu_custom_call" | custom-call | tf_op jit(solution)/shard_map/later_states/pallas_call | solution.py:435
  11.4 0.5 %later_states.9 = f32[128,640]{1,0:T(8,128)S(1)} custom-call(s32[1]{0:T(128)} %bitcast.5.active, bf16[160,384]{1,0:T(8,128)(2,1)S(1)} %collective-permute-done.1.rows.refs_1_.refs_0_, bf16[128,384]{1,0:T(8,128)(2,1)S(1)} %add_convert_fusion.7._, bf16[128,2048]{1,0:T(8,128)(2,1)S(1)} %copy-done, bf16[128,2,256]{2,1,0:T(2,128)(2,1)S(1)} %copy-done.1, ...), custom_call_target="tpu_custom_call" | custom-call | tf_op jit(solution)/shard_map/later_states/pallas_call | solution.py:435
  11.9 0.0 collective-permute-done.2.refs_0_
  11.9 0.1 add_convert_fusion.1._
  12.0 1.3 %collective-permute-start.8 = (bf16[128,640]{1,0:T(8,128)(2,1)S(1)}, bf16[128,640]{1,0:T(8,128)(2,1)S(1)}, u32[]{:S(2)}, u32[]{:S(2)}) collective-permute-start(bf16[128,640]{1,0:T(8,128)(2,1)S(1)} %add_convert_fusion.1._), channel_id=1, source_target_pairs={{4,8},{5,9},{6,10},{7,11},{20,24},{21,25},{22,26},{23,27}} | collective-permute-start | bytes 491528 | tf_op jit(solution)/shard_map/ppermute | solution.py:397
  13.3 1.4 %collective-permute-done.6.refs_0_ = bf16[128,512]{1,0:T(8,128)(2,1)S(1)} collective-permute-done((bf16[128,512]{1,0:T(8,128)(2,1)S(1)}, bf16[128,512]{1,0:T(8,128)(2,1)S(1)}, u32[]{:S(2)}, u32[]{:S(2)}) %collective-permute-start.6) | collective-permute-done | bytes 131104 | tf_op jit(solution)/shard_map/ppermute | solution.py:397
  14.7 1.3 %collective-permute-start.7 = (bf16[128,512]{1,0:T(8,128)(2,1)S(1)}, bf16[128,512]{1,0:T(8,128)(2,1)S(1)}, u32[]{:S(2)}, u32[]{:S(2)}) collective-permute-start(bf16[128,512]{1,0:T(8,128)(2,1)S(1)} %add_convert_fusion.5), channel_id=1, source_target_pairs={{4,8},{5,9},{6,10},{7,11},{20,24},{21,25},{22,26},{23,27}} | collective-permute-start | bytes 393224 | tf_op jit(solution)/shard_map/ppermute | solution.py:397
  16.0 0.3 collective-permute-done.5.refs_1_
  16.3 0.7 %collective-permute-start.3 = (bf16[8,2560]{1,0:T(8,128)(2,1)}, bf16[8,2560]{1,0:T(8,128)(2,1)S(1)}, u32[]{:S(2)}, u32[]{:S(2)}) collective-permute-start(bf16[8,2560]{1,0:T(8,128)(2,1)} %get-tuple-element.37._), channel_id=1, source_target_pairs={{8,12},{9,13},{10,14},{11,15},{24,28},{25,29},{26,30},{27,31}} | collective-permute-start | bytes 122888 | tf_op jit(solution)/shard_map/ppermute | solution.py:397
  17.0 0.5 %later_states.11 = f32[128,512]{1,0:T(8,128)S(1)} custom-call(s32[1]{0:T(128)} %bitcast.5.active, bf16[160,384]{1,0:T(8,128)(2,1)S(1)} %collective-permute-done.1.rows.refs_1_.refs_0_, bf16[128,640]{1,0:T(8,128)(2,1)S(1)} %add_convert_fusion.1._, bf16[128,2048]{1,0:T(8,128)(2,1)S(1)} %copy-done, bf16[128,2,256]{2,1,0:T(2,128)(2,1)S(1)} %copy-done.1, ...), custom_call_target="tpu_custom_call" | custom-call | tf_op jit(solution)/shard_map/later_states/pallas_call | solution.py:435
  17.5 1.3 %collective-permute-start.10 = (bf16[128,512]{1,0:T(8,128)(2,1)S(1)}, bf16[128,512]{1,0:T(8,128)(2,1)S(1)}, u32[]{:S(2)}, u32[]{:S(2)}) collective-permute-start(bf16[128,512]{1,0:T(8,128)(2,1)S(1)} %add_convert_fusion.4._), channel_id=1, source_target_pairs={{4,8},{5,9},{6,10},{7,11},{20,24},{21,25},{22,26},{23,27}} | collective-permute-start | bytes 393224 | tf_op jit(solution)/shard_map/ppermute | solution.py:397
  18.9 0.0 copy-start.11
  18.9 0.0 copy-start.26
  19.0 0.6 %copy-done.8 = bf16[128,384]{1,0:T(8,128)(2,1)} copy-done((bf16[128,384]{1,0:T(8,128)(2,1)}, bf16[128,384]{1,0:T(8,128)(2,1)S(1)}, u32[]{:S(2)}) %copy-start.8) | copy-done | bytes 98328
  19.5 0.7 %collective-permute-start.11 = (bf16[128,384]{1,0:T(8,128)(2,1)S(1)}, bf16[128,384]{1,0:T(8,128)(2,1)S(1)}, u32[]{:S(2)}, u32[]{:S(2)}) collective-permute-start(bf16[128,384]{1,0:T(8,128)(2,1)S(1)} %add_convert_fusion.6._), channel_id=1, source_target_pairs={{8,12},{9,13},{10,14},{11,15},{24,28},{25,29},{26,30},{27,31}} | collective-permute-start | bytes 294920 | tf_op jit(solution)/shard_map/ppermute | solution.py:397
  20.2 0.0 copy-start.29
  20.2 1.4 %gates.1 = (f32[128,2048]{1,0:T(8,128)S(1)}, f32[128,2048]{1,0:T(8,128)S(1)}, f32[32,128]{1,0:T(8,128)S(1)}, f32[32,128]{1,0:T(8,128)S(1)}) custom-call(bf16[128,384]{1,0:T(8,128)(2,1)S(1)} %add_convert_fusion.6._, bf16[128,2048]{1,0:T(8,128)(2,1)} %z_hbm.1, f32[32,128]{1,0:T(8,128)S(1)} %bitcast.12, f32[1,32]{1,0:T(1,128)S(1)} %bitcast.20), custom_call_target="tpu_custom_call" | custom-call | tf_op jit(solution)/shard_map/gates/pallas_call | solution.py:446
  21.7 0.7 %add_convert_fusion = bf16[128,640]{1,0:T(8,128)(2,1)} fusion(f32[128,640]{1,0:T(8,128)S(1)} %later_states.13, bf16[128,640]{1,0:T(8,128)(2,1)S(1)} %collective-permute-done.8.refs_1_, f32[640]{0:T(1024)S(1)} %copy-done.29), kind=kLoop, calls=%fused_computation | loop fusion | flops 327680 | bytes 657920 | tf_op jit(solution)/shard_map/convert_element_type | solution.py:502
  22.4 1.4 %collective-permute-start.13 = (bf16[128,640]{1,0:T(8,128)(2,1)}, bf16[128,640]{1,0:T(8,128)(2,1)}, u32[]{:S(2)}, u32[]{:S(2)}) collective-permute-start(bf16[128,640]{1,0:T(8,128)(2,1)} %add_convert_fusion), channel_id=1, source_target_pairs={{8,12},{9,13},{10,14},{11,15},{24,28},{25,29},{26,30},{27,31}} | collective-permute-start | bytes 491528 | tf_op jit(solution)/shard_map/ppermute | solution.py:397
  23.8 0.7 %add_convert_fusion.3 = bf16[128,512]{1,0:T(8,128)(2,1)} fusion(f32[128,512]{1,0:T(8,128)S(1)} %later_states.14, bf16[128,512]{1,0:T(8,128)(2,1)S(1)} %collective-permute-done.7.refs_1_, f32[512]{0:T(512)S(1)} %bitcast.17), kind=kLoop, calls=%fused_computation.3 | loop fusion | flops 262144 | bytes 526336 | tf_op jit(solution)/shard_map/convert_element_type | solution.py:502
  24.5 1.3 %collective-permute-start.9 = (bf16[128,512]{1,0:T(8,128)(2,1)}, bf16[128,512]{1,0:T(8,128)(2,1)}, u32[]{:S(2)}, u32[]{:S(2)}) collective-permute-start(bf16[128,512]{1,0:T(8,128)(2,1)} %add_convert_fusion.3), channel_id=1, source_target_pairs={{8,12},{9,13},{10,14},{11,15},{24,28},{25,29},{26,30},{27,31}} | collective-permute-start | bytes 393224 | tf_op jit(solution)/shard_map/ppermute | solution.py:397
  25.9 0.7 %add_convert_fusion.2 = bf16[128,512]{1,0:T(8,128)(2,1)} fusion(f32[128,512]{1,0:T(8,128)S(1)} %later_states.15, bf16[128,512]{1,0:T(8,128)(2,1)S(1)} %collective-permute-done.10.refs_2_, f32[512]{0:T(512)S(1)} %bitcast.15), kind=kLoop, calls=%fused_computation.2 | loop fusion | flops 262144 | bytes 526336 | tf_op jit(solution)/shard_map/convert_element_type | solution.py:502
  26.6 1.3 %collective-permute-start.12 = (bf16[128,512]{1,0:T(8,128)(2,1)}, bf16[128,512]{1,0:T(8,128)(2,1)}, u32[]{:S(2)}, u32[]{:S(2)}) collective-permute-start(bf16[128,512]{1,0:T(8,128)(2,1)} %add_convert_fusion.2), channel_id=1, source_target_pairs={{8,12},{9,13},{10,14},{11,15},{24,28},{25,29},{26,30},{27,31}} | collective-permute-start | bytes 393224 | tf_op jit(solution)/shard_map/ppermute | solution.py:397
  28.0 0.7 %copy-done.27 = f32[32]{0:T(128)S(1)} copy-done((f32[32]{0:T(128)S(1)}, f32[32]{0:T(128)}, u32[]{:S(2)}) %copy-start.27) | copy-done | bytes 152
  28.6 0.8 %copy-done.15 = bf16[8,2560]{1,0:T(8,128)(2,1)S(1)} copy-done((bf16[8,2560]{1,0:T(8,128)(2,1)S(1)}, bf16[8,2560]{1,0:T(8,128)(2,1)}, u32[]{:S(2)}) %copy-start.15) | copy-done | bytes 40984
  29.4 0.7 %copy-done.17 = f32[32,128]{1,0:T(8,128)S(1)} copy-done((f32[32,128]{1,0:T(8,128)S(1)}, f32[32,128]{1,0:T(8,128)}, u32[]{:S(2)}) %copy-start.17) | copy-done | bytes 16408
  30.1 0.7 %copy-done.19 = f32[32,128]{1,0:T(8,128)S(1)} copy-done((f32[32,128]{1,0:T(8,128)S(1)}, f32[32,128]{1,0:T(8,128)}, u32[]{:S(2)}) %copy-start.19) | copy-done | bytes 16408
  30.8 1.9 %intra.1 = (f32[128,2048]{1,0:T(8,128)S(1)}, bf16[128,256]{1,0:T(8,128)(2,1)S(1)}) custom-call(bf16[8,2560]{1,0:T(8,128)(2,1)S(1)} %collective-permute-done.rows.refs_0_, bf16[160,384]{1,0:T(8,128)(2,1)S(1)} %collective-permute-done.1.rows.refs_1_.refs_0_, bf16[8,2560]{1,0:T(8,128)(2,1)S(1)} %copy-done.15, bf16[128,2048]{1,0:T(8,128)(2,1)S(1)} %copy-done, ...), custom_call_target="tpu_custom_call" | custom-call | flops 134217728 | bytes 3145728 | tf_op jit(solution)/shard_map/intra/pallas_call | solution.py:456
  32.8 0.2 gated.4.refs_0_
  33.0 0.7 %copy-done.7 = bf16[128,512]{1,0:T(8,128)(2,1)S(1)} copy-done((bf16[128,512]{1,0:T(8,128)(2,1)S(1)}, bf16[128,512]{1,0:T(8,128)(2,1)}, u32[]{:S(2)}) %copy-start.7) | copy-done | bytes 131096
  33.7 1.1 %gated.3.refs_0_ = f32[128,512]{1,0:T(8,128)S(1)} custom-call(s32[1]{0:T(128)} %bitcast.which, bf16[128,256]{1,0:T(8,128)(2,1)S(1)} %get-tuple-element.46.c, f32[128,2048]{1,0:T(8,128)S(1)} %get-tuple-element.47.y_part, f32[128,2048]{1,0:T(8,128)S(1)} %get-tuple-element.48.lead, bf16[128,512]{1,0:T(8,128)(2,1)S(1)} %collective-permute-done.6.refs_0_, ...), custom_call_target="tpu_custom_call" | custom-call | tf_op jit(solution)/shard_map/gated/pallas_call | solution.py:528
  34.8 1.1 %gated.5.refs_1_ = f32[128,640]{1,0:T(8,128)S(1)} custom-call(s32[1]{0:T(128)} %bitcast.which, bf16[128,256]{1,0:T(8,128)(2,1)S(1)} %get-tuple-element.46.c, f32[128,2048]{1,0:T(8,128)S(1)} %get-tuple-element.47.y_part, f32[128,2048]{1,0:T(8,128)S(1)} %get-tuple-element.48.lead, bf16[128,640]{1,0:T(8,128)(2,1)S(1)} %collective-permute-done.2.refs_0_, ...), custom_call_target="tpu_custom_call" | custom-call | tf_op jit(solution)/shard_map/gated/pallas_call | solution.py:528
  35.9 0.9 %outputs.2.refs_4_ = bf16[128,2048]{1,0:T(8,128)(2,1)} custom-call(s32[1]{0:T(128)} %bitcast.which, bf16[128,256]{1,0:T(8,128)(2,1)S(1)} %get-tuple-element.46.c, f32[128,2048]{1,0:T(8,128)S(1)} %get-tuple-element.47.y_part, f32[128,2048]{1,0:T(8,128)S(1)} %get-tuple-element.48.lead, f32[1,2048]{1,0:T(1,128)S(1)} %get-tuple-element.49.gain, ...), custom_call_target="tpu_custom_call" | custom-call | tf_op jit(solution)/shard_map/outputs/pallas_call | solution.py:555
  36.9 2.0 %outputs.3 = bf16[128,2048]{1,0:T(8,128)(2,1)} custom-call(s32[1]{0:T(128)} %bitcast.which, bf16[128,256]{1,0:T(8,128)(2,1)S(1)} %get-tuple-element.46.c, f32[128,2048]{1,0:T(8,128)S(1)} %get-tuple-element.47.y_part, f32[128,2048]{1,0:T(8,128)S(1)} %get-tuple-element.48.lead, f32[1,2048]{1,0:T(1,128)S(1)} %get-tuple-element.49.gain, ...), custom_call_target="tpu_custom_call", output_to_operand_aliasing={{}: (9, {})} | custom-call | tf_op jit(solution)/shard_map/outputs/pallas_call | solution.py:555
  (70 shorter events, 0.4 us)
Async XLA Ops:
  0.0 1.5 %copy-start = (bf16[128,2048]{1,0:T(8,128)(2,1)S(1)}, bf16[128,2048]{1,0:T(8,128)(2,1)}, u32[]{:S(2)}) copy-start(bf16[128,2048]{1,0:T(8,128)(2,1)} %x.23) | copy-start | bytes 1572868
  0.0 1.5 %copy-start.1 = (bf16[128,2,256]{2,1,0:T(2,128)(2,1)S(1)}, bf16[128,2,256]{2,1,0:T(2,128)(2,1)}, u32[]{:S(2)}) copy-start(bf16[128,2,256]{2,1,0:T(2,128)(2,1)} %bc.23) | copy-start | bytes 393220
  0.0 1.5 %copy-start.2 = (f32[4,2048]{1,0:T(4,128)S(1)}, f32[4,2048]{1,0:T(4,128)}, u32[]{:S(2)}) copy-start(f32[4,2048]{1,0:T(4,128)} %taps_x.21) | copy-start | bytes 98308
  0.0 1.5 %copy-start.3 = (f32[4,2,256]{2,1,0:T(2,128)S(1)}, f32[4,2,256]{2,1,0:T(2,128)}, u32[]{:S(2)}) copy-start(f32[4,2,256]{2,1,0:T(2,128)} %taps_bc.21) | copy-start | bytes 24580
  0.1 9.1 %collective-permute-start.1 = (bf16[160,384]{1,0:T(8,128)(2,1)S(1)}, bf16[160,384]{1,0:T(8,128)(2,1)S(1)}, u32[]{:S(2)}, u32[]{:S(2)}) collective-permute-start(bf16[160,384]{1,0:T(8,128)(2,1)S(1)} %get-tuple-element.29._), channel_id=1, source_target_pairs={{0,4},{1,5},{2,6},{3,7},{16,20},{17,21},{18,22},{19,23}} | collective-permute-start | bytes 368648 | tf_op jit(solution)/shard_map/ppermute | solution.py:397
  1.6 1.4 %copy-start.10 = (f32[128,32]{0,1:T(8,128)S(1)}, f32[128,32]{0,1:T(8,128)}, u32[]{:S(2)}) copy-start(f32[128,32]{0,1:T(8,128)} %param.12) | copy-start | bytes 49156
  1.6 1.4 %copy-start.20 = (f32[2048]{0:T(1024)S(1)}, f32[2048]{0:T(1024)}, u32[]{:S(2)}) copy-start(f32[2048]{0:T(1024)} %param.17) | copy-start | bytes 24580
  1.6 1.3 %copy-start.25 = (f32[32]{0:T(128)S(1)}, f32[32]{0:T(128)}, u32[]{:S(2)}) copy-start(f32[32]{0:T(128)} %param.15) | copy-start | bytes 388
  1.6 10.3 %collective-permute-start.2 = (bf16[128,640]{1,0:T(8,128)(2,1)S(1)}, bf16[128,640]{1,0:T(8,128)(2,1)S(1)}, u32[]{:S(2)}, u32[]{:S(2)}) collective-permute-start(bf16[128,640]{1,0:T(8,128)(2,1)S(1)} %next_states.3._), channel_id=1, source_target_pairs={{0,4},{1,5},{2,6},{3,7},{16,20},{17,21},{18,22},{19,23}} | collective-permute-start | bytes 491528 | tf_op jit(solution)/shard_map/ppermute | solution.py:397
  4.1 10.6 %copy-start.23 = (f32[1,512]{1,0:T(1,128)}, f32[1,512]{1,0:T(1,128)S(1)}, u32[]{:S(2)}) copy-start(f32[1,512]{1,0:T(1,128)S(1)} %get-tuple-element.39) | copy-start | bytes 6148
  4.1 13.3 %copy-start.21 = (f32[1,512]{1,0:T(1,128)}, f32[1,512]{1,0:T(1,128)S(1)}, u32[]{:S(2)}) copy-start(f32[1,512]{1,0:T(1,128)S(1)} %get-tuple-element.38) | copy-start | bytes 6148
  4.1 13.3 %collective-permute-start = (bf16[8,2560]{1,0:T(8,128)(2,1)}, bf16[8,2560]{1,0:T(8,128)(2,1)S(1)}, u32[]{:S(2)}, u32[]{:S(2)}) collective-permute-start(bf16[8,2560]{1,0:T(8,128)(2,1)} %get-tuple-element.37._), channel_id=1, source_target_pairs={{4,8},{5,9},{6,10},{7,11},{20,24},{21,25},{22,26},{23,27}} | collective-permute-start | bytes 122888 | tf_op jit(solution)/shard_map/ppermute | solution.py:397
  6.5 8.2 %collective-permute-start.6 = (bf16[128,512]{1,0:T(8,128)(2,1)S(1)}, bf16[128,512]{1,0:T(8,128)(2,1)S(1)}, u32[]{:S(2)}, u32[]{:S(2)}) collective-permute-start(bf16[128,512]{1,0:T(8,128)(2,1)S(1)} %next_states.4._), channel_id=1, source_target_pairs={{0,4},{1,5},{2,6},{3,7},{16,20},{17,21},{18,22},{19,23}} | collective-permute-start | bytes 393224 | tf_op jit(solution)/shard_map/ppermute | solution.py:397
  7.8 8.5 %collective-permute-start.5 = (bf16[128,512]{1,0:T(8,128)(2,1)S(1)}, bf16[128,512]{1,0:T(8,128)(2,1)S(1)}, u32[]{:S(2)}, u32[]{:S(2)}) collective-permute-start(bf16[128,512]{1,0:T(8,128)(2,1)S(1)} %next_states.5), channel_id=1, source_target_pairs={{0,4},{1,5},{2,6},{3,7},{16,20},{17,21},{18,22},{19,23}} | collective-permute-start | bytes 393224 | tf_op jit(solution)/shard_map/ppermute | solution.py:397
  9.2 2.7 %copy-start.28 = (f32[640]{0:T(1024)}, f32[640]{0:T(1024)S(1)}, u32[]{:S(2)}) copy-start(f32[640]{0:T(1024)S(1)} %reduce) | copy-start | bytes 7684
  9.6 9.3 %collective-permute-start.4 = (bf16[128,384]{1,0:T(8,128)(2,1)S(1)}, bf16[128,384]{1,0:T(8,128)(2,1)S(1)}, u32[]{:S(2)}, u32[]{:S(2)}) collective-permute-start(bf16[128,384]{1,0:T(8,128)(2,1)S(1)} %add_convert_fusion.7._), channel_id=1, source_target_pairs={{4,8},{5,9},{6,10},{7,11},{20,24},{21,25},{22,26},{23,27}} | collective-permute-start | bytes 294920 | tf_op jit(solution)/shard_map/ppermute | solution.py:397
  12.0 9.7 %collective-permute-start.8 = (bf16[128,640]{1,0:T(8,128)(2,1)S(1)}, bf16[128,640]{1,0:T(8,128)(2,1)S(1)}, u32[]{:S(2)}, u32[]{:S(2)}) collective-permute-start(bf16[128,640]{1,0:T(8,128)(2,1)S(1)} %add_convert_fusion.1._), channel_id=1, source_target_pairs={{4,8},{5,9},{6,10},{7,11},{20,24},{21,25},{22,26},{23,27}} | collective-permute-start | bytes 491528 | tf_op jit(solution)/shard_map/ppermute | solution.py:397
  14.7 9.1 %collective-permute-start.7 = (bf16[128,512]{1,0:T(8,128)(2,1)S(1)}, bf16[128,512]{1,0:T(8,128)(2,1)S(1)}, u32[]{:S(2)}, u32[]{:S(2)}) collective-permute-start(bf16[128,512]{1,0:T(8,128)(2,1)S(1)} %add_convert_fusion.5), channel_id=1, source_target_pairs={{4,8},{5,9},{6,10},{7,11},{20,24},{21,25},{22,26},{23,27}} | collective-permute-start | bytes 393224 | tf_op jit(solution)/shard_map/ppermute | solution.py:397
  16.3 9.6 %collective-permute-start.3 = (bf16[8,2560]{1,0:T(8,128)(2,1)}, bf16[8,2560]{1,0:T(8,128)(2,1)S(1)}, u32[]{:S(2)}, u32[]{:S(2)}) collective-permute-start(bf16[8,2560]{1,0:T(8,128)(2,1)} %get-tuple-element.37._), channel_id=1, source_target_pairs={{8,12},{9,13},{10,14},{11,15},{24,28},{25,29},{26,30},{27,31}} | collective-permute-start | bytes 122888 | tf_op jit(solution)/shard_map/ppermute | solution.py:397
  17.5 8.4 %collective-permute-start.10 = (bf16[128,512]{1,0:T(8,128)(2,1)S(1)}, bf16[128,512]{1,0:T(8,128)(2,1)S(1)}, u32[]{:S(2)}, u32[]{:S(2)}) collective-permute-start(bf16[128,512]{1,0:T(8,128)(2,1)S(1)} %add_convert_fusion.4._), channel_id=1, source_target_pairs={{4,8},{5,9},{6,10},{7,11},{20,24},{21,25},{22,26},{23,27}} | collective-permute-start | bytes 393224 | tf_op jit(solution)/shard_map/ppermute | solution.py:397
  18.9 1.3 %copy-start.11 = (f32[128,32]{0,1:T(8,128)S(1)}, f32[128,32]{0,1:T(8,128)}, u32[]{:S(2)}) copy-start(f32[128,32]{0,1:T(8,128)} %param.12) | copy-start | bytes 49156
  18.9 1.3 %copy-start.26 = (f32[32]{0:T(128)S(1)}, f32[32]{0:T(128)}, u32[]{:S(2)}) copy-start(f32[32]{0:T(128)} %param.15) | copy-start | bytes 388
  18.9 0.6 %copy-start.8 = (bf16[128,384]{1,0:T(8,128)(2,1)}, bf16[128,384]{1,0:T(8,128)(2,1)S(1)}, u32[]{:S(2)}) copy-start(bf16[128,384]{1,0:T(8,128)(2,1)S(1)} %collective-permute-done.4.refs_1_) | copy-start | bytes 294916
  19.5 6.3 %collective-permute-start.11 = (bf16[128,384]{1,0:T(8,128)(2,1)S(1)}, bf16[128,384]{1,0:T(8,128)(2,1)S(1)}, u32[]{:S(2)}, u32[]{:S(2)}) collective-permute-start(bf16[128,384]{1,0:T(8,128)(2,1)S(1)} %add_convert_fusion.6._), channel_id=1, source_target_pairs={{8,12},{9,13},{10,14},{11,15},{24,28},{25,29},{26,30},{27,31}} | collective-permute-start | bytes 294920 | tf_op jit(solution)/shard_map/ppermute | solution.py:397
  20.2 1.4 %copy-start.29 = (f32[640]{0:T(1024)S(1)}, f32[640]{0:T(1024)}, u32[]{:S(2)}) copy-start(f32[640]{0:T(1024)} %copy-done.28) | copy-start | bytes 7684
  21.6 0.8 %copy-start.16 = (f32[32,128]{1,0:T(8,128)}, f32[32,128]{1,0:T(8,128)S(1)}, u32[]{:S(2)}) copy-start(f32[32,128]{1,0:T(8,128)S(1)} %get-tuple-element.44.refs_8_) | copy-start | bytes 49156
  21.6 0.8 %copy-start.18 = (f32[32,128]{1,0:T(8,128)}, f32[32,128]{1,0:T(8,128)S(1)}, u32[]{:S(2)}) copy-start(f32[32,128]{1,0:T(8,128)S(1)} %get-tuple-element.45.refs_9_) | copy-start | bytes 49156
  21.7 2.2 %copy-start.24 = (f32[1,512]{1,0:T(1,128)S(1)}, f32[1,512]{1,0:T(1,128)}, u32[]{:S(2)}) copy-start(f32[1,512]{1,0:T(1,128)} %copy-done.23) | copy-start | bytes 6148
  22.4 3.5 %copy-start.22 = (f32[1,512]{1,0:T(1,128)S(1)}, f32[1,512]{1,0:T(1,128)}, u32[]{:S(2)}) copy-start(f32[1,512]{1,0:T(1,128)} %copy-done.21) | copy-start | bytes 6148
  22.4 12.4 %collective-permute-start.13 = (bf16[128,640]{1,0:T(8,128)(2,1)}, bf16[128,640]{1,0:T(8,128)(2,1)}, u32[]{:S(2)}, u32[]{:S(2)}) collective-permute-start(bf16[128,640]{1,0:T(8,128)(2,1)} %add_convert_fusion), channel_id=1, source_target_pairs={{8,12},{9,13},{10,14},{11,15},{24,28},{25,29},{26,30},{27,31}} | collective-permute-start | bytes 491528 | tf_op jit(solution)/shard_map/ppermute | solution.py:397
  23.8 0.7 %copy-start.6 = (bf16[128,512]{1,0:T(8,128)(2,1)}, bf16[128,512]{1,0:T(8,128)(2,1)S(1)}, u32[]{:S(2)}) copy-start(bf16[128,512]{1,0:T(8,128)(2,1)S(1)} %collective-permute-done.7.refs_1_) | copy-start | bytes 393220
  24.5 8.4 %collective-permute-start.9 = (bf16[128,512]{1,0:T(8,128)(2,1)}, bf16[128,512]{1,0:T(8,128)(2,1)}, u32[]{:S(2)}, u32[]{:S(2)}) collective-permute-start(bf16[128,512]{1,0:T(8,128)(2,1)} %add_convert_fusion.3), channel_id=1, source_target_pairs={{8,12},{9,13},{10,14},{11,15},{24,28},{25,29},{26,30},{27,31}} | collective-permute-start | bytes 393224 | tf_op jit(solution)/shard_map/ppermute | solution.py:397
  25.9 0.8 %copy-start.14 = (bf16[8,2560]{1,0:T(8,128)(2,1)}, bf16[8,2560]{1,0:T(8,128)(2,1)S(1)}, u32[]{:S(2)}) copy-start(bf16[8,2560]{1,0:T(8,128)(2,1)S(1)} %collective-permute-done.3.refs_2_) | copy-start | bytes 122884
  25.9 0.8 %copy-start.4 = (bf16[128,512]{1,0:T(8,128)(2,1)}, bf16[128,512]{1,0:T(8,128)(2,1)S(1)}, u32[]{:S(2)}) copy-start(bf16[128,512]{1,0:T(8,128)(2,1)S(1)} %collective-permute-done.10.refs_2_) | copy-start | bytes 393220
  25.9 0.8 %copy-start.12 = (bf16[128,384]{1,0:T(8,128)(2,1)}, bf16[128,384]{1,0:T(8,128)(2,1)S(1)}, u32[]{:S(2)}) copy-start(bf16[128,384]{1,0:T(8,128)(2,1)S(1)} %collective-permute-done.11.refs_2_) | copy-start | bytes 294916
  26.6 10.2 %collective-permute-start.12 = (bf16[128,512]{1,0:T(8,128)(2,1)}, bf16[128,512]{1,0:T(8,128)(2,1)}, u32[]{:S(2)}, u32[]{:S(2)}) collective-permute-start(bf16[128,512]{1,0:T(8,128)(2,1)} %add_convert_fusion.2), channel_id=1, source_target_pairs={{8,12},{9,13},{10,14},{11,15},{24,28},{25,29},{26,30},{27,31}} | collective-permute-start | bytes 393224 | tf_op jit(solution)/shard_map/ppermute | solution.py:397
  28.0 0.7 %copy-start.27 = (f32[32]{0:T(128)S(1)}, f32[32]{0:T(128)}, u32[]{:S(2)}) copy-start(f32[32]{0:T(128)} %param.16) | copy-start | bytes 388
  28.6 0.8 %copy-start.15 = (bf16[8,2560]{1,0:T(8,128)(2,1)S(1)}, bf16[8,2560]{1,0:T(8,128)(2,1)}, u32[]{:S(2)}) copy-start(bf16[8,2560]{1,0:T(8,128)(2,1)} %copy-done.14) | copy-start | bytes 122884
  29.4 0.7 %copy-start.17 = (f32[32,128]{1,0:T(8,128)S(1)}, f32[32,128]{1,0:T(8,128)}, u32[]{:S(2)}) copy-start(f32[32,128]{1,0:T(8,128)} %copy-done.16) | copy-start | bytes 49156
  30.1 0.7 %copy-start.19 = (f32[32,128]{1,0:T(8,128)S(1)}, f32[32,128]{1,0:T(8,128)}, u32[]{:S(2)}) copy-start(f32[32,128]{1,0:T(8,128)} %copy-done.18) | copy-start | bytes 49156
  30.8 1.9 %copy-start.9 = (bf16[128,384]{1,0:T(8,128)(2,1)S(1)}, bf16[128,384]{1,0:T(8,128)(2,1)}, u32[]{:S(2)}) copy-start(bf16[128,384]{1,0:T(8,128)(2,1)} %copy-done.8) | copy-start | bytes 294916
  30.8 1.9 %copy-start.13 = (bf16[128,384]{1,0:T(8,128)(2,1)S(1)}, bf16[128,384]{1,0:T(8,128)(2,1)}, u32[]{:S(2)}) copy-start(bf16[128,384]{1,0:T(8,128)(2,1)} %copy-done.12) | copy-start | bytes 294916
  32.8 0.9 %copy-start.7 = (bf16[128,512]{1,0:T(8,128)(2,1)S(1)}, bf16[128,512]{1,0:T(8,128)(2,1)}, u32[]{:S(2)}) copy-start(bf16[128,512]{1,0:T(8,128)(2,1)} %copy-done.6) | copy-start | bytes 393220
  35.9 0.9 %copy-start.5 = (bf16[128,512]{1,0:T(8,128)(2,1)S(1)}, bf16[128,512]{1,0:T(8,128)(2,1)}, u32[]{:S(2)}) copy-start(bf16[128,512]{1,0:T(8,128)(2,1)} %copy-done.4) | copy-start | bytes 393220

commit v13 on v12

--- a/solution.py
+++ b/solution.py
@@ -178,7 +178,9 @@
         head_rows(low, high, x, bc, taps_x, taps_bc, scale, out)
 
 
-def prepare_kernel(cuts, _, x, bc, dt_raw, a_log, gain, pack, gain_out, scale, *decays):
+def prepare_kernel(
+    cuts, _, x, bc, dt_raw, a_log, gain, skip, pack, gain_out, skip_out, scale, *decays
+):
     tokens, width = x.shape
     groups, both = bc.shape[1:]
     pack[:, :width] = x[tokens - 2 * RIM :, :].astype(F32)[-RIM:].astype(BF16)
@@ -186,6 +188,7 @@
     for g in range(groups):
         pack[:, width + g * both : width + (g + 1) * both] = last_bc[:, g].astype(BF16)
     gain_out[...] = gain[...]
+    skip_out[...] = skip[...]
     row = scales(groups, width // dt_raw.shape[0], dt_raw, a_log, scale)
     for decay, (low, high) in zip(decays, cuts):
         decay[...] = row[:, low:high]
@@ -404,7 +407,7 @@
             out_shape=[jax.ShapeDtypeStruct((state_dim + extra, high - low), BF16), scale_shape],
             in_specs=[scalar] + in_hbm,
             scratch_shapes=landed + [pltpu.SemaphoreType.DMA((len(operands),))],
-            compiler_params=params(16),
+            compiler_params=params(6),
             name="first_states",
         )(here(place == 0), *pinned)
 
@@ -413,7 +416,7 @@
             functools.partial(next_kernel, low, high),
             out_shape=jax.ShapeDtypeStruct((state_dim, high - low), BF16),
             in_specs=[scalar, anywhere] + [in_vmem] * (len(sources) + 1),
-            compiler_params=params(16),
+            compiler_params=params(6),
             name="next_states",
         )(here(place == 0), token, *sources, scale)
 
@@ -423,20 +426,21 @@
             out_shape=[
                 jax.ShapeDtypeStruct((RIM, width + groups * both), BF16),
                 jax.ShapeDtypeStruct((1, width), F32),
+                jax.ShapeDtypeStruct((1, heads), F32),
                 scale_shape,
             ]
             + [jax.ShapeDtypeStruct((1, high - low), F32) for low, high in cuts],
-            in_specs=[anywhere] + [in_vmem] * 5,
-            compiler_params=params(16),
+            in_specs=[anywhere] + [in_vmem] * 6,
+            compiler_params=params(6),
             name="prepared",
-        )(token, x_in, bc_in, dt_t, a_row, gain)
+        )(token, x_in, bc_in, dt_t, a_row, gain, d_row)
 
     def later_states(condition, rows, token, scale, low, high):
         return pl.pallas_call(
             functools.partial(later_kernel, low, high),
             out_shape=jax.ShapeDtypeStruct((state_dim, high - low), F32),
             in_specs=[scalar, in_vmem, anywhere] + [in_vmem] * (len(sources) + 1),
-            compiler_params=params(16),
+            compiler_params=params(6),
             name="later_states",
         )(here(condition), rows, token, *sources, scale)
 
@@ -448,31 +452,31 @@
             out_shape=[scale_shape, scale_shape, per_head, per_head],
             in_specs=[anywhere, pl.BlockSpec(memory_space=pltpu.HBM)] + [in_vmem] * 2,
             scratch_shapes=[pltpu.VMEM(z_in.shape, z_in.dtype), pltpu.SemaphoreType.DMA],
-            compiler_params=params(16),
+            compiler_params=params(6),
             name="gates",
         )(token, pltpu.with_memory_space_constraint(z_in, pltpu.HBM), dt_t, a_row)
 
-    def intra(befores, gate, dt, cum):
+    def intra(befores, gate, dt, cum, skip):
         return pl.pallas_call(
             functools.partial(intra_kernel, len(befores)),
             out_shape=[
                 scale_shape, jax.ShapeDtypeStruct((tokens, groups * state_dim), BF16)
             ],
             in_specs=[in_vmem] * (len(befores) + 8),
-            compiler_params=params(24),
+            compiler_params=params(10),
             cost_estimate=pl.CostEstimate(
                 flops=4 * tokens * tokens * width,
                 bytes_accessed=12 * tokens * width,
                 transcendentals=tokens * tokens * heads,
             ),
             name="intra",
-        )(*befores, x_in, bc_in, gate, conv_x, conv_bc, dt, cum, d_row)
+        )(*befores, x_in, bc_in, gate, conv_x, conv_bc, dt, cum, skip)
 
     gate_parts = None
     if devices <= CHAIN_MOST:
         first, scale = first_states(*cuts[0])
         sent = [first, next_states(first, scale, *cuts[1])]
-        last, gain, scale_own, *decays = prepared(sent[-1])
+        last, gain, d_row, scale_own, *decays = prepared(sent[-1])
         token = last
         for cut in cuts[2:]:
             sent.append(next_states(token, scale, *cut))
@@ -508,7 +512,7 @@
             rows, after = befores[0], token
         which = place - 1
     else:
-        last, gain, scale, *decays = prepared(a_row)
+        last, gain, d_row, scale, *decays = prepared(a_row)
         befores = [shifted(last, along)]
         arrived = []
         for decay, cut in zip(decays, cuts):
@@ -517,7 +521,7 @@
         which = jnp.zeros_like(place)
     which = which.astype(jnp.int32).reshape(1)
     gate, lead, dt, cum = gate_parts or gates(a_row)
-    y_part, c_act = intra(befores, gate, dt, cum)
+    y_part, c_act = intra(befores, gate, dt, cum, d_row)
 
     common = [which, c_act, y_part, lead]
     common_specs = [scalar] + [in_vmem] * 3
@@ -529,7 +533,7 @@
                 functools.partial(gated_kernel, low),
                 out_shape=jax.ShapeDtypeStruct((tokens, high - low), F32),
                 in_specs=common_specs + [in_vmem] * len(seen),
-                compiler_params=params(16),
+                compiler_params=params(6),
                 name="gated",
             )(*common, *seen)
         )
@@ -562,7 +566,7 @@
                 pltpu.SemaphoreType.DMA((len(cuts) + groups,)),
             ],
             input_output_aliases=aliases,
-            compiler_params=params(16),
+            compiler_params=params(6),
             name="outputs",
         )(*common, gain, *inputs)
     return out

time: 39.5 us -> 41.7 us (1.056)
  local copies, waits for them, and re-layouts: 4.26 us -> 6.58 us
    unnamed x60 -> x64, local copies, waits for them, and re-layouts: 4.26 us -> 6.58 us
  transfers between devices with their start and end apart: 14 -> 14, of which waited for: 2 -> 2; matrix products, arithmetic and copies ran while one was open for 6% -> 6% of each run, Pallas kernels for 25% -> 24%
where the time goes in v13:
time: 41.7 us; the launch traced here: 41 us
  starting transfers between devices  18.2 us (44%)
  Pallas kernels  11.7 us (28%)
  local copies, waits for them, and re-layouts  6.58 us (16%)
  other arithmetic  2.38 us (6%)
  waiting for transfers between devices  1.59 us (4%)
  between operations  0.55 us (1%)
    ppermute x14, starting transfers between devices, shifted(): return lax.ppermute(value, 'seq', route)  18.2 us
    unnamed x64, local copies, waits for them, and re-layouts  6.58 us
    pallas_call x2, Pallas kernels, shards(): pl.pallas_call(functools.partial(output_kernel, begin, spans, unready), o...  2.88 us
    pallas_call x3, Pallas kernels, shards(): pl.pallas_call(functools.partial(gated_kernel, low), out_shape=jax.ShapeD...  2.4 us
    convert_element_type x8, other arithmetic, shards(): token = joined.astype(BF16)  2.34 us
    pallas_call x1, Pallas kernels, intra(): pl.pallas_call(functools.partial(intra_kernel, len(befores)), out_shape=[...  1.91 us
    pallas_call x8, Pallas kernels, later_states(): pl.pallas_call(functools.partial(later_kernel, low, high), out_shape=jax....  1.84 us
    ppermute x14, waiting for transfers between devices, shifted(): return lax.ppermute(value, 'seq', route)  1.59 us
  transfers between devices with their start and end apart: 14, of which 2 were waited for; matrix products, arithmetic and copies ran while one was open for 6% of the time, Pallas kernels for 24%

profile of v13, /device:TPU:8, one launch (start us, length us, event | category | flops | bytes accessed | tf_op | source)
XLA Modules:
  0.0 41.0 jit_solution(15625559809887416843)
XLA Ops:
  0.0 0.1 first_states.1
  0.1 1.4 %collective-permute-start.1 = (bf16[160,384]{1,0:T(8,128)(2,1)S(1)}, bf16[160,384]{1,0:T(8,128)(2,1)S(1)}, u32[]{:S(2)}, u32[]{:S(2)}) collective-permute-start(bf16[160,384]{1,0:T(8,128)(2,1)S(1)} %get-tuple-element.30._), channel_id=1, source_target_pairs={{0,4},{1,5},{2,6},{3,7},{16,20},{17,21},{18,22},{19,23}} | collective-permute-start | bytes 368648 | tf_op jit(solution)/shard_map/ppermute | solution.py:400
  1.6 0.0 copy-start.10
  1.6 0.0 copy-start.20
  1.6 1.3 %collective-permute-start.2 = (bf16[128,640]{1,0:T(8,128)(2,1)S(1)}, bf16[128,640]{1,0:T(8,128)(2,1)S(1)}, u32[]{:S(2)}, u32[]{:S(2)}) collective-permute-start(bf16[128,640]{1,0:T(8,128)(2,1)S(1)} %next_states.3._), channel_id=1, source_target_pairs={{0,4},{1,5},{2,6},{3,7},{16,20},{17,21},{18,22},{19,23}} | collective-permute-start | bytes 491528 | tf_op jit(solution)/shard_map/ppermute | solution.py:400
  2.9 0.6 %copy-done.25 = f32[32]{0:T(128)S(1)} copy-done((f32[32]{0:T(128)S(1)}, f32[32]{0:T(128)}, u32[]{:S(2)}) %copy-start.25) | copy-done | bytes 152
  3.6 0.0 copy-done.27
  3.6 1.2 %prepared.1 = (bf16[8,2560]{1,0:T(8,128)(2,1)}, f32[1,2048]{1,0:T(1,128)S(1)}, f32[1,32]{1,0:T(1,128)S(1)}, f32[128,2048]{1,0:T(8,128)S(1)}, f32[1,384]{1,0:T(1,...) custom-call(bf16[128,640]{1,0:T(8,128)(2,1)S(1)} %next_states.3._, ...), custom_call_target="tpu_custom_call" | custom-call | tf_op jit(solution)/shard_map/prepared/pallas_call | solution.py:424
  4.8 0.5 %copy-done.28 = f32[1,32]{1,0:T(1,128)} copy-done((f32[1,32]{1,0:T(1,128)}, f32[1,32]{1,0:T(1,128)S(1)}, u32[]{:S(2)}) %copy-start.28) | copy-done | bytes 152
  5.3 2.3 %collective-permute-start = (bf16[8,2560]{1,0:T(8,128)(2,1)}, bf16[8,2560]{1,0:T(8,128)(2,1)S(1)}, u32[]{:S(2)}, u32[]{:S(2)}) collective-permute-start(bf16[8,2560]{1,0:T(8,128)(2,1)} %get-tuple-element.38._), channel_id=1, source_target_pairs={{4,8},{5,9},{6,10},{7,11},{20,24},{21,25},{22,26},{23,27}} | collective-permute-start | bytes 122888 | tf_op jit(solution)/shard_map/ppermute | solution.py:400
  7.7 1.3 %collective-permute-start.6 = (bf16[128,512]{1,0:T(8,128)(2,1)S(1)}, bf16[128,512]{1,0:T(8,128)(2,1)S(1)}, u32[]{:S(2)}, u32[]{:S(2)}) collective-permute-start(bf16[128,512]{1,0:T(8,128)(2,1)S(1)} %next_states.4._), channel_id=1, source_target_pairs={{0,4},{1,5},{2,6},{3,7},{16,20},{17,21},{18,22},{19,23}} | collective-permute-start | bytes 393224 | tf_op jit(solution)/shard_map/ppermute | solution.py:400
  9.0 1.3 %collective-permute-start.5 = (bf16[128,512]{1,0:T(8,128)(2,1)S(1)}, bf16[128,512]{1,0:T(8,128)(2,1)S(1)}, u32[]{:S(2)}, u32[]{:S(2)}) collective-permute-start(bf16[128,512]{1,0:T(8,128)(2,1)S(1)} %next_states.5), channel_id=1, source_target_pairs={{0,4},{1,5},{2,6},{3,7},{16,20},{17,21},{18,22},{19,23}} | collective-permute-start | bytes 393224 | tf_op jit(solution)/shard_map/ppermute | solution.py:400
  10.3 0.0 copy-start.30
  10.4 0.4 later_states.8
  10.8 1.3 %collective-permute-start.4 = (bf16[128,384]{1,0:T(8,128)(2,1)S(1)}, bf16[128,384]{1,0:T(8,128)(2,1)S(1)}, u32[]{:S(2)}, u32[]{:S(2)}) collective-permute-start(bf16[128,384]{1,0:T(8,128)(2,1)S(1)} %add_convert_fusion.7._), channel_id=1, source_target_pairs={{4,8},{5,9},{6,10},{7,11},{20,24},{21,25},{22,26},{23,27}} | collective-permute-start | bytes 294920 | tf_op jit(solution)/shard_map/ppermute | solution.py:400
  12.1 0.5 %later_states.10 = f32[128,512]{1,0:T(8,128)S(1)} custom-call(s32[1]{0:T(128)} %bitcast.6.active, bf16[160,384]{1,0:T(8,128)(2,1)S(1)} %collective-permute-done.1.rows.refs_1_.refs_0_, bf16[128,384]{1,0:T(8,128)(2,1)S(1)} %add_convert_fusion.7._, bf16[128,2048]{1,0:T(8,128)(2,1)S(1)} %copy-done, bf16[128,2,256]{2,1,0:T(2,128)(2,1)S(1)} %copy-done.1, ...), custom_call_target="tpu_custom_call" | custom-call | tf_op jit(solution)/shard_map/later_states/pallas_call | solution.py:439
  12.6 0.5 %later_states.9 = f32[128,640]{1,0:T(8,128)S(1)} custom-call(s32[1]{0:T(128)} %bitcast.6.active, bf16[160,384]{1,0:T(8,128)(2,1)S(1)} %collective-permute-done.1.rows.refs_1_.refs_0_, bf16[128,384]{1,0:T(8,128)(2,1)S(1)} %add_convert_fusion.7._, bf16[128,2048]{1,0:T(8,128)(2,1)S(1)} %copy-done, bf16[128,2,256]{2,1,0:T(2,128)(2,1)S(1)} %copy-done.1, ...), custom_call_target="tpu_custom_call" | custom-call | tf_op jit(solution)/shard_map/later_states/pallas_call | solution.py:439
  13.1 0.1 add_convert_fusion.1._
  13.1 1.3 %collective-permute-start.8 = (bf16[128,640]{1,0:T(8,128)(2,1)S(1)}, bf16[128,640]{1,0:T(8,128)(2,1)S(1)}, u32[]{:S(2)}, u32[]{:S(2)}) collective-permute-start(bf16[128,640]{1,0:T(8,128)(2,1)S(1)} %add_convert_fusion.1._), channel_id=1, source_target_pairs={{4,8},{5,9},{6,10},{7,11},{20,24},{21,25},{22,26},{23,27}} | collective-permute-start | bytes 491528 | tf_op jit(solution)/shard_map/ppermute | solution.py:400
  14.4 1.2 %collective-permute-done.6.refs_0_ = bf16[128,512]{1,0:T(8,128)(2,1)S(1)} collective-permute-done((bf16[128,512]{1,0:T(8,128)(2,1)S(1)}, bf16[128,512]{1,0:T(8,128)(2,1)S(1)}, u32[]{:S(2)}, u32[]{:S(2)}) %collective-permute-start.6) | collective-permute-done | bytes 131104 | tf_op jit(solution)/shard_map/ppermute | solution.py:400
  15.6 1.3 %collective-permute-start.7 = (bf16[128,512]{1,0:T(8,128)(2,1)S(1)}, bf16[128,512]{1,0:T(8,128)(2,1)S(1)}, u32[]{:S(2)}, u32[]{:S(2)}) collective-permute-start(bf16[128,512]{1,0:T(8,128)(2,1)S(1)} %add_convert_fusion.5), channel_id=1, source_target_pairs={{4,8},{5,9},{6,10},{7,11},{20,24},{21,25},{22,26},{23,27}} | collective-permute-start | bytes 393224 | tf_op jit(solution)/shard_map/ppermute | solution.py:400
  16.9 0.4 collective-permute-done.5.refs_1_
  17.3 0.7 %collective-permute-start.3 = (bf16[8,2560]{1,0:T(8,128)(2,1)}, bf16[8,2560]{1,0:T(8,128)(2,1)S(1)}, u32[]{:S(2)}, u32[]{:S(2)}) collective-permute-start(bf16[8,2560]{1,0:T(8,128)(2,1)} %get-tuple-element.38._), channel_id=1, source_target_pairs={{8,12},{9,13},{10,14},{11,15},{24,28},{25,29},{26,30},{27,31}} | collective-permute-start | bytes 122888 | tf_op jit(solution)/shard_map/ppermute | solution.py:400
  18.0 0.5 %later_states.11 = f32[128,512]{1,0:T(8,128)S(1)} custom-call(s32[1]{0:T(128)} %bitcast.6.active, bf16[160,384]{1,0:T(8,128)(2,1)S(1)} %collective-permute-done.1.rows.refs_1_.refs_0_, bf16[128,640]{1,0:T(8,128)(2,1)S(1)} %add_convert_fusion.1._, bf16[128,2048]{1,0:T(8,128)(2,1)S(1)} %copy-done, bf16[128,2,256]{2,1,0:T(2,128)(2,1)S(1)} %copy-done.1, ...), custom_call_target="tpu_custom_call" | custom-call | tf_op jit(solution)/shard_map/later_states/pallas_call | solution.py:439
  18.5 1.3 %collective-permute-start.10 = (bf16[128,512]{1,0:T(8,128)(2,1)S(1)}, bf16[128,512]{1,0:T(8,128)(2,1)S(1)}, u32[]{:S(2)}, u32[]{:S(2)}) collective-permute-start(bf16[128,512]{1,0:T(8,128)(2,1)S(1)} %add_convert_fusion.4._), channel_id=1, source_target_pairs={{4,8},{5,9},{6,10},{7,11},{20,24},{21,25},{22,26},{23,27}} | collective-permute-start | bytes 393224 | tf_op jit(solution)/shard_map/ppermute | solution.py:400
  19.9 0.0 copy-start.26
  20.0 0.6 %copy-done.8 = bf16[128,384]{1,0:T(8,128)(2,1)} copy-done((bf16[128,384]{1,0:T(8,128)(2,1)}, bf16[128,384]{1,0:T(8,128)(2,1)S(1)}, u32[]{:S(2)}) %copy-start.8) | copy-done | bytes 98328
  20.6 0.7 %collective-permute-start.11 = (bf16[128,384]{1,0:T(8,128)(2,1)S(1)}, bf16[128,384]{1,0:T(8,128)(2,1)S(1)}, u32[]{:S(2)}, u32[]{:S(2)}) collective-permute-start(bf16[128,384]{1,0:T(8,128)(2,1)S(1)} %add_convert_fusion.6._), channel_id=1, source_target_pairs={{8,12},{9,13},{10,14},{11,15},{24,28},{25,29},{26,30},{27,31}} | collective-permute-start | bytes 294920 | tf_op jit(solution)/shard_map/ppermute | solution.py:400
  21.3 1.4 %gates.1 = (f32[128,2048]{1,0:T(8,128)S(1)}, f32[128,2048]{1,0:T(8,128)S(1)}, f32[32,128]{1,0:T(8,128)S(1)}, f32[32,128]{1,0:T(8,128)S(1)}) custom-call(bf16[128,384]{1,0:T(8,128)(2,1)S(1)} %add_convert_fusion.6._, bf16[128,2048]{1,0:T(8,128)(2,1)} %z_hbm.1, f32[32,128]{1,0:T(8,128)S(1)} %bitcast.12, f32[1,32]{1,0:T(1,128)S(1)} %bitcast.20), custom_call_target="tpu_custom_call" | custom-call | tf_op jit(solution)/shard_map/gates/pallas_call | solution.py:450
  22.7 0.6 %copy-done.16 = f32[32,128]{1,0:T(8,128)} copy-done((f32[32,128]{1,0:T(8,128)}, f32[32,128]{1,0:T(8,128)S(1)}, u32[]{:S(2)}) %copy-start.16) | copy-done | bytes 16408
  23.3 0.6 %copy-done.18 = f32[32,128]{1,0:T(8,128)} copy-done((f32[32,128]{1,0:T(8,128)}, f32[32,128]{1,0:T(8,128)S(1)}, u32[]{:S(2)}) %copy-start.18) | copy-done | bytes 16408
  23.9 0.7 %add_convert_fusion = bf16[128,640]{1,0:T(8,128)(2,1)} fusion(f32[128,640]{1,0:T(8,128)S(1)} %later_states.13, bf16[128,640]{1,0:T(8,128)(2,1)S(1)} %collective-permute-done.8.refs_1_, f32[640]{0:T(1024)S(1)} %copy-done.31), kind=kLoop, calls=%fused_computation | loop fusion | flops 327680 | bytes 657920 | tf_op jit(solution)/shard_map/convert_element_type | solution.py:506
  24.6 1.5 %collective-permute-start.13 = (bf16[128,640]{1,0:T(8,128)(2,1)}, bf16[128,640]{1,0:T(8,128)(2,1)}, u32[]{:S(2)}, u32[]{:S(2)}) collective-permute-start(bf16[128,640]{1,0:T(8,128)(2,1)} %add_convert_fusion), channel_id=1, source_target_pairs={{8,12},{9,13},{10,14},{11,15},{24,28},{25,29},{26,30},{27,31}} | collective-permute-start | bytes 491528 | tf_op jit(solution)/shard_map/ppermute | solution.py:400
  26.1 0.7 %add_convert_fusion.3 = bf16[128,512]{1,0:T(8,128)(2,1)} fusion(f32[128,512]{1,0:T(8,128)S(1)} %later_states.14, bf16[128,512]{1,0:T(8,128)(2,1)S(1)} %collective-permute-done.7.refs_1_, f32[512]{0:T(512)S(1)} %bitcast.17), kind=kLoop, calls=%fused_computation.3 | loop fusion | flops 262144 | bytes 526336 | tf_op jit(solution)/shard_map/convert_element_type | solution.py:506
  26.8 1.3 %collective-permute-start.9 = (bf16[128,512]{1,0:T(8,128)(2,1)}, bf16[128,512]{1,0:T(8,128)(2,1)}, u32[]{:S(2)}, u32[]{:S(2)}) collective-permute-start(bf16[128,512]{1,0:T(8,128)(2,1)} %add_convert_fusion.3), channel_id=1, source_target_pairs={{8,12},{9,13},{10,14},{11,15},{24,28},{25,29},{26,30},{27,31}} | collective-permute-start | bytes 393224 | tf_op jit(solution)/shard_map/ppermute | solution.py:400
  28.1 0.7 %add_convert_fusion.2 = bf16[128,512]{1,0:T(8,128)(2,1)} fusion(f32[128,512]{1,0:T(8,128)S(1)} %later_states.15, bf16[128,512]{1,0:T(8,128)(2,1)S(1)} %collective-permute-done.10.refs_2_, f32[512]{0:T(512)S(1)} %bitcast.15), kind=kLoop, calls=%fused_computation.2 | loop fusion | flops 262144 | bytes 526336 | tf_op jit(solution)/shard_map/convert_element_type | solution.py:506
  28.9 1.3 %collective-permute-start.12 = (bf16[128,512]{1,0:T(8,128)(2,1)}, bf16[128,512]{1,0:T(8,128)(2,1)}, u32[]{:S(2)}, u32[]{:S(2)}) collective-permute-start(bf16[128,512]{1,0:T(8,128)(2,1)} %add_convert_fusion.2), channel_id=1, source_target_pairs={{8,12},{9,13},{10,14},{11,15},{24,28},{25,29},{26,30},{27,31}} | collective-permute-start | bytes 393224 | tf_op jit(solution)/shard_map/ppermute | solution.py:400
  30.2 0.6 %copy-done.29 = f32[1,32]{1,0:T(1,128)S(1)} copy-done((f32[1,32]{1,0:T(1,128)S(1)}, f32[1,32]{1,0:T(1,128)}, u32[]{:S(2)}) %copy-start.29) | copy-done | bytes 152
  30.8 0.8 %copy-done.15 = bf16[8,2560]{1,0:T(8,128)(2,1)S(1)} copy-done((bf16[8,2560]{1,0:T(8,128)(2,1)S(1)}, bf16[8,2560]{1,0:T(8,128)(2,1)}, u32[]{:S(2)}) %copy-start.15) | copy-done | bytes 40984
  31.6 0.7 %copy-done.17 = f32[32,128]{1,0:T(8,128)S(1)} copy-done((f32[32,128]{1,0:T(8,128)S(1)}, f32[32,128]{1,0:T(8,128)}, u32[]{:S(2)}) %copy-start.17) | copy-done | bytes 16408
  32.3 0.7 %copy-done.19 = f32[32,128]{1,0:T(8,128)S(1)} copy-done((f32[32,128]{1,0:T(8,128)S(1)}, f32[32,128]{1,0:T(8,128)}, u32[]{:S(2)}) %copy-start.19) | copy-done | bytes 16408
  33.0 1.9 %intra.1 = (f32[128,2048]{1,0:T(8,128)S(1)}, bf16[128,256]{1,0:T(8,128)(2,1)S(1)}) custom-call(bf16[8,2560]{1,0:T(8,128)(2,1)S(1)} %collective-permute-done.rows.refs_0_, bf16[160,384]{1,0:T(8,128)(2,1)S(1)} %collective-permute-done.1.rows.refs_1_.refs_0_, bf16[8,2560]{1,0:T(8,128)(2,1)S(1)} %copy-done.15, bf16[128,2048]{1,0:T(8,128)(2,1)S(1)} %copy-done, ...), custom_call_target="tpu_custom_call" | custom-call | flops 134217728 | bytes 3145728 | tf_op jit(solution)/shard_map/intra/pallas_call | solution.py:460
  35.0 0.2 gated.4.refs_0_
  35.2 0.7 %copy-done.7 = bf16[128,512]{1,0:T(8,128)(2,1)S(1)} copy-done((bf16[128,512]{1,0:T(8,128)(2,1)S(1)}, bf16[128,512]{1,0:T(8,128)(2,1)}, u32[]{:S(2)}) %copy-start.7) | copy-done | bytes 131096
  35.9 1.1 %gated.3.refs_0_ = f32[128,512]{1,0:T(8,128)S(1)} custom-call(s32[1]{0:T(128)} %bitcast.which, bf16[128,256]{1,0:T(8,128)(2,1)S(1)} %get-tuple-element.48.c, f32[128,2048]{1,0:T(8,128)S(1)} %get-tuple-element.49.y_part, f32[128,2048]{1,0:T(8,128)S(1)} %get-tuple-element.50.lead, bf16[128,512]{1,0:T(8,128)(2,1)S(1)} %collective-permute-done.6.refs_0_, ...), custom_call_target="tpu_custom_call" | custom-call | tf_op jit(solution)/shard_map/gated/pallas_call | solution.py:532
  37.0 1.1 %gated.5.refs_1_ = f32[128,640]{1,0:T(8,128)S(1)} custom-call(s32[1]{0:T(128)} %bitcast.which, bf16[128,256]{1,0:T(8,128)(2,1)S(1)} %get-tuple-element.48.c, f32[128,2048]{1,0:T(8,128)S(1)} %get-tuple-element.49.y_part, f32[128,2048]{1,0:T(8,128)S(1)} %get-tuple-element.50.lead, bf16[128,640]{1,0:T(8,128)(2,1)S(1)} %collective-permute-done.2.refs_0_, ...), custom_call_target="tpu_custom_call" | custom-call | tf_op jit(solution)/shard_map/gated/pallas_call | solution.py:532
  38.1 0.9 %outputs.2.refs_4_ = bf16[128,2048]{1,0:T(8,128)(2,1)} custom-call(s32[1]{0:T(128)} %bitcast.which, bf16[128,256]{1,0:T(8,128)(2,1)S(1)} %get-tuple-element.48.c, f32[128,2048]{1,0:T(8,128)S(1)} %get-tuple-element.49.y_part, f32[128,2048]{1,0:T(8,128)S(1)} %get-tuple-element.50.lead, f32[1,2048]{1,0:T(1,128)S(1)} %get-tuple-element.51.gain, ...), custom_call_target="tpu_custom_call" | custom-call | tf_op jit(solution)/shard_map/outputs/pallas_call | solution.py:559
  39.0 2.0 %outputs.3 = bf16[128,2048]{1,0:T(8,128)(2,1)} custom-call(s32[1]{0:T(128)} %bitcast.which, bf16[128,256]{1,0:T(8,128)(2,1)S(1)} %get-tuple-element.48.c, f32[128,2048]{1,0:T(8,128)S(1)} %get-tuple-element.49.y_part, f32[128,2048]{1,0:T(8,128)S(1)} %get-tuple-element.50.lead, f32[1,2048]{1,0:T(1,128)S(1)} %get-tuple-element.51.gain, ...), custom_call_target="tpu_custom_call", output_to_operand_aliasing={{}: (9, {})} | custom-call | tf_op jit(solution)/shard_map/outputs/pallas_call | solution.py:559
  (74 shorter events, 0.4 us)
Async XLA Ops:
  0.0 1.5 %copy-start = (bf16[128,2048]{1,0:T(8,128)(2,1)S(1)}, bf16[128,2048]{1,0:T(8,128)(2,1)}, u32[]{:S(2)}) copy-start(bf16[128,2048]{1,0:T(8,128)(2,1)} %x.23) | copy-start | bytes 1572868
  0.0 1.5 %copy-start.1 = (bf16[128,2,256]{2,1,0:T(2,128)(2,1)S(1)}, bf16[128,2,256]{2,1,0:T(2,128)(2,1)}, u32[]{:S(2)}) copy-start(bf16[128,2,256]{2,1,0:T(2,128)(2,1)} %bc.23) | copy-start | bytes 393220
  0.0 1.5 %copy-start.2 = (f32[4,2048]{1,0:T(4,128)S(1)}, f32[4,2048]{1,0:T(4,128)}, u32[]{:S(2)}) copy-start(f32[4,2048]{1,0:T(4,128)} %taps_x.21) | copy-start | bytes 98308
  0.0 1.5 %copy-start.3 = (f32[4,2,256]{2,1,0:T(2,128)S(1)}, f32[4,2,256]{2,1,0:T(2,128)}, u32[]{:S(2)}) copy-start(f32[4,2,256]{2,1,0:T(2,128)} %taps_bc.21) | copy-start | bytes 24580
  0.1 10.3 %collective-permute-start.1 = (bf16[160,384]{1,0:T(8,128)(2,1)S(1)}, bf16[160,384]{1,0:T(8,128)(2,1)S(1)}, u32[]{:S(2)}, u32[]{:S(2)}) collective-permute-start(bf16[160,384]{1,0:T(8,128)(2,1)S(1)} %get-tuple-element.30._), channel_id=1, source_target_pairs={{0,4},{1,5},{2,6},{3,7},{16,20},{17,21},{18,22},{19,23}} | collective-permute-start | bytes 368648 | tf_op jit(solution)/shard_map/ppermute | solution.py:400
  1.6 1.4 %copy-start.10 = (f32[128,32]{0,1:T(8,128)S(1)}, f32[128,32]{0,1:T(8,128)}, u32[]{:S(2)}) copy-start(f32[128,32]{0,1:T(8,128)} %param.12) | copy-start | bytes 49156
  1.6 1.4 %copy-start.20 = (f32[2048]{0:T(1024)S(1)}, f32[2048]{0:T(1024)}, u32[]{:S(2)}) copy-start(f32[2048]{0:T(1024)} %param.17) | copy-start | bytes 24580
  1.6 11.5 %collective-permute-start.2 = (bf16[128,640]{1,0:T(8,128)(2,1)S(1)}, bf16[128,640]{1,0:T(8,128)(2,1)S(1)}, u32[]{:S(2)}, u32[]{:S(2)}) collective-permute-start(bf16[128,640]{1,0:T(8,128)(2,1)S(1)} %next_states.3._), channel_id=1, source_target_pairs={{0,4},{1,5},{2,6},{3,7},{16,20},{17,21},{18,22},{19,23}} | collective-permute-start | bytes 491528 | tf_op jit(solution)/shard_map/ppermute | solution.py:400
  2.9 0.7 %copy-start.25 = (f32[32]{0:T(128)S(1)}, f32[32]{0:T(128)}, u32[]{:S(2)}) copy-start(f32[32]{0:T(128)} %param.15) | copy-start | bytes 388
  2.9 0.7 %copy-start.27 = (f32[32]{0:T(128)S(1)}, f32[32]{0:T(128)}, u32[]{:S(2)}) copy-start(f32[32]{0:T(128)} %param.16) | copy-start | bytes 388
  4.8 0.5 %copy-start.28 = (f32[1,32]{1,0:T(1,128)}, f32[1,32]{1,0:T(1,128)S(1)}, u32[]{:S(2)}) copy-start(f32[1,32]{1,0:T(1,128)S(1)} %get-tuple-element.47.refs_10_) | copy-start | bytes 388
  5.3 10.3 %copy-start.23 = (f32[1,512]{1,0:T(1,128)}, f32[1,512]{1,0:T(1,128)S(1)}, u32[]{:S(2)}) copy-start(f32[1,512]{1,0:T(1,128)S(1)} %get-tuple-element.40) | copy-start | bytes 6148
  5.3 13.2 %copy-start.21 = (f32[1,512]{1,0:T(1,128)}, f32[1,512]{1,0:T(1,128)S(1)}, u32[]{:S(2)}) copy-start(f32[1,512]{1,0:T(1,128)S(1)} %get-tuple-element.39) | copy-start | bytes 6148
  5.3 13.2 %collective-permute-start = (bf16[8,2560]{1,0:T(8,128)(2,1)}, bf16[8,2560]{1,0:T(8,128)(2,1)S(1)}, u32[]{:S(2)}, u32[]{:S(2)}) collective-permute-start(bf16[8,2560]{1,0:T(8,128)(2,1)} %get-tuple-element.38._), channel_id=1, source_target_pairs={{4,8},{5,9},{6,10},{7,11},{20,24},{21,25},{22,26},{23,27}} | collective-permute-start | bytes 122888 | tf_op jit(solution)/shard_map/ppermute | solution.py:400
  7.7 7.9 %collective-permute-start.6 = (bf16[128,512]{1,0:T(8,128)(2,1)S(1)}, bf16[128,512]{1,0:T(8,128)(2,1)S(1)}, u32[]{:S(2)}, u32[]{:S(2)}) collective-permute-start(bf16[128,512]{1,0:T(8,128)(2,1)S(1)} %next_states.4._), channel_id=1, source_target_pairs={{0,4},{1,5},{2,6},{3,7},{16,20},{17,21},{18,22},{19,23}} | collective-permute-start | bytes 393224 | tf_op jit(solution)/shard_map/ppermute | solution.py:400
  9.0 8.4 %collective-permute-start.5 = (bf16[128,512]{1,0:T(8,128)(2,1)S(1)}, bf16[128,512]{1,0:T(8,128)(2,1)S(1)}, u32[]{:S(2)}, u32[]{:S(2)}) collective-permute-start(bf16[128,512]{1,0:T(8,128)(2,1)S(1)} %next_states.5), channel_id=1, source_target_pairs={{0,4},{1,5},{2,6},{3,7},{16,20},{17,21},{18,22},{19,23}} | collective-permute-start | bytes 393224 | tf_op jit(solution)/shard_map/ppermute | solution.py:400
  10.3 2.7 %copy-start.30 = (f32[640]{0:T(1024)}, f32[640]{0:T(1024)S(1)}, u32[]{:S(2)}) copy-start(f32[640]{0:T(1024)S(1)} %reduce) | copy-start | bytes 7684
  10.8 9.1 %collective-permute-start.4 = (bf16[128,384]{1,0:T(8,128)(2,1)S(1)}, bf16[128,384]{1,0:T(8,128)(2,1)S(1)}, u32[]{:S(2)}, u32[]{:S(2)}) collective-permute-start(bf16[128,384]{1,0:T(8,128)(2,1)S(1)} %add_convert_fusion.7._), channel_id=1, source_target_pairs={{4,8},{5,9},{6,10},{7,11},{20,24},{21,25},{22,26},{23,27}} | collective-permute-start | bytes 294920 | tf_op jit(solution)/shard_map/ppermute | solution.py:400
  13.1 10.8 %collective-permute-start.8 = (bf16[128,640]{1,0:T(8,128)(2,1)S(1)}, bf16[128,640]{1,0:T(8,128)(2,1)S(1)}, u32[]{:S(2)}, u32[]{:S(2)}) collective-permute-start(bf16[128,640]{1,0:T(8,128)(2,1)S(1)} %add_convert_fusion.1._), channel_id=1, source_target_pairs={{4,8},{5,9},{6,10},{7,11},{20,24},{21,25},{22,26},{23,27}} | collective-permute-start | bytes 491528 | tf_op jit(solution)/shard_map/ppermute | solution.py:400
  15.6 10.4 %collective-permute-start.7 = (bf16[128,512]{1,0:T(8,128)(2,1)S(1)}, bf16[128,512]{1,0:T(8,128)(2,1)S(1)}, u32[]{:S(2)}, u32[]{:S(2)}) collective-permute-start(bf16[128,512]{1,0:T(8,128)(2,1)S(1)} %add_convert_fusion.5), channel_id=1, source_target_pairs={{4,8},{5,9},{6,10},{7,11},{20,24},{21,25},{22,26},{23,27}} | collective-permute-start | bytes 393224 | tf_op jit(solution)/shard_map/ppermute | solution.py:400
  17.3 10.7 %collective-permute-start.3 = (bf16[8,2560]{1,0:T(8,128)(2,1)}, bf16[8,2560]{1,0:T(8,128)(2,1)S(1)}, u32[]{:S(2)}, u32[]{:S(2)}) collective-permute-start(bf16[8,2560]{1,0:T(8,128)(2,1)} %get-tuple-element.38._), channel_id=1, source_target_pairs={{8,12},{9,13},{10,14},{11,15},{24,28},{25,29},{26,30},{27,31}} | collective-permute-start | bytes 122888 | tf_op jit(solution)/shard_map/ppermute | solution.py:400
  18.5 9.6 %collective-permute-start.10 = (bf16[128,512]{1,0:T(8,128)(2,1)S(1)}, bf16[128,512]{1,0:T(8,128)(2,1)S(1)}, u32[]{:S(2)}, u32[]{:S(2)}) collective-permute-start(bf16[128,512]{1,0:T(8,128)(2,1)S(1)} %add_convert_fusion.4._), channel_id=1, source_target_pairs={{4,8},{5,9},{6,10},{7,11},{20,24},{21,25},{22,26},{23,27}} | collective-permute-start | bytes 393224 | tf_op jit(solution)/shard_map/ppermute | solution.py:400
  19.9 1.3 %copy-start.11 = (f32[128,32]{0,1:T(8,128)S(1)}, f32[128,32]{0,1:T(8,128)}, u32[]{:S(2)}) copy-start(f32[128,32]{0,1:T(8,128)} %param.12) | copy-start | bytes 49156
  19.9 1.3 %copy-start.26 = (f32[32]{0:T(128)S(1)}, f32[32]{0:T(128)}, u32[]{:S(2)}) copy-start(f32[32]{0:T(128)} %param.15) | copy-start | bytes 388
  19.9 0.6 %copy-start.8 = (bf16[128,384]{1,0:T(8,128)(2,1)}, bf16[128,384]{1,0:T(8,128)(2,1)S(1)}, u32[]{:S(2)}) copy-start(bf16[128,384]{1,0:T(8,128)(2,1)S(1)} %collective-permute-done.4.refs_1_) | copy-start | bytes 294916
  20.6 7.5 %collective-permute-start.11 = (bf16[128,384]{1,0:T(8,128)(2,1)S(1)}, bf16[128,384]{1,0:T(8,128)(2,1)S(1)}, u32[]{:S(2)}, u32[]{:S(2)}) collective-permute-start(bf16[128,384]{1,0:T(8,128)(2,1)S(1)} %add_convert_fusion.6._), channel_id=1, source_target_pairs={{8,12},{9,13},{10,14},{11,15},{24,28},{25,29},{26,30},{27,31}} | collective-permute-start | bytes 294920 | tf_op jit(solution)/shard_map/ppermute | solution.py:400
  21.3 2.6 %copy-start.31 = (f32[640]{0:T(1024)S(1)}, f32[640]{0:T(1024)}, u32[]{:S(2)}) copy-start(f32[640]{0:T(1024)} %copy-done.30) | copy-start | bytes 7684
  22.7 0.6 %copy-start.16 = (f32[32,128]{1,0:T(8,128)}, f32[32,128]{1,0:T(8,128)S(1)}, u32[]{:S(2)}) copy-start(f32[32,128]{1,0:T(8,128)S(1)} %get-tuple-element.45.refs_8_) | copy-start | bytes 49156
  23.3 0.6 %copy-start.18 = (f32[32,128]{1,0:T(8,128)}, f32[32,128]{1,0:T(8,128)S(1)}, u32[]{:S(2)}) copy-start(f32[32,128]{1,0:T(8,128)S(1)} %get-tuple-element.46.refs_9_) | copy-start | bytes 49156
  23.9 2.2 %copy-start.24 = (f32[1,512]{1,0:T(1,128)S(1)}, f32[1,512]{1,0:T(1,128)}, u32[]{:S(2)}) copy-start(f32[1,512]{1,0:T(1,128)} %copy-done.23) | copy-start | bytes 6148
  24.6 3.5 %copy-start.22 = (f32[1,512]{1,0:T(1,128)S(1)}, f32[1,512]{1,0:T(1,128)}, u32[]{:S(2)}) copy-start(f32[1,512]{1,0:T(1,128)} %copy-done.21) | copy-start | bytes 6148
  24.6 12.4 %collective-permute-start.13 = (bf16[128,640]{1,0:T(8,128)(2,1)}, bf16[128,640]{1,0:T(8,128)(2,1)}, u32[]{:S(2)}, u32[]{:S(2)}) collective-permute-start(bf16[128,640]{1,0:T(8,128)(2,1)} %add_convert_fusion), channel_id=1, source_target_pairs={{8,12},{9,13},{10,14},{11,15},{24,28},{25,29},{26,30},{27,31}} | collective-permute-start | bytes 491528 | tf_op jit(solution)/shard_map/ppermute | solution.py:400
  26.1 0.7 %copy-start.6 = (bf16[128,512]{1,0:T(8,128)(2,1)}, bf16[128,512]{1,0:T(8,128)(2,1)S(1)}, u32[]{:S(2)}) copy-start(bf16[128,512]{1,0:T(8,128)(2,1)S(1)} %collective-permute-done.7.refs_1_) | copy-start | bytes 393220
  26.8 8.4 %collective-permute-start.9 = (bf16[128,512]{1,0:T(8,128)(2,1)}, bf16[128,512]{1,0:T(8,128)(2,1)}, u32[]{:S(2)}, u32[]{:S(2)}) collective-permute-start(bf16[128,512]{1,0:T(8,128)(2,1)} %add_convert_fusion.3), channel_id=1, source_target_pairs={{8,12},{9,13},{10,14},{11,15},{24,28},{25,29},{26,30},{27,31}} | collective-permute-start | bytes 393224 | tf_op jit(solution)/shard_map/ppermute | solution.py:400
  28.1 0.8 %copy-start.14 = (bf16[8,2560]{1,0:T(8,128)(2,1)}, bf16[8,2560]{1,0:T(8,128)(2,1)S(1)}, u32[]{:S(2)}) copy-start(bf16[8,2560]{1,0:T(8,128)(2,1)S(1)} %collective-permute-done.3.refs_2_) | copy-start | bytes 122884
  28.1 0.8 %copy-start.4 = (bf16[128,512]{1,0:T(8,128)(2,1)}, bf16[128,512]{1,0:T(8,128)(2,1)S(1)}, u32[]{:S(2)}) copy-start(bf16[128,512]{1,0:T(8,128)(2,1)S(1)} %collective-permute-done.10.refs_2_) | copy-start | bytes 393220
  28.1 0.7 %copy-start.12 = (bf16[128,384]{1,0:T(8,128)(2,1)}, bf16[128,384]{1,0:T(8,128)(2,1)S(1)}, u32[]{:S(2)}) copy-start(bf16[128,384]{1,0:T(8,128)(2,1)S(1)} %collective-permute-done.11.refs_2_) | copy-start | bytes 294916
  28.9 10.2 %collective-permute-start.12 = (bf16[128,512]{1,0:T(8,128)(2,1)}, bf16[128,512]{1,0:T(8,128)(2,1)}, u32[]{:S(2)}, u32[]{:S(2)}) collective-permute-start(bf16[128,512]{1,0:T(8,128)(2,1)} %add_convert_fusion.2), channel_id=1, source_target_pairs={{8,12},{9,13},{10,14},{11,15},{24,28},{25,29},{26,30},{27,31}} | collective-permute-start | bytes 393224 | tf_op jit(solution)/shard_map/ppermute | solution.py:400
  30.2 0.6 %copy-start.29 = (f32[1,32]{1,0:T(1,128)S(1)}, f32[1,32]{1,0:T(1,128)}, u32[]{:S(2)}) copy-start(f32[1,32]{1,0:T(1,128)} %copy-done.28) | copy-start | bytes 388
  30.8 0.8 %copy-start.15 = (bf16[8,2560]{1,0:T(8,128)(2,1)S(1)}, bf16[8,2560]{1,0:T(8,128)(2,1)}, u32[]{:S(2)}) copy-start(bf16[8,2560]{1,0:T(8,128)(2,1)} %copy-done.14) | copy-start | bytes 122884
  31.6 0.7 %copy-start.17 = (f32[32,128]{1,0:T(8,128)S(1)}, f32[32,128]{1,0:T(8,128)}, u32[]{:S(2)}) copy-start(f32[32,128]{1,0:T(8,128)} %copy-done.16) | copy-start | bytes 49156
  32.3 0.7 %copy-start.19 = (f32[32,128]{1,0:T(8,128)S(1)}, f32[32,128]{1,0:T(8,128)}, u32[]{:S(2)}) copy-start(f32[32,128]{1,0:T(8,128)} %copy-done.18) | copy-start | bytes 49156
  33.0 1.9 %copy-start.9 = (bf16[128,384]{1,0:T(8,128)(2,1)S(1)}, bf16[128,384]{1,0:T(8,128)(2,1)}, u32[]{:S(2)}) copy-start(bf16[128,384]{1,0:T(8,128)(2,1)} %copy-done.8) | copy-start | bytes 294916
  33.0 1.9 %copy-start.13 = (bf16[128,384]{1,0:T(8,128)(2,1)S(1)}, bf16[128,384]{1,0:T(8,128)(2,1)}, u32[]{:S(2)}) copy-start(bf16[128,384]{1,0:T(8,128)(2,1)} %copy-done.12) | copy-start | bytes 294916
  35.0 0.9 %copy-start.7 = (bf16[128,512]{1,0:T(8,128)(2,1)S(1)}, bf16[128,512]{1,0:T(8,128)(2,1)}, u32[]{:S(2)}) copy-start(bf16[128,512]{1,0:T(8,128)(2,1)} %copy-done.6) | copy-start | bytes 393220
  38.1 0.9 %copy-start.5 = (bf16[128,512]{1,0:T(8,128)(2,1)S(1)}, bf16[128,512]{1,0:T(8,128)(2,1)}, u32[]{:S(2)}) copy-start(bf16[128,512]{1,0:T(8,128)(2,1)} %copy-done.4) | copy-start | bytes 393220

commit v14 on v13

--- a/solution.py
+++ b/solution.py
@@ -407,7 +407,7 @@
             out_shape=[jax.ShapeDtypeStruct((state_dim + extra, high - low), BF16), scale_shape],
             in_specs=[scalar] + in_hbm,
             scratch_shapes=landed + [pltpu.SemaphoreType.DMA((len(operands),))],
-            compiler_params=params(6),
+            compiler_params=params(8),
             name="first_states",
         )(here(place == 0), *pinned)
 
@@ -416,7 +416,7 @@
             functools.partial(next_kernel, low, high),
             out_shape=jax.ShapeDtypeStruct((state_dim, high - low), BF16),
             in_specs=[scalar, anywhere] + [in_vmem] * (len(sources) + 1),
-            compiler_params=params(6),
+            compiler_params=params(8),
             name="next_states",
         )(here(place == 0), token, *sources, scale)
 
@@ -431,7 +431,7 @@
             ]
             + [jax.ShapeDtypeStruct((1, high - low), F32) for low, high in cuts],
             in_specs=[anywhere] + [in_vmem] * 6,
-            compiler_params=params(6),
+            compiler_params=params(8),
             name="prepared",
         )(token, x_in, bc_in, dt_t, a_row, gain, d_row)
 
@@ -440,7 +440,7 @@
             functools.partial(later_kernel, low, high),
             out_shape=jax.ShapeDtypeStruct((state_dim, high - low), F32),
             in_specs=[scalar, in_vmem, anywhere] + [in_vmem] * (len(sources) + 1),
-            compiler_params=params(6),
+            compiler_params=params(8),
             name="later_states",
         )(here(condition), rows, token, *sources, scale)
 
@@ -450,11 +450,11 @@
         return pl.pallas_call(
             functools.partial(gate_kernel, groups),
             out_shape=[scale_shape, scale_shape, per_head, per_head],
-            in_specs=[anywhere, pl.BlockSpec(memory_space=pltpu.HBM)] + [in_vmem] * 2,
+            in_specs=[anywhere, anywhere] + [in_vmem] * 2,
             scratch_shapes=[pltpu.VMEM(z_in.shape, z_in.dtype), pltpu.SemaphoreType.DMA],
-            compiler_params=params(6),
+            compiler_params=params(8),
             name="gates",
-        )(token, pltpu.with_memory_space_constraint(z_in, pltpu.HBM), dt_t, a_row)
+        )(token, z_in, dt_t, a_row)
 
     def intra(befores, gate, dt, cum, skip):
         return pl.pallas_call(
@@ -463,7 +463,7 @@
                 scale_shape, jax.ShapeDtypeStruct((tokens, groups * state_dim), BF16)
             ],
             in_specs=[in_vmem] * (len(befores) + 8),
-            compiler_params=params(10),
+            compiler_params=params(16),
             cost_estimate=pl.CostEstimate(
                 flops=4 * tokens * tokens * width,
                 bytes_accessed=12 * tokens * width,
@@ -533,7 +533,7 @@
                 functools.partial(gated_kernel, low),
                 out_shape=jax.ShapeDtypeStruct((tokens, high - low), F32),
                 in_specs=common_specs + [in_vmem] * len(seen),
-                compiler_params=params(6),
+                compiler_params=params(8),
                 name="gated",
             )(*common, *seen)
         )
@@ -566,7 +566,7 @@
                 pltpu.SemaphoreType.DMA((len(cuts) + groups,)),
             ],
             input_output_aliases=aliases,
-            compiler_params=params(6),
+            compiler_params=params(8),
             name="outputs",
         )(*common, gain, *inputs)
     return out

time: 41.7 us -> 41.3 us (level)
  Pallas kernels: 11.7 us -> 11.2 us
    pallas_call x1, Pallas kernels: 1.37 us -> 0.91 us  [gates(): pl.pallas_call(functools.partial(gate_kernel, groups), out_shape=[scale_s...]
    unnamed x64 -> x66, local copies, waits for them, and re-layouts: 6.58 us -> 6.66 us
  transfers between devices with their start and end apart: 14 -> 14, of which waited for: 2 -> 2; matrix products, arithmetic and copies ran while one was open for 6% -> 6% of each run, Pallas kernels for 24% -> 23%
where the time goes in v14:
time: 41.3 us; the launch traced here: 40.6 us
  starting transfers between devices  18.2 us (44%)
  Pallas kernels  11.2 us (27%)
  local copies, waits for them, and re-layouts  6.66 us (16%)
  other arithmetic  2.38 us (6%)
  waiting for transfers between devices  1.59 us (4%)
  between operations  0.56 us (1%)
    ppermute x14, starting transfers between devices, shifted(): return lax.ppermute(value, 'seq', route)  18.2 us
    unnamed x66, local copies, waits for them, and re-layouts  6.66 us
    pallas_call x2, Pallas kernels, shards(): pl.pallas_call(functools.partial(output_kernel, begin, spans, unready), o...  2.88 us
    pallas_call x3, Pallas kernels, shards(): pl.pallas_call(functools.partial(gated_kernel, low), out_shape=jax.ShapeD...  2.4 us
    convert_element_type x8, other arithmetic, shards(): token = joined.astype(BF16)  2.35 us
    pallas_call x1, Pallas kernels, intra(): pl.pallas_call(functools.partial(intra_kernel, len(befores)), out_shape=[...  1.9 us
    pallas_call x8, Pallas kernels, later_states(): pl.pallas_call(functools.partial(later_kernel, low, high), out_shape=jax....  1.84 us
    ppermute x14, waiting for transfers between devices, shifted(): return lax.ppermute(value, 'seq', route)  1.59 us
  transfers between devices with their start and end apart: 14, of which 2 were waited for; matrix products, arithmetic and copies ran while one was open for 6% of the time, Pallas kernels for 23%

profile of v14, /device:TPU:8, one launch (start us, length us, event | category | flops | bytes accessed | tf_op | source)
XLA Modules:
  0.0 40.6 jit_solution(10177952321023403717)
XLA Ops:
  0.0 0.1 first_states.1
  0.1 1.4 %collective-permute-start.1 = (bf16[160,384]{1,0:T(8,128)(2,1)S(1)}, bf16[160,384]{1,0:T(8,128)(2,1)S(1)}, u32[]{:S(2)}, u32[]{:S(2)}) collective-permute-start(bf16[160,384]{1,0:T(8,128)(2,1)S(1)} %get-tuple-element.30._), channel_id=1, source_target_pairs={{0,4},{1,5},{2,6},{3,7},{16,20},{17,21},{18,22},{19,23}} | collective-permute-start | bytes 368648 | tf_op jit(solution)/shard_map/ppermute | solution.py:400
  1.6 0.0 copy-start.11
  1.6 0.0 copy-start.21
  1.6 1.3 %collective-permute-start.2 = (bf16[128,640]{1,0:T(8,128)(2,1)S(1)}, bf16[128,640]{1,0:T(8,128)(2,1)S(1)}, u32[]{:S(2)}, u32[]{:S(2)}) collective-permute-start(bf16[128,640]{1,0:T(8,128)(2,1)S(1)} %next_states.3._), channel_id=1, source_target_pairs={{0,4},{1,5},{2,6},{3,7},{16,20},{17,21},{18,22},{19,23}} | collective-permute-start | bytes 491528 | tf_op jit(solution)/shard_map/ppermute | solution.py:400
  2.9 0.6 %copy-done.26 = f32[32]{0:T(128)S(1)} copy-done((f32[32]{0:T(128)S(1)}, f32[32]{0:T(128)}, u32[]{:S(2)}) %copy-start.26) | copy-done | bytes 152
  3.6 0.0 copy-done.28
  3.6 1.2 %prepared.1 = (bf16[8,2560]{1,0:T(8,128)(2,1)}, f32[1,2048]{1,0:T(1,128)S(1)}, f32[1,32]{1,0:T(1,128)S(1)}, f32[128,2048]{1,0:T(8,128)S(1)}, f32[1,384]{1,0:T(1,...) custom-call(bf16[128,640]{1,0:T(8,128)(2,1)S(1)} %next_states.3._, ...), custom_call_target="tpu_custom_call" | custom-call | tf_op jit(solution)/shard_map/prepared/pallas_call | solution.py:424
  4.8 0.6 %copy-done.29 = f32[1,32]{1,0:T(1,128)} copy-done((f32[1,32]{1,0:T(1,128)}, f32[1,32]{1,0:T(1,128)S(1)}, u32[]{:S(2)}) %copy-start.29) | copy-done | bytes 152
  5.3 2.3 %collective-permute-start = (bf16[8,2560]{1,0:T(8,128)(2,1)}, bf16[8,2560]{1,0:T(8,128)(2,1)S(1)}, u32[]{:S(2)}, u32[]{:S(2)}) collective-permute-start(bf16[8,2560]{1,0:T(8,128)(2,1)} %get-tuple-element.38._), channel_id=1, source_target_pairs={{4,8},{5,9},{6,10},{7,11},{20,24},{21,25},{22,26},{23,27}} | collective-permute-start | bytes 122888 | tf_op jit(solution)/shard_map/ppermute | solution.py:400
  7.7 1.3 %collective-permute-start.6 = (bf16[128,512]{1,0:T(8,128)(2,1)S(1)}, bf16[128,512]{1,0:T(8,128)(2,1)S(1)}, u32[]{:S(2)}, u32[]{:S(2)}) collective-permute-start(bf16[128,512]{1,0:T(8,128)(2,1)S(1)} %next_states.4._), channel_id=1, source_target_pairs={{0,4},{1,5},{2,6},{3,7},{16,20},{17,21},{18,22},{19,23}} | collective-permute-start | bytes 393224 | tf_op jit(solution)/shard_map/ppermute | solution.py:400
  9.0 1.3 %collective-permute-start.5 = (bf16[128,512]{1,0:T(8,128)(2,1)S(1)}, bf16[128,512]{1,0:T(8,128)(2,1)S(1)}, u32[]{:S(2)}, u32[]{:S(2)}) collective-permute-start(bf16[128,512]{1,0:T(8,128)(2,1)S(1)} %next_states.5), channel_id=1, source_target_pairs={{0,4},{1,5},{2,6},{3,7},{16,20},{17,21},{18,22},{19,23}} | collective-permute-start | bytes 393224 | tf_op jit(solution)/shard_map/ppermute | solution.py:400
  10.4 0.0 copy-start.31
  10.4 0.4 later_states.8
  10.8 1.3 %collective-permute-start.4 = (bf16[128,384]{1,0:T(8,128)(2,1)S(1)}, bf16[128,384]{1,0:T(8,128)(2,1)S(1)}, u32[]{:S(2)}, u32[]{:S(2)}) collective-permute-start(bf16[128,384]{1,0:T(8,128)(2,1)S(1)} %add_convert_fusion.7._), channel_id=1, source_target_pairs={{4,8},{5,9},{6,10},{7,11},{20,24},{21,25},{22,26},{23,27}} | collective-permute-start | bytes 294920 | tf_op jit(solution)/shard_map/ppermute | solution.py:400
  12.1 0.5 %later_states.10 = f32[128,512]{1,0:T(8,128)S(1)} custom-call(s32[1]{0:T(128)} %bitcast.6.active, bf16[160,384]{1,0:T(8,128)(2,1)S(1)} %collective-permute-done.1.rows.refs_1_.refs_0_, bf16[128,384]{1,0:T(8,128)(2,1)S(1)} %add_convert_fusion.7._, bf16[128,2048]{1,0:T(8,128)(2,1)S(1)} %copy-done, bf16[128,2,256]{2,1,0:T(2,128)(2,1)S(1)} %copy-done.1, ...), custom_call_target="tpu_custom_call" | custom-call | tf_op jit(solution)/shard_map/later_states/pallas_call | solution.py:439
  12.6 0.5 %later_states.9 = f32[128,640]{1,0:T(8,128)S(1)} custom-call(s32[1]{0:T(128)} %bitcast.6.active, bf16[160,384]{1,0:T(8,128)(2,1)S(1)} %collective-permute-done.1.rows.refs_1_.refs_0_, bf16[128,384]{1,0:T(8,128)(2,1)S(1)} %add_convert_fusion.7._, bf16[128,2048]{1,0:T(8,128)(2,1)S(1)} %copy-done, bf16[128,2,256]{2,1,0:T(2,128)(2,1)S(1)} %copy-done.1, ...), custom_call_target="tpu_custom_call" | custom-call | tf_op jit(solution)/shard_map/later_states/pallas_call | solution.py:439
  13.1 0.1 add_convert_fusion.1._
  13.2 1.3 %collective-permute-start.8 = (bf16[128,640]{1,0:T(8,128)(2,1)S(1)}, bf16[128,640]{1,0:T(8,128)(2,1)S(1)}, u32[]{:S(2)}, u32[]{:S(2)}) collective-permute-start(bf16[128,640]{1,0:T(8,128)(2,1)S(1)} %add_convert_fusion.1._), channel_id=1, source_target_pairs={{4,8},{5,9},{6,10},{7,11},{20,24},{21,25},{22,26},{23,27}} | collective-permute-start | bytes 491528 | tf_op jit(solution)/shard_map/ppermute | solution.py:400
  14.5 1.2 %collective-permute-done.6.refs_0_ = bf16[128,512]{1,0:T(8,128)(2,1)S(1)} collective-permute-done((bf16[128,512]{1,0:T(8,128)(2,1)S(1)}, bf16[128,512]{1,0:T(8,128)(2,1)S(1)}, u32[]{:S(2)}, u32[]{:S(2)}) %collective-permute-start.6) | collective-permute-done | bytes 131104 | tf_op jit(solution)/shard_map/ppermute | solution.py:400
  15.7 1.3 %collective-permute-start.7 = (bf16[128,512]{1,0:T(8,128)(2,1)S(1)}, bf16[128,512]{1,0:T(8,128)(2,1)S(1)}, u32[]{:S(2)}, u32[]{:S(2)}) collective-permute-start(bf16[128,512]{1,0:T(8,128)(2,1)S(1)} %add_convert_fusion.5), channel_id=1, source_target_pairs={{4,8},{5,9},{6,10},{7,11},{20,24},{21,25},{22,26},{23,27}} | collective-permute-start | bytes 393224 | tf_op jit(solution)/shard_map/ppermute | solution.py:400
  17.0 0.4 collective-permute-done.5.refs_1_
  17.4 0.7 %collective-permute-start.3 = (bf16[8,2560]{1,0:T(8,128)(2,1)}, bf16[8,2560]{1,0:T(8,128)(2,1)S(1)}, u32[]{:S(2)}, u32[]{:S(2)}) collective-permute-start(bf16[8,2560]{1,0:T(8,128)(2,1)} %get-tuple-element.38._), channel_id=1, source_target_pairs={{8,12},{9,13},{10,14},{11,15},{24,28},{25,29},{26,30},{27,31}} | collective-permute-start | bytes 122888 | tf_op jit(solution)/shard_map/ppermute | solution.py:400
  18.0 0.5 %later_states.11 = f32[128,512]{1,0:T(8,128)S(1)} custom-call(s32[1]{0:T(128)} %bitcast.6.active, bf16[160,384]{1,0:T(8,128)(2,1)S(1)} %collective-permute-done.1.rows.refs_1_.refs_0_, bf16[128,640]{1,0:T(8,128)(2,1)S(1)} %add_convert_fusion.1._, bf16[128,2048]{1,0:T(8,128)(2,1)S(1)} %copy-done, bf16[128,2,256]{2,1,0:T(2,128)(2,1)S(1)} %copy-done.1, ...), custom_call_target="tpu_custom_call" | custom-call | tf_op jit(solution)/shard_map/later_states/pallas_call | solution.py:439
  18.6 1.3 %collective-permute-start.10 = (bf16[128,512]{1,0:T(8,128)(2,1)S(1)}, bf16[128,512]{1,0:T(8,128)(2,1)S(1)}, u32[]{:S(2)}, u32[]{:S(2)}) collective-permute-start(bf16[128,512]{1,0:T(8,128)(2,1)S(1)} %add_convert_fusion.4._), channel_id=1, source_target_pairs={{4,8},{5,9},{6,10},{7,11},{20,24},{21,25},{22,26},{23,27}} | collective-permute-start | bytes 393224 | tf_op jit(solution)/shard_map/ppermute | solution.py:400
  19.9 0.0 copy-start.4
  20.0 0.6 %copy-done.9 = bf16[128,384]{1,0:T(8,128)(2,1)} copy-done((bf16[128,384]{1,0:T(8,128)(2,1)}, bf16[128,384]{1,0:T(8,128)(2,1)S(1)}, u32[]{:S(2)}) %copy-start.9) | copy-done | bytes 98328
  20.6 0.7 %collective-permute-start.11 = (bf16[128,384]{1,0:T(8,128)(2,1)S(1)}, bf16[128,384]{1,0:T(8,128)(2,1)S(1)}, u32[]{:S(2)}, u32[]{:S(2)}) collective-permute-start(bf16[128,384]{1,0:T(8,128)(2,1)S(1)} %add_convert_fusion.6._), channel_id=1, source_target_pairs={{8,12},{9,13},{10,14},{11,15},{24,28},{25,29},{26,30},{27,31}} | collective-permute-start | bytes 294920 | tf_op jit(solution)/shard_map/ppermute | solution.py:400
  21.3 0.9 %gates.1 = (f32[128,2048]{1,0:T(8,128)S(1)}, f32[128,2048]{1,0:T(8,128)S(1)}, f32[32,128]{1,0:T(8,128)S(1)}, f32[32,128]{1,0:T(8,128)S(1)}) custom-call(bf16[128,384]{1,0:T(8,128)(2,1)S(1)} %add_convert_fusion.6._, bf16[128,2048]{1,0:T(8,128)(2,1)S(1)} %copy-done.4, f32[32,128]{1,0:T(8,128)S(1)} %bitcast.12, f32[1,32]{1,0:T(1,128)S(1)} %bitcast.20), custom_call_target="tpu_custom_call" | custom-call | tf_op jit(solution)/shard_map/gates/pallas_call | solution.py:450
  22.3 0.6 %copy-done.17 = f32[32,128]{1,0:T(8,128)} copy-done((f32[32,128]{1,0:T(8,128)}, f32[32,128]{1,0:T(8,128)S(1)}, u32[]{:S(2)}) %copy-start.17) | copy-done | bytes 16408
  22.9 0.6 %copy-done.19 = f32[32,128]{1,0:T(8,128)} copy-done((f32[32,128]{1,0:T(8,128)}, f32[32,128]{1,0:T(8,128)S(1)}, u32[]{:S(2)}) %copy-start.19) | copy-done | bytes 16408
  23.5 0.7 %add_convert_fusion = bf16[128,640]{1,0:T(8,128)(2,1)} fusion(f32[128,640]{1,0:T(8,128)S(1)} %later_states.13, bf16[128,640]{1,0:T(8,128)(2,1)S(1)} %collective-permute-done.8.refs_1_, f32[640]{0:T(1024)S(1)} %copy-done.32), kind=kLoop, calls=%fused_computation | loop fusion | flops 327680 | bytes 657920 | tf_op jit(solution)/shard_map/convert_element_type | solution.py:506
  24.2 1.4 %collective-permute-start.13 = (bf16[128,640]{1,0:T(8,128)(2,1)}, bf16[128,640]{1,0:T(8,128)(2,1)}, u32[]{:S(2)}, u32[]{:S(2)}) collective-permute-start(bf16[128,640]{1,0:T(8,128)(2,1)} %add_convert_fusion), channel_id=1, source_target_pairs={{8,12},{9,13},{10,14},{11,15},{24,28},{25,29},{26,30},{27,31}} | collective-permute-start | bytes 491528 | tf_op jit(solution)/shard_map/ppermute | solution.py:400
  25.6 0.7 %add_convert_fusion.3 = bf16[128,512]{1,0:T(8,128)(2,1)} fusion(f32[128,512]{1,0:T(8,128)S(1)} %later_states.14, bf16[128,512]{1,0:T(8,128)(2,1)S(1)} %collective-permute-done.7.refs_1_, f32[512]{0:T(512)S(1)} %bitcast.17), kind=kLoop, calls=%fused_computation.3 | loop fusion | flops 262144 | bytes 526336 | tf_op jit(solution)/shard_map/convert_element_type | solution.py:506
  26.4 1.3 %collective-permute-start.9 = (bf16[128,512]{1,0:T(8,128)(2,1)}, bf16[128,512]{1,0:T(8,128)(2,1)}, u32[]{:S(2)}, u32[]{:S(2)}) collective-permute-start(bf16[128,512]{1,0:T(8,128)(2,1)} %add_convert_fusion.3), channel_id=1, source_target_pairs={{8,12},{9,13},{10,14},{11,15},{24,28},{25,29},{26,30},{27,31}} | collective-permute-start | bytes 393224 | tf_op jit(solution)/shard_map/ppermute | solution.py:400
  27.7 0.7 %add_convert_fusion.2 = bf16[128,512]{1,0:T(8,128)(2,1)} fusion(f32[128,512]{1,0:T(8,128)S(1)} %later_states.15, bf16[128,512]{1,0:T(8,128)(2,1)S(1)} %collective-permute-done.10.refs_2_, f32[512]{0:T(512)S(1)} %bitcast.15), kind=kLoop, calls=%fused_computation.2 | loop fusion | flops 262144 | bytes 526336 | tf_op jit(solution)/shard_map/convert_element_type | solution.py:506
  28.4 1.3 %collective-permute-start.12 = (bf16[128,512]{1,0:T(8,128)(2,1)}, bf16[128,512]{1,0:T(8,128)(2,1)}, u32[]{:S(2)}, u32[]{:S(2)}) collective-permute-start(bf16[128,512]{1,0:T(8,128)(2,1)} %add_convert_fusion.2), channel_id=1, source_target_pairs={{8,12},{9,13},{10,14},{11,15},{24,28},{25,29},{26,30},{27,31}} | collective-permute-start | bytes 393224 | tf_op jit(solution)/shard_map/ppermute | solution.py:400
  29.7 0.7 %copy-done.30 = f32[1,32]{1,0:T(1,128)S(1)} copy-done((f32[1,32]{1,0:T(1,128)S(1)}, f32[1,32]{1,0:T(1,128)}, u32[]{:S(2)}) %copy-start.30) | copy-done | bytes 152
  30.4 0.8 %copy-done.16 = bf16[8,2560]{1,0:T(8,128)(2,1)S(1)} copy-done((bf16[8,2560]{1,0:T(8,128)(2,1)S(1)}, bf16[8,2560]{1,0:T(8,128)(2,1)}, u32[]{:S(2)}) %copy-start.16) | copy-done | bytes 40984
  31.2 0.7 %copy-done.18 = f32[32,128]{1,0:T(8,128)S(1)} copy-done((f32[32,128]{1,0:T(8,128)S(1)}, f32[32,128]{1,0:T(8,128)}, u32[]{:S(2)}) %copy-start.18) | copy-done | bytes 16408
  31.9 0.7 %copy-done.20 = f32[32,128]{1,0:T(8,128)S(1)} copy-done((f32[32,128]{1,0:T(8,128)S(1)}, f32[32,128]{1,0:T(8,128)}, u32[]{:S(2)}) %copy-start.20) | copy-done | bytes 16408
  32.6 1.9 %intra.1 = (f32[128,2048]{1,0:T(8,128)S(1)}, bf16[128,256]{1,0:T(8,128)(2,1)S(1)}) custom-call(bf16[8,2560]{1,0:T(8,128)(2,1)S(1)} %collective-permute-done.rows.refs_0_, bf16[160,384]{1,0:T(8,128)(2,1)S(1)} %collective-permute-done.1.rows.refs_1_.refs_0_, bf16[8,2560]{1,0:T(8,128)(2,1)S(1)} %copy-done.16, bf16[128,2048]{1,0:T(8,128)(2,1)S(1)} %copy-done, ...), custom_call_target="tpu_custom_call" | custom-call | flops 134217728 | bytes 3145728 | tf_op jit(solution)/shard_map/intra/pallas_call | solution.py:460
  34.6 0.2 gated.4.refs_0_
  34.8 0.7 %copy-done.8 = bf16[128,512]{1,0:T(8,128)(2,1)S(1)} copy-done((bf16[128,512]{1,0:T(8,128)(2,1)S(1)}, bf16[128,512]{1,0:T(8,128)(2,1)}, u32[]{:S(2)}) %copy-start.8) | copy-done | bytes 131096
  35.5 1.1 %gated.3.refs_0_ = f32[128,512]{1,0:T(8,128)S(1)} custom-call(s32[1]{0:T(128)} %bitcast.which, bf16[128,256]{1,0:T(8,128)(2,1)S(1)} %get-tuple-element.48.c, f32[128,2048]{1,0:T(8,128)S(1)} %get-tuple-element.49.y_part, f32[128,2048]{1,0:T(8,128)S(1)} %get-tuple-element.50.lead, bf16[128,512]{1,0:T(8,128)(2,1)S(1)} %collective-permute-done.6.refs_0_, ...), custom_call_target="tpu_custom_call" | custom-call | tf_op jit(solution)/shard_map/gated/pallas_call | solution.py:532
  36.6 1.1 %gated.5.refs_1_ = f32[128,640]{1,0:T(8,128)S(1)} custom-call(s32[1]{0:T(128)} %bitcast.which, bf16[128,256]{1,0:T(8,128)(2,1)S(1)} %get-tuple-element.48.c, f32[128,2048]{1,0:T(8,128)S(1)} %get-tuple-element.49.y_part, f32[128,2048]{1,0:T(8,128)S(1)} %get-tuple-element.50.lead, bf16[128,640]{1,0:T(8,128)(2,1)S(1)} %collective-permute-done.2.refs_0_, ...), custom_call_target="tpu_custom_call" | custom-call | tf_op jit(solution)/shard_map/gated/pallas_call | solution.py:532
  37.7 0.9 %outputs.2.refs_4_ = bf16[128,2048]{1,0:T(8,128)(2,1)} custom-call(s32[1]{0:T(128)} %bitcast.which, bf16[128,256]{1,0:T(8,128)(2,1)S(1)} %get-tuple-element.48.c, f32[128,2048]{1,0:T(8,128)S(1)} %get-tuple-element.49.y_part, f32[128,2048]{1,0:T(8,128)S(1)} %get-tuple-element.50.lead, f32[1,2048]{1,0:T(1,128)S(1)} %get-tuple-element.51.gain, ...), custom_call_target="tpu_custom_call" | custom-call | tf_op jit(solution)/shard_map/outputs/pallas_call | solution.py:559
  38.7 2.0 %outputs.3 = bf16[128,2048]{1,0:T(8,128)(2,1)} custom-call(s32[1]{0:T(128)} %bitcast.which, bf16[128,256]{1,0:T(8,128)(2,1)S(1)} %get-tuple-element.48.c, f32[128,2048]{1,0:T(8,128)S(1)} %get-tuple-element.49.y_part, f32[128,2048]{1,0:T(8,128)S(1)} %get-tuple-element.50.lead, f32[1,2048]{1,0:T(1,128)S(1)} %get-tuple-element.51.gain, ...), custom_call_target="tpu_custom_call", output_to_operand_aliasing={{}: (9, {})} | custom-call | tf_op jit(solution)/shard_map/outputs/pallas_call | solution.py:559
  (76 shorter events, 0.4 us)
Async XLA Ops:
  0.0 1.5 %copy-start = (bf16[128,2048]{1,0:T(8,128)(2,1)S(1)}, bf16[128,2048]{1,0:T(8,128)(2,1)}, u32[]{:S(2)}) copy-start(bf16[128,2048]{1,0:T(8,128)(2,1)} %x.23) | copy-start | bytes 1572868
  0.0 1.5 %copy-start.1 = (bf16[128,2,256]{2,1,0:T(2,128)(2,1)S(1)}, bf16[128,2,256]{2,1,0:T(2,128)(2,1)}, u32[]{:S(2)}) copy-start(bf16[128,2,256]{2,1,0:T(2,128)(2,1)} %bc.23) | copy-start | bytes 393220
  0.0 1.5 %copy-start.2 = (f32[4,2048]{1,0:T(4,128)S(1)}, f32[4,2048]{1,0:T(4,128)}, u32[]{:S(2)}) copy-start(f32[4,2048]{1,0:T(4,128)} %taps_x.21) | copy-start | bytes 98308
  0.0 1.5 %copy-start.3 = (f32[4,2,256]{2,1,0:T(2,128)S(1)}, f32[4,2,256]{2,1,0:T(2,128)}, u32[]{:S(2)}) copy-start(f32[4,2,256]{2,1,0:T(2,128)} %taps_bc.21) | copy-start | bytes 24580
  0.1 10.3 %collective-permute-start.1 = (bf16[160,384]{1,0:T(8,128)(2,1)S(1)}, bf16[160,384]{1,0:T(8,128)(2,1)S(1)}, u32[]{:S(2)}, u32[]{:S(2)}) collective-permute-start(bf16[160,384]{1,0:T(8,128)(2,1)S(1)} %get-tuple-element.30._), channel_id=1, source_target_pairs={{0,4},{1,5},{2,6},{3,7},{16,20},{17,21},{18,22},{19,23}} | collective-permute-start | bytes 368648 | tf_op jit(solution)/shard_map/ppermute | solution.py:400
  1.6 1.4 %copy-start.11 = (f32[128,32]{0,1:T(8,128)S(1)}, f32[128,32]{0,1:T(8,128)}, u32[]{:S(2)}) copy-start(f32[128,32]{0,1:T(8,128)} %param.12) | copy-start | bytes 49156
  1.6 1.4 %copy-start.21 = (f32[2048]{0:T(1024)S(1)}, f32[2048]{0:T(1024)}, u32[]{:S(2)}) copy-start(f32[2048]{0:T(1024)} %param.17) | copy-start | bytes 24580
  1.6 11.5 %collective-permute-start.2 = (bf16[128,640]{1,0:T(8,128)(2,1)S(1)}, bf16[128,640]{1,0:T(8,128)(2,1)S(1)}, u32[]{:S(2)}, u32[]{:S(2)}) collective-permute-start(bf16[128,640]{1,0:T(8,128)(2,1)S(1)} %next_states.3._), channel_id=1, source_target_pairs={{0,4},{1,5},{2,6},{3,7},{16,20},{17,21},{18,22},{19,23}} | collective-permute-start | bytes 491528 | tf_op jit(solution)/shard_map/ppermute | solution.py:400
  2.9 0.7 %copy-start.26 = (f32[32]{0:T(128)S(1)}, f32[32]{0:T(128)}, u32[]{:S(2)}) copy-start(f32[32]{0:T(128)} %param.15) | copy-start | bytes 388
  2.9 0.7 %copy-start.28 = (f32[32]{0:T(128)S(1)}, f32[32]{0:T(128)}, u32[]{:S(2)}) copy-start(f32[32]{0:T(128)} %param.16) | copy-start | bytes 388
  4.8 0.6 %copy-start.29 = (f32[1,32]{1,0:T(1,128)}, f32[1,32]{1,0:T(1,128)S(1)}, u32[]{:S(2)}) copy-start(f32[1,32]{1,0:T(1,128)S(1)} %get-tuple-element.47.refs_10_) | copy-start | bytes 388
  5.3 10.3 %copy-start.24 = (f32[1,512]{1,0:T(1,128)}, f32[1,512]{1,0:T(1,128)S(1)}, u32[]{:S(2)}) copy-start(f32[1,512]{1,0:T(1,128)S(1)} %get-tuple-element.40) | copy-start | bytes 6148
  5.3 13.2 %copy-start.22 = (f32[1,512]{1,0:T(1,128)}, f32[1,512]{1,0:T(1,128)S(1)}, u32[]{:S(2)}) copy-start(f32[1,512]{1,0:T(1,128)S(1)} %get-tuple-element.39) | copy-start | bytes 6148
  5.3 13.2 %collective-permute-start = (bf16[8,2560]{1,0:T(8,128)(2,1)}, bf16[8,2560]{1,0:T(8,128)(2,1)S(1)}, u32[]{:S(2)}, u32[]{:S(2)}) collective-permute-start(bf16[8,2560]{1,0:T(8,128)(2,1)} %get-tuple-element.38._), channel_id=1, source_target_pairs={{4,8},{5,9},{6,10},{7,11},{20,24},{21,25},{22,26},{23,27}} | collective-permute-start | bytes 122888 | tf_op jit(solution)/shard_map/ppermute | solution.py:400
  7.7 7.9 %collective-permute-start.6 = (bf16[128,512]{1,0:T(8,128)(2,1)S(1)}, bf16[128,512]{1,0:T(8,128)(2,1)S(1)}, u32[]{:S(2)}, u32[]{:S(2)}) collective-permute-start(bf16[128,512]{1,0:T(8,128)(2,1)S(1)} %next_states.4._), channel_id=1, source_target_pairs={{0,4},{1,5},{2,6},{3,7},{16,20},{17,21},{18,22},{19,23}} | collective-permute-start | bytes 393224 | tf_op jit(solution)/shard_map/ppermute | solution.py:400
  9.0 8.4 %collective-permute-start.5 = (bf16[128,512]{1,0:T(8,128)(2,1)S(1)}, bf16[128,512]{1,0:T(8,128)(2,1)S(1)}, u32[]{:S(2)}, u32[]{:S(2)}) collective-permute-start(bf16[128,512]{1,0:T(8,128)(2,1)S(1)} %next_states.5), channel_id=1, source_target_pairs={{0,4},{1,5},{2,6},{3,7},{16,20},{17,21},{18,22},{19,23}} | collective-permute-start | bytes 393224 | tf_op jit(solution)/shard_map/ppermute | solution.py:400
  10.4 2.7 %copy-start.31 = (f32[640]{0:T(1024)}, f32[640]{0:T(1024)S(1)}, u32[]{:S(2)}) copy-start(f32[640]{0:T(1024)S(1)} %reduce) | copy-start | bytes 7684
  10.8 9.1 %collective-permute-start.4 = (bf16[128,384]{1,0:T(8,128)(2,1)S(1)}, bf16[128,384]{1,0:T(8,128)(2,1)S(1)}, u32[]{:S(2)}, u32[]{:S(2)}) collective-permute-start(bf16[128,384]{1,0:T(8,128)(2,1)S(1)} %add_convert_fusion.7._), channel_id=1, source_target_pairs={{4,8},{5,9},{6,10},{7,11},{20,24},{21,25},{22,26},{23,27}} | collective-permute-start | bytes 294920 | tf_op jit(solution)/shard_map/ppermute | solution.py:400
  13.2 10.3 %collective-permute-start.8 = (bf16[128,640]{1,0:T(8,128)(2,1)S(1)}, bf16[128,640]{1,0:T(8,128)(2,1)S(1)}, u32[]{:S(2)}, u32[]{:S(2)}) collective-permute-start(bf16[128,640]{1,0:T(8,128)(2,1)S(1)} %add_convert_fusion.1._), channel_id=1, source_target_pairs={{4,8},{5,9},{6,10},{7,11},{20,24},{21,25},{22,26},{23,27}} | collective-permute-start | bytes 491528 | tf_op jit(solution)/shard_map/ppermute | solution.py:400
  15.7 9.9 %collective-permute-start.7 = (bf16[128,512]{1,0:T(8,128)(2,1)S(1)}, bf16[128,512]{1,0:T(8,128)(2,1)S(1)}, u32[]{:S(2)}, u32[]{:S(2)}) collective-permute-start(bf16[128,512]{1,0:T(8,128)(2,1)S(1)} %add_convert_fusion.5), channel_id=1, source_target_pairs={{4,8},{5,9},{6,10},{7,11},{20,24},{21,25},{22,26},{23,27}} | collective-permute-start | bytes 393224 | tf_op jit(solution)/shard_map/ppermute | solution.py:400
  17.4 10.3 %collective-permute-start.3 = (bf16[8,2560]{1,0:T(8,128)(2,1)}, bf16[8,2560]{1,0:T(8,128)(2,1)S(1)}, u32[]{:S(2)}, u32[]{:S(2)}) collective-permute-start(bf16[8,2560]{1,0:T(8,128)(2,1)} %get-tuple-element.38._), channel_id=1, source_target_pairs={{8,12},{9,13},{10,14},{11,15},{24,28},{25,29},{26,30},{27,31}} | collective-permute-start | bytes 122888 | tf_op jit(solution)/shard_map/ppermute | solution.py:400
  18.6 9.1 %collective-permute-start.10 = (bf16[128,512]{1,0:T(8,128)(2,1)S(1)}, bf16[128,512]{1,0:T(8,128)(2,1)S(1)}, u32[]{:S(2)}, u32[]{:S(2)}) collective-permute-start(bf16[128,512]{1,0:T(8,128)(2,1)S(1)} %add_convert_fusion.4._), channel_id=1, source_target_pairs={{4,8},{5,9},{6,10},{7,11},{20,24},{21,25},{22,26},{23,27}} | collective-permute-start | bytes 393224 | tf_op jit(solution)/shard_map/ppermute | solution.py:400
  19.9 1.4 %copy-start.4 = (bf16[128,2048]{1,0:T(8,128)(2,1)S(1)}, bf16[128,2048]{1,0:T(8,128)(2,1)}, u32[]{:S(2)}) copy-start(bf16[128,2048]{1,0:T(8,128)(2,1)} %z_hbm.1) | copy-start | bytes 1572868
  20.0 1.3 %copy-start.12 = (f32[128,32]{0,1:T(8,128)S(1)}, f32[128,32]{0,1:T(8,128)}, u32[]{:S(2)}) copy-start(f32[128,32]{0,1:T(8,128)} %param.12) | copy-start | bytes 49156
  20.0 1.3 %copy-start.27 = (f32[32]{0:T(128)S(1)}, f32[32]{0:T(128)}, u32[]{:S(2)}) copy-start(f32[32]{0:T(128)} %param.15) | copy-start | bytes 388
  20.0 0.6 %copy-start.9 = (bf16[128,384]{1,0:T(8,128)(2,1)}, bf16[128,384]{1,0:T(8,128)(2,1)S(1)}, u32[]{:S(2)}) copy-start(bf16[128,384]{1,0:T(8,128)(2,1)S(1)} %collective-permute-done.4.refs_1_) | copy-start | bytes 294916
  20.6 7.0 %collective-permute-start.11 = (bf16[128,384]{1,0:T(8,128)(2,1)S(1)}, bf16[128,384]{1,0:T(8,128)(2,1)S(1)}, u32[]{:S(2)}, u32[]{:S(2)}) collective-permute-start(bf16[128,384]{1,0:T(8,128)(2,1)S(1)} %add_convert_fusion.6._), channel_id=1, source_target_pairs={{8,12},{9,13},{10,14},{11,15},{24,28},{25,29},{26,30},{27,31}} | collective-permute-start | bytes 294920 | tf_op jit(solution)/shard_map/ppermute | solution.py:400
  21.3 2.1 %copy-start.32 = (f32[640]{0:T(1024)S(1)}, f32[640]{0:T(1024)}, u32[]{:S(2)}) copy-start(f32[640]{0:T(1024)} %copy-done.31) | copy-start | bytes 7684
  22.2 0.6 %copy-start.17 = (f32[32,128]{1,0:T(8,128)}, f32[32,128]{1,0:T(8,128)S(1)}, u32[]{:S(2)}) copy-start(f32[32,128]{1,0:T(8,128)S(1)} %get-tuple-element.45.refs_8_) | copy-start | bytes 49156
  22.9 0.6 %copy-start.19 = (f32[32,128]{1,0:T(8,128)}, f32[32,128]{1,0:T(8,128)S(1)}, u32[]{:S(2)}) copy-start(f32[32,128]{1,0:T(8,128)S(1)} %get-tuple-element.46.refs_9_) | copy-start | bytes 49156
  23.5 2.2 %copy-start.25 = (f32[1,512]{1,0:T(1,128)S(1)}, f32[1,512]{1,0:T(1,128)}, u32[]{:S(2)}) copy-start(f32[1,512]{1,0:T(1,128)} %copy-done.24) | copy-start | bytes 6148
  24.2 3.5 %copy-start.23 = (f32[1,512]{1,0:T(1,128)S(1)}, f32[1,512]{1,0:T(1,128)}, u32[]{:S(2)}) copy-start(f32[1,512]{1,0:T(1,128)} %copy-done.22) | copy-start | bytes 6148
  24.2 12.4 %collective-permute-start.13 = (bf16[128,640]{1,0:T(8,128)(2,1)}, bf16[128,640]{1,0:T(8,128)(2,1)}, u32[]{:S(2)}, u32[]{:S(2)}) collective-permute-start(bf16[128,640]{1,0:T(8,128)(2,1)} %add_convert_fusion), channel_id=1, source_target_pairs={{8,12},{9,13},{10,14},{11,15},{24,28},{25,29},{26,30},{27,31}} | collective-permute-start | bytes 491528 | tf_op jit(solution)/shard_map/ppermute | solution.py:400
  25.6 0.7 %copy-start.7 = (bf16[128,512]{1,0:T(8,128)(2,1)}, bf16[128,512]{1,0:T(8,128)(2,1)S(1)}, u32[]{:S(2)}) copy-start(bf16[128,512]{1,0:T(8,128)(2,1)S(1)} %collective-permute-done.7.refs_1_) | copy-start | bytes 393220
  26.4 8.4 %collective-permute-start.9 = (bf16[128,512]{1,0:T(8,128)(2,1)}, bf16[128,512]{1,0:T(8,128)(2,1)}, u32[]{:S(2)}, u32[]{:S(2)}) collective-permute-start(bf16[128,512]{1,0:T(8,128)(2,1)} %add_convert_fusion.3), channel_id=1, source_target_pairs={{8,12},{9,13},{10,14},{11,15},{24,28},{25,29},{26,30},{27,31}} | collective-permute-start | bytes 393224 | tf_op jit(solution)/shard_map/ppermute | solution.py:400
  27.7 0.8 %copy-start.15 = (bf16[8,2560]{1,0:T(8,128)(2,1)}, bf16[8,2560]{1,0:T(8,128)(2,1)S(1)}, u32[]{:S(2)}) copy-start(bf16[8,2560]{1,0:T(8,128)(2,1)S(1)} %collective-permute-done.3.refs_2_) | copy-start | bytes 122884
  27.7 0.8 %copy-start.5 = (bf16[128,512]{1,0:T(8,128)(2,1)}, bf16[128,512]{1,0:T(8,128)(2,1)S(1)}, u32[]{:S(2)}) copy-start(bf16[128,512]{1,0:T(8,128)(2,1)S(1)} %collective-permute-done.10.refs_2_) | copy-start | bytes 393220
  27.7 0.7 %copy-start.13 = (bf16[128,384]{1,0:T(8,128)(2,1)}, bf16[128,384]{1,0:T(8,128)(2,1)S(1)}, u32[]{:S(2)}) copy-start(bf16[128,384]{1,0:T(8,128)(2,1)S(1)} %collective-permute-done.11.refs_2_) | copy-start | bytes 294916
  28.4 10.2 %collective-permute-start.12 = (bf16[128,512]{1,0:T(8,128)(2,1)}, bf16[128,512]{1,0:T(8,128)(2,1)}, u32[]{:S(2)}, u32[]{:S(2)}) collective-permute-start(bf16[128,512]{1,0:T(8,128)(2,1)} %add_convert_fusion.2), channel_id=1, source_target_pairs={{8,12},{9,13},{10,14},{11,15},{24,28},{25,29},{26,30},{27,31}} | collective-permute-start | bytes 393224 | tf_op jit(solution)/shard_map/ppermute | solution.py:400
  29.7 0.7 %copy-start.30 = (f32[1,32]{1,0:T(1,128)S(1)}, f32[1,32]{1,0:T(1,128)}, u32[]{:S(2)}) copy-start(f32[1,32]{1,0:T(1,128)} %copy-done.29) | copy-start | bytes 388
  30.4 0.8 %copy-start.16 = (bf16[8,2560]{1,0:T(8,128)(2,1)S(1)}, bf16[8,2560]{1,0:T(8,128)(2,1)}, u32[]{:S(2)}) copy-start(bf16[8,2560]{1,0:T(8,128)(2,1)} %copy-done.15) | copy-start | bytes 122884
  31.2 0.7 %copy-start.18 = (f32[32,128]{1,0:T(8,128)S(1)}, f32[32,128]{1,0:T(8,128)}, u32[]{:S(2)}) copy-start(f32[32,128]{1,0:T(8,128)} %copy-done.17) | copy-start | bytes 49156
  31.9 0.7 %copy-start.20 = (f32[32,128]{1,0:T(8,128)S(1)}, f32[32,128]{1,0:T(8,128)}, u32[]{:S(2)}) copy-start(f32[32,128]{1,0:T(8,128)} %copy-done.19) | copy-start | bytes 49156
  32.6 1.9 %copy-start.10 = (bf16[128,384]{1,0:T(8,128)(2,1)S(1)}, bf16[128,384]{1,0:T(8,128)(2,1)}, u32[]{:S(2)}) copy-start(bf16[128,384]{1,0:T(8,128)(2,1)} %copy-done.9) | copy-start | bytes 294916
  32.6 1.9 %copy-start.14 = (bf16[128,384]{1,0:T(8,128)(2,1)S(1)}, bf16[128,384]{1,0:T(8,128)(2,1)}, u32[]{:S(2)}) copy-start(bf16[128,384]{1,0:T(8,128)(2,1)} %copy-done.13) | copy-start | bytes 294916
  34.6 0.9 %copy-start.8 = (bf16[128,512]{1,0:T(8,128)(2,1)S(1)}, bf16[128,512]{1,0:T(8,128)(2,1)}, u32[]{:S(2)}) copy-start(bf16[128,512]{1,0:T(8,128)(2,1)} %copy-done.7) | copy-start | bytes 393220
  37.7 0.9 %copy-start.6 = (bf16[128,512]{1,0:T(8,128)(2,1)S(1)}, bf16[128,512]{1,0:T(8,128)(2,1)}, u32[]{:S(2)}) copy-start(bf16[128,512]{1,0:T(8,128)(2,1)} %copy-done.5) | copy-start | bytes 393220

commit v15 on v11

--- a/solution.py
+++ b/solution.py
@@ -178,7 +178,9 @@
         head_rows(low, high, x, bc, taps_x, taps_bc, scale, out)
 
 
-def prepare_kernel(cuts, _, x, bc, dt_raw, a_log, gain, pack, gain_out, scale, *decays):
+def prepare_kernel(
+    cuts, _, x, bc, dt_raw, a_log, gain, skip, pack, gain_out, skip_out, scale, *decays
+):
     tokens, width = x.shape
     groups, both = bc.shape[1:]
     pack[:, :width] = x[tokens - 2 * RIM :, :].astype(F32)[-RIM:].astype(BF16)
@@ -186,6 +188,7 @@
     for g in range(groups):
         pack[:, width + g * both : width + (g + 1) * both] = last_bc[:, g].astype(BF16)
     gain_out[...] = gain[...]
+    skip_out[...] = skip[...]
     row = scales(groups, width // dt_raw.shape[0], dt_raw, a_log, scale)
     for decay, (low, high) in zip(decays, cuts):
         decay[...] = row[:, low:high]
@@ -407,13 +410,14 @@
             out_shape=[
                 jax.ShapeDtypeStruct((RIM, width + groups * both), BF16),
                 jax.ShapeDtypeStruct((1, width), F32),
+                jax.ShapeDtypeStruct((1, heads), F32),
                 scale_shape,
             ]
             + [jax.ShapeDtypeStruct((1, high - low), F32) for low, high in cuts],
-            in_specs=[anywhere] + [in_vmem] * 5,
+            in_specs=[anywhere] + [in_vmem] * 6,
             compiler_params=params(16),
             name="prepared",
-        )(token, x_in, bc_in, dt_t, a_row, gain)
+        )(token, x_in, bc_in, dt_t, a_row, gain, d_row)
 
     def later_states(condition, rows, token, scale, low, high):
         return pl.pallas_call(
@@ -425,7 +429,7 @@
         )(here(condition), rows, token, *sources, scale)
 
     along = [(i, i + 1) for i in range(devices - 1)]
-    def intra(token, befores):
+    def intra(token, befores, skip):
         return pl.pallas_call(
             functools.partial(intra_kernel, len(befores)),
             out_shape=[
@@ -440,12 +444,12 @@
                 transcendentals=tokens * tokens * heads,
             ),
             name="intra",
-        )(token, *befores, x_in, bc_in, z_in, conv_x, conv_bc, dt_t, a_row, d_row)
+        )(token, *befores, x_in, bc_in, z_in, conv_x, conv_bc, dt_t, a_row, skip)
 
     if devices <= CHAIN_MOST:
         first, scale = first_states(*cuts[0])
         sent = [first, next_states(first, scale, *cuts[1])]
-        last, gain, scale_own, *decays = prepared(sent[-1])
+        last, gain, d_row, scale_own, *decays = prepared(sent[-1])
         token = last
         for cut in cuts[2:]:
             sent.append(next_states(token, scale, *cut))
@@ -458,8 +462,9 @@
         rows, token = arrived[0][0], last
         for hop in range(1, devices - 1):
             runs = place == 1 if hop == 1 else (place >= 2) & (place < devices - 1)
-            after = token
             for i, cut in enumerate(cuts):
+                if hop == 1:
+                    after = last if i == 0 else made_at[1 if i == len(cuts) - 1 else 0]
                 if hop <= 2:
                     made = later_states(runs, rows, after, scale_own, *cut)
                     states = [made] if i == 0 else states + [made]
@@ -469,15 +474,15 @@
                 before, *_ = lax.optimization_barrier((arrived[i][-1], token) + early)
                 joined = decays[i] * before[:state_dim].astype(F32) + states[i]
                 token = joined.astype(BF16)
-                after = token if hop == 1 else after
+                made_at = [token] if i == 0 else made_at + [token]
+                if hop == 1 and i == 1 and late:
+                    moved, _ = lax.optimization_barrier((last, token))
+                    befores.append(shifted(moved, late))
                 arrived[i].append(shifted(token, along[hop : hop + 1]))
-            if hop == 1 and late:
-                moved, _ = lax.optimization_barrier((last, token))
-                befores.append(shifted(moved, late))
-            rows = befores[0]
+            rows, after = befores[0], token
         which = place - 1
     else:
-        last, gain, scale, *decays = prepared(a_row)
+        last, gain, d_row, scale, *decays = prepared(a_row)
         befores = [shifted(last, along)]
         arrived = []
         for decay, cut in zip(decays, cuts):
@@ -485,7 +490,7 @@
             arrived.append([doubling(state, decay, devices)])
         which = jnp.zeros_like(place)
     which = which.astype(jnp.int32).reshape(1)
-    y_part, lead, c_act = intra(a_row, befores)
+    y_part, lead, c_act = intra(a_row, befores, d_row)
 
     common = [which, c_act, y_part, lead]
     common_specs = [scalar] + [in_vmem] * 3

time: 30 us -> 30.8 us (1.027)
  waiting for transfers between devices: 9.75 us -> 10.6 us
    ppermute x14, waiting for transfers between devices: 9.75 us -> 10.6 us  [shifted(): return lax.ppermute(value, 'seq', route)]
  transfers between devices with their start and end apart: 14 -> 14, of which waited for: 4 -> 3; matrix products, arithmetic and copies ran while one was open for 1% -> 1% of each run, Pallas kernels for 15% -> 14%
where the time goes in v15:
time: 30.8 us; the launch traced here: 30.5 us
  starting transfers between devices  12.7 us (41%)
  waiting for transfers between devices  10.6 us (34%)
  Pallas kernels  5.49 us (18%)
  local copies, waits for them, and re-layouts  0.83 us (3%)
  between operations  0.46 us (1%)
  other arithmetic  0.38 us (1%)
    ppermute x14, starting transfers between devices, shifted(): return lax.ppermute(value, 'seq', route)  12.7 us
    ppermute x14, waiting for transfers between devices, shifted(): return lax.ppermute(value, 'seq', route)  10.6 us
    pallas_call x1, Pallas kernels, intra(): pl.pallas_call(functools.partial(intra_kernel, len(befores)), out_shape=[...  2.16 us
    pallas_call x2, Pallas kernels, shards(): pl.pallas_call(functools.partial(output_kernel, begin, spans, unready), o...  1.96 us
    unnamed x18, local copies, waits for them, and re-layouts  0.83 us
  transfers between devices with their start and end apart: 14, of which 3 were waited for; matrix products, arithmetic and copies ran while one was open for 1% of the time, Pallas kernels for 14%

profile of v15, /device:TPU:30, one launch (start us, length us, event | category | flops | bytes accessed | tf_op | source)
XLA Modules:
  0.0 30.5 jit_solution(10336303124985637718)
XLA Ops:
  0.0 0.0 copy-start.3
  0.0 0.1 first_states.1
  0.1 0.8 %collective-permute-start.1 = (bf16[160,384]{1,0:T(8,128)(2,1)S(1)}, bf16[160,384]{1,0:T(8,128)(2,1)S(1)}, u32[]{:S(2)}, u32[]{:S(2)}) collective-permute-start(bf16[160,384]{1,0:T(8,128)(2,1)S(1)} %get-tuple-element.27._), channel_id=1, source_target_pairs={{0,4},{1,5},{2,6},{3,7},{16,20},{17,21},{18,22},{19,23}} | collective-permute-start | bytes 368648 | tf_op jit(solution)/shard_map/ppermute | solution.py:384
  0.9 0.1 copy-done
  1.0 0.0 copy-done.1
  1.1 0.0 copy-done.2
  1.1 0.0 copy-done.3
  1.1 0.7 %collective-permute-start.2 = (bf16[128,640]{1,0:T(8,128)(2,1)S(1)}, bf16[128,640]{1,0:T(8,128)(2,1)S(1)}, u32[]{:S(2)}, u32[]{:S(2)}) collective-permute-start(bf16[128,640]{1,0:T(8,128)(2,1)S(1)} %next_states.3._), channel_id=1, source_target_pairs={{0,4},{1,5},{2,6},{3,7},{16,20},{17,21},{18,22},{19,23}} | collective-permute-start | bytes 491528 | tf_op jit(solution)/shard_map/ppermute | solution.py:384
  1.8 0.0 copy-start.7
  1.8 0.0 copy-start.8
  1.8 0.6 %copy-done.7 = f32[32]{0:T(128)S(1)} copy-done((f32[32]{0:T(128)S(1)}, f32[32]{0:T(128)}, u32[]{:S(2)}) %copy-start.7) | copy-done | bytes 152
  2.4 0.0 copy-done.8
  2.4 0.6 %prepared.1 = (bf16[8,2560]{1,0:T(8,128)(2,1)S(1)}, f32[1,2048]{1,0:T(1,128)S(1)}, f32[1,32]{1,0:T(1,128)S(1)}, f32[128,2048]{1,0:T(8,128)S(1)}, f32[1,384]{1,0:...) custom-call(bf16[128,640]{1,0:T(8,128)(2,1)S(1)} %next_states.3._, ...), custom_call_target="tpu_custom_call" | custom-call | tf_op jit(solution)/shard_map/prepared/pallas_call | solution.py:408
  3.1 0.7 %collective-permute-start = (bf16[8,2560]{1,0:T(8,128)(2,1)S(1)}, bf16[8,2560]{1,0:T(8,128)(2,1)S(1)}, u32[]{:S(2)}, u32[]{:S(2)}) collective-permute-start(bf16[8,2560]{1,0:T(8,128)(2,1)S(1)} %get-tuple-element.35._), channel_id=1, source_target_pairs={{4,8},{5,9},{6,10},{7,11},{20,24},{21,25},{22,26},{23,27}} | collective-permute-start | bytes 122888 | tf_op jit(solution)/shard_map/ppermute | solution.py:384
  3.8 0.7 %collective-permute-start.4 = (bf16[128,512]{1,0:T(8,128)(2,1)S(1)}, bf16[128,512]{1,0:T(8,128)(2,1)S(1)}, u32[]{:S(2)}, u32[]{:S(2)}) collective-permute-start(bf16[128,512]{1,0:T(8,128)(2,1)S(1)} %next_states.4._), channel_id=1, source_target_pairs={{0,4},{1,5},{2,6},{3,7},{16,20},{17,21},{18,22},{19,23}} | collective-permute-start | bytes 393224 | tf_op jit(solution)/shard_map/ppermute | solution.py:384
  4.5 0.7 %collective-permute-start.8 = (bf16[128,512]{1,0:T(8,128)(2,1)S(1)}, bf16[128,512]{1,0:T(8,128)(2,1)S(1)}, u32[]{:S(2)}, u32[]{:S(2)}) collective-permute-start(bf16[128,512]{1,0:T(8,128)(2,1)S(1)} %next_states.5), channel_id=1, source_target_pairs={{0,4},{1,5},{2,6},{3,7},{16,20},{17,21},{18,22},{19,23}} | collective-permute-start | bytes 393224 | tf_op jit(solution)/shard_map/ppermute | solution.py:384
  5.2 0.0 collective-permute-done.1.rows.refs_1_.refs_0_
  5.2 0.7 %collective-permute-start.7 = (bf16[128,384]{1,0:T(8,128)(2,1)S(1)}, bf16[128,384]{1,0:T(8,128)(2,1)S(1)}, u32[]{:S(2)}, u32[]{:S(2)}) collective-permute-start(bf16[128,384]{1,0:T(8,128)(2,1)S(1)} %add_convert_fusion.7._), channel_id=1, source_target_pairs={{4,8},{5,9},{6,10},{7,11},{20,24},{21,25},{22,26},{23,27}} | collective-permute-start | bytes 294920 | tf_op jit(solution)/shard_map/ppermute | solution.py:384
  6.0 0.0 collective-permute-done.2.refs_0_
  6.0 0.1 add_convert_fusion.1._
  6.0 0.7 %collective-permute-start.6 = (bf16[128,640]{1,0:T(8,128)(2,1)S(1)}, bf16[128,640]{1,0:T(8,128)(2,1)S(1)}, u32[]{:S(2)}, u32[]{:S(2)}) collective-permute-start(bf16[128,640]{1,0:T(8,128)(2,1)S(1)} %add_convert_fusion.1._), channel_id=1, source_target_pairs={{4,8},{5,9},{6,10},{7,11},{20,24},{21,25},{22,26},{23,27}} | collective-permute-start | bytes 491528 | tf_op jit(solution)/shard_map/ppermute | solution.py:384
  6.7 0.0 collective-permute-done.4.refs_0_
  6.8 0.7 %collective-permute-start.5 = (bf16[128,512]{1,0:T(8,128)(2,1)S(1)}, bf16[128,512]{1,0:T(8,128)(2,1)S(1)}, u32[]{:S(2)}, u32[]{:S(2)}) collective-permute-start(bf16[128,512]{1,0:T(8,128)(2,1)S(1)} %add_convert_fusion.5), channel_id=1, source_target_pairs={{4,8},{5,9},{6,10},{7,11},{20,24},{21,25},{22,26},{23,27}} | collective-permute-start | bytes 393224 | tf_op jit(solution)/shard_map/ppermute | solution.py:384
  7.4 0.0 collective-permute-done.8.refs_1_
  7.4 1.3 %collective-permute-start.3 = (bf16[8,2560]{1,0:T(8,128)(2,1)S(1)}, bf16[8,2560]{1,0:T(8,128)(2,1)S(1)}, u32[]{:S(2)}, u32[]{:S(2)}) collective-permute-start(bf16[8,2560]{1,0:T(8,128)(2,1)S(1)} %get-tuple-element.35._), channel_id=1, source_target_pairs={{8,12},{9,13},{10,14},{11,15},{24,28},{25,29},{26,30},{27,31}} | collective-permute-start | bytes 122888 | tf_op jit(solution)/shard_map/ppermute | solution.py:384
  8.8 0.0 collective-permute-done.refs_0_.rows
  8.8 0.7 %collective-permute-start.10 = (bf16[128,512]{1,0:T(8,128)(2,1)S(1)}, bf16[128,512]{1,0:T(8,128)(2,1)S(1)}, u32[]{:S(2)}, u32[]{:S(2)}) collective-permute-start(bf16[128,512]{1,0:T(8,128)(2,1)S(1)} %add_convert_fusion.4._), channel_id=1, source_target_pairs={{4,8},{5,9},{6,10},{7,11},{20,24},{21,25},{22,26},{23,27}} | collective-permute-start | bytes 393224 | tf_op jit(solution)/shard_map/ppermute | solution.py:384
  9.6 0.0 collective-permute-done.7.refs_1_
  9.6 1.3 %collective-permute-start.11 = (bf16[128,384]{1,0:T(8,128)(2,1)S(1)}, bf16[128,384]{1,0:T(8,128)(2,1)S(1)}, u32[]{:S(2)}, u32[]{:S(2)}) collective-permute-start(bf16[128,384]{1,0:T(8,128)(2,1)S(1)} %add_convert_fusion.6), channel_id=1, source_target_pairs={{8,12},{9,13},{10,14},{11,15},{24,28},{25,29},{26,30},{27,31}} | collective-permute-start | bytes 294920 | tf_op jit(solution)/shard_map/ppermute | solution.py:384
  10.9 0.0 collective-permute-done.6.refs_1_
  10.9 0.1 add_convert_fusion
  11.0 0.0 copy-start.4
  11.0 1.4 %collective-permute-start.13 = (bf16[128,640]{1,0:T(8,128)(2,1)S(1)}, bf16[128,640]{1,0:T(8,128)(2,1)S(1)}, u32[]{:S(2)}, u32[]{:S(2)}) collective-permute-start(bf16[128,640]{1,0:T(8,128)(2,1)S(1)} %add_convert_fusion), channel_id=1, source_target_pairs={{8,12},{9,13},{10,14},{11,15},{24,28},{25,29},{26,30},{27,31}} | collective-permute-start | bytes 491528 | tf_op jit(solution)/shard_map/ppermute | solution.py:384
  12.4 0.0 collective-permute-done.5.refs_1_
  12.5 1.3 %collective-permute-start.9 = (bf16[128,512]{1,0:T(8,128)(2,1)S(1)}, bf16[128,512]{1,0:T(8,128)(2,1)S(1)}, u32[]{:S(2)}, u32[]{:S(2)}) collective-permute-start(bf16[128,512]{1,0:T(8,128)(2,1)S(1)} %add_convert_fusion.3), channel_id=1, source_target_pairs={{8,12},{9,13},{10,14},{11,15},{24,28},{25,29},{26,30},{27,31}} | collective-permute-start | bytes 393224 | tf_op jit(solution)/shard_map/ppermute | solution.py:384
  13.8 0.0 collective-permute-done.3.refs_2_
  13.8 0.0 collective-permute-done.10.refs_2_
  13.8 5.2 %collective-permute-done.11.refs_2_ = bf16[128,384]{1,0:T(8,128)(2,1)S(1)} collective-permute-done((bf16[128,384]{1,0:T(8,128)(2,1)S(1)}, bf16[128,384]{1,0:T(8,128)(2,1)S(1)}, u32[]{:S(2)}, u32[]{:S(2)}) %collective-permute-start.11) | collective-permute-done | bytes 98336 | tf_op jit(solution)/shard_map/ppermute | solution.py:384
  19.0 1.3 %collective-permute-start.12 = (bf16[128,512]{1,0:T(8,128)(2,1)S(1)}, bf16[128,512]{1,0:T(8,128)(2,1)S(1)}, u32[]{:S(2)}, u32[]{:S(2)}) collective-permute-start(bf16[128,512]{1,0:T(8,128)(2,1)S(1)} %add_convert_fusion.2), channel_id=1, source_target_pairs={{8,12},{9,13},{10,14},{11,15},{24,28},{25,29},{26,30},{27,31}} | collective-permute-start | bytes 393224 | tf_op jit(solution)/shard_map/ppermute | solution.py:384
  20.3 2.2 %intra.1 = (f32[128,2048]{1,0:T(8,128)S(1)}, f32[128,2048]{1,0:T(8,128)S(1)}, bf16[128,256]{1,0:T(8,128)(2,1)S(1)}) custom-call(f32[1,32]{1,0:T(1,128)S(1)} %bitcast.20, bf16[8,2560]{1,0:T(8,128)(2,1)S(1)} %collective-permute-done.refs_0_.rows, bf16[160,384]{1,0:T(8,128)(2,1)S(1)} %collective-permute-done.1.rows.refs_1_.refs_0_, ...), custom_call_target="tpu_custom_call" | custom-call | flops 134217728 | bytes 3145728 | tf_op jit(solution)/shard_map/intra/pallas_call | solution.py:433
  22.5 0.2 gated.4.refs_0_
  22.7 5.3 %collective-permute-done.9.refs_2_ = bf16[128,512]{1,0:T(8,128)(2,1)S(1)} collective-permute-done((bf16[128,512]{1,0:T(8,128)(2,1)S(1)}, bf16[128,512]{1,0:T(8,128)(2,1)S(1)}, u32[]{:S(2)}, u32[]{:S(2)}) %collective-permute-start.9) | collective-permute-done | bytes 131104 | tf_op jit(solution)/shard_map/ppermute | solution.py:384
  28.0 0.2 gated.3.refs_0_
  28.2 0.0 collective-permute-done.13.refs_2_
  28.2 0.2 gated.5.refs_1_
  28.4 0.9 %outputs.2.refs_4_ = bf16[128,2048]{1,0:T(8,128)(2,1)} custom-call(s32[1]{0:T(128)} %bitcast.which, bf16[128,256]{1,0:T(8,128)(2,1)S(1)} %get-tuple-element.37.c, f32[128,2048]{1,0:T(8,128)S(1)} %get-tuple-element.38.y_part, f32[128,2048]{1,0:T(8,128)S(1)} %get-tuple-element.39.lead, f32[1,2048]{1,0:T(1,128)S(1)} %get-tuple-element.40.gain, ...), custom_call_target="tpu_custom_call" | custom-call | tf_op jit(solution)/shard_map/outputs/pallas_call | solution.py:528
  29.3 0.1 collective-permute-done.12.refs_3_
  29.4 1.0 %outputs.3 = bf16[128,2048]{1,0:T(8,128)(2,1)} custom-call(s32[1]{0:T(128)} %bitcast.which, bf16[128,256]{1,0:T(8,128)(2,1)S(1)} %get-tuple-element.37.c, f32[128,2048]{1,0:T(8,128)S(1)} %get-tuple-element.38.y_part, f32[128,2048]{1,0:T(8,128)S(1)} %get-tuple-element.39.lead, f32[1,2048]{1,0:T(1,128)S(1)} %get-tuple-element.40.gain, ...), custom_call_target="tpu_custom_call", output_to_operand_aliasing={{}: (9, {})} | custom-call | tf_op jit(solution)/shard_map/outputs/pallas_call | solution.py:528
  (27 shorter events, 0.4 us)
Async XLA Ops:
  0.0 1.0 %copy-start = (bf16[128,2048]{1,0:T(8,128)(2,1)S(1)}, bf16[128,2048]{1,0:T(8,128)(2,1)}, u32[]{:S(2)}) copy-start(bf16[128,2048]{1,0:T(8,128)(2,1)} %x.23) | copy-start | bytes 1572868
  0.0 1.1 %copy-start.1 = (bf16[128,2,256]{2,1,0:T(2,128)(2,1)S(1)}, bf16[128,2,256]{2,1,0:T(2,128)(2,1)}, u32[]{:S(2)}) copy-start(bf16[128,2,256]{2,1,0:T(2,128)(2,1)} %bc.23) | copy-start | bytes 393220
  0.0 1.1 %copy-start.2 = (f32[4,2048]{1,0:T(4,128)S(1)}, f32[4,2048]{1,0:T(4,128)}, u32[]{:S(2)}) copy-start(f32[4,2048]{1,0:T(4,128)} %taps_x.21) | copy-start | bytes 98308
  0.0 1.1 %copy-start.3 = (f32[4,2,256]{2,1,0:T(2,128)S(1)}, f32[4,2,256]{2,1,0:T(2,128)}, u32[]{:S(2)}) copy-start(f32[4,2,256]{2,1,0:T(2,128)} %taps_bc.21) | copy-start | bytes 24580
  0.1 5.1 %collective-permute-start.1 = (bf16[160,384]{1,0:T(8,128)(2,1)S(1)}, bf16[160,384]{1,0:T(8,128)(2,1)S(1)}, u32[]{:S(2)}, u32[]{:S(2)}) collective-permute-start(bf16[160,384]{1,0:T(8,128)(2,1)S(1)} %get-tuple-element.27._), channel_id=1, source_target_pairs={{0,4},{1,5},{2,6},{3,7},{16,20},{17,21},{18,22},{19,23}} | collective-permute-start | bytes 368648 | tf_op jit(solution)/shard_map/ppermute | solution.py:384
  1.1 0.7 %copy-start.5 = (f32[128,32]{0,1:T(8,128)S(1)}, f32[128,32]{0,1:T(8,128)}, u32[]{:S(2)}) copy-start(f32[128,32]{0,1:T(8,128)} %param.12) | copy-start | bytes 49156
  1.1 0.7 %copy-start.6 = (f32[2048]{0:T(1024)S(1)}, f32[2048]{0:T(1024)}, u32[]{:S(2)}) copy-start(f32[2048]{0:T(1024)} %param.17) | copy-start | bytes 24580
  1.1 4.9 %collective-permute-start.2 = (bf16[128,640]{1,0:T(8,128)(2,1)S(1)}, bf16[128,640]{1,0:T(8,128)(2,1)S(1)}, u32[]{:S(2)}, u32[]{:S(2)}) collective-permute-start(bf16[128,640]{1,0:T(8,128)(2,1)S(1)} %next_states.3._), channel_id=1, source_target_pairs={{0,4},{1,5},{2,6},{3,7},{16,20},{17,21},{18,22},{19,23}} | collective-permute-start | bytes 491528 | tf_op jit(solution)/shard_map/ppermute | solution.py:384
  1.8 0.7 %copy-start.7 = (f32[32]{0:T(128)S(1)}, f32[32]{0:T(128)}, u32[]{:S(2)}) copy-start(f32[32]{0:T(128)} %param.15) | copy-start | bytes 388
  1.8 0.7 %copy-start.8 = (f32[32]{0:T(128)S(1)}, f32[32]{0:T(128)}, u32[]{:S(2)}) copy-start(f32[32]{0:T(128)} %param.16) | copy-start | bytes 388
  3.1 5.8 %collective-permute-start = (bf16[8,2560]{1,0:T(8,128)(2,1)S(1)}, bf16[8,2560]{1,0:T(8,128)(2,1)S(1)}, u32[]{:S(2)}, u32[]{:S(2)}) collective-permute-start(bf16[8,2560]{1,0:T(8,128)(2,1)S(1)} %get-tuple-element.35._), channel_id=1, source_target_pairs={{4,8},{5,9},{6,10},{7,11},{20,24},{21,25},{22,26},{23,27}} | collective-permute-start | bytes 122888 | tf_op jit(solution)/shard_map/ppermute | solution.py:384
  3.8 3.0 %collective-permute-start.4 = (bf16[128,512]{1,0:T(8,128)(2,1)S(1)}, bf16[128,512]{1,0:T(8,128)(2,1)S(1)}, u32[]{:S(2)}, u32[]{:S(2)}) collective-permute-start(bf16[128,512]{1,0:T(8,128)(2,1)S(1)} %next_states.4._), channel_id=1, source_target_pairs={{0,4},{1,5},{2,6},{3,7},{16,20},{17,21},{18,22},{19,23}} | collective-permute-start | bytes 393224 | tf_op jit(solution)/shard_map/ppermute | solution.py:384
  4.5 3.0 %collective-permute-start.8 = (bf16[128,512]{1,0:T(8,128)(2,1)S(1)}, bf16[128,512]{1,0:T(8,128)(2,1)S(1)}, u32[]{:S(2)}, u32[]{:S(2)}) collective-permute-start(bf16[128,512]{1,0:T(8,128)(2,1)S(1)} %next_states.5), channel_id=1, source_target_pairs={{0,4},{1,5},{2,6},{3,7},{16,20},{17,21},{18,22},{19,23}} | collective-permute-start | bytes 393224 | tf_op jit(solution)/shard_map/ppermute | solution.py:384
  5.2 4.3 %collective-permute-start.7 = (bf16[128,384]{1,0:T(8,128)(2,1)S(1)}, bf16[128,384]{1,0:T(8,128)(2,1)S(1)}, u32[]{:S(2)}, u32[]{:S(2)}) collective-permute-start(bf16[128,384]{1,0:T(8,128)(2,1)S(1)} %add_convert_fusion.7._), channel_id=1, source_target_pairs={{4,8},{5,9},{6,10},{7,11},{20,24},{21,25},{22,26},{23,27}} | collective-permute-start | bytes 294920 | tf_op jit(solution)/shard_map/ppermute | solution.py:384
  6.0 4.9 %collective-permute-start.6 = (bf16[128,640]{1,0:T(8,128)(2,1)S(1)}, bf16[128,640]{1,0:T(8,128)(2,1)S(1)}, u32[]{:S(2)}, u32[]{:S(2)}) collective-permute-start(bf16[128,640]{1,0:T(8,128)(2,1)S(1)} %add_convert_fusion.1._), channel_id=1, source_target_pairs={{4,8},{5,9},{6,10},{7,11},{20,24},{21,25},{22,26},{23,27}} | collective-permute-start | bytes 491528 | tf_op jit(solution)/shard_map/ppermute | solution.py:384
  6.8 5.7 %collective-permute-start.5 = (bf16[128,512]{1,0:T(8,128)(2,1)S(1)}, bf16[128,512]{1,0:T(8,128)(2,1)S(1)}, u32[]{:S(2)}, u32[]{:S(2)}) collective-permute-start(bf16[128,512]{1,0:T(8,128)(2,1)S(1)} %add_convert_fusion.5), channel_id=1, source_target_pairs={{4,8},{5,9},{6,10},{7,11},{20,24},{21,25},{22,26},{23,27}} | collective-permute-start | bytes 393224 | tf_op jit(solution)/shard_map/ppermute | solution.py:384
  7.4 6.3 %collective-permute-start.3 = (bf16[8,2560]{1,0:T(8,128)(2,1)S(1)}, bf16[8,2560]{1,0:T(8,128)(2,1)S(1)}, u32[]{:S(2)}, u32[]{:S(2)}) collective-permute-start(bf16[8,2560]{1,0:T(8,128)(2,1)S(1)} %get-tuple-element.35._), channel_id=1, source_target_pairs={{8,12},{9,13},{10,14},{11,15},{24,28},{25,29},{26,30},{27,31}} | collective-permute-start | bytes 122888 | tf_op jit(solution)/shard_map/ppermute | solution.py:384
  8.8 5.0 %collective-permute-start.10 = (bf16[128,512]{1,0:T(8,128)(2,1)S(1)}, bf16[128,512]{1,0:T(8,128)(2,1)S(1)}, u32[]{:S(2)}, u32[]{:S(2)}) collective-permute-start(bf16[128,512]{1,0:T(8,128)(2,1)S(1)} %add_convert_fusion.4._), channel_id=1, source_target_pairs={{4,8},{5,9},{6,10},{7,11},{20,24},{21,25},{22,26},{23,27}} | collective-permute-start | bytes 393224 | tf_op jit(solution)/shard_map/ppermute | solution.py:384
  9.6 9.4 %collective-permute-start.11 = (bf16[128,384]{1,0:T(8,128)(2,1)S(1)}, bf16[128,384]{1,0:T(8,128)(2,1)S(1)}, u32[]{:S(2)}, u32[]{:S(2)}) collective-permute-start(bf16[128,384]{1,0:T(8,128)(2,1)S(1)} %add_convert_fusion.6), channel_id=1, source_target_pairs={{8,12},{9,13},{10,14},{11,15},{24,28},{25,29},{26,30},{27,31}} | collective-permute-start | bytes 294920 | tf_op jit(solution)/shard_map/ppermute | solution.py:384
  11.0 9.3 %copy-start.4 = (bf16[128,2048]{1,0:T(8,128)(2,1)S(1)}, bf16[128,2048]{1,0:T(8,128)(2,1)}, u32[]{:S(2)}) copy-start(bf16[128,2048]{1,0:T(8,128)(2,1)} %refs_5_.1) | copy-start | bytes 1572868
  11.0 17.2 %collective-permute-start.13 = (bf16[128,640]{1,0:T(8,128)(2,1)S(1)}, bf16[128,640]{1,0:T(8,128)(2,1)S(1)}, u32[]{:S(2)}, u32[]{:S(2)}) collective-permute-start(bf16[128,640]{1,0:T(8,128)(2,1)S(1)} %add_convert_fusion), channel_id=1, source_target_pairs={{8,12},{9,13},{10,14},{11,15},{24,28},{25,29},{26,30},{27,31}} | collective-permute-start | bytes 491528 | tf_op jit(solution)/shard_map/ppermute | solution.py:384
  12.5 15.5 %collective-permute-start.9 = (bf16[128,512]{1,0:T(8,128)(2,1)S(1)}, bf16[128,512]{1,0:T(8,128)(2,1)S(1)}, u32[]{:S(2)}, u32[]{:S(2)}) collective-permute-start(bf16[128,512]{1,0:T(8,128)(2,1)S(1)} %add_convert_fusion.3), channel_id=1, source_target_pairs={{8,12},{9,13},{10,14},{11,15},{24,28},{25,29},{26,30},{27,31}} | collective-permute-start | bytes 393224 | tf_op jit(solution)/shard_map/ppermute | solution.py:384
  19.0 10.4 %collective-permute-start.12 = (bf16[128,512]{1,0:T(8,128)(2,1)S(1)}, bf16[128,512]{1,0:T(8,128)(2,1)S(1)}, u32[]{:S(2)}, u32[]{:S(2)}) collective-permute-start(bf16[128,512]{1,0:T(8,128)(2,1)S(1)} %add_convert_fusion.2), channel_id=1, source_target_pairs={{8,12},{9,13},{10,14},{11,15},{24,28},{25,29},{26,30},{27,31}} | collective-permute-start | bytes 393224 | tf_op jit(solution)/shard_map/ppermute | solution.py:384

commit v16 on v11

--- a/solution.py
+++ b/solution.py
@@ -11,7 +11,7 @@
 F32 = jnp.float32
 BF16 = jnp.bfloat16
 CHAIN_MOST = 4
-PARTS = (3, 5, 4, 4)
+PARTS = (1, 1, 1, 1)
 CHUNK = 128
 RIM = 8
 
@@ -465,7 +465,7 @@
                     states = [made] if i == 0 else states + [made]
                 early = ()
                 if hop == devices - 2 and hop > 1 and i == len(cuts) - 1:
-                    early = (arrived[0][-1], befores[-1])
+                    early = (befores[-1],)
                 before, *_ = lax.optimization_barrier((arrived[i][-1], token) + early)
                 joined = decays[i] * before[:state_dim].astype(F32) + states[i]
                 token = joined.astype(BF16)

time: 30 us -> 30.2 us (level)
  the two profiles are of different devices: /device:TPU:30 before, /device:TPU:20 now
where the time goes in v16:
time: 30.2 us; the launch traced here: 29.8 us
  starting transfers between devices  15.9 us (53%)
  Pallas kernels  7.22 us (24%)
  waiting for transfers between devices  4.52 us (15%)
  other arithmetic  0.95 us (3%)
  local copies, waits for them, and re-layouts  0.83 us (3%)
  between operations  0.45 us (1%)
    ppermute x14, starting transfers between devices, shifted(): return lax.ppermute(value, 'seq', route)  15.9 us
    ppermute x14, waiting for transfers between devices, shifted(): return lax.ppermute(value, 'seq', route)  4.52 us
    pallas_call x1, Pallas kernels, intra(): pl.pallas_call(functools.partial(intra_kernel, len(befores)), out_shape=[...  2.16 us
    pallas_call x2, Pallas kernels, shards(): pl.pallas_call(functools.partial(output_kernel, begin, spans, unready), o...  1.97 us
    pallas_call x8, Pallas kernels, later_states(): pl.pallas_call(functools.partial(later_kernel, low, high), out_shape=jax....  1.84 us
    convert_element_type x8, other arithmetic, shards(): token = joined.astype(BF16)  0.95 us
    unnamed x18, local copies, waits for them, and re-layouts  0.83 us
    pallas_call x1, Pallas kernels, prepared(): pl.pallas_call(functools.partial(prepare_kernel, cuts), out_shape=[jax.Sh...  0.62 us
  transfers between devices with their start and end apart: 14, of which 4 were waited for; matrix products, arithmetic and copies ran while one was open for 3% of the time, Pallas kernels for 20%

profile of v16, /device:TPU:20, one launch (start us, length us, event | category | flops | bytes accessed | tf_op | source)
XLA Modules:
  0.0 29.8 jit_solution(14802596605717294075)
XLA Ops:
  0.0 0.1 first_states.1
  0.1 0.8 %collective-permute-start.1 = (bf16[144,512]{1,0:T(8,128)(2,1)S(1)}, bf16[144,512]{1,0:T(8,128)(2,1)S(1)}, u32[]{:S(2)}, u32[]{:S(2)}) collective-permute-start(bf16[144,512]{1,0:T(8,128)(2,1)S(1)} %get-tuple-element.26._), channel_id=1, source_target_pairs={{0,4},{1,5},{2,6},{3,7},{16,20},{17,21},{18,22},{19,23}} | collective-permute-start | bytes 442376 | tf_op jit(solution)/shard_map/ppermute | solution.py:381
  0.9 0.1 copy-done
  1.0 0.0 copy-done.1
  1.1 0.0 copy-done.3
  1.1 0.0 copy-start.7
  1.1 0.7 %collective-permute-start.4 = (bf16[128,512]{1,0:T(8,128)(2,1)S(1)}, bf16[128,512]{1,0:T(8,128)(2,1)S(1)}, u32[]{:S(2)}, u32[]{:S(2)}) collective-permute-start(bf16[128,512]{1,0:T(8,128)(2,1)S(1)} %next_states.3._), channel_id=1, source_target_pairs={{0,4},{1,5},{2,6},{3,7},{16,20},{17,21},{18,22},{19,23}} | collective-permute-start | bytes 393224 | tf_op jit(solution)/shard_map/ppermute | solution.py:381
  1.8 0.6 %prepared.1 = (bf16[8,2560]{1,0:T(8,128)(2,1)S(1)}, f32[1,2048]{1,0:T(1,128)S(1)}, f32[128,2048]{1,0:T(8,128)S(1)}, f32[1,512]{1,0:T(1,128)S(1)}, f32[1,512]{1,0...) custom-call(bf16[128,512]{1,0:T(8,128)(2,1)S(1)} %next_states.3._, bf16[128,2048]{1,0:T(8,128)(2,1)S(1)} %copy-done, ...), custom_call_target="tpu_custom_call" | custom-call | tf_op jit(solution)/shard_map/prepared/pallas_call | solution.py:405
  2.4 1.3 %collective-permute-start = (bf16[8,2560]{1,0:T(8,128)(2,1)S(1)}, bf16[8,2560]{1,0:T(8,128)(2,1)S(1)}, u32[]{:S(2)}, u32[]{:S(2)}) collective-permute-start(bf16[8,2560]{1,0:T(8,128)(2,1)S(1)} %get-tuple-element.38._), channel_id=1, source_target_pairs={{4,8},{5,9},{6,10},{7,11},{20,24},{21,25},{22,26},{23,27}} | collective-permute-start | bytes 122888 | tf_op jit(solution)/shard_map/ppermute | solution.py:381
  3.8 0.7 %collective-permute-start.3 = (bf16[128,512]{1,0:T(8,128)(2,1)S(1)}, bf16[128,512]{1,0:T(8,128)(2,1)S(1)}, u32[]{:S(2)}, u32[]{:S(2)}) collective-permute-start(bf16[128,512]{1,0:T(8,128)(2,1)S(1)} %next_states.4._), channel_id=1, source_target_pairs={{0,4},{1,5},{2,6},{3,7},{16,20},{17,21},{18,22},{19,23}} | collective-permute-start | bytes 393224 | tf_op jit(solution)/shard_map/ppermute | solution.py:381
  4.5 0.7 %collective-permute-start.2 = (bf16[128,512]{1,0:T(8,128)(2,1)S(1)}, bf16[128,512]{1,0:T(8,128)(2,1)S(1)}, u32[]{:S(2)}, u32[]{:S(2)}) collective-permute-start(bf16[128,512]{1,0:T(8,128)(2,1)S(1)} %next_states.5), channel_id=1, source_target_pairs={{0,4},{1,5},{2,6},{3,7},{16,20},{17,21},{18,22},{19,23}} | collective-permute-start | bytes 393224 | tf_op jit(solution)/shard_map/ppermute | solution.py:381
  5.1 0.0 collective-permute-done.1.rows.refs_1_.refs_0_
  5.2 1.3 %collective-permute-start.8 = (bf16[128,512]{1,0:T(8,128)(2,1)S(1)}, bf16[128,512]{1,0:T(8,128)(2,1)S(1)}, u32[]{:S(2)}, u32[]{:S(2)}) collective-permute-start(bf16[128,512]{1,0:T(8,128)(2,1)S(1)} %add_convert_fusion.7._), channel_id=1, source_target_pairs={{4,8},{5,9},{6,10},{7,11},{20,24},{21,25},{22,26},{23,27}} | collective-permute-start | bytes 393224 | tf_op jit(solution)/shard_map/ppermute | solution.py:381
  6.5 0.0 collective-permute-done.4.refs_0_
  6.6 1.3 %collective-permute-start.7 = (bf16[128,512]{1,0:T(8,128)(2,1)S(1)}, bf16[128,512]{1,0:T(8,128)(2,1)S(1)}, u32[]{:S(2)}, u32[]{:S(2)}) collective-permute-start(bf16[128,512]{1,0:T(8,128)(2,1)S(1)} %add_convert_fusion.6._), channel_id=1, source_target_pairs={{4,8},{5,9},{6,10},{7,11},{20,24},{21,25},{22,26},{23,27}} | collective-permute-start | bytes 393224 | tf_op jit(solution)/shard_map/ppermute | solution.py:381
  7.9 0.0 collective-permute-done.3.refs_0_
  8.0 1.3 %collective-permute-start.6 = (bf16[128,512]{1,0:T(8,128)(2,1)S(1)}, bf16[128,512]{1,0:T(8,128)(2,1)S(1)}, u32[]{:S(2)}, u32[]{:S(2)}) collective-permute-start(bf16[128,512]{1,0:T(8,128)(2,1)S(1)} %add_convert_fusion.5._), channel_id=1, source_target_pairs={{4,8},{5,9},{6,10},{7,11},{20,24},{21,25},{22,26},{23,27}} | collective-permute-start | bytes 393224 | tf_op jit(solution)/shard_map/ppermute | solution.py:381
  9.3 0.0 collective-permute-done.2.refs_1_
  9.3 1.3 %collective-permute-start.10 = (bf16[128,512]{1,0:T(8,128)(2,1)S(1)}, bf16[128,512]{1,0:T(8,128)(2,1)S(1)}, u32[]{:S(2)}, u32[]{:S(2)}) collective-permute-start(bf16[128,512]{1,0:T(8,128)(2,1)S(1)} %add_convert_fusion.4._), channel_id=1, source_target_pairs={{4,8},{5,9},{6,10},{7,11},{20,24},{21,25},{22,26},{23,27}} | collective-permute-start | bytes 393224 | tf_op jit(solution)/shard_map/ppermute | solution.py:381
  10.6 0.0 collective-permute-done.refs_0_.rows
  10.7 1.3 %collective-permute-start.5 = (bf16[8,2560]{1,0:T(8,128)(2,1)S(1)}, bf16[8,2560]{1,0:T(8,128)(2,1)S(1)}, u32[]{:S(2)}, u32[]{:S(2)}) collective-permute-start(bf16[8,2560]{1,0:T(8,128)(2,1)S(1)} %get-tuple-element.38._), channel_id=1, source_target_pairs={{8,12},{9,13},{10,14},{11,15},{24,28},{25,29},{26,30},{27,31}} | collective-permute-start | bytes 122888 | tf_op jit(solution)/shard_map/ppermute | solution.py:381
  12.0 0.5 %later_states.15 = f32[128,512]{1,0:T(8,128)S(1)} custom-call(s32[1]{0:T(128)} %bitcast.11.active, bf16[8,2560]{1,0:T(8,128)(2,1)S(1)} %collective-permute-done.refs_0_.rows, bf16[128,512]{1,0:T(8,128)(2,1)S(1)} %add_convert_fusion.4._, bf16[128,2048]{1,0:T(8,128)(2,1)S(1)} %copy-done, bf16[128,2,256]{2,1,0:T(2,128)(2,1)S(1)} %copy-done.1, ...), custom_call_target="tpu_custom_call" | custom-call | tf_op jit(solution)/shard_map/later_states/pallas_call | solution.py:419
  12.4 0.5 %later_states.14 = f32[128,512]{1,0:T(8,128)S(1)} custom-call(s32[1]{0:T(128)} %bitcast.11.active, bf16[8,2560]{1,0:T(8,128)(2,1)S(1)} %collective-permute-done.refs_0_.rows, bf16[128,512]{1,0:T(8,128)(2,1)S(1)} %add_convert_fusion.4._, bf16[128,2048]{1,0:T(8,128)(2,1)S(1)} %copy-done, bf16[128,2,256]{2,1,0:T(2,128)(2,1)S(1)} %copy-done.1, ...), custom_call_target="tpu_custom_call" | custom-call | tf_op jit(solution)/shard_map/later_states/pallas_call | solution.py:419
  12.9 0.4 %later_states.13 = f32[128,512]{1,0:T(8,128)S(1)} custom-call(s32[1]{0:T(128)} %bitcast.11.active, bf16[8,2560]{1,0:T(8,128)(2,1)S(1)} %collective-permute-done.refs_0_.rows, bf16[128,512]{1,0:T(8,128)(2,1)S(1)} %add_convert_fusion.4._, bf16[128,2048]{1,0:T(8,128)(2,1)S(1)} %copy-done, bf16[128,2,256]{2,1,0:T(2,128)(2,1)S(1)} %copy-done.1, ...), custom_call_target="tpu_custom_call" | custom-call | tf_op jit(solution)/shard_map/later_states/pallas_call | solution.py:419
  13.3 0.4 %later_states.12 = f32[128,512]{1,0:T(8,128)S(1)} custom-call(s32[1]{0:T(128)} %bitcast.11.active, bf16[8,2560]{1,0:T(8,128)(2,1)S(1)} %collective-permute-done.refs_0_.rows, bf16[128,512]{1,0:T(8,128)(2,1)S(1)} %add_convert_fusion.4._, bf16[128,2048]{1,0:T(8,128)(2,1)S(1)} %copy-done, bf16[128,2,256]{2,1,0:T(2,128)(2,1)S(1)} %copy-done.1, ...), custom_call_target="tpu_custom_call" | custom-call | tf_op jit(solution)/shard_map/later_states/pallas_call | solution.py:419
  13.8 1.3 %collective-permute-done.8.refs_1_ = bf16[128,512]{1,0:T(8,128)(2,1)S(1)} collective-permute-done((bf16[128,512]{1,0:T(8,128)(2,1)S(1)}, bf16[128,512]{1,0:T(8,128)(2,1)S(1)}, u32[]{:S(2)}, u32[]{:S(2)}) %collective-permute-start.8) | collective-permute-done | bytes 131104 | tf_op jit(solution)/shard_map/ppermute | solution.py:381
  15.1 1.3 %collective-permute-start.12 = (bf16[128,512]{1,0:T(8,128)(2,1)S(1)}, bf16[128,512]{1,0:T(8,128)(2,1)S(1)}, u32[]{:S(2)}, u32[]{:S(2)}) collective-permute-start(bf16[128,512]{1,0:T(8,128)(2,1)S(1)} %add_convert_fusion.3), channel_id=1, source_target_pairs={{8,12},{9,13},{10,14},{11,15},{24,28},{25,29},{26,30},{27,31}} | collective-permute-start | bytes 393224 | tf_op jit(solution)/shard_map/ppermute | solution.py:381
  16.4 1.5 %collective-permute-done.7.refs_1_ = bf16[128,512]{1,0:T(8,128)(2,1)S(1)} collective-permute-done((bf16[128,512]{1,0:T(8,128)(2,1)S(1)}, bf16[128,512]{1,0:T(8,128)(2,1)S(1)}, u32[]{:S(2)}, u32[]{:S(2)}) %collective-permute-start.7) | collective-permute-done | bytes 131104 | tf_op jit(solution)/shard_map/ppermute | solution.py:381
  17.9 0.0 copy-start.4
  18.0 1.4 %collective-permute-start.13 = (bf16[128,512]{1,0:T(8,128)(2,1)S(1)}, bf16[128,512]{1,0:T(8,128)(2,1)S(1)}, u32[]{:S(2)}, u32[]{:S(2)}) collective-permute-start(bf16[128,512]{1,0:T(8,128)(2,1)S(1)} %add_convert_fusion.2), channel_id=1, source_target_pairs={{8,12},{9,13},{10,14},{11,15},{24,28},{25,29},{26,30},{27,31}} | collective-permute-start | bytes 393224 | tf_op jit(solution)/shard_map/ppermute | solution.py:381
  19.4 1.5 %collective-permute-done.6.refs_1_ = bf16[128,512]{1,0:T(8,128)(2,1)S(1)} collective-permute-done((bf16[128,512]{1,0:T(8,128)(2,1)S(1)}, bf16[128,512]{1,0:T(8,128)(2,1)S(1)}, u32[]{:S(2)}, u32[]{:S(2)}) %collective-permute-start.6) | collective-permute-done | bytes 131104 | tf_op jit(solution)/shard_map/ppermute | solution.py:381
  20.9 1.3 %collective-permute-start.9 = (bf16[128,512]{1,0:T(8,128)(2,1)S(1)}, bf16[128,512]{1,0:T(8,128)(2,1)S(1)}, u32[]{:S(2)}, u32[]{:S(2)}) collective-permute-start(bf16[128,512]{1,0:T(8,128)(2,1)S(1)} %add_convert_fusion.1), channel_id=1, source_target_pairs={{8,12},{9,13},{10,14},{11,15},{24,28},{25,29},{26,30},{27,31}} | collective-permute-start | bytes 393224 | tf_op jit(solution)/shard_map/ppermute | solution.py:381
  22.2 0.0 collective-permute-done.5.refs_2_
  22.3 0.2 collective-permute-done.10.refs_2_
  22.5 0.7 %add_convert_fusion = bf16[128,512]{1,0:T(8,128)(2,1)} fusion(f32[128,512]{1,0:T(8,128)S(1)} %later_states.15, bf16[128,512]{1,0:T(8,128)(2,1)S(1)} %collective-permute-done.10.refs_2_, f32[512]{0:T(512)S(1)} %bitcast.17), kind=kLoop, calls=%fused_computation | loop fusion | flops 262144 | bytes 526336 | tf_op jit(solution)/shard_map/convert_element_type | solution.py:471
  23.1 1.3 %collective-permute-start.11 = (bf16[128,512]{1,0:T(8,128)(2,1)}, bf16[128,512]{1,0:T(8,128)(2,1)S(1)}, u32[]{:S(2)}, u32[]{:S(2)}) collective-permute-start(bf16[128,512]{1,0:T(8,128)(2,1)} %add_convert_fusion), channel_id=1, source_target_pairs={{8,12},{9,13},{10,14},{11,15},{24,28},{25,29},{26,30},{27,31}} | collective-permute-start | bytes 393224 | tf_op jit(solution)/shard_map/ppermute | solution.py:381
  24.4 0.0 copy-start.8
  24.4 0.6 %copy-done.8 = f32[32]{0:T(128)S(1)} copy-done((f32[32]{0:T(128)S(1)}, f32[32]{0:T(128)}, u32[]{:S(2)}) %copy-start.8) | copy-done | bytes 152
  25.1 2.2 %intra.1 = (f32[128,2048]{1,0:T(8,128)S(1)}, f32[128,2048]{1,0:T(8,128)S(1)}, bf16[128,256]{1,0:T(8,128)(2,1)S(1)}) custom-call(f32[1,32]{1,0:T(1,128)S(1)} %bitcast.26, bf16[8,2560]{1,0:T(8,128)(2,1)S(1)} %collective-permute-done.refs_0_.rows, bf16[144,512]{1,0:T(8,128)(2,1)S(1)} %collective-permute-done.1.rows.refs_1_.refs_0_, ...), custom_call_target="tpu_custom_call" | custom-call | flops 134217728 | bytes 3145728 | tf_op jit(solution)/shard_map/intra/pallas_call | solution.py:429
  27.3 0.0 collective-permute-done.12.refs_2_
  27.3 0.2 gated.4.refs_0_
  27.5 0.0 collective-permute-done.13.refs_2_
  27.5 0.2 gated.5.refs_1_
  27.7 0.9 %outputs.2.refs_4_ = bf16[128,2048]{1,0:T(8,128)(2,1)} custom-call(s32[1]{0:T(128)} %bitcast.which, bf16[128,256]{1,0:T(8,128)(2,1)S(1)} %get-tuple-element.39.c, f32[128,2048]{1,0:T(8,128)S(1)} %get-tuple-element.40.y_part, f32[128,2048]{1,0:T(8,128)S(1)} %get-tuple-element.41.lead, f32[1,2048]{1,0:T(1,128)S(1)} %get-tuple-element.42.gain, ...), custom_call_target="tpu_custom_call" | custom-call | tf_op jit(solution)/shard_map/outputs/pallas_call | solution.py:523
  28.6 0.0 collective-permute-done.9.refs_2_
  28.6 0.2 gated.3.refs_0_
  28.8 0.0 collective-permute-done.11.refs_3_
  28.8 1.1 %outputs.3 = bf16[128,2048]{1,0:T(8,128)(2,1)} custom-call(s32[1]{0:T(128)} %bitcast.which, bf16[128,256]{1,0:T(8,128)(2,1)S(1)} %get-tuple-element.39.c, f32[128,2048]{1,0:T(8,128)S(1)} %get-tuple-element.40.y_part, f32[128,2048]{1,0:T(8,128)S(1)} %get-tuple-element.41.lead, f32[1,2048]{1,0:T(1,128)S(1)} %get-tuple-element.42.gain, ...), custom_call_target="tpu_custom_call", output_to_operand_aliasing={{}: (9, {})} | custom-call | tf_op jit(solution)/shard_map/outputs/pallas_call | solution.py:523
  (25 shorter events, 0.4 us)
Async XLA Ops:
  0.0 1.0 %copy-start = (bf16[128,2048]{1,0:T(8,128)(2,1)S(1)}, bf16[128,2048]{1,0:T(8,128)(2,1)}, u32[]{:S(2)}) copy-start(bf16[128,2048]{1,0:T(8,128)(2,1)} %x.23) | copy-start | bytes 1572868
  0.0 1.1 %copy-start.1 = (bf16[128,2,256]{2,1,0:T(2,128)(2,1)S(1)}, bf16[128,2,256]{2,1,0:T(2,128)(2,1)}, u32[]{:S(2)}) copy-start(bf16[128,2,256]{2,1,0:T(2,128)(2,1)} %bc.23) | copy-start | bytes 393220
  0.0 1.1 %copy-start.2 = (f32[4,2048]{1,0:T(4,128)S(1)}, f32[4,2048]{1,0:T(4,128)}, u32[]{:S(2)}) copy-start(f32[4,2048]{1,0:T(4,128)} %taps_x.21) | copy-start | bytes 98308
  0.0 1.1 %copy-start.3 = (f32[4,2,256]{2,1,0:T(2,128)S(1)}, f32[4,2,256]{2,1,0:T(2,128)}, u32[]{:S(2)}) copy-start(f32[4,2,256]{2,1,0:T(2,128)} %taps_bc.21) | copy-start | bytes 24580
  0.1 5.1 %collective-permute-start.1 = (bf16[144,512]{1,0:T(8,128)(2,1)S(1)}, bf16[144,512]{1,0:T(8,128)(2,1)S(1)}, u32[]{:S(2)}, u32[]{:S(2)}) collective-permute-start(bf16[144,512]{1,0:T(8,128)(2,1)S(1)} %get-tuple-element.26._), channel_id=1, source_target_pairs={{0,4},{1,5},{2,6},{3,7},{16,20},{17,21},{18,22},{19,23}} | collective-permute-start | bytes 442376 | tf_op jit(solution)/shard_map/ppermute | solution.py:381
  1.1 0.7 %copy-start.5 = (f32[128,32]{0,1:T(8,128)S(1)}, f32[128,32]{0,1:T(8,128)}, u32[]{:S(2)}) copy-start(f32[128,32]{0,1:T(8,128)} %param.12) | copy-start | bytes 49156
  1.1 0.7 %copy-start.6 = (f32[2048]{0:T(1024)S(1)}, f32[2048]{0:T(1024)}, u32[]{:S(2)}) copy-start(f32[2048]{0:T(1024)} %param.17) | copy-start | bytes 24580
  1.1 0.7 %copy-start.7 = (f32[32]{0:T(128)S(1)}, f32[32]{0:T(128)}, u32[]{:S(2)}) copy-start(f32[32]{0:T(128)} %param.15) | copy-start | bytes 388
  1.1 5.4 %collective-permute-start.4 = (bf16[128,512]{1,0:T(8,128)(2,1)S(1)}, bf16[128,512]{1,0:T(8,128)(2,1)S(1)}, u32[]{:S(2)}, u32[]{:S(2)}) collective-permute-start(bf16[128,512]{1,0:T(8,128)(2,1)S(1)} %next_states.3._), channel_id=1, source_target_pairs={{0,4},{1,5},{2,6},{3,7},{16,20},{17,21},{18,22},{19,23}} | collective-permute-start | bytes 393224 | tf_op jit(solution)/shard_map/ppermute | solution.py:381
  2.4 8.2 %collective-permute-start = (bf16[8,2560]{1,0:T(8,128)(2,1)S(1)}, bf16[8,2560]{1,0:T(8,128)(2,1)S(1)}, u32[]{:S(2)}, u32[]{:S(2)}) collective-permute-start(bf16[8,2560]{1,0:T(8,128)(2,1)S(1)} %get-tuple-element.38._), channel_id=1, source_target_pairs={{4,8},{5,9},{6,10},{7,11},{20,24},{21,25},{22,26},{23,27}} | collective-permute-start | bytes 122888 | tf_op jit(solution)/shard_map/ppermute | solution.py:381
  3.8 4.1 %collective-permute-start.3 = (bf16[128,512]{1,0:T(8,128)(2,1)S(1)}, bf16[128,512]{1,0:T(8,128)(2,1)S(1)}, u32[]{:S(2)}, u32[]{:S(2)}) collective-permute-start(bf16[128,512]{1,0:T(8,128)(2,1)S(1)} %next_states.4._), channel_id=1, source_target_pairs={{0,4},{1,5},{2,6},{3,7},{16,20},{17,21},{18,22},{19,23}} | collective-permute-start | bytes 393224 | tf_op jit(solution)/shard_map/ppermute | solution.py:381
  4.5 4.8 %collective-permute-start.2 = (bf16[128,512]{1,0:T(8,128)(2,1)S(1)}, bf16[128,512]{1,0:T(8,128)(2,1)S(1)}, u32[]{:S(2)}, u32[]{:S(2)}) collective-permute-start(bf16[128,512]{1,0:T(8,128)(2,1)S(1)} %next_states.5), channel_id=1, source_target_pairs={{0,4},{1,5},{2,6},{3,7},{16,20},{17,21},{18,22},{19,23}} | collective-permute-start | bytes 393224 | tf_op jit(solution)/shard_map/ppermute | solution.py:381
  5.2 9.9 %collective-permute-start.8 = (bf16[128,512]{1,0:T(8,128)(2,1)S(1)}, bf16[128,512]{1,0:T(8,128)(2,1)S(1)}, u32[]{:S(2)}, u32[]{:S(2)}) collective-permute-start(bf16[128,512]{1,0:T(8,128)(2,1)S(1)} %add_convert_fusion.7._), channel_id=1, source_target_pairs={{4,8},{5,9},{6,10},{7,11},{20,24},{21,25},{22,26},{23,27}} | collective-permute-start | bytes 393224 | tf_op jit(solution)/shard_map/ppermute | solution.py:381
  6.6 11.3 %collective-permute-start.7 = (bf16[128,512]{1,0:T(8,128)(2,1)S(1)}, bf16[128,512]{1,0:T(8,128)(2,1)S(1)}, u32[]{:S(2)}, u32[]{:S(2)}) collective-permute-start(bf16[128,512]{1,0:T(8,128)(2,1)S(1)} %add_convert_fusion.6._), channel_id=1, source_target_pairs={{4,8},{5,9},{6,10},{7,11},{20,24},{21,25},{22,26},{23,27}} | collective-permute-start | bytes 393224 | tf_op jit(solution)/shard_map/ppermute | solution.py:381
  8.0 12.9 %collective-permute-start.6 = (bf16[128,512]{1,0:T(8,128)(2,1)S(1)}, bf16[128,512]{1,0:T(8,128)(2,1)S(1)}, u32[]{:S(2)}, u32[]{:S(2)}) collective-permute-start(bf16[128,512]{1,0:T(8,128)(2,1)S(1)} %add_convert_fusion.5._), channel_id=1, source_target_pairs={{4,8},{5,9},{6,10},{7,11},{20,24},{21,25},{22,26},{23,27}} | collective-permute-start | bytes 393224 | tf_op jit(solution)/shard_map/ppermute | solution.py:381
  9.3 13.1 %collective-permute-start.10 = (bf16[128,512]{1,0:T(8,128)(2,1)S(1)}, bf16[128,512]{1,0:T(8,128)(2,1)S(1)}, u32[]{:S(2)}, u32[]{:S(2)}) collective-permute-start(bf16[128,512]{1,0:T(8,128)(2,1)S(1)} %add_convert_fusion.4._), channel_id=1, source_target_pairs={{4,8},{5,9},{6,10},{7,11},{20,24},{21,25},{22,26},{23,27}} | collective-permute-start | bytes 393224 | tf_op jit(solution)/shard_map/ppermute | solution.py:381
  10.7 11.6 %collective-permute-start.5 = (bf16[8,2560]{1,0:T(8,128)(2,1)S(1)}, bf16[8,2560]{1,0:T(8,128)(2,1)S(1)}, u32[]{:S(2)}, u32[]{:S(2)}) collective-permute-start(bf16[8,2560]{1,0:T(8,128)(2,1)S(1)} %get-tuple-element.38._), channel_id=1, source_target_pairs={{8,12},{9,13},{10,14},{11,15},{24,28},{25,29},{26,30},{27,31}} | collective-permute-start | bytes 122888 | tf_op jit(solution)/shard_map/ppermute | solution.py:381
  15.1 12.1 %collective-permute-start.12 = (bf16[128,512]{1,0:T(8,128)(2,1)S(1)}, bf16[128,512]{1,0:T(8,128)(2,1)S(1)}, u32[]{:S(2)}, u32[]{:S(2)}) collective-permute-start(bf16[128,512]{1,0:T(8,128)(2,1)S(1)} %add_convert_fusion.3), channel_id=1, source_target_pairs={{8,12},{9,13},{10,14},{11,15},{24,28},{25,29},{26,30},{27,31}} | collective-permute-start | bytes 393224 | tf_op jit(solution)/shard_map/ppermute | solution.py:381
  17.9 6.5 %copy-start.4 = (bf16[128,2048]{1,0:T(8,128)(2,1)S(1)}, bf16[128,2048]{1,0:T(8,128)(2,1)}, u32[]{:S(2)}) copy-start(bf16[128,2048]{1,0:T(8,128)(2,1)} %refs_5_.1) | copy-start | bytes 1572868
  18.0 9.5 %collective-permute-start.13 = (bf16[128,512]{1,0:T(8,128)(2,1)S(1)}, bf16[128,512]{1,0:T(8,128)(2,1)S(1)}, u32[]{:S(2)}, u32[]{:S(2)}) collective-permute-start(bf16[128,512]{1,0:T(8,128)(2,1)S(1)} %add_convert_fusion.2), channel_id=1, source_target_pairs={{8,12},{9,13},{10,14},{11,15},{24,28},{25,29},{26,30},{27,31}} | collective-permute-start | bytes 393224 | tf_op jit(solution)/shard_map/ppermute | solution.py:381
  20.9 7.6 %collective-permute-start.9 = (bf16[128,512]{1,0:T(8,128)(2,1)S(1)}, bf16[128,512]{1,0:T(8,128)(2,1)S(1)}, u32[]{:S(2)}, u32[]{:S(2)}) collective-permute-start(bf16[128,512]{1,0:T(8,128)(2,1)S(1)} %add_convert_fusion.1), channel_id=1, source_target_pairs={{8,12},{9,13},{10,14},{11,15},{24,28},{25,29},{26,30},{27,31}} | collective-permute-start | bytes 393224 | tf_op jit(solution)/shard_map/ppermute | solution.py:381
  23.1 5.6 %collective-permute-start.11 = (bf16[128,512]{1,0:T(8,128)(2,1)}, bf16[128,512]{1,0:T(8,128)(2,1)S(1)}, u32[]{:S(2)}, u32[]{:S(2)}) collective-permute-start(bf16[128,512]{1,0:T(8,128)(2,1)} %add_convert_fusion), channel_id=1, source_target_pairs={{8,12},{9,13},{10,14},{11,15},{24,28},{25,29},{26,30},{27,31}} | collective-permute-start | bytes 393224 | tf_op jit(solution)/shard_map/ppermute | solution.py:381
  24.4 0.7 %copy-start.8 = (f32[32]{0:T(128)S(1)}, f32[32]{0:T(128)}, u32[]{:S(2)}) copy-start(f32[32]{0:T(128)} %param.16) | copy-start | bytes 388

commit v17 on v16

--- a/solution.py
+++ b/solution.py
@@ -178,7 +178,12 @@
         head_rows(low, high, x, bc, taps_x, taps_bc, scale, out)
 
 
-def prepare_kernel(cuts, _, x, bc, dt_raw, a_log, gain, pack, gain_out, scale, *decays):
+def prepare_kernel(
+    cuts, _, x, bc, dt_raw, a_log, gain, skip_hbm, pack, gain_out, skip_out, scale, *refs
+):
+    decays, sem = refs[:-1], refs[-1]
+    skip_copy = pltpu.make_async_copy(skip_hbm, skip_out, sem.at[0])
+    skip_copy.start()
     tokens, width = x.shape
     groups, both = bc.shape[1:]
     pack[:, :width] = x[tokens - 2 * RIM :, :].astype(F32)[-RIM:].astype(BF16)
@@ -189,6 +194,7 @@
     row = scales(groups, width // dt_raw.shape[0], dt_raw, a_log, scale)
     for decay, (low, high) in zip(decays, cuts):
         decay[...] = row[:, low:high]
+    skip_copy.wait()
 
 
 def rows_before(rows, begin, stop, keep, state_dim):
@@ -388,7 +394,7 @@
             out_shape=[jax.ShapeDtypeStruct((state_dim + extra, high - low), BF16), scale_shape],
             in_specs=[scalar] + in_hbm,
             scratch_shapes=landed + [pltpu.SemaphoreType.DMA((len(operands),))],
-            compiler_params=params(16),
+            compiler_params=params(8),
             name="first_states",
         )(here(place == 0), *pinned)
 
@@ -397,7 +403,7 @@
             functools.partial(next_kernel, low, high),
             out_shape=jax.ShapeDtypeStruct((state_dim, high - low), BF16),
             in_specs=[scalar, anywhere] + [in_vmem] * (len(sources) + 1),
-            compiler_params=params(16),
+            compiler_params=params(8),
             name="next_states",
         )(here(place == 0), token, *sources, scale)
 
@@ -407,25 +413,30 @@
             out_shape=[
                 jax.ShapeDtypeStruct((RIM, width + groups * both), BF16),
                 jax.ShapeDtypeStruct((1, width), F32),
+                jax.ShapeDtypeStruct((1, heads), F32),
                 scale_shape,
             ]
             + [jax.ShapeDtypeStruct((1, high - low), F32) for low, high in cuts],
-            in_specs=[anywhere] + [in_vmem] * 5,
-            compiler_params=params(16),
+            in_specs=[anywhere] + [in_vmem] * 5 + [pl.BlockSpec(memory_space=pltpu.HBM)],
+            scratch_shapes=[pltpu.SemaphoreType.DMA((1,))],
+            compiler_params=params(8),
             name="prepared",
-        )(token, x_in, bc_in, dt_t, a_row, gain)
+        )(
+            token, x_in, bc_in, dt_t, a_row, gain,
+            pltpu.with_memory_space_constraint(d_row, pltpu.HBM),
+        )
 
     def later_states(condition, rows, token, scale, low, high):
         return pl.pallas_call(
             functools.partial(later_kernel, low, high),
             out_shape=jax.ShapeDtypeStruct((state_dim, high - low), F32),
             in_specs=[scalar, in_vmem, anywhere] + [in_vmem] * (len(sources) + 1),
-            compiler_params=params(16),
+            compiler_params=params(8),
             name="later_states",
         )(here(condition), rows, token, *sources, scale)
 
     along = [(i, i + 1) for i in range(devices - 1)]
-    def intra(token, befores):
+    def intra(token, befores, skip):
         return pl.pallas_call(
             functools.partial(intra_kernel, len(befores)),
             out_shape=[
@@ -433,19 +444,19 @@
             ],
             in_specs=[anywhere] + [in_vmem] * (len(befores) + 8),
             scratch_shapes=[pltpu.VMEM((tokens, cols), F32)],
-            compiler_params=params(24),
+            compiler_params=params(12),
             cost_estimate=pl.CostEstimate(
                 flops=4 * tokens * tokens * width,
                 bytes_accessed=12 * tokens * width,
                 transcendentals=tokens * tokens * heads,
             ),
             name="intra",
-        )(token, *befores, x_in, bc_in, z_in, conv_x, conv_bc, dt_t, a_row, d_row)
+        )(token, *befores, x_in, bc_in, z_in, conv_x, conv_bc, dt_t, a_row, skip)
 
     if devices <= CHAIN_MOST:
         first, scale = first_states(*cuts[0])
         sent = [first, next_states(first, scale, *cuts[1])]
-        last, gain, scale_own, *decays = prepared(sent[-1])
+        last, gain, d_row, scale_own, *decays = prepared(sent[-1])
         token = last
         for cut in cuts[2:]:
             sent.append(next_states(token, scale, *cut))
@@ -477,7 +488,7 @@
             rows = befores[0]
         which = place - 1
     else:
-        last, gain, scale, *decays = prepared(a_row)
+        last, gain, d_row, scale, *decays = prepared(a_row)
         befores = [shifted(last, along)]
         arrived = []
         for decay, cut in zip(decays, cuts):
@@ -485,7 +496,7 @@
             arrived.append([doubling(state, decay, devices)])
         which = jnp.zeros_like(place)
     which = which.astype(jnp.int32).reshape(1)
-    y_part, lead, c_act = intra(a_row, befores)
+    y_part, lead, c_act = intra(a_row, befores, d_row)
 
     common = [which, c_act, y_part, lead]
     common_specs = [scalar] + [in_vmem] * 3
@@ -497,7 +508,7 @@
                 functools.partial(gated_kernel, low),
                 out_shape=jax.ShapeDtypeStruct((tokens, high - low), F32),
                 in_specs=common_specs + [in_vmem] * len(seen),
-                compiler_params=params(16),
+                compiler_params=params(8),
                 name="gated",
             )(*common, *seen)
         )
@@ -530,7 +541,7 @@
                 pltpu.SemaphoreType.DMA((len(cuts) + groups,)),
             ],
             input_output_aliases=aliases,
-            compiler_params=params(16),
+            compiler_params=params(8),
             name="outputs",
         )(*common, gain, *inputs)
     return out

time: 30.2 us -> 30.8 us (1.020)
  the two profiles are of different devices: /device:TPU:20 before, /device:TPU:30 now
where the time goes in v17:
time: 30.8 us; the launch traced here: 30.5 us
  starting transfers between devices  12.7 us (41%)
  waiting for transfers between devices  9.62 us (31%)
  Pallas kernels  5.92 us (19%)
  other arithmetic  0.98 us (3%)
  local copies, waits for them, and re-layouts  0.82 us (3%)
  between operations  0.43 us (1%)
    ppermute x14, starting transfers between devices, shifted(): return lax.ppermute(value, 'seq', route)  12.7 us
    ppermute x14, waiting for transfers between devices, shifted(): return lax.ppermute(value, 'seq', route)  9.62 us
    pallas_call x1, Pallas kernels, intra(): pl.pallas_call(functools.partial(intra_kernel, len(befores)), out_shape=[...  2.16 us
    pallas_call x2, Pallas kernels, shards(): pl.pallas_call(functools.partial(output_kernel, begin, spans, unready), o...  1.96 us
    pallas_call x1, Pallas kernels, prepared(): pl.pallas_call(functools.partial(prepare_kernel, cuts), out_shape=[jax.Sh...  1.08 us
    convert_element_type x8, other arithmetic, shards(): token = joined.astype(BF16)  0.98 us
    unnamed x16, local copies, waits for them, and re-layouts  0.82 us
  transfers between devices with their start and end apart: 14, of which 5 were waited for; matrix products, arithmetic and copies ran while one was open for 3% of the time, Pallas kernels for 16%

profile of v17, /device:TPU:30, one launch (start us, length us, event | category | flops | bytes accessed | tf_op | source)
XLA Modules:
  0.0 30.5 jit_solution(15691666537243577637)
XLA Ops:
  0.0 0.0 copy-start.3
  0.0 0.1 first_states.1
  0.1 0.8 %collective-permute-start.1 = (bf16[144,512]{1,0:T(8,128)(2,1)S(1)}, bf16[144,512]{1,0:T(8,128)(2,1)S(1)}, u32[]{:S(2)}, u32[]{:S(2)}) collective-permute-start(bf16[144,512]{1,0:T(8,128)(2,1)S(1)} %get-tuple-element.27._), channel_id=1, source_target_pairs={{0,4},{1,5},{2,6},{3,7},{16,20},{17,21},{18,22},{19,23}} | collective-permute-start | bytes 442376 | tf_op jit(solution)/shard_map/ppermute | solution.py:387
  0.9 0.1 copy-done
  1.0 0.0 copy-done.1
  1.1 0.0 copy-done.2
  1.1 0.0 copy-done.3
  1.1 0.7 %collective-permute-start.4 = (bf16[128,512]{1,0:T(8,128)(2,1)S(1)}, bf16[128,512]{1,0:T(8,128)(2,1)S(1)}, u32[]{:S(2)}, u32[]{:S(2)}) collective-permute-start(bf16[128,512]{1,0:T(8,128)(2,1)S(1)} %next_states.3._), channel_id=1, source_target_pairs={{0,4},{1,5},{2,6},{3,7},{16,20},{17,21},{18,22},{19,23}} | collective-permute-start | bytes 393224 | tf_op jit(solution)/shard_map/ppermute | solution.py:387
  1.8 0.0 copy-start.7
  1.8 0.0 copy-done.5
  1.8 0.0 copy-done.6
  1.8 0.6 %copy-done.7 = f32[32]{0:T(128)S(1)} copy-done((f32[32]{0:T(128)S(1)}, f32[32]{0:T(128)}, u32[]{:S(2)}) %copy-start.7) | copy-done | bytes 152
  2.4 1.1 %prepared.1 = (bf16[8,2560]{1,0:T(8,128)(2,1)S(1)}, f32[1,2048]{1,0:T(1,128)S(1)}, f32[1,32]{1,0:T(1,128)S(1)}, f32[128,2048]{1,0:T(8,128)S(1)}, f32[1,512]{1,0:...) custom-call(bf16[128,512]{1,0:T(8,128)(2,1)S(1)} %next_states.3._, ...), custom_call_target="tpu_custom_call" | custom-call | tf_op jit(solution)/shard_map/prepared/pallas_call | solution.py:411
  3.5 0.7 %collective-permute-start = (bf16[8,2560]{1,0:T(8,128)(2,1)S(1)}, bf16[8,2560]{1,0:T(8,128)(2,1)S(1)}, u32[]{:S(2)}, u32[]{:S(2)}) collective-permute-start(bf16[8,2560]{1,0:T(8,128)(2,1)S(1)} %get-tuple-element.39._), channel_id=1, source_target_pairs={{4,8},{5,9},{6,10},{7,11},{20,24},{21,25},{22,26},{23,27}} | collective-permute-start | bytes 122888 | tf_op jit(solution)/shard_map/ppermute | solution.py:387
  4.2 0.7 %collective-permute-start.3 = (bf16[128,512]{1,0:T(8,128)(2,1)S(1)}, bf16[128,512]{1,0:T(8,128)(2,1)S(1)}, u32[]{:S(2)}, u32[]{:S(2)}) collective-permute-start(bf16[128,512]{1,0:T(8,128)(2,1)S(1)} %next_states.4._), channel_id=1, source_target_pairs={{0,4},{1,5},{2,6},{3,7},{16,20},{17,21},{18,22},{19,23}} | collective-permute-start | bytes 393224 | tf_op jit(solution)/shard_map/ppermute | solution.py:387
  4.9 0.7 %collective-permute-start.2 = (bf16[128,512]{1,0:T(8,128)(2,1)S(1)}, bf16[128,512]{1,0:T(8,128)(2,1)S(1)}, u32[]{:S(2)}, u32[]{:S(2)}) collective-permute-start(bf16[128,512]{1,0:T(8,128)(2,1)S(1)} %next_states.5), channel_id=1, source_target_pairs={{0,4},{1,5},{2,6},{3,7},{16,20},{17,21},{18,22},{19,23}} | collective-permute-start | bytes 393224 | tf_op jit(solution)/shard_map/ppermute | solution.py:387
  5.6 0.0 collective-permute-done.1.rows.refs_1_.refs_0_
  5.7 0.7 %collective-permute-start.8 = (bf16[128,512]{1,0:T(8,128)(2,1)S(1)}, bf16[128,512]{1,0:T(8,128)(2,1)S(1)}, u32[]{:S(2)}, u32[]{:S(2)}) collective-permute-start(bf16[128,512]{1,0:T(8,128)(2,1)S(1)} %add_convert_fusion.7._), channel_id=1, source_target_pairs={{4,8},{5,9},{6,10},{7,11},{20,24},{21,25},{22,26},{23,27}} | collective-permute-start | bytes 393224 | tf_op jit(solution)/shard_map/ppermute | solution.py:387
  6.3 0.0 collective-permute-done.4.refs_0_
  6.4 0.7 %collective-permute-start.7 = (bf16[128,512]{1,0:T(8,128)(2,1)S(1)}, bf16[128,512]{1,0:T(8,128)(2,1)S(1)}, u32[]{:S(2)}, u32[]{:S(2)}) collective-permute-start(bf16[128,512]{1,0:T(8,128)(2,1)S(1)} %add_convert_fusion.6._), channel_id=1, source_target_pairs={{4,8},{5,9},{6,10},{7,11},{20,24},{21,25},{22,26},{23,27}} | collective-permute-start | bytes 393224 | tf_op jit(solution)/shard_map/ppermute | solution.py:387
  7.1 0.0 collective-permute-done.3.refs_0_
  7.2 0.7 %collective-permute-start.6 = (bf16[128,512]{1,0:T(8,128)(2,1)S(1)}, bf16[128,512]{1,0:T(8,128)(2,1)S(1)}, u32[]{:S(2)}, u32[]{:S(2)}) collective-permute-start(bf16[128,512]{1,0:T(8,128)(2,1)S(1)} %add_convert_fusion.5._), channel_id=1, source_target_pairs={{4,8},{5,9},{6,10},{7,11},{20,24},{21,25},{22,26},{23,27}} | collective-permute-start | bytes 393224 | tf_op jit(solution)/shard_map/ppermute | solution.py:387
  7.9 0.0 collective-permute-done.2.refs_1_
  7.9 0.7 %collective-permute-start.10 = (bf16[128,512]{1,0:T(8,128)(2,1)S(1)}, bf16[128,512]{1,0:T(8,128)(2,1)S(1)}, u32[]{:S(2)}, u32[]{:S(2)}) collective-permute-start(bf16[128,512]{1,0:T(8,128)(2,1)S(1)} %add_convert_fusion.4._), channel_id=1, source_target_pairs={{4,8},{5,9},{6,10},{7,11},{20,24},{21,25},{22,26},{23,27}} | collective-permute-start | bytes 393224 | tf_op jit(solution)/shard_map/ppermute | solution.py:387
  8.6 0.0 collective-permute-done.refs_0_.rows
  8.6 1.3 %collective-permute-start.5 = (bf16[8,2560]{1,0:T(8,128)(2,1)S(1)}, bf16[8,2560]{1,0:T(8,128)(2,1)S(1)}, u32[]{:S(2)}, u32[]{:S(2)}) collective-permute-start(bf16[8,2560]{1,0:T(8,128)(2,1)S(1)} %get-tuple-element.39._), channel_id=1, source_target_pairs={{8,12},{9,13},{10,14},{11,15},{24,28},{25,29},{26,30},{27,31}} | collective-permute-start | bytes 122888 | tf_op jit(solution)/shard_map/ppermute | solution.py:387
  10.0 0.0 collective-permute-done.8.refs_1_
  10.0 1.3 %collective-permute-start.12 = (bf16[128,512]{1,0:T(8,128)(2,1)S(1)}, bf16[128,512]{1,0:T(8,128)(2,1)S(1)}, u32[]{:S(2)}, u32[]{:S(2)}) collective-permute-start(bf16[128,512]{1,0:T(8,128)(2,1)S(1)} %add_convert_fusion.3), channel_id=1, source_target_pairs={{8,12},{9,13},{10,14},{11,15},{24,28},{25,29},{26,30},{27,31}} | collective-permute-start | bytes 393224 | tf_op jit(solution)/shard_map/ppermute | solution.py:387
  11.3 0.0 collective-permute-done.7.refs_1_
  11.4 0.0 copy-start.4
  11.4 1.4 %collective-permute-start.13 = (bf16[128,512]{1,0:T(8,128)(2,1)S(1)}, bf16[128,512]{1,0:T(8,128)(2,1)S(1)}, u32[]{:S(2)}, u32[]{:S(2)}) collective-permute-start(bf16[128,512]{1,0:T(8,128)(2,1)S(1)} %add_convert_fusion.2), channel_id=1, source_target_pairs={{8,12},{9,13},{10,14},{11,15},{24,28},{25,29},{26,30},{27,31}} | collective-permute-start | bytes 393224 | tf_op jit(solution)/shard_map/ppermute | solution.py:387
  12.8 0.0 collective-permute-done.6.refs_1_
  12.9 1.3 %collective-permute-start.9 = (bf16[128,512]{1,0:T(8,128)(2,1)S(1)}, bf16[128,512]{1,0:T(8,128)(2,1)S(1)}, u32[]{:S(2)}, u32[]{:S(2)}) collective-permute-start(bf16[128,512]{1,0:T(8,128)(2,1)S(1)} %add_convert_fusion.1), channel_id=1, source_target_pairs={{8,12},{9,13},{10,14},{11,15},{24,28},{25,29},{26,30},{27,31}} | collective-permute-start | bytes 393224 | tf_op jit(solution)/shard_map/ppermute | solution.py:387
  14.2 1.2 %collective-permute-done.5.refs_2_ = bf16[8,2560]{1,0:T(8,128)(2,1)S(1)} collective-permute-done((bf16[8,2560]{1,0:T(8,128)(2,1)S(1)}, bf16[8,2560]{1,0:T(8,128)(2,1)S(1)}, u32[]{:S(2)}, u32[]{:S(2)}) %collective-permute-start.5) | collective-permute-done | bytes 40992 | tf_op jit(solution)/shard_map/ppermute | solution.py:387
  15.4 0.0 collective-permute-done.10.refs_2_
  15.4 0.7 %add_convert_fusion = bf16[128,512]{1,0:T(8,128)(2,1)} fusion(f32[128,512]{1,0:T(8,128)S(1)} %later_states.15, bf16[128,512]{1,0:T(8,128)(2,1)S(1)} %collective-permute-done.10.refs_2_, f32[512]{0:T(512)S(1)} %bitcast.17), kind=kLoop, calls=%fused_computation | loop fusion | flops 262144 | bytes 526336 | tf_op jit(solution)/shard_map/convert_element_type | solution.py:482
  16.1 1.3 %collective-permute-start.11 = (bf16[128,512]{1,0:T(8,128)(2,1)}, bf16[128,512]{1,0:T(8,128)(2,1)S(1)}, u32[]{:S(2)}, u32[]{:S(2)}) collective-permute-start(bf16[128,512]{1,0:T(8,128)(2,1)} %add_convert_fusion), channel_id=1, source_target_pairs={{8,12},{9,13},{10,14},{11,15},{24,28},{25,29},{26,30},{27,31}} | collective-permute-start | bytes 393224 | tf_op jit(solution)/shard_map/ppermute | solution.py:387
  17.4 0.0 copy-done.4
  17.4 2.2 %intra.1 = (f32[128,2048]{1,0:T(8,128)S(1)}, f32[128,2048]{1,0:T(8,128)S(1)}, bf16[128,256]{1,0:T(8,128)(2,1)S(1)}) custom-call(f32[1,32]{1,0:T(1,128)S(1)} %bitcast.26, bf16[8,2560]{1,0:T(8,128)(2,1)S(1)} %collective-permute-done.refs_0_.rows, bf16[144,512]{1,0:T(8,128)(2,1)S(1)} %collective-permute-done.1.rows.refs_1_.refs_0_, ...), custom_call_target="tpu_custom_call" | custom-call | flops 134217728 | bytes 3145728 | tf_op jit(solution)/shard_map/intra/pallas_call | solution.py:440
  19.6 2.4 %collective-permute-done.12.refs_2_ = bf16[128,512]{1,0:T(8,128)(2,1)S(1)} collective-permute-done((bf16[128,512]{1,0:T(8,128)(2,1)S(1)}, bf16[128,512]{1,0:T(8,128)(2,1)S(1)}, u32[]{:S(2)}, u32[]{:S(2)}) %collective-permute-start.12) | collective-permute-done | bytes 131104 | tf_op jit(solution)/shard_map/ppermute | solution.py:387
  22.0 0.2 gated.4.refs_0_
  22.2 3.1 %collective-permute-done.13.refs_2_ = bf16[128,512]{1,0:T(8,128)(2,1)S(1)} collective-permute-done((bf16[128,512]{1,0:T(8,128)(2,1)S(1)}, bf16[128,512]{1,0:T(8,128)(2,1)S(1)}, u32[]{:S(2)}, u32[]{:S(2)}) %collective-permute-start.13) | collective-permute-done | bytes 131104 | tf_op jit(solution)/shard_map/ppermute | solution.py:387
  25.2 0.2 gated.5.refs_1_
  25.4 0.9 %outputs.2.refs_4_ = bf16[128,2048]{1,0:T(8,128)(2,1)} custom-call(s32[1]{0:T(128)} %bitcast.which, bf16[128,256]{1,0:T(8,128)(2,1)S(1)} %get-tuple-element.41.c, f32[128,2048]{1,0:T(8,128)S(1)} %get-tuple-element.42.y_part, f32[128,2048]{1,0:T(8,128)S(1)} %get-tuple-element.43.lead, f32[1,2048]{1,0:T(1,128)S(1)} %get-tuple-element.44.gain, ...), custom_call_target="tpu_custom_call" | custom-call | tf_op jit(solution)/shard_map/outputs/pallas_call | solution.py:534
  26.3 0.8 %collective-permute-done.9.refs_2_ = bf16[128,512]{1,0:T(8,128)(2,1)S(1)} collective-permute-done((bf16[128,512]{1,0:T(8,128)(2,1)S(1)}, bf16[128,512]{1,0:T(8,128)(2,1)S(1)}, u32[]{:S(2)}, u32[]{:S(2)}) %collective-permute-start.9) | collective-permute-done | bytes 131104 | tf_op jit(solution)/shard_map/ppermute | solution.py:387
  27.1 0.2 gated.3.refs_0_
  27.3 2.1 %collective-permute-done.11.refs_3_ = bf16[128,512]{1,0:T(8,128)(2,1)S(1)} collective-permute-done((bf16[128,512]{1,0:T(8,128)(2,1)}, bf16[128,512]{1,0:T(8,128)(2,1)S(1)}, u32[]{:S(2)}, u32[]{:S(2)}) %collective-permute-start.11) | collective-permute-done | bytes 131104 | tf_op jit(solution)/shard_map/ppermute | solution.py:387
  29.4 1.0 %outputs.3 = bf16[128,2048]{1,0:T(8,128)(2,1)} custom-call(s32[1]{0:T(128)} %bitcast.which, bf16[128,256]{1,0:T(8,128)(2,1)S(1)} %get-tuple-element.41.c, f32[128,2048]{1,0:T(8,128)S(1)} %get-tuple-element.42.y_part, f32[128,2048]{1,0:T(8,128)S(1)} %get-tuple-element.43.lead, f32[1,2048]{1,0:T(1,128)S(1)} %get-tuple-element.44.gain, ...), custom_call_target="tpu_custom_call", output_to_operand_aliasing={{}: (9, {})} | custom-call | tf_op jit(solution)/shard_map/outputs/pallas_call | solution.py:534
  (23 shorter events, 0.4 us)
Async XLA Ops:
  0.0 1.0 %copy-start = (bf16[128,2048]{1,0:T(8,128)(2,1)S(1)}, bf16[128,2048]{1,0:T(8,128)(2,1)}, u32[]{:S(2)}) copy-start(bf16[128,2048]{1,0:T(8,128)(2,1)} %x.23) | copy-start | bytes 1572868
  0.0 1.1 %copy-start.1 = (bf16[128,2,256]{2,1,0:T(2,128)(2,1)S(1)}, bf16[128,2,256]{2,1,0:T(2,128)(2,1)}, u32[]{:S(2)}) copy-start(bf16[128,2,256]{2,1,0:T(2,128)(2,1)} %bc.23) | copy-start | bytes 393220
  0.0 1.1 %copy-start.2 = (f32[4,2048]{1,0:T(4,128)S(1)}, f32[4,2048]{1,0:T(4,128)}, u32[]{:S(2)}) copy-start(f32[4,2048]{1,0:T(4,128)} %taps_x.21) | copy-start | bytes 98308
  0.0 1.1 %copy-start.3 = (f32[4,2,256]{2,1,0:T(2,128)S(1)}, f32[4,2,256]{2,1,0:T(2,128)}, u32[]{:S(2)}) copy-start(f32[4,2,256]{2,1,0:T(2,128)} %taps_bc.21) | copy-start | bytes 24580
  0.1 5.5 %collective-permute-start.1 = (bf16[144,512]{1,0:T(8,128)(2,1)S(1)}, bf16[144,512]{1,0:T(8,128)(2,1)S(1)}, u32[]{:S(2)}, u32[]{:S(2)}) collective-permute-start(bf16[144,512]{1,0:T(8,128)(2,1)S(1)} %get-tuple-element.27._), channel_id=1, source_target_pairs={{0,4},{1,5},{2,6},{3,7},{16,20},{17,21},{18,22},{19,23}} | collective-permute-start | bytes 442376 | tf_op jit(solution)/shard_map/ppermute | solution.py:387
  1.1 0.7 %copy-start.5 = (f32[128,32]{0,1:T(8,128)S(1)}, f32[128,32]{0,1:T(8,128)}, u32[]{:S(2)}) copy-start(f32[128,32]{0,1:T(8,128)} %param.12) | copy-start | bytes 49156
  1.1 0.7 %copy-start.6 = (f32[2048]{0:T(1024)S(1)}, f32[2048]{0:T(1024)}, u32[]{:S(2)}) copy-start(f32[2048]{0:T(1024)} %param.17) | copy-start | bytes 24580
  1.1 5.3 %collective-permute-start.4 = (bf16[128,512]{1,0:T(8,128)(2,1)S(1)}, bf16[128,512]{1,0:T(8,128)(2,1)S(1)}, u32[]{:S(2)}, u32[]{:S(2)}) collective-permute-start(bf16[128,512]{1,0:T(8,128)(2,1)S(1)} %next_states.3._), channel_id=1, source_target_pairs={{0,4},{1,5},{2,6},{3,7},{16,20},{17,21},{18,22},{19,23}} | collective-permute-start | bytes 393224 | tf_op jit(solution)/shard_map/ppermute | solution.py:387
  1.8 0.7 %copy-start.7 = (f32[32]{0:T(128)S(1)}, f32[32]{0:T(128)}, u32[]{:S(2)}) copy-start(f32[32]{0:T(128)} %param.15) | copy-start | bytes 388
  3.5 5.1 %collective-permute-start = (bf16[8,2560]{1,0:T(8,128)(2,1)S(1)}, bf16[8,2560]{1,0:T(8,128)(2,1)S(1)}, u32[]{:S(2)}, u32[]{:S(2)}) collective-permute-start(bf16[8,2560]{1,0:T(8,128)(2,1)S(1)} %get-tuple-element.39._), channel_id=1, source_target_pairs={{4,8},{5,9},{6,10},{7,11},{20,24},{21,25},{22,26},{23,27}} | collective-permute-start | bytes 122888 | tf_op jit(solution)/shard_map/ppermute | solution.py:387
  4.2 2.9 %collective-permute-start.3 = (bf16[128,512]{1,0:T(8,128)(2,1)S(1)}, bf16[128,512]{1,0:T(8,128)(2,1)S(1)}, u32[]{:S(2)}, u32[]{:S(2)}) collective-permute-start(bf16[128,512]{1,0:T(8,128)(2,1)S(1)} %next_states.4._), channel_id=1, source_target_pairs={{0,4},{1,5},{2,6},{3,7},{16,20},{17,21},{18,22},{19,23}} | collective-permute-start | bytes 393224 | tf_op jit(solution)/shard_map/ppermute | solution.py:387
  4.9 2.9 %collective-permute-start.2 = (bf16[128,512]{1,0:T(8,128)(2,1)S(1)}, bf16[128,512]{1,0:T(8,128)(2,1)S(1)}, u32[]{:S(2)}, u32[]{:S(2)}) collective-permute-start(bf16[128,512]{1,0:T(8,128)(2,1)S(1)} %next_states.5), channel_id=1, source_target_pairs={{0,4},{1,5},{2,6},{3,7},{16,20},{17,21},{18,22},{19,23}} | collective-permute-start | bytes 393224 | tf_op jit(solution)/shard_map/ppermute | solution.py:387
  5.7 4.3 %collective-permute-start.8 = (bf16[128,512]{1,0:T(8,128)(2,1)S(1)}, bf16[128,512]{1,0:T(8,128)(2,1)S(1)}, u32[]{:S(2)}, u32[]{:S(2)}) collective-permute-start(bf16[128,512]{1,0:T(8,128)(2,1)S(1)} %add_convert_fusion.7._), channel_id=1, source_target_pairs={{4,8},{5,9},{6,10},{7,11},{20,24},{21,25},{22,26},{23,27}} | collective-permute-start | bytes 393224 | tf_op jit(solution)/shard_map/ppermute | solution.py:387
  6.4 4.9 %collective-permute-start.7 = (bf16[128,512]{1,0:T(8,128)(2,1)S(1)}, bf16[128,512]{1,0:T(8,128)(2,1)S(1)}, u32[]{:S(2)}, u32[]{:S(2)}) collective-permute-start(bf16[128,512]{1,0:T(8,128)(2,1)S(1)} %add_convert_fusion.6._), channel_id=1, source_target_pairs={{4,8},{5,9},{6,10},{7,11},{20,24},{21,25},{22,26},{23,27}} | collective-permute-start | bytes 393224 | tf_op jit(solution)/shard_map/ppermute | solution.py:387
  7.2 5.7 %collective-permute-start.6 = (bf16[128,512]{1,0:T(8,128)(2,1)S(1)}, bf16[128,512]{1,0:T(8,128)(2,1)S(1)}, u32[]{:S(2)}, u32[]{:S(2)}) collective-permute-start(bf16[128,512]{1,0:T(8,128)(2,1)S(1)} %add_convert_fusion.5._), channel_id=1, source_target_pairs={{4,8},{5,9},{6,10},{7,11},{20,24},{21,25},{22,26},{23,27}} | collective-permute-start | bytes 393224 | tf_op jit(solution)/shard_map/ppermute | solution.py:387
  7.9 7.5 %collective-permute-start.10 = (bf16[128,512]{1,0:T(8,128)(2,1)S(1)}, bf16[128,512]{1,0:T(8,128)(2,1)S(1)}, u32[]{:S(2)}, u32[]{:S(2)}) collective-permute-start(bf16[128,512]{1,0:T(8,128)(2,1)S(1)} %add_convert_fusion.4._), channel_id=1, source_target_pairs={{4,8},{5,9},{6,10},{7,11},{20,24},{21,25},{22,26},{23,27}} | collective-permute-start | bytes 393224 | tf_op jit(solution)/shard_map/ppermute | solution.py:387
  8.6 6.8 %collective-permute-start.5 = (bf16[8,2560]{1,0:T(8,128)(2,1)S(1)}, bf16[8,2560]{1,0:T(8,128)(2,1)S(1)}, u32[]{:S(2)}, u32[]{:S(2)}) collective-permute-start(bf16[8,2560]{1,0:T(8,128)(2,1)S(1)} %get-tuple-element.39._), channel_id=1, source_target_pairs={{8,12},{9,13},{10,14},{11,15},{24,28},{25,29},{26,30},{27,31}} | collective-permute-start | bytes 122888 | tf_op jit(solution)/shard_map/ppermute | solution.py:387
  10.0 11.9 %collective-permute-start.12 = (bf16[128,512]{1,0:T(8,128)(2,1)S(1)}, bf16[128,512]{1,0:T(8,128)(2,1)S(1)}, u32[]{:S(2)}, u32[]{:S(2)}) collective-permute-start(bf16[128,512]{1,0:T(8,128)(2,1)S(1)} %add_convert_fusion.3), channel_id=1, source_target_pairs={{8,12},{9,13},{10,14},{11,15},{24,28},{25,29},{26,30},{27,31}} | collective-permute-start | bytes 393224 | tf_op jit(solution)/shard_map/ppermute | solution.py:387
  11.4 6.0 %copy-start.4 = (bf16[128,2048]{1,0:T(8,128)(2,1)S(1)}, bf16[128,2048]{1,0:T(8,128)(2,1)}, u32[]{:S(2)}) copy-start(bf16[128,2048]{1,0:T(8,128)(2,1)} %refs_5_.1) | copy-start | bytes 1572868
  11.4 13.8 %collective-permute-start.13 = (bf16[128,512]{1,0:T(8,128)(2,1)S(1)}, bf16[128,512]{1,0:T(8,128)(2,1)S(1)}, u32[]{:S(2)}, u32[]{:S(2)}) collective-permute-start(bf16[128,512]{1,0:T(8,128)(2,1)S(1)} %add_convert_fusion.2), channel_id=1, source_target_pairs={{8,12},{9,13},{10,14},{11,15},{24,28},{25,29},{26,30},{27,31}} | collective-permute-start | bytes 393224 | tf_op jit(solution)/shard_map/ppermute | solution.py:387
  12.9 14.2 %collective-permute-start.9 = (bf16[128,512]{1,0:T(8,128)(2,1)S(1)}, bf16[128,512]{1,0:T(8,128)(2,1)S(1)}, u32[]{:S(2)}, u32[]{:S(2)}) collective-permute-start(bf16[128,512]{1,0:T(8,128)(2,1)S(1)} %add_convert_fusion.1), channel_id=1, source_target_pairs={{8,12},{9,13},{10,14},{11,15},{24,28},{25,29},{26,30},{27,31}} | collective-permute-start | bytes 393224 | tf_op jit(solution)/shard_map/ppermute | solution.py:387
  16.1 13.3 %collective-permute-start.11 = (bf16[128,512]{1,0:T(8,128)(2,1)}, bf16[128,512]{1,0:T(8,128)(2,1)S(1)}, u32[]{:S(2)}, u32[]{:S(2)}) collective-permute-start(bf16[128,512]{1,0:T(8,128)(2,1)} %add_convert_fusion), channel_id=1, source_target_pairs={{8,12},{9,13},{10,14},{11,15},{24,28},{25,29},{26,30},{27,31}} | collective-permute-start | bytes 393224 | tf_op jit(solution)/shard_map/ppermute | solution.py:387

commit v18 on v16

--- a/solution.py
+++ b/solution.py
@@ -199,7 +199,8 @@
     return pltpu.roll(below, (RIM - keep * (begin // step + 1)) % below.shape[0], 0)[:RIM]
 
 
-def later_kernel(low, high, active, rows, _, x, bc, taps_x, taps_bc, scale, state):
+def later_kernel(low, high, active, rows, _, x, bc, taps_x, taps_bc, scale, *refs):
+    state = refs[-1]
     both = bc.shape[2]
     state_dim = both // 2
     keep = taps_x.shape[0] - 1
@@ -415,14 +416,14 @@
             name="prepared",
         )(token, x_in, bc_in, dt_t, a_row, gain)
 
-    def later_states(condition, rows, token, scale, low, high):
+    def later_states(condition, rows, token, scale, low, high, at_hand=()):
         return pl.pallas_call(
             functools.partial(later_kernel, low, high),
             out_shape=jax.ShapeDtypeStruct((state_dim, high - low), F32),
-            in_specs=[scalar, in_vmem, anywhere] + [in_vmem] * (len(sources) + 1),
+            in_specs=[scalar, in_vmem, anywhere] + [in_vmem] * (len(sources) + 1 + len(at_hand)),
             compiler_params=params(16),
             name="later_states",
-        )(here(condition), rows, token, *sources, scale)
+        )(here(condition), rows, token, *sources, scale, *at_hand)
 
     along = [(i, i + 1) for i in range(devices - 1)]
     def intra(token, befores):
@@ -461,11 +462,13 @@
             after = token
             for i, cut in enumerate(cuts):
                 if hop <= 2:
-                    made = later_states(runs, rows, after, scale_own, *cut)
+                    made = later_states(
+                        runs, rows, after, scale_own, *cut, at_hand=() if hop == 1 else (d_row,)
+                    )
                     states = [made] if i == 0 else states + [made]
                 early = ()
                 if hop == devices - 2 and hop > 1 and i == len(cuts) - 1:
-                    early = (befores[-1],)
+                    early = (arrived[0][-1], befores[-1])
                 before, *_ = lax.optimization_barrier((arrived[i][-1], token) + early)
                 joined = decays[i] * before[:state_dim].astype(F32) + states[i]
                 token = joined.astype(BF16)

time: 30.2 us -> 29.6 us (0.980)
  the two profiles are of different devices: /device:TPU:20 before, /device:TPU:30 now
where the time goes in v18:
time: 29.6 us; the launch traced here: 29.3 us
  starting transfers between devices  12.7 us (43%)
  waiting for transfers between devices  9.55 us (32%)
  Pallas kernels  5.42 us (18%)
  local copies, waits for them, and re-layouts  0.84 us (3%)
  between operations  0.43 us (1%)
  other arithmetic  0.31 us (1%)
    ppermute x14, starting transfers between devices, shifted(): return lax.ppermute(value, 'seq', route)  12.7 us
    ppermute x14, waiting for transfers between devices, shifted(): return lax.ppermute(value, 'seq', route)  9.55 us
    pallas_call x1, Pallas kernels, intra(): pl.pallas_call(functools.partial(intra_kernel, len(befores)), out_shape=[...  2.16 us
    pallas_call x2, Pallas kernels, shards(): pl.pallas_call(functools.partial(output_kernel, begin, spans, unready), o...  1.96 us
    unnamed x18, local copies, waits for them, and re-layouts  0.84 us
    pallas_call x1, Pallas kernels, prepared(): pl.pallas_call(functools.partial(prepare_kernel, cuts), out_shape=[jax.Sh...  0.62 us
  transfers between devices with their start and end apart: 14, of which 4 were waited for; matrix products, arithmetic and copies ran while one was open for 1% of the time, Pallas kernels for 15%

profile of v18, /device:TPU:30, one launch (start us, length us, event | category | flops | bytes accessed | tf_op | source)
XLA Modules:
  0.0 29.3 jit_solution(7356067616589245042)
XLA Ops:
  0.0 0.0 copy-start.3
  0.0 0.1 first_states.1
  0.1 0.8 %collective-permute-start.1 = (bf16[144,512]{1,0:T(8,128)(2,1)S(1)}, bf16[144,512]{1,0:T(8,128)(2,1)S(1)}, u32[]{:S(2)}, u32[]{:S(2)}) collective-permute-start(bf16[144,512]{1,0:T(8,128)(2,1)S(1)} %get-tuple-element.26._), channel_id=1, source_target_pairs={{0,4},{1,5},{2,6},{3,7},{16,20},{17,21},{18,22},{19,23}} | collective-permute-start | bytes 442376 | tf_op jit(solution)/shard_map/ppermute | solution.py:382
  0.9 0.1 copy-done
  1.0 0.0 copy-done.1
  1.1 0.0 copy-done.2
  1.1 0.0 copy-done.3
  1.1 0.0 copy-start.8
  1.1 0.7 %collective-permute-start.4 = (bf16[128,512]{1,0:T(8,128)(2,1)S(1)}, bf16[128,512]{1,0:T(8,128)(2,1)S(1)}, u32[]{:S(2)}, u32[]{:S(2)}) collective-permute-start(bf16[128,512]{1,0:T(8,128)(2,1)S(1)} %next_states.3._), channel_id=1, source_target_pairs={{0,4},{1,5},{2,6},{3,7},{16,20},{17,21},{18,22},{19,23}} | collective-permute-start | bytes 393224 | tf_op jit(solution)/shard_map/ppermute | solution.py:382
  1.8 0.0 copy-done.5
  1.8 0.0 copy-done.7
  1.8 0.0 copy-done.8
  1.8 0.6 %prepared.1 = (bf16[8,2560]{1,0:T(8,128)(2,1)S(1)}, f32[1,2048]{1,0:T(1,128)S(1)}, f32[128,2048]{1,0:T(8,128)S(1)}, f32[1,512]{1,0:T(1,128)S(1)}, f32[1,512]{1,0...) custom-call(bf16[128,512]{1,0:T(8,128)(2,1)S(1)} %next_states.3._, bf16[128,2048]{1,0:T(8,128)(2,1)S(1)} %copy-done, ...), custom_call_target="tpu_custom_call" | custom-call | tf_op jit(solution)/shard_map/prepared/pallas_call | solution.py:406
  2.4 0.7 %collective-permute-start = (bf16[8,2560]{1,0:T(8,128)(2,1)S(1)}, bf16[8,2560]{1,0:T(8,128)(2,1)S(1)}, u32[]{:S(2)}, u32[]{:S(2)}) collective-permute-start(bf16[8,2560]{1,0:T(8,128)(2,1)S(1)} %get-tuple-element.38._), channel_id=1, source_target_pairs={{4,8},{5,9},{6,10},{7,11},{20,24},{21,25},{22,26},{23,27}} | collective-permute-start | bytes 122888 | tf_op jit(solution)/shard_map/ppermute | solution.py:382
  3.1 0.7 %collective-permute-start.3 = (bf16[128,512]{1,0:T(8,128)(2,1)S(1)}, bf16[128,512]{1,0:T(8,128)(2,1)S(1)}, u32[]{:S(2)}, u32[]{:S(2)}) collective-permute-start(bf16[128,512]{1,0:T(8,128)(2,1)S(1)} %next_states.4._), channel_id=1, source_target_pairs={{0,4},{1,5},{2,6},{3,7},{16,20},{17,21},{18,22},{19,23}} | collective-permute-start | bytes 393224 | tf_op jit(solution)/shard_map/ppermute | solution.py:382
  3.8 0.7 %collective-permute-start.2 = (bf16[128,512]{1,0:T(8,128)(2,1)S(1)}, bf16[128,512]{1,0:T(8,128)(2,1)S(1)}, u32[]{:S(2)}, u32[]{:S(2)}) collective-permute-start(bf16[128,512]{1,0:T(8,128)(2,1)S(1)} %next_states.5), channel_id=1, source_target_pairs={{0,4},{1,5},{2,6},{3,7},{16,20},{17,21},{18,22},{19,23}} | collective-permute-start | bytes 393224 | tf_op jit(solution)/shard_map/ppermute | solution.py:382
  4.5 0.0 collective-permute-done.1.rows.refs_1_.refs_0_
  4.6 0.7 %collective-permute-start.8 = (bf16[128,512]{1,0:T(8,128)(2,1)S(1)}, bf16[128,512]{1,0:T(8,128)(2,1)S(1)}, u32[]{:S(2)}, u32[]{:S(2)}) collective-permute-start(bf16[128,512]{1,0:T(8,128)(2,1)S(1)} %add_convert_fusion.7._), channel_id=1, source_target_pairs={{4,8},{5,9},{6,10},{7,11},{20,24},{21,25},{22,26},{23,27}} | collective-permute-start | bytes 393224 | tf_op jit(solution)/shard_map/ppermute | solution.py:382
  5.3 0.0 collective-permute-done.4.refs_0_
  5.3 0.7 %collective-permute-start.7 = (bf16[128,512]{1,0:T(8,128)(2,1)S(1)}, bf16[128,512]{1,0:T(8,128)(2,1)S(1)}, u32[]{:S(2)}, u32[]{:S(2)}) collective-permute-start(bf16[128,512]{1,0:T(8,128)(2,1)S(1)} %add_convert_fusion.6._), channel_id=1, source_target_pairs={{4,8},{5,9},{6,10},{7,11},{20,24},{21,25},{22,26},{23,27}} | collective-permute-start | bytes 393224 | tf_op jit(solution)/shard_map/ppermute | solution.py:382
  6.0 0.0 collective-permute-done.3.refs_0_
  6.1 0.7 %collective-permute-start.6 = (bf16[128,512]{1,0:T(8,128)(2,1)S(1)}, bf16[128,512]{1,0:T(8,128)(2,1)S(1)}, u32[]{:S(2)}, u32[]{:S(2)}) collective-permute-start(bf16[128,512]{1,0:T(8,128)(2,1)S(1)} %add_convert_fusion.5._), channel_id=1, source_target_pairs={{4,8},{5,9},{6,10},{7,11},{20,24},{21,25},{22,26},{23,27}} | collective-permute-start | bytes 393224 | tf_op jit(solution)/shard_map/ppermute | solution.py:382
  6.8 0.0 collective-permute-done.2.refs_1_
  6.8 0.7 %collective-permute-start.10 = (bf16[128,512]{1,0:T(8,128)(2,1)S(1)}, bf16[128,512]{1,0:T(8,128)(2,1)S(1)}, u32[]{:S(2)}, u32[]{:S(2)}) collective-permute-start(bf16[128,512]{1,0:T(8,128)(2,1)S(1)} %add_convert_fusion.4._), channel_id=1, source_target_pairs={{4,8},{5,9},{6,10},{7,11},{20,24},{21,25},{22,26},{23,27}} | collective-permute-start | bytes 393224 | tf_op jit(solution)/shard_map/ppermute | solution.py:382
  7.5 0.0 collective-permute-done.refs_0_.rows
  7.5 1.3 %collective-permute-start.5 = (bf16[8,2560]{1,0:T(8,128)(2,1)S(1)}, bf16[8,2560]{1,0:T(8,128)(2,1)S(1)}, u32[]{:S(2)}, u32[]{:S(2)}) collective-permute-start(bf16[8,2560]{1,0:T(8,128)(2,1)S(1)} %get-tuple-element.38._), channel_id=1, source_target_pairs={{8,12},{9,13},{10,14},{11,15},{24,28},{25,29},{26,30},{27,31}} | collective-permute-start | bytes 122888 | tf_op jit(solution)/shard_map/ppermute | solution.py:382
  8.8 0.0 copy-start.6
  8.8 0.6 %copy-done.6 = f32[32]{0:T(128)S(1)} copy-done((f32[32]{0:T(128)S(1)}, f32[32]{0:T(128)}, u32[]{:S(2)}) %copy-start.6) | copy-done | bytes 152
  9.5 0.0 collective-permute-done.8.refs_1_
  9.5 1.3 %collective-permute-start.11 = (bf16[128,512]{1,0:T(8,128)(2,1)S(1)}, bf16[128,512]{1,0:T(8,128)(2,1)S(1)}, u32[]{:S(2)}, u32[]{:S(2)}) collective-permute-start(bf16[128,512]{1,0:T(8,128)(2,1)S(1)} %add_convert_fusion.3), channel_id=1, source_target_pairs={{8,12},{9,13},{10,14},{11,15},{24,28},{25,29},{26,30},{27,31}} | collective-permute-start | bytes 393224 | tf_op jit(solution)/shard_map/ppermute | solution.py:382
  10.8 0.0 collective-permute-done.7.refs_1_
  10.9 0.0 copy-start.4
  10.9 1.4 %collective-permute-start.13 = (bf16[128,512]{1,0:T(8,128)(2,1)S(1)}, bf16[128,512]{1,0:T(8,128)(2,1)S(1)}, u32[]{:S(2)}, u32[]{:S(2)}) collective-permute-start(bf16[128,512]{1,0:T(8,128)(2,1)S(1)} %add_convert_fusion.2), channel_id=1, source_target_pairs={{8,12},{9,13},{10,14},{11,15},{24,28},{25,29},{26,30},{27,31}} | collective-permute-start | bytes 393224 | tf_op jit(solution)/shard_map/ppermute | solution.py:382
  12.3 0.0 collective-permute-done.6.refs_1_
  12.4 1.3 %collective-permute-start.9 = (bf16[128,512]{1,0:T(8,128)(2,1)S(1)}, bf16[128,512]{1,0:T(8,128)(2,1)S(1)}, u32[]{:S(2)}, u32[]{:S(2)}) collective-permute-start(bf16[128,512]{1,0:T(8,128)(2,1)S(1)} %add_convert_fusion.1), channel_id=1, source_target_pairs={{8,12},{9,13},{10,14},{11,15},{24,28},{25,29},{26,30},{27,31}} | collective-permute-start | bytes 393224 | tf_op jit(solution)/shard_map/ppermute | solution.py:382
  13.7 0.7 %collective-permute-done.5.refs_2_ = bf16[8,2560]{1,0:T(8,128)(2,1)S(1)} collective-permute-done((bf16[8,2560]{1,0:T(8,128)(2,1)S(1)}, bf16[8,2560]{1,0:T(8,128)(2,1)S(1)}, u32[]{:S(2)}, u32[]{:S(2)}) %collective-permute-start.5) | collective-permute-done | bytes 40992 | tf_op jit(solution)/shard_map/ppermute | solution.py:382
  14.4 0.0 collective-permute-done.10.refs_2_
  14.4 6.6 %collective-permute-done.11.refs_2_ = bf16[128,512]{1,0:T(8,128)(2,1)S(1)} collective-permute-done((bf16[128,512]{1,0:T(8,128)(2,1)S(1)}, bf16[128,512]{1,0:T(8,128)(2,1)S(1)}, u32[]{:S(2)}, u32[]{:S(2)}) %collective-permute-start.11) | collective-permute-done | bytes 131104 | tf_op jit(solution)/shard_map/ppermute | solution.py:382
  21.0 1.3 %collective-permute-start.12 = (bf16[128,512]{1,0:T(8,128)(2,1)S(1)}, bf16[128,512]{1,0:T(8,128)(2,1)S(1)}, u32[]{:S(2)}, u32[]{:S(2)}) collective-permute-start(bf16[128,512]{1,0:T(8,128)(2,1)S(1)} %add_convert_fusion), channel_id=1, source_target_pairs={{8,12},{9,13},{10,14},{11,15},{24,28},{25,29},{26,30},{27,31}} | collective-permute-start | bytes 393224 | tf_op jit(solution)/shard_map/ppermute | solution.py:382
  22.3 2.2 %intra.1 = (f32[128,2048]{1,0:T(8,128)S(1)}, f32[128,2048]{1,0:T(8,128)S(1)}, bf16[128,256]{1,0:T(8,128)(2,1)S(1)}) custom-call(f32[1,32]{1,0:T(1,128)S(1)} %bitcast.31, bf16[8,2560]{1,0:T(8,128)(2,1)S(1)} %collective-permute-done.refs_0_.rows, bf16[144,512]{1,0:T(8,128)(2,1)S(1)} %collective-permute-done.1.rows.refs_1_.refs_0_, ...), custom_call_target="tpu_custom_call" | custom-call | flops 134217728 | bytes 3145728 | tf_op jit(solution)/shard_map/intra/pallas_call | solution.py:430
  24.5 0.2 gated.4.refs_0_
  24.7 0.0 collective-permute-done.13.refs_2_
  24.7 0.2 gated.5.refs_1_
  24.9 0.9 %outputs.2.refs_4_ = bf16[128,2048]{1,0:T(8,128)(2,1)} custom-call(s32[1]{0:T(128)} %bitcast.which, bf16[128,256]{1,0:T(8,128)(2,1)S(1)} %get-tuple-element.39.c, f32[128,2048]{1,0:T(8,128)S(1)} %get-tuple-element.40.y_part, f32[128,2048]{1,0:T(8,128)S(1)} %get-tuple-element.41.lead, f32[1,2048]{1,0:T(1,128)S(1)} %get-tuple-element.42.gain, ...), custom_call_target="tpu_custom_call" | custom-call | tf_op jit(solution)/shard_map/outputs/pallas_call | solution.py:526
  25.8 1.0 %collective-permute-done.9.refs_2_ = bf16[128,512]{1,0:T(8,128)(2,1)S(1)} collective-permute-done((bf16[128,512]{1,0:T(8,128)(2,1)S(1)}, bf16[128,512]{1,0:T(8,128)(2,1)S(1)}, u32[]{:S(2)}, u32[]{:S(2)}) %collective-permute-start.9) | collective-permute-done | bytes 131104 | tf_op jit(solution)/shard_map/ppermute | solution.py:382
  26.8 0.2 gated.3.refs_0_
  27.0 1.2 %collective-permute-done.12.refs_3_ = bf16[128,512]{1,0:T(8,128)(2,1)S(1)} collective-permute-done((bf16[128,512]{1,0:T(8,128)(2,1)S(1)}, bf16[128,512]{1,0:T(8,128)(2,1)S(1)}, u32[]{:S(2)}, u32[]{:S(2)}) %collective-permute-start.12) | collective-permute-done | bytes 131104 | tf_op jit(solution)/shard_map/ppermute | solution.py:382
  28.2 1.0 %outputs.3 = bf16[128,2048]{1,0:T(8,128)(2,1)} custom-call(s32[1]{0:T(128)} %bitcast.which, bf16[128,256]{1,0:T(8,128)(2,1)S(1)} %get-tuple-element.39.c, f32[128,2048]{1,0:T(8,128)S(1)} %get-tuple-element.40.y_part, f32[128,2048]{1,0:T(8,128)S(1)} %get-tuple-element.41.lead, f32[1,2048]{1,0:T(1,128)S(1)} %get-tuple-element.42.gain, ...), custom_call_target="tpu_custom_call", output_to_operand_aliasing={{}: (9, {})} | custom-call | tf_op jit(solution)/shard_map/outputs/pallas_call | solution.py:526
  (25 shorter events, 0.4 us)
Async XLA Ops:
  0.0 1.0 %copy-start = (bf16[128,2048]{1,0:T(8,128)(2,1)S(1)}, bf16[128,2048]{1,0:T(8,128)(2,1)}, u32[]{:S(2)}) copy-start(bf16[128,2048]{1,0:T(8,128)(2,1)} %x.23) | copy-start | bytes 1572868
  0.0 1.1 %copy-start.1 = (bf16[128,2,256]{2,1,0:T(2,128)(2,1)S(1)}, bf16[128,2,256]{2,1,0:T(2,128)(2,1)}, u32[]{:S(2)}) copy-start(bf16[128,2,256]{2,1,0:T(2,128)(2,1)} %bc.23) | copy-start | bytes 393220
  0.0 1.1 %copy-start.2 = (f32[4,2048]{1,0:T(4,128)S(1)}, f32[4,2048]{1,0:T(4,128)}, u32[]{:S(2)}) copy-start(f32[4,2048]{1,0:T(4,128)} %taps_x.21) | copy-start | bytes 98308
  0.0 1.1 %copy-start.3 = (f32[4,2,256]{2,1,0:T(2,128)S(1)}, f32[4,2,256]{2,1,0:T(2,128)}, u32[]{:S(2)}) copy-start(f32[4,2,256]{2,1,0:T(2,128)} %taps_bc.21) | copy-start | bytes 24580
  0.1 4.4 %collective-permute-start.1 = (bf16[144,512]{1,0:T(8,128)(2,1)S(1)}, bf16[144,512]{1,0:T(8,128)(2,1)S(1)}, u32[]{:S(2)}, u32[]{:S(2)}) collective-permute-start(bf16[144,512]{1,0:T(8,128)(2,1)S(1)} %get-tuple-element.26._), channel_id=1, source_target_pairs={{0,4},{1,5},{2,6},{3,7},{16,20},{17,21},{18,22},{19,23}} | collective-permute-start | bytes 442376 | tf_op jit(solution)/shard_map/ppermute | solution.py:382
  1.1 0.7 %copy-start.5 = (f32[128,32]{0,1:T(8,128)S(1)}, f32[128,32]{0,1:T(8,128)}, u32[]{:S(2)}) copy-start(f32[128,32]{0,1:T(8,128)} %param.12) | copy-start | bytes 49156
  1.1 0.7 %copy-start.7 = (f32[2048]{0:T(1024)S(1)}, f32[2048]{0:T(1024)}, u32[]{:S(2)}) copy-start(f32[2048]{0:T(1024)} %param.17) | copy-start | bytes 24580
  1.1 0.7 %copy-start.8 = (f32[32]{0:T(128)S(1)}, f32[32]{0:T(128)}, u32[]{:S(2)}) copy-start(f32[32]{0:T(128)} %param.15) | copy-start | bytes 388
  1.1 4.2 %collective-permute-start.4 = (bf16[128,512]{1,0:T(8,128)(2,1)S(1)}, bf16[128,512]{1,0:T(8,128)(2,1)S(1)}, u32[]{:S(2)}, u32[]{:S(2)}) collective-permute-start(bf16[128,512]{1,0:T(8,128)(2,1)S(1)} %next_states.3._), channel_id=1, source_target_pairs={{0,4},{1,5},{2,6},{3,7},{16,20},{17,21},{18,22},{19,23}} | collective-permute-start | bytes 393224 | tf_op jit(solution)/shard_map/ppermute | solution.py:382
  2.4 5.1 %collective-permute-start = (bf16[8,2560]{1,0:T(8,128)(2,1)S(1)}, bf16[8,2560]{1,0:T(8,128)(2,1)S(1)}, u32[]{:S(2)}, u32[]{:S(2)}) collective-permute-start(bf16[8,2560]{1,0:T(8,128)(2,1)S(1)} %get-tuple-element.38._), channel_id=1, source_target_pairs={{4,8},{5,9},{6,10},{7,11},{20,24},{21,25},{22,26},{23,27}} | collective-permute-start | bytes 122888 | tf_op jit(solution)/shard_map/ppermute | solution.py:382
  3.1 2.9 %collective-permute-start.3 = (bf16[128,512]{1,0:T(8,128)(2,1)S(1)}, bf16[128,512]{1,0:T(8,128)(2,1)S(1)}, u32[]{:S(2)}, u32[]{:S(2)}) collective-permute-start(bf16[128,512]{1,0:T(8,128)(2,1)S(1)} %next_states.4._), channel_id=1, source_target_pairs={{0,4},{1,5},{2,6},{3,7},{16,20},{17,21},{18,22},{19,23}} | collective-permute-start | bytes 393224 | tf_op jit(solution)/shard_map/ppermute | solution.py:382
  3.8 2.9 %collective-permute-start.2 = (bf16[128,512]{1,0:T(8,128)(2,1)S(1)}, bf16[128,512]{1,0:T(8,128)(2,1)S(1)}, u32[]{:S(2)}, u32[]{:S(2)}) collective-permute-start(bf16[128,512]{1,0:T(8,128)(2,1)S(1)} %next_states.5), channel_id=1, source_target_pairs={{0,4},{1,5},{2,6},{3,7},{16,20},{17,21},{18,22},{19,23}} | collective-permute-start | bytes 393224 | tf_op jit(solution)/shard_map/ppermute | solution.py:382
  4.6 4.9 %collective-permute-start.8 = (bf16[128,512]{1,0:T(8,128)(2,1)S(1)}, bf16[128,512]{1,0:T(8,128)(2,1)S(1)}, u32[]{:S(2)}, u32[]{:S(2)}) collective-permute-start(bf16[128,512]{1,0:T(8,128)(2,1)S(1)} %add_convert_fusion.7._), channel_id=1, source_target_pairs={{4,8},{5,9},{6,10},{7,11},{20,24},{21,25},{22,26},{23,27}} | collective-permute-start | bytes 393224 | tf_op jit(solution)/shard_map/ppermute | solution.py:382
  5.3 5.5 %collective-permute-start.7 = (bf16[128,512]{1,0:T(8,128)(2,1)S(1)}, bf16[128,512]{1,0:T(8,128)(2,1)S(1)}, u32[]{:S(2)}, u32[]{:S(2)}) collective-permute-start(bf16[128,512]{1,0:T(8,128)(2,1)S(1)} %add_convert_fusion.6._), channel_id=1, source_target_pairs={{4,8},{5,9},{6,10},{7,11},{20,24},{21,25},{22,26},{23,27}} | collective-permute-start | bytes 393224 | tf_op jit(solution)/shard_map/ppermute | solution.py:382
  6.1 6.3 %collective-permute-start.6 = (bf16[128,512]{1,0:T(8,128)(2,1)S(1)}, bf16[128,512]{1,0:T(8,128)(2,1)S(1)}, u32[]{:S(2)}, u32[]{:S(2)}) collective-permute-start(bf16[128,512]{1,0:T(8,128)(2,1)S(1)} %add_convert_fusion.5._), channel_id=1, source_target_pairs={{4,8},{5,9},{6,10},{7,11},{20,24},{21,25},{22,26},{23,27}} | collective-permute-start | bytes 393224 | tf_op jit(solution)/shard_map/ppermute | solution.py:382
  6.8 7.5 %collective-permute-start.10 = (bf16[128,512]{1,0:T(8,128)(2,1)S(1)}, bf16[128,512]{1,0:T(8,128)(2,1)S(1)}, u32[]{:S(2)}, u32[]{:S(2)}) collective-permute-start(bf16[128,512]{1,0:T(8,128)(2,1)S(1)} %add_convert_fusion.4._), channel_id=1, source_target_pairs={{4,8},{5,9},{6,10},{7,11},{20,24},{21,25},{22,26},{23,27}} | collective-permute-start | bytes 393224 | tf_op jit(solution)/shard_map/ppermute | solution.py:382
  7.5 6.8 %collective-permute-start.5 = (bf16[8,2560]{1,0:T(8,128)(2,1)S(1)}, bf16[8,2560]{1,0:T(8,128)(2,1)S(1)}, u32[]{:S(2)}, u32[]{:S(2)}) collective-permute-start(bf16[8,2560]{1,0:T(8,128)(2,1)S(1)} %get-tuple-element.38._), channel_id=1, source_target_pairs={{8,12},{9,13},{10,14},{11,15},{24,28},{25,29},{26,30},{27,31}} | collective-permute-start | bytes 122888 | tf_op jit(solution)/shard_map/ppermute | solution.py:382
  8.8 0.7 %copy-start.6 = (f32[32]{0:T(128)S(1)}, f32[32]{0:T(128)}, u32[]{:S(2)}) copy-start(f32[32]{0:T(128)} %param.16) | copy-start | bytes 388
  9.5 11.5 %collective-permute-start.11 = (bf16[128,512]{1,0:T(8,128)(2,1)S(1)}, bf16[128,512]{1,0:T(8,128)(2,1)S(1)}, u32[]{:S(2)}, u32[]{:S(2)}) collective-permute-start(bf16[128,512]{1,0:T(8,128)(2,1)S(1)} %add_convert_fusion.3), channel_id=1, source_target_pairs={{8,12},{9,13},{10,14},{11,15},{24,28},{25,29},{26,30},{27,31}} | collective-permute-start | bytes 393224 | tf_op jit(solution)/shard_map/ppermute | solution.py:382
  10.9 11.4 %copy-start.4 = (bf16[128,2048]{1,0:T(8,128)(2,1)S(1)}, bf16[128,2048]{1,0:T(8,128)(2,1)}, u32[]{:S(2)}) copy-start(bf16[128,2048]{1,0:T(8,128)(2,1)} %refs_5_.1) | copy-start | bytes 1572868
  10.9 13.8 %collective-permute-start.13 = (bf16[128,512]{1,0:T(8,128)(2,1)S(1)}, bf16[128,512]{1,0:T(8,128)(2,1)S(1)}, u32[]{:S(2)}, u32[]{:S(2)}) collective-permute-start(bf16[128,512]{1,0:T(8,128)(2,1)S(1)} %add_convert_fusion.2), channel_id=1, source_target_pairs={{8,12},{9,13},{10,14},{11,15},{24,28},{25,29},{26,30},{27,31}} | collective-permute-start | bytes 393224 | tf_op jit(solution)/shard_map/ppermute | solution.py:382
  12.4 14.4 %collective-permute-start.9 = (bf16[128,512]{1,0:T(8,128)(2,1)S(1)}, bf16[128,512]{1,0:T(8,128)(2,1)S(1)}, u32[]{:S(2)}, u32[]{:S(2)}) collective-permute-start(bf16[128,512]{1,0:T(8,128)(2,1)S(1)} %add_convert_fusion.1), channel_id=1, source_target_pairs={{8,12},{9,13},{10,14},{11,15},{24,28},{25,29},{26,30},{27,31}} | collective-permute-start | bytes 393224 | tf_op jit(solution)/shard_map/ppermute | solution.py:382
  21.0 7.2 %collective-permute-start.12 = (bf16[128,512]{1,0:T(8,128)(2,1)S(1)}, bf16[128,512]{1,0:T(8,128)(2,1)S(1)}, u32[]{:S(2)}, u32[]{:S(2)}) collective-permute-start(bf16[128,512]{1,0:T(8,128)(2,1)S(1)} %add_convert_fusion), channel_id=1, source_target_pairs={{8,12},{9,13},{10,14},{11,15},{24,28},{25,29},{26,30},{27,31}} | collective-permute-start | bytes 393224 | tf_op jit(solution)/shard_map/ppermute | solution.py:382

commit v19 on v18

--- a/solution.py
+++ b/solution.py
@@ -225,7 +225,9 @@
 
 def intra_kernel(count, _, *refs):
     sources, refs = refs[:count], refs[count:]
-    x, bc, z, taps_x, taps_bc, dt_raw, a_log, d_skip, y_part, lead, c_act, wide = refs
+    x, bc, z_hbm, taps_x, taps_bc, dt_raw, a_log, d_skip, y_part, lead, c_act, wide, z, sem = refs
+    z_copy = pltpu.make_async_copy(z_hbm, z, sem.at[0])
+    z_copy.start()
     tokens, width = x.shape
     groups, both = bc.shape[1:]
     state_dim = both // 2
@@ -256,6 +258,8 @@
         inner = lax.dot_general(c, b, (((1,), (1,)), ((), ())), preferred_element_type=F32)
         inner = jnp.where(t_at >= s_at, inner, 0.0)
         wide[...] = spread(leading[g * heads : (g + 1) * heads], head_dim, 2)
+        if g == 0:
+            z_copy.wait()
         for first in range(0, heads, 2):
             here = slice(first * head_dim, first * head_dim + pair)
             cut = slice(g * cols + here.start, g * cols + here.stop)
@@ -368,6 +372,7 @@
     sources = [x_in, bc_in, conv_x, conv_bc]
     operands = sources + [dt_t, a_row]
     pinned = [pltpu.with_memory_space_constraint(v, pltpu.HBM) for v in operands]
+    z_pinned = pltpu.with_memory_space_constraint(z_in, pltpu.HBM)
     landed = [pltpu.VMEM(v.shape, v.dtype) for v in operands]
     scale_shape = jax.ShapeDtypeStruct((tokens, width), F32)
     scalar = pl.BlockSpec(memory_space=pltpu.SMEM)
@@ -432,8 +437,15 @@
             out_shape=[
                 scale_shape, scale_shape, jax.ShapeDtypeStruct((tokens, groups * state_dim), BF16)
             ],
-            in_specs=[anywhere] + [in_vmem] * (len(befores) + 8),
-            scratch_shapes=[pltpu.VMEM((tokens, cols), F32)],
+            in_specs=[anywhere]
+            + [in_vmem] * (len(befores) + 2)
+            + [pl.BlockSpec(memory_space=pltpu.HBM)]
+            + [in_vmem] * 5,
+            scratch_shapes=[
+                pltpu.VMEM((tokens, cols), F32),
+                pltpu.VMEM(z_in.shape, z_in.dtype),
+                pltpu.SemaphoreType.DMA((1,)),
+            ],
             compiler_params=params(24),
             cost_estimate=pl.CostEstimate(
                 flops=4 * tokens * tokens * width,
@@ -441,7 +453,7 @@
                 transcendentals=tokens * tokens * heads,
             ),
             name="intra",
-        )(token, *befores, x_in, bc_in, z_in, conv_x, conv_bc, dt_t, a_row, d_row)
+        )(token, *befores, x_in, bc_in, z_pinned, conv_x, conv_bc, dt_t, a_row, d_row)
 
     if devices <= CHAIN_MOST:
         first, scale = first_states(*cuts[0])
@@ -468,7 +480,7 @@
                     states = [made] if i == 0 else states + [made]
                 early = ()
                 if hop == devices - 2 and hop > 1 and i == len(cuts) - 1:
-                    early = (arrived[0][-1], befores[-1])
+                    early = (befores[-1],)
                 before, *_ = lax.optimization_barrier((arrived[i][-1], token) + early)
                 joined = decays[i] * before[:state_dim].astype(F32) + states[i]
                 token = joined.astype(BF16)

time: 29.6 us -> 29.8 us (level)
  Pallas kernels: 5.42 us -> 6.25 us
  waiting for transfers between devices: 9.55 us -> 8.87 us
    pallas_call x1, Pallas kernels: 2.16 us -> 3 us  [intra(): pl.pallas_call(functools.partial(intra_kernel, len(befores)), out_shape=[...]
    ppermute x14, waiting for transfers between devices: 9.55 us -> 8.87 us  [shifted(): return lax.ppermute(value, 'seq', route)]
    unnamed x18 -> x16, local copies, waits for them, and re-layouts: 0.84 us -> 0.84 us
  transfers between devices with their start and end apart: 14 -> 14, of which waited for: 4 -> 5; matrix products, arithmetic and copies ran while one was open for 1% -> 1% of each run, Pallas kernels for 15% -> 18%
where the time goes in v19:
time: 29.8 us; the launch traced here: 29.3 us
  starting transfers between devices  12.6 us (42%)
  waiting for transfers between devices  8.87 us (30%)
  Pallas kernels  6.25 us (21%)
  local copies, waits for them, and re-layouts  0.84 us (3%)
  between operations  0.41 us (1%)
  other arithmetic  0.31 us (1%)
    ppermute x14, starting transfers between devices, shifted(): return lax.ppermute(value, 'seq', route)  12.6 us
    ppermute x14, waiting for transfers between devices, shifted(): return lax.ppermute(value, 'seq', route)  8.87 us
    pallas_call x1, Pallas kernels, intra(): pl.pallas_call(functools.partial(intra_kernel, len(befores)), out_shape=[...  3 us
    pallas_call x2, Pallas kernels, shards(): pl.pallas_call(functools.partial(output_kernel, begin, spans, unready), o...  1.96 us
    unnamed x16, local copies, waits for them, and re-layouts  0.84 us
    pallas_call x1, Pallas kernels, prepared(): pl.pallas_call(functools.partial(prepare_kernel, cuts), out_shape=[jax.Sh...  0.62 us
  transfers between devices with their start and end apart: 14, of which 5 were waited for; matrix products, arithmetic and copies ran while one was open for 1% of the time, Pallas kernels for 18%

profile of v19, /device:TPU:30, one launch (start us, length us, event | category | flops | bytes accessed | tf_op | source)
XLA Modules:
  0.0 29.3 jit_solution(11586188717685727344)
XLA Ops:
  0.0 0.0 copy-start
  0.0 0.0 copy-start.3
  0.0 0.1 first_states.1
  0.1 0.8 %collective-permute-start.1 = (bf16[144,512]{1,0:T(8,128)(2,1)S(1)}, bf16[144,512]{1,0:T(8,128)(2,1)S(1)}, u32[]{:S(2)}, u32[]{:S(2)}) collective-permute-start(bf16[144,512]{1,0:T(8,128)(2,1)S(1)} %get-tuple-element.26._), channel_id=1, source_target_pairs={{0,4},{1,5},{2,6},{3,7},{16,20},{17,21},{18,22},{19,23}} | collective-permute-start | bytes 442376 | tf_op jit(solution)/shard_map/ppermute | solution.py:387
  0.9 0.1 copy-done
  1.0 0.0 copy-done.1
  1.1 0.0 copy-done.2
  1.1 0.0 copy-done.3
  1.1 0.0 copy-start.7
  1.1 0.7 %collective-permute-start.4 = (bf16[128,512]{1,0:T(8,128)(2,1)S(1)}, bf16[128,512]{1,0:T(8,128)(2,1)S(1)}, u32[]{:S(2)}, u32[]{:S(2)}) collective-permute-start(bf16[128,512]{1,0:T(8,128)(2,1)S(1)} %next_states.3._), channel_id=1, source_target_pairs={{0,4},{1,5},{2,6},{3,7},{16,20},{17,21},{18,22},{19,23}} | collective-permute-start | bytes 393224 | tf_op jit(solution)/shard_map/ppermute | solution.py:387
  1.8 0.0 copy-done.4
  1.8 0.0 copy-done.6
  1.8 0.0 copy-done.7
  1.8 0.6 %prepared.1 = (bf16[8,2560]{1,0:T(8,128)(2,1)S(1)}, f32[1,2048]{1,0:T(1,128)S(1)}, f32[128,2048]{1,0:T(8,128)S(1)}, f32[1,512]{1,0:T(1,128)S(1)}, f32[1,512]{1,0...) custom-call(bf16[128,512]{1,0:T(8,128)(2,1)S(1)} %next_states.3._, bf16[128,2048]{1,0:T(8,128)(2,1)S(1)} %copy-done, ...), custom_call_target="tpu_custom_call" | custom-call | tf_op jit(solution)/shard_map/prepared/pallas_call | solution.py:411
  2.4 0.7 %collective-permute-start = (bf16[8,2560]{1,0:T(8,128)(2,1)S(1)}, bf16[8,2560]{1,0:T(8,128)(2,1)S(1)}, u32[]{:S(2)}, u32[]{:S(2)}) collective-permute-start(bf16[8,2560]{1,0:T(8,128)(2,1)S(1)} %get-tuple-element.38._), channel_id=1, source_target_pairs={{4,8},{5,9},{6,10},{7,11},{20,24},{21,25},{22,26},{23,27}} | collective-permute-start | bytes 122888 | tf_op jit(solution)/shard_map/ppermute | solution.py:387
  3.1 0.7 %collective-permute-start.3 = (bf16[128,512]{1,0:T(8,128)(2,1)S(1)}, bf16[128,512]{1,0:T(8,128)(2,1)S(1)}, u32[]{:S(2)}, u32[]{:S(2)}) collective-permute-start(bf16[128,512]{1,0:T(8,128)(2,1)S(1)} %next_states.4._), channel_id=1, source_target_pairs={{0,4},{1,5},{2,6},{3,7},{16,20},{17,21},{18,22},{19,23}} | collective-permute-start | bytes 393224 | tf_op jit(solution)/shard_map/ppermute | solution.py:387
  3.8 0.7 %collective-permute-start.2 = (bf16[128,512]{1,0:T(8,128)(2,1)S(1)}, bf16[128,512]{1,0:T(8,128)(2,1)S(1)}, u32[]{:S(2)}, u32[]{:S(2)}) collective-permute-start(bf16[128,512]{1,0:T(8,128)(2,1)S(1)} %next_states.5), channel_id=1, source_target_pairs={{0,4},{1,5},{2,6},{3,7},{16,20},{17,21},{18,22},{19,23}} | collective-permute-start | bytes 393224 | tf_op jit(solution)/shard_map/ppermute | solution.py:387
  4.5 0.0 collective-permute-done.1.rows.refs_1_.refs_0_
  4.6 0.7 %collective-permute-start.8 = (bf16[128,512]{1,0:T(8,128)(2,1)S(1)}, bf16[128,512]{1,0:T(8,128)(2,1)S(1)}, u32[]{:S(2)}, u32[]{:S(2)}) collective-permute-start(bf16[128,512]{1,0:T(8,128)(2,1)S(1)} %add_convert_fusion.7._), channel_id=1, source_target_pairs={{4,8},{5,9},{6,10},{7,11},{20,24},{21,25},{22,26},{23,27}} | collective-permute-start | bytes 393224 | tf_op jit(solution)/shard_map/ppermute | solution.py:387
  5.3 0.0 collective-permute-done.4.refs_0_
  5.3 0.7 %collective-permute-start.7 = (bf16[128,512]{1,0:T(8,128)(2,1)S(1)}, bf16[128,512]{1,0:T(8,128)(2,1)S(1)}, u32[]{:S(2)}, u32[]{:S(2)}) collective-permute-start(bf16[128,512]{1,0:T(8,128)(2,1)S(1)} %add_convert_fusion.6._), channel_id=1, source_target_pairs={{4,8},{5,9},{6,10},{7,11},{20,24},{21,25},{22,26},{23,27}} | collective-permute-start | bytes 393224 | tf_op jit(solution)/shard_map/ppermute | solution.py:387
  6.0 0.0 collective-permute-done.3.refs_0_
  6.1 0.7 %collective-permute-start.6 = (bf16[128,512]{1,0:T(8,128)(2,1)S(1)}, bf16[128,512]{1,0:T(8,128)(2,1)S(1)}, u32[]{:S(2)}, u32[]{:S(2)}) collective-permute-start(bf16[128,512]{1,0:T(8,128)(2,1)S(1)} %add_convert_fusion.5._), channel_id=1, source_target_pairs={{4,8},{5,9},{6,10},{7,11},{20,24},{21,25},{22,26},{23,27}} | collective-permute-start | bytes 393224 | tf_op jit(solution)/shard_map/ppermute | solution.py:387
  6.8 0.0 collective-permute-done.2.refs_1_
  6.8 0.7 %collective-permute-start.10 = (bf16[128,512]{1,0:T(8,128)(2,1)S(1)}, bf16[128,512]{1,0:T(8,128)(2,1)S(1)}, u32[]{:S(2)}, u32[]{:S(2)}) collective-permute-start(bf16[128,512]{1,0:T(8,128)(2,1)S(1)} %add_convert_fusion.4._), channel_id=1, source_target_pairs={{4,8},{5,9},{6,10},{7,11},{20,24},{21,25},{22,26},{23,27}} | collective-permute-start | bytes 393224 | tf_op jit(solution)/shard_map/ppermute | solution.py:387
  7.5 0.0 collective-permute-done.refs_0_.rows
  7.5 1.3 %collective-permute-start.5 = (bf16[8,2560]{1,0:T(8,128)(2,1)S(1)}, bf16[8,2560]{1,0:T(8,128)(2,1)S(1)}, u32[]{:S(2)}, u32[]{:S(2)}) collective-permute-start(bf16[8,2560]{1,0:T(8,128)(2,1)S(1)} %get-tuple-element.38._), channel_id=1, source_target_pairs={{8,12},{9,13},{10,14},{11,15},{24,28},{25,29},{26,30},{27,31}} | collective-permute-start | bytes 122888 | tf_op jit(solution)/shard_map/ppermute | solution.py:387
  8.8 0.0 copy-start.5
  8.8 0.6 %copy-done.5 = f32[32]{0:T(128)S(1)} copy-done((f32[32]{0:T(128)S(1)}, f32[32]{0:T(128)}, u32[]{:S(2)}) %copy-start.5) | copy-done | bytes 152
  9.5 0.0 collective-permute-done.8.refs_1_
  9.5 1.3 %collective-permute-start.12 = (bf16[128,512]{1,0:T(8,128)(2,1)S(1)}, bf16[128,512]{1,0:T(8,128)(2,1)S(1)}, u32[]{:S(2)}, u32[]{:S(2)}) collective-permute-start(bf16[128,512]{1,0:T(8,128)(2,1)S(1)} %add_convert_fusion.3), channel_id=1, source_target_pairs={{8,12},{9,13},{10,14},{11,15},{24,28},{25,29},{26,30},{27,31}} | collective-permute-start | bytes 393224 | tf_op jit(solution)/shard_map/ppermute | solution.py:387
  10.8 0.0 collective-permute-done.7.refs_1_
  10.9 1.3 %collective-permute-start.13 = (bf16[128,512]{1,0:T(8,128)(2,1)S(1)}, bf16[128,512]{1,0:T(8,128)(2,1)S(1)}, u32[]{:S(2)}, u32[]{:S(2)}) collective-permute-start(bf16[128,512]{1,0:T(8,128)(2,1)S(1)} %add_convert_fusion.2), channel_id=1, source_target_pairs={{8,12},{9,13},{10,14},{11,15},{24,28},{25,29},{26,30},{27,31}} | collective-permute-start | bytes 393224 | tf_op jit(solution)/shard_map/ppermute | solution.py:387
  12.2 0.0 collective-permute-done.6.refs_1_
  12.3 1.3 %collective-permute-start.9 = (bf16[128,512]{1,0:T(8,128)(2,1)S(1)}, bf16[128,512]{1,0:T(8,128)(2,1)S(1)}, u32[]{:S(2)}, u32[]{:S(2)}) collective-permute-start(bf16[128,512]{1,0:T(8,128)(2,1)S(1)} %add_convert_fusion.1), channel_id=1, source_target_pairs={{8,12},{9,13},{10,14},{11,15},{24,28},{25,29},{26,30},{27,31}} | collective-permute-start | bytes 393224 | tf_op jit(solution)/shard_map/ppermute | solution.py:387
  13.6 0.8 %collective-permute-done.5.refs_2_ = bf16[8,2560]{1,0:T(8,128)(2,1)S(1)} collective-permute-done((bf16[8,2560]{1,0:T(8,128)(2,1)S(1)}, bf16[8,2560]{1,0:T(8,128)(2,1)S(1)}, u32[]{:S(2)}, u32[]{:S(2)}) %collective-permute-start.5) | collective-permute-done | bytes 40992 | tf_op jit(solution)/shard_map/ppermute | solution.py:387
  14.4 0.0 collective-permute-done.10.refs_2_
  14.4 1.3 %collective-permute-start.11 = (bf16[128,512]{1,0:T(8,128)(2,1)S(1)}, bf16[128,512]{1,0:T(8,128)(2,1)S(1)}, u32[]{:S(2)}, u32[]{:S(2)}) collective-permute-start(bf16[128,512]{1,0:T(8,128)(2,1)S(1)} %add_convert_fusion), channel_id=1, source_target_pairs={{8,12},{9,13},{10,14},{11,15},{24,28},{25,29},{26,30},{27,31}} | collective-permute-start | bytes 393224 | tf_op jit(solution)/shard_map/ppermute | solution.py:387
  15.7 3.0 %intra.1 = (f32[128,2048]{1,0:T(8,128)S(1)}, f32[128,2048]{1,0:T(8,128)S(1)}, bf16[128,256]{1,0:T(8,128)(2,1)S(1)}) custom-call(f32[1,32]{1,0:T(1,128)S(1)} %bitcast.31, bf16[8,2560]{1,0:T(8,128)(2,1)S(1)} %collective-permute-done.refs_0_.rows, bf16[144,512]{1,0:T(8,128)(2,1)S(1)} %collective-permute-done.1.rows.refs_1_.refs_0_, ...), custom_call_target="tpu_custom_call" | custom-call | flops 134217728 | bytes 3145728 | tf_op jit(solution)/shard_map/intra/pallas_call | solution.py:435
  18.7 2.4 %collective-permute-done.12.refs_2_ = bf16[128,512]{1,0:T(8,128)(2,1)S(1)} collective-permute-done((bf16[128,512]{1,0:T(8,128)(2,1)S(1)}, bf16[128,512]{1,0:T(8,128)(2,1)S(1)}, u32[]{:S(2)}, u32[]{:S(2)}) %collective-permute-start.12) | collective-permute-done | bytes 131104 | tf_op jit(solution)/shard_map/ppermute | solution.py:387
  21.1 0.2 gated.4.refs_0_
  21.3 2.8 %collective-permute-done.13.refs_2_ = bf16[128,512]{1,0:T(8,128)(2,1)S(1)} collective-permute-done((bf16[128,512]{1,0:T(8,128)(2,1)S(1)}, bf16[128,512]{1,0:T(8,128)(2,1)S(1)}, u32[]{:S(2)}, u32[]{:S(2)}) %collective-permute-start.13) | collective-permute-done | bytes 131104 | tf_op jit(solution)/shard_map/ppermute | solution.py:387
  24.1 0.2 gated.5.refs_1_
  24.3 0.9 %outputs.2.refs_4_ = bf16[128,2048]{1,0:T(8,128)(2,1)} custom-call(s32[1]{0:T(128)} %bitcast.which, bf16[128,256]{1,0:T(8,128)(2,1)S(1)} %get-tuple-element.39.c, f32[128,2048]{1,0:T(8,128)S(1)} %get-tuple-element.40.y_part, f32[128,2048]{1,0:T(8,128)S(1)} %get-tuple-element.41.lead, f32[1,2048]{1,0:T(1,128)S(1)} %get-tuple-element.42.gain, ...), custom_call_target="tpu_custom_call" | custom-call | tf_op jit(solution)/shard_map/outputs/pallas_call | solution.py:538
  25.2 1.6 %collective-permute-done.9.refs_2_ = bf16[128,512]{1,0:T(8,128)(2,1)S(1)} collective-permute-done((bf16[128,512]{1,0:T(8,128)(2,1)S(1)}, bf16[128,512]{1,0:T(8,128)(2,1)S(1)}, u32[]{:S(2)}, u32[]{:S(2)}) %collective-permute-start.9) | collective-permute-done | bytes 131104 | tf_op jit(solution)/shard_map/ppermute | solution.py:387
  26.8 0.2 gated.3.refs_0_
  27.0 1.2 %collective-permute-done.11.refs_3_ = bf16[128,512]{1,0:T(8,128)(2,1)S(1)} collective-permute-done((bf16[128,512]{1,0:T(8,128)(2,1)S(1)}, bf16[128,512]{1,0:T(8,128)(2,1)S(1)}, u32[]{:S(2)}, u32[]{:S(2)}) %collective-permute-start.11) | collective-permute-done | bytes 131104 | tf_op jit(solution)/shard_map/ppermute | solution.py:387
  28.2 1.1 %outputs.3 = bf16[128,2048]{1,0:T(8,128)(2,1)} custom-call(s32[1]{0:T(128)} %bitcast.which, bf16[128,256]{1,0:T(8,128)(2,1)S(1)} %get-tuple-element.39.c, f32[128,2048]{1,0:T(8,128)S(1)} %get-tuple-element.40.y_part, f32[128,2048]{1,0:T(8,128)S(1)} %get-tuple-element.41.lead, f32[1,2048]{1,0:T(1,128)S(1)} %get-tuple-element.42.gain, ...), custom_call_target="tpu_custom_call", output_to_operand_aliasing={{}: (9, {})} | custom-call | tf_op jit(solution)/shard_map/outputs/pallas_call | solution.py:538
  (23 shorter events, 0.4 us)
Async XLA Ops:
  0.0 1.0 %copy-start = (bf16[128,2048]{1,0:T(8,128)(2,1)S(1)}, bf16[128,2048]{1,0:T(8,128)(2,1)}, u32[]{:S(2)}) copy-start(bf16[128,2048]{1,0:T(8,128)(2,1)} %x.23) | copy-start | bytes 1572868
  0.0 1.1 %copy-start.1 = (bf16[128,2,256]{2,1,0:T(2,128)(2,1)S(1)}, bf16[128,2,256]{2,1,0:T(2,128)(2,1)}, u32[]{:S(2)}) copy-start(bf16[128,2,256]{2,1,0:T(2,128)(2,1)} %bc.23) | copy-start | bytes 393220
  0.0 1.1 %copy-start.2 = (f32[4,2048]{1,0:T(4,128)S(1)}, f32[4,2048]{1,0:T(4,128)}, u32[]{:S(2)}) copy-start(f32[4,2048]{1,0:T(4,128)} %taps_x.21) | copy-start | bytes 98308
  0.0 1.1 %copy-start.3 = (f32[4,2,256]{2,1,0:T(2,128)S(1)}, f32[4,2,256]{2,1,0:T(2,128)}, u32[]{:S(2)}) copy-start(f32[4,2,256]{2,1,0:T(2,128)} %taps_bc.21) | copy-start | bytes 24580
  0.1 4.4 %collective-permute-start.1 = (bf16[144,512]{1,0:T(8,128)(2,1)S(1)}, bf16[144,512]{1,0:T(8,128)(2,1)S(1)}, u32[]{:S(2)}, u32[]{:S(2)}) collective-permute-start(bf16[144,512]{1,0:T(8,128)(2,1)S(1)} %get-tuple-element.26._), channel_id=1, source_target_pairs={{0,4},{1,5},{2,6},{3,7},{16,20},{17,21},{18,22},{19,23}} | collective-permute-start | bytes 442376 | tf_op jit(solution)/shard_map/ppermute | solution.py:387
  1.1 0.7 %copy-start.4 = (f32[128,32]{0,1:T(8,128)S(1)}, f32[128,32]{0,1:T(8,128)}, u32[]{:S(2)}) copy-start(f32[128,32]{0,1:T(8,128)} %param.12) | copy-start | bytes 49156
  1.1 0.7 %copy-start.6 = (f32[2048]{0:T(1024)S(1)}, f32[2048]{0:T(1024)}, u32[]{:S(2)}) copy-start(f32[2048]{0:T(1024)} %param.17) | copy-start | bytes 24580
  1.1 0.7 %copy-start.7 = (f32[32]{0:T(128)S(1)}, f32[32]{0:T(128)}, u32[]{:S(2)}) copy-start(f32[32]{0:T(128)} %param.15) | copy-start | bytes 388
  1.1 4.2 %collective-permute-start.4 = (bf16[128,512]{1,0:T(8,128)(2,1)S(1)}, bf16[128,512]{1,0:T(8,128)(2,1)S(1)}, u32[]{:S(2)}, u32[]{:S(2)}) collective-permute-start(bf16[128,512]{1,0:T(8,128)(2,1)S(1)} %next_states.3._), channel_id=1, source_target_pairs={{0,4},{1,5},{2,6},{3,7},{16,20},{17,21},{18,22},{19,23}} | collective-permute-start | bytes 393224 | tf_op jit(solution)/shard_map/ppermute | solution.py:387
  2.4 5.1 %collective-permute-start = (bf16[8,2560]{1,0:T(8,128)(2,1)S(1)}, bf16[8,2560]{1,0:T(8,128)(2,1)S(1)}, u32[]{:S(2)}, u32[]{:S(2)}) collective-permute-start(bf16[8,2560]{1,0:T(8,128)(2,1)S(1)} %get-tuple-element.38._), channel_id=1, source_target_pairs={{4,8},{5,9},{6,10},{7,11},{20,24},{21,25},{22,26},{23,27}} | collective-permute-start | bytes 122888 | tf_op jit(solution)/shard_map/ppermute | solution.py:387
  3.1 2.9 %collective-permute-start.3 = (bf16[128,512]{1,0:T(8,128)(2,1)S(1)}, bf16[128,512]{1,0:T(8,128)(2,1)S(1)}, u32[]{:S(2)}, u32[]{:S(2)}) collective-permute-start(bf16[128,512]{1,0:T(8,128)(2,1)S(1)} %next_states.4._), channel_id=1, source_target_pairs={{0,4},{1,5},{2,6},{3,7},{16,20},{17,21},{18,22},{19,23}} | collective-permute-start | bytes 393224 | tf_op jit(solution)/shard_map/ppermute | solution.py:387
  3.8 2.9 %collective-permute-start.2 = (bf16[128,512]{1,0:T(8,128)(2,1)S(1)}, bf16[128,512]{1,0:T(8,128)(2,1)S(1)}, u32[]{:S(2)}, u32[]{:S(2)}) collective-permute-start(bf16[128,512]{1,0:T(8,128)(2,1)S(1)} %next_states.5), channel_id=1, source_target_pairs={{0,4},{1,5},{2,6},{3,7},{16,20},{17,21},{18,22},{19,23}} | collective-permute-start | bytes 393224 | tf_op jit(solution)/shard_map/ppermute | solution.py:387
  4.6 4.9 %collective-permute-start.8 = (bf16[128,512]{1,0:T(8,128)(2,1)S(1)}, bf16[128,512]{1,0:T(8,128)(2,1)S(1)}, u32[]{:S(2)}, u32[]{:S(2)}) collective-permute-start(bf16[128,512]{1,0:T(8,128)(2,1)S(1)} %add_convert_fusion.7._), channel_id=1, source_target_pairs={{4,8},{5,9},{6,10},{7,11},{20,24},{21,25},{22,26},{23,27}} | collective-permute-start | bytes 393224 | tf_op jit(solution)/shard_map/ppermute | solution.py:387
  5.3 5.5 %collective-permute-start.7 = (bf16[128,512]{1,0:T(8,128)(2,1)S(1)}, bf16[128,512]{1,0:T(8,128)(2,1)S(1)}, u32[]{:S(2)}, u32[]{:S(2)}) collective-permute-start(bf16[128,512]{1,0:T(8,128)(2,1)S(1)} %add_convert_fusion.6._), channel_id=1, source_target_pairs={{4,8},{5,9},{6,10},{7,11},{20,24},{21,25},{22,26},{23,27}} | collective-permute-start | bytes 393224 | tf_op jit(solution)/shard_map/ppermute | solution.py:387
  6.1 6.1 %collective-permute-start.6 = (bf16[128,512]{1,0:T(8,128)(2,1)S(1)}, bf16[128,512]{1,0:T(8,128)(2,1)S(1)}, u32[]{:S(2)}, u32[]{:S(2)}) collective-permute-start(bf16[128,512]{1,0:T(8,128)(2,1)S(1)} %add_convert_fusion.5._), channel_id=1, source_target_pairs={{4,8},{5,9},{6,10},{7,11},{20,24},{21,25},{22,26},{23,27}} | collective-permute-start | bytes 393224 | tf_op jit(solution)/shard_map/ppermute | solution.py:387
  6.8 7.5 %collective-permute-start.10 = (bf16[128,512]{1,0:T(8,128)(2,1)S(1)}, bf16[128,512]{1,0:T(8,128)(2,1)S(1)}, u32[]{:S(2)}, u32[]{:S(2)}) collective-permute-start(bf16[128,512]{1,0:T(8,128)(2,1)S(1)} %add_convert_fusion.4._), channel_id=1, source_target_pairs={{4,8},{5,9},{6,10},{7,11},{20,24},{21,25},{22,26},{23,27}} | collective-permute-start | bytes 393224 | tf_op jit(solution)/shard_map/ppermute | solution.py:387
  7.5 6.8 %collective-permute-start.5 = (bf16[8,2560]{1,0:T(8,128)(2,1)S(1)}, bf16[8,2560]{1,0:T(8,128)(2,1)S(1)}, u32[]{:S(2)}, u32[]{:S(2)}) collective-permute-start(bf16[8,2560]{1,0:T(8,128)(2,1)S(1)} %get-tuple-element.38._), channel_id=1, source_target_pairs={{8,12},{9,13},{10,14},{11,15},{24,28},{25,29},{26,30},{27,31}} | collective-permute-start | bytes 122888 | tf_op jit(solution)/shard_map/ppermute | solution.py:387
  8.8 0.7 %copy-start.5 = (f32[32]{0:T(128)S(1)}, f32[32]{0:T(128)}, u32[]{:S(2)}) copy-start(f32[32]{0:T(128)} %param.16) | copy-start | bytes 388
  9.5 11.6 %collective-permute-start.12 = (bf16[128,512]{1,0:T(8,128)(2,1)S(1)}, bf16[128,512]{1,0:T(8,128)(2,1)S(1)}, u32[]{:S(2)}, u32[]{:S(2)}) collective-permute-start(bf16[128,512]{1,0:T(8,128)(2,1)S(1)} %add_convert_fusion.3), channel_id=1, source_target_pairs={{8,12},{9,13},{10,14},{11,15},{24,28},{25,29},{26,30},{27,31}} | collective-permute-start | bytes 393224 | tf_op jit(solution)/shard_map/ppermute | solution.py:387
  10.9 13.2 %collective-permute-start.13 = (bf16[128,512]{1,0:T(8,128)(2,1)S(1)}, bf16[128,512]{1,0:T(8,128)(2,1)S(1)}, u32[]{:S(2)}, u32[]{:S(2)}) collective-permute-start(bf16[128,512]{1,0:T(8,128)(2,1)S(1)} %add_convert_fusion.2), channel_id=1, source_target_pairs={{8,12},{9,13},{10,14},{11,15},{24,28},{25,29},{26,30},{27,31}} | collective-permute-start | bytes 393224 | tf_op jit(solution)/shard_map/ppermute | solution.py:387
  12.3 14.6 %collective-permute-start.9 = (bf16[128,512]{1,0:T(8,128)(2,1)S(1)}, bf16[128,512]{1,0:T(8,128)(2,1)S(1)}, u32[]{:S(2)}, u32[]{:S(2)}) collective-permute-start(bf16[128,512]{1,0:T(8,128)(2,1)S(1)} %add_convert_fusion.1), channel_id=1, source_target_pairs={{8,12},{9,13},{10,14},{11,15},{24,28},{25,29},{26,30},{27,31}} | collective-permute-start | bytes 393224 | tf_op jit(solution)/shard_map/ppermute | solution.py:387
  14.4 13.8 %collective-permute-start.11 = (bf16[128,512]{1,0:T(8,128)(2,1)S(1)}, bf16[128,512]{1,0:T(8,128)(2,1)S(1)}, u32[]{:S(2)}, u32[]{:S(2)}) collective-permute-start(bf16[128,512]{1,0:T(8,128)(2,1)S(1)} %add_convert_fusion), channel_id=1, source_target_pairs={{8,12},{9,13},{10,14},{11,15},{24,28},{25,29},{26,30},{27,31}} | collective-permute-start | bytes 393224 | tf_op jit(solution)/shard_map/ppermute | solution.py:387

commit v20 on v18

--- a/solution.py
+++ b/solution.py
@@ -445,15 +445,15 @@
 
     if devices <= CHAIN_MOST:
         first, scale = first_states(*cuts[0])
-        sent = [first, next_states(first, scale, *cuts[1])]
-        last, gain, scale_own, *decays = prepared(sent[-1])
-        token = last
-        for cut in cuts[2:]:
+        last, gain, scale_own, *decays = prepared(first)
+        sent, token = [first], last
+        for cut in cuts[1:]:
             sent.append(next_states(token, scale, *cut))
             token = sent[-1]
         soon = along[1 : max(devices - 2, 1)]
         late = along[max(devices - 2, 1) :]
-        befores = [shifted(last, soon)] if soon else []
+        rows, _ = lax.optimization_barrier((last, sent[1]))
+        befores = [shifted(rows, soon)] if soon else []
         arrived = [[shifted(v, along[:1])] for v in sent]
         befores.append(arrived[0][0])
         rows, token = arrived[0][0], last

time: 29.6 us -> 29.6 us (level)
  no operation moved by 1% of the time
where the time goes in v20:
time: 29.6 us; the launch traced here: 29.3 us
  starting transfers between devices  12.7 us (43%)
  waiting for transfers between devices  9.45 us (32%)
  Pallas kernels  5.41 us (18%)
  local copies, waits for them, and re-layouts  0.95 us (3%)
  between operations  0.41 us (1%)
  other arithmetic  0.31 us (1%)
    ppermute x14, starting transfers between devices, shifted(): return lax.ppermute(value, 'seq', route)  12.7 us
    ppermute x14, waiting for transfers between devices, shifted(): return lax.ppermute(value, 'seq', route)  9.45 us
    pallas_call x1, Pallas kernels, intra(): pl.pallas_call(functools.partial(intra_kernel, len(befores)), out_shape=[...  2.16 us
    pallas_call x2, Pallas kernels, shards(): pl.pallas_call(functools.partial(output_kernel, begin, spans, unready), o...  1.96 us
    unnamed x18, local copies, waits for them, and re-layouts  0.95 us
    pallas_call x1, Pallas kernels, prepared(): pl.pallas_call(functools.partial(prepare_kernel, cuts), out_shape=[jax.Sh...  0.62 us
  transfers between devices with their start and end apart: 14, of which 4 were waited for; matrix products, arithmetic and copies ran while one was open for 1% of the time, Pallas kernels for 15%

profile of v20, /device:TPU:30, one launch (start us, length us, event | category | flops | bytes accessed | tf_op | source)
XLA Modules:
  0.0 29.3 jit_solution(12948587572139465042)
XLA Ops:
  0.0 0.0 copy-start.7
  0.0 0.1 first_states.1
  0.1 0.0 copy-start.8
  0.1 0.8 %collective-permute-start.1 = (bf16[144,512]{1,0:T(8,128)(2,1)S(1)}, bf16[144,512]{1,0:T(8,128)(2,1)S(1)}, u32[]{:S(2)}, u32[]{:S(2)}) collective-permute-start(bf16[144,512]{1,0:T(8,128)(2,1)S(1)} %get-tuple-element.27._), channel_id=1, source_target_pairs={{0,4},{1,5},{2,6},{3,7},{16,20},{17,21},{18,22},{19,23}} | collective-permute-start | bytes 442376 | tf_op jit(solution)/shard_map/ppermute | solution.py:382
  0.9 0.1 copy-done
  1.0 0.0 copy-done.1
  1.1 0.0 copy-done.5
  1.1 0.0 copy-done.7
  1.1 0.0 copy-done.8
  1.1 0.0 copy-start.3
  1.1 0.6 %prepared.1 = (bf16[8,2560]{1,0:T(8,128)(2,1)S(1)}, f32[1,2048]{1,0:T(1,128)S(1)}, f32[128,2048]{1,0:T(8,128)S(1)}, f32[1,512]{1,0:T(1,128)S(1)}, f32[1,512]{1,0...) custom-call(bf16[144,512]{1,0:T(8,128)(2,1)S(1)} %get-tuple-element.27._, bf16[128,2048]{1,0:T(8,128)(2,1)S(1)} %copy-done, ...), custom_call_target="tpu_custom_call" | custom-call | tf_op jit(solution)/shard_map/prepared/pallas_call | solution.py:406
  1.7 0.1 copy-done.2
  1.8 0.7 %collective-permute-start.4 = (bf16[128,512]{1,0:T(8,128)(2,1)S(1)}, bf16[128,512]{1,0:T(8,128)(2,1)S(1)}, u32[]{:S(2)}, u32[]{:S(2)}) collective-permute-start(bf16[128,512]{1,0:T(8,128)(2,1)S(1)} %next_states.3._), channel_id=1, source_target_pairs={{0,4},{1,5},{2,6},{3,7},{16,20},{17,21},{18,22},{19,23}} | collective-permute-start | bytes 393224 | tf_op jit(solution)/shard_map/ppermute | solution.py:382
  2.5 0.7 %collective-permute-start = (bf16[8,2560]{1,0:T(8,128)(2,1)S(1)}, bf16[8,2560]{1,0:T(8,128)(2,1)S(1)}, u32[]{:S(2)}, u32[]{:S(2)}) collective-permute-start(bf16[8,2560]{1,0:T(8,128)(2,1)S(1)} %get-tuple-element.40._), channel_id=1, source_target_pairs={{4,8},{5,9},{6,10},{7,11},{20,24},{21,25},{22,26},{23,27}} | collective-permute-start | bytes 122888 | tf_op jit(solution)/shard_map/ppermute | solution.py:382
  3.2 0.7 %collective-permute-start.3 = (bf16[128,512]{1,0:T(8,128)(2,1)S(1)}, bf16[128,512]{1,0:T(8,128)(2,1)S(1)}, u32[]{:S(2)}, u32[]{:S(2)}) collective-permute-start(bf16[128,512]{1,0:T(8,128)(2,1)S(1)} %next_states.4._), channel_id=1, source_target_pairs={{0,4},{1,5},{2,6},{3,7},{16,20},{17,21},{18,22},{19,23}} | collective-permute-start | bytes 393224 | tf_op jit(solution)/shard_map/ppermute | solution.py:382
  3.9 0.7 %collective-permute-start.2 = (bf16[128,512]{1,0:T(8,128)(2,1)S(1)}, bf16[128,512]{1,0:T(8,128)(2,1)S(1)}, u32[]{:S(2)}, u32[]{:S(2)}) collective-permute-start(bf16[128,512]{1,0:T(8,128)(2,1)S(1)} %next_states.5), channel_id=1, source_target_pairs={{0,4},{1,5},{2,6},{3,7},{16,20},{17,21},{18,22},{19,23}} | collective-permute-start | bytes 393224 | tf_op jit(solution)/shard_map/ppermute | solution.py:382
  4.6 0.0 collective-permute-done.1.rows.refs_1_.refs_0_
  4.6 0.7 %collective-permute-start.8 = (bf16[128,512]{1,0:T(8,128)(2,1)S(1)}, bf16[128,512]{1,0:T(8,128)(2,1)S(1)}, u32[]{:S(2)}, u32[]{:S(2)}) collective-permute-start(bf16[128,512]{1,0:T(8,128)(2,1)S(1)} %add_convert_fusion.7._), channel_id=1, source_target_pairs={{4,8},{5,9},{6,10},{7,11},{20,24},{21,25},{22,26},{23,27}} | collective-permute-start | bytes 393224 | tf_op jit(solution)/shard_map/ppermute | solution.py:382
  5.3 0.0 collective-permute-done.4.refs_0_
  5.4 0.7 %collective-permute-start.7 = (bf16[128,512]{1,0:T(8,128)(2,1)S(1)}, bf16[128,512]{1,0:T(8,128)(2,1)S(1)}, u32[]{:S(2)}, u32[]{:S(2)}) collective-permute-start(bf16[128,512]{1,0:T(8,128)(2,1)S(1)} %add_convert_fusion.6._), channel_id=1, source_target_pairs={{4,8},{5,9},{6,10},{7,11},{20,24},{21,25},{22,26},{23,27}} | collective-permute-start | bytes 393224 | tf_op jit(solution)/shard_map/ppermute | solution.py:382
  6.1 0.0 collective-permute-done.3.refs_0_
  6.2 0.7 %collective-permute-start.6 = (bf16[128,512]{1,0:T(8,128)(2,1)S(1)}, bf16[128,512]{1,0:T(8,128)(2,1)S(1)}, u32[]{:S(2)}, u32[]{:S(2)}) collective-permute-start(bf16[128,512]{1,0:T(8,128)(2,1)S(1)} %add_convert_fusion.5._), channel_id=1, source_target_pairs={{4,8},{5,9},{6,10},{7,11},{20,24},{21,25},{22,26},{23,27}} | collective-permute-start | bytes 393224 | tf_op jit(solution)/shard_map/ppermute | solution.py:382
  6.8 0.0 collective-permute-done.2.refs_1_
  6.9 0.7 %collective-permute-start.10 = (bf16[128,512]{1,0:T(8,128)(2,1)S(1)}, bf16[128,512]{1,0:T(8,128)(2,1)S(1)}, u32[]{:S(2)}, u32[]{:S(2)}) collective-permute-start(bf16[128,512]{1,0:T(8,128)(2,1)S(1)} %add_convert_fusion.4._), channel_id=1, source_target_pairs={{4,8},{5,9},{6,10},{7,11},{20,24},{21,25},{22,26},{23,27}} | collective-permute-start | bytes 393224 | tf_op jit(solution)/shard_map/ppermute | solution.py:382
  7.6 0.0 collective-permute-done.refs_0_.rows
  7.6 1.3 %collective-permute-start.5 = (bf16[8,2560]{1,0:T(8,128)(2,1)S(1)}, bf16[8,2560]{1,0:T(8,128)(2,1)S(1)}, u32[]{:S(2)}, u32[]{:S(2)}) collective-permute-start(bf16[8,2560]{1,0:T(8,128)(2,1)S(1)} %get-tuple-element.40._), channel_id=1, source_target_pairs={{8,12},{9,13},{10,14},{11,15},{24,28},{25,29},{26,30},{27,31}} | collective-permute-start | bytes 122888 | tf_op jit(solution)/shard_map/ppermute | solution.py:382
  8.9 0.0 copy-start.6
  8.9 0.6 %copy-done.6 = f32[32]{0:T(128)S(1)} copy-done((f32[32]{0:T(128)S(1)}, f32[32]{0:T(128)}, u32[]{:S(2)}) %copy-start.6) | copy-done | bytes 152
  9.6 0.0 collective-permute-done.8.refs_1_
  9.6 1.3 %collective-permute-start.11 = (bf16[128,512]{1,0:T(8,128)(2,1)S(1)}, bf16[128,512]{1,0:T(8,128)(2,1)S(1)}, u32[]{:S(2)}, u32[]{:S(2)}) collective-permute-start(bf16[128,512]{1,0:T(8,128)(2,1)S(1)} %add_convert_fusion.3), channel_id=1, source_target_pairs={{8,12},{9,13},{10,14},{11,15},{24,28},{25,29},{26,30},{27,31}} | collective-permute-start | bytes 393224 | tf_op jit(solution)/shard_map/ppermute | solution.py:382
  10.9 0.0 collective-permute-done.7.refs_1_
  11.0 0.0 copy-start.4
  11.0 1.4 %collective-permute-start.13 = (bf16[128,512]{1,0:T(8,128)(2,1)S(1)}, bf16[128,512]{1,0:T(8,128)(2,1)S(1)}, u32[]{:S(2)}, u32[]{:S(2)}) collective-permute-start(bf16[128,512]{1,0:T(8,128)(2,1)S(1)} %add_convert_fusion.2), channel_id=1, source_target_pairs={{8,12},{9,13},{10,14},{11,15},{24,28},{25,29},{26,30},{27,31}} | collective-permute-start | bytes 393224 | tf_op jit(solution)/shard_map/ppermute | solution.py:382
  12.4 0.0 collective-permute-done.6.refs_1_
  12.5 1.3 %collective-permute-start.9 = (bf16[128,512]{1,0:T(8,128)(2,1)S(1)}, bf16[128,512]{1,0:T(8,128)(2,1)S(1)}, u32[]{:S(2)}, u32[]{:S(2)}) collective-permute-start(bf16[128,512]{1,0:T(8,128)(2,1)S(1)} %add_convert_fusion.1), channel_id=1, source_target_pairs={{8,12},{9,13},{10,14},{11,15},{24,28},{25,29},{26,30},{27,31}} | collective-permute-start | bytes 393224 | tf_op jit(solution)/shard_map/ppermute | solution.py:382
  13.8 0.7 %collective-permute-done.5.refs_2_ = bf16[8,2560]{1,0:T(8,128)(2,1)S(1)} collective-permute-done((bf16[8,2560]{1,0:T(8,128)(2,1)S(1)}, bf16[8,2560]{1,0:T(8,128)(2,1)S(1)}, u32[]{:S(2)}, u32[]{:S(2)}) %collective-permute-start.5) | collective-permute-done | bytes 40992 | tf_op jit(solution)/shard_map/ppermute | solution.py:382
  14.4 0.0 collective-permute-done.10.refs_2_
  14.4 6.4 %collective-permute-done.11.refs_2_ = bf16[128,512]{1,0:T(8,128)(2,1)S(1)} collective-permute-done((bf16[128,512]{1,0:T(8,128)(2,1)S(1)}, bf16[128,512]{1,0:T(8,128)(2,1)S(1)}, u32[]{:S(2)}, u32[]{:S(2)}) %collective-permute-start.11) | collective-permute-done | bytes 131104 | tf_op jit(solution)/shard_map/ppermute | solution.py:382
  20.9 1.3 %collective-permute-start.12 = (bf16[128,512]{1,0:T(8,128)(2,1)S(1)}, bf16[128,512]{1,0:T(8,128)(2,1)S(1)}, u32[]{:S(2)}, u32[]{:S(2)}) collective-permute-start(bf16[128,512]{1,0:T(8,128)(2,1)S(1)} %add_convert_fusion), channel_id=1, source_target_pairs={{8,12},{9,13},{10,14},{11,15},{24,28},{25,29},{26,30},{27,31}} | collective-permute-start | bytes 393224 | tf_op jit(solution)/shard_map/ppermute | solution.py:382
  22.2 2.2 %intra.1 = (f32[128,2048]{1,0:T(8,128)S(1)}, f32[128,2048]{1,0:T(8,128)S(1)}, bf16[128,256]{1,0:T(8,128)(2,1)S(1)}) custom-call(f32[1,32]{1,0:T(1,128)S(1)} %bitcast.31, bf16[8,2560]{1,0:T(8,128)(2,1)S(1)} %collective-permute-done.refs_0_.rows, bf16[144,512]{1,0:T(8,128)(2,1)S(1)} %collective-permute-done.1.rows.refs_1_.refs_0_, ...), custom_call_target="tpu_custom_call" | custom-call | flops 134217728 | bytes 3145728 | tf_op jit(solution)/shard_map/intra/pallas_call | solution.py:430
  24.3 0.2 gated.4.refs_0_
  24.5 0.0 collective-permute-done.13.refs_2_
  24.5 0.2 gated.5.refs_1_
  24.7 0.9 %outputs.2.refs_4_ = bf16[128,2048]{1,0:T(8,128)(2,1)} custom-call(s32[1]{0:T(128)} %bitcast.which, bf16[128,256]{1,0:T(8,128)(2,1)S(1)} %get-tuple-element.41.c, f32[128,2048]{1,0:T(8,128)S(1)} %get-tuple-element.42.y_part, f32[128,2048]{1,0:T(8,128)S(1)} %get-tuple-element.43.lead, f32[1,2048]{1,0:T(1,128)S(1)} %get-tuple-element.44.gain, ...), custom_call_target="tpu_custom_call" | custom-call | tf_op jit(solution)/shard_map/outputs/pallas_call | solution.py:526
  25.7 1.1 %collective-permute-done.9.refs_2_ = bf16[128,512]{1,0:T(8,128)(2,1)S(1)} collective-permute-done((bf16[128,512]{1,0:T(8,128)(2,1)S(1)}, bf16[128,512]{1,0:T(8,128)(2,1)S(1)}, u32[]{:S(2)}, u32[]{:S(2)}) %collective-permute-start.9) | collective-permute-done | bytes 131104 | tf_op jit(solution)/shard_map/ppermute | solution.py:382
  26.8 0.2 gated.3.refs_0_
  27.0 1.2 %collective-permute-done.12.refs_3_ = bf16[128,512]{1,0:T(8,128)(2,1)S(1)} collective-permute-done((bf16[128,512]{1,0:T(8,128)(2,1)S(1)}, bf16[128,512]{1,0:T(8,128)(2,1)S(1)}, u32[]{:S(2)}, u32[]{:S(2)}) %collective-permute-start.12) | collective-permute-done | bytes 131104 | tf_op jit(solution)/shard_map/ppermute | solution.py:382
  28.2 1.0 %outputs.3 = bf16[128,2048]{1,0:T(8,128)(2,1)} custom-call(s32[1]{0:T(128)} %bitcast.which, bf16[128,256]{1,0:T(8,128)(2,1)S(1)} %get-tuple-element.41.c, f32[128,2048]{1,0:T(8,128)S(1)} %get-tuple-element.42.y_part, f32[128,2048]{1,0:T(8,128)S(1)} %get-tuple-element.43.lead, f32[1,2048]{1,0:T(1,128)S(1)} %get-tuple-element.44.gain, ...), custom_call_target="tpu_custom_call", output_to_operand_aliasing={{}: (9, {})} | custom-call | tf_op jit(solution)/shard_map/outputs/pallas_call | solution.py:526
  (25 shorter events, 0.4 us)
Async XLA Ops:
  0.0 1.0 %copy-start = (bf16[128,2048]{1,0:T(8,128)(2,1)S(1)}, bf16[128,2048]{1,0:T(8,128)(2,1)}, u32[]{:S(2)}) copy-start(bf16[128,2048]{1,0:T(8,128)(2,1)} %x.23) | copy-start | bytes 1572868
  0.0 1.1 %copy-start.1 = (bf16[128,2,256]{2,1,0:T(2,128)(2,1)S(1)}, bf16[128,2,256]{2,1,0:T(2,128)(2,1)}, u32[]{:S(2)}) copy-start(bf16[128,2,256]{2,1,0:T(2,128)(2,1)} %bc.23) | copy-start | bytes 393220
  0.0 1.1 %copy-start.5 = (f32[128,32]{0,1:T(8,128)S(1)}, f32[128,32]{0,1:T(8,128)}, u32[]{:S(2)}) copy-start(f32[128,32]{0,1:T(8,128)} %param.12) | copy-start | bytes 49156
  0.0 1.1 %copy-start.7 = (f32[2048]{0:T(1024)S(1)}, f32[2048]{0:T(1024)}, u32[]{:S(2)}) copy-start(f32[2048]{0:T(1024)} %param.17) | copy-start | bytes 24580
  0.1 1.0 %copy-start.8 = (f32[32]{0:T(128)S(1)}, f32[32]{0:T(128)}, u32[]{:S(2)}) copy-start(f32[32]{0:T(128)} %param.15) | copy-start | bytes 388
  0.1 4.5 %collective-permute-start.1 = (bf16[144,512]{1,0:T(8,128)(2,1)S(1)}, bf16[144,512]{1,0:T(8,128)(2,1)S(1)}, u32[]{:S(2)}, u32[]{:S(2)}) collective-permute-start(bf16[144,512]{1,0:T(8,128)(2,1)S(1)} %get-tuple-element.27._), channel_id=1, source_target_pairs={{0,4},{1,5},{2,6},{3,7},{16,20},{17,21},{18,22},{19,23}} | collective-permute-start | bytes 442376 | tf_op jit(solution)/shard_map/ppermute | solution.py:382
  1.1 0.8 %copy-start.2 = (f32[4,2048]{1,0:T(4,128)S(1)}, f32[4,2048]{1,0:T(4,128)}, u32[]{:S(2)}) copy-start(f32[4,2048]{1,0:T(4,128)} %taps_x.21) | copy-start | bytes 98308
  1.1 0.8 %copy-start.3 = (f32[4,2,256]{2,1,0:T(2,128)S(1)}, f32[4,2,256]{2,1,0:T(2,128)}, u32[]{:S(2)}) copy-start(f32[4,2,256]{2,1,0:T(2,128)} %taps_bc.21) | copy-start | bytes 24580
  1.8 3.5 %collective-permute-start.4 = (bf16[128,512]{1,0:T(8,128)(2,1)S(1)}, bf16[128,512]{1,0:T(8,128)(2,1)S(1)}, u32[]{:S(2)}, u32[]{:S(2)}) collective-permute-start(bf16[128,512]{1,0:T(8,128)(2,1)S(1)} %next_states.3._), channel_id=1, source_target_pairs={{0,4},{1,5},{2,6},{3,7},{16,20},{17,21},{18,22},{19,23}} | collective-permute-start | bytes 393224 | tf_op jit(solution)/shard_map/ppermute | solution.py:382
  2.5 5.1 %collective-permute-start = (bf16[8,2560]{1,0:T(8,128)(2,1)S(1)}, bf16[8,2560]{1,0:T(8,128)(2,1)S(1)}, u32[]{:S(2)}, u32[]{:S(2)}) collective-permute-start(bf16[8,2560]{1,0:T(8,128)(2,1)S(1)} %get-tuple-element.40._), channel_id=1, source_target_pairs={{4,8},{5,9},{6,10},{7,11},{20,24},{21,25},{22,26},{23,27}} | collective-permute-start | bytes 122888 | tf_op jit(solution)/shard_map/ppermute | solution.py:382
  3.2 2.9 %collective-permute-start.3 = (bf16[128,512]{1,0:T(8,128)(2,1)S(1)}, bf16[128,512]{1,0:T(8,128)(2,1)S(1)}, u32[]{:S(2)}, u32[]{:S(2)}) collective-permute-start(bf16[128,512]{1,0:T(8,128)(2,1)S(1)} %next_states.4._), channel_id=1, source_target_pairs={{0,4},{1,5},{2,6},{3,7},{16,20},{17,21},{18,22},{19,23}} | collective-permute-start | bytes 393224 | tf_op jit(solution)/shard_map/ppermute | solution.py:382
  3.9 2.9 %collective-permute-start.2 = (bf16[128,512]{1,0:T(8,128)(2,1)S(1)}, bf16[128,512]{1,0:T(8,128)(2,1)S(1)}, u32[]{:S(2)}, u32[]{:S(2)}) collective-permute-start(bf16[128,512]{1,0:T(8,128)(2,1)S(1)} %next_states.5), channel_id=1, source_target_pairs={{0,4},{1,5},{2,6},{3,7},{16,20},{17,21},{18,22},{19,23}} | collective-permute-start | bytes 393224 | tf_op jit(solution)/shard_map/ppermute | solution.py:382
  4.6 4.9 %collective-permute-start.8 = (bf16[128,512]{1,0:T(8,128)(2,1)S(1)}, bf16[128,512]{1,0:T(8,128)(2,1)S(1)}, u32[]{:S(2)}, u32[]{:S(2)}) collective-permute-start(bf16[128,512]{1,0:T(8,128)(2,1)S(1)} %add_convert_fusion.7._), channel_id=1, source_target_pairs={{4,8},{5,9},{6,10},{7,11},{20,24},{21,25},{22,26},{23,27}} | collective-permute-start | bytes 393224 | tf_op jit(solution)/shard_map/ppermute | solution.py:382
  5.4 5.5 %collective-permute-start.7 = (bf16[128,512]{1,0:T(8,128)(2,1)S(1)}, bf16[128,512]{1,0:T(8,128)(2,1)S(1)}, u32[]{:S(2)}, u32[]{:S(2)}) collective-permute-start(bf16[128,512]{1,0:T(8,128)(2,1)S(1)} %add_convert_fusion.6._), channel_id=1, source_target_pairs={{4,8},{5,9},{6,10},{7,11},{20,24},{21,25},{22,26},{23,27}} | collective-permute-start | bytes 393224 | tf_op jit(solution)/shard_map/ppermute | solution.py:382
  6.2 6.3 %collective-permute-start.6 = (bf16[128,512]{1,0:T(8,128)(2,1)S(1)}, bf16[128,512]{1,0:T(8,128)(2,1)S(1)}, u32[]{:S(2)}, u32[]{:S(2)}) collective-permute-start(bf16[128,512]{1,0:T(8,128)(2,1)S(1)} %add_convert_fusion.5._), channel_id=1, source_target_pairs={{4,8},{5,9},{6,10},{7,11},{20,24},{21,25},{22,26},{23,27}} | collective-permute-start | bytes 393224 | tf_op jit(solution)/shard_map/ppermute | solution.py:382
  6.9 7.5 %collective-permute-start.10 = (bf16[128,512]{1,0:T(8,128)(2,1)S(1)}, bf16[128,512]{1,0:T(8,128)(2,1)S(1)}, u32[]{:S(2)}, u32[]{:S(2)}) collective-permute-start(bf16[128,512]{1,0:T(8,128)(2,1)S(1)} %add_convert_fusion.4._), channel_id=1, source_target_pairs={{4,8},{5,9},{6,10},{7,11},{20,24},{21,25},{22,26},{23,27}} | collective-permute-start | bytes 393224 | tf_op jit(solution)/shard_map/ppermute | solution.py:382
  7.6 6.8 %collective-permute-start.5 = (bf16[8,2560]{1,0:T(8,128)(2,1)S(1)}, bf16[8,2560]{1,0:T(8,128)(2,1)S(1)}, u32[]{:S(2)}, u32[]{:S(2)}) collective-permute-start(bf16[8,2560]{1,0:T(8,128)(2,1)S(1)} %get-tuple-element.40._), channel_id=1, source_target_pairs={{8,12},{9,13},{10,14},{11,15},{24,28},{25,29},{26,30},{27,31}} | collective-permute-start | bytes 122888 | tf_op jit(solution)/shard_map/ppermute | solution.py:382
  8.9 0.7 %copy-start.6 = (f32[32]{0:T(128)S(1)}, f32[32]{0:T(128)}, u32[]{:S(2)}) copy-start(f32[32]{0:T(128)} %param.16) | copy-start | bytes 388
  9.6 11.2 %collective-permute-start.11 = (bf16[128,512]{1,0:T(8,128)(2,1)S(1)}, bf16[128,512]{1,0:T(8,128)(2,1)S(1)}, u32[]{:S(2)}, u32[]{:S(2)}) collective-permute-start(bf16[128,512]{1,0:T(8,128)(2,1)S(1)} %add_convert_fusion.3), channel_id=1, source_target_pairs={{8,12},{9,13},{10,14},{11,15},{24,28},{25,29},{26,30},{27,31}} | collective-permute-start | bytes 393224 | tf_op jit(solution)/shard_map/ppermute | solution.py:382
  11.0 11.2 %copy-start.4 = (bf16[128,2048]{1,0:T(8,128)(2,1)S(1)}, bf16[128,2048]{1,0:T(8,128)(2,1)}, u32[]{:S(2)}) copy-start(bf16[128,2048]{1,0:T(8,128)(2,1)} %refs_5_.1) | copy-start | bytes 1572868
  11.0 13.6 %collective-permute-start.13 = (bf16[128,512]{1,0:T(8,128)(2,1)S(1)}, bf16[128,512]{1,0:T(8,128)(2,1)S(1)}, u32[]{:S(2)}, u32[]{:S(2)}) collective-permute-start(bf16[128,512]{1,0:T(8,128)(2,1)S(1)} %add_convert_fusion.2), channel_id=1, source_target_pairs={{8,12},{9,13},{10,14},{11,15},{24,28},{25,29},{26,30},{27,31}} | collective-permute-start | bytes 393224 | tf_op jit(solution)/shard_map/ppermute | solution.py:382
  12.5 14.3 %collective-permute-start.9 = (bf16[128,512]{1,0:T(8,128)(2,1)S(1)}, bf16[128,512]{1,0:T(8,128)(2,1)S(1)}, u32[]{:S(2)}, u32[]{:S(2)}) collective-permute-start(bf16[128,512]{1,0:T(8,128)(2,1)S(1)} %add_convert_fusion.1), channel_id=1, source_target_pairs={{8,12},{9,13},{10,14},{11,15},{24,28},{25,29},{26,30},{27,31}} | collective-permute-start | bytes 393224 | tf_op jit(solution)/shard_map/ppermute | solution.py:382
  20.9 7.3 %collective-permute-start.12 = (bf16[128,512]{1,0:T(8,128)(2,1)S(1)}, bf16[128,512]{1,0:T(8,128)(2,1)S(1)}, u32[]{:S(2)}, u32[]{:S(2)}) collective-permute-start(bf16[128,512]{1,0:T(8,128)(2,1)S(1)} %add_convert_fusion), channel_id=1, source_target_pairs={{8,12},{9,13},{10,14},{11,15},{24,28},{25,29},{26,30},{27,31}} | collective-permute-start | bytes 393224 | tf_op jit(solution)/shard_map/ppermute | solution.py:382

commit v21 on v19

--- a/solution.py
+++ b/solution.py
@@ -225,7 +225,7 @@
 
 def intra_kernel(count, _, *refs):
     sources, refs = refs[:count], refs[count:]
-    x, bc, z_hbm, taps_x, taps_bc, dt_raw, a_log, d_skip, y_part, lead, c_act, wide, z, sem = refs
+    x, bc, z_hbm, taps_x, taps_bc, dt_raw, a_log, d_skip, y_part, lead, c_act, z, sem = refs
     z_copy = pltpu.make_async_copy(z_hbm, z, sem.at[0])
     z_copy.start()
     tokens, width = x.shape
@@ -257,9 +257,9 @@
         c_act[:, g * state_dim : (g + 1) * state_dim] = c
         inner = lax.dot_general(c, b, (((1,), (1,)), ((), ())), preferred_element_type=F32)
         inner = jnp.where(t_at >= s_at, inner, 0.0)
-        wide[...] = spread(leading[g * heads : (g + 1) * heads], head_dim, 2)
-        if g == 0:
-            z_copy.wait()
+        lead[:, g * cols : (g + 1) * cols] = spread(
+            leading[g * heads : (g + 1) * heads], head_dim, 2
+        )
         for first in range(0, heads, 2):
             here = slice(first * head_dim, first * head_dim + pair)
             cut = slice(g * cols + here.start, g * cols + here.stop)
@@ -275,9 +275,13 @@
                 gap = jnp.minimum(cum_t[:, h : h + 1] - cum[h : h + 1, :], 0.0)
                 weights.append((jnp.exp(gap) * dt[h : h + 1, :] * inner).astype(BF16))
             y = jnp.dot(jnp.concatenate(weights, axis=1), blocks, preferred_element_type=F32)
-            gate = silu(z[:, cut].astype(F32))
-            y_part[:, cut] = (y + skip[:, cut] * full) * gate
-            lead[:, cut] = wide[:, here] * gate
+            y_part[:, cut] = y + skip[:, cut] * full
+    z_copy.wait()
+    for at in range(0, width, CHUNK):
+        cut = slice(at, at + CHUNK)
+        gate = silu(z[:, cut].astype(F32))
+        y_part[:, cut] = y_part[:, cut] * gate
+        lead[:, cut] = lead[:, cut] * gate
 
 
 def gated_slice(low, which, c, y_part, lead, arrived):
@@ -442,7 +446,6 @@
             + [pl.BlockSpec(memory_space=pltpu.HBM)]
             + [in_vmem] * 5,
             scratch_shapes=[
-                pltpu.VMEM((tokens, cols), F32),
                 pltpu.VMEM(z_in.shape, z_in.dtype),
                 pltpu.SemaphoreType.DMA((1,)),
             ],
@@ -457,15 +460,15 @@
 
     if devices <= CHAIN_MOST:
         first, scale = first_states(*cuts[0])
-        sent = [first, next_states(first, scale, *cuts[1])]
-        last, gain, scale_own, *decays = prepared(sent[-1])
-        token = last
-        for cut in cuts[2:]:
+        last, gain, scale_own, *decays = prepared(first)
+        sent, token = [first], last
+        for cut in cuts[1:]:
             sent.append(next_states(token, scale, *cut))
             token = sent[-1]
         soon = along[1 : max(devices - 2, 1)]
         late = along[max(devices - 2, 1) :]
-        befores = [shifted(last, soon)] if soon else []
+        rows, _ = lax.optimization_barrier((last, sent[1]))
+        befores = [shifted(rows, soon)] if soon else []
         arrived = [[shifted(v, along[:1])] for v in sent]
         befores.append(arrived[0][0])
         rows, token = arrived[0][0], last

time: 29.8 us -> 29.7 us (level)
  Pallas kernels: 6.25 us -> 5.79 us
  waiting for transfers between devices: 8.87 us -> 9.23 us
    pallas_call x1, Pallas kernels: 3 us -> 2.55 us  [intra(): pl.pallas_call(functools.partial(intra_kernel, len(befores)), out_shape=[...]
    ppermute x14, waiting for transfers between devices: 8.87 us -> 9.23 us  [shifted(): return lax.ppermute(value, 'seq', route)]
  transfers between devices with their start and end apart: 14 -> 14, of which waited for: 5 -> 5; matrix products, arithmetic and copies ran while one was open for 1% -> 1% of each run, Pallas kernels for 18% -> 16%
where the time goes in v21:
time: 29.7 us; the launch traced here: 29.3 us
  starting transfers between devices  12.6 us (42%)
  waiting for transfers between devices  9.23 us (31%)
  Pallas kernels  5.79 us (19%)
  local copies, waits for them, and re-layouts  0.94 us (3%)
  between operations  0.39 us (1%)
  other arithmetic  0.31 us (1%)
    ppermute x14, starting transfers between devices, shifted(): return lax.ppermute(value, 'seq', route)  12.6 us
    ppermute x14, waiting for transfers between devices, shifted(): return lax.ppermute(value, 'seq', route)  9.23 us
    pallas_call x1, Pallas kernels, intra(): pl.pallas_call(functools.partial(intra_kernel, len(befores)), out_shape=[...  2.55 us
    pallas_call x2, Pallas kernels, shards(): pl.pallas_call(functools.partial(output_kernel, begin, spans, unready), o...  1.96 us
    unnamed x16, local copies, waits for them, and re-layouts  0.94 us
    pallas_call x1, Pallas kernels, prepared(): pl.pallas_call(functools.partial(prepare_kernel, cuts), out_shape=[jax.Sh...  0.62 us
  transfers between devices with their start and end apart: 14, of which 5 were waited for; matrix products, arithmetic and copies ran while one was open for 1% of the time, Pallas kernels for 16%

profile of v21, /device:TPU:30, one launch (start us, length us, event | category | flops | bytes accessed | tf_op | source)
XLA Modules:
  0.0 29.3 jit_solution(784172821221453357)
XLA Ops:
  0.0 0.0 copy-start.6
  0.0 0.1 first_states.1
  0.1 0.0 copy-start.7
  0.1 0.8 %collective-permute-start.1 = (bf16[144,512]{1,0:T(8,128)(2,1)S(1)}, bf16[144,512]{1,0:T(8,128)(2,1)S(1)}, u32[]{:S(2)}, u32[]{:S(2)}) collective-permute-start(bf16[144,512]{1,0:T(8,128)(2,1)S(1)} %get-tuple-element.27._), channel_id=1, source_target_pairs={{0,4},{1,5},{2,6},{3,7},{16,20},{17,21},{18,22},{19,23}} | collective-permute-start | bytes 442376 | tf_op jit(solution)/shard_map/ppermute | solution.py:391
  0.9 0.1 copy-done
  1.0 0.0 copy-done.1
  1.1 0.0 copy-done.4
  1.1 0.0 copy-done.6
  1.1 0.0 copy-done.7
  1.1 0.0 copy-start.3
  1.1 0.6 %prepared.1 = (bf16[8,2560]{1,0:T(8,128)(2,1)S(1)}, f32[1,2048]{1,0:T(1,128)S(1)}, f32[128,2048]{1,0:T(8,128)S(1)}, f32[1,512]{1,0:T(1,128)S(1)}, f32[1,512]{1,0...) custom-call(bf16[144,512]{1,0:T(8,128)(2,1)S(1)} %get-tuple-element.27._, bf16[128,2048]{1,0:T(8,128)(2,1)S(1)} %copy-done, ...), custom_call_target="tpu_custom_call" | custom-call | tf_op jit(solution)/shard_map/prepared/pallas_call | solution.py:415
  1.7 0.1 copy-done.2
  1.8 0.0 copy-done.3
  1.8 0.7 %collective-permute-start.4 = (bf16[128,512]{1,0:T(8,128)(2,1)S(1)}, bf16[128,512]{1,0:T(8,128)(2,1)S(1)}, u32[]{:S(2)}, u32[]{:S(2)}) collective-permute-start(bf16[128,512]{1,0:T(8,128)(2,1)S(1)} %next_states.3._), channel_id=1, source_target_pairs={{0,4},{1,5},{2,6},{3,7},{16,20},{17,21},{18,22},{19,23}} | collective-permute-start | bytes 393224 | tf_op jit(solution)/shard_map/ppermute | solution.py:391
  2.5 0.7 %collective-permute-start = (bf16[8,2560]{1,0:T(8,128)(2,1)S(1)}, bf16[8,2560]{1,0:T(8,128)(2,1)S(1)}, u32[]{:S(2)}, u32[]{:S(2)}) collective-permute-start(bf16[8,2560]{1,0:T(8,128)(2,1)S(1)} %get-tuple-element.40._), channel_id=1, source_target_pairs={{4,8},{5,9},{6,10},{7,11},{20,24},{21,25},{22,26},{23,27}} | collective-permute-start | bytes 122888 | tf_op jit(solution)/shard_map/ppermute | solution.py:391
  3.2 0.7 %collective-permute-start.3 = (bf16[128,512]{1,0:T(8,128)(2,1)S(1)}, bf16[128,512]{1,0:T(8,128)(2,1)S(1)}, u32[]{:S(2)}, u32[]{:S(2)}) collective-permute-start(bf16[128,512]{1,0:T(8,128)(2,1)S(1)} %next_states.4._), channel_id=1, source_target_pairs={{0,4},{1,5},{2,6},{3,7},{16,20},{17,21},{18,22},{19,23}} | collective-permute-start | bytes 393224 | tf_op jit(solution)/shard_map/ppermute | solution.py:391
  3.9 0.7 %collective-permute-start.2 = (bf16[128,512]{1,0:T(8,128)(2,1)S(1)}, bf16[128,512]{1,0:T(8,128)(2,1)S(1)}, u32[]{:S(2)}, u32[]{:S(2)}) collective-permute-start(bf16[128,512]{1,0:T(8,128)(2,1)S(1)} %next_states.5), channel_id=1, source_target_pairs={{0,4},{1,5},{2,6},{3,7},{16,20},{17,21},{18,22},{19,23}} | collective-permute-start | bytes 393224 | tf_op jit(solution)/shard_map/ppermute | solution.py:391
  4.6 0.0 collective-permute-done.1.rows.refs_1_.refs_0_
  4.6 0.7 %collective-permute-start.8 = (bf16[128,512]{1,0:T(8,128)(2,1)S(1)}, bf16[128,512]{1,0:T(8,128)(2,1)S(1)}, u32[]{:S(2)}, u32[]{:S(2)}) collective-permute-start(bf16[128,512]{1,0:T(8,128)(2,1)S(1)} %add_convert_fusion.7._), channel_id=1, source_target_pairs={{4,8},{5,9},{6,10},{7,11},{20,24},{21,25},{22,26},{23,27}} | collective-permute-start | bytes 393224 | tf_op jit(solution)/shard_map/ppermute | solution.py:391
  5.3 0.0 collective-permute-done.4.refs_0_
  5.4 0.7 %collective-permute-start.7 = (bf16[128,512]{1,0:T(8,128)(2,1)S(1)}, bf16[128,512]{1,0:T(8,128)(2,1)S(1)}, u32[]{:S(2)}, u32[]{:S(2)}) collective-permute-start(bf16[128,512]{1,0:T(8,128)(2,1)S(1)} %add_convert_fusion.6._), channel_id=1, source_target_pairs={{4,8},{5,9},{6,10},{7,11},{20,24},{21,25},{22,26},{23,27}} | collective-permute-start | bytes 393224 | tf_op jit(solution)/shard_map/ppermute | solution.py:391
  6.1 0.0 collective-permute-done.3.refs_0_
  6.2 0.7 %collective-permute-start.6 = (bf16[128,512]{1,0:T(8,128)(2,1)S(1)}, bf16[128,512]{1,0:T(8,128)(2,1)S(1)}, u32[]{:S(2)}, u32[]{:S(2)}) collective-permute-start(bf16[128,512]{1,0:T(8,128)(2,1)S(1)} %add_convert_fusion.5._), channel_id=1, source_target_pairs={{4,8},{5,9},{6,10},{7,11},{20,24},{21,25},{22,26},{23,27}} | collective-permute-start | bytes 393224 | tf_op jit(solution)/shard_map/ppermute | solution.py:391
  6.8 0.0 collective-permute-done.2.refs_1_
  6.9 0.7 %collective-permute-start.10 = (bf16[128,512]{1,0:T(8,128)(2,1)S(1)}, bf16[128,512]{1,0:T(8,128)(2,1)S(1)}, u32[]{:S(2)}, u32[]{:S(2)}) collective-permute-start(bf16[128,512]{1,0:T(8,128)(2,1)S(1)} %add_convert_fusion.4._), channel_id=1, source_target_pairs={{4,8},{5,9},{6,10},{7,11},{20,24},{21,25},{22,26},{23,27}} | collective-permute-start | bytes 393224 | tf_op jit(solution)/shard_map/ppermute | solution.py:391
  7.6 0.0 collective-permute-done.refs_0_.rows
  7.6 1.3 %collective-permute-start.5 = (bf16[8,2560]{1,0:T(8,128)(2,1)S(1)}, bf16[8,2560]{1,0:T(8,128)(2,1)S(1)}, u32[]{:S(2)}, u32[]{:S(2)}) collective-permute-start(bf16[8,2560]{1,0:T(8,128)(2,1)S(1)} %get-tuple-element.40._), channel_id=1, source_target_pairs={{8,12},{9,13},{10,14},{11,15},{24,28},{25,29},{26,30},{27,31}} | collective-permute-start | bytes 122888 | tf_op jit(solution)/shard_map/ppermute | solution.py:391
  8.9 0.0 copy-start.5
  8.9 0.6 %copy-done.5 = f32[32]{0:T(128)S(1)} copy-done((f32[32]{0:T(128)S(1)}, f32[32]{0:T(128)}, u32[]{:S(2)}) %copy-start.5) | copy-done | bytes 152
  9.6 0.0 collective-permute-done.8.refs_1_
  9.6 1.3 %collective-permute-start.12 = (bf16[128,512]{1,0:T(8,128)(2,1)S(1)}, bf16[128,512]{1,0:T(8,128)(2,1)S(1)}, u32[]{:S(2)}, u32[]{:S(2)}) collective-permute-start(bf16[128,512]{1,0:T(8,128)(2,1)S(1)} %add_convert_fusion.3), channel_id=1, source_target_pairs={{8,12},{9,13},{10,14},{11,15},{24,28},{25,29},{26,30},{27,31}} | collective-permute-start | bytes 393224 | tf_op jit(solution)/shard_map/ppermute | solution.py:391
  10.9 0.0 collective-permute-done.7.refs_1_
  11.0 1.3 %collective-permute-start.13 = (bf16[128,512]{1,0:T(8,128)(2,1)S(1)}, bf16[128,512]{1,0:T(8,128)(2,1)S(1)}, u32[]{:S(2)}, u32[]{:S(2)}) collective-permute-start(bf16[128,512]{1,0:T(8,128)(2,1)S(1)} %add_convert_fusion.2), channel_id=1, source_target_pairs={{8,12},{9,13},{10,14},{11,15},{24,28},{25,29},{26,30},{27,31}} | collective-permute-start | bytes 393224 | tf_op jit(solution)/shard_map/ppermute | solution.py:391
  12.3 0.0 collective-permute-done.6.refs_1_
  12.3 1.3 %collective-permute-start.9 = (bf16[128,512]{1,0:T(8,128)(2,1)S(1)}, bf16[128,512]{1,0:T(8,128)(2,1)S(1)}, u32[]{:S(2)}, u32[]{:S(2)}) collective-permute-start(bf16[128,512]{1,0:T(8,128)(2,1)S(1)} %add_convert_fusion.1), channel_id=1, source_target_pairs={{8,12},{9,13},{10,14},{11,15},{24,28},{25,29},{26,30},{27,31}} | collective-permute-start | bytes 393224 | tf_op jit(solution)/shard_map/ppermute | solution.py:391
  13.6 0.8 %collective-permute-done.5.refs_2_ = bf16[8,2560]{1,0:T(8,128)(2,1)S(1)} collective-permute-done((bf16[8,2560]{1,0:T(8,128)(2,1)S(1)}, bf16[8,2560]{1,0:T(8,128)(2,1)S(1)}, u32[]{:S(2)}, u32[]{:S(2)}) %collective-permute-start.5) | collective-permute-done | bytes 40992 | tf_op jit(solution)/shard_map/ppermute | solution.py:391
  14.4 0.0 collective-permute-done.10.refs_2_
  14.5 1.3 %collective-permute-start.11 = (bf16[128,512]{1,0:T(8,128)(2,1)S(1)}, bf16[128,512]{1,0:T(8,128)(2,1)S(1)}, u32[]{:S(2)}, u32[]{:S(2)}) collective-permute-start(bf16[128,512]{1,0:T(8,128)(2,1)S(1)} %add_convert_fusion), channel_id=1, source_target_pairs={{8,12},{9,13},{10,14},{11,15},{24,28},{25,29},{26,30},{27,31}} | collective-permute-start | bytes 393224 | tf_op jit(solution)/shard_map/ppermute | solution.py:391
  15.8 2.5 %intra.1 = (f32[128,2048]{1,0:T(8,128)S(1)}, f32[128,2048]{1,0:T(8,128)S(1)}, bf16[128,256]{1,0:T(8,128)(2,1)S(1)}) custom-call(f32[1,32]{1,0:T(1,128)S(1)} %bitcast.31, bf16[8,2560]{1,0:T(8,128)(2,1)S(1)} %collective-permute-done.refs_0_.rows, bf16[144,512]{1,0:T(8,128)(2,1)S(1)} %collective-permute-done.1.rows.refs_1_.refs_0_, ...), custom_call_target="tpu_custom_call" | custom-call | flops 134217728 | bytes 3145728 | tf_op jit(solution)/shard_map/intra/pallas_call | solution.py:439
  18.3 2.6 %collective-permute-done.12.refs_2_ = bf16[128,512]{1,0:T(8,128)(2,1)S(1)} collective-permute-done((bf16[128,512]{1,0:T(8,128)(2,1)S(1)}, bf16[128,512]{1,0:T(8,128)(2,1)S(1)}, u32[]{:S(2)}, u32[]{:S(2)}) %collective-permute-start.12) | collective-permute-done | bytes 131104 | tf_op jit(solution)/shard_map/ppermute | solution.py:391
  20.9 0.2 gated.4.refs_0_
  21.1 2.9 %collective-permute-done.13.refs_2_ = bf16[128,512]{1,0:T(8,128)(2,1)S(1)} collective-permute-done((bf16[128,512]{1,0:T(8,128)(2,1)S(1)}, bf16[128,512]{1,0:T(8,128)(2,1)S(1)}, u32[]{:S(2)}, u32[]{:S(2)}) %collective-permute-start.13) | collective-permute-done | bytes 131104 | tf_op jit(solution)/shard_map/ppermute | solution.py:391
  24.0 0.2 gated.5.refs_1_
  24.2 0.9 %outputs.2.refs_4_ = bf16[128,2048]{1,0:T(8,128)(2,1)} custom-call(s32[1]{0:T(128)} %bitcast.which, bf16[128,256]{1,0:T(8,128)(2,1)S(1)} %get-tuple-element.41.c, f32[128,2048]{1,0:T(8,128)S(1)} %get-tuple-element.42.y_part, f32[128,2048]{1,0:T(8,128)S(1)} %get-tuple-element.43.lead, f32[1,2048]{1,0:T(1,128)S(1)} %get-tuple-element.44.gain, ...), custom_call_target="tpu_custom_call" | custom-call | tf_op jit(solution)/shard_map/outputs/pallas_call | solution.py:541
  25.1 1.7 %collective-permute-done.9.refs_2_ = bf16[128,512]{1,0:T(8,128)(2,1)S(1)} collective-permute-done((bf16[128,512]{1,0:T(8,128)(2,1)S(1)}, bf16[128,512]{1,0:T(8,128)(2,1)S(1)}, u32[]{:S(2)}, u32[]{:S(2)}) %collective-permute-start.9) | collective-permute-done | bytes 131104 | tf_op jit(solution)/shard_map/ppermute | solution.py:391
  26.8 0.2 gated.3.refs_0_
  27.0 1.2 %collective-permute-done.11.refs_3_ = bf16[128,512]{1,0:T(8,128)(2,1)S(1)} collective-permute-done((bf16[128,512]{1,0:T(8,128)(2,1)S(1)}, bf16[128,512]{1,0:T(8,128)(2,1)S(1)}, u32[]{:S(2)}, u32[]{:S(2)}) %collective-permute-start.11) | collective-permute-done | bytes 131104 | tf_op jit(solution)/shard_map/ppermute | solution.py:391
  28.2 1.1 %outputs.3 = bf16[128,2048]{1,0:T(8,128)(2,1)} custom-call(s32[1]{0:T(128)} %bitcast.which, bf16[128,256]{1,0:T(8,128)(2,1)S(1)} %get-tuple-element.41.c, f32[128,2048]{1,0:T(8,128)S(1)} %get-tuple-element.42.y_part, f32[128,2048]{1,0:T(8,128)S(1)} %get-tuple-element.43.lead, f32[1,2048]{1,0:T(1,128)S(1)} %get-tuple-element.44.gain, ...), custom_call_target="tpu_custom_call", output_to_operand_aliasing={{}: (9, {})} | custom-call | tf_op jit(solution)/shard_map/outputs/pallas_call | solution.py:541
  (23 shorter events, 0.4 us)
Async XLA Ops:
  0.0 1.0 %copy-start = (bf16[128,2048]{1,0:T(8,128)(2,1)S(1)}, bf16[128,2048]{1,0:T(8,128)(2,1)}, u32[]{:S(2)}) copy-start(bf16[128,2048]{1,0:T(8,128)(2,1)} %x.23) | copy-start | bytes 1572868
  0.0 1.1 %copy-start.1 = (bf16[128,2,256]{2,1,0:T(2,128)(2,1)S(1)}, bf16[128,2,256]{2,1,0:T(2,128)(2,1)}, u32[]{:S(2)}) copy-start(bf16[128,2,256]{2,1,0:T(2,128)(2,1)} %bc.23) | copy-start | bytes 393220
  0.0 1.1 %copy-start.4 = (f32[128,32]{0,1:T(8,128)S(1)}, f32[128,32]{0,1:T(8,128)}, u32[]{:S(2)}) copy-start(f32[128,32]{0,1:T(8,128)} %param.12) | copy-start | bytes 49156
  0.0 1.1 %copy-start.6 = (f32[2048]{0:T(1024)S(1)}, f32[2048]{0:T(1024)}, u32[]{:S(2)}) copy-start(f32[2048]{0:T(1024)} %param.17) | copy-start | bytes 24580
  0.1 1.0 %copy-start.7 = (f32[32]{0:T(128)S(1)}, f32[32]{0:T(128)}, u32[]{:S(2)}) copy-start(f32[32]{0:T(128)} %param.15) | copy-start | bytes 388
  0.1 4.5 %collective-permute-start.1 = (bf16[144,512]{1,0:T(8,128)(2,1)S(1)}, bf16[144,512]{1,0:T(8,128)(2,1)S(1)}, u32[]{:S(2)}, u32[]{:S(2)}) collective-permute-start(bf16[144,512]{1,0:T(8,128)(2,1)S(1)} %get-tuple-element.27._), channel_id=1, source_target_pairs={{0,4},{1,5},{2,6},{3,7},{16,20},{17,21},{18,22},{19,23}} | collective-permute-start | bytes 442376 | tf_op jit(solution)/shard_map/ppermute | solution.py:391
  1.1 0.8 %copy-start.2 = (f32[4,2048]{1,0:T(4,128)S(1)}, f32[4,2048]{1,0:T(4,128)}, u32[]{:S(2)}) copy-start(f32[4,2048]{1,0:T(4,128)} %taps_x.21) | copy-start | bytes 98308
  1.1 0.8 %copy-start.3 = (f32[4,2,256]{2,1,0:T(2,128)S(1)}, f32[4,2,256]{2,1,0:T(2,128)}, u32[]{:S(2)}) copy-start(f32[4,2,256]{2,1,0:T(2,128)} %taps_bc.21) | copy-start | bytes 24580
  1.8 3.5 %collective-permute-start.4 = (bf16[128,512]{1,0:T(8,128)(2,1)S(1)}, bf16[128,512]{1,0:T(8,128)(2,1)S(1)}, u32[]{:S(2)}, u32[]{:S(2)}) collective-permute-start(bf16[128,512]{1,0:T(8,128)(2,1)S(1)} %next_states.3._), channel_id=1, source_target_pairs={{0,4},{1,5},{2,6},{3,7},{16,20},{17,21},{18,22},{19,23}} | collective-permute-start | bytes 393224 | tf_op jit(solution)/shard_map/ppermute | solution.py:391
  2.5 5.1 %collective-permute-start = (bf16[8,2560]{1,0:T(8,128)(2,1)S(1)}, bf16[8,2560]{1,0:T(8,128)(2,1)S(1)}, u32[]{:S(2)}, u32[]{:S(2)}) collective-permute-start(bf16[8,2560]{1,0:T(8,128)(2,1)S(1)} %get-tuple-element.40._), channel_id=1, source_target_pairs={{4,8},{5,9},{6,10},{7,11},{20,24},{21,25},{22,26},{23,27}} | collective-permute-start | bytes 122888 | tf_op jit(solution)/shard_map/ppermute | solution.py:391
  3.2 2.9 %collective-permute-start.3 = (bf16[128,512]{1,0:T(8,128)(2,1)S(1)}, bf16[128,512]{1,0:T(8,128)(2,1)S(1)}, u32[]{:S(2)}, u32[]{:S(2)}) collective-permute-start(bf16[128,512]{1,0:T(8,128)(2,1)S(1)} %next_states.4._), channel_id=1, source_target_pairs={{0,4},{1,5},{2,6},{3,7},{16,20},{17,21},{18,22},{19,23}} | collective-permute-start | bytes 393224 | tf_op jit(solution)/shard_map/ppermute | solution.py:391
  3.9 2.9 %collective-permute-start.2 = (bf16[128,512]{1,0:T(8,128)(2,1)S(1)}, bf16[128,512]{1,0:T(8,128)(2,1)S(1)}, u32[]{:S(2)}, u32[]{:S(2)}) collective-permute-start(bf16[128,512]{1,0:T(8,128)(2,1)S(1)} %next_states.5), channel_id=1, source_target_pairs={{0,4},{1,5},{2,6},{3,7},{16,20},{17,21},{18,22},{19,23}} | collective-permute-start | bytes 393224 | tf_op jit(solution)/shard_map/ppermute | solution.py:391
  4.6 4.9 %collective-permute-start.8 = (bf16[128,512]{1,0:T(8,128)(2,1)S(1)}, bf16[128,512]{1,0:T(8,128)(2,1)S(1)}, u32[]{:S(2)}, u32[]{:S(2)}) collective-permute-start(bf16[128,512]{1,0:T(8,128)(2,1)S(1)} %add_convert_fusion.7._), channel_id=1, source_target_pairs={{4,8},{5,9},{6,10},{7,11},{20,24},{21,25},{22,26},{23,27}} | collective-permute-start | bytes 393224 | tf_op jit(solution)/shard_map/ppermute | solution.py:391
  5.4 5.5 %collective-permute-start.7 = (bf16[128,512]{1,0:T(8,128)(2,1)S(1)}, bf16[128,512]{1,0:T(8,128)(2,1)S(1)}, u32[]{:S(2)}, u32[]{:S(2)}) collective-permute-start(bf16[128,512]{1,0:T(8,128)(2,1)S(1)} %add_convert_fusion.6._), channel_id=1, source_target_pairs={{4,8},{5,9},{6,10},{7,11},{20,24},{21,25},{22,26},{23,27}} | collective-permute-start | bytes 393224 | tf_op jit(solution)/shard_map/ppermute | solution.py:391
  6.2 6.1 %collective-permute-start.6 = (bf16[128,512]{1,0:T(8,128)(2,1)S(1)}, bf16[128,512]{1,0:T(8,128)(2,1)S(1)}, u32[]{:S(2)}, u32[]{:S(2)}) collective-permute-start(bf16[128,512]{1,0:T(8,128)(2,1)S(1)} %add_convert_fusion.5._), channel_id=1, source_target_pairs={{4,8},{5,9},{6,10},{7,11},{20,24},{21,25},{22,26},{23,27}} | collective-permute-start | bytes 393224 | tf_op jit(solution)/shard_map/ppermute | solution.py:391
  6.9 7.5 %collective-permute-start.10 = (bf16[128,512]{1,0:T(8,128)(2,1)S(1)}, bf16[128,512]{1,0:T(8,128)(2,1)S(1)}, u32[]{:S(2)}, u32[]{:S(2)}) collective-permute-start(bf16[128,512]{1,0:T(8,128)(2,1)S(1)} %add_convert_fusion.4._), channel_id=1, source_target_pairs={{4,8},{5,9},{6,10},{7,11},{20,24},{21,25},{22,26},{23,27}} | collective-permute-start | bytes 393224 | tf_op jit(solution)/shard_map/ppermute | solution.py:391
  7.6 6.8 %collective-permute-start.5 = (bf16[8,2560]{1,0:T(8,128)(2,1)S(1)}, bf16[8,2560]{1,0:T(8,128)(2,1)S(1)}, u32[]{:S(2)}, u32[]{:S(2)}) collective-permute-start(bf16[8,2560]{1,0:T(8,128)(2,1)S(1)} %get-tuple-element.40._), channel_id=1, source_target_pairs={{8,12},{9,13},{10,14},{11,15},{24,28},{25,29},{26,30},{27,31}} | collective-permute-start | bytes 122888 | tf_op jit(solution)/shard_map/ppermute | solution.py:391
  8.9 0.7 %copy-start.5 = (f32[32]{0:T(128)S(1)}, f32[32]{0:T(128)}, u32[]{:S(2)}) copy-start(f32[32]{0:T(128)} %param.16) | copy-start | bytes 388
  9.6 11.3 %collective-permute-start.12 = (bf16[128,512]{1,0:T(8,128)(2,1)S(1)}, bf16[128,512]{1,0:T(8,128)(2,1)S(1)}, u32[]{:S(2)}, u32[]{:S(2)}) collective-permute-start(bf16[128,512]{1,0:T(8,128)(2,1)S(1)} %add_convert_fusion.3), channel_id=1, source_target_pairs={{8,12},{9,13},{10,14},{11,15},{24,28},{25,29},{26,30},{27,31}} | collective-permute-start | bytes 393224 | tf_op jit(solution)/shard_map/ppermute | solution.py:391
  11.0 13.0 %collective-permute-start.13 = (bf16[128,512]{1,0:T(8,128)(2,1)S(1)}, bf16[128,512]{1,0:T(8,128)(2,1)S(1)}, u32[]{:S(2)}, u32[]{:S(2)}) collective-permute-start(bf16[128,512]{1,0:T(8,128)(2,1)S(1)} %add_convert_fusion.2), channel_id=1, source_target_pairs={{8,12},{9,13},{10,14},{11,15},{24,28},{25,29},{26,30},{27,31}} | collective-permute-start | bytes 393224 | tf_op jit(solution)/shard_map/ppermute | solution.py:391
  12.3 14.5 %collective-permute-start.9 = (bf16[128,512]{1,0:T(8,128)(2,1)S(1)}, bf16[128,512]{1,0:T(8,128)(2,1)S(1)}, u32[]{:S(2)}, u32[]{:S(2)}) collective-permute-start(bf16[128,512]{1,0:T(8,128)(2,1)S(1)} %add_convert_fusion.1), channel_id=1, source_target_pairs={{8,12},{9,13},{10,14},{11,15},{24,28},{25,29},{26,30},{27,31}} | collective-permute-start | bytes 393224 | tf_op jit(solution)/shard_map/ppermute | solution.py:391
  14.5 13.7 %collective-permute-start.11 = (bf16[128,512]{1,0:T(8,128)(2,1)S(1)}, bf16[128,512]{1,0:T(8,128)(2,1)S(1)}, u32[]{:S(2)}, u32[]{:S(2)}) collective-permute-start(bf16[128,512]{1,0:T(8,128)(2,1)S(1)} %add_convert_fusion), channel_id=1, source_target_pairs={{8,12},{9,13},{10,14},{11,15},{24,28},{25,29},{26,30},{27,31}} | collective-permute-start | bytes 393224 | tf_op jit(solution)/shard_map/ppermute | solution.py:391

commit v22 on v20

--- a/solution.py
+++ b/solution.py
@@ -12,7 +12,7 @@
 BF16 = jnp.bfloat16
 CHAIN_MOST = 4
 PARTS = (1, 1, 1, 1)
-CHUNK = 128
+CHUNK = 256
 RIM = 8
 
 

time: 29.6 us -> 29.7 us (level)
  no operation moved by 1% of the time
where the time goes in v22:
time: 29.7 us; the launch traced here: 29.3 us
  starting transfers between devices  12.7 us (43%)
  waiting for transfers between devices  9.49 us (32%)
  Pallas kernels  5.41 us (18%)
  local copies, waits for them, and re-layouts  0.95 us (3%)
  between operations  0.41 us (1%)
  other arithmetic  0.31 us (1%)
    ppermute x14, starting transfers between devices, shifted(): return lax.ppermute(value, 'seq', route)  12.7 us
    ppermute x14, waiting for transfers between devices, shifted(): return lax.ppermute(value, 'seq', route)  9.49 us
    pallas_call x1, Pallas kernels, intra(): pl.pallas_call(functools.partial(intra_kernel, len(befores)), out_shape=[...  2.16 us
    pallas_call x2, Pallas kernels, shards(): pl.pallas_call(functools.partial(output_kernel, begin, spans, unready), o...  1.96 us
    unnamed x18, local copies, waits for them, and re-layouts  0.95 us
    pallas_call x1, Pallas kernels, prepared(): pl.pallas_call(functools.partial(prepare_kernel, cuts), out_shape=[jax.Sh...  0.62 us
  transfers between devices with their start and end apart: 14, of which 4 were waited for; matrix products, arithmetic and copies ran while one was open for 1% of the time, Pallas kernels for 15%

profile of v22, /device:TPU:30, one launch (start us, length us, event | category | flops | bytes accessed | tf_op | source)
XLA Modules:
  0.0 29.3 jit_solution(9829191996244037122)
XLA Ops:
  0.0 0.0 copy-start.7
  0.0 0.1 first_states.1
  0.1 0.0 copy-start.8
  0.1 0.8 %collective-permute-start.1 = (bf16[144,512]{1,0:T(8,128)(2,1)S(1)}, bf16[144,512]{1,0:T(8,128)(2,1)S(1)}, u32[]{:S(2)}, u32[]{:S(2)}) collective-permute-start(bf16[144,512]{1,0:T(8,128)(2,1)S(1)} %get-tuple-element.27._), channel_id=1, source_target_pairs={{0,4},{1,5},{2,6},{3,7},{16,20},{17,21},{18,22},{19,23}} | collective-permute-start | bytes 442376 | tf_op jit(solution)/shard_map/ppermute | solution.py:382
  0.9 0.1 copy-done
  1.0 0.0 copy-done.1
  1.1 0.0 copy-done.5
  1.1 0.0 copy-done.7
  1.1 0.0 copy-done.8
  1.1 0.0 copy-start.3
  1.1 0.6 %prepared.1 = (bf16[8,2560]{1,0:T(8,128)(2,1)S(1)}, f32[1,2048]{1,0:T(1,128)S(1)}, f32[128,2048]{1,0:T(8,128)S(1)}, f32[1,512]{1,0:T(1,128)S(1)}, f32[1,512]{1,0...) custom-call(bf16[144,512]{1,0:T(8,128)(2,1)S(1)} %get-tuple-element.27._, bf16[128,2048]{1,0:T(8,128)(2,1)S(1)} %copy-done, ...), custom_call_target="tpu_custom_call" | custom-call | tf_op jit(solution)/shard_map/prepared/pallas_call | solution.py:406
  1.7 0.1 copy-done.2
  1.8 0.7 %collective-permute-start.4 = (bf16[128,512]{1,0:T(8,128)(2,1)S(1)}, bf16[128,512]{1,0:T(8,128)(2,1)S(1)}, u32[]{:S(2)}, u32[]{:S(2)}) collective-permute-start(bf16[128,512]{1,0:T(8,128)(2,1)S(1)} %next_states.3._), channel_id=1, source_target_pairs={{0,4},{1,5},{2,6},{3,7},{16,20},{17,21},{18,22},{19,23}} | collective-permute-start | bytes 393224 | tf_op jit(solution)/shard_map/ppermute | solution.py:382
  2.5 0.7 %collective-permute-start = (bf16[8,2560]{1,0:T(8,128)(2,1)S(1)}, bf16[8,2560]{1,0:T(8,128)(2,1)S(1)}, u32[]{:S(2)}, u32[]{:S(2)}) collective-permute-start(bf16[8,2560]{1,0:T(8,128)(2,1)S(1)} %get-tuple-element.40._), channel_id=1, source_target_pairs={{4,8},{5,9},{6,10},{7,11},{20,24},{21,25},{22,26},{23,27}} | collective-permute-start | bytes 122888 | tf_op jit(solution)/shard_map/ppermute | solution.py:382
  3.2 0.7 %collective-permute-start.3 = (bf16[128,512]{1,0:T(8,128)(2,1)S(1)}, bf16[128,512]{1,0:T(8,128)(2,1)S(1)}, u32[]{:S(2)}, u32[]{:S(2)}) collective-permute-start(bf16[128,512]{1,0:T(8,128)(2,1)S(1)} %next_states.4._), channel_id=1, source_target_pairs={{0,4},{1,5},{2,6},{3,7},{16,20},{17,21},{18,22},{19,23}} | collective-permute-start | bytes 393224 | tf_op jit(solution)/shard_map/ppermute | solution.py:382
  3.9 0.7 %collective-permute-start.2 = (bf16[128,512]{1,0:T(8,128)(2,1)S(1)}, bf16[128,512]{1,0:T(8,128)(2,1)S(1)}, u32[]{:S(2)}, u32[]{:S(2)}) collective-permute-start(bf16[128,512]{1,0:T(8,128)(2,1)S(1)} %next_states.5), channel_id=1, source_target_pairs={{0,4},{1,5},{2,6},{3,7},{16,20},{17,21},{18,22},{19,23}} | collective-permute-start | bytes 393224 | tf_op jit(solution)/shard_map/ppermute | solution.py:382
  4.6 0.0 collective-permute-done.1.rows.refs_1_.refs_0_
  4.6 0.7 %collective-permute-start.8 = (bf16[128,512]{1,0:T(8,128)(2,1)S(1)}, bf16[128,512]{1,0:T(8,128)(2,1)S(1)}, u32[]{:S(2)}, u32[]{:S(2)}) collective-permute-start(bf16[128,512]{1,0:T(8,128)(2,1)S(1)} %add_convert_fusion.7._), channel_id=1, source_target_pairs={{4,8},{5,9},{6,10},{7,11},{20,24},{21,25},{22,26},{23,27}} | collective-permute-start | bytes 393224 | tf_op jit(solution)/shard_map/ppermute | solution.py:382
  5.3 0.0 collective-permute-done.4.refs_0_
  5.4 0.7 %collective-permute-start.7 = (bf16[128,512]{1,0:T(8,128)(2,1)S(1)}, bf16[128,512]{1,0:T(8,128)(2,1)S(1)}, u32[]{:S(2)}, u32[]{:S(2)}) collective-permute-start(bf16[128,512]{1,0:T(8,128)(2,1)S(1)} %add_convert_fusion.6._), channel_id=1, source_target_pairs={{4,8},{5,9},{6,10},{7,11},{20,24},{21,25},{22,26},{23,27}} | collective-permute-start | bytes 393224 | tf_op jit(solution)/shard_map/ppermute | solution.py:382
  6.1 0.0 collective-permute-done.3.refs_0_
  6.2 0.7 %collective-permute-start.6 = (bf16[128,512]{1,0:T(8,128)(2,1)S(1)}, bf16[128,512]{1,0:T(8,128)(2,1)S(1)}, u32[]{:S(2)}, u32[]{:S(2)}) collective-permute-start(bf16[128,512]{1,0:T(8,128)(2,1)S(1)} %add_convert_fusion.5._), channel_id=1, source_target_pairs={{4,8},{5,9},{6,10},{7,11},{20,24},{21,25},{22,26},{23,27}} | collective-permute-start | bytes 393224 | tf_op jit(solution)/shard_map/ppermute | solution.py:382
  6.8 0.0 collective-permute-done.2.refs_1_
  6.9 0.7 %collective-permute-start.10 = (bf16[128,512]{1,0:T(8,128)(2,1)S(1)}, bf16[128,512]{1,0:T(8,128)(2,1)S(1)}, u32[]{:S(2)}, u32[]{:S(2)}) collective-permute-start(bf16[128,512]{1,0:T(8,128)(2,1)S(1)} %add_convert_fusion.4._), channel_id=1, source_target_pairs={{4,8},{5,9},{6,10},{7,11},{20,24},{21,25},{22,26},{23,27}} | collective-permute-start | bytes 393224 | tf_op jit(solution)/shard_map/ppermute | solution.py:382
  7.6 0.0 collective-permute-done.refs_0_.rows
  7.6 1.3 %collective-permute-start.5 = (bf16[8,2560]{1,0:T(8,128)(2,1)S(1)}, bf16[8,2560]{1,0:T(8,128)(2,1)S(1)}, u32[]{:S(2)}, u32[]{:S(2)}) collective-permute-start(bf16[8,2560]{1,0:T(8,128)(2,1)S(1)} %get-tuple-element.40._), channel_id=1, source_target_pairs={{8,12},{9,13},{10,14},{11,15},{24,28},{25,29},{26,30},{27,31}} | collective-permute-start | bytes 122888 | tf_op jit(solution)/shard_map/ppermute | solution.py:382
  8.9 0.0 copy-start.6
  8.9 0.6 %copy-done.6 = f32[32]{0:T(128)S(1)} copy-done((f32[32]{0:T(128)S(1)}, f32[32]{0:T(128)}, u32[]{:S(2)}) %copy-start.6) | copy-done | bytes 152
  9.6 0.0 collective-permute-done.8.refs_1_
  9.6 1.3 %collective-permute-start.11 = (bf16[128,512]{1,0:T(8,128)(2,1)S(1)}, bf16[128,512]{1,0:T(8,128)(2,1)S(1)}, u32[]{:S(2)}, u32[]{:S(2)}) collective-permute-start(bf16[128,512]{1,0:T(8,128)(2,1)S(1)} %add_convert_fusion.3), channel_id=1, source_target_pairs={{8,12},{9,13},{10,14},{11,15},{24,28},{25,29},{26,30},{27,31}} | collective-permute-start | bytes 393224 | tf_op jit(solution)/shard_map/ppermute | solution.py:382
  10.9 0.0 collective-permute-done.7.refs_1_
  11.0 0.0 copy-start.4
  11.0 1.4 %collective-permute-start.13 = (bf16[128,512]{1,0:T(8,128)(2,1)S(1)}, bf16[128,512]{1,0:T(8,128)(2,1)S(1)}, u32[]{:S(2)}, u32[]{:S(2)}) collective-permute-start(bf16[128,512]{1,0:T(8,128)(2,1)S(1)} %add_convert_fusion.2), channel_id=1, source_target_pairs={{8,12},{9,13},{10,14},{11,15},{24,28},{25,29},{26,30},{27,31}} | collective-permute-start | bytes 393224 | tf_op jit(solution)/shard_map/ppermute | solution.py:382
  12.4 0.0 collective-permute-done.6.refs_1_
  12.5 1.3 %collective-permute-start.9 = (bf16[128,512]{1,0:T(8,128)(2,1)S(1)}, bf16[128,512]{1,0:T(8,128)(2,1)S(1)}, u32[]{:S(2)}, u32[]{:S(2)}) collective-permute-start(bf16[128,512]{1,0:T(8,128)(2,1)S(1)} %add_convert_fusion.1), channel_id=1, source_target_pairs={{8,12},{9,13},{10,14},{11,15},{24,28},{25,29},{26,30},{27,31}} | collective-permute-start | bytes 393224 | tf_op jit(solution)/shard_map/ppermute | solution.py:382
  13.8 0.7 %collective-permute-done.5.refs_2_ = bf16[8,2560]{1,0:T(8,128)(2,1)S(1)} collective-permute-done((bf16[8,2560]{1,0:T(8,128)(2,1)S(1)}, bf16[8,2560]{1,0:T(8,128)(2,1)S(1)}, u32[]{:S(2)}, u32[]{:S(2)}) %collective-permute-start.5) | collective-permute-done | bytes 40992 | tf_op jit(solution)/shard_map/ppermute | solution.py:382
  14.4 0.0 collective-permute-done.10.refs_2_
  14.4 6.5 %collective-permute-done.11.refs_2_ = bf16[128,512]{1,0:T(8,128)(2,1)S(1)} collective-permute-done((bf16[128,512]{1,0:T(8,128)(2,1)S(1)}, bf16[128,512]{1,0:T(8,128)(2,1)S(1)}, u32[]{:S(2)}, u32[]{:S(2)}) %collective-permute-start.11) | collective-permute-done | bytes 131104 | tf_op jit(solution)/shard_map/ppermute | solution.py:382
  21.0 1.3 %collective-permute-start.12 = (bf16[128,512]{1,0:T(8,128)(2,1)S(1)}, bf16[128,512]{1,0:T(8,128)(2,1)S(1)}, u32[]{:S(2)}, u32[]{:S(2)}) collective-permute-start(bf16[128,512]{1,0:T(8,128)(2,1)S(1)} %add_convert_fusion), channel_id=1, source_target_pairs={{8,12},{9,13},{10,14},{11,15},{24,28},{25,29},{26,30},{27,31}} | collective-permute-start | bytes 393224 | tf_op jit(solution)/shard_map/ppermute | solution.py:382
  22.3 2.2 %intra.1 = (f32[128,2048]{1,0:T(8,128)S(1)}, f32[128,2048]{1,0:T(8,128)S(1)}, bf16[128,256]{1,0:T(8,128)(2,1)S(1)}) custom-call(f32[1,32]{1,0:T(1,128)S(1)} %bitcast.31, bf16[8,2560]{1,0:T(8,128)(2,1)S(1)} %collective-permute-done.refs_0_.rows, bf16[144,512]{1,0:T(8,128)(2,1)S(1)} %collective-permute-done.1.rows.refs_1_.refs_0_, ...), custom_call_target="tpu_custom_call" | custom-call | flops 134217728 | bytes 3145728 | tf_op jit(solution)/shard_map/intra/pallas_call | solution.py:430
  24.5 0.2 gated.4.refs_0_
  24.6 0.0 collective-permute-done.13.refs_2_
  24.7 0.2 gated.5.refs_1_
  24.8 0.9 %outputs.2.refs_4_ = bf16[128,2048]{1,0:T(8,128)(2,1)} custom-call(s32[1]{0:T(128)} %bitcast.which, bf16[128,256]{1,0:T(8,128)(2,1)S(1)} %get-tuple-element.41.c, f32[128,2048]{1,0:T(8,128)S(1)} %get-tuple-element.42.y_part, f32[128,2048]{1,0:T(8,128)S(1)} %get-tuple-element.43.lead, f32[1,2048]{1,0:T(1,128)S(1)} %get-tuple-element.44.gain, ...), custom_call_target="tpu_custom_call" | custom-call | tf_op jit(solution)/shard_map/outputs/pallas_call | solution.py:526
  25.8 1.1 %collective-permute-done.9.refs_2_ = bf16[128,512]{1,0:T(8,128)(2,1)S(1)} collective-permute-done((bf16[128,512]{1,0:T(8,128)(2,1)S(1)}, bf16[128,512]{1,0:T(8,128)(2,1)S(1)}, u32[]{:S(2)}, u32[]{:S(2)}) %collective-permute-start.9) | collective-permute-done | bytes 131104 | tf_op jit(solution)/shard_map/ppermute | solution.py:382
  26.8 0.2 gated.3.refs_0_
  27.0 1.2 %collective-permute-done.12.refs_3_ = bf16[128,512]{1,0:T(8,128)(2,1)S(1)} collective-permute-done((bf16[128,512]{1,0:T(8,128)(2,1)S(1)}, bf16[128,512]{1,0:T(8,128)(2,1)S(1)}, u32[]{:S(2)}, u32[]{:S(2)}) %collective-permute-start.12) | collective-permute-done | bytes 131104 | tf_op jit(solution)/shard_map/ppermute | solution.py:382
  28.2 1.0 %outputs.3 = bf16[128,2048]{1,0:T(8,128)(2,1)} custom-call(s32[1]{0:T(128)} %bitcast.which, bf16[128,256]{1,0:T(8,128)(2,1)S(1)} %get-tuple-element.41.c, f32[128,2048]{1,0:T(8,128)S(1)} %get-tuple-element.42.y_part, f32[128,2048]{1,0:T(8,128)S(1)} %get-tuple-element.43.lead, f32[1,2048]{1,0:T(1,128)S(1)} %get-tuple-element.44.gain, ...), custom_call_target="tpu_custom_call", output_to_operand_aliasing={{}: (9, {})} | custom-call | tf_op jit(solution)/shard_map/outputs/pallas_call | solution.py:526
  (25 shorter events, 0.4 us)
Async XLA Ops:
  0.0 1.0 %copy-start = (bf16[128,2048]{1,0:T(8,128)(2,1)S(1)}, bf16[128,2048]{1,0:T(8,128)(2,1)}, u32[]{:S(2)}) copy-start(bf16[128,2048]{1,0:T(8,128)(2,1)} %x.23) | copy-start | bytes 1572868
  0.0 1.1 %copy-start.1 = (bf16[128,2,256]{2,1,0:T(2,128)(2,1)S(1)}, bf16[128,2,256]{2,1,0:T(2,128)(2,1)}, u32[]{:S(2)}) copy-start(bf16[128,2,256]{2,1,0:T(2,128)(2,1)} %bc.23) | copy-start | bytes 393220
  0.0 1.1 %copy-start.5 = (f32[128,32]{0,1:T(8,128)S(1)}, f32[128,32]{0,1:T(8,128)}, u32[]{:S(2)}) copy-start(f32[128,32]{0,1:T(8,128)} %param.12) | copy-start | bytes 49156
  0.0 1.1 %copy-start.7 = (f32[2048]{0:T(1024)S(1)}, f32[2048]{0:T(1024)}, u32[]{:S(2)}) copy-start(f32[2048]{0:T(1024)} %param.17) | copy-start | bytes 24580
  0.1 1.0 %copy-start.8 = (f32[32]{0:T(128)S(1)}, f32[32]{0:T(128)}, u32[]{:S(2)}) copy-start(f32[32]{0:T(128)} %param.15) | copy-start | bytes 388
  0.1 4.5 %collective-permute-start.1 = (bf16[144,512]{1,0:T(8,128)(2,1)S(1)}, bf16[144,512]{1,0:T(8,128)(2,1)S(1)}, u32[]{:S(2)}, u32[]{:S(2)}) collective-permute-start(bf16[144,512]{1,0:T(8,128)(2,1)S(1)} %get-tuple-element.27._), channel_id=1, source_target_pairs={{0,4},{1,5},{2,6},{3,7},{16,20},{17,21},{18,22},{19,23}} | collective-permute-start | bytes 442376 | tf_op jit(solution)/shard_map/ppermute | solution.py:382
  1.1 0.8 %copy-start.2 = (f32[4,2048]{1,0:T(4,128)S(1)}, f32[4,2048]{1,0:T(4,128)}, u32[]{:S(2)}) copy-start(f32[4,2048]{1,0:T(4,128)} %taps_x.21) | copy-start | bytes 98308
  1.1 0.8 %copy-start.3 = (f32[4,2,256]{2,1,0:T(2,128)S(1)}, f32[4,2,256]{2,1,0:T(2,128)}, u32[]{:S(2)}) copy-start(f32[4,2,256]{2,1,0:T(2,128)} %taps_bc.21) | copy-start | bytes 24580
  1.8 3.5 %collective-permute-start.4 = (bf16[128,512]{1,0:T(8,128)(2,1)S(1)}, bf16[128,512]{1,0:T(8,128)(2,1)S(1)}, u32[]{:S(2)}, u32[]{:S(2)}) collective-permute-start(bf16[128,512]{1,0:T(8,128)(2,1)S(1)} %next_states.3._), channel_id=1, source_target_pairs={{0,4},{1,5},{2,6},{3,7},{16,20},{17,21},{18,22},{19,23}} | collective-permute-start | bytes 393224 | tf_op jit(solution)/shard_map/ppermute | solution.py:382
  2.5 5.1 %collective-permute-start = (bf16[8,2560]{1,0:T(8,128)(2,1)S(1)}, bf16[8,2560]{1,0:T(8,128)(2,1)S(1)}, u32[]{:S(2)}, u32[]{:S(2)}) collective-permute-start(bf16[8,2560]{1,0:T(8,128)(2,1)S(1)} %get-tuple-element.40._), channel_id=1, source_target_pairs={{4,8},{5,9},{6,10},{7,11},{20,24},{21,25},{22,26},{23,27}} | collective-permute-start | bytes 122888 | tf_op jit(solution)/shard_map/ppermute | solution.py:382
  3.2 2.9 %collective-permute-start.3 = (bf16[128,512]{1,0:T(8,128)(2,1)S(1)}, bf16[128,512]{1,0:T(8,128)(2,1)S(1)}, u32[]{:S(2)}, u32[]{:S(2)}) collective-permute-start(bf16[128,512]{1,0:T(8,128)(2,1)S(1)} %next_states.4._), channel_id=1, source_target_pairs={{0,4},{1,5},{2,6},{3,7},{16,20},{17,21},{18,22},{19,23}} | collective-permute-start | bytes 393224 | tf_op jit(solution)/shard_map/ppermute | solution.py:382
  3.9 2.9 %collective-permute-start.2 = (bf16[128,512]{1,0:T(8,128)(2,1)S(1)}, bf16[128,512]{1,0:T(8,128)(2,1)S(1)}, u32[]{:S(2)}, u32[]{:S(2)}) collective-permute-start(bf16[128,512]{1,0:T(8,128)(2,1)S(1)} %next_states.5), channel_id=1, source_target_pairs={{0,4},{1,5},{2,6},{3,7},{16,20},{17,21},{18,22},{19,23}} | collective-permute-start | bytes 393224 | tf_op jit(solution)/shard_map/ppermute | solution.py:382
  4.6 4.9 %collective-permute-start.8 = (bf16[128,512]{1,0:T(8,128)(2,1)S(1)}, bf16[128,512]{1,0:T(8,128)(2,1)S(1)}, u32[]{:S(2)}, u32[]{:S(2)}) collective-permute-start(bf16[128,512]{1,0:T(8,128)(2,1)S(1)} %add_convert_fusion.7._), channel_id=1, source_target_pairs={{4,8},{5,9},{6,10},{7,11},{20,24},{21,25},{22,26},{23,27}} | collective-permute-start | bytes 393224 | tf_op jit(solution)/shard_map/ppermute | solution.py:382
  5.4 5.5 %collective-permute-start.7 = (bf16[128,512]{1,0:T(8,128)(2,1)S(1)}, bf16[128,512]{1,0:T(8,128)(2,1)S(1)}, u32[]{:S(2)}, u32[]{:S(2)}) collective-permute-start(bf16[128,512]{1,0:T(8,128)(2,1)S(1)} %add_convert_fusion.6._), channel_id=1, source_target_pairs={{4,8},{5,9},{6,10},{7,11},{20,24},{21,25},{22,26},{23,27}} | collective-permute-start | bytes 393224 | tf_op jit(solution)/shard_map/ppermute | solution.py:382
  6.2 6.3 %collective-permute-start.6 = (bf16[128,512]{1,0:T(8,128)(2,1)S(1)}, bf16[128,512]{1,0:T(8,128)(2,1)S(1)}, u32[]{:S(2)}, u32[]{:S(2)}) collective-permute-start(bf16[128,512]{1,0:T(8,128)(2,1)S(1)} %add_convert_fusion.5._), channel_id=1, source_target_pairs={{4,8},{5,9},{6,10},{7,11},{20,24},{21,25},{22,26},{23,27}} | collective-permute-start | bytes 393224 | tf_op jit(solution)/shard_map/ppermute | solution.py:382
  6.9 7.5 %collective-permute-start.10 = (bf16[128,512]{1,0:T(8,128)(2,1)S(1)}, bf16[128,512]{1,0:T(8,128)(2,1)S(1)}, u32[]{:S(2)}, u32[]{:S(2)}) collective-permute-start(bf16[128,512]{1,0:T(8,128)(2,1)S(1)} %add_convert_fusion.4._), channel_id=1, source_target_pairs={{4,8},{5,9},{6,10},{7,11},{20,24},{21,25},{22,26},{23,27}} | collective-permute-start | bytes 393224 | tf_op jit(solution)/shard_map/ppermute | solution.py:382
  7.6 6.8 %collective-permute-start.5 = (bf16[8,2560]{1,0:T(8,128)(2,1)S(1)}, bf16[8,2560]{1,0:T(8,128)(2,1)S(1)}, u32[]{:S(2)}, u32[]{:S(2)}) collective-permute-start(bf16[8,2560]{1,0:T(8,128)(2,1)S(1)} %get-tuple-element.40._), channel_id=1, source_target_pairs={{8,12},{9,13},{10,14},{11,15},{24,28},{25,29},{26,30},{27,31}} | collective-permute-start | bytes 122888 | tf_op jit(solution)/shard_map/ppermute | solution.py:382
  8.9 0.7 %copy-start.6 = (f32[32]{0:T(128)S(1)}, f32[32]{0:T(128)}, u32[]{:S(2)}) copy-start(f32[32]{0:T(128)} %param.16) | copy-start | bytes 388
  9.6 11.3 %collective-permute-start.11 = (bf16[128,512]{1,0:T(8,128)(2,1)S(1)}, bf16[128,512]{1,0:T(8,128)(2,1)S(1)}, u32[]{:S(2)}, u32[]{:S(2)}) collective-permute-start(bf16[128,512]{1,0:T(8,128)(2,1)S(1)} %add_convert_fusion.3), channel_id=1, source_target_pairs={{8,12},{9,13},{10,14},{11,15},{24,28},{25,29},{26,30},{27,31}} | collective-permute-start | bytes 393224 | tf_op jit(solution)/shard_map/ppermute | solution.py:382
  11.0 11.3 %copy-start.4 = (bf16[128,2048]{1,0:T(8,128)(2,1)S(1)}, bf16[128,2048]{1,0:T(8,128)(2,1)}, u32[]{:S(2)}) copy-start(bf16[128,2048]{1,0:T(8,128)(2,1)} %refs_5_.1) | copy-start | bytes 1572868
  11.0 13.7 %collective-permute-start.13 = (bf16[128,512]{1,0:T(8,128)(2,1)S(1)}, bf16[128,512]{1,0:T(8,128)(2,1)S(1)}, u32[]{:S(2)}, u32[]{:S(2)}) collective-permute-start(bf16[128,512]{1,0:T(8,128)(2,1)S(1)} %add_convert_fusion.2), channel_id=1, source_target_pairs={{8,12},{9,13},{10,14},{11,15},{24,28},{25,29},{26,30},{27,31}} | collective-permute-start | bytes 393224 | tf_op jit(solution)/shard_map/ppermute | solution.py:382
  12.5 14.4 %collective-permute-start.9 = (bf16[128,512]{1,0:T(8,128)(2,1)S(1)}, bf16[128,512]{1,0:T(8,128)(2,1)S(1)}, u32[]{:S(2)}, u32[]{:S(2)}) collective-permute-start(bf16[128,512]{1,0:T(8,128)(2,1)S(1)} %add_convert_fusion.1), channel_id=1, source_target_pairs={{8,12},{9,13},{10,14},{11,15},{24,28},{25,29},{26,30},{27,31}} | collective-permute-start | bytes 393224 | tf_op jit(solution)/shard_map/ppermute | solution.py:382
  21.0 7.3 %collective-permute-start.12 = (bf16[128,512]{1,0:T(8,128)(2,1)S(1)}, bf16[128,512]{1,0:T(8,128)(2,1)S(1)}, u32[]{:S(2)}, u32[]{:S(2)}) collective-permute-start(bf16[128,512]{1,0:T(8,128)(2,1)S(1)} %add_convert_fusion), channel_id=1, source_target_pairs={{8,12},{9,13},{10,14},{11,15},{24,28},{25,29},{26,30},{27,31}} | collective-permute-start | bytes 393224 | tf_op jit(solution)/shard_map/ppermute | solution.py:382
